TPU v7x, 32 devices: a whole 2x2x4 slice. The times are simulated.
32 devices in a mesh: group: 2 (over y), fm: 4 (over z), kl: 2 (over x), pol: 2 (over core).
Axes of the slice: x: 2, y: 2, z: 4, core: 2. Of those that a mesh axis runs over, the one named last changes fastest.
Arguments:
- visibility: bfloat16 [64, 4, 96, 1024], P(('group', 'fm'), None, 'kl', 'pol'), parts along dimension 0, may hold values from -6 to 6
- beam_transfer: bfloat16 [8, 32, 1024, 1024], P(('group', 'fm'), None, 'pol', 'kl'), parts along dimension 0, may hold values from -0.1875 to 0.1875
- tile_mask: int32 [4, 8, 8], P('fm', 'pol', 'kl'), may hold values 0 or 1
- first_block: int32 [4], P('fm'), may hold values from 0 to 7, as said below
- eigen_modes: bfloat16 [8, 32, 24], P(('group', 'fm')), parts along dimension 0, may hold values from -1 to 1
- signal_noise: float32 [8, 24], P(('group', 'fm')), parts along dimension 0, may hold values from 0.1 to 10
Outputs:
- filtered: bfloat16 [64, 4, 96, 1024], P(('group', 'fm'), None, 'pol', 'kl'), parts along dimension 0
There are 2 independent parts, one for each index of `group`. A program takes and returns all parts, laid end to end along the dimension named above; an argument that names none is the same for every part. Nothing has to cross between parts.
Inputs may be any that keep to these rules, and one draw needn't show every extreme that they name: first_block never decreases along the m-modes; the first m-mode starts at block 0 and the last at block 7.
All inputs are finite; a program needn't handle non-finite values. No bound on the sum of `tile_mask` on one device may be relied on, other than what follows from the above.
Results may differ from a plain program's by a relative error of at most 0.01.
Values may be sent and summed in bfloat16 or wider, within the bound.
No kernel may reach another device: no remote copies, remote signals or barrier semaphores. Data moves between devices by JAX's collectives and lax.ppermute only.
A program may use at most 64 MiB of HBM per device.

v0:
```python
import jax
import jax.numpy as jnp
from jax import lax
from jax.sharding import PartitionSpec as P

TILE = 128


def per_device(visibility, beam_transfer, tile_mask, first_block, eigen_modes, signal_noise):
    owned_modes = beam_transfer.shape[0]
    freq_total = beam_transfer.shape[1]
    base_half = beam_transfer.shape[2]
    ell_local = beam_transfer.shape[3]
    base_tiles = base_half // TILE
    ell_tiles = ell_local // TILE
    block_ids = lax.axis_index("kl") * ell_tiles + jnp.arange(ell_tiles, dtype=jnp.int32)
    inside = (first_block[:, None] <= block_ids[None, :]).astype(jnp.int32)
    keep_tiles = tile_mask * inside[:, None, :]
    shaped = beam_transfer.reshape(owned_modes, freq_total, base_tiles, TILE, ell_tiles, TILE)
    masked_beam = shaped * keep_tiles.astype(jnp.bfloat16)[:, None, :, None, :, None]
    masked_beam = masked_beam.reshape(owned_modes, freq_total, base_half, ell_local)
    arrived = lax.all_to_all(visibility, "fm", split_axis=1, concat_axis=0, tiled=True)
    partial_value = jnp.einsum(
        "fmrb,mfbl->fmrl",
        lax.all_gather(arrived, "kl", axis=2, tiled=True),
        masked_beam,
        preferred_element_type=jnp.float32,
    )
    sky_sum = lax.psum_scatter(
        partial_value.astype(jnp.bfloat16), "pol", scatter_dimension=2, tiled=True
    ).astype(jnp.float32)
    modes_float = eigen_modes.astype(jnp.float32)
    coeffs = jnp.einsum("mfk,fmrl->mkrl", modes_float, sky_sum, precision=lax.Precision.HIGHEST)
    ratios = signal_noise / (1.0 + signal_noise)
    weighted = (coeffs * ratios[:, :, None, None]).astype(jnp.bfloat16)
    filtered = jnp.einsum(
        "mfk,mkrl->fmrl", eigen_modes, weighted, preferred_element_type=jnp.float32
    ).astype(jnp.bfloat16)
    return lax.all_to_all(filtered, "fm", split_axis=0, concat_axis=1, tiled=True)


def solution(mesh):
    placed = (
        P(("group", "fm"), None, "kl", "pol"),
        P(("group", "fm"), None, "pol", "kl"),
        P("fm", "pol", "kl"),
        P("fm"),
        P(("group", "fm"), None, None),
        P(("group", "fm"), None),
    )
    return jax.shard_map(
        per_device,
        mesh=mesh,
        in_specs=placed,
        out_specs=P(("group", "fm"), None, "pol", "kl"),
        check_vma=False,
    )
```

profile of v0, /device:TPU:12, one launch (start us, length us, event | category | flops | bytes accessed | tf_op | source)
XLA Modules:
  0.0 170.0 jit_solution(12435642968819853056)
XLA Ops:
  6.5 0.0 copy-start
  6.5 0.0 all-gather.2.cloned.1.call-start
  6.5 1.5 copy.9
  8.1 0.0 copy-start.1
  8.1 40.4 %all_to_all.36 = bf16[8,4,48,512]{3,2,0,1:T(8,128)(2,1)} all-to-all(bf16[8,4,48,512]{3,2,0,1:T(8,128)(2,1)S(1)} %copy.9), channel_id=1, replica_groups=mesh['group'=2,'fm'=4,'kl'=2,'pol'=2] {'fm'}, dimensions={1} | all-to-all | bytes 3145728 | tf_op jit(solution)/shard_map/all_to_all | solution.py:22
  48.4 0.0 all-gather.2.cloned.1.call-update
  48.5 0.0 reduce-scatter.2.cloned.1.call-start
  49.2 0.0 copy-done.1
  49.2 0.2 mul.44
  49.4 0.1 copy.21
  49.5 44.4 %all-gather.2.cloned.1.call-done = bf16[32,1,96,512]{3,2,0,1:T(8,128)(2,1)} async-done(((bf16[32,1,48,512]{3,2,0,1:T(8,128)(2,1)}), bf16[32,1,96,512]{3,2,0,1:T(8,128)(2,1)}) %all-gather.2.cloned.1.call-update) | async-done | bytes 3145744 | tf_op jit(solution)/shard_map/all_gather | solution.py:25
  93.9 12.1 %convert_bitcast_fusion = bf16[32,1,96,512]{3,2,0,1:T(8,128)(2,1)} fusion(bf16[1,32,512,512]{3,2,1,0:T(8,128)(2,1)} %param.7, bf16[512,512]{1,0:T(8,128)(2,1)S(1)} %bitcast.54, bf16[32,1,96,512]{3,2,0,1:T(8,128)(2,1)} %all-gather.2.cloned.1.call-done), kind=kOutput, calls=%fused_computation.5 | convolution fusion | flops 1645740032 | bytes 23592960 | tf_op jit(solution)/shard_map/fmrb,mfbl->fmrl/dot_general | solution.py:23
  106.1 0.0 copy-start.2
  106.1 0.0 reduce-scatter.2.cloned.1.call-update
  106.1 0.6 copy-done.2
  106.7 10.7 %reduce-scatter.2.cloned.1.call-done = bf16[32,1,48,512]{3,2,0,1:T(8,128)(2,1)} async-done(((bf16[32,1,96,512]{3,2,0,1:T(8,128)(2,1)}), bf16[32,1,48,512]{3,2,0,1:T(8,128)(2,1)}) %reduce-scatter.2.cloned.1.call-update) | async-done | bytes 1572880 | tf_op jit(solution)/shard_map/reduce_scatter | solution.py:29
  117.4 0.0 copy-done
  117.4 2.4 %fusion.11 = bf16[24,48,512]{2,0,1:T(8,128)(2,1)S(1)} fusion(bf16[32,48,512]{2,1,0:T(8,128)(2,1)} %bitcast.53, f32[24]{0:T(128)S(1)} %fusion.17, bf16[1,32,24]{1,2,0:T(8,128)(2,1)S(1)} %copy-done), kind=kOutput, calls=%fused_computation.11 | convolution fusion | flops 38928384 | bytes 2754144 | tf_op jit(solution)/shard_map/mfk,fmrl->mkrl/dot_general | solution.py:33
  119.8 0.6 fusion.10
  120.5 0.9 copy.10
  121.3 40.6 %all_to_all.37 = bf16[32,1,48,512]{3,2,1,0:T(8,128)(2,1)S(1)} all-to-all(bf16[32,1,48,512]{3,2,1,0:T(8,128)(2,1)S(1)} %copy.10), channel_id=1, replica_groups=mesh['group'=2,'fm'=4,'kl'=2,'pol'=2] {'fm'}, dimensions={0} | all-to-all | bytes 3145728 | tf_op jit(solution)/shard_map/all_to_all | solution.py:39
  161.9 1.2 copy.20
  (3 shorter events, 0.0 us)
Async XLA Ops:
  6.5 110.9 %copy-start = (bf16[1,32,24]{1,2,0:T(8,128)(2,1)S(1)}, bf16[1,32,24]{1,2,0:T(8,128)(2,1)}, u32[]{:S(2)}) copy-start(bf16[1,32,24]{1,2,0:T(8,128)(2,1)} %param.10) | copy-start | bytes 4612
  6.5 87.4 %all-gather.2.cloned.1.call-start = ((), (), s32[]{:S(2)}) async-start(), calls=%async_computation.3 | async-start | bytes 4718592 | tf_op jit(solution)/shard_map/all_gather | solution.py:25
  8.1 41.1 %copy-start.1 = (s32[1,4,4]{2,1,0:T(4,128)S(1)}, s32[1,4,4]{2,1,0:T(4,128)}, u32[]{:S(2)}) copy-start(s32[1,4,4]{2,1,0:T(4,128)} %param.8) | copy-start | bytes 196
  48.5 68.9 %reduce-scatter.2.cloned.1.call-start = ((), (), s32[]{:S(2)}) async-start(), calls=%async_computation.4 | async-start | bytes 4718592 | tf_op jit(solution)/shard_map/reduce_scatter | solution.py:29
  106.1 0.7 copy-start.2
Sparse Core Ops, SparseCore 0:
  48.6 45.2 all-gather.1
  106.2 11.1 reduce-scatter.1
where the time goes:
time: 173 us; the launch traced here: 170 us
  blocking collectives  80.9 us (47%)
  waiting for transfers between devices  55.1 us (32%)
  matrix products  15.2 us (9%)
  between operations  14.1 us (8%)
  local copies, waits for them, and re-layouts  4.56 us (3%)
    all_gather x1, waiting for transfers between devices, per_device(): lax.all_gather(arrived, 'kl', axis=2, tiled=True)  44.4 us
    all_to_all x1, blocking collectives, per_device(): lax.all_to_all(filtered, 'fm', split_axis=0, concat_axis=1, tiled=True)  40.6 us
    all_to_all x1, blocking collectives, per_device(): lax.all_to_all(visibility, 'fm', split_axis=1, concat_axis=0, tiled=True)  40.4 us
    dot_general x1, matrix products, per_device(): jnp.einsum('fmrb,mfbl->fmrl', lax.all_gather(arrived, 'kl', axis=2, tiled...  12.1 us
    reduce_scatter x1, waiting for transfers between devices, per_device(): lax.psum_scatter(partial_value.astype(jnp.bfloat16), 'pol', scatter_dimen...  10.7 us
  transfers between devices with their start and end apart: 2, of which 2 were waited for; matrix products, arithmetic and copies ran while one was open for 0% of the time, Pallas kernels for 0%

commit v1 on v0

--- a/solution.py
+++ b/solution.py
@@ -1,18 +1,200 @@
+import functools
 import jax
 import jax.numpy as jnp
 from jax import lax
+from jax.experimental import pallas as pl
+from jax.experimental.pallas import tpu as pltpu
 from jax.sharding import PartitionSpec as P
 
 TILE = 128
-
-
-def per_device(visibility, beam_transfer, tile_mask, first_block, eigen_modes, signal_noise):
-    owned_modes = beam_transfer.shape[0]
-    freq_total = beam_transfer.shape[1]
-    base_half = beam_transfer.shape[2]
-    ell_local = beam_transfer.shape[3]
-    base_tiles = base_half // TILE
-    ell_tiles = ell_local // TILE
+ROWS = 16
+STEP_F = 4
+VMEM_LIMIT = 40 * 1024 * 1024
+
+
+def project_kernel(where, *refs, parts, freqs, rows):
+    mine, others = refs[:parts], refs[parts:2 * parts]
+    beam_ref, modes_ref, stay_ref, leave_ref, mask, sky, lines = refs[2 * parts:]
+    piece, step = pl.program_id(0), pl.program_id(1)
+    base_tiles, ell_tiles = mask.shape[0] // TILE, mask.shape[1] // TILE
+
+    @pl.when((piece == 0) & (step == 0))
+    def _():
+        for b in range(base_tiles):
+            for l in range(ell_tiles):
+                kept = where[parts + 1 + b * ell_tiles + l].astype(jnp.float32)
+                mask[b * TILE:(b + 1) * TILE, l * TILE:(l + 1) * TILE] = jnp.full(
+                    (TILE, TILE), kept, jnp.float32
+                ).astype(jnp.bfloat16)
+
+    for which in range(parts):
+
+        @pl.when(piece == which)
+        def _():
+            lines[:, :rows] = mine[which][pl.ds(step * STEP_F, STEP_F)]
+            lines[:, rows:] = others[which][pl.ds(step * STEP_F, STEP_F)]
+
+    for u in range(STEP_F):
+        sky[piece * freqs + step * STEP_F + u] = jnp.dot(
+            lines[u], beam_ref[u] * mask[...], preferred_element_type=jnp.float32
+        ).astype(jnp.bfloat16)
+
+    @pl.when((piece == parts - 1) & (step == freqs // STEP_F - 1))
+    def _():
+        own = where[parts]
+        for ref, first in ((stay_ref, (1 - own) * rows), (leave_ref, own * rows)):
+            for g in range(rows // ROWS):
+                start = pl.multiple_of(first + g * ROWS, ROWS)
+                block = sky[:, pl.ds(start, ROWS), :].reshape(sky.shape[0] * ROWS, sky.shape[2])
+                value = jnp.dot(modes_ref[...], block, preferred_element_type=jnp.float32)
+                ref[:, g * ROWS:(g + 1) * ROWS, :] = value.astype(jnp.bfloat16).reshape(
+                    ref.shape[0], ROWS, ref.shape[2]
+                )
+
+
+def project(where, mine, others, beam, modes, n_modes):
+    parts = len(mine)
+    freqs, rows, base = mine[0].shape
+    ell = beam.shape[2]
+    whole = pl.BlockSpec((freqs, rows, base), lambda j, i, s: (0, 0, 0))
+    out = jax.ShapeDtypeStruct((n_modes, rows, ell), jnp.bfloat16)
+    out_spec = pl.BlockSpec((n_modes, rows, ell), lambda j, i, s: (0, 0, 0))
+    steps = freqs // STEP_F
+    return pl.pallas_call(
+        functools.partial(project_kernel, parts=parts, freqs=freqs, rows=rows),
+        grid_spec=pltpu.PrefetchScalarGridSpec(
+            num_scalar_prefetch=1,
+            grid=(parts, steps),
+            in_specs=[whole] * (2 * parts)
+            + [
+                pl.BlockSpec((STEP_F, base, ell), lambda j, i, s: (s[j] * steps + i, 0, 0)),
+                pl.BlockSpec(modes.shape, lambda j, i, s: (0, 0)),
+            ],
+            out_specs=[out_spec, out_spec],
+            scratch_shapes=[
+                pltpu.VMEM((base, ell), jnp.bfloat16),
+                pltpu.VMEM((parts * freqs, 2 * rows, ell), jnp.bfloat16),
+                pltpu.VMEM((STEP_F, 2 * rows, base), jnp.bfloat16),
+            ],
+        ),
+        out_shape=[out, out],
+        compiler_params=pltpu.CompilerParams(vmem_limit_bytes=VMEM_LIMIT),
+        cost_estimate=pl.CostEstimate(
+            flops=4 * parts * freqs * rows * base * ell,
+            bytes_accessed=2 * beam.size + 4 * parts * mine[0].size,
+            transcendentals=0,
+        ),
+    )(where, *mine, *others, beam, modes)
+
+
+def restore_kernel(stay_ref, came_ref, ratio_ref, modes_ref, *outs):
+    n_modes, rows, ell = stay_ref.shape
+    freqs = outs[0].shape[0]
+    for g in range(rows // ROWS):
+        span = slice(g * ROWS, (g + 1) * ROWS)
+        total = stay_ref[:, span, :].astype(jnp.float32) + came_ref[:, span, :].astype(jnp.float32)
+        weighted = (total * ratio_ref[...]).astype(jnp.bfloat16).reshape(n_modes * ROWS, ell)
+        for which, out in enumerate(outs):
+            size = freqs * ROWS
+            value = jnp.dot(
+                modes_ref[which * size:(which + 1) * size, :], weighted, preferred_element_type=jnp.float32
+            )
+            out[:, span, :] = value.astype(jnp.bfloat16).reshape(freqs, ROWS, ell)
+
+
+def restore(stay, came, ratios, modes, parts, freqs):
+    _, rows, ell = stay.shape
+    vmem = pl.BlockSpec(memory_space=pltpu.VMEM)
+    return pl.pallas_call(
+        restore_kernel,
+        in_specs=[vmem] * 4,
+        out_specs=[vmem] * parts,
+        out_shape=[jax.ShapeDtypeStruct((freqs, rows, ell), jnp.bfloat16)] * parts,
+        compiler_params=pltpu.CompilerParams(vmem_limit_bytes=VMEM_LIMIT),
+        cost_estimate=pl.CostEstimate(
+            flops=2 * modes.size * rows // ROWS * ell, bytes_accessed=4 * stay.size, transcendentals=0
+        ),
+    )(stay, came, ratios, modes)
+
+
+def gather_kernel(where, *refs, chunks):
+    pieces, out, sems = refs[:-2], refs[-2], refs[-1]
+    parts = len(pieces) // len(chunks)
+    copies = []
+    for c, (first, rows) in enumerate(chunks):
+        for j in range(parts):
+            n = c * parts + j
+            copies.append(
+                pltpu.make_async_copy(pieces[n], out.at[:, where[j], first:first + rows, :], sems.at[n])
+            )
+    for copy in copies:
+        copy.start()
+    for copy in copies:
+        copy.wait()
+
+
+def gather_pieces(where, pieces, chunks, shape):
+    flat = [piece for group in pieces for piece in group]
+    anywhere = pl.BlockSpec(memory_space=pl.ANY)
+    return pl.pallas_call(
+        functools.partial(gather_kernel, chunks=chunks),
+        grid_spec=pltpu.PrefetchScalarGridSpec(
+            num_scalar_prefetch=1,
+            grid=(),
+            in_specs=[anywhere] * len(flat),
+            out_specs=anywhere,
+            scratch_shapes=[pltpu.SemaphoreType.DMA((len(flat),))],
+        ),
+        out_shape=jax.ShapeDtypeStruct(shape, jnp.bfloat16),
+        cost_estimate=pl.CostEstimate(flops=0, bytes_accessed=4 * len(flat) * flat[0].size, transcendentals=0),
+    )(where, *flat)
+
+
+def chunked(visibility, beam_transfer, tile_mask, first_block, eigen_modes, signal_noise, chunks):
+    freqs, parts, _, base = visibility.shape
+    _, freq_total, _, ell = beam_transfer.shape
+    n_modes = eigen_modes.shape[2]
+    base_tiles, ell_tiles = base // TILE, ell // TILE
+    z, x, p = lax.axis_index("fm"), lax.axis_index("kl"), lax.axis_index("pol")
+    order = jnp.stack([z ^ j for j in range(parts)]).astype(jnp.int32)
+    swaps = [[(i, i ^ j) for i in range(parts)] for j in range(parts)]
+    other = [(0, 1), (1, 0)]
+
+    sends = [
+        [
+            lax.dynamic_slice(
+                visibility, (0, z ^ j, first, 0), (freqs, 1, rows, base)
+            ).reshape(freqs, rows, base)
+            for j in range(parts)
+        ]
+        for first, rows in chunks
+    ]
+    block_ids = x * ell_tiles + jnp.arange(ell_tiles, dtype=jnp.int32)
+    keep = tile_mask[0] * (first_block[0] <= block_ids).astype(jnp.int32)[None, :]
+    where = jnp.concatenate([order, (x == p).astype(jnp.int32)[None], keep.reshape(-1)])
+    near = eigen_modes[0].reshape(parts, freqs, n_modes)[order].reshape(freq_total, n_modes)
+    eye = jnp.eye(ROWS, dtype=jnp.bfloat16)
+    down = (near.T[:, None, :, None] * eye[None, :, None, :]).reshape(n_modes * ROWS, freq_total * ROWS)
+    up = (near[:, None, :, None] * eye[None, :, None, :]).reshape(freq_total * ROWS, n_modes * ROWS)
+    ratio = signal_noise[0] / (1.0 + signal_noise[0])
+    ratios = jnp.broadcast_to(ratio[:, None, None], (n_modes, 1, ell))
+    beam = beam_transfer.reshape(freq_total, base, ell)
+
+    returned = []
+    for send in sends:
+        mine = [send[0]] + [lax.ppermute(send[j], "fm", swaps[j]) for j in range(1, parts)]
+        others = [lax.ppermute(piece, "kl", other) for piece in mine]
+        stay, leave = project(where, mine, others, beam, down, n_modes)
+        came = lax.ppermute(leave, "pol", other)
+        outs = restore(stay, came, ratios, up, parts, freqs)
+        returned.append([outs[0]] + [lax.ppermute(outs[j], "fm", swaps[j]) for j in range(1, parts)])
+    out_rows = sum(rows for _, rows in chunks)
+    return gather_pieces(order, returned, chunks, (freqs, parts, out_rows, ell))
+
+
+def plain(visibility, beam_transfer, tile_mask, first_block, eigen_modes, signal_noise):
+    owned_modes, freq_total, base_half, ell_local = beam_transfer.shape
+    base_tiles, ell_tiles = base_half // TILE, ell_local // TILE
     block_ids = lax.axis_index("kl") * ell_tiles + jnp.arange(ell_tiles, dtype=jnp.int32)
     inside = (first_block[:, None] <= block_ids[None, :]).astype(jnp.int32)
     keep_tiles = tile_mask * inside[:, None, :]
@@ -39,6 +221,24 @@
     return lax.all_to_all(filtered, "fm", split_axis=0, concat_axis=1, tiled=True)
 
 
+def per_device(*args, sizes):
+    visibility, beam_transfer = args[0], args[1]
+    freqs, modes, rows, _ = visibility.shape
+    fits = (
+        sizes["kl"] == 2
+        and sizes["pol"] == 2
+        and modes == sizes["fm"]
+        and modes & (modes - 1) == 0
+        and beam_transfer.shape[0] == 1
+        and rows % ROWS == 0
+        and freqs % STEP_F == 0
+    )
+    if not fits:
+        return plain(*args)
+    chunks = [(first, ROWS) for first in range(0, rows, ROWS)]
+    return chunked(*args, chunks=chunks)
+
+
 def solution(mesh):
     placed = (
         P(("group", "fm"), None, "kl", "pol"),
@@ -49,7 +249,7 @@
         P(("group", "fm"), None),
     )
     return jax.shard_map(
-        per_device,
+        functools.partial(per_device, sizes=dict(mesh.shape)),
         mesh=mesh,
         in_specs=placed,
         out_specs=P(("group", "fm"), None, "pol", "kl"),

time: 173 us -> 190 us (1.098)
  Pallas kernels: 0 us -> 85 us
  blocking collectives: 80.9 us -> 0 us
  starting transfers between devices: 0.04 us -> 40.7 us
  matrix products: 15.2 us -> 0 us
  waiting for transfers between devices: 55.1 us -> 40.9 us
  between operations: 14.1 us -> 0.89 us
  local copies, waits for them, and re-layouts: 4.56 us -> 14.9 us
  other arithmetic: 0.02 us -> 4.55 us
    pallas_call x0 -> x7, Pallas kernels: none -> 85 us  [the longest x1 49.5 us: gather_pieces(): pl.pallas_call(functools.partial(gather_kernel, chunks=chunks), grid_spec...]
    all_to_all x2 -> x0, blocking collectives: 80.9 us -> none  [the longest x1 40.6 us: per_device(): lax.all_to_all(filtered, 'fm', split_axis=0, concat_axis=1, tiled=True)]
    all_gather x1 -> x0, waiting for transfers between devices: 44.4 us -> none  [per_device(): lax.all_gather(arrived, 'kl', axis=2, tiled=True)]
    ppermute x0 -> x33, waiting for transfers between devices: none -> 40.9 us  [the longest x9 24.1 us: chunked(): lax.ppermute(outs[j], 'fm', swaps[j])]
    ppermute x0 -> x33, starting transfers between devices: none -> 40.7 us  [the longest x12 15.5 us: chunked(): others = [lax.ppermute(piece, 'kl', other) for piece in mine]]
    dot_general x3 -> x0, matrix products: 15.2 us -> none  [the longest x1 12.1 us: per_device(): jnp.einsum('fmrb,mfbl->fmrl', lax.all_gather(arrived, 'kl', axis=2, tiled...]
    reduce_scatter x1 -> x0, waiting for transfers between devices: 10.7 us -> none  [per_device(): lax.psum_scatter(partial_value.astype(jnp.bfloat16), 'pol', scatter_dimen...]
    mul x1 -> x4, local copies, waits for them, and re-layouts: 0.2 us -> 10.3 us  [the longest x1 6.14 us: chunked(): near.T[:, None, :, None] * eye[None, :, None, :]]
  transfers between devices with their start and end apart: 2 -> 33, of which waited for: 2 -> 10; matrix products, arithmetic and copies ran while one was open for 0% -> 9% of each run, Pallas kernels for 0% -> 19%
where the time goes in v1:
time: 190 us; the launch traced here: 187 us
  Pallas kernels  85 us (45%)
  waiting for transfers between devices  40.9 us (22%)
  starting transfers between devices  40.7 us (21%)
  local copies, waits for them, and re-layouts  14.9 us (8%)
  other arithmetic  4.55 us (2%)
    pallas_call x1, Pallas kernels, gather_pieces(): pl.pallas_call(functools.partial(gather_kernel, chunks=chunks), grid_spec...  49.5 us
    pallas_call x3, Pallas kernels, project(): pl.pallas_call(functools.partial(project_kernel, parts=parts, freqs=freqs...  34 us
    ppermute x9, waiting for transfers between devices, chunked(): lax.ppermute(outs[j], 'fm', swaps[j])  24.1 us
    ppermute x9, waiting for transfers between devices, chunked(): lax.ppermute(send[j], 'fm', swaps[j])  16.7 us
    ppermute x12, starting transfers between devices, chunked(): others = [lax.ppermute(piece, 'kl', other) for piece in mine]  15.5 us
    ppermute x9, starting transfers between devices, chunked(): lax.ppermute(outs[j], 'fm', swaps[j])  12.8 us
    ppermute x9, starting transfers between devices, chunked(): lax.ppermute(send[j], 'fm', swaps[j])  11.9 us
    mul x1, local copies, waits for them, and re-layouts, chunked(): near.T[:, None, :, None] * eye[None, :, None, :]  6.14 us
  transfers between devices with their start and end apart: 33, of which 10 were waited for; matrix products, arithmetic and copies ran while one was open for 9% of the time, Pallas kernels for 19%

profile of v1, /device:TPU:12, one launch (start us, length us, event | category | flops | bytes accessed | tf_op | source)
XLA Modules:
  0.0 187.0 jit_solution(3423899929613111058)
XLA Ops:
  2.2 2.6 %collective-permute-start.23 = (bf16[8,16,512]{2,1,0:T(8,128)(2,1)S(1)}, bf16[8,16,512]{2,1,0:T(8,128)(2,1)S(1)}, u32[]{:S(2)}, u32[]{:S(2)}) collective-permute-start(bf16[8,16,512]{2,1,0:T(8,128)(2,1)S(1)} %get-tuple-element.52), channel_id=1, source_target_pairs={{0,8},{4,12},{8,0},{12,4},{1,9},{5,13},{9,1},{13,5},{2,10},{6,14},... | collective-permute-start | bytes 393224 | tf_op jit(solution)/shard_map/ppermute | solution.py:185
  8.1 3.1 %collective-permute-start.12 = (bf16[8,16,512]{2,1,0:T(8,128)(2,1)S(1)}, bf16[8,16,512]{2,1,0:T(8,128)(2,1)S(1)}, u32[]{:S(2)}, u32[]{:S(2)}) collective-permute-start(bf16[8,16,512]{2,1,0:T(8,128)(2,1)S(1)} %get-tuple-element.45), channel_id=1, source_target_pairs={{0,8},{4,12},{8,0},{12,4},{1,9},{5,13},{9,1},{13,5},{2,10},{6,14},... | collective-permute-start | bytes 393224 | tf_op jit(solution)/shard_map/ppermute | solution.py:185
  11.2 3.2 %collective-permute-done.23.refs_2_ = bf16[8,16,512]{2,1,0:T(8,128)(2,1)S(1)} collective-permute-done((bf16[8,16,512]{2,1,0:T(8,128)(2,1)S(1)}, bf16[8,16,512]{2,1,0:T(8,128)(2,1)S(1)}, u32[]{:S(2)}, u32[]{:S(2)}) %collective-permute-start.23) | collective-permute-done | bytes 131104 | tf_op jit(solution)/shard_map/ppermute | solution.py:185
  14.8 10.3 %collective-permute-done.24.refs_3_ = bf16[8,16,512]{2,1,0:T(8,128)(2,1)S(1)} collective-permute-done((bf16[8,16,512]{2,1,0:T(8,128)(2,1)S(1)}, bf16[8,16,512]{2,1,0:T(8,128)(2,1)S(1)}, u32[]{:S(2)}, u32[]{:S(2)}) %collective-permute-start.24) | collective-permute-done | bytes 131104 | tf_op jit(solution)/shard_map/ppermute | solution.py:185
  26.6 2.9 %collective-permute-start.1 = (bf16[8,16,512]{2,1,0:T(8,128)(2,1)S(1)}, bf16[8,16,512]{2,1,0:T(8,128)(2,1)S(1)}, u32[]{:S(2)}, u32[]{:S(2)}) collective-permute-start(bf16[8,16,512]{2,1,0:T(8,128)(2,1)S(1)} %get-tuple-element.49), channel_id=1, source_target_pairs={{0,8},{4,12},{8,0},{12,4},{1,9},{5,13},{9,1},{13,5},{2,10},{6,14},... | collective-permute-start | bytes 393224 | tf_op jit(solution)/shard_map/ppermute | solution.py:185
  40.6 1.9 %broadcast_multiply_fusion.1 = bf16[24,16,32,16]{3,2,1,0:T(8,128)(2,1)} fusion(bf16[16,16]{1,0:T(8,128)(2,1)S(1)} %fusion, bf16[24,32]{1,0:T(8,128)(2,1)S(1)} %copy.9), kind=kLoop, calls=%fused_computation.2 | loop fusion | flops 196608 | bytes 395264 | tf_op jit(solution)/shard_map/mul | solution.py:177
  47.3 1.9 %collective-permute-start.6 = (bf16[8,16,512]{2,1,0:T(8,128)(2,1)S(1)}, bf16[8,16,512]{2,1,0:T(8,128)(2,1)}, u32[]{:S(2)}, u32[]{:S(2)}) collective-permute-start(bf16[8,16,512]{2,1,0:T(8,128)(2,1)S(1)} %collective-permute-done.2.refs_3_), channel_id=1, source_target_pairs={{0,2},{2,0},{1,3},{3,1},{4,6},{6,4},{5,7},{7,5},{8,10},{10,8},{9,1... | collective-permute-start | bytes 393224 | tf_op jit(solution)/shard_map/ppermute | solution.py:186
  50.0 6.1 %mul.55.refs_9_ = bf16[384,512]{1,0:T(8,128)(2,1)S(1)} reshape(bf16[24,16,32,16]{3,2,1,0:T(8,128)(2,1)} %broadcast_multiply_fusion.1) | data formatting | bytes 786432 | tf_op jit(solution)/shard_map/mul | solution.py:177
  56.3 11.3 %shard_map.68 = (bf16[24,16,512]{2,1,0:T(8,128)(2,1)S(1)}, bf16[24,16,512]{2,1,0:T(8,128)(2,1)}) custom-call(s32[21]{0:T(128)S(1)} %concatenate.23.where, bf16[8,16,512]{2,1,0:T(8,128)(2,1)S(1)} %get-tuple-element.43.refs_0_, bf16[8,16,512]{2,1,0:T(8,128)(2,1)S(1)} %collective-permute-done.22.refs_1_, ...), custom_call_target="tpu_custom_call" | custom-call | flops 536870912 | bytes 17825792 | tf_op jit(solution)/shard_map/pallas_call | solution.py:63
  67.6 11.3 %shard_map.66 = (bf16[24,16,512]{2,1,0:T(8,128)(2,1)S(1)}, bf16[24,16,512]{2,1,0:T(8,128)(2,1)}) custom-call(s32[21]{0:T(128)S(1)} %concatenate.23.where, bf16[8,16,512]{2,1,0:T(8,128)(2,1)S(1)} %get-tuple-element.47.refs_0_, bf16[8,16,512]{2,1,0:T(8,128)(2,1)S(1)} %collective-permute-done.11.refs_1_, ...), custom_call_target="tpu_custom_call" | custom-call | flops 536870912 | bytes 17825792 | tf_op jit(solution)/shard_map/pallas_call | solution.py:63
  79.5 11.4 %shard_map.64 = (bf16[24,16,512]{2,1,0:T(8,128)(2,1)S(1)}, bf16[24,16,512]{2,1,0:T(8,128)(2,1)}) custom-call(s32[21]{0:T(128)S(1)} %concatenate.23.where, bf16[8,16,512]{2,1,0:T(8,128)(2,1)S(1)} %get-tuple-element.51.refs_0_, bf16[8,16,512]{2,1,0:T(8,128)(2,1)S(1)} %collective-permute-done.refs_1_, bf16[8,16,512]{2,1,0:T(8,128)(2,1)S(1)} %collective-permute-done.1.refs_2_, ...), custom_call_target="tpu_custom_call" | custom-call | flops 536870912 | bytes 17825792 | tf_op jit(solution)/shard_map/pallas_call | solution.py:63
  90.8 1.9 %broadcast_multiply_fusion = bf16[32,16,24,16]{3,2,1,0:T(8,128)(2,1)} fusion(bf16[16,16]{1,0:T(8,128)(2,1)S(1)} %fusion, bf16[32,24]{1,0:T(8,128)(2,1)S(1)} %bitcast.52), kind=kLoop, calls=%fused_computation.1 | loop fusion | flops 196608 | bytes 395264 | tf_op jit(solution)/shard_map/mul | solution.py:178
  92.7 4.1 %mul.59.modes_ref = bf16[512,384]{1,0:T(8,128)(2,1)S(1)} reshape(bf16[32,16,24,16]{3,2,1,0:T(8,128)(2,1)} %broadcast_multiply_fusion) | data formatting | bytes 786432 | tf_op jit(solution)/shard_map/mul | solution.py:178
  97.4 2.6 %collective-permute-start.30 = (bf16[8,16,512]{2,1,0:T(8,128)(2,1)S(1)}, bf16[8,16,512]{2,1,0:T(8,128)(2,1)S(1)}, u32[]{:S(2)}, u32[]{:S(2)}) collective-permute-start(bf16[8,16,512]{2,1,0:T(8,128)(2,1)S(1)} %get-tuple-element.38), channel_id=1, source_target_pairs={{0,4},{4,0},{8,12},{12,8},{1,5},{5,1},{9,13},{13,9},{2,6},{6,2},{1... | collective-permute-start | bytes 393224 | tf_op jit(solution)/shard_map/ppermute | solution.py:190
  100.0 2.8 %collective-permute-start.31 = (bf16[8,16,512]{2,1,0:T(8,128)(2,1)S(1)}, bf16[8,16,512]{2,1,0:T(8,128)(2,1)S(1)}, u32[]{:S(2)}, u32[]{:S(2)}) collective-permute-start(bf16[8,16,512]{2,1,0:T(8,128)(2,1)S(1)} %get-tuple-element.39), channel_id=1, source_target_pairs={{0,8},{4,12},{8,0},{12,4},{1,9},{5,13},{9,1},{13,5},{2,10},{6,14},... | collective-permute-start | bytes 393224 | tf_op jit(solution)/shard_map/ppermute | solution.py:190
  103.3 1.7 collective-permute-start.19
  105.0 1.9 %collective-permute-start.20 = (bf16[8,16,512]{2,1,0:T(8,128)(2,1)S(1)}, bf16[8,16,512]{2,1,0:T(8,128)(2,1)S(1)}, u32[]{:S(2)}, u32[]{:S(2)}) collective-permute-start(bf16[8,16,512]{2,1,0:T(8,128)(2,1)S(1)} %get-tuple-element.33), channel_id=1, source_target_pairs={{0,8},{4,12},{8,0},{12,4},{1,9},{5,13},{9,1},{13,5},{2,10},{6,14},... | collective-permute-start | bytes 393224 | tf_op jit(solution)/shard_map/ppermute | solution.py:190
  108.0 3.5 %collective-permute-done.31.refs_10_ = bf16[8,16,512]{2,1,0:T(8,128)(2,1)S(1)} collective-permute-done((bf16[8,16,512]{2,1,0:T(8,128)(2,1)S(1)}, bf16[8,16,512]{2,1,0:T(8,128)(2,1)S(1)}, u32[]{:S(2)}, u32[]{:S(2)}) %collective-permute-start.31) | collective-permute-done | bytes 131104 | tf_op jit(solution)/shard_map/ppermute | solution.py:190
  111.6 11.4 %collective-permute-done.32.refs_11_ = bf16[8,16,512]{2,1,0:T(8,128)(2,1)S(1)} collective-permute-done((bf16[8,16,512]{2,1,0:T(8,128)(2,1)S(1)}, bf16[8,16,512]{2,1,0:T(8,128)(2,1)S(1)}, u32[]{:S(2)}, u32[]{:S(2)}) %collective-permute-start.32) | collective-permute-done | bytes 131104 | tf_op jit(solution)/shard_map/ppermute | solution.py:190
  123.0 3.9 %collective-permute-start.9 = (bf16[8,16,512]{2,1,0:T(8,128)(2,1)S(1)}, bf16[8,16,512]{2,1,0:T(8,128)(2,1)S(1)}, u32[]{:S(2)}, u32[]{:S(2)}) collective-permute-start(bf16[8,16,512]{2,1,0:T(8,128)(2,1)S(1)} %get-tuple-element.27), channel_id=1, source_target_pairs={{0,8},{4,12},{8,0},{12,4},{1,9},{5,13},{9,1},{13,5},{2,10},{6,14},... | collective-permute-start | bytes 393224 | tf_op jit(solution)/shard_map/ppermute | solution.py:190
  127.6 3.8 %collective-permute-done.21.refs_7_ = bf16[8,16,512]{2,1,0:T(8,128)(2,1)S(1)} collective-permute-done((bf16[8,16,512]{2,1,0:T(8,128)(2,1)S(1)}, bf16[8,16,512]{2,1,0:T(8,128)(2,1)S(1)}, u32[]{:S(2)}, u32[]{:S(2)}) %collective-permute-start.21) | collective-permute-done | bytes 131104 | tf_op jit(solution)/shard_map/ppermute | solution.py:190
  131.4 3.0 %collective-permute-done.10.refs_3_ = bf16[8,16,512]{2,1,0:T(8,128)(2,1)S(1)} collective-permute-done((bf16[8,16,512]{2,1,0:T(8,128)(2,1)S(1)}, bf16[8,16,512]{2,1,0:T(8,128)(2,1)S(1)}, u32[]{:S(2)}, u32[]{:S(2)}) %collective-permute-start.10) | collective-permute-done | bytes 131104 | tf_op jit(solution)/shard_map/ppermute | solution.py:190
  134.4 2.4 %collective-permute-done.9.refs_2_ = bf16[8,16,512]{2,1,0:T(8,128)(2,1)S(1)} collective-permute-done((bf16[8,16,512]{2,1,0:T(8,128)(2,1)S(1)}, bf16[8,16,512]{2,1,0:T(8,128)(2,1)S(1)}, u32[]{:S(2)}, u32[]{:S(2)}) %collective-permute-start.9) | collective-permute-done | bytes 131104 | tf_op jit(solution)/shard_map/ppermute | solution.py:190
  137.4 49.5 %shard_map.70 = bf16[8,4,48,512]{3,2,1,0:T(8,128)(2,1)} custom-call(s32[4]{0:T(128)} %pad_add_fusion.where, bf16[8,16,512]{2,1,0:T(8,128)(2,1)} %copy-done.2, bf16[8,16,512]{2,1,0:T(8,128)(2,1)} %copy-done.10, bf16[8,16,512]{2,1,0:T(8,128)(2,1)} %copy-done.11, bf16[8,16,512]{2,1,0:T(8,128)(2,1)} %copy-done.9, bf16[8,16,512]{2,1,0:T(8,128)(2,1)} %copy-done.1, ...), custom_call_target="tpu_custom_call" | custom-call | bytes 3145728 | tf_op jit(solution)/shard_map/pallas_call | solution.py:139
  (97 shorter events, 27.7 us)
Async XLA Ops:
  2.2 12.2 %collective-permute-start.23 = (bf16[8,16,512]{2,1,0:T(8,128)(2,1)S(1)}, bf16[8,16,512]{2,1,0:T(8,128)(2,1)S(1)}, u32[]{:S(2)}, u32[]{:S(2)}) collective-permute-start(bf16[8,16,512]{2,1,0:T(8,128)(2,1)S(1)} %get-tuple-element.52), channel_id=1, source_target_pairs={{0,8},{4,12},{8,0},{12,4},{1,9},{5,13},{9,1},{13,5},{2,10},{6,14},... | collective-permute-start | bytes 393224 | tf_op jit(solution)/shard_map/ppermute | solution.py:185
  4.8 20.3 %collective-permute-start.24 = (bf16[8,16,512]{2,1,0:T(8,128)(2,1)S(1)}, bf16[8,16,512]{2,1,0:T(8,128)(2,1)S(1)}, u32[]{:S(2)}, u32[]{:S(2)}) collective-permute-start(bf16[8,16,512]{2,1,0:T(8,128)(2,1)S(1)} %get-tuple-element.41), channel_id=1, source_target_pairs={{0,12},{4,8},{8,4},{12,0},{1,13},{5,9},{9,5},{13,1},{2,14},{6,10},... | collective-permute-start | bytes 393224 | tf_op jit(solution)/shard_map/ppermute | solution.py:185
  5.2 21.3 %collective-permute-start.25 = (bf16[8,16,512]{2,1,0:T(8,128)(2,1)S(1)}, bf16[8,16,512]{2,1,0:T(8,128)(2,1)S(1)}, u32[]{:S(2)}, u32[]{:S(2)}) collective-permute-start(bf16[8,16,512]{2,1,0:T(8,128)(2,1)S(1)} %get-tuple-element.43.refs_0_), channel_id=1, source_target_pairs={{0,2},{2,0},{1,3},{3,1},{4,6},{6,4},{5,7},{7,5},{8,10},{10,8},{9,1... | collective-permute-start | bytes 393224 | tf_op jit(solution)/shard_map/ppermute | solution.py:186
  6.7 19.9 %collective-permute-start.11 = (bf16[8,16,512]{2,1,0:T(8,128)(2,1)S(1)}, bf16[8,16,512]{2,1,0:T(8,128)(2,1)S(1)}, u32[]{:S(2)}, u32[]{:S(2)}) collective-permute-start(bf16[8,16,512]{2,1,0:T(8,128)(2,1)S(1)} %get-tuple-element.46), channel_id=1, source_target_pairs={{0,4},{4,0},{8,12},{12,8},{1,5},{5,1},{9,13},{13,9},{2,6},{6,2},{1... | collective-permute-start | bytes 393224 | tf_op jit(solution)/shard_map/ppermute | solution.py:185
  8.1 21.4 %collective-permute-start.12 = (bf16[8,16,512]{2,1,0:T(8,128)(2,1)S(1)}, bf16[8,16,512]{2,1,0:T(8,128)(2,1)S(1)}, u32[]{:S(2)}, u32[]{:S(2)}) collective-permute-start(bf16[8,16,512]{2,1,0:T(8,128)(2,1)S(1)} %get-tuple-element.45), channel_id=1, source_target_pairs={{0,8},{4,12},{8,0},{12,4},{1,9},{5,13},{9,1},{13,5},{2,10},{6,14},... | collective-permute-start | bytes 393224 | tf_op jit(solution)/shard_map/ppermute | solution.py:185
  14.4 17.7 %collective-permute-start.13 = (bf16[8,16,512]{2,1,0:T(8,128)(2,1)S(1)}, bf16[8,16,512]{2,1,0:T(8,128)(2,1)S(1)}, u32[]{:S(2)}, u32[]{:S(2)}) collective-permute-start(bf16[8,16,512]{2,1,0:T(8,128)(2,1)S(1)} %get-tuple-element.44), channel_id=1, source_target_pairs={{0,12},{4,8},{8,4},{12,0},{1,13},{5,9},{9,5},{13,1},{2,14},{6,10},... | collective-permute-start | bytes 393224 | tf_op jit(solution)/shard_map/ppermute | solution.py:185
  32.1 11.1 %collective-permute-start.26 = (bf16[8,16,512]{2,1,0:T(8,128)(2,1)S(1)}, bf16[8,16,512]{2,1,0:T(8,128)(2,1)S(1)}, u32[]{:S(2)}, u32[]{:S(2)}) collective-permute-start(bf16[8,16,512]{2,1,0:T(8,128)(2,1)S(1)} %collective-permute-done.22.refs_1_), channel_id=1, source_target_pairs={{0,2},{2,0},{1,3},{3,1},{4,6},{6,4},{5,7},{7,5},{8,10},{10,8},{9,1... | collective-permute-start | bytes 393224 | tf_op jit(solution)/shard_map/ppermute | solution.py:186
  34.1 11.1 %collective-permute-start.28 = (bf16[8,16,512]{2,1,0:T(8,128)(2,1)S(1)}, bf16[8,16,512]{2,1,0:T(8,128)(2,1)S(1)}, u32[]{:S(2)}, u32[]{:S(2)}) collective-permute-start(bf16[8,16,512]{2,1,0:T(8,128)(2,1)S(1)} %collective-permute-done.24.refs_3_), channel_id=1, source_target_pairs={{0,2},{2,0},{1,3},{3,1},{4,6},{6,4},{5,7},{7,5},{8,10},{10,8},{9,1... | collective-permute-start | bytes 393224 | tf_op jit(solution)/shard_map/ppermute | solution.py:186
  43.1 35.8 %collective-permute-start.3 = (bf16[8,16,512]{2,1,0:T(8,128)(2,1)S(1)}, bf16[8,16,512]{2,1,0:T(8,128)(2,1)S(1)}, u32[]{:S(2)}, u32[]{:S(2)}) collective-permute-start(bf16[8,16,512]{2,1,0:T(8,128)(2,1)S(1)} %get-tuple-element.51.refs_0_), channel_id=1, source_target_pairs={{0,2},{2,0},{1,3},{3,1},{4,6},{6,4},{5,7},{7,5},{8,10},{10,8},{9,1... | collective-permute-start | bytes 393224 | tf_op jit(solution)/shard_map/ppermute | solution.py:186
  43.7 23.9 %collective-permute-start.17 = (bf16[8,16,512]{2,1,0:T(8,128)(2,1)S(1)}, bf16[8,16,512]{2,1,0:T(8,128)(2,1)}, u32[]{:S(2)}, u32[]{:S(2)}) collective-permute-start(bf16[8,16,512]{2,1,0:T(8,128)(2,1)S(1)} %collective-permute-done.13.refs_3_), channel_id=1, source_target_pairs={{0,2},{2,0},{1,3},{3,1},{4,6},{6,4},{5,7},{7,5},{8,10},{10,8},{9,1... | collective-permute-start | bytes 393224 | tf_op jit(solution)/shard_map/ppermute | solution.py:186
  45.2 34.2 %collective-permute-start.4 = (bf16[8,16,512]{2,1,0:T(8,128)(2,1)S(1)}, bf16[8,16,512]{2,1,0:T(8,128)(2,1)S(1)}, u32[]{:S(2)}, u32[]{:S(2)}) collective-permute-start(bf16[8,16,512]{2,1,0:T(8,128)(2,1)S(1)} %collective-permute-done.refs_1_), channel_id=1, source_target_pairs={{0,2},{2,0},{1,3},{3,1},{4,6},{6,4},{5,7},{7,5},{8,10},{10,8},{9,1... | collective-permute-start | bytes 393224 | tf_op jit(solution)/shard_map/ppermute | solution.py:186
  45.8 33.7 %collective-permute-start.5 = (bf16[8,16,512]{2,1,0:T(8,128)(2,1)S(1)}, bf16[8,16,512]{2,1,0:T(8,128)(2,1)}, u32[]{:S(2)}, u32[]{:S(2)}) collective-permute-start(bf16[8,16,512]{2,1,0:T(8,128)(2,1)S(1)} %collective-permute-done.1.refs_2_), channel_id=1, source_target_pairs={{0,2},{2,0},{1,3},{3,1},{4,6},{6,4},{5,7},{7,5},{8,10},{10,8},{9,1... | collective-permute-start | bytes 393224 | tf_op jit(solution)/shard_map/ppermute | solution.py:186
  47.3 32.2 %collective-permute-start.6 = (bf16[8,16,512]{2,1,0:T(8,128)(2,1)S(1)}, bf16[8,16,512]{2,1,0:T(8,128)(2,1)}, u32[]{:S(2)}, u32[]{:S(2)}) collective-permute-start(bf16[8,16,512]{2,1,0:T(8,128)(2,1)S(1)} %collective-permute-done.2.refs_3_), channel_id=1, source_target_pairs={{0,2},{2,0},{1,3},{3,1},{4,6},{6,4},{5,7},{7,5},{8,10},{10,8},{9,1... | collective-permute-start | bytes 393224 | tf_op jit(solution)/shard_map/ppermute | solution.py:186
  67.6 29.2 %collective-permute-start.29 = (bf16[24,16,512]{2,1,0:T(8,128)(2,1)}, bf16[24,16,512]{2,1,0:T(8,128)(2,1)S(1)}, u32[]{:S(2)}, u32[]{:S(2)}) collective-permute-start(bf16[24,16,512]{2,1,0:T(8,128)(2,1)} %get-tuple-element.36), channel_id=1, source_target_pairs={{0,1},{1,0},{2,3},{3,2},{4,5},{5,4},{6,7},{7,6},{8,9},{9,8},{10,11... | collective-permute-start | bytes 1179656 | tf_op jit(solution)/shard_map/ppermute | solution.py:188
  78.9 23.9 %collective-permute-start.18 = (bf16[24,16,512]{2,1,0:T(8,128)(2,1)}, bf16[24,16,512]{2,1,0:T(8,128)(2,1)S(1)}, u32[]{:S(2)}, u32[]{:S(2)}) collective-permute-start(bf16[24,16,512]{2,1,0:T(8,128)(2,1)} %get-tuple-element.30), channel_id=1, source_target_pairs={{0,1},{1,0},{2,3},{3,2},{4,5},{5,4},{6,7},{7,6},{8,9},{9,8},{10,11... | collective-permute-start | bytes 1179656 | tf_op jit(solution)/shard_map/ppermute | solution.py:188
  90.8 14.2 %collective-permute-start.7 = (bf16[24,16,512]{2,1,0:T(8,128)(2,1)}, bf16[24,16,512]{2,1,0:T(8,128)(2,1)S(1)}, u32[]{:S(2)}, u32[]{:S(2)}) collective-permute-start(bf16[24,16,512]{2,1,0:T(8,128)(2,1)} %get-tuple-element.24), channel_id=1, source_target_pairs={{0,1},{1,0},{2,3},{3,2},{4,5},{5,4},{6,7},{7,6},{8,9},{9,8},{10,11... | collective-permute-start | bytes 1179656 | tf_op jit(solution)/shard_map/ppermute | solution.py:188
  100.0 11.6 %collective-permute-start.31 = (bf16[8,16,512]{2,1,0:T(8,128)(2,1)S(1)}, bf16[8,16,512]{2,1,0:T(8,128)(2,1)S(1)}, u32[]{:S(2)}, u32[]{:S(2)}) collective-permute-start(bf16[8,16,512]{2,1,0:T(8,128)(2,1)S(1)} %get-tuple-element.39), channel_id=1, source_target_pairs={{0,8},{4,12},{8,0},{12,4},{1,9},{5,13},{9,1},{13,5},{2,10},{6,14},... | collective-permute-start | bytes 393224 | tf_op jit(solution)/shard_map/ppermute | solution.py:190
  102.8 20.2 %collective-permute-start.32 = (bf16[8,16,512]{2,1,0:T(8,128)(2,1)S(1)}, bf16[8,16,512]{2,1,0:T(8,128)(2,1)S(1)}, u32[]{:S(2)}, u32[]{:S(2)}) collective-permute-start(bf16[8,16,512]{2,1,0:T(8,128)(2,1)S(1)} %get-tuple-element.40), channel_id=1, source_target_pairs={{0,12},{4,8},{8,4},{12,0},{1,13},{5,9},{9,5},{13,1},{2,14},{6,10},... | collective-permute-start | bytes 393224 | tf_op jit(solution)/shard_map/ppermute | solution.py:190
  103.3 19.6 %collective-permute-start.19 = (bf16[8,16,512]{2,1,0:T(8,128)(2,1)S(1)}, bf16[8,16,512]{2,1,0:T(8,128)(2,1)S(1)}, u32[]{:S(2)}, u32[]{:S(2)}) collective-permute-start(bf16[8,16,512]{2,1,0:T(8,128)(2,1)S(1)} %get-tuple-element.32), channel_id=1, source_target_pairs={{0,4},{4,0},{8,12},{12,8},{1,5},{5,1},{9,13},{13,9},{2,6},{6,2},{1... | collective-permute-start | bytes 393224 | tf_op jit(solution)/shard_map/ppermute | solution.py:190
  105.0 22.6 %collective-permute-start.20 = (bf16[8,16,512]{2,1,0:T(8,128)(2,1)S(1)}, bf16[8,16,512]{2,1,0:T(8,128)(2,1)S(1)}, u32[]{:S(2)}, u32[]{:S(2)}) collective-permute-start(bf16[8,16,512]{2,1,0:T(8,128)(2,1)S(1)} %get-tuple-element.33), channel_id=1, source_target_pairs={{0,8},{4,12},{8,0},{12,4},{1,9},{5,13},{9,1},{13,5},{2,10},{6,14},... | collective-permute-start | bytes 393224 | tf_op jit(solution)/shard_map/ppermute | solution.py:190
  108.0 23.3 %collective-permute-start.21 = (bf16[8,16,512]{2,1,0:T(8,128)(2,1)S(1)}, bf16[8,16,512]{2,1,0:T(8,128)(2,1)S(1)}, u32[]{:S(2)}, u32[]{:S(2)}) collective-permute-start(bf16[8,16,512]{2,1,0:T(8,128)(2,1)S(1)} %get-tuple-element.34), channel_id=1, source_target_pairs={{0,12},{4,8},{8,4},{12,0},{1,13},{5,9},{9,5},{13,1},{2,14},{6,10},... | collective-permute-start | bytes 393224 | tf_op jit(solution)/shard_map/ppermute | solution.py:190
  111.6 22.8 %collective-permute-start.10 = (bf16[8,16,512]{2,1,0:T(8,128)(2,1)S(1)}, bf16[8,16,512]{2,1,0:T(8,128)(2,1)S(1)}, u32[]{:S(2)}, u32[]{:S(2)}) collective-permute-start(bf16[8,16,512]{2,1,0:T(8,128)(2,1)S(1)} %get-tuple-element.28), channel_id=1, source_target_pairs={{0,12},{4,8},{8,4},{12,0},{1,13},{5,9},{9,5},{13,1},{2,14},{6,10},... | collective-permute-start | bytes 393224 | tf_op jit(solution)/shard_map/ppermute | solution.py:190
  123.0 11.5 %collective-permute-start.8 = (bf16[8,16,512]{2,1,0:T(8,128)(2,1)S(1)}, bf16[8,16,512]{2,1,0:T(8,128)(2,1)S(1)}, u32[]{:S(2)}, u32[]{:S(2)}) collective-permute-start(bf16[8,16,512]{2,1,0:T(8,128)(2,1)S(1)} %get-tuple-element.26), channel_id=1, source_target_pairs={{0,4},{4,0},{8,12},{12,8},{1,5},{5,1},{9,13},{13,9},{2,6},{6,2},{1... | collective-permute-start | bytes 393224 | tf_op jit(solution)/shard_map/ppermute | solution.py:190
  123.0 13.8 %collective-permute-start.9 = (bf16[8,16,512]{2,1,0:T(8,128)(2,1)S(1)}, bf16[8,16,512]{2,1,0:T(8,128)(2,1)S(1)}, u32[]{:S(2)}, u32[]{:S(2)}) collective-permute-start(bf16[8,16,512]{2,1,0:T(8,128)(2,1)S(1)} %get-tuple-element.27), channel_id=1, source_target_pairs={{0,8},{4,12},{8,0},{12,4},{1,9},{5,13},{9,1},{13,5},{2,10},{6,14},... | collective-permute-start | bytes 393224 | tf_op jit(solution)/shard_map/ppermute | solution.py:190
  (23 other events, 291.8 us)

commit v2 on v1

v2 whole, which is shorter than its diff:
```python
import functools
import jax
import jax.numpy as jnp
from jax import lax
from jax.experimental import pallas as pl
from jax.experimental.pallas import tpu as pltpu
from jax.sharding import PartitionSpec as P

TILE = 128
WIDE = 256
ROWS = 16
STEP_F = 4
VMEM_LIMIT = 40 * 1024 * 1024


def after(value, *earlier):
    return lax.optimization_barrier((value, earlier))[0]


def spread_kernel(modes_ref, down_ref, up_ref):
    freq, n_modes = modes_ref.shape
    modes = modes_ref[...]

    def pick(shape, axis):
        big = lax.broadcasted_iota(jnp.int32, shape, axis) // ROWS
        small = lax.broadcasted_iota(jnp.int32, shape, 1 - axis)
        return jnp.where(big == small, 1.0, 0.0).astype(jnp.bfloat16)

    def lane(shape):
        rows = lax.broadcasted_iota(jnp.int32, shape, 0) % ROWS
        columns = lax.broadcasted_iota(jnp.int32, shape, 1) % ROWS
        return rows == columns

    def dot(a, b, dims):
        return lax.dot_general(a, b, (dims, ((), ())), preferred_element_type=jnp.float32)

    tall = dot(pick((n_modes * ROWS, n_modes), 0), modes, ((1,), (1,))).astype(jnp.bfloat16)
    value = dot(tall, pick((freq, freq * ROWS), 1), ((1,), (0,)))
    down_ref[...] = jnp.where(lane(value.shape), value, 0.0).astype(jnp.bfloat16)
    tall = dot(pick((freq * ROWS, freq), 0), modes, ((1,), (0,))).astype(jnp.bfloat16)
    value = dot(tall, pick((n_modes, n_modes * ROWS), 1), ((1,), (0,)))
    up_ref[...] = jnp.where(lane(value.shape), value, 0.0).astype(jnp.bfloat16)


def spread(modes):
    freq, n_modes = modes.shape
    vmem = pl.BlockSpec(memory_space=pltpu.VMEM)
    return pl.pallas_call(
        spread_kernel,
        in_specs=[vmem],
        out_specs=[vmem, vmem],
        out_shape=[
            jax.ShapeDtypeStruct((n_modes * ROWS, freq * ROWS), jnp.bfloat16),
            jax.ShapeDtypeStruct((freq * ROWS, n_modes * ROWS), jnp.bfloat16),
        ],
        compiler_params=pltpu.CompilerParams(vmem_limit_bytes=VMEM_LIMIT),
        cost_estimate=pl.CostEstimate(
            flops=2 * 256 * n_modes * freq * freq, bytes_accessed=4 * 256 * n_modes * freq, transcendentals=0
        ),
    )(modes)


def project_kernel(where, *refs, parts, freqs, rows):
    mine, others = refs[:parts], refs[parts:2 * parts]
    beam_ref, modes_ref, stay_ref, leave_ref, mask, sky, lines = refs[2 * parts:]
    piece, step = pl.program_id(0), pl.program_id(1)
    ell_tiles, _, base = mask.shape
    base_tiles, both = base // TILE, 2 * rows

    @pl.when((piece == 0) & (step == 0))
    def _():
        for b in range(base_tiles):
            for l in range(ell_tiles):
                kept = where[parts + 1 + b * ell_tiles + l].astype(jnp.float32)
                mask[l, :, b * TILE:(b + 1) * TILE] = jnp.full((ROWS, TILE), kept, jnp.float32).astype(jnp.bfloat16)

    for which in range(parts):

        @pl.when(piece == which)
        def _():
            for u in range(STEP_F):
                for start in range(0, both, ROWS):
                    from_ref, row = (mine[which], start) if start < rows else (others[which], start - rows)
                    value = from_ref[u, row:row + ROWS, :]
                    for l in range(ell_tiles):
                        lines[u, l, start:start + ROWS, :] = value * mask[l]

    first = where[piece] * freqs + step * STEP_F
    per = WIDE // TILE
    for u in range(STEP_F):
        for n in range(ell_tiles // per):
            value = jnp.dot(
                lines[u, n * per:(n + 1) * per].reshape(per * both, base),
                beam_ref[u, :, n * WIDE:(n + 1) * WIDE],
                preferred_element_type=jnp.float32,
            )
            for k in range(per):
                at = n * WIDE + k * TILE
                sky[first + u, :, at:at + TILE] = value[
                    k * both:(k + 1) * both, k * TILE:(k + 1) * TILE
                ].astype(jnp.bfloat16)

    @pl.when((piece == parts - 1) & (step == freqs // STEP_F - 1))
    def _():
        own = where[parts]
        for ref, low in ((stay_ref, (1 - own) * rows), (leave_ref, own * rows)):
            for g in range(rows // ROWS):
                start = pl.multiple_of(low + g * ROWS, ROWS)
                block = sky[:, pl.ds(start, ROWS), :].reshape(sky.shape[0] * ROWS, sky.shape[2])
                value = jnp.dot(modes_ref[...], block, preferred_element_type=jnp.float32)
                ref[:, g * ROWS:(g + 1) * ROWS, :] = value.astype(jnp.bfloat16).reshape(
                    ref.shape[0], ROWS, ref.shape[2]
                )


def project(where, mine, others, beam, modes, n_modes):
    parts = len(mine)
    freqs, rows, base = mine[0].shape
    ell = beam.shape[2]
    steps = freqs // STEP_F

    def block_of(which):
        def index(j, i, s):
            return (jnp.where(j == which, i, jnp.where(j < which, 0, steps - 1)), 0, 0)

        return pl.BlockSpec((STEP_F, rows, base), index)

    out = jax.ShapeDtypeStruct((n_modes, rows, ell), jnp.bfloat16)
    out_spec = pl.BlockSpec((n_modes, rows, ell), lambda j, i, s: (0, 0, 0))
    return pl.pallas_call(
        functools.partial(project_kernel, parts=parts, freqs=freqs, rows=rows),
        grid_spec=pltpu.PrefetchScalarGridSpec(
            num_scalar_prefetch=1,
            grid=(parts, steps),
            in_specs=[block_of(j) for j in range(parts)] * 2
            + [
                pl.BlockSpec((STEP_F, base, ell), lambda j, i, s: (s[j] * steps + i, 0, 0)),
                pl.BlockSpec(modes.shape, lambda j, i, s: (0, 0)),
            ],
            out_specs=[out_spec, out_spec],
            scratch_shapes=[
                pltpu.VMEM((ell // TILE, ROWS, base), jnp.bfloat16),
                pltpu.VMEM((parts * freqs, 2 * rows, ell), jnp.bfloat16),
                pltpu.VMEM((STEP_F, ell // TILE, 2 * rows, base), jnp.bfloat16),
            ],
        ),
        out_shape=[out, out],
        compiler_params=pltpu.CompilerParams(vmem_limit_bytes=VMEM_LIMIT),
        cost_estimate=pl.CostEstimate(
            flops=4 * parts * freqs * rows * base * ell,
            bytes_accessed=2 * beam.size + 4 * parts * mine[0].size,
            transcendentals=0,
        ),
    )(where, *mine, *others, beam, modes)


def restore_kernel(where, stay_ref, came_ref, ratio_ref, modes_ref, *outs):
    n_modes, rows, ell = stay_ref.shape
    size = outs[0].shape[0] * ROWS
    for g in range(rows // ROWS):
        span = slice(g * ROWS, (g + 1) * ROWS)
        total = stay_ref[:, span, :].astype(jnp.float32) + came_ref[:, span, :].astype(jnp.float32)
        weighted = (total * ratio_ref[...]).astype(jnp.bfloat16).reshape(n_modes * ROWS, ell)
        for which, out in enumerate(outs):
            start = pl.multiple_of(where[which] * size, size)
            value = jnp.dot(modes_ref[pl.ds(start, size), :], weighted, preferred_element_type=jnp.float32)
            out[:, span, :] = value.astype(jnp.bfloat16).reshape(out.shape[0], ROWS, ell)


def restore(where, stay, came, ratios, modes, parts, freqs):
    _, rows, ell = stay.shape
    vmem = pl.BlockSpec(memory_space=pltpu.VMEM)
    return pl.pallas_call(
        restore_kernel,
        grid_spec=pltpu.PrefetchScalarGridSpec(
            num_scalar_prefetch=1, grid=(), in_specs=[vmem] * 4, out_specs=[vmem] * parts
        ),
        out_shape=[jax.ShapeDtypeStruct((freqs, rows, ell), jnp.bfloat16)] * parts,
        compiler_params=pltpu.CompilerParams(vmem_limit_bytes=VMEM_LIMIT),
        cost_estimate=pl.CostEstimate(
            flops=2 * modes.size * rows // ROWS * ell, bytes_accessed=8 * stay.size, transcendentals=0
        ),
    )(where, stay, came, ratios, modes)


def place_kernel(where, *refs, parts):
    pieces, out = refs[:parts], refs[-1]
    for which in range(parts):

        @pl.when(pl.program_id(0) == which)
        def _():
            out[:, 0] = pieces[which][...]


def place(where, pieces, first, shape, into=None):
    parts = len(pieces)
    freqs, rows, ell = pieces[0].shape

    def block_of(which):
        def index(j, g, s):
            return (0, jnp.where(j == which, g, jnp.where(j < which, 0, rows // ROWS - 1)), 0)

        return pl.BlockSpec((freqs, ROWS, ell), index)

    extra = [] if into is None else [into]
    return pl.pallas_call(
        functools.partial(place_kernel, parts=parts),
        grid_spec=pltpu.PrefetchScalarGridSpec(
            num_scalar_prefetch=1,
            grid=(parts, rows // ROWS),
            in_specs=[block_of(j) for j in range(parts)] + [pl.BlockSpec(memory_space=pl.ANY)] * len(extra),
            out_specs=pl.BlockSpec((freqs, 1, ROWS, ell), lambda j, g, s: (0, s[j], first // ROWS + g, 0)),
        ),
        out_shape=jax.ShapeDtypeStruct(shape, jnp.bfloat16),
        input_output_aliases={parts + 1: 0} if extra else {},
        compiler_params=pltpu.CompilerParams(vmem_limit_bytes=VMEM_LIMIT),
        cost_estimate=pl.CostEstimate(flops=0, bytes_accessed=4 * parts * pieces[0].size, transcendentals=0),
    )(where, *pieces, *extra)


def chunked(visibility, beam_transfer, tile_mask, first_block, eigen_modes, signal_noise, chunks):
    freqs, parts, rows_all, base = visibility.shape
    _, freq_total, _, ell = beam_transfer.shape
    n_modes = eigen_modes.shape[2]
    ell_tiles = ell // TILE
    z, x, p = lax.axis_index("fm"), lax.axis_index("kl"), lax.axis_index("pol")
    other = [(0, 1), (1, 0)]

    def along_z(value, j):
        return lax.ppermute(value, "fm", [(i, i ^ j) for i in range(parts)])

    def along_x(value):
        return lax.ppermute(value, "kl", other)

    def cut(chunk, j):
        first, rows = chunk
        return lax.dynamic_slice(visibility, (0, z ^ j, first, 0), (freqs, 1, rows, base)).reshape(freqs, rows, base)

    order = jnp.stack([z ^ j for j in range(parts)]).astype(jnp.int32)
    block_ids = x * ell_tiles + jnp.arange(ell_tiles, dtype=jnp.int32)
    keep = tile_mask[0] * (first_block[0] <= block_ids).astype(jnp.int32)[None, :]
    where = jnp.concatenate([order, (x == p).astype(jnp.int32)[None], keep.reshape(-1)])
    down, up = spread(eigen_modes[0])
    ratio = signal_noise[0] / (1.0 + signal_noise[0])
    ratios = jnp.broadcast_to(ratio[:, None, None], (n_modes, 1, ell))
    beam = beam_transfer.reshape(freq_total, base, ell)
    shape = (freqs, parts, rows_all, ell)

    def filter_rows(mine, others):
        stay, leave = project(where, mine, others, beam, down, n_modes)
        came = lax.ppermute(leave, "pol", other)
        return leave, restore(where, stay, came, ratios, up, parts, freqs)

    a, b = [[cut(chunk, j) for j in range(parts)] for chunk in chunks]
    got_a, got_b = [a[0]] + [None] * 3, [b[0]] + [None] * 3
    side_a, side_b = [None] * 4, [None] * 4
    for j in (2, 3, 1):
        got_a[j] = along_z(a[j], j)
    got_b[2] = along_z(b[2], 2)
    side_a[0] = along_x(a[0])
    got_b[1] = along_z(after(b[1], got_a[1]), 1)
    side_b[0] = along_x(after(b[0], side_a[0]))
    side_a[1] = along_x(after(got_a[1], side_a[0]))
    got_b[3] = along_z(after(b[3], got_a[2]), 3)
    side_a[2] = along_x(after(got_a[2], side_b[0]))
    side_a[3] = along_x(after(got_a[3], side_a[1]))
    side_b[1] = along_x(after(got_b[1], side_a[2]))
    side_b[2] = along_x(after(got_b[2], side_a[3]))
    leave_a, outs_a = filter_rows(got_a, side_a)
    side_b[3] = along_x(after(got_b[3], outs_a[0]))
    back_a = [outs_a[0]] + [along_z(after(outs_a[j], got_b[3]), j) for j in range(1, parts)]
    leave_b, outs_b = filter_rows(got_b, side_b)
    back_b = [outs_b[0]] + [along_z(outs_b[j], j) for j in range(1, parts)]
    result = place(where, back_a, chunks[0][0], shape)
    return place(where, back_b, chunks[1][0], shape, into=result)


def plain(visibility, beam_transfer, tile_mask, first_block, eigen_modes, signal_noise):
    owned_modes, freq_total, base_half, ell_local = beam_transfer.shape
    base_tiles, ell_tiles = base_half // TILE, ell_local // TILE
    block_ids = lax.axis_index("kl") * ell_tiles + jnp.arange(ell_tiles, dtype=jnp.int32)
    inside = (first_block[:, None] <= block_ids[None, :]).astype(jnp.int32)
    keep_tiles = tile_mask * inside[:, None, :]
    shaped = beam_transfer.reshape(owned_modes, freq_total, base_tiles, TILE, ell_tiles, TILE)
    masked_beam = shaped * keep_tiles.astype(jnp.bfloat16)[:, None, :, None, :, None]
    masked_beam = masked_beam.reshape(owned_modes, freq_total, base_half, ell_local)
    arrived = lax.all_to_all(visibility, "fm", split_axis=1, concat_axis=0, tiled=True)
    partial_value = jnp.einsum(
        "fmrb,mfbl->fmrl",
        lax.all_gather(arrived, "kl", axis=2, tiled=True),
        masked_beam,
        preferred_element_type=jnp.float32,
    )
    sky_sum = lax.psum_scatter(
        partial_value.astype(jnp.bfloat16), "pol", scatter_dimension=2, tiled=True
    ).astype(jnp.float32)
    modes_float = eigen_modes.astype(jnp.float32)
    coeffs = jnp.einsum("mfk,fmrl->mkrl", modes_float, sky_sum, precision=lax.Precision.HIGHEST)
    ratios = signal_noise / (1.0 + signal_noise)
    weighted = (coeffs * ratios[:, :, None, None]).astype(jnp.bfloat16)
    filtered = jnp.einsum(
        "mfk,mkrl->fmrl", eigen_modes, weighted, preferred_element_type=jnp.float32
    ).astype(jnp.bfloat16)
    return lax.all_to_all(filtered, "fm", split_axis=0, concat_axis=1, tiled=True)


def per_device(*args, sizes):
    visibility, beam_transfer = args[0], args[1]
    freqs, modes, rows, _ = visibility.shape
    fits = (
        sizes["kl"] == 2
        and sizes["pol"] == 2
        and modes == sizes["fm"] == 4
        and beam_transfer.shape[0] == 1
        and rows % ROWS == 0
        and rows >= 2 * ROWS
        and freqs % STEP_F == 0
        and beam_transfer.shape[3] % WIDE == 0
    )
    if not fits:
        return plain(*args)
    return chunked(*args, chunks=[(0, ROWS), (ROWS, rows - ROWS)])


def solution(mesh):
    placed = (
        P(("group", "fm"), None, "kl", "pol"),
        P(("group", "fm"), None, "pol", "kl"),
        P("fm", "pol", "kl"),
        P("fm"),
        P(("group", "fm"), None, None),
        P(("group", "fm"), None),
    )
    return jax.shard_map(
        functools.partial(per_device, sizes=dict(mesh.shape)),
        mesh=mesh,
        in_specs=placed,
        out_specs=P(("group", "fm"), None, "pol", "kl"),
        check_vma=False,
    )
```

time: 190 us -> 128 us (0.67)
  the two profiles are of different devices: /device:TPU:12 before, /device:TPU:0 now
where the time goes in v2:
time: 128 us
  waiting for transfers between devices  65.1 us (51%)
  Pallas kernels  30.5 us (24%)
  starting transfers between devices  28.6 us (22%)
  local copies, waits for them, and re-layouts  2.86 us (2%)
    ppermute x12, waiting for transfers between devices, along_z(): return lax.ppermute(value, 'fm', [(i, i ^ j) for i in range(parts)])  46.6 us
    pallas_call x2, Pallas kernels, project(): pl.pallas_call(functools.partial(project_kernel, parts=parts, freqs=freqs...  21.9 us
    ppermute x12, starting transfers between devices, along_z(): return lax.ppermute(value, 'fm', [(i, i ^ j) for i in range(parts)])  20.3 us
    ppermute x8, waiting for transfers between devices, along_x(): return lax.ppermute(value, 'kl', other)  18.5 us
    ppermute x8, starting transfers between devices, along_x(): return lax.ppermute(value, 'kl', other)  8.17 us
    pallas_call x2, Pallas kernels, place(): pl.pallas_call(functools.partial(place_kernel, parts=parts), grid_spec=pl...  5.54 us
  transfers between devices with their start and end apart: 22, of which 11 were waited for; matrix products, arithmetic and copies ran while one was open for 1% of the time, Pallas kernels for 4%

profile of v2, /device:TPU:0, one launch (start us, length us, event | category | flops | bytes accessed | tf_op | source)
XLA Modules:
  0.0 127.8 jit_solution(7294861469726099747)
XLA Ops:
  1.2 3.1 %collective-permute-start = (bf16[8,16,512]{2,1,0:T(8,128)(2,1)S(1)}, bf16[8,16,512]{2,1,0:T(8,128)(2,1)S(1)}, u32[]{:S(2)}, u32[]{:S(2)}) collective-permute-start(bf16[8,16,512]{2,1,0:T(8,128)(2,1)S(1)} %get-tuple-element.59), channel_id=1, source_target_pairs={{0,4},{4,0},{8,12},{12,8},{1,5},{5,1},{9,13},{13,9},{2,6},{6,2},{1... | collective-permute-start | bytes 393224 | tf_op jit(solution)/shard_map/ppermute | solution.py:230
  4.3 1.5 %collective-permute-start.5 = (bf16[8,16,512]{2,1,0:T(8,128)(2,1)S(1)}, bf16[8,16,512]{2,1,0:T(8,128)(2,1)S(1)}, u32[]{:S(2)}, u32[]{:S(2)}) collective-permute-start(bf16[8,16,512]{2,1,0:T(8,128)(2,1)S(1)} %get-tuple-element.60.refs_0_), channel_id=1, source_target_pairs={{0,2},{2,0},{1,3},{3,1},{4,6},{6,4},{5,7},{7,5},{8,10},{10,8},{9,1... | collective-permute-start | bytes 393224 | tf_op jit(solution)/shard_map/ppermute | solution.py:233
  7.0 2.2 %collective-permute-done.5.refs_4_ = bf16[8,16,512]{2,1,0:T(8,128)(2,1)S(1)} collective-permute-done((bf16[8,16,512]{2,1,0:T(8,128)(2,1)S(1)}, bf16[8,16,512]{2,1,0:T(8,128)(2,1)S(1)}, u32[]{:S(2)}, u32[]{:S(2)}) %collective-permute-start.5) | collective-permute-done | bytes 131104 | tf_op jit(solution)/shard_map/ppermute | solution.py:233
  9.2 1.5 %collective-permute-start.6 = (bf16[8,32,512]{2,1,0:T(8,128)(2,1)S(1)}, bf16[8,32,512]{2,1,0:T(8,128)(2,1)S(1)}, u32[]{:S(2)}, u32[]{:S(2)}) collective-permute-start(bf16[8,32,512]{2,1,0:T(8,128)(2,1)S(1)} %get-tuple-element.33.refs_0_), channel_id=1, source_target_pairs={{0,2},{2,0},{1,3},{3,1},{4,6},{6,4},{5,7},{7,5},{8,10},{10,8},{9,1... | collective-permute-start | bytes 786440 | tf_op jit(solution)/shard_map/ppermute | solution.py:233
  10.7 2.5 %collective-permute-start.9 = (bf16[8,16,512]{2,1,0:T(8,128)(2,1)S(1)}, bf16[8,16,512]{2,1,0:T(8,128)(2,1)S(1)}, u32[]{:S(2)}, u32[]{:S(2)}) collective-permute-start(bf16[8,16,512]{2,1,0:T(8,128)(2,1)S(1)} %get-tuple-element.57), channel_id=1, source_target_pairs={{0,12},{4,8},{8,4},{12,0},{1,13},{5,9},{9,5},{13,1},{2,14},{6,10},... | collective-permute-start | bytes 393224 | tf_op jit(solution)/shard_map/ppermute | solution.py:230
  13.8 4.2 %collective-permute-done.9.refs_3_ = bf16[8,16,512]{2,1,0:T(8,128)(2,1)S(1)} collective-permute-done((bf16[8,16,512]{2,1,0:T(8,128)(2,1)S(1)}, bf16[8,16,512]{2,1,0:T(8,128)(2,1)S(1)}, u32[]{:S(2)}, u32[]{:S(2)}) %collective-permute-start.9) | collective-permute-done | bytes 131104 | tf_op jit(solution)/shard_map/ppermute | solution.py:230
  18.9 1.5 %collective-permute-start.11 = (bf16[8,16,512]{2,1,0:T(8,128)(2,1)S(1)}, bf16[8,16,512]{2,1,0:T(8,128)(2,1)S(1)}, u32[]{:S(2)}, u32[]{:S(2)}) collective-permute-start(bf16[8,16,512]{2,1,0:T(8,128)(2,1)S(1)} %collective-permute-done.9.refs_3_), channel_id=1, source_target_pairs={{0,2},{2,0},{1,3},{3,1},{4,6},{6,4},{5,7},{7,5},{8,10},{10,8},{9,1... | collective-permute-start | bytes 393224 | tf_op jit(solution)/shard_map/ppermute | solution.py:233
  20.4 3.4 %collective-permute-done.3.refs_2_ = bf16[8,16,512]{2,1,0:T(8,128)(2,1)S(1)} collective-permute-done((bf16[8,16,512]{2,1,0:T(8,128)(2,1)S(1)}, bf16[8,16,512]{2,1,0:T(8,128)(2,1)S(1)}, u32[]{:S(2)}, u32[]{:S(2)}) %collective-permute-start.3) | collective-permute-done | bytes 131104 | tf_op jit(solution)/shard_map/ppermute | solution.py:230
  26.0 2.8 %collective-permute-done.7.refs_6_ = bf16[8,16,512]{2,1,0:T(8,128)(2,1)S(1)} collective-permute-done((bf16[8,16,512]{2,1,0:T(8,128)(2,1)S(1)}, bf16[8,16,512]{2,1,0:T(8,128)(2,1)S(1)}, u32[]{:S(2)}, u32[]{:S(2)}) %collective-permute-start.7) | collective-permute-done | bytes 131104 | tf_op jit(solution)/shard_map/ppermute | solution.py:233
  28.8 10.8 %shard_map.65 = (bf16[24,16,512]{2,1,0:T(8,128)(2,1)S(1)}, bf16[24,16,512]{2,1,0:T(8,128)(2,1)S(1)}) custom-call(s32[21]{0:T(128)S(1)} %concatenate.3.where, bf16[8,16,512]{2,1,0:T(8,128)(2,1)S(1)} %get-tuple-element.60.refs_0_, bf16[8,16,512]{2,1,0:T(8,128)(2,1)S(1)} %collective-permute-done.refs_1_, ...), custom_call_target="tpu_custom_call" | custom-call | flops 536870912 | bytes 17825792 | tf_op jit(solution)/shard_map/pallas_call | solution.py:130
  41.0 1.9 %collective-permute-start.1 = (bf16[8,32,512]{2,1,0:T(8,128)(2,1)S(1)}, bf16[8,32,512]{2,1,0:T(8,128)(2,1)S(1)}, u32[]{:S(2)}, u32[]{:S(2)}) collective-permute-start(bf16[8,32,512]{2,1,0:T(8,128)(2,1)S(1)} %get-tuple-element.31), channel_id=1, source_target_pairs={{0,4},{4,0},{8,12},{12,8},{1,5},{5,1},{9,13},{13,9},{2,6},{6,2},{1... | collective-permute-start | bytes 786440 | tf_op jit(solution)/shard_map/ppermute | solution.py:230
  44.1 11.5 %collective-permute-done.2.refs_2_ = bf16[8,32,512]{2,1,0:T(8,128)(2,1)S(1)} collective-permute-done((bf16[8,32,512]{2,1,0:T(8,128)(2,1)S(1)}, bf16[8,32,512]{2,1,0:T(8,128)(2,1)S(1)}, u32[]{:S(2)}, u32[]{:S(2)}) %collective-permute-start.2) | collective-permute-done | bytes 262176 | tf_op jit(solution)/shard_map/ppermute | solution.py:230
  58.8 2.1 %collective-permute-done.4.refs_3_ = bf16[8,32,512]{2,1,0:T(8,128)(2,1)S(1)} collective-permute-done((bf16[8,32,512]{2,1,0:T(8,128)(2,1)S(1)}, bf16[8,32,512]{2,1,0:T(8,128)(2,1)S(1)}, u32[]{:S(2)}, u32[]{:S(2)}) %collective-permute-start.4) | collective-permute-done | bytes 262176 | tf_op jit(solution)/shard_map/ppermute | solution.py:230
  61.4 3.4 %collective-permute-done.12.refs_6_ = bf16[8,32,512]{2,1,0:T(8,128)(2,1)S(1)} collective-permute-done((bf16[8,32,512]{2,1,0:T(8,128)(2,1)S(1)}, bf16[8,32,512]{2,1,0:T(8,128)(2,1)S(1)}, u32[]{:S(2)}, u32[]{:S(2)}) %collective-permute-start.12) | collective-permute-done | bytes 262176 | tf_op jit(solution)/shard_map/ppermute | solution.py:233
  64.8 5.6 %collective-permute-done.8.refs_5_ = bf16[8,32,512]{2,1,0:T(8,128)(2,1)S(1)} collective-permute-done((bf16[8,32,512]{2,1,0:T(8,128)(2,1)S(1)}, bf16[8,32,512]{2,1,0:T(8,128)(2,1)S(1)}, u32[]{:S(2)}, u32[]{:S(2)}) %collective-permute-start.8) | collective-permute-done | bytes 262176 | tf_op jit(solution)/shard_map/ppermute | solution.py:233
  70.4 3.7 %collective-permute-done.14.refs_7_ = bf16[8,32,512]{2,1,0:T(8,128)(2,1)S(1)} collective-permute-done((bf16[8,32,512]{2,1,0:T(8,128)(2,1)S(1)}, bf16[8,32,512]{2,1,0:T(8,128)(2,1)S(1)}, u32[]{:S(2)}, u32[]{:S(2)}) %collective-permute-start.14) | collective-permute-done | bytes 262176 | tf_op jit(solution)/shard_map/ppermute | solution.py:233
  74.1 11.2 %shard_map.67 = (bf16[24,32,512]{2,1,0:T(8,128)(2,1)S(1)}, bf16[24,32,512]{2,1,0:T(8,128)(2,1)S(1)}) custom-call(s32[21]{0:T(128)S(1)} %concatenate.3.where, bf16[8,32,512]{2,1,0:T(8,128)(2,1)S(1)} %get-tuple-element.33.refs_0_, bf16[8,32,512]{2,1,0:T(8,128)(2,1)S(1)} %collective-permute-done.1.refs_1_, ...), custom_call_target="tpu_custom_call" | custom-call | flops 1073741824 | bytes 18874368 | tf_op jit(solution)/shard_map/pallas_call | solution.py:130
  85.4 2.9 %collective-permute-start.21 = (bf16[8,16,512]{2,1,0:T(8,128)(2,1)S(1)}, bf16[8,16,512]{2,1,0:T(8,128)(2,1)S(1)}, u32[]{:S(2)}, u32[]{:S(2)}) collective-permute-start(bf16[8,16,512]{2,1,0:T(8,128)(2,1)S(1)} %get-tuple-element.56), channel_id=1, source_target_pairs={{0,12},{4,8},{8,4},{12,0},{1,13},{5,9},{9,5},{13,1},{2,14},{6,10},... | collective-permute-start | bytes 393224 | tf_op jit(solution)/shard_map/ppermute | solution.py:230
  89.7 2.8 %collective-permute-start.17 = (bf16[8,32,512]{2,1,0:T(8,128)(2,1)S(1)}, bf16[8,32,512]{2,1,0:T(8,128)(2,1)S(1)}, u32[]{:S(2)}, u32[]{:S(2)}) collective-permute-start(bf16[8,32,512]{2,1,0:T(8,128)(2,1)S(1)} %get-tuple-element.49), channel_id=1, source_target_pairs={{0,8},{4,12},{8,0},{12,4},{1,9},{5,13},{9,1},{13,5},{2,10},{6,14},... | collective-permute-start | bytes 786440 | tf_op jit(solution)/shard_map/ppermute | solution.py:230
  92.5 1.6 %collective-permute-start.18 = (bf16[8,32,512]{2,1,0:T(8,128)(2,1)S(1)}, bf16[8,32,512]{2,1,0:T(8,128)(2,1)S(1)}, u32[]{:S(2)}, u32[]{:S(2)}) collective-permute-start(bf16[8,32,512]{2,1,0:T(8,128)(2,1)S(1)} %get-tuple-element.50), channel_id=1, source_target_pairs={{0,12},{4,8},{8,4},{12,0},{1,13},{5,9},{9,5},{13,1},{2,14},{6,10},... | collective-permute-start | bytes 786440 | tf_op jit(solution)/shard_map/ppermute | solution.py:230
  94.2 2.7 %collective-permute-start.19 = (bf16[8,16,512]{2,1,0:T(8,128)(2,1)S(1)}, bf16[8,16,512]{2,1,0:T(8,128)(2,1)S(1)}, u32[]{:S(2)}, u32[]{:S(2)}) collective-permute-start(bf16[8,16,512]{2,1,0:T(8,128)(2,1)S(1)} %get-tuple-element.52), channel_id=1, source_target_pairs={{0,4},{4,0},{8,12},{12,8},{1,5},{5,1},{9,13},{13,9},{2,6},{6,2},{1... | collective-permute-start | bytes 393224 | tf_op jit(solution)/shard_map/ppermute | solution.py:230
  96.9 25.4 %collective-permute-done.20.refs_2_ = bf16[8,16,512]{2,1,0:T(8,128)(2,1)S(1)} collective-permute-done((bf16[8,16,512]{2,1,0:T(8,128)(2,1)S(1)}, bf16[8,16,512]{2,1,0:T(8,128)(2,1)S(1)}, u32[]{:S(2)}, u32[]{:S(2)}) %collective-permute-start.20) | collective-permute-done | bytes 131104 | tf_op jit(solution)/shard_map/ppermute | solution.py:230
  122.3 2.0 %shard_map.69.refs_4_ = bf16[8,4,48,512]{3,2,1,0:T(8,128)(2,1)} custom-call(s32[21]{0:T(128)S(1)} %concatenate.3.where, bf16[8,16,512]{2,1,0:T(8,128)(2,1)S(1)} %get-tuple-element.43.refs_0_, bf16[8,16,512]{2,1,0:T(8,128)(2,1)S(1)} %collective-permute-done.19.refs_1_, bf16[8,16,512]{2,1,0:T(8,128)(2,1)S(1)} %collective-permute-done.20.refs_2_, ...), custom_call_target="tpu_custom_call" | custom-call | bytes 1048576 | tf_op jit(solution)/shard_map/pallas_call | solution.py:206
  124.2 3.6 %shard_map.70 = bf16[8,4,48,512]{3,2,1,0:T(8,128)(2,1)} custom-call(s32[21]{0:T(128)S(1)} %concatenate.3.where, bf16[8,32,512]{2,1,0:T(8,128)(2,1)S(1)} %get-tuple-element.47.refs_0_, bf16[8,32,512]{2,1,0:T(8,128)(2,1)S(1)} %collective-permute-done.16.refs_1_, ...), custom_call_target="tpu_custom_call", output_to_operand_aliasing={{}: (5, {})} | custom-call | bytes 2097152 | tf_op jit(solution)/shard_map/pallas_call | solution.py:206
  (44 shorter events, 13.3 us)
Async XLA Ops:
  0.0 25.0 %copy-start.1 = (s32[1,4,4]{2,1,0:T(4,128)S(1)}, s32[1,4,4]{2,1,0:T(4,128)}, u32[]{:S(2)}) copy-start(s32[1,4,4]{2,1,0:T(4,128)} %param.8) | copy-start | bytes 196
  0.0 25.2 %copy-start = (bf16[1,32,24]{1,2,0:T(8,128)(2,1)S(1)}, bf16[1,32,24]{1,2,0:T(8,128)(2,1)}, u32[]{:S(2)}) copy-start(bf16[1,32,24]{1,2,0:T(8,128)(2,1)} %param.10) | copy-start | bytes 4612
  1.2 12.0 %collective-permute-start = (bf16[8,16,512]{2,1,0:T(8,128)(2,1)S(1)}, bf16[8,16,512]{2,1,0:T(8,128)(2,1)S(1)}, u32[]{:S(2)}, u32[]{:S(2)}) collective-permute-start(bf16[8,16,512]{2,1,0:T(8,128)(2,1)S(1)} %get-tuple-element.59), channel_id=1, source_target_pairs={{0,4},{4,0},{8,12},{12,8},{1,5},{5,1},{9,13},{13,9},{2,6},{6,2},{1... | collective-permute-start | bytes 393224 | tf_op jit(solution)/shard_map/ppermute | solution.py:230
  4.3 5.0 %collective-permute-start.5 = (bf16[8,16,512]{2,1,0:T(8,128)(2,1)S(1)}, bf16[8,16,512]{2,1,0:T(8,128)(2,1)S(1)}, u32[]{:S(2)}, u32[]{:S(2)}) collective-permute-start(bf16[8,16,512]{2,1,0:T(8,128)(2,1)S(1)} %get-tuple-element.60.refs_0_), channel_id=1, source_target_pairs={{0,2},{2,0},{1,3},{3,1},{4,6},{6,4},{5,7},{7,5},{8,10},{10,8},{9,1... | collective-permute-start | bytes 393224 | tf_op jit(solution)/shard_map/ppermute | solution.py:233
  9.2 14.6 %collective-permute-start.6 = (bf16[8,32,512]{2,1,0:T(8,128)(2,1)S(1)}, bf16[8,32,512]{2,1,0:T(8,128)(2,1)S(1)}, u32[]{:S(2)}, u32[]{:S(2)}) collective-permute-start(bf16[8,32,512]{2,1,0:T(8,128)(2,1)S(1)} %get-tuple-element.33.refs_0_), channel_id=1, source_target_pairs={{0,2},{2,0},{1,3},{3,1},{4,6},{6,4},{5,7},{7,5},{8,10},{10,8},{9,1... | collective-permute-start | bytes 786440 | tf_op jit(solution)/shard_map/ppermute | solution.py:233
  10.7 7.3 %collective-permute-start.9 = (bf16[8,16,512]{2,1,0:T(8,128)(2,1)S(1)}, bf16[8,16,512]{2,1,0:T(8,128)(2,1)S(1)}, u32[]{:S(2)}, u32[]{:S(2)}) collective-permute-start(bf16[8,16,512]{2,1,0:T(8,128)(2,1)S(1)} %get-tuple-element.57), channel_id=1, source_target_pairs={{0,12},{4,8},{8,4},{12,0},{1,13},{5,9},{9,5},{13,1},{2,14},{6,10},... | collective-permute-start | bytes 393224 | tf_op jit(solution)/shard_map/ppermute | solution.py:230
  13.2 5.7 %collective-permute-start.10 = (bf16[8,16,512]{2,1,0:T(8,128)(2,1)S(1)}, bf16[8,16,512]{2,1,0:T(8,128)(2,1)S(1)}, u32[]{:S(2)}, u32[]{:S(2)}) collective-permute-start(bf16[8,16,512]{2,1,0:T(8,128)(2,1)S(1)} %collective-permute-done.refs_1_), channel_id=1, source_target_pairs={{0,2},{2,0},{1,3},{3,1},{4,6},{6,4},{5,7},{7,5},{8,10},{10,8},{9,1... | collective-permute-start | bytes 393224 | tf_op jit(solution)/shard_map/ppermute | solution.py:233
  13.7 10.1 %collective-permute-start.3 = (bf16[8,16,512]{2,1,0:T(8,128)(2,1)S(1)}, bf16[8,16,512]{2,1,0:T(8,128)(2,1)S(1)}, u32[]{:S(2)}, u32[]{:S(2)}) collective-permute-start(bf16[8,16,512]{2,1,0:T(8,128)(2,1)S(1)} %get-tuple-element.58), channel_id=1, source_target_pairs={{0,8},{4,12},{8,0},{12,4},{1,9},{5,13},{9,1},{13,5},{2,10},{6,14},... | collective-permute-start | bytes 393224 | tf_op jit(solution)/shard_map/ppermute | solution.py:230
  18.9 7.1 %collective-permute-start.11 = (bf16[8,16,512]{2,1,0:T(8,128)(2,1)S(1)}, bf16[8,16,512]{2,1,0:T(8,128)(2,1)S(1)}, u32[]{:S(2)}, u32[]{:S(2)}) collective-permute-start(bf16[8,16,512]{2,1,0:T(8,128)(2,1)S(1)} %collective-permute-done.9.refs_3_), channel_id=1, source_target_pairs={{0,2},{2,0},{1,3},{3,1},{4,6},{6,4},{5,7},{7,5},{8,10},{10,8},{9,1... | collective-permute-start | bytes 393224 | tf_op jit(solution)/shard_map/ppermute | solution.py:233
  23.8 5.0 %collective-permute-start.7 = (bf16[8,16,512]{2,1,0:T(8,128)(2,1)S(1)}, bf16[8,16,512]{2,1,0:T(8,128)(2,1)S(1)}, u32[]{:S(2)}, u32[]{:S(2)}) collective-permute-start(bf16[8,16,512]{2,1,0:T(8,128)(2,1)S(1)} %collective-permute-done.3.refs_2_), channel_id=1, source_target_pairs={{0,2},{2,0},{1,3},{3,1},{4,6},{6,4},{5,7},{7,5},{8,10},{10,8},{9,1... | collective-permute-start | bytes 393224 | tf_op jit(solution)/shard_map/ppermute | solution.py:233
  39.5 18.1 %collective-permute-start.13 = (bf16[24,16,512]{2,1,0:T(8,128)(2,1)S(1)}, bf16[24,16,512]{2,1,0:T(8,128)(2,1)S(1)}, u32[]{:S(2)}, u32[]{:S(2)}) collective-permute-start(bf16[24,16,512]{2,1,0:T(8,128)(2,1)S(1)} %get-tuple-element.41), channel_id=1, source_target_pairs={{0,1},{1,0},{2,3},{3,2},{4,5},{5,4},{6,7},{7,6},{8,9},{9,8},{10,11... | collective-permute-start | bytes 1179656 | tf_op jit(solution)/shard_map/ppermute | solution.py:251
  39.6 16.0 %collective-permute-start.2 = (bf16[8,32,512]{2,1,0:T(8,128)(2,1)S(1)}, bf16[8,32,512]{2,1,0:T(8,128)(2,1)S(1)}, u32[]{:S(2)}, u32[]{:S(2)}) collective-permute-start(bf16[8,32,512]{2,1,0:T(8,128)(2,1)S(1)} %get-tuple-element.62), channel_id=1, source_target_pairs={{0,8},{4,12},{8,0},{12,4},{1,9},{5,13},{9,1},{13,5},{2,10},{6,14},... | collective-permute-start | bytes 786440 | tf_op jit(solution)/shard_map/ppermute | solution.py:230
  41.0 15.1 %collective-permute-start.1 = (bf16[8,32,512]{2,1,0:T(8,128)(2,1)S(1)}, bf16[8,32,512]{2,1,0:T(8,128)(2,1)S(1)}, u32[]{:S(2)}, u32[]{:S(2)}) collective-permute-start(bf16[8,32,512]{2,1,0:T(8,128)(2,1)S(1)} %get-tuple-element.31), channel_id=1, source_target_pairs={{0,4},{4,0},{8,12},{12,8},{1,5},{5,1},{9,13},{13,9},{2,6},{6,2},{1... | collective-permute-start | bytes 786440 | tf_op jit(solution)/shard_map/ppermute | solution.py:230
  42.9 18.0 %collective-permute-start.4 = (bf16[8,32,512]{2,1,0:T(8,128)(2,1)S(1)}, bf16[8,32,512]{2,1,0:T(8,128)(2,1)S(1)}, u32[]{:S(2)}, u32[]{:S(2)}) collective-permute-start(bf16[8,32,512]{2,1,0:T(8,128)(2,1)S(1)} %get-tuple-element.32), channel_id=1, source_target_pairs={{0,12},{4,8},{8,4},{12,0},{1,13},{5,9},{9,5},{13,1},{2,14},{6,10},... | collective-permute-start | bytes 786440 | tf_op jit(solution)/shard_map/ppermute | solution.py:230
  55.6 9.2 %collective-permute-start.12 = (bf16[8,32,512]{2,1,0:T(8,128)(2,1)S(1)}, bf16[8,32,512]{2,1,0:T(8,128)(2,1)S(1)}, u32[]{:S(2)}, u32[]{:S(2)}) collective-permute-start(bf16[8,32,512]{2,1,0:T(8,128)(2,1)S(1)} %collective-permute-done.2.refs_2_), channel_id=1, source_target_pairs={{0,2},{2,0},{1,3},{3,1},{4,6},{6,4},{5,7},{7,5},{8,10},{10,8},{9,1... | collective-permute-start | bytes 786440 | tf_op jit(solution)/shard_map/ppermute | solution.py:233
  56.1 14.3 %collective-permute-start.8 = (bf16[8,32,512]{2,1,0:T(8,128)(2,1)S(1)}, bf16[8,32,512]{2,1,0:T(8,128)(2,1)S(1)}, u32[]{:S(2)}, u32[]{:S(2)}) collective-permute-start(bf16[8,32,512]{2,1,0:T(8,128)(2,1)S(1)} %collective-permute-done.1.refs_1_), channel_id=1, source_target_pairs={{0,2},{2,0},{1,3},{3,1},{4,6},{6,4},{5,7},{7,5},{8,10},{10,8},{9,1... | collective-permute-start | bytes 786440 | tf_op jit(solution)/shard_map/ppermute | solution.py:233
  60.9 13.2 %collective-permute-start.14 = (bf16[8,32,512]{2,1,0:T(8,128)(2,1)S(1)}, bf16[8,32,512]{2,1,0:T(8,128)(2,1)S(1)}, u32[]{:S(2)}, u32[]{:S(2)}) collective-permute-start(bf16[8,32,512]{2,1,0:T(8,128)(2,1)S(1)} %collective-permute-done.4.refs_3_), channel_id=1, source_target_pairs={{0,2},{2,0},{1,3},{3,1},{4,6},{6,4},{5,7},{7,5},{8,10},{10,8},{9,1... | collective-permute-start | bytes 786440 | tf_op jit(solution)/shard_map/ppermute | solution.py:233
  85.3 3.0 %collective-permute-start.15 = (bf16[24,32,512]{2,1,0:T(8,128)(2,1)S(1)}, bf16[24,32,512]{2,1,0:T(8,128)(2,1)S(1)}, u32[]{:S(2)}, u32[]{:S(2)}) collective-permute-start(bf16[24,32,512]{2,1,0:T(8,128)(2,1)S(1)} %get-tuple-element.46), channel_id=1, source_target_pairs={{0,1},{1,0},{2,3},{3,2},{4,5},{5,4},{6,7},{7,6},{8,9},{9,8},{10,11... | collective-permute-start | bytes 2359304 | tf_op jit(solution)/shard_map/ppermute | solution.py:251
  85.4 8.7 %collective-permute-start.21 = (bf16[8,16,512]{2,1,0:T(8,128)(2,1)S(1)}, bf16[8,16,512]{2,1,0:T(8,128)(2,1)S(1)}, u32[]{:S(2)}, u32[]{:S(2)}) collective-permute-start(bf16[8,16,512]{2,1,0:T(8,128)(2,1)S(1)} %get-tuple-element.56), channel_id=1, source_target_pairs={{0,12},{4,8},{8,4},{12,0},{1,13},{5,9},{9,5},{13,1},{2,14},{6,10},... | collective-permute-start | bytes 393224 | tf_op jit(solution)/shard_map/ppermute | solution.py:230
  89.7 34.6 %collective-permute-start.16 = (bf16[8,32,512]{2,1,0:T(8,128)(2,1)S(1)}, bf16[8,32,512]{2,1,0:T(8,128)(2,1)S(1)}, u32[]{:S(2)}, u32[]{:S(2)}) collective-permute-start(bf16[8,32,512]{2,1,0:T(8,128)(2,1)S(1)} %get-tuple-element.48), channel_id=1, source_target_pairs={{0,4},{4,0},{8,12},{12,8},{1,5},{5,1},{9,13},{13,9},{2,6},{6,2},{1... | collective-permute-start | bytes 786440 | tf_op jit(solution)/shard_map/ppermute | solution.py:230
  89.7 34.5 %collective-permute-start.17 = (bf16[8,32,512]{2,1,0:T(8,128)(2,1)S(1)}, bf16[8,32,512]{2,1,0:T(8,128)(2,1)S(1)}, u32[]{:S(2)}, u32[]{:S(2)}) collective-permute-start(bf16[8,32,512]{2,1,0:T(8,128)(2,1)S(1)} %get-tuple-element.49), channel_id=1, source_target_pairs={{0,8},{4,12},{8,0},{12,4},{1,9},{5,13},{9,1},{13,5},{2,10},{6,14},... | collective-permute-start | bytes 786440 | tf_op jit(solution)/shard_map/ppermute | solution.py:230
  92.5 31.8 %collective-permute-start.18 = (bf16[8,32,512]{2,1,0:T(8,128)(2,1)S(1)}, bf16[8,32,512]{2,1,0:T(8,128)(2,1)S(1)}, u32[]{:S(2)}, u32[]{:S(2)}) collective-permute-start(bf16[8,32,512]{2,1,0:T(8,128)(2,1)S(1)} %get-tuple-element.50), channel_id=1, source_target_pairs={{0,12},{4,8},{8,4},{12,0},{1,13},{5,9},{9,5},{13,1},{2,14},{6,10},... | collective-permute-start | bytes 786440 | tf_op jit(solution)/shard_map/ppermute | solution.py:230
  94.1 28.2 %collective-permute-start.20 = (bf16[8,16,512]{2,1,0:T(8,128)(2,1)S(1)}, bf16[8,16,512]{2,1,0:T(8,128)(2,1)S(1)}, u32[]{:S(2)}, u32[]{:S(2)}) collective-permute-start(bf16[8,16,512]{2,1,0:T(8,128)(2,1)S(1)} %get-tuple-element.54), channel_id=1, source_target_pairs={{0,8},{4,12},{8,0},{12,4},{1,9},{5,13},{9,1},{13,5},{2,10},{6,14},... | collective-permute-start | bytes 393224 | tf_op jit(solution)/shard_map/ppermute | solution.py:230
  94.2 28.1 %collective-permute-start.19 = (bf16[8,16,512]{2,1,0:T(8,128)(2,1)S(1)}, bf16[8,16,512]{2,1,0:T(8,128)(2,1)S(1)}, u32[]{:S(2)}, u32[]{:S(2)}) collective-permute-start(bf16[8,16,512]{2,1,0:T(8,128)(2,1)S(1)} %get-tuple-element.52), channel_id=1, source_target_pairs={{0,4},{4,0},{8,12},{12,8},{1,5},{5,1},{9,13},{13,9},{2,6},{6,2},{1... | collective-permute-start | bytes 393224 | tf_op jit(solution)/shard_map/ppermute | solution.py:230
  (1 other events, 15.3 us)

commit v3 on v2

v3 whole, which is shorter than its diff:
```python
import functools
import jax
import jax.numpy as jnp
from jax import lax
from jax.experimental import pallas as pl
from jax.experimental.pallas import tpu as pltpu
from jax.sharding import PartitionSpec as P

TILE = 128
PARTS = 4
WIDE = 256
ROWS = 16
STEP_F = 4
VMEM_LIMIT = 40 * 1024 * 1024


def spread_kernel(where, modes_ref, down_ref, up_ref, *, parts):
    freq, n_modes = modes_ref.shape
    modes = modes_ref[...]
    freqs = freq // parts

    def pick(shape, axis):
        big = lax.broadcasted_iota(jnp.int32, shape, axis) // ROWS
        small = lax.broadcasted_iota(jnp.int32, shape, 1 - axis)
        if freq in shape:
            piece, within = big // freqs, big % freqs
            big = within
            for j in range(parts):
                big = jnp.where(piece == j, where[j] * freqs + within, big)
        return jnp.where(big == small, 1.0, 0.0).astype(jnp.bfloat16)

    def lane(shape):
        rows = lax.broadcasted_iota(jnp.int32, shape, 0) % ROWS
        columns = lax.broadcasted_iota(jnp.int32, shape, 1) % ROWS
        return rows == columns

    def dot(a, b, dims):
        return lax.dot_general(a, b, (dims, ((), ())), preferred_element_type=jnp.float32)

    tall = dot(pick((n_modes * ROWS, n_modes), 0), modes, ((1,), (1,))).astype(jnp.bfloat16)
    value = dot(tall, pick((freq, freq * ROWS), 1), ((1,), (0,)))
    down_ref[...] = jnp.where(lane(value.shape), value, 0.0).astype(jnp.bfloat16)
    tall = dot(pick((freq * ROWS, freq), 0), modes, ((1,), (0,))).astype(jnp.bfloat16)
    value = dot(tall, pick((n_modes, n_modes * ROWS), 1), ((1,), (0,)))
    up_ref[...] = jnp.where(lane(value.shape), value, 0.0).astype(jnp.bfloat16)


def spread(where, modes, parts):
    freq, n_modes = modes.shape
    vmem = pl.BlockSpec(memory_space=pltpu.VMEM)
    return pl.pallas_call(
        functools.partial(spread_kernel, parts=parts),
        grid_spec=pltpu.PrefetchScalarGridSpec(
            num_scalar_prefetch=1, grid=(), in_specs=[vmem], out_specs=[vmem, vmem]
        ),
        out_shape=[
            jax.ShapeDtypeStruct((n_modes * ROWS, freq * ROWS), jnp.bfloat16),
            jax.ShapeDtypeStruct((freq * ROWS, n_modes * ROWS), jnp.bfloat16),
        ],
        compiler_params=pltpu.CompilerParams(vmem_limit_bytes=VMEM_LIMIT),
        cost_estimate=pl.CostEstimate(flops=1024, bytes_accessed=1024, transcendentals=0),
    )(where, modes)


def project_kernel(where, *refs, pieces, before, last, freqs, rows, step_f):
    count = len(pieces)
    mine, others, refs = refs[:count], refs[count:2 * count], refs[2 * count:]
    beam_ref, refs = refs[0], refs[1:]
    earlier, refs = (refs[0], refs[1:]) if before else (None, refs)
    if last:
        modes_ref, stay_ref, leave_ref, sky, mask, lines = refs
    else:
        sky, mask, lines = refs
    piece, step = pl.program_id(0), pl.program_id(1)
    ell_tiles, _, base = mask.shape
    base_tiles, both = base // TILE, 2 * rows

    @pl.when((piece == 0) & (step == 0))
    def _():
        for b in range(base_tiles):
            for l in range(ell_tiles):
                kept = where[PARTS + 1 + b * ell_tiles + l].astype(jnp.float32)
                mask[l, :, b * TILE:(b + 1) * TILE] = jnp.full((ROWS, TILE), kept, jnp.float32).astype(jnp.bfloat16)

    for which in range(count):

        @pl.when(piece == which)
        def _():
            for u in range(step_f):
                for start in range(0, both, ROWS):
                    from_ref, row = (mine[which], start) if start < rows else (others[which], start - rows)
                    value = from_ref[u, row:row + ROWS, :]
                    for l in range(ell_tiles):
                        lines[u, l, start:start + ROWS, :] = value * mask[l]

    first = piece * freqs + step * step_f
    per = WIDE // TILE
    for u in range(step_f):
        for n in range(ell_tiles // per):
            value = jnp.dot(
                lines[u, n * per:(n + 1) * per].reshape(per * both, base),
                beam_ref[u, :, n * WIDE:(n + 1) * WIDE],
                preferred_element_type=jnp.float32,
            )
            for k in range(per):
                at = n * WIDE + k * TILE
                sky[first + u, :, at:at + TILE] = value[
                    k * both:(k + 1) * both, k * TILE:(k + 1) * TILE
                ].astype(jnp.bfloat16)

    if not last:
        return

    @pl.when((piece == count - 1) & (step == freqs // step_f - 1))
    def _():
        own = where[PARTS]
        split = before * ROWS
        for ref, low in ((stay_ref, (1 - own) * rows), (leave_ref, own * rows)):
            for g in range(rows // ROWS):
                start = pl.multiple_of(low + g * ROWS, ROWS)
                value = jnp.zeros((modes_ref.shape[0], sky.shape[2]), jnp.float32)
                for part, low_f, high_f in ((earlier, 0, split), (sky, split, modes_ref.shape[1])):
                    if part is not None:
                        value += jnp.dot(
                            modes_ref[:, low_f:high_f],
                            part[:, pl.ds(start, ROWS), :].reshape(high_f - low_f, sky.shape[2]),
                            preferred_element_type=jnp.float32,
                        )
                ref[:, g * ROWS:(g + 1) * ROWS, :] = value.astype(jnp.bfloat16).reshape(
                    ref.shape[0], ROWS, ref.shape[2]
                )


def project(where, mine, others, beam, pieces, n_modes, earlier=None, modes=None):
    freqs, rows, base = mine[0].shape
    ell = beam.shape[2]
    step_f = STEP_F if len(pieces) > 1 else STEP_F // 2
    steps = freqs // step_f
    base_piece, last = pieces[0], modes is not None

    def block_of(which):
        def index(j, i, s):
            return (jnp.where(j == which, i, jnp.where(j < which, 0, steps - 1)), 0, 0)

        return pl.BlockSpec((step_f, rows, base), index)

    def whole(shape):
        return pl.BlockSpec(shape, lambda j, i, s: (0,) * len(shape))

    in_specs = [block_of(j) for j in range(len(pieces))] * 2
    in_specs += [pl.BlockSpec((step_f, base, ell), lambda j, i, s: (s[base_piece + j] * steps + i, 0, 0))]
    operands = [*mine, *others, beam]
    sky = (len(pieces) * freqs, 2 * rows, ell)
    scratch = [
        pltpu.VMEM((ell // TILE, ROWS, base), jnp.bfloat16),
        pltpu.VMEM((step_f, ell // TILE, 2 * rows, base), jnp.bfloat16),
    ]
    before = 0 if earlier is None else earlier.shape[0]
    if before:
        in_specs, operands = in_specs + [whole(earlier.shape)], operands + [earlier]
    if last:
        in_specs, operands = in_specs + [whole(modes.shape)], operands + [modes]
        scratch = [pltpu.VMEM(sky, jnp.bfloat16)] + scratch
        shapes = [(n_modes, rows, ell)] * 2
    else:
        shapes = [sky]
    return pl.pallas_call(
        functools.partial(
            project_kernel, pieces=pieces, before=before, last=last, freqs=freqs, rows=rows, step_f=step_f
        ),
        grid_spec=pltpu.PrefetchScalarGridSpec(
            num_scalar_prefetch=1,
            grid=(len(pieces), steps),
            in_specs=in_specs,
            out_specs=[whole(shape) for shape in shapes],
            scratch_shapes=scratch,
        ),
        out_shape=[jax.ShapeDtypeStruct(shape, jnp.bfloat16) for shape in shapes],
        compiler_params=pltpu.CompilerParams(vmem_limit_bytes=VMEM_LIMIT),
        cost_estimate=pl.CostEstimate(flops=1024, bytes_accessed=1024, transcendentals=0),
    )(where, *operands)


def restore_kernel(stay_ref, came_ref, ratio_ref, modes_ref, *outs):
    n_modes, rows, ell = stay_ref.shape
    size = outs[0].shape[0] * ROWS
    for g in range(rows // ROWS):
        span = slice(g * ROWS, (g + 1) * ROWS)
        total = stay_ref[:, span, :].astype(jnp.float32) + came_ref[:, span, :].astype(jnp.float32)
        weighted = (total * ratio_ref[...]).astype(jnp.bfloat16).reshape(n_modes * ROWS, ell)
        for which, out in enumerate(outs):
            value = jnp.dot(
                modes_ref[which * size:(which + 1) * size, :], weighted, preferred_element_type=jnp.float32
            )
            out[:, span, :] = value.astype(jnp.bfloat16).reshape(out.shape[0], ROWS, ell)


def restore(stay, came, ratios, modes, parts, freqs):
    _, rows, ell = stay.shape
    vmem = pl.BlockSpec(memory_space=pltpu.VMEM)
    return pl.pallas_call(
        restore_kernel,
        in_specs=[vmem] * 4,
        out_specs=[vmem] * parts,
        out_shape=[jax.ShapeDtypeStruct((freqs, rows, ell), jnp.bfloat16)] * parts,
        compiler_params=pltpu.CompilerParams(vmem_limit_bytes=VMEM_LIMIT),
        cost_estimate=pl.CostEstimate(flops=1024, bytes_accessed=1024, transcendentals=0),
    )(stay, came, ratios, modes)


def place_kernel(where, *refs, first):
    pieces, out, sems = refs[:PARTS], refs[-2], refs[-1]
    rows = pieces[0].shape[1]
    copies = [
        pltpu.make_async_copy(pieces[j], out.at[:, where[j], first:first + rows, :], sems.at[j])
        for j in range(PARTS)
    ]
    for copy in copies:
        copy.start()
    for copy in copies:
        copy.wait()


def place(where, pieces, first, shape, into=None):
    extra = [] if into is None else [into]
    anywhere = pl.BlockSpec(memory_space=pl.ANY)
    return pl.pallas_call(
        functools.partial(place_kernel, first=first),
        grid_spec=pltpu.PrefetchScalarGridSpec(
            num_scalar_prefetch=1,
            grid=(),
            in_specs=[pl.BlockSpec(memory_space=pltpu.VMEM)] * PARTS + [anywhere] * len(extra),
            out_specs=anywhere,
            scratch_shapes=[pltpu.SemaphoreType.DMA((PARTS,))],
        ),
        out_shape=jax.ShapeDtypeStruct(shape, jnp.bfloat16),
        input_output_aliases={PARTS + 1: 0} if extra else {},
        compiler_params=pltpu.CompilerParams(vmem_limit_bytes=VMEM_LIMIT),
        cost_estimate=pl.CostEstimate(flops=1024, bytes_accessed=1024, transcendentals=0),
    )(where, *pieces, *extra)


def chunked(visibility, beam_transfer, tile_mask, first_block, eigen_modes, signal_noise, chunks):
    freqs, parts, rows_all, base = visibility.shape
    _, freq_total, _, ell = beam_transfer.shape
    n_modes = eigen_modes.shape[2]
    ell_tiles = ell // TILE
    z, x, p = lax.axis_index("fm"), lax.axis_index("kl"), lax.axis_index("pol")
    other = [(0, 1), (1, 0)]

    def along_z(value, j):
        return lax.ppermute(value, "fm", [(i, i ^ j) for i in range(parts)])

    def along_x(value):
        return lax.ppermute(value, "kl", other)

    def cut(chunk, j):
        first, rows = chunk
        return lax.dynamic_slice(visibility, (0, z ^ j, first, 0), (freqs, 1, rows, base)).reshape(freqs, rows, base)

    order = jnp.stack([z ^ j for j in range(parts)]).astype(jnp.int32)
    block_ids = x * ell_tiles + jnp.arange(ell_tiles, dtype=jnp.int32)
    keep = tile_mask[0] * (first_block[0] <= block_ids).astype(jnp.int32)[None, :]
    where = jnp.concatenate([order, (x == p).astype(jnp.int32)[None], keep.reshape(-1)])
    down, up = spread(where, eigen_modes[0], parts)
    ratio = signal_noise[0] / (1.0 + signal_noise[0])
    ratios = jnp.broadcast_to(ratio[:, None, None], (n_modes, 1, ell))
    beam = beam_transfer.reshape(freq_total, base, ell)
    shape = (freqs, parts, rows_all, ell)

    a, b = [[cut(chunk, j) for j in range(parts)] for chunk in chunks]

    def half(mine, others, pieces, earlier=None, modes=None):
        return project(
            where, [mine[j] for j in pieces], [others[j] for j in pieces], beam, pieces, n_modes, earlier, modes
        )

    ga, gb, xa, xb, ba, bb = ({} for _ in range(6))
    ga[0], gb[0] = a[0], b[0]
    for j in (2, 3, 1):
        ga[j] = along_z(a[j], j)
    xa[0], xa[1], xb[0] = along_x(ga[0]), along_x(ga[1]), along_x(gb[0])
    ga, gb, xa, xb, b, where, beam, down, up = lax.optimization_barrier((ga, gb, xa, xb, b, where, beam, down, up))
    gb[2], gb[1] = along_z(b[2], 2), along_z(b[1], 1)
    xa[2], xa[3] = along_x(ga[2]), along_x(ga[3])
    xb[1] = along_x(gb[1])
    sky_a, = half(ga, xa, (0, 1))
    stay_a, leave_a = half(ga, xa, (2, 3), sky_a, down)
    gb, xb, b, stay_a, leave_a = lax.optimization_barrier((gb, xb, b, stay_a, leave_a))
    gb[3] = along_z(b[3], 3)
    xb[2] = along_x(gb[2])
    outs_a = restore(stay_a, lax.ppermute(leave_a, "pol", other), ratios, up, parts, freqs)
    sky_b, = half(gb, xb, (0, 1))
    gb, xb, outs_a, sky_b = lax.optimization_barrier((gb, xb, outs_a, sky_b))
    xb[3] = along_x(gb[3])
    ba = [outs_a[0]] + [along_z(outs_a[j], j) for j in range(1, parts)]
    stay_b, leave_b = half(gb, xb, (2, 3), sky_b, down)
    ba, stay_b, leave_b = lax.optimization_barrier((ba, stay_b, leave_b))
    outs_b = restore(stay_b, lax.ppermute(leave_b, "pol", other), ratios, up, parts, freqs)
    bb = [outs_b[0]] + [along_z(outs_b[j], j) for j in range(1, parts)]
    result = place(where, ba, chunks[0][0], shape)
    return place(where, bb, chunks[1][0], shape, into=result)


def plain(visibility, beam_transfer, tile_mask, first_block, eigen_modes, signal_noise):
    owned_modes, freq_total, base_half, ell_local = beam_transfer.shape
    base_tiles, ell_tiles = base_half // TILE, ell_local // TILE
    block_ids = lax.axis_index("kl") * ell_tiles + jnp.arange(ell_tiles, dtype=jnp.int32)
    inside = (first_block[:, None] <= block_ids[None, :]).astype(jnp.int32)
    keep_tiles = tile_mask * inside[:, None, :]
    shaped = beam_transfer.reshape(owned_modes, freq_total, base_tiles, TILE, ell_tiles, TILE)
    masked_beam = shaped * keep_tiles.astype(jnp.bfloat16)[:, None, :, None, :, None]
    masked_beam = masked_beam.reshape(owned_modes, freq_total, base_half, ell_local)
    arrived = lax.all_to_all(visibility, "fm", split_axis=1, concat_axis=0, tiled=True)
    partial_value = jnp.einsum(
        "fmrb,mfbl->fmrl",
        lax.all_gather(arrived, "kl", axis=2, tiled=True),
        masked_beam,
        preferred_element_type=jnp.float32,
    )
    sky_sum = lax.psum_scatter(
        partial_value.astype(jnp.bfloat16), "pol", scatter_dimension=2, tiled=True
    ).astype(jnp.float32)
    modes_float = eigen_modes.astype(jnp.float32)
    coeffs = jnp.einsum("mfk,fmrl->mkrl", modes_float, sky_sum, precision=lax.Precision.HIGHEST)
    ratios = signal_noise / (1.0 + signal_noise)
    weighted = (coeffs * ratios[:, :, None, None]).astype(jnp.bfloat16)
    filtered = jnp.einsum(
        "mfk,mkrl->fmrl", eigen_modes, weighted, preferred_element_type=jnp.float32
    ).astype(jnp.bfloat16)
    return lax.all_to_all(filtered, "fm", split_axis=0, concat_axis=1, tiled=True)


def per_device(*args, sizes):
    visibility, beam_transfer = args[0], args[1]
    freqs, modes, rows, _ = visibility.shape
    fits = (
        sizes["kl"] == 2
        and sizes["pol"] == 2
        and modes == sizes["fm"] == PARTS
        and beam_transfer.shape[0] == 1
        and rows % ROWS == 0
        and rows >= 2 * ROWS
        and freqs % STEP_F == 0
        and beam_transfer.shape[3] % WIDE == 0
    )
    if not fits:
        return plain(*args)
    return chunked(*args, chunks=[(0, ROWS), (ROWS, rows - ROWS)])


def solution(mesh):
    placed = (
        P(("group", "fm"), None, "kl", "pol"),
        P(("group", "fm"), None, "pol", "kl"),
        P("fm", "pol", "kl"),
        P("fm"),
        P(("group", "fm"), None, None),
        P(("group", "fm"), None),
    )
    return jax.shard_map(
        functools.partial(per_device, sizes=dict(mesh.shape)),
        mesh=mesh,
        in_specs=placed,
        out_specs=P(("group", "fm"), None, "pol", "kl"),
        check_vma=False,
    )
```

time: 128 us -> 110 us (0.86)
  the two profiles are of different devices: /device:TPU:0 before, /device:TPU:12 now
where the time goes in v3:
time: 110 us; the launch traced here: 109 us
  waiting for transfers between devices  53.4 us (49%)
  Pallas kernels  29.4 us (27%)
  starting transfers between devices  22.6 us (21%)
  local copies, waits for them, and re-layouts  2.86 us (3%)
    ppermute x12, waiting for transfers between devices, along_z(): return lax.ppermute(value, 'fm', [(i, i ^ j) for i in range(parts)])  42.6 us
    pallas_call x4, Pallas kernels, project(): pl.pallas_call(functools.partial(project_kernel, pieces=pieces, before=be...  24 us
    ppermute x12, starting transfers between devices, along_z(): return lax.ppermute(value, 'fm', [(i, i ^ j) for i in range(parts)])  15.9 us
    ppermute x8, waiting for transfers between devices, along_x(): return lax.ppermute(value, 'kl', other)  8.53 us
    ppermute x8, starting transfers between devices, along_x(): return lax.ppermute(value, 'kl', other)  6.66 us
    pallas_call x2, Pallas kernels, place(): pl.pallas_call(functools.partial(place_kernel, first=first), grid_spec=pl...  2.9 us
    reshape x2, local copies, waits for them, and re-layouts, cut(): lax.dynamic_slice(visibility, (0, z ^ j, first, 0), (freqs, 1, rows, base))  2.41 us
    ppermute x1, waiting for transfers between devices, chunked(): lax.ppermute(leave_b, 'pol', other)  2.28 us
  transfers between devices with their start and end apart: 22, of which 12 were waited for; matrix products, arithmetic and copies ran while one was open for 2% of the time, Pallas kernels for 25%

profile of v3, /device:TPU:12, one launch (start us, length us, event | category | flops | bytes accessed | tf_op | source)
XLA Modules:
  0.0 109.1 jit_solution(16834354067618068033)
XLA Ops:
  2.9 1.6 %collective-permute-start.5 = (bf16[8,32,512]{2,1,0:T(8,128)(2,1)S(1)}, bf16[8,32,512]{2,1,0:T(8,128)(2,1)S(1)}, u32[]{:S(2)}, u32[]{:S(2)}) collective-permute-start(bf16[8,32,512]{2,1,0:T(8,128)(2,1)S(1)} %get-tuple-element.74.refs_0_), channel_id=1, source_target_pairs={{0,2},{2,0},{1,3},{3,1},{4,6},{6,4},{5,7},{7,5},{8,10},{10,8},{9,1... | collective-permute-start | bytes 786440 | tf_op jit(solution)/shard_map/ppermute | solution.py:255
  4.5 2.7 %collective-permute-start.2 = (bf16[8,16,512]{2,1,0:T(8,128)(2,1)S(1)}, bf16[8,16,512]{2,1,0:T(8,128)(2,1)S(1)}, u32[]{:S(2)}, u32[]{:S(2)}) collective-permute-start(bf16[8,16,512]{2,1,0:T(8,128)(2,1)S(1)} %get-tuple-element.111), channel_id=1, source_target_pairs={{0,12},{4,8},{8,4},{12,0},{1,13},{5,9},{9,5},{13,1},{2,14},{6,10},... | collective-permute-start | bytes 393224 | tf_op jit(solution)/shard_map/ppermute | solution.py:252
  9.0 1.5 %collective-permute-start.4 = (bf16[8,16,512]{2,1,0:T(8,128)(2,1)S(1)}, bf16[8,16,512]{2,1,0:T(8,128)(2,1)S(1)}, u32[]{:S(2)}, u32[]{:S(2)}) collective-permute-start(bf16[8,16,512]{2,1,0:T(8,128)(2,1)S(1)} %collective-permute-done.refs_1_), channel_id=1, source_target_pairs={{0,2},{2,0},{1,3},{3,1},{4,6},{6,4},{5,7},{7,5},{8,10},{10,8},{9,1... | collective-permute-start | bytes 393224 | tf_op jit(solution)/shard_map/ppermute | solution.py:255
  12.7 4.2 %collective-permute-done.2.refs_1_ = bf16[8,16,512]{2,1,0:T(8,128)(2,1)S(1)} collective-permute-done((bf16[8,16,512]{2,1,0:T(8,128)(2,1)S(1)}, bf16[8,16,512]{2,1,0:T(8,128)(2,1)S(1)}, u32[]{:S(2)}, u32[]{:S(2)}) %collective-permute-start.2) | collective-permute-done | bytes 131104 | tf_op jit(solution)/shard_map/ppermute | solution.py:252
  17.8 2.3 %collective-permute-start.6 = (bf16[8,32,512]{2,1,0:T(8,128)(2,1)S(1)}, bf16[8,32,512]{2,1,0:T(8,128)(2,1)S(1)}, u32[]{:S(2)}, u32[]{:S(2)}) collective-permute-start(bf16[8,32,512]{2,1,0:T(8,128)(2,1)S(1)} %get-tuple-element.60), channel_id=1, source_target_pairs={{0,4},{4,0},{8,12},{12,8},{1,5},{5,1},{9,13},{13,9},{2,6},{6,2},{1... | collective-permute-start | bytes 786440 | tf_op jit(solution)/shard_map/ppermute | solution.py:252
  20.1 1.3 %collective-permute-start.7 = (bf16[8,32,512]{2,1,0:T(8,128)(2,1)S(1)}, bf16[8,32,512]{2,1,0:T(8,128)(2,1)S(1)}, u32[]{:S(2)}, u32[]{:S(2)}) collective-permute-start(bf16[8,32,512]{2,1,0:T(8,128)(2,1)S(1)} %get-tuple-element.61), channel_id=1, source_target_pairs={{0,8},{4,12},{8,0},{12,4},{1,9},{5,13},{9,1},{13,5},{2,10},{6,14},... | collective-permute-start | bytes 786440 | tf_op jit(solution)/shard_map/ppermute | solution.py:252
  21.4 8.9 %collective-permute-done.6.refs_1_ = bf16[8,32,512]{2,1,0:T(8,128)(2,1)S(1)} collective-permute-done((bf16[8,32,512]{2,1,0:T(8,128)(2,1)S(1)}, bf16[8,32,512]{2,1,0:T(8,128)(2,1)S(1)}, u32[]{:S(2)}, u32[]{:S(2)}) %collective-permute-start.6) | collective-permute-done | bytes 262176 | tf_op jit(solution)/shard_map/ppermute | solution.py:252
  30.6 1.6 %collective-permute-start.9 = (bf16[8,16,512]{2,1,0:T(8,128)(2,1)S(1)}, bf16[8,16,512]{2,1,0:T(8,128)(2,1)S(1)}, u32[]{:S(2)}, u32[]{:S(2)}) collective-permute-start(bf16[8,16,512]{2,1,0:T(8,128)(2,1)S(1)} %collective-permute-done.1.refs_0_), channel_id=1, source_target_pairs={{0,2},{2,0},{1,3},{3,1},{4,6},{6,4},{5,7},{7,5},{8,10},{10,8},{9,1... | collective-permute-start | bytes 393224 | tf_op jit(solution)/shard_map/ppermute | solution.py:255
  32.6 5.6 %shard_map.65.refs_5_ = bf16[16,32,512]{2,1,0:T(8,128)(2,1)S(1)} custom-call(s32[21]{0:T(128)S(1)} %concatenate.3.where, bf16[8,16,512]{2,1,0:T(8,128)(2,1)S(1)} %get-tuple-element.67.refs_0_, bf16[8,16,512]{2,1,0:T(8,128)(2,1)S(1)} %collective-permute-done.refs_1_, bf16[8,16,512]{2,1,0:T(8,128)(2,1)S(1)} %collective-permute-done.3.refs_2_, ...), custom_call_target="tpu_custom_call" | custom-call | flops 1024 | bytes 1024 | tf_op jit(solution)/shard_map/pallas_call | solution.py:167
  38.3 3.0 %collective-permute-done.9.refs_2_ = bf16[8,16,512]{2,1,0:T(8,128)(2,1)S(1)} collective-permute-done((bf16[8,16,512]{2,1,0:T(8,128)(2,1)S(1)}, bf16[8,16,512]{2,1,0:T(8,128)(2,1)S(1)}, u32[]{:S(2)}, u32[]{:S(2)}) %collective-permute-start.9) | collective-permute-done | bytes 131104 | tf_op jit(solution)/shard_map/ppermute | solution.py:255
  41.3 1.4 %collective-permute-done.10.refs_3_ = bf16[8,16,512]{2,1,0:T(8,128)(2,1)S(1)} collective-permute-done((bf16[8,16,512]{2,1,0:T(8,128)(2,1)S(1)}, bf16[8,16,512]{2,1,0:T(8,128)(2,1)S(1)}, u32[]{:S(2)}, u32[]{:S(2)}) %collective-permute-start.10) | collective-permute-done | bytes 131104 | tf_op jit(solution)/shard_map/ppermute | solution.py:255
  42.7 6.2 %shard_map.66 = (bf16[24,16,512]{2,1,0:T(8,128)(2,1)S(1)}, bf16[24,16,512]{2,1,0:T(8,128)(2,1)S(1)}) custom-call(s32[21]{0:T(128)S(1)} %concatenate.3.where, bf16[8,16,512]{2,1,0:T(8,128)(2,1)S(1)} %collective-permute-done.1.refs_0_, bf16[8,16,512]{2,1,0:T(8,128)(2,1)S(1)} %collective-permute-done.2.refs_1_, ...), custom_call_target="tpu_custom_call" | custom-call | flops 1024 | bytes 1024 | tf_op jit(solution)/shard_map/pallas_call | solution.py:167
  50.3 5.6 %shard_map.68.refs_5_ = bf16[16,64,512]{2,1,0:T(8,128)(2,1)S(1)} custom-call(s32[21]{0:T(128)S(1)} %concatenate.3.where, bf16[8,32,512]{2,1,0:T(8,128)(2,1)S(1)} %get-tuple-element.74.refs_0_, bf16[8,32,512]{2,1,0:T(8,128)(2,1)S(1)} %collective-permute-done.6.refs_1_, bf16[8,32,512]{2,1,0:T(8,128)(2,1)S(1)} %collective-permute-done.5.refs_2_, ...), custom_call_target="tpu_custom_call" | custom-call | flops 1024 | bytes 1024 | tf_op jit(solution)/shard_map/pallas_call | solution.py:167
  56.5 6.8 %collective-permute-done.11.refs_1_ = bf16[8,32,512]{2,1,0:T(8,128)(2,1)S(1)} collective-permute-done((bf16[8,32,512]{2,1,0:T(8,128)(2,1)S(1)}, bf16[8,32,512]{2,1,0:T(8,128)(2,1)S(1)}, u32[]{:S(2)}, u32[]{:S(2)}) %collective-permute-start.11) | collective-permute-done | bytes 262176 | tf_op jit(solution)/shard_map/ppermute | solution.py:252
  63.6 2.4 %collective-permute-start.15 = (bf16[8,16,512]{2,1,0:T(8,128)(2,1)S(1)}, bf16[8,16,512]{2,1,0:T(8,128)(2,1)S(1)}, u32[]{:S(2)}, u32[]{:S(2)}) collective-permute-start(bf16[8,16,512]{2,1,0:T(8,128)(2,1)S(1)} %get-tuple-element.89), channel_id=1, source_target_pairs={{0,8},{4,12},{8,0},{12,4},{1,9},{5,13},{9,1},{13,5},{2,10},{6,14},... | collective-permute-start | bytes 393224 | tf_op jit(solution)/shard_map/ppermute | solution.py:252
  67.1 4.1 %collective-permute-done.17.refs_3_ = bf16[8,32,512]{2,1,0:T(8,128)(2,1)S(1)} collective-permute-done((bf16[8,32,512]{2,1,0:T(8,128)(2,1)S(1)}, bf16[8,32,512]{2,1,0:T(8,128)(2,1)S(1)}, u32[]{:S(2)}, u32[]{:S(2)}) %collective-permute-start.17) | collective-permute-done | bytes 262176 | tf_op jit(solution)/shard_map/ppermute | solution.py:255
  71.2 6.6 %shard_map.69 = (bf16[24,32,512]{2,1,0:T(8,128)(2,1)S(1)}, bf16[24,32,512]{2,1,0:T(8,128)(2,1)S(1)}) custom-call(s32[21]{0:T(128)S(1)} %concatenate.3.where, bf16[8,32,512]{2,1,0:T(8,128)(2,1)S(1)} %collective-permute-done.7.refs_0_, bf16[8,32,512]{2,1,0:T(8,128)(2,1)S(1)} %collective-permute-done.11.refs_1_, ...), custom_call_target="tpu_custom_call" | custom-call | flops 1024 | bytes 1024 | tf_op jit(solution)/shard_map/pallas_call | solution.py:167
  78.0 2.3 %collective-permute-done.18.came_ref = bf16[24,32,512]{2,1,0:T(8,128)(2,1)S(1)} collective-permute-done((bf16[24,32,512]{2,1,0:T(8,128)(2,1)S(1)}, bf16[24,32,512]{2,1,0:T(8,128)(2,1)S(1)}, u32[]{:S(2)}, u32[]{:S(2)}) %collective-permute-start.18) | collective-permute-done | bytes 786464 | tf_op jit(solution)/shard_map/ppermute | solution.py:299
  81.2 2.4 %collective-permute-start.20 = (bf16[8,32,512]{2,1,0:T(8,128)(2,1)S(1)}, bf16[8,32,512]{2,1,0:T(8,128)(2,1)S(1)}, u32[]{:S(2)}, u32[]{:S(2)}) collective-permute-start(bf16[8,32,512]{2,1,0:T(8,128)(2,1)S(1)} %get-tuple-element.101), channel_id=1, source_target_pairs={{0,8},{4,12},{8,0},{12,4},{1,9},{5,13},{9,1},{13,5},{2,10},{6,14},... | collective-permute-start | bytes 786440 | tf_op jit(solution)/shard_map/ppermute | solution.py:252
  84.6 1.4 %shard_map.71.refs_4_ = bf16[8,4,48,512]{3,2,1,0:T(8,128)(2,1)} custom-call(s32[21]{0:T(128)S(1)} %concatenate.3.where, bf16[8,16,512]{2,1,0:T(8,128)(2,1)S(1)} %get-tuple-element.103.refs_0_, bf16[8,16,512]{2,1,0:T(8,128)(2,1)S(1)} %collective-permute-done.14.refs_1_, bf16[8,16,512]{2,1,0:T(8,128)(2,1)S(1)} %collective-permute-done.15.refs_2_, ...), custom_call_target="tpu_custom_call" | custom-call | flops 1024 | bytes 1024 | tf_op jit(solution)/shard_map/pallas_call | solution.py:227
  86.0 6.0 %collective-permute-done.19.refs_1_ = bf16[8,32,512]{2,1,0:T(8,128)(2,1)S(1)} collective-permute-done((bf16[8,32,512]{2,1,0:T(8,128)(2,1)S(1)}, bf16[8,32,512]{2,1,0:T(8,128)(2,1)S(1)}, u32[]{:S(2)}, u32[]{:S(2)}) %collective-permute-start.19) | collective-permute-done | bytes 262176 | tf_op jit(solution)/shard_map/ppermute | solution.py:252
  92.0 9.5 %collective-permute-done.20.refs_2_ = bf16[8,32,512]{2,1,0:T(8,128)(2,1)S(1)} collective-permute-done((bf16[8,32,512]{2,1,0:T(8,128)(2,1)S(1)}, bf16[8,32,512]{2,1,0:T(8,128)(2,1)S(1)}, u32[]{:S(2)}, u32[]{:S(2)}) %collective-permute-start.20) | collective-permute-done | bytes 262176 | tf_op jit(solution)/shard_map/ppermute | solution.py:252
  101.5 6.1 %collective-permute-done.21.refs_3_ = bf16[8,32,512]{2,1,0:T(8,128)(2,1)S(1)} collective-permute-done((bf16[8,32,512]{2,1,0:T(8,128)(2,1)S(1)}, bf16[8,32,512]{2,1,0:T(8,128)(2,1)S(1)}, u32[]{:S(2)}, u32[]{:S(2)}) %collective-permute-start.21) | collective-permute-done | bytes 262176 | tf_op jit(solution)/shard_map/ppermute | solution.py:252
  107.6 1.5 %shard_map.72 = bf16[8,4,48,512]{3,2,1,0:T(8,128)(2,1)} custom-call(s32[21]{0:T(128)S(1)} %concatenate.3.where, bf16[8,32,512]{2,1,0:T(8,128)(2,1)S(1)} %get-tuple-element.99.refs_0_, bf16[8,32,512]{2,1,0:T(8,128)(2,1)S(1)} %collective-permute-done.19.refs_1_, ...), custom_call_target="tpu_custom_call", output_to_operand_aliasing={{}: (5, {})} | custom-call | flops 1024 | bytes 1024 | tf_op jit(solution)/shard_map/pallas_call | solution.py:227
  (46 shorter events, 13.5 us)
Async XLA Ops:
  0.0 11.3 %copy-start = (bf16[1,32,24]{1,2,0:T(8,128)(2,1)S(1)}, bf16[1,32,24]{1,2,0:T(8,128)(2,1)}, u32[]{:S(2)}) copy-start(bf16[1,32,24]{1,2,0:T(8,128)(2,1)} %param.10) | copy-start | bytes 4612
  1.2 7.8 %collective-permute-start = (bf16[8,16,512]{2,1,0:T(8,128)(2,1)S(1)}, bf16[8,16,512]{2,1,0:T(8,128)(2,1)S(1)}, u32[]{:S(2)}, u32[]{:S(2)}) collective-permute-start(bf16[8,16,512]{2,1,0:T(8,128)(2,1)S(1)} %get-tuple-element.113), channel_id=1, source_target_pairs={{0,4},{4,0},{8,12},{12,8},{1,5},{5,1},{9,13},{13,9},{2,6},{6,2},{1... | collective-permute-start | bytes 393224 | tf_op jit(solution)/shard_map/ppermute | solution.py:252
  2.9 14.9 %collective-permute-start.5 = (bf16[8,32,512]{2,1,0:T(8,128)(2,1)S(1)}, bf16[8,32,512]{2,1,0:T(8,128)(2,1)S(1)}, u32[]{:S(2)}, u32[]{:S(2)}) collective-permute-start(bf16[8,32,512]{2,1,0:T(8,128)(2,1)S(1)} %get-tuple-element.74.refs_0_), channel_id=1, source_target_pairs={{0,2},{2,0},{1,3},{3,1},{4,6},{6,4},{5,7},{7,5},{8,10},{10,8},{9,1... | collective-permute-start | bytes 786440 | tf_op jit(solution)/shard_map/ppermute | solution.py:255
  4.5 12.4 %collective-permute-start.2 = (bf16[8,16,512]{2,1,0:T(8,128)(2,1)S(1)}, bf16[8,16,512]{2,1,0:T(8,128)(2,1)S(1)}, u32[]{:S(2)}, u32[]{:S(2)}) collective-permute-start(bf16[8,16,512]{2,1,0:T(8,128)(2,1)S(1)} %get-tuple-element.111), channel_id=1, source_target_pairs={{0,12},{4,8},{8,4},{12,0},{1,13},{5,9},{9,5},{13,1},{2,14},{6,10},... | collective-permute-start | bytes 393224 | tf_op jit(solution)/shard_map/ppermute | solution.py:252
  7.2 10.6 %collective-permute-start.1 = (bf16[8,16,512]{2,1,0:T(8,128)(2,1)S(1)}, bf16[8,16,512]{2,1,0:T(8,128)(2,1)S(1)}, u32[]{:S(2)}, u32[]{:S(2)}) collective-permute-start(bf16[8,16,512]{2,1,0:T(8,128)(2,1)S(1)} %get-tuple-element.112), channel_id=1, source_target_pairs={{0,8},{4,12},{8,0},{12,4},{1,9},{5,13},{9,1},{13,5},{2,10},{6,14},... | collective-permute-start | bytes 393224 | tf_op jit(solution)/shard_map/ppermute | solution.py:252
  8.4 9.4 %collective-permute-start.3 = (bf16[8,16,512]{2,1,0:T(8,128)(2,1)S(1)}, bf16[8,16,512]{2,1,0:T(8,128)(2,1)S(1)}, u32[]{:S(2)}, u32[]{:S(2)}) collective-permute-start(bf16[8,16,512]{2,1,0:T(8,128)(2,1)S(1)} %get-tuple-element.67.refs_0_), channel_id=1, source_target_pairs={{0,2},{2,0},{1,3},{3,1},{4,6},{6,4},{5,7},{7,5},{8,10},{10,8},{9,1... | collective-permute-start | bytes 393224 | tf_op jit(solution)/shard_map/ppermute | solution.py:255
  9.0 8.9 %collective-permute-start.4 = (bf16[8,16,512]{2,1,0:T(8,128)(2,1)S(1)}, bf16[8,16,512]{2,1,0:T(8,128)(2,1)S(1)}, u32[]{:S(2)}, u32[]{:S(2)}) collective-permute-start(bf16[8,16,512]{2,1,0:T(8,128)(2,1)S(1)} %collective-permute-done.refs_1_), channel_id=1, source_target_pairs={{0,2},{2,0},{1,3},{3,1},{4,6},{6,4},{5,7},{7,5},{8,10},{10,8},{9,1... | collective-permute-start | bytes 393224 | tf_op jit(solution)/shard_map/ppermute | solution.py:255
  17.8 12.4 %collective-permute-start.6 = (bf16[8,32,512]{2,1,0:T(8,128)(2,1)S(1)}, bf16[8,32,512]{2,1,0:T(8,128)(2,1)S(1)}, u32[]{:S(2)}, u32[]{:S(2)}) collective-permute-start(bf16[8,32,512]{2,1,0:T(8,128)(2,1)S(1)} %get-tuple-element.60), channel_id=1, source_target_pairs={{0,4},{4,0},{8,12},{12,8},{1,5},{5,1},{9,13},{13,9},{2,6},{6,2},{1... | collective-permute-start | bytes 786440 | tf_op jit(solution)/shard_map/ppermute | solution.py:252
  20.1 28.8 %collective-permute-start.7 = (bf16[8,32,512]{2,1,0:T(8,128)(2,1)S(1)}, bf16[8,32,512]{2,1,0:T(8,128)(2,1)S(1)}, u32[]{:S(2)}, u32[]{:S(2)}) collective-permute-start(bf16[8,32,512]{2,1,0:T(8,128)(2,1)S(1)} %get-tuple-element.61), channel_id=1, source_target_pairs={{0,8},{4,12},{8,0},{12,4},{1,9},{5,13},{9,1},{13,5},{2,10},{6,14},... | collective-permute-start | bytes 786440 | tf_op jit(solution)/shard_map/ppermute | solution.py:252
  30.2 18.6 %collective-permute-start.8 = (bf16[8,32,512]{2,1,0:T(8,128)(2,1)S(1)}, bf16[8,32,512]{2,1,0:T(8,128)(2,1)S(1)}, u32[]{:S(2)}, u32[]{:S(2)}) collective-permute-start(bf16[8,32,512]{2,1,0:T(8,128)(2,1)S(1)} %collective-permute-done.6.refs_1_), channel_id=1, source_target_pairs={{0,2},{2,0},{1,3},{3,1},{4,6},{6,4},{5,7},{7,5},{8,10},{10,8},{9,1... | collective-permute-start | bytes 786440 | tf_op jit(solution)/shard_map/ppermute | solution.py:255
  30.6 10.7 %collective-permute-start.9 = (bf16[8,16,512]{2,1,0:T(8,128)(2,1)S(1)}, bf16[8,16,512]{2,1,0:T(8,128)(2,1)S(1)}, u32[]{:S(2)}, u32[]{:S(2)}) collective-permute-start(bf16[8,16,512]{2,1,0:T(8,128)(2,1)S(1)} %collective-permute-done.1.refs_0_), channel_id=1, source_target_pairs={{0,2},{2,0},{1,3},{3,1},{4,6},{6,4},{5,7},{7,5},{8,10},{10,8},{9,1... | collective-permute-start | bytes 393224 | tf_op jit(solution)/shard_map/ppermute | solution.py:255
  32.3 10.4 %collective-permute-start.10 = (bf16[8,16,512]{2,1,0:T(8,128)(2,1)S(1)}, bf16[8,16,512]{2,1,0:T(8,128)(2,1)S(1)}, u32[]{:S(2)}, u32[]{:S(2)}) collective-permute-start(bf16[8,16,512]{2,1,0:T(8,128)(2,1)S(1)} %collective-permute-done.2.refs_1_), channel_id=1, source_target_pairs={{0,2},{2,0},{1,3},{3,1},{4,6},{6,4},{5,7},{7,5},{8,10},{10,8},{9,1... | collective-permute-start | bytes 393224 | tf_op jit(solution)/shard_map/ppermute | solution.py:255
  38.2 12.0 %copy-start.2 = (f32[1,24]{1,0:T(1,128)S(1)}, f32[1,24]{1,0:T(1,128)}, u32[]{:S(2)}) copy-start(f32[1,24]{1,0:T(1,128)} %param.11) | copy-start | bytes 292
  48.9 7.0 %collective-permute-start.13 = (bf16[24,16,512]{2,1,0:T(8,128)(2,1)S(1)}, bf16[24,16,512]{2,1,0:T(8,128)(2,1)S(1)}, u32[]{:S(2)}, u32[]{:S(2)}) collective-permute-start(bf16[24,16,512]{2,1,0:T(8,128)(2,1)S(1)} %get-tuple-element.81), channel_id=1, source_target_pairs={{0,1},{1,0},{2,3},{3,2},{4,5},{5,4},{6,7},{7,6},{8,9},{9,8},{10,11... | collective-permute-start | bytes 1179656 | tf_op jit(solution)/shard_map/ppermute | solution.py:292
  49.0 14.3 %collective-permute-start.11 = (bf16[8,32,512]{2,1,0:T(8,128)(2,1)S(1)}, bf16[8,32,512]{2,1,0:T(8,128)(2,1)S(1)}, u32[]{:S(2)}, u32[]{:S(2)}) collective-permute-start(bf16[8,32,512]{2,1,0:T(8,128)(2,1)S(1)} %get-tuple-element.77), channel_id=1, source_target_pairs={{0,12},{4,8},{8,4},{12,0},{1,13},{5,9},{9,5},{13,1},{2,14},{6,10},... | collective-permute-start | bytes 786440 | tf_op jit(solution)/shard_map/ppermute | solution.py:252
  49.9 13.4 %collective-permute-start.12 = (bf16[8,32,512]{2,1,0:T(8,128)(2,1)S(1)}, bf16[8,32,512]{2,1,0:T(8,128)(2,1)S(1)}, u32[]{:S(2)}, u32[]{:S(2)}) collective-permute-start(bf16[8,32,512]{2,1,0:T(8,128)(2,1)S(1)} %collective-permute-done.7.refs_0_), channel_id=1, source_target_pairs={{0,2},{2,0},{1,3},{3,1},{4,6},{6,4},{5,7},{7,5},{8,10},{10,8},{9,1... | collective-permute-start | bytes 786440 | tf_op jit(solution)/shard_map/ppermute | solution.py:255
  63.3 7.9 %collective-permute-start.17 = (bf16[8,32,512]{2,1,0:T(8,128)(2,1)S(1)}, bf16[8,32,512]{2,1,0:T(8,128)(2,1)S(1)}, u32[]{:S(2)}, u32[]{:S(2)}) collective-permute-start(bf16[8,32,512]{2,1,0:T(8,128)(2,1)S(1)} %collective-permute-done.11.refs_1_), channel_id=1, source_target_pairs={{0,2},{2,0},{1,3},{3,1},{4,6},{6,4},{5,7},{7,5},{8,10},{10,8},{9,1... | collective-permute-start | bytes 786440 | tf_op jit(solution)/shard_map/ppermute | solution.py:255
  63.6 14.2 %collective-permute-start.14 = (bf16[8,16,512]{2,1,0:T(8,128)(2,1)S(1)}, bf16[8,16,512]{2,1,0:T(8,128)(2,1)S(1)}, u32[]{:S(2)}, u32[]{:S(2)}) collective-permute-start(bf16[8,16,512]{2,1,0:T(8,128)(2,1)S(1)} %get-tuple-element.88), channel_id=1, source_target_pairs={{0,4},{4,0},{8,12},{12,8},{1,5},{5,1},{9,13},{13,9},{2,6},{6,2},{1... | collective-permute-start | bytes 393224 | tf_op jit(solution)/shard_map/ppermute | solution.py:252
  63.6 14.2 %collective-permute-start.15 = (bf16[8,16,512]{2,1,0:T(8,128)(2,1)S(1)}, bf16[8,16,512]{2,1,0:T(8,128)(2,1)S(1)}, u32[]{:S(2)}, u32[]{:S(2)}) collective-permute-start(bf16[8,16,512]{2,1,0:T(8,128)(2,1)S(1)} %get-tuple-element.89), channel_id=1, source_target_pairs={{0,8},{4,12},{8,0},{12,4},{1,9},{5,13},{9,1},{13,5},{2,10},{6,14},... | collective-permute-start | bytes 393224 | tf_op jit(solution)/shard_map/ppermute | solution.py:252
  66.0 12.0 %collective-permute-start.16 = (bf16[8,16,512]{2,1,0:T(8,128)(2,1)S(1)}, bf16[8,16,512]{2,1,0:T(8,128)(2,1)S(1)}, u32[]{:S(2)}, u32[]{:S(2)}) collective-permute-start(bf16[8,16,512]{2,1,0:T(8,128)(2,1)S(1)} %get-tuple-element.90), channel_id=1, source_target_pairs={{0,12},{4,8},{8,4},{12,0},{1,13},{5,9},{9,5},{13,1},{2,14},{6,10},... | collective-permute-start | bytes 393224 | tf_op jit(solution)/shard_map/ppermute | solution.py:252
  78.0 2.3 %collective-permute-start.18 = (bf16[24,32,512]{2,1,0:T(8,128)(2,1)S(1)}, bf16[24,32,512]{2,1,0:T(8,128)(2,1)S(1)}, u32[]{:S(2)}, u32[]{:S(2)}) collective-permute-start(bf16[24,32,512]{2,1,0:T(8,128)(2,1)S(1)} %get-tuple-element.98), channel_id=1, source_target_pairs={{0,1},{1,0},{2,3},{3,2},{4,5},{5,4},{6,7},{7,6},{8,9},{9,8},{10,11... | collective-permute-start | bytes 2359304 | tf_op jit(solution)/shard_map/ppermute | solution.py:299
  81.1 10.9 %collective-permute-start.19 = (bf16[8,32,512]{2,1,0:T(8,128)(2,1)S(1)}, bf16[8,32,512]{2,1,0:T(8,128)(2,1)S(1)}, u32[]{:S(2)}, u32[]{:S(2)}) collective-permute-start(bf16[8,32,512]{2,1,0:T(8,128)(2,1)S(1)} %get-tuple-element.100), channel_id=1, source_target_pairs={{0,4},{4,0},{8,12},{12,8},{1,5},{5,1},{9,13},{13,9},{2,6},{6,2},{1... | collective-permute-start | bytes 786440 | tf_op jit(solution)/shard_map/ppermute | solution.py:252
  81.2 20.3 %collective-permute-start.20 = (bf16[8,32,512]{2,1,0:T(8,128)(2,1)S(1)}, bf16[8,32,512]{2,1,0:T(8,128)(2,1)S(1)}, u32[]{:S(2)}, u32[]{:S(2)}) collective-permute-start(bf16[8,32,512]{2,1,0:T(8,128)(2,1)S(1)} %get-tuple-element.101), channel_id=1, source_target_pairs={{0,8},{4,12},{8,0},{12,4},{1,9},{5,13},{9,1},{13,5},{2,10},{6,14},... | collective-permute-start | bytes 786440 | tf_op jit(solution)/shard_map/ppermute | solution.py:252
  83.6 24.0 %collective-permute-start.21 = (bf16[8,32,512]{2,1,0:T(8,128)(2,1)S(1)}, bf16[8,32,512]{2,1,0:T(8,128)(2,1)S(1)}, u32[]{:S(2)}, u32[]{:S(2)}) collective-permute-start(bf16[8,32,512]{2,1,0:T(8,128)(2,1)S(1)} %get-tuple-element.102), channel_id=1, source_target_pairs={{0,12},{4,8},{8,4},{12,0},{1,13},{5,9},{9,5},{13,1},{2,14},{6,10},... | collective-permute-start | bytes 786440 | tf_op jit(solution)/shard_map/ppermute | solution.py:252
  (1 other events, 11.1 us)

commit v4 on v0

--- a/solution.py
+++ b/solution.py
@@ -1,18 +1,284 @@
+import functools
 import jax
 import jax.numpy as jnp
 from jax import lax
+from jax.experimental import pallas as pl
+from jax.experimental.pallas import tpu as pltpu
 from jax.sharding import PartitionSpec as P
 
 TILE = 128
-
-
-def per_device(visibility, beam_transfer, tile_mask, first_block, eigen_modes, signal_noise):
-    owned_modes = beam_transfer.shape[0]
-    freq_total = beam_transfer.shape[1]
-    base_half = beam_transfer.shape[2]
-    ell_local = beam_transfer.shape[3]
-    base_tiles = base_half // TILE
-    ell_tiles = ell_local // TILE
+PARTS = 4
+ROWS = 16
+VMEM_LIMIT = 24 * 1024 * 1024
+
+
+def spread_kernel(where, modes_ref, down_ref, up_ref, *, parts):
+    freq, n_modes = modes_ref.shape
+    modes = modes_ref[...]
+    freqs = freq // parts
+
+    def pick(shape, axis):
+        big = lax.broadcasted_iota(jnp.int32, shape, axis) // ROWS
+        small = lax.broadcasted_iota(jnp.int32, shape, 1 - axis)
+        if freq in shape:
+            piece, within = big // freqs, big % freqs
+            big = within
+            for j in range(parts):
+                big = jnp.where(piece == j, where[j] * freqs + within, big)
+        return jnp.where(big == small, 1.0, 0.0).astype(jnp.bfloat16)
+
+    def lane(shape):
+        rows = lax.broadcasted_iota(jnp.int32, shape, 0) % ROWS
+        columns = lax.broadcasted_iota(jnp.int32, shape, 1) % ROWS
+        return rows == columns
+
+    def dot(a, b, dims):
+        return lax.dot_general(a, b, (dims, ((), ())), preferred_element_type=jnp.float32)
+
+    tall = dot(pick((n_modes * ROWS, n_modes), 0), modes, ((1,), (1,))).astype(jnp.bfloat16)
+    value = dot(tall, pick((freq, freq * ROWS), 1), ((1,), (0,)))
+    down_ref[...] = jnp.where(lane(value.shape), value, 0.0).astype(jnp.bfloat16)
+    tall = dot(pick((freq * ROWS, freq), 0), modes, ((1,), (0,))).astype(jnp.bfloat16)
+    value = dot(tall, pick((n_modes, n_modes * ROWS), 1), ((1,), (0,)))
+    up_ref[...] = jnp.where(lane(value.shape), value, 0.0).astype(jnp.bfloat16)
+
+
+def spread(where, modes, parts):
+    freq, n_modes = modes.shape
+    vmem = pl.BlockSpec(memory_space=pltpu.VMEM)
+    return pl.pallas_call(
+        functools.partial(spread_kernel, parts=parts),
+        grid_spec=pltpu.PrefetchScalarGridSpec(
+            num_scalar_prefetch=1, grid=(), in_specs=[vmem], out_specs=[vmem, vmem]
+        ),
+        out_shape=[
+            jax.ShapeDtypeStruct((n_modes * ROWS, freq * ROWS), jnp.bfloat16),
+            jax.ShapeDtypeStruct((freq * ROWS, n_modes * ROWS), jnp.bfloat16),
+        ],
+        compiler_params=pltpu.CompilerParams(vmem_limit_bytes=VMEM_LIMIT),
+        cost_estimate=pl.CostEstimate(flops=1024, bytes_accessed=1024, transcendentals=0),
+    )(where, modes)
+
+
+def hold_kernel(where, beam, held, mask, sems):
+    freq, base, ell = held.shape
+    ell_tiles, base_tiles = ell // TILE, base // TILE
+    copies = [pltpu.make_async_copy(beam.at[f], held.at[f], sems.at[f]) for f in range(freq)]
+    for copy in copies:
+        copy.start()
+    for b in range(base_tiles):
+        for l in range(ell_tiles):
+            kept = where[PARTS + 1 + b * ell_tiles + l].astype(jnp.float32)
+            mask[b * TILE:(b + 1) * TILE, l * TILE:(l + 1) * TILE] = jnp.full(
+                (TILE, TILE), kept, jnp.float32
+            ).astype(jnp.bfloat16)
+    for f, copy in enumerate(copies):
+        copy.wait()
+        held[f] = held[f] * mask[...]
+
+
+def hold(where, beam):
+    freq, base, ell = beam.shape
+    return pl.pallas_call(
+        hold_kernel,
+        grid_spec=pltpu.PrefetchScalarGridSpec(
+            num_scalar_prefetch=1,
+            grid=(),
+            in_specs=[pl.BlockSpec(memory_space=pl.ANY)],
+            out_specs=pl.BlockSpec(memory_space=pltpu.VMEM),
+            scratch_shapes=[pltpu.VMEM((base, ell), jnp.bfloat16), pltpu.SemaphoreType.DMA((freq,))],
+        ),
+        out_shape=pltpu.VMEM(beam.shape, beam.dtype),
+        compiler_params=pltpu.CompilerParams(vmem_limit_bytes=VMEM_LIMIT),
+        cost_estimate=pl.CostEstimate(flops=1024, bytes_accessed=1024, transcendentals=0),
+    )(where, beam)
+
+
+def project_kernel(where, mine, others, held, stay_ref, leave_ref, *, piece):
+    freqs, rows, _ = mine.shape
+    first = where[piece] * freqs
+    own = where[PARTS] == 1
+    for f in range(freqs):
+        a, b = mine[f], others[f]
+        lines = jnp.concatenate([jnp.where(own, a, b), jnp.where(own, b, a)], axis=0)
+        value = jnp.dot(lines, held[first + f], preferred_element_type=jnp.float32).astype(jnp.bfloat16)
+        stay_ref[f] = value[:rows]
+        leave_ref[f] = value[rows:]
+
+
+def project(where, mine, others, held, piece):
+    freqs, rows, _ = mine.shape
+    ell = held.shape[2]
+    vmem = pl.BlockSpec(memory_space=pltpu.VMEM)
+    return pl.pallas_call(
+        functools.partial(project_kernel, piece=piece),
+        grid_spec=pltpu.PrefetchScalarGridSpec(
+            num_scalar_prefetch=1, grid=(), in_specs=[vmem] * 3, out_specs=[vmem] * 2
+        ),
+        out_shape=[jax.ShapeDtypeStruct((freqs, rows, ell), jnp.bfloat16)] * 2,
+        compiler_params=pltpu.CompilerParams(vmem_limit_bytes=VMEM_LIMIT),
+        cost_estimate=pl.CostEstimate(flops=1024, bytes_accessed=1024, transcendentals=0),
+    )(where, mine, others, pltpu.with_memory_space_constraint(held, pltpu.VMEM))
+
+
+def contract(modes, skies):
+    block = jnp.concatenate([sky[...].reshape(sky.shape[0] * ROWS, sky.shape[2]) for sky in skies], axis=0)
+    return jnp.dot(modes, block, preferred_element_type=jnp.float32)
+
+
+def reduce_kernel(modes_ref, *refs):
+    out = refs[-1]
+    out[...] = contract(modes_ref[...], refs[:-1]).astype(jnp.bfloat16).reshape(out.shape)
+
+
+def by_rows(count, ell, first=0):
+    return pl.BlockSpec((count, ROWS, ell), lambda g: (0, g + first // ROWS, 0))
+
+
+def fixed(shape):
+    return pl.BlockSpec(shape, lambda g: (0,) * len(shape))
+
+
+def sky_specs(skies, first):
+    return [by_rows(sky.shape[0], sky.shape[2], first if n == 0 else 0) for n, sky in enumerate(skies)]
+
+
+def reduce(modes, skies, first, n_modes):
+    _, rows, ell = skies[-1].shape
+    return pl.pallas_call(
+        reduce_kernel,
+        grid=(rows // ROWS,),
+        in_specs=[fixed(modes.shape)] + sky_specs(skies, first),
+        out_specs=by_rows(n_modes, ell),
+        out_shape=jax.ShapeDtypeStruct((n_modes, rows, ell), jnp.bfloat16),
+        compiler_params=pltpu.CompilerParams(vmem_limit_bytes=VMEM_LIMIT),
+        cost_estimate=pl.CostEstimate(flops=1024, bytes_accessed=1024, transcendentals=0),
+    )(modes, *skies)
+
+
+def restore_kernel(down_ref, up_ref, ratio_ref, came_ref, *refs):
+    skies, outs = refs[:-PARTS], refs[-PARTS:]
+    n_modes, _, ell = came_ref.shape
+    size = outs[0].shape[0] * ROWS
+    total = contract(down_ref[...], skies).reshape(came_ref.shape) + came_ref[...].astype(jnp.float32)
+    weighted = (total * ratio_ref[...]).astype(jnp.bfloat16).reshape(n_modes * ROWS, ell)
+    for which, out in enumerate(outs):
+        value = jnp.dot(up_ref[which * size:(which + 1) * size, :], weighted, preferred_element_type=jnp.float32)
+        out[...] = value.astype(jnp.bfloat16).reshape(out.shape)
+
+
+def restore(skies, first, came, ratios, down, up, freqs):
+    n_modes, rows, ell = came.shape
+    return pl.pallas_call(
+        restore_kernel,
+        grid=(rows // ROWS,),
+        in_specs=[fixed(down.shape), fixed(up.shape), fixed(ratios.shape), by_rows(n_modes, ell)]
+        + sky_specs(skies, first),
+        out_specs=[by_rows(freqs, ell)] * PARTS,
+        out_shape=[jax.ShapeDtypeStruct((freqs, rows, ell), jnp.bfloat16)] * PARTS,
+        compiler_params=pltpu.CompilerParams(vmem_limit_bytes=VMEM_LIMIT),
+        cost_estimate=pl.CostEstimate(flops=1024, bytes_accessed=1024, transcendentals=0),
+    )(down, up, ratios, came, *skies)
+
+
+def place_kernel(where, *refs, spots, first):
+    count = len(spots)
+    pieces, out, sems = refs[:count], refs[-2], refs[-1]
+    rows = pieces[0].shape[1]
+    copies = [
+        pltpu.make_async_copy(pieces[n], out.at[:, where[j], first:first + rows, :], sems.at[n])
+        for n, j in enumerate(spots)
+    ]
+    for copy in copies:
+        copy.start()
+    for copy in copies:
+        copy.wait()
+
+
+def place(where, pieces, spots, first, shape, into=None):
+    count = len(spots)
+    extra = [] if into is None else [into]
+    anywhere = pl.BlockSpec(memory_space=pl.ANY)
+    return pl.pallas_call(
+        functools.partial(place_kernel, spots=spots, first=first),
+        grid_spec=pltpu.PrefetchScalarGridSpec(
+            num_scalar_prefetch=1,
+            grid=(),
+            in_specs=[pl.BlockSpec(memory_space=pltpu.VMEM)] * count + [anywhere] * len(extra),
+            out_specs=anywhere,
+            scratch_shapes=[pltpu.SemaphoreType.DMA((count,))],
+        ),
+        out_shape=jax.ShapeDtypeStruct(shape, jnp.bfloat16),
+        input_output_aliases={count + 1: 0} if extra else {},
+        compiler_params=pltpu.CompilerParams(vmem_limit_bytes=VMEM_LIMIT),
+        cost_estimate=pl.CostEstimate(flops=1024, bytes_accessed=1024, transcendentals=0),
+    )(where, *[pieces[j] for j in spots], *extra)
+
+
+def staged(visibility, beam_transfer, tile_mask, first_block, eigen_modes, signal_noise):
+    freqs, parts, rows_all, base = visibility.shape
+    _, freq_total, _, ell = beam_transfer.shape
+    n_modes = eigen_modes.shape[2]
+    ell_tiles = ell // TILE
+    z, x, p = lax.axis_index("fm"), lax.axis_index("kl"), lax.axis_index("pol")
+    other = [(0, 1), (1, 0)]
+
+    def along_z(value, j):
+        return lax.ppermute(value, "fm", [(i, i ^ j) for i in range(parts)])
+
+    def along_x(value):
+        return lax.ppermute(value, "kl", other)
+
+    def cut(j, first, rows):
+        return lax.dynamic_slice(visibility, (0, z ^ j, first, 0), (freqs, 1, rows, base)).reshape(freqs, rows, base)
+
+    order = jnp.stack([z ^ j for j in range(parts)]).astype(jnp.int32)
+    block_ids = x * ell_tiles + jnp.arange(ell_tiles, dtype=jnp.int32)
+    keep = tile_mask[0] * (first_block[0] <= block_ids).astype(jnp.int32)[None, :]
+    where = jnp.concatenate([order, (x == p).astype(jnp.int32)[None], keep.reshape(-1)])
+    down, up = spread(where, eigen_modes[0], parts)
+    ratio = signal_noise[0] / (1.0 + signal_noise[0])
+    ratios = jnp.broadcast_to(ratio[:, None, None], (n_modes, 1, ell))
+    beam = beam_transfer.reshape(freq_total, base, ell)
+    shape = (freqs, parts, rows_all, ell)
+
+    fence = lax.optimization_barrier
+    most = rows_all - ROWS
+    a = [cut(j, 0, ROWS) for j in range(1, parts)]
+    mine = cut(0, 0, rows_all)
+    b = [cut(j, ROWS, most) for j in range(1, parts)]
+    a = [along_z(a[j - 1], j) for j in (1, 2, 3)]
+    others = along_x(mine)
+    held = hold(where, beam)
+    stay_own, leave_own = project(where, mine, others, held, 0)
+    a, b, held, stay_own, leave_own, down, up = fence((a, b, held, stay_own, leave_own, down, up))
+    b[0], b[1] = along_z(b[0], 1), along_z(b[1], 2)
+    skies = [project(where, a[j - 1], along_x(a[j - 1]), held, j) for j in (1, 2, 3)]
+    stay_a = [stay_own] + [stay for stay, _ in skies]
+    gone = reduce(down, [leave_own] + [leave for _, leave in skies], 0, n_modes)
+    b, held, stay_a, gone = fence((b, held, stay_a, gone))
+    b[2] = along_z(b[2], 3)
+    x_1, x_2 = along_x(b[0]), along_x(b[1])
+    outs = restore(stay_a, 0, lax.ppermute(gone, "pol", other), ratios, down, up, freqs)
+    stay_1, leave_1 = project(where, b[0], x_1, held, 1)
+    b, x_2, held, outs, stay_1, leave_1 = fence((b, x_2, held, outs, stay_1, leave_1))
+    back_a = [outs[0]] + [along_z(outs[j], j) for j in range(1, parts)]
+    x_3 = along_x(b[2])
+    stay_2, leave_2 = project(where, b[1], x_2, held, 2)
+    stay_3, leave_3 = project(where, b[2], x_3, held, 3)
+    gone = reduce(down, [leave_own, leave_1, leave_2, leave_3], ROWS, n_modes)
+    back_a, stay_2, stay_3, gone = fence((back_a, stay_2, stay_3, gone))
+    came = lax.ppermute(gone, "pol", other)
+    outs = restore([stay_own, stay_1, stay_2, stay_3], ROWS, came, ratios, down, up, freqs)
+    back_b = [outs[0]] + [along_z(outs[j], j) for j in range(1, parts)]
+    result = place(where, back_a, (0, 1, 2, 3), 0, shape)
+    result = place(where, back_b, (0, 1), ROWS, shape, into=result)
+    return place(where, back_b, (2, 3), ROWS, shape, into=result)
+
+
+def plain(visibility, beam_transfer, tile_mask, first_block, eigen_modes, signal_noise):
+    owned_modes, freq_total, base_half, ell_local = beam_transfer.shape
+    base_tiles, ell_tiles = base_half // TILE, ell_local // TILE
     block_ids = lax.axis_index("kl") * ell_tiles + jnp.arange(ell_tiles, dtype=jnp.int32)
     inside = (first_block[:, None] <= block_ids[None, :]).astype(jnp.int32)
     keep_tiles = tile_mask * inside[:, None, :]
@@ -39,6 +305,22 @@
     return lax.all_to_all(filtered, "fm", split_axis=0, concat_axis=1, tiled=True)
 
 
+def per_device(*args, sizes):
+    visibility, beam_transfer = args[0], args[1]
+    _, modes, rows, _ = visibility.shape
+    fits = (
+        sizes["kl"] == 2
+        and sizes["pol"] == 2
+        and modes == sizes["fm"] == PARTS
+        and beam_transfer.shape[0] == 1
+        and rows % ROWS == 0
+        and rows > ROWS
+    )
+    if not fits:
+        return plain(*args)
+    return staged(*args)
+
+
 def solution(mesh):
     placed = (
         P(("group", "fm"), None, "kl", "pol"),
@@ -49,7 +331,7 @@
         P(("group", "fm"), None),
     )
     return jax.shard_map(
-        per_device,
+        functools.partial(per_device, sizes=dict(mesh.shape)),
         mesh=mesh,
         in_specs=placed,
         out_specs=P(("group", "fm"), None, "pol", "kl"),

time: 173 us -> 106 us (0.61); the launches traced: 170 us -> 106 us
  blocking collectives: 80.9 us -> 0 us
  Pallas kernels: 0 us -> 25.3 us
  starting transfers between devices: 0.04 us -> 21.5 us
  matrix products: 15.2 us -> 0 us
  between operations: 14.1 us -> 0.94 us
  waiting for transfers between devices: 55.1 us -> 44.1 us
  local copies, waits for them, and re-layouts: 4.56 us -> 14.1 us
    all_to_all x2 -> x0, blocking collectives: 80.9 us -> none  [the longest x1 40.6 us: per_device(): lax.all_to_all(filtered, 'fm', split_axis=0, concat_axis=1, tiled=True)]
    all_gather x1 -> x0, waiting for transfers between devices: 44.4 us -> none  [per_device(): lax.all_gather(arrived, 'kl', axis=2, tiled=True)]
    ppermute x0 -> x21, waiting for transfers between devices: none -> 44.1 us  [the longest x12 26.4 us: along_z(): return lax.ppermute(value, 'fm', [(i, i ^ j) for i in range(parts)])]
    pallas_call x0 -> x16, Pallas kernels: none -> 25.3 us  [the longest x7 9.55 us: project(): pl.pallas_call(functools.partial(project_kernel, piece=piece), grid_spec=...]
    ppermute x0 -> x21, starting transfers between devices: none -> 21.5 us  [the longest x12 14.7 us: along_z(): return lax.ppermute(value, 'fm', [(i, i ^ j) for i in range(parts)])]
    dot_general x3 -> x0, matrix products: 15.2 us -> none  [the longest x1 12.1 us: per_device(): jnp.einsum('fmrb,mfbl->fmrl', lax.all_gather(arrived, 'kl', axis=2, tiled...]
    reduce_scatter x1 -> x0, waiting for transfers between devices: 10.7 us -> none  [per_device(): lax.psum_scatter(partial_value.astype(jnp.bfloat16), 'pol', scatter_dimen...]
    unnamed x8 -> x21, local copies, waits for them, and re-layouts: 2.24 us -> 11.6 us
  transfers between devices with their start and end apart: 2 -> 21, of which waited for: 2 -> 12; matrix products, arithmetic and copies ran while one was open for 0% -> 1% of each run, Pallas kernels for 0% -> 21%
where the time goes in v4:
time: 106 us
  waiting for transfers between devices  44.1 us (42%)
  Pallas kernels  25.3 us (24%)
  starting transfers between devices  21.5 us (20%)
  local copies, waits for them, and re-layouts  14.1 us (13%)
    ppermute x12, waiting for transfers between devices, along_z(): return lax.ppermute(value, 'fm', [(i, i ^ j) for i in range(parts)])  26.4 us
    ppermute x7, waiting for transfers between devices, along_x(): return lax.ppermute(value, 'kl', other)  15.5 us
    ppermute x12, starting transfers between devices, along_z(): return lax.ppermute(value, 'fm', [(i, i ^ j) for i in range(parts)])  14.7 us
    unnamed x21, local copies, waits for them, and re-layouts  11.6 us
    pallas_call x7, Pallas kernels, project(): pl.pallas_call(functools.partial(project_kernel, piece=piece), grid_spec=...  9.55 us
    ppermute x7, starting transfers between devices, along_x(): return lax.ppermute(value, 'kl', other)  6.73 us
    pallas_call x1, Pallas kernels, hold(): pl.pallas_call(hold_kernel, grid_spec=pltpu.PrefetchScalarGridSpec(num_sc...  6.64 us
    pallas_call x3, Pallas kernels, place(): pl.pallas_call(functools.partial(place_kernel, spots=spots, first=first),...  4.06 us
  transfers between devices with their start and end apart: 21, of which 12 were waited for; matrix products, arithmetic and copies ran while one was open for 1% of the time, Pallas kernels for 21%

profile of v4, /device:TPU:12, one launch (start us, length us, event | category | flops | bytes accessed | tf_op | source)
XLA Modules:
  0.0 106.0 jit_solution(9396979833306220484)
XLA Ops:
  1.0 1.6 %collective-permute-start.3 = (bf16[8,48,512]{2,1,0:T(8,128)(2,1)S(1)}, bf16[8,48,512]{2,1,0:T(8,128)(2,1)S(1)}, u32[]{:S(2)}, u32[]{:S(2)}) collective-permute-start(bf16[8,48,512]{2,1,0:T(8,128)(2,1)S(1)} %dynamic-slice_bitcast_fusion.mine), channel_id=1, source_target_pairs={{0,2},{2,0},{1,3},{3,1},{4,6},{6,4},{5,7},{7,5},{8,10},{10,8},{9,1... | collective-permute-start | bytes 1179656 | tf_op jit(solution)/shard_map/ppermute | solution.py:230
  4.2 2.6 %collective-permute-start.1 = (bf16[8,16,512]{2,1,0:T(8,128)(2,1)S(1)}, bf16[8,16,512]{2,1,0:T(8,128)(2,1)S(1)}, u32[]{:S(2)}, u32[]{:S(2)}) collective-permute-start(bf16[8,16,512]{2,1,0:T(8,128)(2,1)S(1)} %get-tuple-element.131), channel_id=1, source_target_pairs={{0,8},{4,12},{8,0},{12,4},{1,9},{5,13},{9,1},{13,5},{2,10},{6,14},... | collective-permute-start | bytes 393224 | tf_op jit(solution)/shard_map/ppermute | solution.py:227
  8.2 6.6 %shard_map.64.held = bf16[32,512,512]{2,1,0:T(8,128)(2,1)S(1)} custom-call(s32[21]{0:T(128)S(1)} %concatenate.3.where, bf16[32,512,512]{2,1,0:T(8,128)(2,1)} %bitcast.28), custom_call_target="tpu_custom_call" | custom-call | flops 1024 | bytes 1024 | tf_op jit(solution)/shard_map/pallas_call | solution.py:82
  14.8 5.7 %copy-done = bf16[32,512,512]{2,1,0:T(8,128)(2,1)} copy-done((bf16[32,512,512]{2,1,0:T(8,128)(2,1)}, bf16[32,512,512]{2,1,0:T(8,128)(2,1)S(1)}, u32[]{:S(2)}) %copy-start) | copy-done | bytes 16777240
  21.9 5.8 %copy-done.1 = bf16[32,512,512]{2,1,0:T(8,128)(2,1)S(1)} copy-done((bf16[32,512,512]{2,1,0:T(8,128)(2,1)S(1)}, bf16[32,512,512]{2,1,0:T(8,128)(2,1)}, u32[]{:S(2)}) %copy-start.1) | copy-done | bytes 16777240
  29.1 1.4 %collective-permute-start.4 = (bf16[8,32,512]{2,1,0:T(8,128)(2,1)S(1)}, bf16[8,32,512]{2,1,0:T(8,128)(2,1)S(1)}, u32[]{:S(2)}, u32[]{:S(2)}) collective-permute-start(bf16[8,32,512]{2,1,0:T(8,128)(2,1)S(1)} %get-tuple-element.72), channel_id=1, source_target_pairs={{0,4},{4,0},{8,12},{12,8},{1,5},{5,1},{9,13},{13,9},{2,6},{6,2},{1... | collective-permute-start | bytes 786440 | tf_op jit(solution)/shard_map/ppermute | solution.py:227
  30.5 2.2 %collective-permute-start.5 = (bf16[8,32,512]{2,1,0:T(8,128)(2,1)S(1)}, bf16[8,32,512]{2,1,0:T(8,128)(2,1)S(1)}, u32[]{:S(2)}, u32[]{:S(2)}) collective-permute-start(bf16[8,32,512]{2,1,0:T(8,128)(2,1)S(1)} %get-tuple-element.73), channel_id=1, source_target_pairs={{0,8},{4,12},{8,0},{12,4},{1,9},{5,13},{9,1},{13,5},{2,10},{6,14},... | collective-permute-start | bytes 786440 | tf_op jit(solution)/shard_map/ppermute | solution.py:227
  33.3 1.5 %collective-permute-start.7 = (bf16[8,16,512]{2,1,0:T(8,128)(2,1)S(1)}, bf16[8,16,512]{2,1,0:T(8,128)(2,1)S(1)}, u32[]{:S(2)}, u32[]{:S(2)}) collective-permute-start(bf16[8,16,512]{2,1,0:T(8,128)(2,1)S(1)} %collective-permute-done.1.mine), channel_id=1, source_target_pairs={{0,2},{2,0},{1,3},{3,1},{4,6},{6,4},{5,7},{7,5},{8,10},{10,8},{9,1... | collective-permute-start | bytes 393224 | tf_op jit(solution)/shard_map/ppermute | solution.py:230
  35.3 3.9 %collective-permute-done.8.others = bf16[8,16,512]{2,1,0:T(8,128)(2,1)S(1)} collective-permute-done((bf16[8,16,512]{2,1,0:T(8,128)(2,1)S(1)}, bf16[8,16,512]{2,1,0:T(8,128)(2,1)S(1)}, u32[]{:S(2)}, u32[]{:S(2)}) %collective-permute-start.8) | collective-permute-done | bytes 131104 | tf_op jit(solution)/shard_map/ppermute | solution.py:230
  44.6 1.5 %collective-permute-start.10 = (bf16[8,32,512]{2,1,0:T(8,128)(2,1)S(1)}, bf16[8,32,512]{2,1,0:T(8,128)(2,1)S(1)}, u32[]{:S(2)}, u32[]{:S(2)}) collective-permute-start(bf16[8,32,512]{2,1,0:T(8,128)(2,1)S(1)} %collective-permute-done.5.mine), channel_id=1, source_target_pairs={{0,2},{2,0},{1,3},{3,1},{4,6},{6,4},{5,7},{7,5},{8,10},{10,8},{9,1... | collective-permute-start | bytes 786440 | tf_op jit(solution)/shard_map/ppermute | solution.py:230
  46.6 6.6 %collective-permute-done.12.others = bf16[8,32,512]{2,1,0:T(8,128)(2,1)S(1)} collective-permute-done((bf16[8,32,512]{2,1,0:T(8,128)(2,1)S(1)}, bf16[8,32,512]{2,1,0:T(8,128)(2,1)S(1)}, u32[]{:S(2)}, u32[]{:S(2)}) %collective-permute-start.12) | collective-permute-done | bytes 262176 | tf_op jit(solution)/shard_map/ppermute | solution.py:230
  55.5 2.9 %collective-permute-done.10.others = bf16[8,32,512]{2,1,0:T(8,128)(2,1)S(1)} collective-permute-done((bf16[8,32,512]{2,1,0:T(8,128)(2,1)S(1)}, bf16[8,32,512]{2,1,0:T(8,128)(2,1)S(1)}, u32[]{:S(2)}, u32[]{:S(2)}) %collective-permute-start.10) | collective-permute-done | bytes 262176 | tf_op jit(solution)/shard_map/ppermute | solution.py:230
  58.4 1.5 %collective-permute-done.9.mine = bf16[8,32,512]{2,1,0:T(8,128)(2,1)S(1)} collective-permute-done((bf16[8,32,512]{2,1,0:T(8,128)(2,1)S(1)}, bf16[8,32,512]{2,1,0:T(8,128)(2,1)S(1)}, u32[]{:S(2)}, u32[]{:S(2)}) %collective-permute-start.9) | collective-permute-done | bytes 262176 | tf_op jit(solution)/shard_map/ppermute | solution.py:227
  60.6 1.7 %collective-permute-start.14 = (bf16[8,16,512]{2,1,0:T(8,128)(2,1)S(1)}, bf16[8,16,512]{2,1,0:T(8,128)(2,1)S(1)}, u32[]{:S(2)}, u32[]{:S(2)}) collective-permute-start(bf16[8,16,512]{2,1,0:T(8,128)(2,1)S(1)} %get-tuple-element.104), channel_id=1, source_target_pairs={{0,8},{4,12},{8,0},{12,4},{1,9},{5,13},{9,1},{13,5},{2,10},{6,14},... | collective-permute-start | bytes 393224 | tf_op jit(solution)/shard_map/ppermute | solution.py:227
  62.3 1.5 %collective-permute-start.15 = (bf16[8,16,512]{2,1,0:T(8,128)(2,1)S(1)}, bf16[8,16,512]{2,1,0:T(8,128)(2,1)S(1)}, u32[]{:S(2)}, u32[]{:S(2)}) collective-permute-start(bf16[8,16,512]{2,1,0:T(8,128)(2,1)S(1)} %get-tuple-element.105), channel_id=1, source_target_pairs={{0,12},{4,8},{8,4},{12,0},{1,13},{5,9},{9,5},{13,1},{2,14},{6,10},... | collective-permute-start | bytes 393224 | tf_op jit(solution)/shard_map/ppermute | solution.py:227
  65.2 1.8 %collective-permute-done.16.others = bf16[8,32,512]{2,1,0:T(8,128)(2,1)S(1)} collective-permute-done((bf16[8,32,512]{2,1,0:T(8,128)(2,1)S(1)}, bf16[8,32,512]{2,1,0:T(8,128)(2,1)S(1)}, u32[]{:S(2)}, u32[]{:S(2)}) %collective-permute-start.16) | collective-permute-done | bytes 262176 | tf_op jit(solution)/shard_map/ppermute | solution.py:230
  70.8 3.3 %collective-permute-done.15.refs_3_ = bf16[8,16,512]{2,1,0:T(8,128)(2,1)S(1)} collective-permute-done((bf16[8,16,512]{2,1,0:T(8,128)(2,1)S(1)}, bf16[8,16,512]{2,1,0:T(8,128)(2,1)S(1)}, u32[]{:S(2)}, u32[]{:S(2)}) %collective-permute-start.15) | collective-permute-done | bytes 131104 | tf_op jit(solution)/shard_map/ppermute | solution.py:227
  74.1 2.3 %collective-permute-done.17.came_ref = bf16[24,32,512]{2,1,0:T(8,128)(2,1)S(1)} collective-permute-done((bf16[24,32,512]{2,1,0:T(8,128)(2,1)S(1)}, bf16[24,32,512]{2,1,0:T(8,128)(2,1)S(1)}, u32[]{:S(2)}, u32[]{:S(2)}) %collective-permute-start.17) | collective-permute-done | bytes 786464 | tf_op jit(solution)/shard_map/ppermute | solution.py:271
  76.4 1.8 %shard_map.76 = (bf16[8,32,512]{2,1,0:T(8,128)(2,1)S(1)}, bf16[8,32,512]{2,1,0:T(8,128)(2,1)S(1)}, bf16[8,32,512]{2,1,0:T(8,128)(2,1)S(1)}, bf16[8,32,512]{2,1,0:T(8,128)(2,1)S(1)}) custom-call(bf16[384,512]{1,0:T(8,128)(2,1)S(1)} %get-tuple-element.70.modes_ref.down_ref, bf16[512,384]{1,0:T(8,128)(2,1)S(1)} %get-tuple-element.71.up_ref, ...), custom_call_target="tpu_custom_call" | custom-call | flops 1024 | bytes 1024 | tf_op jit(solution)/shard_map/pallas_call | solution.py:172
  78.3 2.0 %collective-permute-start.18 = (bf16[8,32,512]{2,1,0:T(8,128)(2,1)S(1)}, bf16[8,32,512]{2,1,0:T(8,128)(2,1)S(1)}, u32[]{:S(2)}, u32[]{:S(2)}) collective-permute-start(bf16[8,32,512]{2,1,0:T(8,128)(2,1)S(1)} %get-tuple-element.119), channel_id=1, source_target_pairs={{0,8},{4,12},{8,0},{12,4},{1,9},{5,13},{9,1},{13,5},{2,10},{6,14},... | collective-permute-start | bytes 786440 | tf_op jit(solution)/shard_map/ppermute | solution.py:227
  80.3 1.5 %collective-permute-start.19 = (bf16[8,32,512]{2,1,0:T(8,128)(2,1)S(1)}, bf16[8,32,512]{2,1,0:T(8,128)(2,1)S(1)}, u32[]{:S(2)}, u32[]{:S(2)}) collective-permute-start(bf16[8,32,512]{2,1,0:T(8,128)(2,1)S(1)} %get-tuple-element.120), channel_id=1, source_target_pairs={{0,12},{4,8},{8,4},{12,0},{1,13},{5,9},{9,5},{13,1},{2,14},{6,10},... | collective-permute-start | bytes 786440 | tf_op jit(solution)/shard_map/ppermute | solution.py:227
  83.1 5.7 %collective-permute-done.20.refs_1_ = bf16[8,32,512]{2,1,0:T(8,128)(2,1)S(1)} collective-permute-done((bf16[8,32,512]{2,1,0:T(8,128)(2,1)S(1)}, bf16[8,32,512]{2,1,0:T(8,128)(2,1)S(1)}, u32[]{:S(2)}, u32[]{:S(2)}) %collective-permute-start.20) | collective-permute-done | bytes 262176 | tf_op jit(solution)/shard_map/ppermute | solution.py:227
  90.2 8.0 %collective-permute-done.18.refs_0_ = bf16[8,32,512]{2,1,0:T(8,128)(2,1)S(1)} collective-permute-done((bf16[8,32,512]{2,1,0:T(8,128)(2,1)S(1)}, bf16[8,32,512]{2,1,0:T(8,128)(2,1)S(1)}, u32[]{:S(2)}, u32[]{:S(2)}) %collective-permute-start.18) | collective-permute-done | bytes 262176 | tf_op jit(solution)/shard_map/ppermute | solution.py:227
  98.2 6.5 %collective-permute-done.19.refs_1_ = bf16[8,32,512]{2,1,0:T(8,128)(2,1)S(1)} collective-permute-done((bf16[8,32,512]{2,1,0:T(8,128)(2,1)S(1)}, bf16[8,32,512]{2,1,0:T(8,128)(2,1)S(1)}, u32[]{:S(2)}, u32[]{:S(2)}) %collective-permute-start.19) | collective-permute-done | bytes 262176 | tf_op jit(solution)/shard_map/ppermute | solution.py:227
  (67 shorter events, 25.2 us)
Async XLA Ops:
  1.0 20.9 %collective-permute-start.3 = (bf16[8,48,512]{2,1,0:T(8,128)(2,1)S(1)}, bf16[8,48,512]{2,1,0:T(8,128)(2,1)S(1)}, u32[]{:S(2)}, u32[]{:S(2)}) collective-permute-start(bf16[8,48,512]{2,1,0:T(8,128)(2,1)S(1)} %dynamic-slice_bitcast_fusion.mine), channel_id=1, source_target_pairs={{0,2},{2,0},{1,3},{3,1},{4,6},{6,4},{5,7},{7,5},{8,10},{10,8},{9,1... | collective-permute-start | bytes 1179656 | tf_op jit(solution)/shard_map/ppermute | solution.py:230
  3.7 25.4 %collective-permute-start = (bf16[8,16,512]{2,1,0:T(8,128)(2,1)S(1)}, bf16[8,16,512]{2,1,0:T(8,128)(2,1)S(1)}, u32[]{:S(2)}, u32[]{:S(2)}) collective-permute-start(bf16[8,16,512]{2,1,0:T(8,128)(2,1)S(1)} %get-tuple-element.132), channel_id=1, source_target_pairs={{0,4},{4,0},{8,12},{12,8},{1,5},{5,1},{9,13},{13,9},{2,6},{6,2},{1... | collective-permute-start | bytes 393224 | tf_op jit(solution)/shard_map/ppermute | solution.py:227
  4.2 24.9 %collective-permute-start.1 = (bf16[8,16,512]{2,1,0:T(8,128)(2,1)S(1)}, bf16[8,16,512]{2,1,0:T(8,128)(2,1)S(1)}, u32[]{:S(2)}, u32[]{:S(2)}) collective-permute-start(bf16[8,16,512]{2,1,0:T(8,128)(2,1)S(1)} %get-tuple-element.131), channel_id=1, source_target_pairs={{0,8},{4,12},{8,0},{12,4},{1,9},{5,13},{9,1},{13,5},{2,10},{6,14},... | collective-permute-start | bytes 393224 | tf_op jit(solution)/shard_map/ppermute | solution.py:227
  6.8 22.3 %collective-permute-start.2 = (bf16[8,16,512]{2,1,0:T(8,128)(2,1)S(1)}, bf16[8,16,512]{2,1,0:T(8,128)(2,1)S(1)}, u32[]{:S(2)}, u32[]{:S(2)}) collective-permute-start(bf16[8,16,512]{2,1,0:T(8,128)(2,1)S(1)} %get-tuple-element.130), channel_id=1, source_target_pairs={{0,12},{4,8},{8,4},{12,0},{1,13},{5,9},{9,5},{13,1},{2,14},{6,10},... | collective-permute-start | bytes 393224 | tf_op jit(solution)/shard_map/ppermute | solution.py:227
  8.2 13.7 %copy-start.2 = (bf16[8,4,48,512]{3,2,1,0:T(8,128)(2,1)S(1)}, bf16[8,4,48,512]{3,2,1,0:T(8,128)(2,1)}, u32[]{:S(2)}) copy-start(bf16[8,4,48,512]{3,2,1,0:T(8,128)(2,1)} %param.6) | copy-start | bytes 4718596
  29.1 14.8 %collective-permute-start.4 = (bf16[8,32,512]{2,1,0:T(8,128)(2,1)S(1)}, bf16[8,32,512]{2,1,0:T(8,128)(2,1)S(1)}, u32[]{:S(2)}, u32[]{:S(2)}) collective-permute-start(bf16[8,32,512]{2,1,0:T(8,128)(2,1)S(1)} %get-tuple-element.72), channel_id=1, source_target_pairs={{0,4},{4,0},{8,12},{12,8},{1,5},{5,1},{9,13},{13,9},{2,6},{6,2},{1... | collective-permute-start | bytes 786440 | tf_op jit(solution)/shard_map/ppermute | solution.py:227
  30.5 13.4 %collective-permute-start.5 = (bf16[8,32,512]{2,1,0:T(8,128)(2,1)S(1)}, bf16[8,32,512]{2,1,0:T(8,128)(2,1)S(1)}, u32[]{:S(2)}, u32[]{:S(2)}) collective-permute-start(bf16[8,32,512]{2,1,0:T(8,128)(2,1)S(1)} %get-tuple-element.73), channel_id=1, source_target_pairs={{0,8},{4,12},{8,0},{12,4},{1,9},{5,13},{9,1},{13,5},{2,10},{6,14},... | collective-permute-start | bytes 786440 | tf_op jit(solution)/shard_map/ppermute | solution.py:227
  32.7 6.4 %collective-permute-start.8 = (bf16[8,16,512]{2,1,0:T(8,128)(2,1)S(1)}, bf16[8,16,512]{2,1,0:T(8,128)(2,1)S(1)}, u32[]{:S(2)}, u32[]{:S(2)}) collective-permute-start(bf16[8,16,512]{2,1,0:T(8,128)(2,1)S(1)} %collective-permute-done.2.mine), channel_id=1, source_target_pairs={{0,2},{2,0},{1,3},{3,1},{4,6},{6,4},{5,7},{7,5},{8,10},{10,8},{9,1... | collective-permute-start | bytes 393224 | tf_op jit(solution)/shard_map/ppermute | solution.py:230
  33.3 7.5 %collective-permute-start.7 = (bf16[8,16,512]{2,1,0:T(8,128)(2,1)S(1)}, bf16[8,16,512]{2,1,0:T(8,128)(2,1)S(1)}, u32[]{:S(2)}, u32[]{:S(2)}) collective-permute-start(bf16[8,16,512]{2,1,0:T(8,128)(2,1)S(1)} %collective-permute-done.1.mine), channel_id=1, source_target_pairs={{0,2},{2,0},{1,3},{3,1},{4,6},{6,4},{5,7},{7,5},{8,10},{10,8},{9,1... | collective-permute-start | bytes 393224 | tf_op jit(solution)/shard_map/ppermute | solution.py:230
  34.8 7.4 %collective-permute-start.6 = (bf16[8,16,512]{2,1,0:T(8,128)(2,1)S(1)}, bf16[8,16,512]{2,1,0:T(8,128)(2,1)S(1)}, u32[]{:S(2)}, u32[]{:S(2)}) collective-permute-start(bf16[8,16,512]{2,1,0:T(8,128)(2,1)S(1)} %collective-permute-done.mine), channel_id=1, source_target_pairs={{0,2},{2,0},{1,3},{3,1},{4,6},{6,4},{5,7},{7,5},{8,10},{10,8},{9,1... | collective-permute-start | bytes 393224 | tf_op jit(solution)/shard_map/ppermute | solution.py:230
  40.8 12.4 %slice-start = ((s8[16777216]{0:T(1024)(128)(4,1)}), s8[4194304]{0:T(1024)(128)(4,1)S(1)}, s32[]{:S(2)}) async-start(s8[16777216]{0:T(1024)(128)(4,1)} %bitcast.25), calls=%async_computation | async-start | bytes 8388608
  40.8 12.4 %slice-start.1 = ((s8[16777216]{0:T(1024)(128)(4,1)}), s8[4194304]{0:T(1024)(128)(4,1)S(1)}, s32[]{:S(2)}) async-start(s8[16777216]{0:T(1024)(128)(4,1)} %bitcast.25), calls=%async_computation.1 | async-start | bytes 8388608
  44.0 10.7 %collective-permute-start.11 = (bf16[24,16,512]{2,1,0:T(8,128)(2,1)S(1)}, bf16[24,16,512]{2,1,0:T(8,128)(2,1)S(1)}, u32[]{:S(2)}, u32[]{:S(2)}) collective-permute-start(bf16[24,16,512]{2,1,0:T(8,128)(2,1)S(1)} %shard_map.70), channel_id=1, source_target_pairs={{0,1},{1,0},{2,3},{3,2},{4,5},{5,4},{6,7},{7,6},{8,9},{9,8},{10,11... | collective-permute-start | bytes 1179656 | tf_op jit(solution)/shard_map/ppermute | solution.py:262
  44.0 9.2 %collective-permute-start.12 = (bf16[8,32,512]{2,1,0:T(8,128)(2,1)S(1)}, bf16[8,32,512]{2,1,0:T(8,128)(2,1)S(1)}, u32[]{:S(2)}, u32[]{:S(2)}) collective-permute-start(bf16[8,32,512]{2,1,0:T(8,128)(2,1)S(1)} %collective-permute-done.4.mine), channel_id=1, source_target_pairs={{0,2},{2,0},{1,3},{3,1},{4,6},{6,4},{5,7},{7,5},{8,10},{10,8},{9,1... | collective-permute-start | bytes 786440 | tf_op jit(solution)/shard_map/ppermute | solution.py:230
  44.6 13.8 %collective-permute-start.10 = (bf16[8,32,512]{2,1,0:T(8,128)(2,1)S(1)}, bf16[8,32,512]{2,1,0:T(8,128)(2,1)S(1)}, u32[]{:S(2)}, u32[]{:S(2)}) collective-permute-start(bf16[8,32,512]{2,1,0:T(8,128)(2,1)S(1)} %collective-permute-done.5.mine), channel_id=1, source_target_pairs={{0,2},{2,0},{1,3},{3,1},{4,6},{6,4},{5,7},{7,5},{8,10},{10,8},{9,1... | collective-permute-start | bytes 786440 | tf_op jit(solution)/shard_map/ppermute | solution.py:230
  46.1 13.7 %collective-permute-start.9 = (bf16[8,32,512]{2,1,0:T(8,128)(2,1)S(1)}, bf16[8,32,512]{2,1,0:T(8,128)(2,1)S(1)}, u32[]{:S(2)}, u32[]{:S(2)}) collective-permute-start(bf16[8,32,512]{2,1,0:T(8,128)(2,1)S(1)} %get-tuple-element.89), channel_id=1, source_target_pairs={{0,12},{4,8},{8,4},{12,0},{1,13},{5,9},{9,5},{13,1},{2,14},{6,10},... | collective-permute-start | bytes 786440 | tf_op jit(solution)/shard_map/ppermute | solution.py:227
  59.8 7.2 %collective-permute-start.16 = (bf16[8,32,512]{2,1,0:T(8,128)(2,1)S(1)}, bf16[8,32,512]{2,1,0:T(8,128)(2,1)S(1)}, u32[]{:S(2)}, u32[]{:S(2)}) collective-permute-start(bf16[8,32,512]{2,1,0:T(8,128)(2,1)S(1)} %collective-permute-done.9.mine), channel_id=1, source_target_pairs={{0,2},{2,0},{1,3},{3,1},{4,6},{6,4},{5,7},{7,5},{8,10},{10,8},{9,1... | collective-permute-start | bytes 786440 | tf_op jit(solution)/shard_map/ppermute | solution.py:230
  60.4 9.0 %collective-permute-start.13 = (bf16[8,16,512]{2,1,0:T(8,128)(2,1)S(1)}, bf16[8,16,512]{2,1,0:T(8,128)(2,1)S(1)}, u32[]{:S(2)}, u32[]{:S(2)}) collective-permute-start(bf16[8,16,512]{2,1,0:T(8,128)(2,1)S(1)} %get-tuple-element.103), channel_id=1, source_target_pairs={{0,4},{4,0},{8,12},{12,8},{1,5},{5,1},{9,13},{13,9},{2,6},{6,2},{1... | collective-permute-start | bytes 393224 | tf_op jit(solution)/shard_map/ppermute | solution.py:227
  60.6 10.2 %collective-permute-start.14 = (bf16[8,16,512]{2,1,0:T(8,128)(2,1)S(1)}, bf16[8,16,512]{2,1,0:T(8,128)(2,1)S(1)}, u32[]{:S(2)}, u32[]{:S(2)}) collective-permute-start(bf16[8,16,512]{2,1,0:T(8,128)(2,1)S(1)} %get-tuple-element.104), channel_id=1, source_target_pairs={{0,8},{4,12},{8,0},{12,4},{1,9},{5,13},{9,1},{13,5},{2,10},{6,14},... | collective-permute-start | bytes 393224 | tf_op jit(solution)/shard_map/ppermute | solution.py:227
  62.3 11.8 %collective-permute-start.15 = (bf16[8,16,512]{2,1,0:T(8,128)(2,1)S(1)}, bf16[8,16,512]{2,1,0:T(8,128)(2,1)S(1)}, u32[]{:S(2)}, u32[]{:S(2)}) collective-permute-start(bf16[8,16,512]{2,1,0:T(8,128)(2,1)S(1)} %get-tuple-element.105), channel_id=1, source_target_pairs={{0,12},{4,8},{8,4},{12,0},{1,13},{5,9},{9,5},{13,1},{2,14},{6,10},... | collective-permute-start | bytes 393224 | tf_op jit(solution)/shard_map/ppermute | solution.py:227
  74.1 2.3 %collective-permute-start.17 = (bf16[24,32,512]{2,1,0:T(8,128)(2,1)S(1)}, bf16[24,32,512]{2,1,0:T(8,128)(2,1)S(1)}, u32[]{:S(2)}, u32[]{:S(2)}) collective-permute-start(bf16[24,32,512]{2,1,0:T(8,128)(2,1)S(1)} %shard_map.75), channel_id=1, source_target_pairs={{0,1},{1,0},{2,3},{3,2},{4,5},{5,4},{6,7},{7,6},{8,9},{9,8},{10,11... | collective-permute-start | bytes 2359304 | tf_op jit(solution)/shard_map/ppermute | solution.py:271
  78.2 10.7 %collective-permute-start.20 = (bf16[8,32,512]{2,1,0:T(8,128)(2,1)S(1)}, bf16[8,32,512]{2,1,0:T(8,128)(2,1)S(1)}, u32[]{:S(2)}, u32[]{:S(2)}) collective-permute-start(bf16[8,32,512]{2,1,0:T(8,128)(2,1)S(1)} %get-tuple-element.122), channel_id=1, source_target_pairs={{0,4},{4,0},{8,12},{12,8},{1,5},{5,1},{9,13},{13,9},{2,6},{6,2},{1... | collective-permute-start | bytes 786440 | tf_op jit(solution)/shard_map/ppermute | solution.py:227
  78.3 19.9 %collective-permute-start.18 = (bf16[8,32,512]{2,1,0:T(8,128)(2,1)S(1)}, bf16[8,32,512]{2,1,0:T(8,128)(2,1)S(1)}, u32[]{:S(2)}, u32[]{:S(2)}) collective-permute-start(bf16[8,32,512]{2,1,0:T(8,128)(2,1)S(1)} %get-tuple-element.119), channel_id=1, source_target_pairs={{0,8},{4,12},{8,0},{12,4},{1,9},{5,13},{9,1},{13,5},{2,10},{6,14},... | collective-permute-start | bytes 786440 | tf_op jit(solution)/shard_map/ppermute | solution.py:227
  80.3 24.4 %collective-permute-start.19 = (bf16[8,32,512]{2,1,0:T(8,128)(2,1)S(1)}, bf16[8,32,512]{2,1,0:T(8,128)(2,1)S(1)}, u32[]{:S(2)}, u32[]{:S(2)}) collective-permute-start(bf16[8,32,512]{2,1,0:T(8,128)(2,1)S(1)} %get-tuple-element.120), channel_id=1, source_target_pairs={{0,12},{4,8},{8,4},{12,0},{1,13},{5,9},{9,5},{13,1},{2,14},{6,10},... | collective-permute-start | bytes 786440 | tf_op jit(solution)/shard_map/ppermute | solution.py:227
  (7 other events, 57.1 us)

commit v5 on v4

--- a/solution.py
+++ b/solution.py
@@ -12,57 +12,10 @@
 VMEM_LIMIT = 24 * 1024 * 1024
 
 
-def spread_kernel(where, modes_ref, down_ref, up_ref, *, parts):
-    freq, n_modes = modes_ref.shape
-    modes = modes_ref[...]
-    freqs = freq // parts
-
-    def pick(shape, axis):
-        big = lax.broadcasted_iota(jnp.int32, shape, axis) // ROWS
-        small = lax.broadcasted_iota(jnp.int32, shape, 1 - axis)
-        if freq in shape:
-            piece, within = big // freqs, big % freqs
-            big = within
-            for j in range(parts):
-                big = jnp.where(piece == j, where[j] * freqs + within, big)
-        return jnp.where(big == small, 1.0, 0.0).astype(jnp.bfloat16)
-
-    def lane(shape):
-        rows = lax.broadcasted_iota(jnp.int32, shape, 0) % ROWS
-        columns = lax.broadcasted_iota(jnp.int32, shape, 1) % ROWS
-        return rows == columns
-
-    def dot(a, b, dims):
-        return lax.dot_general(a, b, (dims, ((), ())), preferred_element_type=jnp.float32)
-
-    tall = dot(pick((n_modes * ROWS, n_modes), 0), modes, ((1,), (1,))).astype(jnp.bfloat16)
-    value = dot(tall, pick((freq, freq * ROWS), 1), ((1,), (0,)))
-    down_ref[...] = jnp.where(lane(value.shape), value, 0.0).astype(jnp.bfloat16)
-    tall = dot(pick((freq * ROWS, freq), 0), modes, ((1,), (0,))).astype(jnp.bfloat16)
-    value = dot(tall, pick((n_modes, n_modes * ROWS), 1), ((1,), (0,)))
-    up_ref[...] = jnp.where(lane(value.shape), value, 0.0).astype(jnp.bfloat16)
-
-
-def spread(where, modes, parts):
-    freq, n_modes = modes.shape
-    vmem = pl.BlockSpec(memory_space=pltpu.VMEM)
-    return pl.pallas_call(
-        functools.partial(spread_kernel, parts=parts),
-        grid_spec=pltpu.PrefetchScalarGridSpec(
-            num_scalar_prefetch=1, grid=(), in_specs=[vmem], out_specs=[vmem, vmem]
-        ),
-        out_shape=[
-            jax.ShapeDtypeStruct((n_modes * ROWS, freq * ROWS), jnp.bfloat16),
-            jax.ShapeDtypeStruct((freq * ROWS, n_modes * ROWS), jnp.bfloat16),
-        ],
-        compiler_params=pltpu.CompilerParams(vmem_limit_bytes=VMEM_LIMIT),
-        cost_estimate=pl.CostEstimate(flops=1024, bytes_accessed=1024, transcendentals=0),
-    )(where, modes)
-
-
-def hold_kernel(where, beam, held, mask, sems):
+def hold_kernel(where, beam, modes_ref, held, down_ref, up_ref, mask, sems):
     freq, base, ell = held.shape
-    ell_tiles, base_tiles = ell // TILE, base // TILE
+    n_modes = modes_ref.shape[1]
+    ell_tiles, base_tiles, freqs = ell // TILE, base // TILE, freq // PARTS
     copies = [pltpu.make_async_copy(beam.at[f], held.at[f], sems.at[f]) for f in range(freq)]
     for copy in copies:
         copy.start()
@@ -72,26 +25,58 @@
             mask[b * TILE:(b + 1) * TILE, l * TILE:(l + 1) * TILE] = jnp.full(
                 (TILE, TILE), kept, jnp.float32
             ).astype(jnp.bfloat16)
+    modes = modes_ref[...]
+
+    def pick(shape, axis):
+        big = lax.broadcasted_iota(jnp.int32, shape, axis) // ROWS
+        small = lax.broadcasted_iota(jnp.int32, shape, 1 - axis)
+        if freq in shape:
+            piece, within = big // freqs, big % freqs
+            big = within
+            for j in range(PARTS):
+                big = jnp.where(piece == j, where[j] * freqs + within, big)
+        return jnp.where(big == small, 1.0, 0.0).astype(jnp.bfloat16)
+
+    def lane(shape):
+        rows = lax.broadcasted_iota(jnp.int32, shape, 0) % ROWS
+        columns = lax.broadcasted_iota(jnp.int32, shape, 1) % ROWS
+        return rows == columns
+
+    def dot(a, b, dims):
+        return lax.dot_general(a, b, (dims, ((), ())), preferred_element_type=jnp.float32)
+
+    tall = dot(pick((n_modes * ROWS, n_modes), 0), modes, ((1,), (1,))).astype(jnp.bfloat16)
+    value = dot(tall, pick((freq, freq * ROWS), 1), ((1,), (0,)))
+    down_ref[...] = jnp.where(lane(value.shape), value, 0.0).astype(jnp.bfloat16)
+    tall = dot(pick((freq * ROWS, freq), 0), modes, ((1,), (0,))).astype(jnp.bfloat16)
+    value = dot(tall, pick((n_modes, n_modes * ROWS), 1), ((1,), (0,)))
+    up_ref[...] = jnp.where(lane(value.shape), value, 0.0).astype(jnp.bfloat16)
     for f, copy in enumerate(copies):
         copy.wait()
         held[f] = held[f] * mask[...]
 
 
-def hold(where, beam):
+def hold(where, beam, modes):
     freq, base, ell = beam.shape
+    size, wide = freq * ROWS, modes.shape[1] * ROWS
+    vmem = pl.BlockSpec(memory_space=pltpu.VMEM)
     return pl.pallas_call(
         hold_kernel,
         grid_spec=pltpu.PrefetchScalarGridSpec(
             num_scalar_prefetch=1,
             grid=(),
-            in_specs=[pl.BlockSpec(memory_space=pl.ANY)],
-            out_specs=pl.BlockSpec(memory_space=pltpu.VMEM),
+            in_specs=[pl.BlockSpec(memory_space=pl.ANY), vmem],
+            out_specs=[vmem] * 3,
             scratch_shapes=[pltpu.VMEM((base, ell), jnp.bfloat16), pltpu.SemaphoreType.DMA((freq,))],
         ),
-        out_shape=pltpu.VMEM(beam.shape, beam.dtype),
-        compiler_params=pltpu.CompilerParams(vmem_limit_bytes=VMEM_LIMIT),
-        cost_estimate=pl.CostEstimate(flops=1024, bytes_accessed=1024, transcendentals=0),
-    )(where, beam)
+        out_shape=[
+            pltpu.VMEM(beam.shape, beam.dtype),
+            jax.ShapeDtypeStruct((wide, size), jnp.bfloat16),
+            jax.ShapeDtypeStruct((size, wide), jnp.bfloat16),
+        ],
+        compiler_params=pltpu.CompilerParams(vmem_limit_bytes=VMEM_LIMIT),
+        cost_estimate=pl.CostEstimate(flops=1024, bytes_accessed=1024, transcendentals=0),
+    )(where, beam, modes)
 
 
 def project_kernel(where, mine, others, held, stay_ref, leave_ref, *, piece):
@@ -236,7 +221,6 @@
     block_ids = x * ell_tiles + jnp.arange(ell_tiles, dtype=jnp.int32)
     keep = tile_mask[0] * (first_block[0] <= block_ids).astype(jnp.int32)[None, :]
     where = jnp.concatenate([order, (x == p).astype(jnp.int32)[None], keep.reshape(-1)])
-    down, up = spread(where, eigen_modes[0], parts)
     ratio = signal_noise[0] / (1.0 + signal_noise[0])
     ratios = jnp.broadcast_to(ratio[:, None, None], (n_modes, 1, ell))
     beam = beam_transfer.reshape(freq_total, base, ell)
@@ -244,28 +228,27 @@
 
     fence = lax.optimization_barrier
     most = rows_all - ROWS
-    a = [cut(j, 0, ROWS) for j in range(1, parts)]
-    mine = cut(0, 0, rows_all)
-    b = [cut(j, ROWS, most) for j in range(1, parts)]
-    a = [along_z(a[j - 1], j) for j in (1, 2, 3)]
-    others = along_x(mine)
-    held = hold(where, beam)
-    stay_own, leave_own = project(where, mine, others, held, 0)
-    a, b, held, stay_own, leave_own, down, up = fence((a, b, held, stay_own, leave_own, down, up))
-    b[0], b[1] = along_z(b[0], 1), along_z(b[1], 2)
-    skies = [project(where, a[j - 1], along_x(a[j - 1]), held, j) for j in (1, 2, 3)]
+    a = {j: along_z(cut(j, 0, ROWS), j) for j in (3, 2, 1)}
+    mine = [cut(0, 0, rows_all)[n:n + freqs // 2] for n in (0, freqs // 2)]
+    others = [along_x(part) for part in mine]
+    b = {j: cut(j, ROWS, most) for j in (1, 2, 3)}
+    held, down, up = hold(where, beam, eigen_modes[0])
+    (a[3], a[2], a[1]), b, others, down, up = fence(((a[3], a[2], a[1]), b, others, down, up))
+    b[1], b[2] = along_z(b[1], 1), along_z(b[2], 2)
+    stay_own, leave_own = project(where, jnp.concatenate(mine, axis=0), jnp.concatenate(others, axis=0), held, 0)
+    skies = [project(where, a[j], along_x(a[j]), held, j) for j in (1, 2, 3)]
     stay_a = [stay_own] + [stay for stay, _ in skies]
     gone = reduce(down, [leave_own] + [leave for _, leave in skies], 0, n_modes)
-    b, held, stay_a, gone = fence((b, held, stay_a, gone))
-    b[2] = along_z(b[2], 3)
-    x_1, x_2 = along_x(b[0]), along_x(b[1])
+    b, stay_a, gone = fence((b, stay_a, gone))
+    b[3] = along_z(b[3], 3)
+    x_1, x_2 = along_x(b[1]), along_x(b[2])
     outs = restore(stay_a, 0, lax.ppermute(gone, "pol", other), ratios, down, up, freqs)
-    stay_1, leave_1 = project(where, b[0], x_1, held, 1)
-    b, x_2, held, outs, stay_1, leave_1 = fence((b, x_2, held, outs, stay_1, leave_1))
+    stay_1, leave_1 = project(where, b[1], x_1, held, 1)
+    b, x_2, outs, stay_1, leave_1 = fence((b, x_2, outs, stay_1, leave_1))
     back_a = [outs[0]] + [along_z(outs[j], j) for j in range(1, parts)]
-    x_3 = along_x(b[2])
-    stay_2, leave_2 = project(where, b[1], x_2, held, 2)
-    stay_3, leave_3 = project(where, b[2], x_3, held, 3)
+    x_3 = along_x(b[3])
+    stay_2, leave_2 = project(where, b[2], x_2, held, 2)
+    stay_3, leave_3 = project(where, b[3], x_3, held, 3)
     gone = reduce(down, [leave_own, leave_1, leave_2, leave_3], ROWS, n_modes)
     back_a, stay_2, stay_3, gone = fence((back_a, stay_2, stay_3, gone))
     came = lax.ppermute(gone, "pol", other)

time: 106 us -> 93 us (0.88)
  local copies, waits for them, and re-layouts: 14.1 us -> 2.64 us
  waiting for transfers between devices: 44.1 us -> 41.8 us
  starting transfers between devices: 21.5 us -> 22.9 us
    unnamed x21 -> x9, local copies, waits for them, and re-layouts: 11.6 us -> 0.1 us
    ppermute x7 -> x8, waiting for transfers between devices: 15.5 us -> 10.3 us  [along_x(): return lax.ppermute(value, 'kl', other)]
    ppermute x12, waiting for transfers between devices: 26.4 us -> 29.2 us  [along_z(): return lax.ppermute(value, 'fm', [(i, i ^ j) for i in range(parts)])]
    ppermute x7 -> x8, starting transfers between devices: 6.73 us -> 8.22 us  [along_x(): return lax.ppermute(value, 'kl', other)]
    pallas_call x1 -> x0, Pallas kernels: 1.17 us -> none  [spread(): pl.pallas_call(functools.partial(spread_kernel, parts=parts), grid_spec=p...]
    reshape x3 -> x2, local copies, waits for them, and re-layouts: 2.17 us -> 1.15 us  [cut(): lax.dynamic_slice(visibility, (0, z ^ j, first, 0), (freqs, 1, rows, base))]
  transfers between devices with their start and end apart: 21 -> 22, of which waited for: 12 -> 11; matrix products, arithmetic and copies ran while one was open for 1% -> 2% of each run, Pallas kernels for 21% -> 23%
where the time goes in v5:
time: 93 us; the launch traced here: 92.8 us
  waiting for transfers between devices  41.8 us (45%)
  Pallas kernels  24.4 us (26%)
  starting transfers between devices  22.9 us (25%)
  local copies, waits for them, and re-layouts  2.64 us (3%)
    ppermute x12, waiting for transfers between devices, along_z(): return lax.ppermute(value, 'fm', [(i, i ^ j) for i in range(parts)])  29.2 us
    ppermute x12, starting transfers between devices, along_z(): return lax.ppermute(value, 'fm', [(i, i ^ j) for i in range(parts)])  14.7 us
    ppermute x8, waiting for transfers between devices, along_x(): return lax.ppermute(value, 'kl', other)  10.3 us
    pallas_call x7, Pallas kernels, project(): pl.pallas_call(functools.partial(project_kernel, piece=piece), grid_spec=...  9.54 us
    ppermute x8, starting transfers between devices, along_x(): return lax.ppermute(value, 'kl', other)  8.22 us
    pallas_call x1, Pallas kernels, hold(): pl.pallas_call(hold_kernel, grid_spec=pltpu.PrefetchScalarGridSpec(num_sc...  7.04 us
    pallas_call x3, Pallas kernels, place(): pl.pallas_call(functools.partial(place_kernel, spots=spots, first=first),...  4.06 us
    pallas_call x2, Pallas kernels, restore(): pl.pallas_call(restore_kernel, grid=(rows // ROWS,), in_specs=[fixed(down...  2.51 us
  transfers between devices with their start and end apart: 22, of which 11 were waited for; matrix products, arithmetic and copies ran while one was open for 2% of the time, Pallas kernels for 23%

profile of v5, /device:TPU:12, one launch (start us, length us, event | category | flops | bytes accessed | tf_op | source)
XLA Modules:
  0.0 92.8 jit_solution(10409270877873832451)
XLA Ops:
  1.1 1.6 %collective-permute-start = (bf16[8,16,512]{2,1,0:T(8,128)(2,1)S(1)}, bf16[8,16,512]{2,1,0:T(8,128)(2,1)S(1)}, u32[]{:S(2)}, u32[]{:S(2)}) collective-permute-start(bf16[8,16,512]{2,1,0:T(8,128)(2,1)S(1)} %get-tuple-element.130), channel_id=1, source_target_pairs={{0,12},{4,8},{8,4},{12,0},{1,13},{5,9},{9,5},{13,1},{2,14},{6,10},... | collective-permute-start | bytes 393224 | tf_op jit(solution)/shard_map/ppermute | solution.py:212
  6.3 1.6 %collective-permute-start.3 = (bf16[4,48,512]{2,1,0:T(8,128)(2,1)S(1)}, bf16[4,48,512]{2,1,0:T(8,128)(2,1)S(1)}, u32[]{:S(2)}, u32[]{:S(2)}) collective-permute-start(bf16[4,48,512]{2,1,0:T(8,128)(2,1)S(1)} %get-tuple-element.124), channel_id=1, source_target_pairs={{0,2},{2,0},{1,3},{3,1},{4,6},{6,4},{5,7},{7,5},{8,10},{10,8},{9,1... | collective-permute-start | bytes 589832 | tf_op jit(solution)/shard_map/ppermute | solution.py:215
  9.4 7.0 %shard_map.64 = (bf16[32,512,512]{2,1,0:T(8,128)(2,1)S(1)}, bf16[384,512]{1,0:T(8,128)(2,1)S(1)}, bf16[512,384]{1,0:T(8,128)(2,1)S(1)}) custom-call(s32[21]{0:T(128)S(1)} %concatenate.9.where, bf16[32,512,512]{2,1,0:T(8,128)(2,1)} %bitcast.33, bf16[32,24]{1,0:T(8,128)(2,1)S(1)} %bitcast.32), custom_call_target="tpu_custom_call" | custom-call | flops 1024 | bytes 1024 | tf_op jit(solution)/shard_map/pallas_call | solution.py:63
  17.4 2.2 %collective-permute-start.6 = (bf16[8,32,512]{2,1,0:T(8,128)(2,1)S(1)}, bf16[8,32,512]{2,1,0:T(8,128)(2,1)S(1)}, u32[]{:S(2)}, u32[]{:S(2)}) collective-permute-start(bf16[8,32,512]{2,1,0:T(8,128)(2,1)S(1)} %get-tuple-element.69), channel_id=1, source_target_pairs={{0,8},{4,12},{8,0},{12,4},{1,9},{5,13},{9,1},{13,5},{2,10},{6,14},... | collective-permute-start | bytes 786440 | tf_op jit(solution)/shard_map/ppermute | solution.py:212
  19.6 1.5 %collective-permute-start.9 = (bf16[8,16,512]{2,1,0:T(8,128)(2,1)S(1)}, bf16[8,16,512]{2,1,0:T(8,128)(2,1)S(1)}, u32[]{:S(2)}, u32[]{:S(2)}) collective-permute-start(bf16[8,16,512]{2,1,0:T(8,128)(2,1)S(1)} %collective-permute-done.mine), channel_id=1, source_target_pairs={{0,2},{2,0},{1,3},{3,1},{4,6},{6,4},{5,7},{7,5},{8,10},{10,8},{9,1... | collective-permute-start | bytes 393224 | tf_op jit(solution)/shard_map/ppermute | solution.py:215
  21.7 1.5 %collective-permute-start.7 = (bf16[8,16,512]{2,1,0:T(8,128)(2,1)S(1)}, bf16[8,16,512]{2,1,0:T(8,128)(2,1)S(1)}, u32[]{:S(2)}, u32[]{:S(2)}) collective-permute-start(bf16[8,16,512]{2,1,0:T(8,128)(2,1)S(1)} %collective-permute-done.2.mine), channel_id=1, source_target_pairs={{0,2},{2,0},{1,3},{3,1},{4,6},{6,4},{5,7},{7,5},{8,10},{10,8},{9,1... | collective-permute-start | bytes 393224 | tf_op jit(solution)/shard_map/ppermute | solution.py:215
  24.6 1.4 %collective-permute-done.9.others = bf16[8,16,512]{2,1,0:T(8,128)(2,1)S(1)} collective-permute-done((bf16[8,16,512]{2,1,0:T(8,128)(2,1)S(1)}, bf16[8,16,512]{2,1,0:T(8,128)(2,1)S(1)}, u32[]{:S(2)}, u32[]{:S(2)}) %collective-permute-start.9) | collective-permute-done | bytes 131104 | tf_op jit(solution)/shard_map/ppermute | solution.py:215
  30.7 1.6 %collective-permute-start.13 = (bf16[8,32,512]{2,1,0:T(8,128)(2,1)S(1)}, bf16[8,32,512]{2,1,0:T(8,128)(2,1)S(1)}, u32[]{:S(2)}, u32[]{:S(2)}) collective-permute-start(bf16[8,32,512]{2,1,0:T(8,128)(2,1)S(1)} %collective-permute-done.5.mine), channel_id=1, source_target_pairs={{0,2},{2,0},{1,3},{3,1},{4,6},{6,4},{5,7},{7,5},{8,10},{10,8},{9,1... | collective-permute-start | bytes 786440 | tf_op jit(solution)/shard_map/ppermute | solution.py:215
  33.2 6.6 %collective-permute-done.13.others = bf16[8,32,512]{2,1,0:T(8,128)(2,1)S(1)} collective-permute-done((bf16[8,32,512]{2,1,0:T(8,128)(2,1)S(1)}, bf16[8,32,512]{2,1,0:T(8,128)(2,1)S(1)}, u32[]{:S(2)}, u32[]{:S(2)}) %collective-permute-start.13) | collective-permute-done | bytes 262176 | tf_op jit(solution)/shard_map/ppermute | solution.py:215
  39.8 1.4 %shard_map.71 = (bf16[8,32,512]{2,1,0:T(8,128)(2,1)S(1)}, bf16[8,32,512]{2,1,0:T(8,128)(2,1)S(1)}) custom-call(s32[21]{0:T(128)S(1)} %concatenate.9.where, bf16[8,32,512]{2,1,0:T(8,128)(2,1)S(1)} %collective-permute-done.5.mine, bf16[8,32,512]{2,1,0:T(8,128)(2,1)S(1)} %collective-permute-done.13.others, bf16[32,512,512]{2,1,0:T(8,128)(2,1)S(1)} %get-tuple-element.73.held), custom_call_target="tpu_custom_call" | custom-call | flops 1024 | bytes 1024 | tf_op jit(solution)/shard_map/pallas_call | solution.py:98
  42.1 4.1 %collective-permute-done.10.mine = bf16[8,32,512]{2,1,0:T(8,128)(2,1)S(1)} collective-permute-done((bf16[8,32,512]{2,1,0:T(8,128)(2,1)S(1)}, bf16[8,32,512]{2,1,0:T(8,128)(2,1)S(1)}, u32[]{:S(2)}, u32[]{:S(2)}) %collective-permute-start.10) | collective-permute-done | bytes 262176 | tf_op jit(solution)/shard_map/ppermute | solution.py:212
  46.7 1.4 %collective-permute-start.14 = (bf16[8,16,512]{2,1,0:T(8,128)(2,1)S(1)}, bf16[8,16,512]{2,1,0:T(8,128)(2,1)S(1)}, u32[]{:S(2)}, u32[]{:S(2)}) collective-permute-start(bf16[8,16,512]{2,1,0:T(8,128)(2,1)S(1)} %get-tuple-element.100), channel_id=1, source_target_pairs={{0,4},{4,0},{8,12},{12,8},{1,5},{5,1},{9,13},{13,9},{2,6},{6,2},{1... | collective-permute-start | bytes 393224 | tf_op jit(solution)/shard_map/ppermute | solution.py:212
  48.7 1.5 %collective-permute-start.16 = (bf16[8,16,512]{2,1,0:T(8,128)(2,1)S(1)}, bf16[8,16,512]{2,1,0:T(8,128)(2,1)S(1)}, u32[]{:S(2)}, u32[]{:S(2)}) collective-permute-start(bf16[8,16,512]{2,1,0:T(8,128)(2,1)S(1)} %get-tuple-element.102), channel_id=1, source_target_pairs={{0,12},{4,8},{8,4},{12,0},{1,13},{5,9},{9,5},{13,1},{2,14},{6,10},... | collective-permute-start | bytes 393224 | tf_op jit(solution)/shard_map/ppermute | solution.py:212
  50.2 1.4 %shard_map.72 = (bf16[8,32,512]{2,1,0:T(8,128)(2,1)S(1)}, bf16[8,32,512]{2,1,0:T(8,128)(2,1)S(1)}) custom-call(s32[21]{0:T(128)S(1)} %concatenate.9.where, bf16[8,32,512]{2,1,0:T(8,128)(2,1)S(1)} %collective-permute-done.6.mine, bf16[8,32,512]{2,1,0:T(8,128)(2,1)S(1)} %collective-permute-done.11.others, bf16[32,512,512]{2,1,0:T(8,128)(2,1)S(1)} %get-tuple-element.73.held), custom_call_target="tpu_custom_call" | custom-call | flops 1024 | bytes 1024 | tf_op jit(solution)/shard_map/pallas_call | solution.py:98
  51.6 2.1 %collective-permute-done.17.others = bf16[8,32,512]{2,1,0:T(8,128)(2,1)S(1)} collective-permute-done((bf16[8,32,512]{2,1,0:T(8,128)(2,1)S(1)}, bf16[8,32,512]{2,1,0:T(8,128)(2,1)S(1)}, u32[]{:S(2)}, u32[]{:S(2)}) %collective-permute-start.17) | collective-permute-done | bytes 262176 | tf_op jit(solution)/shard_map/ppermute | solution.py:215
  53.8 1.4 %shard_map.73 = (bf16[8,32,512]{2,1,0:T(8,128)(2,1)S(1)}, bf16[8,32,512]{2,1,0:T(8,128)(2,1)S(1)}) custom-call(s32[21]{0:T(128)S(1)} %concatenate.9.where, bf16[8,32,512]{2,1,0:T(8,128)(2,1)S(1)} %collective-permute-done.10.mine, bf16[8,32,512]{2,1,0:T(8,128)(2,1)S(1)} %collective-permute-done.17.others, bf16[32,512,512]{2,1,0:T(8,128)(2,1)S(1)} %get-tuple-element.73.held), custom_call_target="tpu_custom_call" | custom-call | flops 1024 | bytes 1024 | tf_op jit(solution)/shard_map/pallas_call | solution.py:98
  56.1 2.0 %collective-permute-done.15.refs_2_ = bf16[8,16,512]{2,1,0:T(8,128)(2,1)S(1)} collective-permute-done((bf16[8,16,512]{2,1,0:T(8,128)(2,1)S(1)}, bf16[8,16,512]{2,1,0:T(8,128)(2,1)S(1)}, u32[]{:S(2)}, u32[]{:S(2)}) %collective-permute-start.15) | collective-permute-done | bytes 131104 | tf_op jit(solution)/shard_map/ppermute | solution.py:212
  58.1 2.8 %collective-permute-done.16.refs_3_ = bf16[8,16,512]{2,1,0:T(8,128)(2,1)S(1)} collective-permute-done((bf16[8,16,512]{2,1,0:T(8,128)(2,1)S(1)}, bf16[8,16,512]{2,1,0:T(8,128)(2,1)S(1)}, u32[]{:S(2)}, u32[]{:S(2)}) %collective-permute-start.16) | collective-permute-done | bytes 131104 | tf_op jit(solution)/shard_map/ppermute | solution.py:212
  60.9 2.3 %collective-permute-done.18.came_ref = bf16[24,32,512]{2,1,0:T(8,128)(2,1)S(1)} collective-permute-done((bf16[24,32,512]{2,1,0:T(8,128)(2,1)S(1)}, bf16[24,32,512]{2,1,0:T(8,128)(2,1)S(1)}, u32[]{:S(2)}, u32[]{:S(2)}) %collective-permute-start.18) | collective-permute-done | bytes 786464 | tf_op jit(solution)/shard_map/ppermute | solution.py:254
  63.2 1.8 %shard_map.75 = (bf16[8,32,512]{2,1,0:T(8,128)(2,1)S(1)}, bf16[8,32,512]{2,1,0:T(8,128)(2,1)S(1)}, bf16[8,32,512]{2,1,0:T(8,128)(2,1)S(1)}, bf16[8,32,512]{2,1,0:T(8,128)(2,1)S(1)}) custom-call(bf16[384,512]{1,0:T(8,128)(2,1)S(1)} %get-tuple-element.66.modes_ref.down_ref, bf16[512,384]{1,0:T(8,128)(2,1)S(1)} %get-tuple-element.67.up_ref, ...), custom_call_target="tpu_custom_call" | custom-call | flops 1024 | bytes 1024 | tf_op jit(solution)/shard_map/pallas_call | solution.py:157
  65.1 2.5 %collective-permute-start.19 = (bf16[8,32,512]{2,1,0:T(8,128)(2,1)S(1)}, bf16[8,32,512]{2,1,0:T(8,128)(2,1)S(1)}, u32[]{:S(2)}, u32[]{:S(2)}) collective-permute-start(bf16[8,32,512]{2,1,0:T(8,128)(2,1)S(1)} %get-tuple-element.115), channel_id=1, source_target_pairs={{0,8},{4,12},{8,0},{12,4},{1,9},{5,13},{9,1},{13,5},{2,10},{6,14},... | collective-permute-start | bytes 786440 | tf_op jit(solution)/shard_map/ppermute | solution.py:212
  69.9 6.1 %collective-permute-done.21.refs_1_ = bf16[8,32,512]{2,1,0:T(8,128)(2,1)S(1)} collective-permute-done((bf16[8,32,512]{2,1,0:T(8,128)(2,1)S(1)}, bf16[8,32,512]{2,1,0:T(8,128)(2,1)S(1)}, u32[]{:S(2)}, u32[]{:S(2)}) %collective-permute-start.21) | collective-permute-done | bytes 262176 | tf_op jit(solution)/shard_map/ppermute | solution.py:212
  77.3 8.2 %collective-permute-done.19.refs_0_ = bf16[8,32,512]{2,1,0:T(8,128)(2,1)S(1)} collective-permute-done((bf16[8,32,512]{2,1,0:T(8,128)(2,1)S(1)}, bf16[8,32,512]{2,1,0:T(8,128)(2,1)S(1)}, u32[]{:S(2)}, u32[]{:S(2)}) %collective-permute-start.19) | collective-permute-done | bytes 262176 | tf_op jit(solution)/shard_map/ppermute | solution.py:212
  85.5 6.0 %collective-permute-done.20.refs_1_ = bf16[8,32,512]{2,1,0:T(8,128)(2,1)S(1)} collective-permute-done((bf16[8,32,512]{2,1,0:T(8,128)(2,1)S(1)}, bf16[8,32,512]{2,1,0:T(8,128)(2,1)S(1)}, u32[]{:S(2)}, u32[]{:S(2)}) %collective-permute-start.20) | collective-permute-done | bytes 262176 | tf_op jit(solution)/shard_map/ppermute | solution.py:212
  (57 shorter events, 22.0 us)
Async XLA Ops:
  0.0 9.1 %copy-start.2 = (s32[1,4,4]{2,1,0:T(4,128)S(1)}, s32[1,4,4]{2,1,0:T(4,128)}, u32[]{:S(2)}) copy-start(s32[1,4,4]{2,1,0:T(4,128)} %param.8) | copy-start | bytes 196
  0.0 9.2 %copy-start.1 = (bf16[1,32,24]{1,2,0:T(8,128)(2,1)S(1)}, bf16[1,32,24]{1,2,0:T(8,128)(2,1)}, u32[]{:S(2)}) copy-start(bf16[1,32,24]{1,2,0:T(8,128)(2,1)} %param.10) | copy-start | bytes 4612
  1.1 15.4 %collective-permute-start = (bf16[8,16,512]{2,1,0:T(8,128)(2,1)S(1)}, bf16[8,16,512]{2,1,0:T(8,128)(2,1)S(1)}, u32[]{:S(2)}, u32[]{:S(2)}) collective-permute-start(bf16[8,16,512]{2,1,0:T(8,128)(2,1)S(1)} %get-tuple-element.130), channel_id=1, source_target_pairs={{0,12},{4,8},{8,4},{12,0},{1,13},{5,9},{9,5},{13,1},{2,14},{6,10},... | collective-permute-start | bytes 393224 | tf_op jit(solution)/shard_map/ppermute | solution.py:212
  2.7 13.8 %collective-permute-start.1 = (bf16[8,16,512]{2,1,0:T(8,128)(2,1)S(1)}, bf16[8,16,512]{2,1,0:T(8,128)(2,1)S(1)}, u32[]{:S(2)}, u32[]{:S(2)}) collective-permute-start(bf16[8,16,512]{2,1,0:T(8,128)(2,1)S(1)} %get-tuple-element.129), channel_id=1, source_target_pairs={{0,8},{4,12},{8,0},{12,4},{1,9},{5,13},{9,1},{13,5},{2,10},{6,14},... | collective-permute-start | bytes 393224 | tf_op jit(solution)/shard_map/ppermute | solution.py:212
  4.0 12.6 %collective-permute-start.2 = (bf16[8,16,512]{2,1,0:T(8,128)(2,1)S(1)}, bf16[8,16,512]{2,1,0:T(8,128)(2,1)S(1)}, u32[]{:S(2)}, u32[]{:S(2)}) collective-permute-start(bf16[8,16,512]{2,1,0:T(8,128)(2,1)S(1)} %get-tuple-element.128), channel_id=1, source_target_pairs={{0,4},{4,0},{8,12},{12,8},{1,5},{5,1},{9,13},{13,9},{2,6},{6,2},{1... | collective-permute-start | bytes 393224 | tf_op jit(solution)/shard_map/ppermute | solution.py:212
  6.3 10.3 %collective-permute-start.3 = (bf16[4,48,512]{2,1,0:T(8,128)(2,1)S(1)}, bf16[4,48,512]{2,1,0:T(8,128)(2,1)S(1)}, u32[]{:S(2)}, u32[]{:S(2)}) collective-permute-start(bf16[4,48,512]{2,1,0:T(8,128)(2,1)S(1)} %get-tuple-element.124), channel_id=1, source_target_pairs={{0,2},{2,0},{1,3},{3,1},{4,6},{6,4},{5,7},{7,5},{8,10},{10,8},{9,1... | collective-permute-start | bytes 589832 | tf_op jit(solution)/shard_map/ppermute | solution.py:215
  7.8 8.8 %collective-permute-start.4 = (bf16[4,48,512]{2,1,0:T(8,128)(2,1)S(1)}, bf16[4,48,512]{2,1,0:T(8,128)(2,1)S(1)}, u32[]{:S(2)}, u32[]{:S(2)}) collective-permute-start(bf16[4,48,512]{2,1,0:T(8,128)(2,1)S(1)} %get-tuple-element.123), channel_id=1, source_target_pairs={{0,2},{2,0},{1,3},{3,1},{4,6},{6,4},{5,7},{7,5},{8,10},{10,8},{9,1... | collective-permute-start | bytes 589832 | tf_op jit(solution)/shard_map/ppermute | solution.py:215
  16.6 13.9 %collective-permute-start.5 = (bf16[8,32,512]{2,1,0:T(8,128)(2,1)S(1)}, bf16[8,32,512]{2,1,0:T(8,128)(2,1)S(1)}, u32[]{:S(2)}, u32[]{:S(2)}) collective-permute-start(bf16[8,32,512]{2,1,0:T(8,128)(2,1)S(1)} %get-tuple-element.68), channel_id=1, source_target_pairs={{0,4},{4,0},{8,12},{12,8},{1,5},{5,1},{9,13},{13,9},{2,6},{6,2},{1... | collective-permute-start | bytes 786440 | tf_op jit(solution)/shard_map/ppermute | solution.py:212
  17.4 13.2 %collective-permute-start.6 = (bf16[8,32,512]{2,1,0:T(8,128)(2,1)S(1)}, bf16[8,32,512]{2,1,0:T(8,128)(2,1)S(1)}, u32[]{:S(2)}, u32[]{:S(2)}) collective-permute-start(bf16[8,32,512]{2,1,0:T(8,128)(2,1)S(1)} %get-tuple-element.69), channel_id=1, source_target_pairs={{0,8},{4,12},{8,0},{12,4},{1,9},{5,13},{9,1},{13,5},{2,10},{6,14},... | collective-permute-start | bytes 786440 | tf_op jit(solution)/shard_map/ppermute | solution.py:212
  19.6 6.4 %collective-permute-start.9 = (bf16[8,16,512]{2,1,0:T(8,128)(2,1)S(1)}, bf16[8,16,512]{2,1,0:T(8,128)(2,1)S(1)}, u32[]{:S(2)}, u32[]{:S(2)}) collective-permute-start(bf16[8,16,512]{2,1,0:T(8,128)(2,1)S(1)} %collective-permute-done.mine), channel_id=1, source_target_pairs={{0,2},{2,0},{1,3},{3,1},{4,6},{6,4},{5,7},{7,5},{8,10},{10,8},{9,1... | collective-permute-start | bytes 393224 | tf_op jit(solution)/shard_map/ppermute | solution.py:215
  21.1 6.3 %collective-permute-start.8 = (bf16[8,16,512]{2,1,0:T(8,128)(2,1)S(1)}, bf16[8,16,512]{2,1,0:T(8,128)(2,1)S(1)}, u32[]{:S(2)}, u32[]{:S(2)}) collective-permute-start(bf16[8,16,512]{2,1,0:T(8,128)(2,1)S(1)} %collective-permute-done.1.mine), channel_id=1, source_target_pairs={{0,2},{2,0},{1,3},{3,1},{4,6},{6,4},{5,7},{7,5},{8,10},{10,8},{9,1... | collective-permute-start | bytes 393224 | tf_op jit(solution)/shard_map/ppermute | solution.py:215
  21.7 7.1 %collective-permute-start.7 = (bf16[8,16,512]{2,1,0:T(8,128)(2,1)S(1)}, bf16[8,16,512]{2,1,0:T(8,128)(2,1)S(1)}, u32[]{:S(2)}, u32[]{:S(2)}) collective-permute-start(bf16[8,16,512]{2,1,0:T(8,128)(2,1)S(1)} %collective-permute-done.2.mine), channel_id=1, source_target_pairs={{0,2},{2,0},{1,3},{3,1},{4,6},{6,4},{5,7},{7,5},{8,10},{10,8},{9,1... | collective-permute-start | bytes 393224 | tf_op jit(solution)/shard_map/ppermute | solution.py:215
  30.6 10.6 %collective-permute-start.12 = (bf16[24,16,512]{2,1,0:T(8,128)(2,1)S(1)}, bf16[24,16,512]{2,1,0:T(8,128)(2,1)S(1)}, u32[]{:S(2)}, u32[]{:S(2)}) collective-permute-start(bf16[24,16,512]{2,1,0:T(8,128)(2,1)S(1)} %shard_map.69), channel_id=1, source_target_pairs={{0,1},{1,0},{2,3},{3,2},{4,5},{5,4},{6,7},{7,6},{8,9},{9,8},{10,11... | collective-permute-start | bytes 1179656 | tf_op jit(solution)/shard_map/ppermute | solution.py:245
  30.7 9.2 %collective-permute-start.13 = (bf16[8,32,512]{2,1,0:T(8,128)(2,1)S(1)}, bf16[8,32,512]{2,1,0:T(8,128)(2,1)S(1)}, u32[]{:S(2)}, u32[]{:S(2)}) collective-permute-start(bf16[8,32,512]{2,1,0:T(8,128)(2,1)S(1)} %collective-permute-done.5.mine), channel_id=1, source_target_pairs={{0,2},{2,0},{1,3},{3,1},{4,6},{6,4},{5,7},{7,5},{8,10},{10,8},{9,1... | collective-permute-start | bytes 786440 | tf_op jit(solution)/shard_map/ppermute | solution.py:215
  32.2 14.0 %collective-permute-start.10 = (bf16[8,32,512]{2,1,0:T(8,128)(2,1)S(1)}, bf16[8,32,512]{2,1,0:T(8,128)(2,1)S(1)}, u32[]{:S(2)}, u32[]{:S(2)}) collective-permute-start(bf16[8,32,512]{2,1,0:T(8,128)(2,1)S(1)} %get-tuple-element.87), channel_id=1, source_target_pairs={{0,12},{4,8},{8,4},{12,0},{1,13},{5,9},{9,5},{13,1},{2,14},{6,10},... | collective-permute-start | bytes 786440 | tf_op jit(solution)/shard_map/ppermute | solution.py:212
  32.7 13.5 %collective-permute-start.11 = (bf16[8,32,512]{2,1,0:T(8,128)(2,1)S(1)}, bf16[8,32,512]{2,1,0:T(8,128)(2,1)S(1)}, u32[]{:S(2)}, u32[]{:S(2)}) collective-permute-start(bf16[8,32,512]{2,1,0:T(8,128)(2,1)S(1)} %collective-permute-done.6.mine), channel_id=1, source_target_pairs={{0,2},{2,0},{1,3},{3,1},{4,6},{6,4},{5,7},{7,5},{8,10},{10,8},{9,1... | collective-permute-start | bytes 786440 | tf_op jit(solution)/shard_map/ppermute | solution.py:215
  46.2 7.5 %collective-permute-start.17 = (bf16[8,32,512]{2,1,0:T(8,128)(2,1)S(1)}, bf16[8,32,512]{2,1,0:T(8,128)(2,1)S(1)}, u32[]{:S(2)}, u32[]{:S(2)}) collective-permute-start(bf16[8,32,512]{2,1,0:T(8,128)(2,1)S(1)} %collective-permute-done.10.mine), channel_id=1, source_target_pairs={{0,2},{2,0},{1,3},{3,1},{4,6},{6,4},{5,7},{7,5},{8,10},{10,8},{9,1... | collective-permute-start | bytes 786440 | tf_op jit(solution)/shard_map/ppermute | solution.py:215
  46.7 9.3 %collective-permute-start.14 = (bf16[8,16,512]{2,1,0:T(8,128)(2,1)S(1)}, bf16[8,16,512]{2,1,0:T(8,128)(2,1)S(1)}, u32[]{:S(2)}, u32[]{:S(2)}) collective-permute-start(bf16[8,16,512]{2,1,0:T(8,128)(2,1)S(1)} %get-tuple-element.100), channel_id=1, source_target_pairs={{0,4},{4,0},{8,12},{12,8},{1,5},{5,1},{9,13},{13,9},{2,6},{6,2},{1... | collective-permute-start | bytes 393224 | tf_op jit(solution)/shard_map/ppermute | solution.py:212
  48.2 9.9 %collective-permute-start.15 = (bf16[8,16,512]{2,1,0:T(8,128)(2,1)S(1)}, bf16[8,16,512]{2,1,0:T(8,128)(2,1)S(1)}, u32[]{:S(2)}, u32[]{:S(2)}) collective-permute-start(bf16[8,16,512]{2,1,0:T(8,128)(2,1)S(1)} %get-tuple-element.101), channel_id=1, source_target_pairs={{0,8},{4,12},{8,0},{12,4},{1,9},{5,13},{9,1},{13,5},{2,10},{6,14},... | collective-permute-start | bytes 393224 | tf_op jit(solution)/shard_map/ppermute | solution.py:212
  48.7 12.2 %collective-permute-start.16 = (bf16[8,16,512]{2,1,0:T(8,128)(2,1)S(1)}, bf16[8,16,512]{2,1,0:T(8,128)(2,1)S(1)}, u32[]{:S(2)}, u32[]{:S(2)}) collective-permute-start(bf16[8,16,512]{2,1,0:T(8,128)(2,1)S(1)} %get-tuple-element.102), channel_id=1, source_target_pairs={{0,12},{4,8},{8,4},{12,0},{1,13},{5,9},{9,5},{13,1},{2,14},{6,10},... | collective-permute-start | bytes 393224 | tf_op jit(solution)/shard_map/ppermute | solution.py:212
  60.9 2.3 %collective-permute-start.18 = (bf16[24,32,512]{2,1,0:T(8,128)(2,1)S(1)}, bf16[24,32,512]{2,1,0:T(8,128)(2,1)S(1)}, u32[]{:S(2)}, u32[]{:S(2)}) collective-permute-start(bf16[24,32,512]{2,1,0:T(8,128)(2,1)S(1)} %shard_map.74), channel_id=1, source_target_pairs={{0,1},{1,0},{2,3},{3,2},{4,5},{5,4},{6,7},{7,6},{8,9},{9,8},{10,11... | collective-permute-start | bytes 2359304 | tf_op jit(solution)/shard_map/ppermute | solution.py:254
  65.0 11.0 %collective-permute-start.21 = (bf16[8,32,512]{2,1,0:T(8,128)(2,1)S(1)}, bf16[8,32,512]{2,1,0:T(8,128)(2,1)S(1)}, u32[]{:S(2)}, u32[]{:S(2)}) collective-permute-start(bf16[8,32,512]{2,1,0:T(8,128)(2,1)S(1)} %get-tuple-element.118), channel_id=1, source_target_pairs={{0,4},{4,0},{8,12},{12,8},{1,5},{5,1},{9,13},{13,9},{2,6},{6,2},{1... | collective-permute-start | bytes 786440 | tf_op jit(solution)/shard_map/ppermute | solution.py:212
  65.1 20.4 %collective-permute-start.19 = (bf16[8,32,512]{2,1,0:T(8,128)(2,1)S(1)}, bf16[8,32,512]{2,1,0:T(8,128)(2,1)S(1)}, u32[]{:S(2)}, u32[]{:S(2)}) collective-permute-start(bf16[8,32,512]{2,1,0:T(8,128)(2,1)S(1)} %get-tuple-element.115), channel_id=1, source_target_pairs={{0,8},{4,12},{8,0},{12,4},{1,9},{5,13},{9,1},{13,5},{2,10},{6,14},... | collective-permute-start | bytes 786440 | tf_op jit(solution)/shard_map/ppermute | solution.py:212
  67.6 23.9 %collective-permute-start.20 = (bf16[8,32,512]{2,1,0:T(8,128)(2,1)S(1)}, bf16[8,32,512]{2,1,0:T(8,128)(2,1)S(1)}, u32[]{:S(2)}, u32[]{:S(2)}) collective-permute-start(bf16[8,32,512]{2,1,0:T(8,128)(2,1)S(1)} %get-tuple-element.116), channel_id=1, source_target_pairs={{0,12},{4,8},{8,4},{12,0},{1,13},{5,9},{9,5},{13,1},{2,14},{6,10},... | collective-permute-start | bytes 786440 | tf_op jit(solution)/shard_map/ppermute | solution.py:212
  (2 other events, 10.1 us)

commit v6 on v5

--- a/solution.py
+++ b/solution.py
@@ -12,7 +12,7 @@
 VMEM_LIMIT = 24 * 1024 * 1024
 
 
-def hold_kernel(where, beam, modes_ref, held, down_ref, up_ref, mask, sems):
+def hold_kernel(where, tiles, starts, beam, modes_ref, held, down_ref, up_ref, mask, sems):
     freq, base, ell = held.shape
     n_modes = modes_ref.shape[1]
     ell_tiles, base_tiles, freqs = ell // TILE, base // TILE, freq // PARTS
@@ -21,7 +21,7 @@
         copy.start()
     for b in range(base_tiles):
         for l in range(ell_tiles):
-            kept = where[PARTS + 1 + b * ell_tiles + l].astype(jnp.float32)
+            kept = jnp.where(starts[0] <= where[PARTS + 1] + l, tiles[b, l], 0).astype(jnp.float32)
             mask[b * TILE:(b + 1) * TILE, l * TILE:(l + 1) * TILE] = jnp.full(
                 (TILE, TILE), kept, jnp.float32
             ).astype(jnp.bfloat16)
@@ -56,14 +56,14 @@
         held[f] = held[f] * mask[...]
 
 
-def hold(where, beam, modes):
+def hold(where, tiles, starts, beam, modes):
     freq, base, ell = beam.shape
     size, wide = freq * ROWS, modes.shape[1] * ROWS
     vmem = pl.BlockSpec(memory_space=pltpu.VMEM)
     return pl.pallas_call(
         hold_kernel,
         grid_spec=pltpu.PrefetchScalarGridSpec(
-            num_scalar_prefetch=1,
+            num_scalar_prefetch=3,
             grid=(),
             in_specs=[pl.BlockSpec(memory_space=pl.ANY), vmem],
             out_specs=[vmem] * 3,
@@ -76,7 +76,7 @@
         ],
         compiler_params=pltpu.CompilerParams(vmem_limit_bytes=VMEM_LIMIT),
         cost_estimate=pl.CostEstimate(flops=1024, bytes_accessed=1024, transcendentals=0),
-    )(where, beam, modes)
+    )(where, tiles, starts, beam, modes)
 
 
 def project_kernel(where, mine, others, held, stay_ref, leave_ref, *, piece):
@@ -113,7 +113,7 @@
 
 def reduce_kernel(modes_ref, *refs):
     out = refs[-1]
-    out[...] = contract(modes_ref[...], refs[:-1]).astype(jnp.bfloat16).reshape(out.shape)
+    out[...] = contract(modes_ref[...], refs[:-1]).astype(out.dtype).reshape(out.shape)
 
 
 def by_rows(count, ell, first=0):
@@ -128,42 +128,40 @@
     return [by_rows(sky.shape[0], sky.shape[2], first if n == 0 else 0) for n, sky in enumerate(skies)]
 
 
-def reduce(modes, skies, first, n_modes):
+def reduce(modes, skies, first, n_modes, dtype=jnp.bfloat16):
     _, rows, ell = skies[-1].shape
     return pl.pallas_call(
         reduce_kernel,
         grid=(rows // ROWS,),
         in_specs=[fixed(modes.shape)] + sky_specs(skies, first),
         out_specs=by_rows(n_modes, ell),
-        out_shape=jax.ShapeDtypeStruct((n_modes, rows, ell), jnp.bfloat16),
+        out_shape=jax.ShapeDtypeStruct((n_modes, rows, ell), dtype),
         compiler_params=pltpu.CompilerParams(vmem_limit_bytes=VMEM_LIMIT),
         cost_estimate=pl.CostEstimate(flops=1024, bytes_accessed=1024, transcendentals=0),
     )(modes, *skies)
 
 
-def restore_kernel(down_ref, up_ref, ratio_ref, came_ref, *refs):
-    skies, outs = refs[:-PARTS], refs[-PARTS:]
+def restore_kernel(up_ref, ratio_ref, kept_ref, came_ref, *outs, spots):
     n_modes, _, ell = came_ref.shape
     size = outs[0].shape[0] * ROWS
-    total = contract(down_ref[...], skies).reshape(came_ref.shape) + came_ref[...].astype(jnp.float32)
+    total = kept_ref[...] + came_ref[...].astype(jnp.float32)
     weighted = (total * ratio_ref[...]).astype(jnp.bfloat16).reshape(n_modes * ROWS, ell)
-    for which, out in enumerate(outs):
+    for which, out in zip(spots, outs):
         value = jnp.dot(up_ref[which * size:(which + 1) * size, :], weighted, preferred_element_type=jnp.float32)
         out[...] = value.astype(jnp.bfloat16).reshape(out.shape)
 
 
-def restore(skies, first, came, ratios, down, up, freqs):
+def restore(kept, came, ratios, up, freqs, spots):
     n_modes, rows, ell = came.shape
     return pl.pallas_call(
-        restore_kernel,
+        functools.partial(restore_kernel, spots=spots),
         grid=(rows // ROWS,),
-        in_specs=[fixed(down.shape), fixed(up.shape), fixed(ratios.shape), by_rows(n_modes, ell)]
-        + sky_specs(skies, first),
-        out_specs=[by_rows(freqs, ell)] * PARTS,
-        out_shape=[jax.ShapeDtypeStruct((freqs, rows, ell), jnp.bfloat16)] * PARTS,
-        compiler_params=pltpu.CompilerParams(vmem_limit_bytes=VMEM_LIMIT),
-        cost_estimate=pl.CostEstimate(flops=1024, bytes_accessed=1024, transcendentals=0),
-    )(down, up, ratios, came, *skies)
+        in_specs=[fixed(up.shape), fixed(ratios.shape)] + [by_rows(n_modes, ell)] * 2,
+        out_specs=[by_rows(freqs, ell)] * len(spots),
+        out_shape=[jax.ShapeDtypeStruct((freqs, rows, ell), jnp.bfloat16)] * len(spots),
+        compiler_params=pltpu.CompilerParams(vmem_limit_bytes=VMEM_LIMIT),
+        cost_estimate=pl.CostEstimate(flops=1024, bytes_accessed=1024, transcendentals=0),
+    )(up, ratios, kept, came)
 
 
 def place_kernel(where, *refs, spots, first):
@@ -217,46 +215,52 @@
     def cut(j, first, rows):
         return lax.dynamic_slice(visibility, (0, z ^ j, first, 0), (freqs, 1, rows, base)).reshape(freqs, rows, base)
 
-    order = jnp.stack([z ^ j for j in range(parts)]).astype(jnp.int32)
-    block_ids = x * ell_tiles + jnp.arange(ell_tiles, dtype=jnp.int32)
-    keep = tile_mask[0] * (first_block[0] <= block_ids).astype(jnp.int32)[None, :]
-    where = jnp.concatenate([order, (x == p).astype(jnp.int32)[None], keep.reshape(-1)])
+    index = jnp.arange(parts + 2, dtype=jnp.int32)
+    where = jnp.where(
+        index < parts, z ^ index, jnp.where(index == parts, (x == p).astype(jnp.int32), x * ell_tiles)
+    ).astype(jnp.int32)
     ratio = signal_noise[0] / (1.0 + signal_noise[0])
     ratios = jnp.broadcast_to(ratio[:, None, None], (n_modes, 1, ell))
     beam = beam_transfer.reshape(freq_total, base, ell)
     shape = (freqs, parts, rows_all, ell)
 
     fence = lax.optimization_barrier
-    most = rows_all - ROWS
+    most, half = rows_all - ROWS, freqs // 2
     a = {j: along_z(cut(j, 0, ROWS), j) for j in (3, 2, 1)}
-    mine = [cut(0, 0, rows_all)[n:n + freqs // 2] for n in (0, freqs // 2)]
+    mine = [cut(0, 0, rows_all)[n:n + half] for n in (0, half)]
     others = [along_x(part) for part in mine]
     b = {j: cut(j, ROWS, most) for j in (1, 2, 3)}
-    held, down, up = hold(where, beam, eigen_modes[0])
+    held, down, up = hold(where, tile_mask[0], first_block, beam, eigen_modes[0])
     (a[3], a[2], a[1]), b, others, down, up = fence(((a[3], a[2], a[1]), b, others, down, up))
     b[1], b[2] = along_z(b[1], 1), along_z(b[2], 2)
     stay_own, leave_own = project(where, jnp.concatenate(mine, axis=0), jnp.concatenate(others, axis=0), held, 0)
     skies = [project(where, a[j], along_x(a[j]), held, j) for j in (1, 2, 3)]
     stay_a = [stay_own] + [stay for stay, _ in skies]
     gone = reduce(down, [leave_own] + [leave for _, leave in skies], 0, n_modes)
-    b, stay_a, gone = fence((b, stay_a, gone))
+    (b[2], b[1]), b[3], stay_a, gone = fence(((b[2], b[1]), b[3], stay_a, gone))
+    x_2, x_1 = along_x(b[2]), along_x(b[1])
     b[3] = along_z(b[3], 3)
-    x_1, x_2 = along_x(b[1]), along_x(b[2])
-    outs = restore(stay_a, 0, lax.ppermute(gone, "pol", other), ratios, down, up, freqs)
+    kept = reduce(down, stay_a, 0, n_modes, jnp.float32)
+    outs = restore(kept, lax.ppermute(gone, "pol", other), ratios, up, freqs, (0, 1, 2, 3))
     stay_1, leave_1 = project(where, b[1], x_1, held, 1)
-    b, x_2, outs, stay_1, leave_1 = fence((b, x_2, outs, stay_1, leave_1))
+    x_2, b, outs, stay_1, leave_1 = fence((x_2, b, outs, stay_1, leave_1))
     back_a = [outs[0]] + [along_z(outs[j], j) for j in range(1, parts)]
     x_3 = along_x(b[3])
     stay_2, leave_2 = project(where, b[2], x_2, held, 2)
     stay_3, leave_3 = project(where, b[3], x_3, held, 3)
     gone = reduce(down, [leave_own, leave_1, leave_2, leave_3], ROWS, n_modes)
-    back_a, stay_2, stay_3, gone = fence((back_a, stay_2, stay_3, gone))
+    kept = reduce(down, [stay_own, stay_1, stay_2, stay_3], ROWS, n_modes, jnp.float32)
+    (back_a[2], back_a[3], back_a[1]), back_a[0], kept, gone = fence(
+        ((back_a[2], back_a[3], back_a[1]), back_a[0], kept, gone)
+    )
     came = lax.ppermute(gone, "pol", other)
-    outs = restore([stay_own, stay_1, stay_2, stay_3], ROWS, came, ratios, down, up, freqs)
-    back_b = [outs[0]] + [along_z(outs[j], j) for j in range(1, parts)]
+    outs = dict(zip((3, 2), restore(kept, came, ratios, up, freqs, (3, 2))))
+    outs.update(zip((1, 0), restore(kept, came, ratios, up, freqs, (1, 0))))
+    back_b = {j: along_z(outs[j], j) for j in (3, 2, 1)}
+    back_b[0] = outs[0]
     result = place(where, back_a, (0, 1, 2, 3), 0, shape)
-    result = place(where, back_b, (0, 1), ROWS, shape, into=result)
-    return place(where, back_b, (2, 3), ROWS, shape, into=result)
+    result = place(where, back_b, (0,), ROWS, shape, into=result)
+    return place(where, back_b, (3, 2, 1), ROWS, shape, into=result)
 
 
 def plain(visibility, beam_transfer, tile_mask, first_block, eigen_modes, signal_noise):

time: 93 us -> 93.1 us (level)
  the two profiles are of different devices: /device:TPU:12 before, /device:TPU:0 now
where the time goes in v6:
time: 93.1 us; the launch traced here: 93 us
  waiting for transfers between devices  34.7 us (37%)
  starting transfers between devices  29.2 us (31%)
  Pallas kernels  25.6 us (27%)
  local copies, waits for them, and re-layouts  2.39 us (3%)
    ppermute x12, waiting for transfers between devices, along_z(): return lax.ppermute(value, 'fm', [(i, i ^ j) for i in range(parts)])  21.7 us
    ppermute x12, starting transfers between devices, along_z(): return lax.ppermute(value, 'fm', [(i, i ^ j) for i in range(parts)])  20 us
    ppermute x8, waiting for transfers between devices, along_x(): return lax.ppermute(value, 'kl', other)  10.8 us
    pallas_call x7, Pallas kernels, project(): pl.pallas_call(functools.partial(project_kernel, piece=piece), grid_spec=...  9.56 us
    ppermute x8, starting transfers between devices, along_x(): return lax.ppermute(value, 'kl', other)  9.19 us
    pallas_call x1, Pallas kernels, hold(): pl.pallas_call(hold_kernel, grid_spec=pltpu.PrefetchScalarGridSpec(num_sc...  7.04 us
    pallas_call x3, Pallas kernels, place(): pl.pallas_call(functools.partial(place_kernel, spots=spots, first=first),...  4.06 us
    pallas_call x4, Pallas kernels, reduce(): pl.pallas_call(reduce_kernel, grid=(rows // ROWS,), in_specs=[fixed(modes...  2.62 us
  transfers between devices with their start and end apart: 22, of which 10 were waited for; matrix products, arithmetic and copies ran while one was open for 1% of the time, Pallas kernels for 25%

profile of v6, /device:TPU:0, one launch (start us, length us, event | category | flops | bytes accessed | tf_op | source)
XLA Modules:
  0.0 93.0 jit_solution(10205303166115297242)
XLA Ops:
  1.1 5.1 %collective-permute-start = (bf16[8,16,512]{2,1,0:T(8,128)(2,1)S(1)}, bf16[8,16,512]{2,1,0:T(8,128)(2,1)S(1)}, u32[]{:S(2)}, u32[]{:S(2)}) collective-permute-start(bf16[8,16,512]{2,1,0:T(8,128)(2,1)S(1)} %get-tuple-element.128), channel_id=1, source_target_pairs={{0,12},{4,8},{8,4},{12,0},{1,13},{5,9},{9,5},{13,1},{2,14},{6,10},... | collective-permute-start | bytes 393224 | tf_op jit(solution)/shard_map/ppermute | solution.py:210
  7.9 1.7 %collective-permute-start.3 = (bf16[4,48,512]{2,1,0:T(8,128)(2,1)S(1)}, bf16[4,48,512]{2,1,0:T(8,128)(2,1)S(1)}, u32[]{:S(2)}, u32[]{:S(2)}) collective-permute-start(bf16[4,48,512]{2,1,0:T(8,128)(2,1)S(1)} %get-tuple-element.122), channel_id=1, source_target_pairs={{0,2},{2,0},{1,3},{3,1},{4,6},{6,4},{5,7},{7,5},{8,10},{10,8},{9,1... | collective-permute-start | bytes 589832 | tf_op jit(solution)/shard_map/ppermute | solution.py:213
  10.8 7.0 %shard_map.64 = (bf16[32,512,512]{2,1,0:T(8,128)(2,1)S(1)}, bf16[384,512]{1,0:T(8,128)(2,1)S(1)}, bf16[512,384]{1,0:T(8,128)(2,1)S(1)}) custom-call(s32[6]{0:T(128)S(1)} %compare_select_fusion.1.where, s32[4,4]{1,0:T(4,128)S(1)} %bitcast.27, s32[1]{0:T(128)S(6)} %copy.16.starts, bf16[32,512,512]{2,1,0:T(8,128)(2,1)} %bitcast.28, bf16[32,24]{1,0:T(8,128)(2,1)S(1)} %bitcast.26), custom_call_target="tpu_custom_call" | custom-call | flops 1024 | bytes 1024 | tf_op jit(solution)/shard_map/pallas_call | solution.py:63
  18.3 2.3 %collective-permute-start.5 = (bf16[8,32,512]{2,1,0:T(8,128)(2,1)S(1)}, bf16[8,32,512]{2,1,0:T(8,128)(2,1)S(1)}, u32[]{:S(2)}, u32[]{:S(2)}) collective-permute-start(bf16[8,32,512]{2,1,0:T(8,128)(2,1)S(1)} %get-tuple-element.66), channel_id=1, source_target_pairs={{0,8},{4,12},{8,0},{12,4},{1,9},{5,13},{9,1},{13,5},{2,10},{6,14},... | collective-permute-start | bytes 786440 | tf_op jit(solution)/shard_map/ppermute | solution.py:210
  20.5 1.8 %collective-permute-start.6 = (bf16[8,32,512]{2,1,0:T(8,128)(2,1)S(1)}, bf16[8,32,512]{2,1,0:T(8,128)(2,1)S(1)}, u32[]{:S(2)}, u32[]{:S(2)}) collective-permute-start(bf16[8,32,512]{2,1,0:T(8,128)(2,1)S(1)} %get-tuple-element.67), channel_id=1, source_target_pairs={{0,4},{4,0},{8,12},{12,8},{1,5},{5,1},{9,13},{13,9},{2,6},{6,2},{1... | collective-permute-start | bytes 786440 | tf_op jit(solution)/shard_map/ppermute | solution.py:210
  22.3 1.5 %collective-permute-start.7 = (bf16[8,16,512]{2,1,0:T(8,128)(2,1)S(1)}, bf16[8,16,512]{2,1,0:T(8,128)(2,1)S(1)}, u32[]{:S(2)}, u32[]{:S(2)}) collective-permute-start(bf16[8,16,512]{2,1,0:T(8,128)(2,1)S(1)} %collective-permute-done.2.mine), channel_id=1, source_target_pairs={{0,2},{2,0},{1,3},{3,1},{4,6},{6,4},{5,7},{7,5},{8,10},{10,8},{9,1... | collective-permute-start | bytes 393224 | tf_op jit(solution)/shard_map/ppermute | solution.py:213
  24.4 1.5 %collective-permute-start.9 = (bf16[8,16,512]{2,1,0:T(8,128)(2,1)S(1)}, bf16[8,16,512]{2,1,0:T(8,128)(2,1)S(1)}, u32[]{:S(2)}, u32[]{:S(2)}) collective-permute-start(bf16[8,16,512]{2,1,0:T(8,128)(2,1)S(1)} %collective-permute-done.mine), channel_id=1, source_target_pairs={{0,2},{2,0},{1,3},{3,1},{4,6},{6,4},{5,7},{7,5},{8,10},{10,8},{9,1... | collective-permute-start | bytes 393224 | tf_op jit(solution)/shard_map/ppermute | solution.py:213
  33.1 1.6 %collective-permute-start.13 = (bf16[8,32,512]{2,1,0:T(8,128)(2,1)S(1)}, bf16[8,32,512]{2,1,0:T(8,128)(2,1)S(1)}, u32[]{:S(2)}, u32[]{:S(2)}) collective-permute-start(bf16[8,32,512]{2,1,0:T(8,128)(2,1)S(1)} %collective-permute-done.6.mine), channel_id=1, source_target_pairs={{0,2},{2,0},{1,3},{3,1},{4,6},{6,4},{5,7},{7,5},{8,10},{10,8},{9,1... | collective-permute-start | bytes 786440 | tf_op jit(solution)/shard_map/ppermute | solution.py:213
  35.2 1.5 %collective-permute-start.11 = (bf16[8,32,512]{2,1,0:T(8,128)(2,1)S(1)}, bf16[8,32,512]{2,1,0:T(8,128)(2,1)S(1)}, u32[]{:S(2)}, u32[]{:S(2)}) collective-permute-start(bf16[8,32,512]{2,1,0:T(8,128)(2,1)S(1)} %get-tuple-element.86), channel_id=1, source_target_pairs={{0,12},{4,8},{8,4},{12,0},{1,13},{5,9},{9,5},{13,1},{2,14},{6,10},... | collective-permute-start | bytes 786440 | tf_op jit(solution)/shard_map/ppermute | solution.py:210
  37.1 5.2 %collective-permute-done.13.others = bf16[8,32,512]{2,1,0:T(8,128)(2,1)S(1)} collective-permute-done((bf16[8,32,512]{2,1,0:T(8,128)(2,1)S(1)}, bf16[8,32,512]{2,1,0:T(8,128)(2,1)S(1)}, u32[]{:S(2)}, u32[]{:S(2)}) %collective-permute-start.13) | collective-permute-done | bytes 262176 | tf_op jit(solution)/shard_map/ppermute | solution.py:213
  42.2 1.4 %shard_map.72 = (bf16[8,32,512]{2,1,0:T(8,128)(2,1)S(1)}, bf16[8,32,512]{2,1,0:T(8,128)(2,1)S(1)}) custom-call(s32[6]{0:T(128)S(1)} %compare_select_fusion.1.where, bf16[8,32,512]{2,1,0:T(8,128)(2,1)S(1)} %collective-permute-done.6.mine, bf16[8,32,512]{2,1,0:T(8,128)(2,1)S(1)} %collective-permute-done.13.others, bf16[32,512,512]{2,1,0:T(8,128)(2,1)S(1)} %get-tuple-element.71.held), custom_call_target="tpu_custom_call" | custom-call | flops 1024 | bytes 1024 | tf_op jit(solution)/shard_map/pallas_call | solution.py:98
  44.3 3.2 %collective-permute-done.10.others = bf16[8,32,512]{2,1,0:T(8,128)(2,1)S(1)} collective-permute-done((bf16[8,32,512]{2,1,0:T(8,128)(2,1)S(1)}, bf16[8,32,512]{2,1,0:T(8,128)(2,1)S(1)}, u32[]{:S(2)}, u32[]{:S(2)}) %collective-permute-start.10) | collective-permute-done | bytes 262176 | tf_op jit(solution)/shard_map/ppermute | solution.py:213
  47.4 1.5 %collective-permute-start.17 = (bf16[8,32,512]{2,1,0:T(8,128)(2,1)S(1)}, bf16[8,32,512]{2,1,0:T(8,128)(2,1)S(1)}, u32[]{:S(2)}, u32[]{:S(2)}) collective-permute-start(bf16[8,32,512]{2,1,0:T(8,128)(2,1)S(1)} %collective-permute-done.11.mine), channel_id=1, source_target_pairs={{0,2},{2,0},{1,3},{3,1},{4,6},{6,4},{5,7},{7,5},{8,10},{10,8},{9,1... | collective-permute-start | bytes 786440 | tf_op jit(solution)/shard_map/ppermute | solution.py:213
  48.9 1.8 %collective-permute-start.14 = (bf16[8,16,512]{2,1,0:T(8,128)(2,1)S(1)}, bf16[8,16,512]{2,1,0:T(8,128)(2,1)S(1)}, u32[]{:S(2)}, u32[]{:S(2)}) collective-permute-start(bf16[8,16,512]{2,1,0:T(8,128)(2,1)S(1)} %get-tuple-element.98), channel_id=1, source_target_pairs={{0,8},{4,12},{8,0},{12,4},{1,9},{5,13},{9,1},{13,5},{2,10},{6,14},... | collective-permute-start | bytes 393224 | tf_op jit(solution)/shard_map/ppermute | solution.py:210
  50.7 2.3 %collective-permute-start.15 = (bf16[8,16,512]{2,1,0:T(8,128)(2,1)S(1)}, bf16[8,16,512]{2,1,0:T(8,128)(2,1)S(1)}, u32[]{:S(2)}, u32[]{:S(2)}) collective-permute-start(bf16[8,16,512]{2,1,0:T(8,128)(2,1)S(1)} %get-tuple-element.99), channel_id=1, source_target_pairs={{0,12},{4,8},{8,4},{12,0},{1,13},{5,9},{9,5},{13,1},{2,14},{6,10},... | collective-permute-start | bytes 393224 | tf_op jit(solution)/shard_map/ppermute | solution.py:210
  53.0 1.4 %shard_map.73 = (bf16[8,32,512]{2,1,0:T(8,128)(2,1)S(1)}, bf16[8,32,512]{2,1,0:T(8,128)(2,1)S(1)}) custom-call(s32[6]{0:T(128)S(1)} %compare_select_fusion.1.where, bf16[8,32,512]{2,1,0:T(8,128)(2,1)S(1)} %collective-permute-done.5.mine, bf16[8,32,512]{2,1,0:T(8,128)(2,1)S(1)} %collective-permute-done.10.others, bf16[32,512,512]{2,1,0:T(8,128)(2,1)S(1)} %get-tuple-element.71.held), custom_call_target="tpu_custom_call" | custom-call | flops 1024 | bytes 1024 | tf_op jit(solution)/shard_map/pallas_call | solution.py:98
  55.3 1.4 %shard_map.74 = (bf16[8,32,512]{2,1,0:T(8,128)(2,1)S(1)}, bf16[8,32,512]{2,1,0:T(8,128)(2,1)S(1)}) custom-call(s32[6]{0:T(128)S(1)} %compare_select_fusion.1.where, bf16[8,32,512]{2,1,0:T(8,128)(2,1)S(1)} %collective-permute-done.11.mine, bf16[8,32,512]{2,1,0:T(8,128)(2,1)S(1)} %collective-permute-done.17.others, ...), custom_call_target="tpu_custom_call" | custom-call | flops 1024 | bytes 1024 | tf_op jit(solution)/shard_map/pallas_call | solution.py:98
  58.6 2.4 %collective-permute-done.14.refs_2_ = bf16[8,16,512]{2,1,0:T(8,128)(2,1)S(1)} collective-permute-done((bf16[8,16,512]{2,1,0:T(8,128)(2,1)S(1)}, bf16[8,16,512]{2,1,0:T(8,128)(2,1)S(1)}, u32[]{:S(2)}, u32[]{:S(2)}) %collective-permute-start.14) | collective-permute-done | bytes 131104 | tf_op jit(solution)/shard_map/ppermute | solution.py:210
  61.6 2.3 %collective-permute-done.18.came_ref = bf16[24,32,512]{2,1,0:T(8,128)(2,1)S(1)} collective-permute-done((bf16[24,32,512]{2,1,0:T(8,128)(2,1)S(1)}, bf16[24,32,512]{2,1,0:T(8,128)(2,1)S(1)}, u32[]{:S(2)}, u32[]{:S(2)}) %collective-permute-start.18) | collective-permute-done | bytes 786464 | tf_op jit(solution)/shard_map/ppermute | solution.py:256
  64.8 1.7 %collective-permute-start.19 = (bf16[8,32,512]{2,1,0:T(8,128)(2,1)S(1)}, bf16[8,32,512]{2,1,0:T(8,128)(2,1)S(1)}, u32[]{:S(2)}, u32[]{:S(2)}) collective-permute-start(bf16[8,32,512]{2,1,0:T(8,128)(2,1)S(1)} %get-tuple-element.113), channel_id=1, source_target_pairs={{0,12},{4,8},{8,4},{12,0},{1,13},{5,9},{9,5},{13,1},{2,14},{6,10},... | collective-permute-start | bytes 786440 | tf_op jit(solution)/shard_map/ppermute | solution.py:210
  66.5 1.9 %collective-permute-start.20 = (bf16[8,32,512]{2,1,0:T(8,128)(2,1)S(1)}, bf16[8,32,512]{2,1,0:T(8,128)(2,1)S(1)}, u32[]{:S(2)}, u32[]{:S(2)}) collective-permute-start(bf16[8,32,512]{2,1,0:T(8,128)(2,1)S(1)} %get-tuple-element.114), channel_id=1, source_target_pairs={{0,8},{4,12},{8,0},{12,4},{1,9},{5,13},{9,1},{13,5},{2,10},{6,14},... | collective-permute-start | bytes 786440 | tf_op jit(solution)/shard_map/ppermute | solution.py:210
  72.9 3.1 %collective-permute-done.19.refs_0_ = bf16[8,32,512]{2,1,0:T(8,128)(2,1)S(1)} collective-permute-done((bf16[8,32,512]{2,1,0:T(8,128)(2,1)S(1)}, bf16[8,32,512]{2,1,0:T(8,128)(2,1)S(1)}, u32[]{:S(2)}, u32[]{:S(2)}) %collective-permute-start.19) | collective-permute-done | bytes 262176 | tf_op jit(solution)/shard_map/ppermute | solution.py:210
  76.0 15.6 %collective-permute-done.20.refs_1_ = bf16[8,32,512]{2,1,0:T(8,128)(2,1)S(1)} collective-permute-done((bf16[8,32,512]{2,1,0:T(8,128)(2,1)S(1)}, bf16[8,32,512]{2,1,0:T(8,128)(2,1)S(1)}, u32[]{:S(2)}, u32[]{:S(2)}) %collective-permute-start.20) | collective-permute-done | bytes 262176 | tf_op jit(solution)/shard_map/ppermute | solution.py:210
  91.5 1.4 %shard_map.81 = bf16[8,4,48,512]{3,2,1,0:T(8,128)(2,1)} custom-call(s32[6]{0:T(128)S(1)} %compare_select_fusion.1.where, bf16[8,32,512]{2,1,0:T(8,128)(2,1)S(1)} %collective-permute-done.19.refs_0_, bf16[8,32,512]{2,1,0:T(8,128)(2,1)S(1)} %collective-permute-done.20.refs_1_, ...), custom_call_target="tpu_custom_call", output_to_operand_aliasing={{}: (4, {})} | custom-call | flops 1024 | bytes 1024 | tf_op jit(solution)/shard_map/pallas_call | solution.py:185
  (55 shorter events, 21.7 us)
Async XLA Ops:
  0.0 10.6 %copy-start.2 = (bf16[1,32,24]{1,2,0:T(8,128)(2,1)S(1)}, bf16[1,32,24]{1,2,0:T(8,128)(2,1)}, u32[]{:S(2)}) copy-start(bf16[1,32,24]{1,2,0:T(8,128)(2,1)} %param.10) | copy-start | bytes 4612
  0.0 10.7 %copy-start = (s32[1,4,4]{2,1,0:T(4,128)S(1)}, s32[1,4,4]{2,1,0:T(4,128)}, u32[]{:S(2)}) copy-start(s32[1,4,4]{2,1,0:T(4,128)} %param.8) | copy-start | bytes 196
  1.1 16.8 %collective-permute-start = (bf16[8,16,512]{2,1,0:T(8,128)(2,1)S(1)}, bf16[8,16,512]{2,1,0:T(8,128)(2,1)S(1)}, u32[]{:S(2)}, u32[]{:S(2)}) collective-permute-start(bf16[8,16,512]{2,1,0:T(8,128)(2,1)S(1)} %get-tuple-element.128), channel_id=1, source_target_pairs={{0,12},{4,8},{8,4},{12,0},{1,13},{5,9},{9,5},{13,1},{2,14},{6,10},... | collective-permute-start | bytes 393224 | tf_op jit(solution)/shard_map/ppermute | solution.py:210
  6.2 11.7 %collective-permute-start.1 = (bf16[8,16,512]{2,1,0:T(8,128)(2,1)S(1)}, bf16[8,16,512]{2,1,0:T(8,128)(2,1)S(1)}, u32[]{:S(2)}, u32[]{:S(2)}) collective-permute-start(bf16[8,16,512]{2,1,0:T(8,128)(2,1)S(1)} %get-tuple-element.127), channel_id=1, source_target_pairs={{0,8},{4,12},{8,0},{12,4},{1,9},{5,13},{9,1},{13,5},{2,10},{6,14},... | collective-permute-start | bytes 393224 | tf_op jit(solution)/shard_map/ppermute | solution.py:210
  6.2 11.7 %collective-permute-start.2 = (bf16[8,16,512]{2,1,0:T(8,128)(2,1)S(1)}, bf16[8,16,512]{2,1,0:T(8,128)(2,1)S(1)}, u32[]{:S(2)}, u32[]{:S(2)}) collective-permute-start(bf16[8,16,512]{2,1,0:T(8,128)(2,1)S(1)} %get-tuple-element.126), channel_id=1, source_target_pairs={{0,4},{4,0},{8,12},{12,8},{1,5},{5,1},{9,13},{13,9},{2,6},{6,2},{1... | collective-permute-start | bytes 393224 | tf_op jit(solution)/shard_map/ppermute | solution.py:210
  7.9 10.0 %collective-permute-start.3 = (bf16[4,48,512]{2,1,0:T(8,128)(2,1)S(1)}, bf16[4,48,512]{2,1,0:T(8,128)(2,1)S(1)}, u32[]{:S(2)}, u32[]{:S(2)}) collective-permute-start(bf16[4,48,512]{2,1,0:T(8,128)(2,1)S(1)} %get-tuple-element.122), channel_id=1, source_target_pairs={{0,2},{2,0},{1,3},{3,1},{4,6},{6,4},{5,7},{7,5},{8,10},{10,8},{9,1... | collective-permute-start | bytes 589832 | tf_op jit(solution)/shard_map/ppermute | solution.py:213
  9.6 8.7 %collective-permute-start.4 = (bf16[4,48,512]{2,1,0:T(8,128)(2,1)S(1)}, bf16[4,48,512]{2,1,0:T(8,128)(2,1)S(1)}, u32[]{:S(2)}, u32[]{:S(2)}) collective-permute-start(bf16[4,48,512]{2,1,0:T(8,128)(2,1)S(1)} %get-tuple-element.121), channel_id=1, source_target_pairs={{0,2},{2,0},{1,3},{3,1},{4,6},{6,4},{5,7},{7,5},{8,10},{10,8},{9,1... | collective-permute-start | bytes 589832 | tf_op jit(solution)/shard_map/ppermute | solution.py:213
  18.3 14.7 %collective-permute-start.5 = (bf16[8,32,512]{2,1,0:T(8,128)(2,1)S(1)}, bf16[8,32,512]{2,1,0:T(8,128)(2,1)S(1)}, u32[]{:S(2)}, u32[]{:S(2)}) collective-permute-start(bf16[8,32,512]{2,1,0:T(8,128)(2,1)S(1)} %get-tuple-element.66), channel_id=1, source_target_pairs={{0,8},{4,12},{8,0},{12,4},{1,9},{5,13},{9,1},{13,5},{2,10},{6,14},... | collective-permute-start | bytes 786440 | tf_op jit(solution)/shard_map/ppermute | solution.py:210
  20.5 12.4 %collective-permute-start.6 = (bf16[8,32,512]{2,1,0:T(8,128)(2,1)S(1)}, bf16[8,32,512]{2,1,0:T(8,128)(2,1)S(1)}, u32[]{:S(2)}, u32[]{:S(2)}) collective-permute-start(bf16[8,32,512]{2,1,0:T(8,128)(2,1)S(1)} %get-tuple-element.67), channel_id=1, source_target_pairs={{0,4},{4,0},{8,12},{12,8},{1,5},{5,1},{9,13},{13,9},{2,6},{6,2},{1... | collective-permute-start | bytes 786440 | tf_op jit(solution)/shard_map/ppermute | solution.py:210
  22.3 6.1 %collective-permute-start.7 = (bf16[8,16,512]{2,1,0:T(8,128)(2,1)S(1)}, bf16[8,16,512]{2,1,0:T(8,128)(2,1)S(1)}, u32[]{:S(2)}, u32[]{:S(2)}) collective-permute-start(bf16[8,16,512]{2,1,0:T(8,128)(2,1)S(1)} %collective-permute-done.2.mine), channel_id=1, source_target_pairs={{0,2},{2,0},{1,3},{3,1},{4,6},{6,4},{5,7},{7,5},{8,10},{10,8},{9,1... | collective-permute-start | bytes 393224 | tf_op jit(solution)/shard_map/ppermute | solution.py:213
  23.8 6.0 %collective-permute-start.8 = (bf16[8,16,512]{2,1,0:T(8,128)(2,1)S(1)}, bf16[8,16,512]{2,1,0:T(8,128)(2,1)S(1)}, u32[]{:S(2)}, u32[]{:S(2)}) collective-permute-start(bf16[8,16,512]{2,1,0:T(8,128)(2,1)S(1)} %collective-permute-done.1.mine), channel_id=1, source_target_pairs={{0,2},{2,0},{1,3},{3,1},{4,6},{6,4},{5,7},{7,5},{8,10},{10,8},{9,1... | collective-permute-start | bytes 393224 | tf_op jit(solution)/shard_map/ppermute | solution.py:213
  24.4 6.9 %collective-permute-start.9 = (bf16[8,16,512]{2,1,0:T(8,128)(2,1)S(1)}, bf16[8,16,512]{2,1,0:T(8,128)(2,1)S(1)}, u32[]{:S(2)}, u32[]{:S(2)}) collective-permute-start(bf16[8,16,512]{2,1,0:T(8,128)(2,1)S(1)} %collective-permute-done.mine), channel_id=1, source_target_pairs={{0,2},{2,0},{1,3},{3,1},{4,6},{6,4},{5,7},{7,5},{8,10},{10,8},{9,1... | collective-permute-start | bytes 393224 | tf_op jit(solution)/shard_map/ppermute | solution.py:213
  33.0 10.6 %collective-permute-start.12 = (bf16[24,16,512]{2,1,0:T(8,128)(2,1)S(1)}, bf16[24,16,512]{2,1,0:T(8,128)(2,1)S(1)}, u32[]{:S(2)}, u32[]{:S(2)}) collective-permute-start(bf16[24,16,512]{2,1,0:T(8,128)(2,1)S(1)} %shard_map.69), channel_id=1, source_target_pairs={{0,1},{1,0},{2,3},{3,2},{4,5},{5,4},{6,7},{7,6},{8,9},{9,8},{10,11... | collective-permute-start | bytes 1179656 | tf_op jit(solution)/shard_map/ppermute | solution.py:244
  33.1 9.2 %collective-permute-start.13 = (bf16[8,32,512]{2,1,0:T(8,128)(2,1)S(1)}, bf16[8,32,512]{2,1,0:T(8,128)(2,1)S(1)}, u32[]{:S(2)}, u32[]{:S(2)}) collective-permute-start(bf16[8,32,512]{2,1,0:T(8,128)(2,1)S(1)} %collective-permute-done.6.mine), channel_id=1, source_target_pairs={{0,2},{2,0},{1,3},{3,1},{4,6},{6,4},{5,7},{7,5},{8,10},{10,8},{9,1... | collective-permute-start | bytes 786440 | tf_op jit(solution)/shard_map/ppermute | solution.py:213
  34.6 12.8 %collective-permute-start.10 = (bf16[8,32,512]{2,1,0:T(8,128)(2,1)S(1)}, bf16[8,32,512]{2,1,0:T(8,128)(2,1)S(1)}, u32[]{:S(2)}, u32[]{:S(2)}) collective-permute-start(bf16[8,32,512]{2,1,0:T(8,128)(2,1)S(1)} %collective-permute-done.5.mine), channel_id=1, source_target_pairs={{0,2},{2,0},{1,3},{3,1},{4,6},{6,4},{5,7},{7,5},{8,10},{10,8},{9,1... | collective-permute-start | bytes 786440 | tf_op jit(solution)/shard_map/ppermute | solution.py:213
  35.2 12.3 %collective-permute-start.11 = (bf16[8,32,512]{2,1,0:T(8,128)(2,1)S(1)}, bf16[8,32,512]{2,1,0:T(8,128)(2,1)S(1)}, u32[]{:S(2)}, u32[]{:S(2)}) collective-permute-start(bf16[8,32,512]{2,1,0:T(8,128)(2,1)S(1)} %get-tuple-element.86), channel_id=1, source_target_pairs={{0,12},{4,8},{8,4},{12,0},{1,13},{5,9},{9,5},{13,1},{2,14},{6,10},... | collective-permute-start | bytes 786440 | tf_op jit(solution)/shard_map/ppermute | solution.py:210
  47.4 7.9 %collective-permute-start.17 = (bf16[8,32,512]{2,1,0:T(8,128)(2,1)S(1)}, bf16[8,32,512]{2,1,0:T(8,128)(2,1)S(1)}, u32[]{:S(2)}, u32[]{:S(2)}) collective-permute-start(bf16[8,32,512]{2,1,0:T(8,128)(2,1)S(1)} %collective-permute-done.11.mine), channel_id=1, source_target_pairs={{0,2},{2,0},{1,3},{3,1},{4,6},{6,4},{5,7},{7,5},{8,10},{10,8},{9,1... | collective-permute-start | bytes 786440 | tf_op jit(solution)/shard_map/ppermute | solution.py:213
  48.9 12.0 %collective-permute-start.14 = (bf16[8,16,512]{2,1,0:T(8,128)(2,1)S(1)}, bf16[8,16,512]{2,1,0:T(8,128)(2,1)S(1)}, u32[]{:S(2)}, u32[]{:S(2)}) collective-permute-start(bf16[8,16,512]{2,1,0:T(8,128)(2,1)S(1)} %get-tuple-element.98), channel_id=1, source_target_pairs={{0,8},{4,12},{8,0},{12,4},{1,9},{5,13},{9,1},{13,5},{2,10},{6,14},... | collective-permute-start | bytes 393224 | tf_op jit(solution)/shard_map/ppermute | solution.py:210
  50.7 10.2 %collective-permute-start.15 = (bf16[8,16,512]{2,1,0:T(8,128)(2,1)S(1)}, bf16[8,16,512]{2,1,0:T(8,128)(2,1)S(1)}, u32[]{:S(2)}, u32[]{:S(2)}) collective-permute-start(bf16[8,16,512]{2,1,0:T(8,128)(2,1)S(1)} %get-tuple-element.99), channel_id=1, source_target_pairs={{0,12},{4,8},{8,4},{12,0},{1,13},{5,9},{9,5},{13,1},{2,14},{6,10},... | collective-permute-start | bytes 393224 | tf_op jit(solution)/shard_map/ppermute | solution.py:210
  53.0 8.6 %collective-permute-start.16 = (bf16[8,16,512]{2,1,0:T(8,128)(2,1)S(1)}, bf16[8,16,512]{2,1,0:T(8,128)(2,1)S(1)}, u32[]{:S(2)}, u32[]{:S(2)}) collective-permute-start(bf16[8,16,512]{2,1,0:T(8,128)(2,1)S(1)} %get-tuple-element.100), channel_id=1, source_target_pairs={{0,4},{4,0},{8,12},{12,8},{1,5},{5,1},{9,13},{13,9},{2,6},{6,2},{1... | collective-permute-start | bytes 393224 | tf_op jit(solution)/shard_map/ppermute | solution.py:210
  61.6 2.3 %collective-permute-start.18 = (bf16[24,32,512]{2,1,0:T(8,128)(2,1)S(1)}, bf16[24,32,512]{2,1,0:T(8,128)(2,1)S(1)}, u32[]{:S(2)}, u32[]{:S(2)}) collective-permute-start(bf16[24,32,512]{2,1,0:T(8,128)(2,1)S(1)} %shard_map.76), channel_id=1, source_target_pairs={{0,1},{1,0},{2,3},{3,2},{4,5},{5,4},{6,7},{7,6},{8,9},{9,8},{10,11... | collective-permute-start | bytes 2359304 | tf_op jit(solution)/shard_map/ppermute | solution.py:256
  64.8 11.2 %collective-permute-start.19 = (bf16[8,32,512]{2,1,0:T(8,128)(2,1)S(1)}, bf16[8,32,512]{2,1,0:T(8,128)(2,1)S(1)}, u32[]{:S(2)}, u32[]{:S(2)}) collective-permute-start(bf16[8,32,512]{2,1,0:T(8,128)(2,1)S(1)} %get-tuple-element.113), channel_id=1, source_target_pairs={{0,12},{4,8},{8,4},{12,0},{1,13},{5,9},{9,5},{13,1},{2,14},{6,10},... | collective-permute-start | bytes 786440 | tf_op jit(solution)/shard_map/ppermute | solution.py:210
  66.5 25.0 %collective-permute-start.20 = (bf16[8,32,512]{2,1,0:T(8,128)(2,1)S(1)}, bf16[8,32,512]{2,1,0:T(8,128)(2,1)S(1)}, u32[]{:S(2)}, u32[]{:S(2)}) collective-permute-start(bf16[8,32,512]{2,1,0:T(8,128)(2,1)S(1)} %get-tuple-element.114), channel_id=1, source_target_pairs={{0,8},{4,12},{8,0},{12,4},{1,9},{5,13},{9,1},{13,5},{2,10},{6,14},... | collective-permute-start | bytes 786440 | tf_op jit(solution)/shard_map/ppermute | solution.py:210
  69.3 22.2 %collective-permute-start.21 = (bf16[8,32,512]{2,1,0:T(8,128)(2,1)S(1)}, bf16[8,32,512]{2,1,0:T(8,128)(2,1)S(1)}, u32[]{:S(2)}, u32[]{:S(2)}) collective-permute-start(bf16[8,32,512]{2,1,0:T(8,128)(2,1)S(1)} %get-tuple-element.115), channel_id=1, source_target_pairs={{0,4},{4,0},{8,12},{12,8},{1,5},{5,1},{9,13},{13,9},{2,6},{6,2},{1... | collective-permute-start | bytes 786440 | tf_op jit(solution)/shard_map/ppermute | solution.py:210
  (2 other events, 11.2 us)

commit v7 on v6

--- a/solution.py
+++ b/solution.py
@@ -79,31 +79,35 @@
     )(where, tiles, starts, beam, modes)
 
 
-def project_kernel(where, mine, others, held, stay_ref, leave_ref, *, piece):
-    freqs, rows, _ = mine.shape
+def project_kernel(where, *refs, piece, blocks):
+    count = (len(refs) - 3) // 2
+    mine, others = refs[:count], refs[count:2 * count]
+    held, stay_ref, leave_ref = refs[2 * count:]
+    freqs, rows, _ = stay_ref.shape
     first = where[piece] * freqs
     own = where[PARTS] == 1
     for f in range(freqs):
-        a, b = mine[f], others[f]
+        a = jnp.concatenate([mine[n][k] for n, k in blocks[f]], axis=0)
+        b = jnp.concatenate([others[n][k] for n, k in blocks[f]], axis=0)
         lines = jnp.concatenate([jnp.where(own, a, b), jnp.where(own, b, a)], axis=0)
         value = jnp.dot(lines, held[first + f], preferred_element_type=jnp.float32).astype(jnp.bfloat16)
         stay_ref[f] = value[:rows]
         leave_ref[f] = value[rows:]
 
 
-def project(where, mine, others, held, piece):
-    freqs, rows, _ = mine.shape
+def project(where, mine, others, held, piece, blocks):
     ell = held.shape[2]
+    rows = sum(mine[n].shape[1] for n, _ in blocks[0])
     vmem = pl.BlockSpec(memory_space=pltpu.VMEM)
     return pl.pallas_call(
-        functools.partial(project_kernel, piece=piece),
+        functools.partial(project_kernel, piece=piece, blocks=blocks),
         grid_spec=pltpu.PrefetchScalarGridSpec(
-            num_scalar_prefetch=1, grid=(), in_specs=[vmem] * 3, out_specs=[vmem] * 2
+            num_scalar_prefetch=1, grid=(), in_specs=[vmem] * (2 * len(mine) + 1), out_specs=[vmem] * 2
         ),
-        out_shape=[jax.ShapeDtypeStruct((freqs, rows, ell), jnp.bfloat16)] * 2,
-        compiler_params=pltpu.CompilerParams(vmem_limit_bytes=VMEM_LIMIT),
-        cost_estimate=pl.CostEstimate(flops=1024, bytes_accessed=1024, transcendentals=0),
-    )(where, mine, others, pltpu.with_memory_space_constraint(held, pltpu.VMEM))
+        out_shape=[jax.ShapeDtypeStruct((len(blocks), rows, ell), jnp.bfloat16)] * 2,
+        compiler_params=pltpu.CompilerParams(vmem_limit_bytes=VMEM_LIMIT),
+        cost_estimate=pl.CostEstimate(flops=1024, bytes_accessed=1024, transcendentals=0),
+    )(where, *mine, *others, pltpu.with_memory_space_constraint(held, pltpu.VMEM))
 
 
 def contract(modes, skies):
@@ -125,7 +129,7 @@
 
 
 def sky_specs(skies, first):
-    return [by_rows(sky.shape[0], sky.shape[2], first if n == 0 else 0) for n, sky in enumerate(skies)]
+    return [by_rows(sky.shape[0], sky.shape[2], low) for sky, low in zip(skies, first)]
 
 
 def reduce(modes, skies, first, n_modes, dtype=jnp.bfloat16):
@@ -143,22 +147,23 @@
 
 def restore_kernel(up_ref, ratio_ref, kept_ref, came_ref, *outs, spots):
     n_modes, _, ell = came_ref.shape
-    size = outs[0].shape[0] * ROWS
+    freqs = up_ref.shape[0] // ROWS // PARTS
     total = kept_ref[...] + came_ref[...].astype(jnp.float32)
     weighted = (total * ratio_ref[...]).astype(jnp.bfloat16).reshape(n_modes * ROWS, ell)
-    for which, out in zip(spots, outs):
-        value = jnp.dot(up_ref[which * size:(which + 1) * size, :], weighted, preferred_element_type=jnp.float32)
+    for (j, low, high), out in zip(spots, outs):
+        modes = up_ref[(j * freqs + low) * ROWS:(j * freqs + high) * ROWS, :]
+        value = jnp.dot(modes, weighted, preferred_element_type=jnp.float32)
         out[...] = value.astype(jnp.bfloat16).reshape(out.shape)
 
 
-def restore(kept, came, ratios, up, freqs, spots):
+def restore(kept, came, ratios, up, spots):
     n_modes, rows, ell = came.shape
     return pl.pallas_call(
         functools.partial(restore_kernel, spots=spots),
         grid=(rows // ROWS,),
         in_specs=[fixed(up.shape), fixed(ratios.shape)] + [by_rows(n_modes, ell)] * 2,
-        out_specs=[by_rows(freqs, ell)] * len(spots),
-        out_shape=[jax.ShapeDtypeStruct((freqs, rows, ell), jnp.bfloat16)] * len(spots),
+        out_specs=[by_rows(high - low, ell) for _, low, high in spots],
+        out_shape=[jax.ShapeDtypeStruct((high - low, rows, ell), jnp.bfloat16) for _, low, high in spots],
         compiler_params=pltpu.CompilerParams(vmem_limit_bytes=VMEM_LIMIT),
         cost_estimate=pl.CostEstimate(flops=1024, bytes_accessed=1024, transcendentals=0),
     )(up, ratios, kept, came)
@@ -169,8 +174,8 @@
     pieces, out, sems = refs[:count], refs[-2], refs[-1]
     rows = pieces[0].shape[1]
     copies = [
-        pltpu.make_async_copy(pieces[n], out.at[:, where[j], first:first + rows, :], sems.at[n])
-        for n, j in enumerate(spots)
+        pltpu.make_async_copy(pieces[n], out.at[low:high, where[j], first:first + rows, :], sems.at[n])
+        for n, (j, low, high) in enumerate(spots)
     ]
     for copy in copies:
         copy.start()
@@ -195,7 +200,7 @@
         input_output_aliases={count + 1: 0} if extra else {},
         compiler_params=pltpu.CompilerParams(vmem_limit_bytes=VMEM_LIMIT),
         cost_estimate=pl.CostEstimate(flops=1024, bytes_accessed=1024, transcendentals=0),
-    )(where, *[pieces[j] for j in spots], *extra)
+    )(where, *pieces, *extra)
 
 
 def staged(visibility, beam_transfer, tile_mask, first_block, eigen_modes, signal_noise):
@@ -226,41 +231,54 @@
 
     fence = lax.optimization_barrier
     most, half = rows_all - ROWS, freqs // 2
-    a = {j: along_z(cut(j, 0, ROWS), j) for j in (3, 2, 1)}
+    plain_blocks = [[(0, f)] for f in range(freqs)]
+    own_blocks = [[(f // half, f % half)] for f in range(freqs)]
+    near_blocks = [
+        [(0, freqs + f) if f < half else (1, f - half), (1, half + f)] for f in range(freqs)
+    ]
+    groups = [cut(1, n * ROWS, ROWS) for n in range(3)]
+    near_1 = jnp.concatenate([groups[0], groups[1][:half]], axis=0)
+    near_2 = jnp.concatenate([groups[1][half:], groups[2]], axis=0)
+    near_1 = along_z(near_1, 1)
+    a_3, a_2 = along_z(cut(3, 0, ROWS), 3), along_z(cut(2, 0, ROWS), 2)
     mine = [cut(0, 0, rows_all)[n:n + half] for n in (0, half)]
     others = [along_x(part) for part in mine]
-    b = {j: cut(j, ROWS, most) for j in (1, 2, 3)}
+    b_2, b_3 = cut(2, ROWS, most), cut(3, ROWS, most)
     held, down, up = hold(where, tile_mask[0], first_block, beam, eigen_modes[0])
-    (a[3], a[2], a[1]), b, others, down, up = fence(((a[3], a[2], a[1]), b, others, down, up))
-    b[1], b[2] = along_z(b[1], 1), along_z(b[2], 2)
-    stay_own, leave_own = project(where, jnp.concatenate(mine, axis=0), jnp.concatenate(others, axis=0), held, 0)
-    skies = [project(where, a[j], along_x(a[j]), held, j) for j in (1, 2, 3)]
-    stay_a = [stay_own] + [stay for stay, _ in skies]
-    gone = reduce(down, [leave_own] + [leave for _, leave in skies], 0, n_modes)
-    (b[2], b[1]), b[3], stay_a, gone = fence(((b[2], b[1]), b[3], stay_a, gone))
-    x_2, x_1 = along_x(b[2]), along_x(b[1])
-    b[3] = along_z(b[3], 3)
-    kept = reduce(down, stay_a, 0, n_modes, jnp.float32)
-    outs = restore(kept, lax.ppermute(gone, "pol", other), ratios, up, freqs, (0, 1, 2, 3))
-    stay_1, leave_1 = project(where, b[1], x_1, held, 1)
-    x_2, b, outs, stay_1, leave_1 = fence((x_2, b, outs, stay_1, leave_1))
-    back_a = [outs[0]] + [along_z(outs[j], j) for j in range(1, parts)]
-    x_3 = along_x(b[3])
-    stay_2, leave_2 = project(where, b[2], x_2, held, 2)
-    stay_3, leave_3 = project(where, b[3], x_3, held, 3)
-    gone = reduce(down, [leave_own, leave_1, leave_2, leave_3], ROWS, n_modes)
-    kept = reduce(down, [stay_own, stay_1, stay_2, stay_3], ROWS, n_modes, jnp.float32)
-    (back_a[2], back_a[3], back_a[1]), back_a[0], kept, gone = fence(
-        ((back_a[2], back_a[3], back_a[1]), back_a[0], kept, gone)
-    )
+    a_3, a_2, near_1, near_2, b_2, b_3, others, down, up = fence(
+        (a_3, a_2, near_1, near_2, b_2, b_3, others, down, up)
+    )
+    b_2, near_2 = along_z(b_2, 2), along_z(near_2, 1)
+    own = project(where, mine, others, held, 0, own_blocks)
+    x_near = along_x(near_1)
+    skies = [own, project(where, [near_1], [x_near], held, 1, plain_blocks)]
+    skies += [project(where, [part], [along_x(part)], held, j, plain_blocks) for j, part in ((2, a_2), (3, a_3))]
+    gone = reduce(down, [leave for _, leave in skies], (0, 0, 0, 0), n_modes)
+    stay_a = [stay for stay, _ in skies]
+    b_2, near_2, b_3, stay_a, x_near, gone = fence((b_2, near_2, b_3, stay_a, x_near, gone))
+    x_2, x_near_2 = along_x(b_2), along_x(near_2)
+    b_3 = along_z(b_3, 3)
+    kept = reduce(down, stay_a, (0, 0, 0, 0), n_modes, jnp.float32)
+    spots_a = [(2, 0, freqs), (3, 0, half), (3, half, freqs), (1, 0, freqs), (0, 0, freqs)]
+    outs = restore(kept, lax.ppermute(gone, "pol", other), ratios, up, spots_a)
+    near = project(where, [near_1, near_2], [x_near, x_near_2], held, 1, near_blocks)
+    x_2, b_2, b_3, outs, near = fence((x_2, b_2, b_3, outs, near))
+    back_2, back_3, back_1 = along_z(outs[0], 2), along_z(outs[1], 3), along_z(outs[3], 1)
+    x_3 = along_x(b_3)
+    skies = [own, near]
+    skies += [project(where, [part], [x], held, j, plain_blocks) for j, part, x in ((2, b_2, x_2), (3, b_3, x_3))]
+    gone = reduce(down, [leave for _, leave in skies], (ROWS, 0, 0, 0), n_modes)
+    kept = reduce(down, [stay for stay, _ in skies], (ROWS, 0, 0, 0), n_modes, jnp.float32)
+    back_2, back_3, back_1, late, here, kept, gone = fence((back_2, back_3, back_1, outs[2], outs[4], kept, gone))
+    late = along_z(late, 3)
     came = lax.ppermute(gone, "pol", other)
-    outs = dict(zip((3, 2), restore(kept, came, ratios, up, freqs, (3, 2))))
-    outs.update(zip((1, 0), restore(kept, came, ratios, up, freqs, (1, 0))))
-    back_b = {j: along_z(outs[j], j) for j in (3, 2, 1)}
-    back_b[0] = outs[0]
-    result = place(where, back_a, (0, 1, 2, 3), 0, shape)
-    result = place(where, back_b, (0,), ROWS, shape, into=result)
-    return place(where, back_b, (3, 2, 1), ROWS, shape, into=result)
+    spots_b = [(j, 0, freqs) for j in (1, 2, 3, 0)]
+    outs = restore(kept, came, ratios, up, spots_b)
+    outs, late = fence((outs, late))
+    back = [along_z(outs[n], spots_b[n][0]) for n in range(3)]
+    result = place(where, [back_2, back_3, late, back_1, here], spots_a, 0, shape)
+    result = place(where, [outs[3], back[0]], [spots_b[3], spots_b[0]], ROWS, shape, into=result)
+    return place(where, back[1:], spots_b[1:3], ROWS, shape, into=result)
 
 
 def plain(visibility, beam_transfer, tile_mask, first_block, eigen_modes, signal_noise):
@@ -300,8 +318,8 @@
         and sizes["pol"] == 2
         and modes == sizes["fm"] == PARTS
         and beam_transfer.shape[0] == 1
-        and rows % ROWS == 0
-        and rows > ROWS
+        and rows == 3 * ROWS
+        and visibility.shape[0] % 2 == 0
     )
     if not fits:
         return plain(*args)

time: 93.1 us -> 94.4 us (1.014)
  the two profiles are of different devices: /device:TPU:0 before, /device:TPU:12 now
where the time goes in v7:
time: 94.4 us; the launch traced here: 94.2 us
  waiting for transfers between devices  37.6 us (40%)
  starting transfers between devices  27.4 us (29%)
  Pallas kernels  25.1 us (27%)
  local copies, waits for them, and re-layouts  3.07 us (3%)
  between operations  0.97 us (1%)
    ppermute x13, waiting for transfers between devices, along_z(): return lax.ppermute(value, 'fm', [(i, i ^ j) for i in range(parts)])  21.5 us
    ppermute x13, starting transfers between devices, along_z(): return lax.ppermute(value, 'fm', [(i, i ^ j) for i in range(parts)])  18.6 us
    ppermute x8, waiting for transfers between devices, along_x(): return lax.ppermute(value, 'kl', other)  15.4 us
    pallas_call x7, Pallas kernels, project(): pl.pallas_call(functools.partial(project_kernel, piece=piece, blocks=bloc...  9.55 us
    ppermute x8, starting transfers between devices, along_x(): return lax.ppermute(value, 'kl', other)  8.71 us
    pallas_call x1, Pallas kernels, hold(): pl.pallas_call(hold_kernel, grid_spec=pltpu.PrefetchScalarGridSpec(num_sc...  7.06 us
    pallas_call x3, Pallas kernels, place(): pl.pallas_call(functools.partial(place_kernel, spots=spots, first=first),...  4.06 us
    pallas_call x4, Pallas kernels, reduce(): pl.pallas_call(reduce_kernel, grid=(rows // ROWS,), in_specs=[fixed(modes...  2.62 us
  transfers between devices with their start and end apart: 23, of which 9 were waited for; matrix products, arithmetic and copies ran while one was open for 0% of the time, Pallas kernels for 25%

profile of v7, /device:TPU:12, one launch (start us, length us, event | category | flops | bytes accessed | tf_op | source)
XLA Modules:
  0.0 94.2 jit_solution(7644036977945889861)
XLA Ops:
  1.0 1.8 %dynamic-slice_bitcast_fusion.4 = (bf16[8,16,512]{2,1,0:T(8,128)(2,1)S(1)}, bf16[8,16,512]{2,1,0:T(8,128)(2,1)S(1)}, bf16[8,16,512]{2,1,0:T(8,128)(2,1)S(1)}, bf16[8,16,512]{2,1,0:T(8,128)(2,1)}) fusion(bf16[8,4,48,512]{3,2,1,0:T(8,128)(2,1)} %param.6, s32[]{:T(128)S(6)} %select_n.29, s32[]{:T(128)S(6)} %select_n.28, s32[]{:T(128)S(6)} %select_n.27), kind=kLoop, calls=%fused_computation.6 | loop fusion | bytes 1048588 | tf_op jit(solution)/shard_map/reshape | solution.py:221
  3.4 2.7 %collective-permute-start = (bf16[8,16,512]{2,1,0:T(8,128)(2,1)}, bf16[8,16,512]{2,1,0:T(8,128)(2,1)S(1)}, u32[]{:S(2)}, u32[]{:S(2)}) collective-permute-start(bf16[8,16,512]{2,1,0:T(8,128)(2,1)} %get-tuple-element.148), channel_id=1, source_target_pairs={{0,12},{4,8},{8,4},{12,0},{1,13},{5,9},{9,5},{13,1},{2,14},{6,10},... | collective-permute-start | bytes 393224 | tf_op jit(solution)/shard_map/ppermute | solution.py:215
  7.3 1.6 %collective-permute-start.3 = (bf16[4,48,512]{2,1,0:T(8,128)(2,1)S(1)}, bf16[4,48,512]{2,1,0:T(8,128)(2,1)S(1)}, u32[]{:S(2)}, u32[]{:S(2)}) collective-permute-start(bf16[4,48,512]{2,1,0:T(8,128)(2,1)S(1)} %get-tuple-element.140.refs_0_), channel_id=1, source_target_pairs={{0,2},{2,0},{1,3},{3,1},{4,6},{6,4},{5,7},{7,5},{8,10},{10,8},{9,1... | collective-permute-start | bytes 589832 | tf_op jit(solution)/shard_map/ppermute | solution.py:218
  10.2 7.1 %shard_map.64 = (bf16[32,512,512]{2,1,0:T(8,128)(2,1)S(1)}, bf16[384,512]{1,0:T(8,128)(2,1)S(1)}, bf16[512,384]{1,0:T(8,128)(2,1)S(1)}) custom-call(s32[6]{0:T(128)S(1)} %compare_select_fusion.1.where, s32[4,4]{1,0:T(4,128)S(1)} %bitcast.36, s32[1]{0:T(128)S(6)} %copy.20.starts, bf16[32,512,512]{2,1,0:T(8,128)(2,1)} %bitcast.37, bf16[32,24]{1,0:T(8,128)(2,1)S(1)} %bitcast.35), custom_call_target="tpu_custom_call" | custom-call | flops 1024 | bytes 1024 | tf_op jit(solution)/shard_map/pallas_call | solution.py:63
  17.4 3.2 %collective-permute-start.5 = (bf16[8,32,512]{2,1,0:T(8,128)(2,1)S(1)}, bf16[8,32,512]{2,1,0:T(8,128)(2,1)S(1)}, u32[]{:S(2)}, u32[]{:S(2)}) collective-permute-start(bf16[8,32,512]{2,1,0:T(8,128)(2,1)S(1)} %get-tuple-element.75), channel_id=1, source_target_pairs={{0,8},{4,12},{8,0},{12,4},{1,9},{5,13},{9,1},{13,5},{2,10},{6,14},... | collective-permute-start | bytes 786440 | tf_op jit(solution)/shard_map/ppermute | solution.py:215
  20.7 1.5 %collective-permute-start.7 = (bf16[12,16,512]{2,1,0:T(8,128)(2,1)S(1)}, bf16[12,16,512]{2,1,0:T(8,128)(2,1)S(1)}, u32[]{:S(2)}, u32[]{:S(2)}) collective-permute-start(bf16[12,16,512]{2,1,0:T(8,128)(2,1)S(1)} %collective-permute-done.2.refs_0_), channel_id=1, source_target_pairs={{0,2},{2,0},{1,3},{3,1},{4,6},{6,4},{5,7},{7,5},{8,10},{10,8},{9,1... | collective-permute-start | bytes 589832 | tf_op jit(solution)/shard_map/ppermute | solution.py:218
  22.7 1.5 %collective-permute-start.8 = (bf16[8,16,512]{2,1,0:T(8,128)(2,1)S(1)}, bf16[8,16,512]{2,1,0:T(8,128)(2,1)S(1)}, u32[]{:S(2)}, u32[]{:S(2)}) collective-permute-start(bf16[8,16,512]{2,1,0:T(8,128)(2,1)S(1)} %collective-permute-done.1.refs_0_), channel_id=1, source_target_pairs={{0,2},{2,0},{1,3},{3,1},{4,6},{6,4},{5,7},{7,5},{8,10},{10,8},{9,1... | collective-permute-start | bytes 393224 | tf_op jit(solution)/shard_map/ppermute | solution.py:218
  25.5 4.2 %collective-permute-done.9.refs_1_ = bf16[8,16,512]{2,1,0:T(8,128)(2,1)S(1)} collective-permute-done((bf16[8,16,512]{2,1,0:T(8,128)(2,1)S(1)}, bf16[8,16,512]{2,1,0:T(8,128)(2,1)S(1)}, u32[]{:S(2)}, u32[]{:S(2)}) %collective-permute-start.9) | collective-permute-done | bytes 131104 | tf_op jit(solution)/shard_map/ppermute | solution.py:218
  29.7 1.4 %shard_map.68 = (bf16[8,16,512]{2,1,0:T(8,128)(2,1)S(1)}, bf16[8,16,512]{2,1,0:T(8,128)(2,1)S(1)}) custom-call(s32[6]{0:T(128)S(1)} %compare_select_fusion.1.where, bf16[8,16,512]{2,1,0:T(8,128)(2,1)S(1)} %collective-permute-done.refs_0_, bf16[8,16,512]{2,1,0:T(8,128)(2,1)S(1)} %collective-permute-done.9.refs_1_, ...), custom_call_target="tpu_custom_call" | custom-call | flops 1024 | bytes 1024 | tf_op jit(solution)/shard_map/pallas_call | solution.py:102
  31.1 1.4 %shard_map.67 = (bf16[8,16,512]{2,1,0:T(8,128)(2,1)S(1)}, bf16[8,16,512]{2,1,0:T(8,128)(2,1)S(1)}) custom-call(s32[6]{0:T(128)S(1)} %compare_select_fusion.1.where, bf16[8,16,512]{2,1,0:T(8,128)(2,1)S(1)} %collective-permute-done.1.refs_0_, bf16[8,16,512]{2,1,0:T(8,128)(2,1)S(1)} %collective-permute-done.8.refs_1_, ...), custom_call_target="tpu_custom_call" | custom-call | flops 1024 | bytes 1024 | tf_op jit(solution)/shard_map/pallas_call | solution.py:102
  32.5 1.4 %shard_map.66 = (bf16[8,16,512]{2,1,0:T(8,128)(2,1)S(1)}, bf16[8,16,512]{2,1,0:T(8,128)(2,1)S(1)}) custom-call(s32[6]{0:T(128)S(1)} %compare_select_fusion.1.where, bf16[12,16,512]{2,1,0:T(8,128)(2,1)S(1)} %collective-permute-done.2.refs_0_, bf16[12,16,512]{2,1,0:T(8,128)(2,1)S(1)} %collective-permute-done.7.refs_1_.refs_2_, ...), custom_call_target="tpu_custom_call" | custom-call | flops 1024 | bytes 1024 | tf_op jit(solution)/shard_map/pallas_call | solution.py:102
  34.4 1.6 %collective-permute-start.10 = (bf16[8,32,512]{2,1,0:T(8,128)(2,1)S(1)}, bf16[8,32,512]{2,1,0:T(8,128)(2,1)S(1)}, u32[]{:S(2)}, u32[]{:S(2)}) collective-permute-start(bf16[8,32,512]{2,1,0:T(8,128)(2,1)S(1)} %collective-permute-done.5.refs_0_), channel_id=1, source_target_pairs={{0,2},{2,0},{1,3},{3,1},{4,6},{6,4},{5,7},{7,5},{8,10},{10,8},{9,1... | collective-permute-start | bytes 786440 | tf_op jit(solution)/shard_map/ppermute | solution.py:218
  38.1 9.2 %collective-permute-done.13.refs_3_ = bf16[12,16,512]{2,1,0:T(8,128)(2,1)S(1)} collective-permute-done((bf16[12,16,512]{2,1,0:T(8,128)(2,1)S(1)}, bf16[12,16,512]{2,1,0:T(8,128)(2,1)S(1)}, u32[]{:S(2)}, u32[]{:S(2)}) %collective-permute-start.13) | collective-permute-done | bytes 196640 | tf_op jit(solution)/shard_map/ppermute | solution.py:218
  47.3 1.4 %shard_map.72 = (bf16[8,32,512]{2,1,0:T(8,128)(2,1)S(1)}, bf16[8,32,512]{2,1,0:T(8,128)(2,1)S(1)}) custom-call(s32[6]{0:T(128)S(1)} %compare_select_fusion.1.where, bf16[12,16,512]{2,1,0:T(8,128)(2,1)S(1)} %collective-permute-done.2.refs_0_, bf16[12,16,512]{2,1,0:T(8,128)(2,1)S(1)} %collective-permute-done.6.refs_1_, ...), custom_call_target="tpu_custom_call" | custom-call | flops 1024 | bytes 1024 | tf_op jit(solution)/shard_map/pallas_call | solution.py:102
  51.5 2.1 %collective-permute-start.16 = (bf16[8,16,512]{2,1,0:T(8,128)(2,1)S(1)}, bf16[8,16,512]{2,1,0:T(8,128)(2,1)S(1)}, u32[]{:S(2)}, u32[]{:S(2)}) collective-permute-start(bf16[8,16,512]{2,1,0:T(8,128)(2,1)S(1)} %get-tuple-element.111), channel_id=1, source_target_pairs={{0,4},{4,0},{8,12},{12,8},{1,5},{5,1},{9,13},{13,9},{2,6},{6,2},{1... | collective-permute-start | bytes 393224 | tf_op jit(solution)/shard_map/ppermute | solution.py:215
  54.4 1.4 %shard_map.73 = (bf16[8,32,512]{2,1,0:T(8,128)(2,1)S(1)}, bf16[8,32,512]{2,1,0:T(8,128)(2,1)S(1)}) custom-call(s32[6]{0:T(128)S(1)} %compare_select_fusion.1.where, bf16[8,32,512]{2,1,0:T(8,128)(2,1)S(1)} %collective-permute-done.5.refs_0_, bf16[8,32,512]{2,1,0:T(8,128)(2,1)S(1)} %collective-permute-done.10.refs_1_, ...), custom_call_target="tpu_custom_call" | custom-call | flops 1024 | bytes 1024 | tf_op jit(solution)/shard_map/pallas_call | solution.py:102
  55.8 1.9 %collective-permute-done.17.refs_1_ = bf16[8,32,512]{2,1,0:T(8,128)(2,1)S(1)} collective-permute-done((bf16[8,32,512]{2,1,0:T(8,128)(2,1)S(1)}, bf16[8,32,512]{2,1,0:T(8,128)(2,1)S(1)}, u32[]{:S(2)}, u32[]{:S(2)}) %collective-permute-start.17) | collective-permute-done | bytes 262176 | tf_op jit(solution)/shard_map/ppermute | solution.py:218
  57.7 1.4 %shard_map.74 = (bf16[8,32,512]{2,1,0:T(8,128)(2,1)S(1)}, bf16[8,32,512]{2,1,0:T(8,128)(2,1)S(1)}) custom-call(s32[6]{0:T(128)S(1)} %compare_select_fusion.1.where, bf16[8,32,512]{2,1,0:T(8,128)(2,1)S(1)} %collective-permute-done.11.refs_0_, bf16[8,32,512]{2,1,0:T(8,128)(2,1)S(1)} %collective-permute-done.17.refs_1_, ...), custom_call_target="tpu_custom_call" | custom-call | flops 1024 | bytes 1024 | tf_op jit(solution)/shard_map/pallas_call | solution.py:102
  61.1 1.6 %collective-permute-start.19 = (bf16[4,16,512]{2,1,0:T(8,128)(2,1)S(1)}, bf16[4,16,512]{2,1,0:T(8,128)(2,1)S(1)}, u32[]{:S(2)}, u32[]{:S(2)}) collective-permute-start(bf16[4,16,512]{2,1,0:T(8,128)(2,1)S(1)} %get-tuple-element.129), channel_id=1, source_target_pairs={{0,12},{4,8},{8,4},{12,0},{1,13},{5,9},{9,5},{13,1},{2,14},{6,10},... | collective-permute-start | bytes 196616 | tf_op jit(solution)/shard_map/ppermute | solution.py:215
  65.6 3.1 %collective-permute-start.22 = (bf16[8,32,512]{2,1,0:T(8,128)(2,1)S(1)}, bf16[8,32,512]{2,1,0:T(8,128)(2,1)S(1)}, u32[]{:S(2)}, u32[]{:S(2)}) collective-permute-start(bf16[8,32,512]{2,1,0:T(8,128)(2,1)S(1)} %get-tuple-element.133), channel_id=1, source_target_pairs={{0,4},{4,0},{8,12},{12,8},{1,5},{5,1},{9,13},{13,9},{2,6},{6,2},{1... | collective-permute-start | bytes 786440 | tf_op jit(solution)/shard_map/ppermute | solution.py:215
  70.2 1.4 %shard_map.78.refs_2_ = bf16[8,4,48,512]{3,2,1,0:T(8,128)(2,1)} custom-call(s32[6]{0:T(128)S(1)} %compare_select_fusion.1.where, bf16[8,16,512]{2,1,0:T(8,128)(2,1)S(1)} %collective-permute-done.14.refs_0_, bf16[4,16,512]{2,1,0:T(8,128)(2,1)S(1)} %collective-permute-done.15.refs_1_, bf16[4,16,512]{2,1,0:T(8,128)(2,1)S(1)} %collective-permute-done.19.refs_2_, ...), custom_call_target="tpu_custom_call" | custom-call | flops 1024 | bytes 1024 | tf_op jit(solution)/shard_map/pallas_call | solution.py:190
  71.5 7.2 %collective-permute-done.22.refs_1_ = bf16[8,32,512]{2,1,0:T(8,128)(2,1)S(1)} collective-permute-done((bf16[8,32,512]{2,1,0:T(8,128)(2,1)S(1)}, bf16[8,32,512]{2,1,0:T(8,128)(2,1)S(1)}, u32[]{:S(2)}, u32[]{:S(2)}) %collective-permute-start.22) | collective-permute-done | bytes 262176 | tf_op jit(solution)/shard_map/ppermute | solution.py:215
  80.1 7.2 %collective-permute-done.20.refs_0_ = bf16[8,32,512]{2,1,0:T(8,128)(2,1)S(1)} collective-permute-done((bf16[8,32,512]{2,1,0:T(8,128)(2,1)S(1)}, bf16[8,32,512]{2,1,0:T(8,128)(2,1)S(1)}, u32[]{:S(2)}, u32[]{:S(2)}) %collective-permute-start.20) | collective-permute-done | bytes 262176 | tf_op jit(solution)/shard_map/ppermute | solution.py:215
  87.4 5.5 %collective-permute-done.21.refs_1_ = bf16[8,32,512]{2,1,0:T(8,128)(2,1)S(1)} collective-permute-done((bf16[8,32,512]{2,1,0:T(8,128)(2,1)S(1)}, bf16[8,32,512]{2,1,0:T(8,128)(2,1)S(1)}, u32[]{:S(2)}, u32[]{:S(2)}) %collective-permute-start.21) | collective-permute-done | bytes 262176 | tf_op jit(solution)/shard_map/ppermute | solution.py:215
  (57 shorter events, 20.7 us)
Async XLA Ops:
  0.0 10.2 %copy-start = (s32[1,4,4]{2,1,0:T(4,128)S(1)}, s32[1,4,4]{2,1,0:T(4,128)}, u32[]{:S(2)}) copy-start(s32[1,4,4]{2,1,0:T(4,128)} %param.8) | copy-start | bytes 196
  2.9 14.5 %collective-permute-start.2 = (bf16[12,16,512]{2,1,0:T(8,128)(2,1)S(1)}, bf16[12,16,512]{2,1,0:T(8,128)(2,1)S(1)}, u32[]{:S(2)}, u32[]{:S(2)}) collective-permute-start(bf16[12,16,512]{2,1,0:T(8,128)(2,1)S(1)} %pad_maximum_fusion), channel_id=1, source_target_pairs={{0,4},{4,0},{8,12},{12,8},{1,5},{5,1},{9,13},{13,9},{2,6},{6,2},{1... | collective-permute-start | bytes 589832 | tf_op jit(solution)/shard_map/ppermute | solution.py:215
  3.4 14.0 %collective-permute-start = (bf16[8,16,512]{2,1,0:T(8,128)(2,1)}, bf16[8,16,512]{2,1,0:T(8,128)(2,1)S(1)}, u32[]{:S(2)}, u32[]{:S(2)}) collective-permute-start(bf16[8,16,512]{2,1,0:T(8,128)(2,1)} %get-tuple-element.148), channel_id=1, source_target_pairs={{0,12},{4,8},{8,4},{12,0},{1,13},{5,9},{9,5},{13,1},{2,14},{6,10},... | collective-permute-start | bytes 393224 | tf_op jit(solution)/shard_map/ppermute | solution.py:215
  6.1 11.3 %collective-permute-start.1 = (bf16[8,16,512]{2,1,0:T(8,128)(2,1)S(1)}, bf16[8,16,512]{2,1,0:T(8,128)(2,1)S(1)}, u32[]{:S(2)}, u32[]{:S(2)}) collective-permute-start(bf16[8,16,512]{2,1,0:T(8,128)(2,1)S(1)} %get-tuple-element.147), channel_id=1, source_target_pairs={{0,8},{4,12},{8,0},{12,4},{1,9},{5,13},{9,1},{13,5},{2,10},{6,14},... | collective-permute-start | bytes 393224 | tf_op jit(solution)/shard_map/ppermute | solution.py:215
  7.3 10.0 %collective-permute-start.3 = (bf16[4,48,512]{2,1,0:T(8,128)(2,1)S(1)}, bf16[4,48,512]{2,1,0:T(8,128)(2,1)S(1)}, u32[]{:S(2)}, u32[]{:S(2)}) collective-permute-start(bf16[4,48,512]{2,1,0:T(8,128)(2,1)S(1)} %get-tuple-element.140.refs_0_), channel_id=1, source_target_pairs={{0,2},{2,0},{1,3},{3,1},{4,6},{6,4},{5,7},{7,5},{8,10},{10,8},{9,1... | collective-permute-start | bytes 589832 | tf_op jit(solution)/shard_map/ppermute | solution.py:218
  8.9 8.5 %collective-permute-start.4 = (bf16[4,48,512]{2,1,0:T(8,128)(2,1)S(1)}, bf16[4,48,512]{2,1,0:T(8,128)(2,1)S(1)}, u32[]{:S(2)}, u32[]{:S(2)}) collective-permute-start(bf16[4,48,512]{2,1,0:T(8,128)(2,1)S(1)} %get-tuple-element.139.refs_1_), channel_id=1, source_target_pairs={{0,2},{2,0},{1,3},{3,1},{4,6},{6,4},{5,7},{7,5},{8,10},{10,8},{9,1... | collective-permute-start | bytes 589832 | tf_op jit(solution)/shard_map/ppermute | solution.py:218
  17.4 16.9 %collective-permute-start.5 = (bf16[8,32,512]{2,1,0:T(8,128)(2,1)S(1)}, bf16[8,32,512]{2,1,0:T(8,128)(2,1)S(1)}, u32[]{:S(2)}, u32[]{:S(2)}) collective-permute-start(bf16[8,32,512]{2,1,0:T(8,128)(2,1)S(1)} %get-tuple-element.75), channel_id=1, source_target_pairs={{0,8},{4,12},{8,0},{12,4},{1,9},{5,13},{9,1},{13,5},{2,10},{6,14},... | collective-permute-start | bytes 786440 | tf_op jit(solution)/shard_map/ppermute | solution.py:215
  20.7 11.9 %collective-permute-start.7 = (bf16[12,16,512]{2,1,0:T(8,128)(2,1)S(1)}, bf16[12,16,512]{2,1,0:T(8,128)(2,1)S(1)}, u32[]{:S(2)}, u32[]{:S(2)}) collective-permute-start(bf16[12,16,512]{2,1,0:T(8,128)(2,1)S(1)} %collective-permute-done.2.refs_0_), channel_id=1, source_target_pairs={{0,2},{2,0},{1,3},{3,1},{4,6},{6,4},{5,7},{7,5},{8,10},{10,8},{9,1... | collective-permute-start | bytes 589832 | tf_op jit(solution)/shard_map/ppermute | solution.py:218
  22.1 12.1 %collective-permute-start.6 = (bf16[12,16,512]{2,1,0:T(8,128)(2,1)S(1)}, bf16[12,16,512]{2,1,0:T(8,128)(2,1)S(1)}, u32[]{:S(2)}, u32[]{:S(2)}) collective-permute-start(bf16[12,16,512]{2,1,0:T(8,128)(2,1)S(1)} %pad_maximum_fusion.1), channel_id=1, source_target_pairs={{0,4},{4,0},{8,12},{12,8},{1,5},{5,1},{9,13},{13,9},{2,6},{6,2},{1... | collective-permute-start | bytes 589832 | tf_op jit(solution)/shard_map/ppermute | solution.py:215
  22.1 7.6 %collective-permute-start.9 = (bf16[8,16,512]{2,1,0:T(8,128)(2,1)S(1)}, bf16[8,16,512]{2,1,0:T(8,128)(2,1)S(1)}, u32[]{:S(2)}, u32[]{:S(2)}) collective-permute-start(bf16[8,16,512]{2,1,0:T(8,128)(2,1)S(1)} %collective-permute-done.refs_0_), channel_id=1, source_target_pairs={{0,2},{2,0},{1,3},{3,1},{4,6},{6,4},{5,7},{7,5},{8,10},{10,8},{9,1... | collective-permute-start | bytes 393224 | tf_op jit(solution)/shard_map/ppermute | solution.py:218
  22.7 8.5 %collective-permute-start.8 = (bf16[8,16,512]{2,1,0:T(8,128)(2,1)S(1)}, bf16[8,16,512]{2,1,0:T(8,128)(2,1)S(1)}, u32[]{:S(2)}, u32[]{:S(2)}) collective-permute-start(bf16[8,16,512]{2,1,0:T(8,128)(2,1)S(1)} %collective-permute-done.1.refs_0_), channel_id=1, source_target_pairs={{0,2},{2,0},{1,3},{3,1},{4,6},{6,4},{5,7},{7,5},{8,10},{10,8},{9,1... | collective-permute-start | bytes 393224 | tf_op jit(solution)/shard_map/ppermute | solution.py:218
  34.3 14.4 %collective-permute-start.12 = (bf16[24,16,512]{2,1,0:T(8,128)(2,1)S(1)}, bf16[24,16,512]{2,1,0:T(8,128)(2,1)S(1)}, u32[]{:S(2)}, u32[]{:S(2)}) collective-permute-start(bf16[24,16,512]{2,1,0:T(8,128)(2,1)S(1)} %shard_map.69), channel_id=1, source_target_pairs={{0,1},{1,0},{2,3},{3,2},{4,5},{5,4},{6,7},{7,6},{8,9},{9,8},{10,11... | collective-permute-start | bytes 1179656 | tf_op jit(solution)/shard_map/ppermute | solution.py:263
  34.4 15.0 %collective-permute-start.10 = (bf16[8,32,512]{2,1,0:T(8,128)(2,1)S(1)}, bf16[8,32,512]{2,1,0:T(8,128)(2,1)S(1)}, u32[]{:S(2)}, u32[]{:S(2)}) collective-permute-start(bf16[8,32,512]{2,1,0:T(8,128)(2,1)S(1)} %collective-permute-done.5.refs_0_), channel_id=1, source_target_pairs={{0,2},{2,0},{1,3},{3,1},{4,6},{6,4},{5,7},{7,5},{8,10},{10,8},{9,1... | collective-permute-start | bytes 786440 | tf_op jit(solution)/shard_map/ppermute | solution.py:218
  35.9 14.0 %collective-permute-start.11 = (bf16[8,32,512]{2,1,0:T(8,128)(2,1)S(1)}, bf16[8,32,512]{2,1,0:T(8,128)(2,1)S(1)}, u32[]{:S(2)}, u32[]{:S(2)}) collective-permute-start(bf16[8,32,512]{2,1,0:T(8,128)(2,1)S(1)} %get-tuple-element.94), channel_id=1, source_target_pairs={{0,12},{4,8},{8,4},{12,0},{1,13},{5,9},{9,5},{13,1},{2,14},{6,10},... | collective-permute-start | bytes 786440 | tf_op jit(solution)/shard_map/ppermute | solution.py:215
  37.2 10.1 %collective-permute-start.13 = (bf16[12,16,512]{2,1,0:T(8,128)(2,1)S(1)}, bf16[12,16,512]{2,1,0:T(8,128)(2,1)S(1)}, u32[]{:S(2)}, u32[]{:S(2)}) collective-permute-start(bf16[12,16,512]{2,1,0:T(8,128)(2,1)S(1)} %collective-permute-done.6.refs_1_), channel_id=1, source_target_pairs={{0,2},{2,0},{1,3},{3,1},{4,6},{6,4},{5,7},{7,5},{8,10},{10,8},{9,1... | collective-permute-start | bytes 589832 | tf_op jit(solution)/shard_map/ppermute | solution.py:218
  49.9 7.8 %collective-permute-start.17 = (bf16[8,32,512]{2,1,0:T(8,128)(2,1)S(1)}, bf16[8,32,512]{2,1,0:T(8,128)(2,1)S(1)}, u32[]{:S(2)}, u32[]{:S(2)}) collective-permute-start(bf16[8,32,512]{2,1,0:T(8,128)(2,1)S(1)} %collective-permute-done.11.refs_0_), channel_id=1, source_target_pairs={{0,2},{2,0},{1,3},{3,1},{4,6},{6,4},{5,7},{7,5},{8,10},{10,8},{9,1... | collective-permute-start | bytes 786440 | tf_op jit(solution)/shard_map/ppermute | solution.py:218
  50.9 10.0 %collective-permute-start.14 = (bf16[8,16,512]{2,1,0:T(8,128)(2,1)S(1)}, bf16[8,16,512]{2,1,0:T(8,128)(2,1)S(1)}, u32[]{:S(2)}, u32[]{:S(2)}) collective-permute-start(bf16[8,16,512]{2,1,0:T(8,128)(2,1)S(1)} %get-tuple-element.109), channel_id=1, source_target_pairs={{0,8},{4,12},{8,0},{12,4},{1,9},{5,13},{9,1},{13,5},{2,10},{6,14},... | collective-permute-start | bytes 393224 | tf_op jit(solution)/shard_map/ppermute | solution.py:215
  51.5 9.5 %collective-permute-start.16 = (bf16[8,16,512]{2,1,0:T(8,128)(2,1)S(1)}, bf16[8,16,512]{2,1,0:T(8,128)(2,1)S(1)}, u32[]{:S(2)}, u32[]{:S(2)}) collective-permute-start(bf16[8,16,512]{2,1,0:T(8,128)(2,1)S(1)} %get-tuple-element.111), channel_id=1, source_target_pairs={{0,4},{4,0},{8,12},{12,8},{1,5},{5,1},{9,13},{13,9},{2,6},{6,2},{1... | collective-permute-start | bytes 393224 | tf_op jit(solution)/shard_map/ppermute | solution.py:215
  53.7 7.3 %collective-permute-start.15 = (bf16[4,16,512]{2,1,0:T(8,128)(2,1)S(1)}, bf16[4,16,512]{2,1,0:T(8,128)(2,1)S(1)}, u32[]{:S(2)}, u32[]{:S(2)}) collective-permute-start(bf16[4,16,512]{2,1,0:T(8,128)(2,1)S(1)} %get-tuple-element.110), channel_id=1, source_target_pairs={{0,12},{4,8},{8,4},{12,0},{1,13},{5,9},{9,5},{13,1},{2,14},{6,10},... | collective-permute-start | bytes 196616 | tf_op jit(solution)/shard_map/ppermute | solution.py:215
  61.0 2.4 %collective-permute-start.18 = (bf16[24,32,512]{2,1,0:T(8,128)(2,1)S(1)}, bf16[24,32,512]{2,1,0:T(8,128)(2,1)S(1)}, u32[]{:S(2)}, u32[]{:S(2)}) collective-permute-start(bf16[24,32,512]{2,1,0:T(8,128)(2,1)S(1)} %shard_map.76), channel_id=1, source_target_pairs={{0,1},{1,0},{2,3},{3,2},{4,5},{5,4},{6,7},{7,6},{8,9},{9,8},{10,11... | collective-permute-start | bytes 2359304 | tf_op jit(solution)/shard_map/ppermute | solution.py:274
  61.1 4.5 %collective-permute-start.19 = (bf16[4,16,512]{2,1,0:T(8,128)(2,1)S(1)}, bf16[4,16,512]{2,1,0:T(8,128)(2,1)S(1)}, u32[]{:S(2)}, u32[]{:S(2)}) collective-permute-start(bf16[4,16,512]{2,1,0:T(8,128)(2,1)S(1)} %get-tuple-element.129), channel_id=1, source_target_pairs={{0,12},{4,8},{8,4},{12,0},{1,13},{5,9},{9,5},{13,1},{2,14},{6,10},... | collective-permute-start | bytes 196616 | tf_op jit(solution)/shard_map/ppermute | solution.py:215
  65.6 13.2 %collective-permute-start.22 = (bf16[8,32,512]{2,1,0:T(8,128)(2,1)S(1)}, bf16[8,32,512]{2,1,0:T(8,128)(2,1)S(1)}, u32[]{:S(2)}, u32[]{:S(2)}) collective-permute-start(bf16[8,32,512]{2,1,0:T(8,128)(2,1)S(1)} %get-tuple-element.133), channel_id=1, source_target_pairs={{0,4},{4,0},{8,12},{12,8},{1,5},{5,1},{9,13},{13,9},{2,6},{6,2},{1... | collective-permute-start | bytes 786440 | tf_op jit(solution)/shard_map/ppermute | solution.py:215
  68.7 18.7 %collective-permute-start.20 = (bf16[8,32,512]{2,1,0:T(8,128)(2,1)S(1)}, bf16[8,32,512]{2,1,0:T(8,128)(2,1)S(1)}, u32[]{:S(2)}, u32[]{:S(2)}) collective-permute-start(bf16[8,32,512]{2,1,0:T(8,128)(2,1)S(1)} %get-tuple-element.130), channel_id=1, source_target_pairs={{0,8},{4,12},{8,0},{12,4},{1,9},{5,13},{9,1},{13,5},{2,10},{6,14},... | collective-permute-start | bytes 786440 | tf_op jit(solution)/shard_map/ppermute | solution.py:215
  69.4 23.5 %collective-permute-start.21 = (bf16[8,32,512]{2,1,0:T(8,128)(2,1)S(1)}, bf16[8,32,512]{2,1,0:T(8,128)(2,1)S(1)}, u32[]{:S(2)}, u32[]{:S(2)}) collective-permute-start(bf16[8,32,512]{2,1,0:T(8,128)(2,1)S(1)} %get-tuple-element.131), channel_id=1, source_target_pairs={{0,12},{4,8},{8,4},{12,0},{1,13},{5,9},{9,5},{13,1},{2,14},{6,10},... | collective-permute-start | bytes 786440 | tf_op jit(solution)/shard_map/ppermute | solution.py:215
  (3 other events, 20.6 us)

commit v8 on v7

--- a/solution.py
+++ b/solution.py
@@ -231,54 +231,41 @@
 
     fence = lax.optimization_barrier
     most, half = rows_all - ROWS, freqs // 2
-    plain_blocks = [[(0, f)] for f in range(freqs)]
-    own_blocks = [[(f // half, f % half)] for f in range(freqs)]
-    near_blocks = [
-        [(0, freqs + f) if f < half else (1, f - half), (1, half + f)] for f in range(freqs)
-    ]
-    groups = [cut(1, n * ROWS, ROWS) for n in range(3)]
-    near_1 = jnp.concatenate([groups[0], groups[1][:half]], axis=0)
-    near_2 = jnp.concatenate([groups[1][half:], groups[2]], axis=0)
-    near_1 = along_z(near_1, 1)
-    a_3, a_2 = along_z(cut(3, 0, ROWS), 3), along_z(cut(2, 0, ROWS), 2)
+    blocks = [[(0, f)] for f in range(freqs)]
+    halves = [[(f // half, f % half)] for f in range(freqs)]
+    a = {j: along_z(cut(j, 0, ROWS), j) for j in (3, 2, 1)}
     mine = [cut(0, 0, rows_all)[n:n + half] for n in (0, half)]
     others = [along_x(part) for part in mine]
-    b_2, b_3 = cut(2, ROWS, most), cut(3, ROWS, most)
+    b = {j: cut(j, ROWS, most) for j in (1, 2, 3)}
     held, down, up = hold(where, tile_mask[0], first_block, beam, eigen_modes[0])
-    a_3, a_2, near_1, near_2, b_2, b_3, others, down, up = fence(
-        (a_3, a_2, near_1, near_2, b_2, b_3, others, down, up)
-    )
-    b_2, near_2 = along_z(b_2, 2), along_z(near_2, 1)
-    own = project(where, mine, others, held, 0, own_blocks)
-    x_near = along_x(near_1)
-    skies = [own, project(where, [near_1], [x_near], held, 1, plain_blocks)]
-    skies += [project(where, [part], [along_x(part)], held, j, plain_blocks) for j, part in ((2, a_2), (3, a_3))]
+    (a[3], a[2], a[1]), b, others, down, up = fence(((a[3], a[2], a[1]), b, others, down, up))
+    b[1], b[2] = along_z(b[1], 1), along_z(b[2], 2)
+    own = project(where, mine, others, held, 0, halves)
+    skies = [own] + [project(where, [a[j]], [along_x(a[j])], held, j, blocks) for j in (1, 2, 3)]
     gone = reduce(down, [leave for _, leave in skies], (0, 0, 0, 0), n_modes)
     stay_a = [stay for stay, _ in skies]
-    b_2, near_2, b_3, stay_a, x_near, gone = fence((b_2, near_2, b_3, stay_a, x_near, gone))
-    x_2, x_near_2 = along_x(b_2), along_x(near_2)
-    b_3 = along_z(b_3, 3)
+    (b[2], b[1]), b[3], stay_a, gone = fence(((b[2], b[1]), b[3], stay_a, gone))
+    x_2, x_1 = along_x(b[2]), along_x(b[1])
+    b[3] = along_z(b[3], 3)
     kept = reduce(down, stay_a, (0, 0, 0, 0), n_modes, jnp.float32)
-    spots_a = [(2, 0, freqs), (3, 0, half), (3, half, freqs), (1, 0, freqs), (0, 0, freqs)]
-    outs = restore(kept, lax.ppermute(gone, "pol", other), ratios, up, spots_a)
-    near = project(where, [near_1, near_2], [x_near, x_near_2], held, 1, near_blocks)
-    x_2, b_2, b_3, outs, near = fence((x_2, b_2, b_3, outs, near))
-    back_2, back_3, back_1 = along_z(outs[0], 2), along_z(outs[1], 3), along_z(outs[3], 1)
-    x_3 = along_x(b_3)
-    skies = [own, near]
-    skies += [project(where, [part], [x], held, j, plain_blocks) for j, part, x in ((2, b_2, x_2), (3, b_3, x_3))]
+    spots = [(j, 0, freqs) for j in (1, 2, 3, 0)]
+    outs = restore(kept, lax.ppermute(gone, "pol", other), ratios, up, spots)
+    near = project(where, [b[1]], [x_1], held, 1, blocks)
+    x_2, b, outs, near = fence((x_2, b, outs, near))
+    first = {j: along_z(outs[j - 1], j) for j in (1, 2, 3)}
+    first[0] = outs[3]
+    x_3 = along_x(b[3])
+    skies = [own, near] + [project(where, [b[j]], [x], held, j, blocks) for j, x in ((2, x_2), (3, x_3))]
     gone = reduce(down, [leave for _, leave in skies], (ROWS, 0, 0, 0), n_modes)
     kept = reduce(down, [stay for stay, _ in skies], (ROWS, 0, 0, 0), n_modes, jnp.float32)
-    back_2, back_3, back_1, late, here, kept, gone = fence((back_2, back_3, back_1, outs[2], outs[4], kept, gone))
-    late = along_z(late, 3)
-    came = lax.ppermute(gone, "pol", other)
-    spots_b = [(j, 0, freqs) for j in (1, 2, 3, 0)]
-    outs = restore(kept, came, ratios, up, spots_b)
-    outs, late = fence((outs, late))
-    back = [along_z(outs[n], spots_b[n][0]) for n in range(3)]
-    result = place(where, [back_2, back_3, late, back_1, here], spots_a, 0, shape)
-    result = place(where, [outs[3], back[0]], [spots_b[3], spots_b[0]], ROWS, shape, into=result)
-    return place(where, back[1:], spots_b[1:3], ROWS, shape, into=result)
+    (first[2], first[3], first[1]), first[0], kept, gone = fence(
+        ((first[2], first[3], first[1]), first[0], kept, gone)
+    )
+    outs = fence(restore(kept, lax.ppermute(gone, "pol", other), ratios, up, spots))
+    back = [along_z(outs[j - 1], j) for j in (1, 2, 3)]
+    result = place(where, [first[j] for j in (1, 2, 3, 0)], spots, 0, shape)
+    result = place(where, [outs[3], back[0]], [spots[3], spots[0]], ROWS, shape, into=result)
+    return place(where, back[1:], spots[1:3], ROWS, shape, into=result)
 
 
 def plain(visibility, beam_transfer, tile_mask, first_block, eigen_modes, signal_noise):

time: 94.4 us -> 92.1 us (0.976)
  starting transfers between devices: 27.4 us -> 24.9 us
  waiting for transfers between devices: 37.6 us -> 38.7 us
    ppermute x8, waiting for transfers between devices: 15.4 us -> 10.9 us  [along_x(): return lax.ppermute(value, 'kl', other)]
    ppermute x13 -> x12, waiting for transfers between devices: 21.5 us -> 25.6 us  [along_z(): return lax.ppermute(value, 'fm', [(i, i ^ j) for i in range(parts)])]
    ppermute x13 -> x12, starting transfers between devices: 18.6 us -> 15.6 us  [along_z(): return lax.ppermute(value, 'fm', [(i, i ^ j) for i in range(parts)])]
    ppermute x2, waiting for transfers between devices: 0.72 us -> 2.29 us  [the longest x1 2.28 us: staged(): lax.ppermute(gone, 'pol', other)]
    slice x1, local copies, waits for them, and re-layouts: 0.03 us -> 1.05 us  [staged(): mine = [cut(0, 0, rows_all)[n:n + half] for n in (0, half)]]
    slice x1 -> x0, local copies, waits for them, and re-layouts: 1 us -> none  [staged(): near_2 = jnp.concatenate([groups[1][half:], groups[2]], axis=0)]
  transfers between devices with their start and end apart: 23 -> 22, of which waited for: 9 -> 10; matrix products, arithmetic and copies ran while one was open for 0% -> 1% of each run, Pallas kernels for 25% -> 24%
where the time goes in v8:
time: 92.1 us; the launch traced here: 92 us
  waiting for transfers between devices  38.7 us (42%)
  Pallas kernels  25.1 us (27%)
  starting transfers between devices  24.9 us (27%)
  local copies, waits for them, and re-layouts  2.39 us (3%)
    ppermute x12, waiting for transfers between devices, along_z(): return lax.ppermute(value, 'fm', [(i, i ^ j) for i in range(parts)])  25.6 us
    ppermute x12, starting transfers between devices, along_z(): return lax.ppermute(value, 'fm', [(i, i ^ j) for i in range(parts)])  15.6 us
    ppermute x8, waiting for transfers between devices, along_x(): return lax.ppermute(value, 'kl', other)  10.9 us
    pallas_call x7, Pallas kernels, project(): pl.pallas_call(functools.partial(project_kernel, piece=piece, blocks=bloc...  9.56 us
    ppermute x8, starting transfers between devices, along_x(): return lax.ppermute(value, 'kl', other)  9.19 us
    pallas_call x1, Pallas kernels, hold(): pl.pallas_call(hold_kernel, grid_spec=pltpu.PrefetchScalarGridSpec(num_sc...  7.04 us
    pallas_call x3, Pallas kernels, place(): pl.pallas_call(functools.partial(place_kernel, spots=spots, first=first),...  4.06 us
    pallas_call x4, Pallas kernels, reduce(): pl.pallas_call(reduce_kernel, grid=(rows // ROWS,), in_specs=[fixed(modes...  2.62 us
  transfers between devices with their start and end apart: 22, of which 10 were waited for; matrix products, arithmetic and copies ran while one was open for 1% of the time, Pallas kernels for 24%

profile of v8, /device:TPU:12, one launch (start us, length us, event | category | flops | bytes accessed | tf_op | source)
XLA Modules:
  0.0 92.0 jit_solution(9381169358459534519)
XLA Ops:
  1.1 1.6 %collective-permute-start = (bf16[8,16,512]{2,1,0:T(8,128)(2,1)S(1)}, bf16[8,16,512]{2,1,0:T(8,128)(2,1)S(1)}, u32[]{:S(2)}, u32[]{:S(2)}) collective-permute-start(bf16[8,16,512]{2,1,0:T(8,128)(2,1)S(1)} %get-tuple-element.128), channel_id=1, source_target_pairs={{0,12},{4,8},{8,4},{12,0},{1,13},{5,9},{9,5},{13,1},{2,14},{6,10},... | collective-permute-start | bytes 393224 | tf_op jit(solution)/shard_map/ppermute | solution.py:215
  6.3 1.6 %collective-permute-start.3 = (bf16[4,48,512]{2,1,0:T(8,128)(2,1)S(1)}, bf16[4,48,512]{2,1,0:T(8,128)(2,1)S(1)}, u32[]{:S(2)}, u32[]{:S(2)}) collective-permute-start(bf16[4,48,512]{2,1,0:T(8,128)(2,1)S(1)} %get-tuple-element.122.refs_0_), channel_id=1, source_target_pairs={{0,2},{2,0},{1,3},{3,1},{4,6},{6,4},{5,7},{7,5},{8,10},{10,8},{9,1... | collective-permute-start | bytes 589832 | tf_op jit(solution)/shard_map/ppermute | solution.py:218
  9.1 7.0 %shard_map.64 = (bf16[32,512,512]{2,1,0:T(8,128)(2,1)S(1)}, bf16[384,512]{1,0:T(8,128)(2,1)S(1)}, bf16[512,384]{1,0:T(8,128)(2,1)S(1)}) custom-call(s32[6]{0:T(128)S(1)} %compare_select_fusion.1.where, s32[4,4]{1,0:T(4,128)S(1)} %bitcast.27, s32[1]{0:T(128)S(6)} %copy.16.starts, bf16[32,512,512]{2,1,0:T(8,128)(2,1)} %bitcast.28, bf16[32,24]{1,0:T(8,128)(2,1)S(1)} %bitcast.26), custom_call_target="tpu_custom_call" | custom-call | flops 1024 | bytes 1024 | tf_op jit(solution)/shard_map/pallas_call | solution.py:63
  16.6 2.7 %collective-permute-start.5 = (bf16[8,32,512]{2,1,0:T(8,128)(2,1)S(1)}, bf16[8,32,512]{2,1,0:T(8,128)(2,1)S(1)}, u32[]{:S(2)}, u32[]{:S(2)}) collective-permute-start(bf16[8,32,512]{2,1,0:T(8,128)(2,1)S(1)} %get-tuple-element.66), channel_id=1, source_target_pairs={{0,8},{4,12},{8,0},{12,4},{1,9},{5,13},{9,1},{13,5},{2,10},{6,14},... | collective-permute-start | bytes 786440 | tf_op jit(solution)/shard_map/ppermute | solution.py:215
  19.6 1.5 %collective-permute-start.7 = (bf16[8,16,512]{2,1,0:T(8,128)(2,1)S(1)}, bf16[8,16,512]{2,1,0:T(8,128)(2,1)S(1)}, u32[]{:S(2)}, u32[]{:S(2)}) collective-permute-start(bf16[8,16,512]{2,1,0:T(8,128)(2,1)S(1)} %collective-permute-done.2.refs_0_), channel_id=1, source_target_pairs={{0,2},{2,0},{1,3},{3,1},{4,6},{6,4},{5,7},{7,5},{8,10},{10,8},{9,1... | collective-permute-start | bytes 393224 | tf_op jit(solution)/shard_map/ppermute | solution.py:218
  21.6 1.5 %collective-permute-start.9 = (bf16[8,16,512]{2,1,0:T(8,128)(2,1)S(1)}, bf16[8,16,512]{2,1,0:T(8,128)(2,1)S(1)}, u32[]{:S(2)}, u32[]{:S(2)}) collective-permute-start(bf16[8,16,512]{2,1,0:T(8,128)(2,1)S(1)} %collective-permute-done.refs_0_), channel_id=1, source_target_pairs={{0,2},{2,0},{1,3},{3,1},{4,6},{6,4},{5,7},{7,5},{8,10},{10,8},{9,1... | collective-permute-start | bytes 393224 | tf_op jit(solution)/shard_map/ppermute | solution.py:218
  27.1 1.4 %shard_map.67 = (bf16[8,16,512]{2,1,0:T(8,128)(2,1)S(1)}, bf16[8,16,512]{2,1,0:T(8,128)(2,1)S(1)}) custom-call(s32[6]{0:T(128)S(1)} %compare_select_fusion.1.where, bf16[8,16,512]{2,1,0:T(8,128)(2,1)S(1)} %collective-permute-done.1.refs_0_, bf16[8,16,512]{2,1,0:T(8,128)(2,1)S(1)} %collective-permute-done.8.refs_1_, ...), custom_call_target="tpu_custom_call" | custom-call | flops 1024 | bytes 1024 | tf_op jit(solution)/shard_map/pallas_call | solution.py:102
  28.5 1.4 %shard_map.68 = (bf16[8,16,512]{2,1,0:T(8,128)(2,1)S(1)}, bf16[8,16,512]{2,1,0:T(8,128)(2,1)S(1)}) custom-call(s32[6]{0:T(128)S(1)} %compare_select_fusion.1.where, bf16[8,16,512]{2,1,0:T(8,128)(2,1)S(1)} %collective-permute-done.refs_0_, bf16[8,16,512]{2,1,0:T(8,128)(2,1)S(1)} %collective-permute-done.9.refs_1_, ...), custom_call_target="tpu_custom_call" | custom-call | flops 1024 | bytes 1024 | tf_op jit(solution)/shard_map/pallas_call | solution.py:102
  30.3 1.6 %collective-permute-start.13 = (bf16[8,32,512]{2,1,0:T(8,128)(2,1)S(1)}, bf16[8,32,512]{2,1,0:T(8,128)(2,1)S(1)}, u32[]{:S(2)}, u32[]{:S(2)}) collective-permute-start(bf16[8,32,512]{2,1,0:T(8,128)(2,1)S(1)} %collective-permute-done.6.refs_0_), channel_id=1, source_target_pairs={{0,2},{2,0},{1,3},{3,1},{4,6},{6,4},{5,7},{7,5},{8,10},{10,8},{9,1... | collective-permute-start | bytes 786440 | tf_op jit(solution)/shard_map/ppermute | solution.py:218
  33.4 6.1 %collective-permute-done.13.refs_1_ = bf16[8,32,512]{2,1,0:T(8,128)(2,1)S(1)} collective-permute-done((bf16[8,32,512]{2,1,0:T(8,128)(2,1)S(1)}, bf16[8,32,512]{2,1,0:T(8,128)(2,1)S(1)}, u32[]{:S(2)}, u32[]{:S(2)}) %collective-permute-start.13) | collective-permute-done | bytes 262176 | tf_op jit(solution)/shard_map/ppermute | solution.py:218
  39.5 1.4 %shard_map.72 = (bf16[8,32,512]{2,1,0:T(8,128)(2,1)S(1)}, bf16[8,32,512]{2,1,0:T(8,128)(2,1)S(1)}) custom-call(s32[6]{0:T(128)S(1)} %compare_select_fusion.1.where, bf16[8,32,512]{2,1,0:T(8,128)(2,1)S(1)} %collective-permute-done.6.refs_0_, bf16[8,32,512]{2,1,0:T(8,128)(2,1)S(1)} %collective-permute-done.13.refs_1_, ...), custom_call_target="tpu_custom_call" | custom-call | flops 1024 | bytes 1024 | tf_op jit(solution)/shard_map/pallas_call | solution.py:102
  41.5 3.2 %collective-permute-done.10.refs_1_ = bf16[8,32,512]{2,1,0:T(8,128)(2,1)S(1)} collective-permute-done((bf16[8,32,512]{2,1,0:T(8,128)(2,1)S(1)}, bf16[8,32,512]{2,1,0:T(8,128)(2,1)S(1)}, u32[]{:S(2)}, u32[]{:S(2)}) %collective-permute-start.10) | collective-permute-done | bytes 262176 | tf_op jit(solution)/shard_map/ppermute | solution.py:218
  44.7 1.5 %collective-permute-done.11.refs_0_ = bf16[8,32,512]{2,1,0:T(8,128)(2,1)S(1)} collective-permute-done((bf16[8,32,512]{2,1,0:T(8,128)(2,1)S(1)}, bf16[8,32,512]{2,1,0:T(8,128)(2,1)S(1)}, u32[]{:S(2)}, u32[]{:S(2)}) %collective-permute-start.11) | collective-permute-done | bytes 262176 | tf_op jit(solution)/shard_map/ppermute | solution.py:215
  46.1 1.5 %collective-permute-start.17 = (bf16[8,32,512]{2,1,0:T(8,128)(2,1)S(1)}, bf16[8,32,512]{2,1,0:T(8,128)(2,1)S(1)}, u32[]{:S(2)}, u32[]{:S(2)}) collective-permute-start(bf16[8,32,512]{2,1,0:T(8,128)(2,1)S(1)} %collective-permute-done.11.refs_0_), channel_id=1, source_target_pairs={{0,2},{2,0},{1,3},{3,1},{4,6},{6,4},{5,7},{7,5},{8,10},{10,8},{9,1... | collective-permute-start | bytes 786440 | tf_op jit(solution)/shard_map/ppermute | solution.py:218
  49.4 2.6 %collective-permute-start.16 = (bf16[8,16,512]{2,1,0:T(8,128)(2,1)S(1)}, bf16[8,16,512]{2,1,0:T(8,128)(2,1)S(1)}, u32[]{:S(2)}, u32[]{:S(2)}) collective-permute-start(bf16[8,16,512]{2,1,0:T(8,128)(2,1)S(1)} %get-tuple-element.100), channel_id=1, source_target_pairs={{0,4},{4,0},{8,12},{12,8},{1,5},{5,1},{9,13},{13,9},{2,6},{6,2},{1... | collective-permute-start | bytes 393224 | tf_op jit(solution)/shard_map/ppermute | solution.py:215
  52.0 1.4 %shard_map.73 = (bf16[8,32,512]{2,1,0:T(8,128)(2,1)S(1)}, bf16[8,32,512]{2,1,0:T(8,128)(2,1)S(1)}) custom-call(s32[6]{0:T(128)S(1)} %compare_select_fusion.1.where, bf16[8,32,512]{2,1,0:T(8,128)(2,1)S(1)} %collective-permute-done.5.refs_0_, bf16[8,32,512]{2,1,0:T(8,128)(2,1)S(1)} %collective-permute-done.10.refs_1_, ...), custom_call_target="tpu_custom_call" | custom-call | flops 1024 | bytes 1024 | tf_op jit(solution)/shard_map/pallas_call | solution.py:102
  53.4 1.4 %shard_map.74 = (bf16[8,32,512]{2,1,0:T(8,128)(2,1)S(1)}, bf16[8,32,512]{2,1,0:T(8,128)(2,1)S(1)}) custom-call(s32[6]{0:T(128)S(1)} %compare_select_fusion.1.where, bf16[8,32,512]{2,1,0:T(8,128)(2,1)S(1)} %collective-permute-done.11.refs_0_, bf16[8,32,512]{2,1,0:T(8,128)(2,1)S(1)} %collective-permute-done.17.refs_1_, ...), custom_call_target="tpu_custom_call" | custom-call | flops 1024 | bytes 1024 | tf_op jit(solution)/shard_map/pallas_call | solution.py:102
  56.7 3.8 %collective-permute-done.15.refs_2_ = bf16[8,16,512]{2,1,0:T(8,128)(2,1)S(1)} collective-permute-done((bf16[8,16,512]{2,1,0:T(8,128)(2,1)S(1)}, bf16[8,16,512]{2,1,0:T(8,128)(2,1)S(1)}, u32[]{:S(2)}, u32[]{:S(2)}) %collective-permute-start.15) | collective-permute-done | bytes 131104 | tf_op jit(solution)/shard_map/ppermute | solution.py:215
  60.6 2.3 %collective-permute-done.18.came_ref = bf16[24,32,512]{2,1,0:T(8,128)(2,1)S(1)} collective-permute-done((bf16[24,32,512]{2,1,0:T(8,128)(2,1)S(1)}, bf16[24,32,512]{2,1,0:T(8,128)(2,1)S(1)}, u32[]{:S(2)}, u32[]{:S(2)}) %collective-permute-start.18) | collective-permute-done | bytes 786464 | tf_op jit(solution)/shard_map/ppermute | solution.py:264
  64.2 2.2 %collective-permute-start.19 = (bf16[8,32,512]{2,1,0:T(8,128)(2,1)S(1)}, bf16[8,32,512]{2,1,0:T(8,128)(2,1)S(1)}, u32[]{:S(2)}, u32[]{:S(2)}) collective-permute-start(bf16[8,32,512]{2,1,0:T(8,128)(2,1)S(1)} %get-tuple-element.113), channel_id=1, source_target_pairs={{0,8},{4,12},{8,0},{12,4},{1,9},{5,13},{9,1},{13,5},{2,10},{6,14},... | collective-permute-start | bytes 786440 | tf_op jit(solution)/shard_map/ppermute | solution.py:215
  67.7 1.4 %shard_map.78.refs_2_ = bf16[8,4,48,512]{3,2,1,0:T(8,128)(2,1)} custom-call(s32[6]{0:T(128)S(1)} %compare_select_fusion.1.where, bf16[8,16,512]{2,1,0:T(8,128)(2,1)S(1)} %collective-permute-done.16.refs_0_, bf16[8,16,512]{2,1,0:T(8,128)(2,1)S(1)} %collective-permute-done.14.refs_1_, bf16[8,16,512]{2,1,0:T(8,128)(2,1)S(1)} %collective-permute-done.15.refs_2_, ...), custom_call_target="tpu_custom_call" | custom-call | flops 1024 | bytes 1024 | tf_op jit(solution)/shard_map/pallas_call | solution.py:190
  69.0 5.9 %collective-permute-done.21.refs_1_ = bf16[8,32,512]{2,1,0:T(8,128)(2,1)S(1)} collective-permute-done((bf16[8,32,512]{2,1,0:T(8,128)(2,1)S(1)}, bf16[8,32,512]{2,1,0:T(8,128)(2,1)S(1)}, u32[]{:S(2)}, u32[]{:S(2)}) %collective-permute-start.21) | collective-permute-done | bytes 262176 | tf_op jit(solution)/shard_map/ppermute | solution.py:215
  76.3 8.0 %collective-permute-done.19.refs_0_ = bf16[8,32,512]{2,1,0:T(8,128)(2,1)S(1)} collective-permute-done((bf16[8,32,512]{2,1,0:T(8,128)(2,1)S(1)}, bf16[8,32,512]{2,1,0:T(8,128)(2,1)S(1)}, u32[]{:S(2)}, u32[]{:S(2)}) %collective-permute-start.19) | collective-permute-done | bytes 262176 | tf_op jit(solution)/shard_map/ppermute | solution.py:215
  84.3 6.3 %collective-permute-done.20.refs_1_ = bf16[8,32,512]{2,1,0:T(8,128)(2,1)S(1)} collective-permute-done((bf16[8,32,512]{2,1,0:T(8,128)(2,1)S(1)}, bf16[8,32,512]{2,1,0:T(8,128)(2,1)S(1)}, u32[]{:S(2)}, u32[]{:S(2)}) %collective-permute-start.20) | collective-permute-done | bytes 262176 | tf_op jit(solution)/shard_map/ppermute | solution.py:215
  (52 shorter events, 22.0 us)
Async XLA Ops:
  0.0 9.0 %copy-start.2 = (bf16[1,32,24]{1,2,0:T(8,128)(2,1)S(1)}, bf16[1,32,24]{1,2,0:T(8,128)(2,1)}, u32[]{:S(2)}) copy-start(bf16[1,32,24]{1,2,0:T(8,128)(2,1)} %param.10) | copy-start | bytes 4612
  0.0 9.1 %copy-start = (s32[1,4,4]{2,1,0:T(4,128)S(1)}, s32[1,4,4]{2,1,0:T(4,128)}, u32[]{:S(2)}) copy-start(s32[1,4,4]{2,1,0:T(4,128)} %param.8) | copy-start | bytes 196
  1.1 15.2 %collective-permute-start = (bf16[8,16,512]{2,1,0:T(8,128)(2,1)S(1)}, bf16[8,16,512]{2,1,0:T(8,128)(2,1)S(1)}, u32[]{:S(2)}, u32[]{:S(2)}) collective-permute-start(bf16[8,16,512]{2,1,0:T(8,128)(2,1)S(1)} %get-tuple-element.128), channel_id=1, source_target_pairs={{0,12},{4,8},{8,4},{12,0},{1,13},{5,9},{9,5},{13,1},{2,14},{6,10},... | collective-permute-start | bytes 393224 | tf_op jit(solution)/shard_map/ppermute | solution.py:215
  2.7 13.5 %collective-permute-start.1 = (bf16[8,16,512]{2,1,0:T(8,128)(2,1)S(1)}, bf16[8,16,512]{2,1,0:T(8,128)(2,1)S(1)}, u32[]{:S(2)}, u32[]{:S(2)}) collective-permute-start(bf16[8,16,512]{2,1,0:T(8,128)(2,1)S(1)} %get-tuple-element.127), channel_id=1, source_target_pairs={{0,8},{4,12},{8,0},{12,4},{1,9},{5,13},{9,1},{13,5},{2,10},{6,14},... | collective-permute-start | bytes 393224 | tf_op jit(solution)/shard_map/ppermute | solution.py:215
  4.0 12.3 %collective-permute-start.2 = (bf16[8,16,512]{2,1,0:T(8,128)(2,1)S(1)}, bf16[8,16,512]{2,1,0:T(8,128)(2,1)S(1)}, u32[]{:S(2)}, u32[]{:S(2)}) collective-permute-start(bf16[8,16,512]{2,1,0:T(8,128)(2,1)S(1)} %get-tuple-element.126), channel_id=1, source_target_pairs={{0,4},{4,0},{8,12},{12,8},{1,5},{5,1},{9,13},{13,9},{2,6},{6,2},{1... | collective-permute-start | bytes 393224 | tf_op jit(solution)/shard_map/ppermute | solution.py:215
  6.3 10.0 %collective-permute-start.3 = (bf16[4,48,512]{2,1,0:T(8,128)(2,1)S(1)}, bf16[4,48,512]{2,1,0:T(8,128)(2,1)S(1)}, u32[]{:S(2)}, u32[]{:S(2)}) collective-permute-start(bf16[4,48,512]{2,1,0:T(8,128)(2,1)S(1)} %get-tuple-element.122.refs_0_), channel_id=1, source_target_pairs={{0,2},{2,0},{1,3},{3,1},{4,6},{6,4},{5,7},{7,5},{8,10},{10,8},{9,1... | collective-permute-start | bytes 589832 | tf_op jit(solution)/shard_map/ppermute | solution.py:218
  7.8 8.8 %collective-permute-start.4 = (bf16[4,48,512]{2,1,0:T(8,128)(2,1)S(1)}, bf16[4,48,512]{2,1,0:T(8,128)(2,1)S(1)}, u32[]{:S(2)}, u32[]{:S(2)}) collective-permute-start(bf16[4,48,512]{2,1,0:T(8,128)(2,1)S(1)} %get-tuple-element.121.refs_1_), channel_id=1, source_target_pairs={{0,2},{2,0},{1,3},{3,1},{4,6},{6,4},{5,7},{7,5},{8,10},{10,8},{9,1... | collective-permute-start | bytes 589832 | tf_op jit(solution)/shard_map/ppermute | solution.py:218
  16.6 13.6 %collective-permute-start.5 = (bf16[8,32,512]{2,1,0:T(8,128)(2,1)S(1)}, bf16[8,32,512]{2,1,0:T(8,128)(2,1)S(1)}, u32[]{:S(2)}, u32[]{:S(2)}) collective-permute-start(bf16[8,32,512]{2,1,0:T(8,128)(2,1)S(1)} %get-tuple-element.66), channel_id=1, source_target_pairs={{0,8},{4,12},{8,0},{12,4},{1,9},{5,13},{9,1},{13,5},{2,10},{6,14},... | collective-permute-start | bytes 786440 | tf_op jit(solution)/shard_map/ppermute | solution.py:215
  19.3 10.9 %collective-permute-start.6 = (bf16[8,32,512]{2,1,0:T(8,128)(2,1)S(1)}, bf16[8,32,512]{2,1,0:T(8,128)(2,1)S(1)}, u32[]{:S(2)}, u32[]{:S(2)}) collective-permute-start(bf16[8,32,512]{2,1,0:T(8,128)(2,1)S(1)} %get-tuple-element.67), channel_id=1, source_target_pairs={{0,4},{4,0},{8,12},{12,8},{1,5},{5,1},{9,13},{13,9},{2,6},{6,2},{1... | collective-permute-start | bytes 786440 | tf_op jit(solution)/shard_map/ppermute | solution.py:215
  19.6 6.1 %collective-permute-start.7 = (bf16[8,16,512]{2,1,0:T(8,128)(2,1)S(1)}, bf16[8,16,512]{2,1,0:T(8,128)(2,1)S(1)}, u32[]{:S(2)}, u32[]{:S(2)}) collective-permute-start(bf16[8,16,512]{2,1,0:T(8,128)(2,1)S(1)} %collective-permute-done.2.refs_0_), channel_id=1, source_target_pairs={{0,2},{2,0},{1,3},{3,1},{4,6},{6,4},{5,7},{7,5},{8,10},{10,8},{9,1... | collective-permute-start | bytes 393224 | tf_op jit(solution)/shard_map/ppermute | solution.py:218
  21.0 6.0 %collective-permute-start.8 = (bf16[8,16,512]{2,1,0:T(8,128)(2,1)S(1)}, bf16[8,16,512]{2,1,0:T(8,128)(2,1)S(1)}, u32[]{:S(2)}, u32[]{:S(2)}) collective-permute-start(bf16[8,16,512]{2,1,0:T(8,128)(2,1)S(1)} %collective-permute-done.1.refs_0_), channel_id=1, source_target_pairs={{0,2},{2,0},{1,3},{3,1},{4,6},{6,4},{5,7},{7,5},{8,10},{10,8},{9,1... | collective-permute-start | bytes 393224 | tf_op jit(solution)/shard_map/ppermute | solution.py:218
  21.6 6.9 %collective-permute-start.9 = (bf16[8,16,512]{2,1,0:T(8,128)(2,1)S(1)}, bf16[8,16,512]{2,1,0:T(8,128)(2,1)S(1)}, u32[]{:S(2)}, u32[]{:S(2)}) collective-permute-start(bf16[8,16,512]{2,1,0:T(8,128)(2,1)S(1)} %collective-permute-done.refs_0_), channel_id=1, source_target_pairs={{0,2},{2,0},{1,3},{3,1},{4,6},{6,4},{5,7},{7,5},{8,10},{10,8},{9,1... | collective-permute-start | bytes 393224 | tf_op jit(solution)/shard_map/ppermute | solution.py:218
  30.3 10.6 %collective-permute-start.12 = (bf16[24,16,512]{2,1,0:T(8,128)(2,1)S(1)}, bf16[24,16,512]{2,1,0:T(8,128)(2,1)S(1)}, u32[]{:S(2)}, u32[]{:S(2)}) collective-permute-start(bf16[24,16,512]{2,1,0:T(8,128)(2,1)S(1)} %shard_map.69), channel_id=1, source_target_pairs={{0,1},{1,0},{2,3},{3,2},{4,5},{5,4},{6,7},{7,6},{8,9},{9,8},{10,11... | collective-permute-start | bytes 1179656 | tf_op jit(solution)/shard_map/ppermute | solution.py:252
  30.3 9.2 %collective-permute-start.13 = (bf16[8,32,512]{2,1,0:T(8,128)(2,1)S(1)}, bf16[8,32,512]{2,1,0:T(8,128)(2,1)S(1)}, u32[]{:S(2)}, u32[]{:S(2)}) collective-permute-start(bf16[8,32,512]{2,1,0:T(8,128)(2,1)S(1)} %collective-permute-done.6.refs_0_), channel_id=1, source_target_pairs={{0,2},{2,0},{1,3},{3,1},{4,6},{6,4},{5,7},{7,5},{8,10},{10,8},{9,1... | collective-permute-start | bytes 786440 | tf_op jit(solution)/shard_map/ppermute | solution.py:218
  31.9 12.8 %collective-permute-start.10 = (bf16[8,32,512]{2,1,0:T(8,128)(2,1)S(1)}, bf16[8,32,512]{2,1,0:T(8,128)(2,1)S(1)}, u32[]{:S(2)}, u32[]{:S(2)}) collective-permute-start(bf16[8,32,512]{2,1,0:T(8,128)(2,1)S(1)} %collective-permute-done.5.refs_0_), channel_id=1, source_target_pairs={{0,2},{2,0},{1,3},{3,1},{4,6},{6,4},{5,7},{7,5},{8,10},{10,8},{9,1... | collective-permute-start | bytes 786440 | tf_op jit(solution)/shard_map/ppermute | solution.py:218
  32.4 13.7 %collective-permute-start.11 = (bf16[8,32,512]{2,1,0:T(8,128)(2,1)S(1)}, bf16[8,32,512]{2,1,0:T(8,128)(2,1)S(1)}, u32[]{:S(2)}, u32[]{:S(2)}) collective-permute-start(bf16[8,32,512]{2,1,0:T(8,128)(2,1)S(1)} %get-tuple-element.86), channel_id=1, source_target_pairs={{0,12},{4,8},{8,4},{12,0},{1,13},{5,9},{9,5},{13,1},{2,14},{6,10},... | collective-permute-start | bytes 786440 | tf_op jit(solution)/shard_map/ppermute | solution.py:215
  46.1 7.3 %collective-permute-start.17 = (bf16[8,32,512]{2,1,0:T(8,128)(2,1)S(1)}, bf16[8,32,512]{2,1,0:T(8,128)(2,1)S(1)}, u32[]{:S(2)}, u32[]{:S(2)}) collective-permute-start(bf16[8,32,512]{2,1,0:T(8,128)(2,1)S(1)} %collective-permute-done.11.refs_0_), channel_id=1, source_target_pairs={{0,2},{2,0},{1,3},{3,1},{4,6},{6,4},{5,7},{7,5},{8,10},{10,8},{9,1... | collective-permute-start | bytes 786440 | tf_op jit(solution)/shard_map/ppermute | solution.py:218
  47.6 9.1 %collective-permute-start.14 = (bf16[8,16,512]{2,1,0:T(8,128)(2,1)S(1)}, bf16[8,16,512]{2,1,0:T(8,128)(2,1)S(1)}, u32[]{:S(2)}, u32[]{:S(2)}) collective-permute-start(bf16[8,16,512]{2,1,0:T(8,128)(2,1)S(1)} %get-tuple-element.98), channel_id=1, source_target_pairs={{0,8},{4,12},{8,0},{12,4},{1,9},{5,13},{9,1},{13,5},{2,10},{6,14},... | collective-permute-start | bytes 393224 | tf_op jit(solution)/shard_map/ppermute | solution.py:215
  48.0 12.5 %collective-permute-start.15 = (bf16[8,16,512]{2,1,0:T(8,128)(2,1)S(1)}, bf16[8,16,512]{2,1,0:T(8,128)(2,1)S(1)}, u32[]{:S(2)}, u32[]{:S(2)}) collective-permute-start(bf16[8,16,512]{2,1,0:T(8,128)(2,1)S(1)} %get-tuple-element.99), channel_id=1, source_target_pairs={{0,12},{4,8},{8,4},{12,0},{1,13},{5,9},{9,5},{13,1},{2,14},{6,10},... | collective-permute-start | bytes 393224 | tf_op jit(solution)/shard_map/ppermute | solution.py:215
  49.4 11.2 %collective-permute-start.16 = (bf16[8,16,512]{2,1,0:T(8,128)(2,1)S(1)}, bf16[8,16,512]{2,1,0:T(8,128)(2,1)S(1)}, u32[]{:S(2)}, u32[]{:S(2)}) collective-permute-start(bf16[8,16,512]{2,1,0:T(8,128)(2,1)S(1)} %get-tuple-element.100), channel_id=1, source_target_pairs={{0,4},{4,0},{8,12},{12,8},{1,5},{5,1},{9,13},{13,9},{2,6},{6,2},{1... | collective-permute-start | bytes 393224 | tf_op jit(solution)/shard_map/ppermute | solution.py:215
  60.6 2.3 %collective-permute-start.18 = (bf16[24,32,512]{2,1,0:T(8,128)(2,1)S(1)}, bf16[24,32,512]{2,1,0:T(8,128)(2,1)S(1)}, u32[]{:S(2)}, u32[]{:S(2)}) collective-permute-start(bf16[24,32,512]{2,1,0:T(8,128)(2,1)S(1)} %shard_map.76), channel_id=1, source_target_pairs={{0,1},{1,0},{2,3},{3,2},{4,5},{5,4},{6,7},{7,6},{8,9},{9,8},{10,11... | collective-permute-start | bytes 2359304 | tf_op jit(solution)/shard_map/ppermute | solution.py:264
  64.1 10.8 %collective-permute-start.21 = (bf16[8,32,512]{2,1,0:T(8,128)(2,1)S(1)}, bf16[8,32,512]{2,1,0:T(8,128)(2,1)S(1)}, u32[]{:S(2)}, u32[]{:S(2)}) collective-permute-start(bf16[8,32,512]{2,1,0:T(8,128)(2,1)S(1)} %get-tuple-element.116), channel_id=1, source_target_pairs={{0,4},{4,0},{8,12},{12,8},{1,5},{5,1},{9,13},{13,9},{2,6},{6,2},{1... | collective-permute-start | bytes 786440 | tf_op jit(solution)/shard_map/ppermute | solution.py:215
  64.2 20.1 %collective-permute-start.19 = (bf16[8,32,512]{2,1,0:T(8,128)(2,1)S(1)}, bf16[8,32,512]{2,1,0:T(8,128)(2,1)S(1)}, u32[]{:S(2)}, u32[]{:S(2)}) collective-permute-start(bf16[8,32,512]{2,1,0:T(8,128)(2,1)S(1)} %get-tuple-element.113), channel_id=1, source_target_pairs={{0,8},{4,12},{8,0},{12,4},{1,9},{5,13},{9,1},{13,5},{2,10},{6,14},... | collective-permute-start | bytes 786440 | tf_op jit(solution)/shard_map/ppermute | solution.py:215
  66.4 24.2 %collective-permute-start.20 = (bf16[8,32,512]{2,1,0:T(8,128)(2,1)S(1)}, bf16[8,32,512]{2,1,0:T(8,128)(2,1)S(1)}, u32[]{:S(2)}, u32[]{:S(2)}) collective-permute-start(bf16[8,32,512]{2,1,0:T(8,128)(2,1)S(1)} %get-tuple-element.114), channel_id=1, source_target_pairs={{0,12},{4,8},{8,4},{12,0},{1,13},{5,9},{9,5},{13,1},{2,14},{6,10},... | collective-permute-start | bytes 786440 | tf_op jit(solution)/shard_map/ppermute | solution.py:215
  (2 other events, 10.3 us)

commit v9 on v8

--- a/solution.py
+++ b/solution.py
@@ -174,7 +174,7 @@
     pieces, out, sems = refs[:count], refs[-2], refs[-1]
     rows = pieces[0].shape[1]
     copies = [
-        pltpu.make_async_copy(pieces[n], out.at[low:high, where[j], first:first + rows, :], sems.at[n])
+        pltpu.make_async_copy(pieces[n], out.at[low:high, where[PARTS + 2 + j], first:first + rows, :], sems.at[n])
         for n, (j, low, high) in enumerate(spots)
     ]
     for copy in copies:
@@ -212,18 +212,18 @@
     other = [(0, 1), (1, 0)]
 
     def along_z(value, j):
-        return lax.ppermute(value, "fm", [(i, i ^ j) for i in range(parts)])
+        return lax.ppermute(value, "fm", [(i, (i + j) % parts) for i in range(parts)])
 
     def along_x(value):
         return lax.ppermute(value, "kl", other)
 
     def cut(j, first, rows):
-        return lax.dynamic_slice(visibility, (0, z ^ j, first, 0), (freqs, 1, rows, base)).reshape(freqs, rows, base)
-
-    index = jnp.arange(parts + 2, dtype=jnp.int32)
-    where = jnp.where(
-        index < parts, z ^ index, jnp.where(index == parts, (x == p).astype(jnp.int32), x * ell_tiles)
-    ).astype(jnp.int32)
+        return lax.dynamic_slice(visibility, (0, (z + j) % parts, first, 0), (freqs, 1, rows, base)).reshape(freqs, rows, base)
+
+    index = jnp.arange(2 * parts + 2, dtype=jnp.int32)
+    where = jnp.where(index < parts, (z - index) % parts, (z + index - parts - 2) % parts)
+    where = jnp.where(index == parts, (x == p).astype(jnp.int32), where)
+    where = jnp.where(index == parts + 1, x * ell_tiles, where).astype(jnp.int32)
     ratio = signal_noise[0] / (1.0 + signal_noise[0])
     ratios = jnp.broadcast_to(ratio[:, None, None], (n_modes, 1, ell))
     beam = beam_transfer.reshape(freq_total, base, ell)
@@ -233,37 +233,35 @@
     most, half = rows_all - ROWS, freqs // 2
     blocks = [[(0, f)] for f in range(freqs)]
     halves = [[(f // half, f % half)] for f in range(freqs)]
-    a = {j: along_z(cut(j, 0, ROWS), j) for j in (3, 2, 1)}
+    a = {j: along_z(cut(j, 0, ROWS), j) for j in (1, 3, 2)}
     mine = [cut(0, 0, rows_all)[n:n + half] for n in (0, half)]
     others = [along_x(part) for part in mine]
     b = {j: cut(j, ROWS, most) for j in (1, 2, 3)}
     held, down, up = hold(where, tile_mask[0], first_block, beam, eigen_modes[0])
-    (a[3], a[2], a[1]), b, others, down, up = fence(((a[3], a[2], a[1]), b, others, down, up))
-    b[1], b[2] = along_z(b[1], 1), along_z(b[2], 2)
+    (a[1], a[3], a[2]), b, others, down, up = fence(((a[1], a[3], a[2]), b, others, down, up))
+    b[1], b[3] = along_z(b[1], 1), along_z(b[3], 3)
     own = project(where, mine, others, held, 0, halves)
     skies = [own] + [project(where, [a[j]], [along_x(a[j])], held, j, blocks) for j in (1, 2, 3)]
     gone = reduce(down, [leave for _, leave in skies], (0, 0, 0, 0), n_modes)
     stay_a = [stay for stay, _ in skies]
-    (b[2], b[1]), b[3], stay_a, gone = fence(((b[2], b[1]), b[3], stay_a, gone))
-    x_2, x_1 = along_x(b[2]), along_x(b[1])
-    b[3] = along_z(b[3], 3)
+    (b[3], b[1]), b[2], stay_a, gone = fence(((b[3], b[1]), b[2], stay_a, gone))
+    x_3, x_1 = along_x(b[3]), along_x(b[1])
+    b[2] = along_z(b[2], 2)
     kept = reduce(down, stay_a, (0, 0, 0, 0), n_modes, jnp.float32)
-    spots = [(j, 0, freqs) for j in (1, 2, 3, 0)]
+    spots = [(j, 0, freqs) for j in (1, 3, 2, 0)]
     outs = restore(kept, lax.ppermute(gone, "pol", other), ratios, up, spots)
     near = project(where, [b[1]], [x_1], held, 1, blocks)
-    x_2, b, outs, near = fence((x_2, b, outs, near))
-    first = {j: along_z(outs[j - 1], j) for j in (1, 2, 3)}
-    first[0] = outs[3]
-    x_3 = along_x(b[3])
-    skies = [own, near] + [project(where, [b[j]], [x], held, j, blocks) for j, x in ((2, x_2), (3, x_3))]
+    x_3, b, outs, near = fence((x_3, b, outs, near))
+    first = [along_z(outs[n], -spots[n][0]) for n in range(3)]
+    x_2 = along_x(b[2])
+    far = [project(where, [b[j]], [x], held, j, blocks) for j, x in ((3, x_3), (2, x_2))]
+    skies = [own, near, far[1], far[0]]
     gone = reduce(down, [leave for _, leave in skies], (ROWS, 0, 0, 0), n_modes)
     kept = reduce(down, [stay for stay, _ in skies], (ROWS, 0, 0, 0), n_modes, jnp.float32)
-    (first[2], first[3], first[1]), first[0], kept, gone = fence(
-        ((first[2], first[3], first[1]), first[0], kept, gone)
-    )
+    first, here, kept, gone = fence((first, outs[3], kept, gone))
     outs = fence(restore(kept, lax.ppermute(gone, "pol", other), ratios, up, spots))
-    back = [along_z(outs[j - 1], j) for j in (1, 2, 3)]
-    result = place(where, [first[j] for j in (1, 2, 3, 0)], spots, 0, shape)
+    back = [along_z(outs[n], -spots[n][0]) for n in range(3)]
+    result = place(where, [*first, here], spots, 0, shape)
     result = place(where, [outs[3], back[0]], [spots[3], spots[0]], ROWS, shape, into=result)
     return place(where, back[1:], spots[1:3], ROWS, shape, into=result)
 

time: 92.1 us -> 93.4 us (1.014)
  the two profiles are of different devices: /device:TPU:12 before, /device:TPU:0 now
where the time goes in v9:
time: 93.4 us; the launch traced here: 93.3 us
  waiting for transfers between devices  40.9 us (44%)
  Pallas kernels  25.1 us (27%)
  starting transfers between devices  24 us (26%)
  local copies, waits for them, and re-layouts  2.4 us (3%)
    ppermute x12, waiting for transfers between devices, along_z(): lax.ppermute(value, 'fm', [(i, (i + j) % parts) for i in range(parts)])  24.5 us
    ppermute x12, starting transfers between devices, along_z(): lax.ppermute(value, 'fm', [(i, (i + j) % parts) for i in range(parts)])  14.7 us
    ppermute x8, waiting for transfers between devices, along_x(): return lax.ppermute(value, 'kl', other)  14.1 us
    pallas_call x7, Pallas kernels, project(): pl.pallas_call(functools.partial(project_kernel, piece=piece, blocks=bloc...  9.57 us
    ppermute x8, starting transfers between devices, along_x(): return lax.ppermute(value, 'kl', other)  9.19 us
    pallas_call x1, Pallas kernels, hold(): pl.pallas_call(hold_kernel, grid_spec=pltpu.PrefetchScalarGridSpec(num_sc...  7.04 us
    pallas_call x3, Pallas kernels, place(): pl.pallas_call(functools.partial(place_kernel, spots=spots, first=first),...  4.06 us
    pallas_call x4, Pallas kernels, reduce(): pl.pallas_call(reduce_kernel, grid=(rows // ROWS,), in_specs=[fixed(modes...  2.62 us
  transfers between devices with their start and end apart: 22, of which 11 were waited for; matrix products, arithmetic and copies ran while one was open for 1% of the time, Pallas kernels for 24%

profile of v9, /device:TPU:0, one launch (start us, length us, event | category | flops | bytes accessed | tf_op | source)
XLA Modules:
  0.0 93.3 jit_solution(7591544716320124734)
XLA Ops:
  1.1 3.1 %collective-permute-start = (bf16[8,16,512]{2,1,0:T(8,128)(2,1)S(1)}, bf16[8,16,512]{2,1,0:T(8,128)(2,1)S(1)}, u32[]{:S(2)}, u32[]{:S(2)}) collective-permute-start(bf16[8,16,512]{2,1,0:T(8,128)(2,1)S(1)} %get-tuple-element.128), channel_id=1, source_target_pairs={{0,4},{4,8},{8,12},{12,0},{1,5},{5,9},{9,13},{13,1},{2,6},{6,10},{... | collective-permute-start | bytes 393224 | tf_op jit(solution)/shard_map/ppermute | solution.py:215
  4.2 2.1 %collective-permute-start.1 = (bf16[8,16,512]{2,1,0:T(8,128)(2,1)S(1)}, bf16[8,16,512]{2,1,0:T(8,128)(2,1)S(1)}, u32[]{:S(2)}, u32[]{:S(2)}) collective-permute-start(bf16[8,16,512]{2,1,0:T(8,128)(2,1)S(1)} %get-tuple-element.127), channel_id=1, source_target_pairs={{0,12},{4,0},{8,4},{12,8},{1,13},{5,1},{9,5},{13,9},{2,14},{6,2},{... | collective-permute-start | bytes 393224 | tf_op jit(solution)/shard_map/ppermute | solution.py:215
  8.3 1.6 %collective-permute-start.3 = (bf16[4,48,512]{2,1,0:T(8,128)(2,1)S(1)}, bf16[4,48,512]{2,1,0:T(8,128)(2,1)S(1)}, u32[]{:S(2)}, u32[]{:S(2)}) collective-permute-start(bf16[4,48,512]{2,1,0:T(8,128)(2,1)S(1)} %get-tuple-element.122.refs_0_), channel_id=1, source_target_pairs={{0,2},{2,0},{1,3},{3,1},{4,6},{6,4},{5,7},{7,5},{8,10},{10,8},{9,1... | collective-permute-start | bytes 589832 | tf_op jit(solution)/shard_map/ppermute | solution.py:218
  11.1 7.0 %shard_map.64 = (bf16[32,512,512]{2,1,0:T(8,128)(2,1)S(1)}, bf16[384,512]{1,0:T(8,128)(2,1)S(1)}, bf16[512,384]{1,0:T(8,128)(2,1)S(1)}) custom-call(s32[10]{0:T(128)S(1)} %compare_select_fusion.6.where, s32[4,4]{1,0:T(4,128)S(1)} %bitcast.27, s32[1]{0:T(128)S(6)} %copy.16.starts, bf16[32,512,512]{2,1,0:T(8,128)(2,1)} %bitcast.28, bf16[32,24]{1,0:T(8,128)(2,1)S(1)} %bitcast.26), custom_call_target="tpu_custom_call" | custom-call | flops 1024 | bytes 1024 | tf_op jit(solution)/shard_map/pallas_call | solution.py:63
  18.3 1.4 %collective-permute-start.5 = (bf16[8,32,512]{2,1,0:T(8,128)(2,1)S(1)}, bf16[8,32,512]{2,1,0:T(8,128)(2,1)S(1)}, u32[]{:S(2)}, u32[]{:S(2)}) collective-permute-start(bf16[8,32,512]{2,1,0:T(8,128)(2,1)S(1)} %get-tuple-element.66), channel_id=1, source_target_pairs={{0,12},{4,0},{8,4},{12,8},{1,13},{5,1},{9,5},{13,9},{2,14},{6,2},{... | collective-permute-start | bytes 786440 | tf_op jit(solution)/shard_map/ppermute | solution.py:215
  20.4 1.5 %collective-permute-start.7 = (bf16[8,16,512]{2,1,0:T(8,128)(2,1)S(1)}, bf16[8,16,512]{2,1,0:T(8,128)(2,1)S(1)}, u32[]{:S(2)}, u32[]{:S(2)}) collective-permute-start(bf16[8,16,512]{2,1,0:T(8,128)(2,1)S(1)} %collective-permute-done.refs_0_), channel_id=1, source_target_pairs={{0,2},{2,0},{1,3},{3,1},{4,6},{6,4},{5,7},{7,5},{8,10},{10,8},{9,1... | collective-permute-start | bytes 393224 | tf_op jit(solution)/shard_map/ppermute | solution.py:218
  22.4 1.5 %collective-permute-start.9 = (bf16[8,16,512]{2,1,0:T(8,128)(2,1)S(1)}, bf16[8,16,512]{2,1,0:T(8,128)(2,1)S(1)}, u32[]{:S(2)}, u32[]{:S(2)}) collective-permute-start(bf16[8,16,512]{2,1,0:T(8,128)(2,1)S(1)} %collective-permute-done.1.refs_0_), channel_id=1, source_target_pairs={{0,2},{2,0},{1,3},{3,1},{4,6},{6,4},{5,7},{7,5},{8,10},{10,8},{9,1... | collective-permute-start | bytes 393224 | tf_op jit(solution)/shard_map/ppermute | solution.py:218
  25.3 1.6 %collective-permute-done.7.refs_1_ = bf16[8,16,512]{2,1,0:T(8,128)(2,1)S(1)} collective-permute-done((bf16[8,16,512]{2,1,0:T(8,128)(2,1)S(1)}, bf16[8,16,512]{2,1,0:T(8,128)(2,1)S(1)}, u32[]{:S(2)}, u32[]{:S(2)}) %collective-permute-start.7) | collective-permute-done | bytes 131104 | tf_op jit(solution)/shard_map/ppermute | solution.py:218
  32.5 1.6 %collective-permute-start.13 = (bf16[8,32,512]{2,1,0:T(8,128)(2,1)S(1)}, bf16[8,32,512]{2,1,0:T(8,128)(2,1)S(1)}, u32[]{:S(2)}, u32[]{:S(2)}) collective-permute-start(bf16[8,32,512]{2,1,0:T(8,128)(2,1)S(1)} %collective-permute-done.6.refs_0_), channel_id=1, source_target_pairs={{0,2},{2,0},{1,3},{3,1},{4,6},{6,4},{5,7},{7,5},{8,10},{10,8},{9,1... | collective-permute-start | bytes 786440 | tf_op jit(solution)/shard_map/ppermute | solution.py:218
  35.9 5.8 %collective-permute-done.13.refs_1_ = bf16[8,32,512]{2,1,0:T(8,128)(2,1)S(1)} collective-permute-done((bf16[8,32,512]{2,1,0:T(8,128)(2,1)S(1)}, bf16[8,32,512]{2,1,0:T(8,128)(2,1)S(1)}, u32[]{:S(2)}, u32[]{:S(2)}) %collective-permute-start.13) | collective-permute-done | bytes 262176 | tf_op jit(solution)/shard_map/ppermute | solution.py:218
  41.7 1.4 %shard_map.72 = (bf16[8,32,512]{2,1,0:T(8,128)(2,1)S(1)}, bf16[8,32,512]{2,1,0:T(8,128)(2,1)S(1)}) custom-call(s32[10]{0:T(128)S(1)} %compare_select_fusion.6.where, bf16[8,32,512]{2,1,0:T(8,128)(2,1)S(1)} %collective-permute-done.6.refs_0_, bf16[8,32,512]{2,1,0:T(8,128)(2,1)S(1)} %collective-permute-done.13.refs_1_, ...), custom_call_target="tpu_custom_call" | custom-call | flops 1024 | bytes 1024 | tf_op jit(solution)/shard_map/pallas_call | solution.py:102
  43.7 3.2 %collective-permute-done.10.refs_1_ = bf16[8,32,512]{2,1,0:T(8,128)(2,1)S(1)} collective-permute-done((bf16[8,32,512]{2,1,0:T(8,128)(2,1)S(1)}, bf16[8,32,512]{2,1,0:T(8,128)(2,1)S(1)}, u32[]{:S(2)}, u32[]{:S(2)}) %collective-permute-start.10) | collective-permute-done | bytes 262176 | tf_op jit(solution)/shard_map/ppermute | solution.py:218
  46.8 2.4 %collective-permute-done.11.refs_0_ = bf16[8,32,512]{2,1,0:T(8,128)(2,1)S(1)} collective-permute-done((bf16[8,32,512]{2,1,0:T(8,128)(2,1)S(1)}, bf16[8,32,512]{2,1,0:T(8,128)(2,1)S(1)}, u32[]{:S(2)}, u32[]{:S(2)}) %collective-permute-start.11) | collective-permute-done | bytes 262176 | tf_op jit(solution)/shard_map/ppermute | solution.py:215
  49.2 1.5 %collective-permute-start.17 = (bf16[8,32,512]{2,1,0:T(8,128)(2,1)S(1)}, bf16[8,32,512]{2,1,0:T(8,128)(2,1)S(1)}, u32[]{:S(2)}, u32[]{:S(2)}) collective-permute-start(bf16[8,32,512]{2,1,0:T(8,128)(2,1)S(1)} %collective-permute-done.11.refs_0_), channel_id=1, source_target_pairs={{0,2},{2,0},{1,3},{3,1},{4,6},{6,4},{5,7},{7,5},{8,10},{10,8},{9,1... | collective-permute-start | bytes 786440 | tf_op jit(solution)/shard_map/ppermute | solution.py:218
  50.7 1.9 %collective-permute-start.14 = (bf16[8,16,512]{2,1,0:T(8,128)(2,1)S(1)}, bf16[8,16,512]{2,1,0:T(8,128)(2,1)S(1)}, u32[]{:S(2)}, u32[]{:S(2)}) collective-permute-start(bf16[8,16,512]{2,1,0:T(8,128)(2,1)S(1)} %get-tuple-element.98), channel_id=1, source_target_pairs={{0,12},{4,0},{8,4},{12,8},{1,13},{5,1},{9,5},{13,9},{2,14},{6,2},{... | collective-permute-start | bytes 393224 | tf_op jit(solution)/shard_map/ppermute | solution.py:215
  53.1 1.4 %shard_map.74 = (bf16[8,32,512]{2,1,0:T(8,128)(2,1)S(1)}, bf16[8,32,512]{2,1,0:T(8,128)(2,1)S(1)}) custom-call(s32[10]{0:T(128)S(1)} %compare_select_fusion.6.where, bf16[8,32,512]{2,1,0:T(8,128)(2,1)S(1)} %collective-permute-done.5.refs_0_, bf16[8,32,512]{2,1,0:T(8,128)(2,1)S(1)} %collective-permute-done.10.refs_1_, ...), custom_call_target="tpu_custom_call" | custom-call | flops 1024 | bytes 1024 | tf_op jit(solution)/shard_map/pallas_call | solution.py:102
  54.5 2.6 %collective-permute-done.17.refs_1_ = bf16[8,32,512]{2,1,0:T(8,128)(2,1)S(1)} collective-permute-done((bf16[8,32,512]{2,1,0:T(8,128)(2,1)S(1)}, bf16[8,32,512]{2,1,0:T(8,128)(2,1)S(1)}, u32[]{:S(2)}, u32[]{:S(2)}) %collective-permute-start.17) | collective-permute-done | bytes 262176 | tf_op jit(solution)/shard_map/ppermute | solution.py:218
  57.1 1.4 %shard_map.73 = (bf16[8,32,512]{2,1,0:T(8,128)(2,1)S(1)}, bf16[8,32,512]{2,1,0:T(8,128)(2,1)S(1)}) custom-call(s32[10]{0:T(128)S(1)} %compare_select_fusion.6.where, bf16[8,32,512]{2,1,0:T(8,128)(2,1)S(1)} %collective-permute-done.11.refs_0_, bf16[8,32,512]{2,1,0:T(8,128)(2,1)S(1)} %collective-permute-done.17.refs_1_, ...), custom_call_target="tpu_custom_call" | custom-call | flops 1024 | bytes 1024 | tf_op jit(solution)/shard_map/pallas_call | solution.py:102
  60.7 3.2 %collective-permute-done.16.refs_2_ = bf16[8,16,512]{2,1,0:T(8,128)(2,1)S(1)} collective-permute-done((bf16[8,16,512]{2,1,0:T(8,128)(2,1)S(1)}, bf16[8,16,512]{2,1,0:T(8,128)(2,1)S(1)}, u32[]{:S(2)}, u32[]{:S(2)}) %collective-permute-start.16) | collective-permute-done | bytes 131104 | tf_op jit(solution)/shard_map/ppermute | solution.py:215
  64.0 2.3 %collective-permute-done.18.came_ref = bf16[24,32,512]{2,1,0:T(8,128)(2,1)S(1)} collective-permute-done((bf16[24,32,512]{2,1,0:T(8,128)(2,1)S(1)}, bf16[24,32,512]{2,1,0:T(8,128)(2,1)S(1)}, u32[]{:S(2)}, u32[]{:S(2)}) %collective-permute-start.18) | collective-permute-done | bytes 786464 | tf_op jit(solution)/shard_map/ppermute | solution.py:262
  67.5 2.5 %collective-permute-start.21 = (bf16[8,32,512]{2,1,0:T(8,128)(2,1)S(1)}, bf16[8,32,512]{2,1,0:T(8,128)(2,1)S(1)}, u32[]{:S(2)}, u32[]{:S(2)}) collective-permute-start(bf16[8,32,512]{2,1,0:T(8,128)(2,1)S(1)} %get-tuple-element.116), channel_id=1, source_target_pairs={{0,12},{4,0},{8,4},{12,8},{1,13},{5,1},{9,5},{13,9},{2,14},{6,2},{... | collective-permute-start | bytes 786440 | tf_op jit(solution)/shard_map/ppermute | solution.py:215
  70.7 1.4 %shard_map.78.refs_2_ = bf16[8,4,48,512]{3,2,1,0:T(8,128)(2,1)} custom-call(s32[10]{0:T(128)S(1)} %compare_select_fusion.6.where, bf16[8,16,512]{2,1,0:T(8,128)(2,1)S(1)} %collective-permute-done.14.refs_0_, bf16[8,16,512]{2,1,0:T(8,128)(2,1)S(1)} %collective-permute-done.15.refs_1_, bf16[8,16,512]{2,1,0:T(8,128)(2,1)S(1)} %collective-permute-done.16.refs_2_, ...), custom_call_target="tpu_custom_call" | custom-call | flops 1024 | bytes 1024 | tf_op jit(solution)/shard_map/pallas_call | solution.py:190
  72.0 11.1 %collective-permute-done.21.refs_1_ = bf16[8,32,512]{2,1,0:T(8,128)(2,1)S(1)} collective-permute-done((bf16[8,32,512]{2,1,0:T(8,128)(2,1)S(1)}, bf16[8,32,512]{2,1,0:T(8,128)(2,1)S(1)}, u32[]{:S(2)}, u32[]{:S(2)}) %collective-permute-start.21) | collective-permute-done | bytes 262176 | tf_op jit(solution)/shard_map/ppermute | solution.py:215
  84.5 7.4 %collective-permute-done.20.refs_1_ = bf16[8,32,512]{2,1,0:T(8,128)(2,1)S(1)} collective-permute-done((bf16[8,32,512]{2,1,0:T(8,128)(2,1)S(1)}, bf16[8,32,512]{2,1,0:T(8,128)(2,1)S(1)}, u32[]{:S(2)}, u32[]{:S(2)}) %collective-permute-start.20) | collective-permute-done | bytes 262176 | tf_op jit(solution)/shard_map/ppermute | solution.py:215
  (52 shorter events, 21.8 us)
Async XLA Ops:
  0.0 11.0 %copy-start.2 = (bf16[1,32,24]{1,2,0:T(8,128)(2,1)S(1)}, bf16[1,32,24]{1,2,0:T(8,128)(2,1)}, u32[]{:S(2)}) copy-start(bf16[1,32,24]{1,2,0:T(8,128)(2,1)} %param.10) | copy-start | bytes 4612
  0.0 11.1 %copy-start = (s32[1,4,4]{2,1,0:T(4,128)S(1)}, s32[1,4,4]{2,1,0:T(4,128)}, u32[]{:S(2)}) copy-start(s32[1,4,4]{2,1,0:T(4,128)} %param.8) | copy-start | bytes 196
  1.1 17.2 %collective-permute-start = (bf16[8,16,512]{2,1,0:T(8,128)(2,1)S(1)}, bf16[8,16,512]{2,1,0:T(8,128)(2,1)S(1)}, u32[]{:S(2)}, u32[]{:S(2)}) collective-permute-start(bf16[8,16,512]{2,1,0:T(8,128)(2,1)S(1)} %get-tuple-element.128), channel_id=1, source_target_pairs={{0,4},{4,8},{8,12},{12,0},{1,5},{5,9},{9,13},{13,1},{2,6},{6,10},{... | collective-permute-start | bytes 393224 | tf_op jit(solution)/shard_map/ppermute | solution.py:215
  4.2 14.1 %collective-permute-start.1 = (bf16[8,16,512]{2,1,0:T(8,128)(2,1)S(1)}, bf16[8,16,512]{2,1,0:T(8,128)(2,1)S(1)}, u32[]{:S(2)}, u32[]{:S(2)}) collective-permute-start(bf16[8,16,512]{2,1,0:T(8,128)(2,1)S(1)} %get-tuple-element.127), channel_id=1, source_target_pairs={{0,12},{4,0},{8,4},{12,8},{1,13},{5,1},{9,5},{13,9},{2,14},{6,2},{... | collective-permute-start | bytes 393224 | tf_op jit(solution)/shard_map/ppermute | solution.py:215
  6.3 12.0 %collective-permute-start.2 = (bf16[8,16,512]{2,1,0:T(8,128)(2,1)S(1)}, bf16[8,16,512]{2,1,0:T(8,128)(2,1)S(1)}, u32[]{:S(2)}, u32[]{:S(2)}) collective-permute-start(bf16[8,16,512]{2,1,0:T(8,128)(2,1)S(1)} %get-tuple-element.126), channel_id=1, source_target_pairs={{0,8},{4,12},{8,0},{12,4},{1,9},{5,13},{9,1},{13,5},{2,10},{6,14},... | collective-permute-start | bytes 393224 | tf_op jit(solution)/shard_map/ppermute | solution.py:215
  8.3 10.1 %collective-permute-start.3 = (bf16[4,48,512]{2,1,0:T(8,128)(2,1)S(1)}, bf16[4,48,512]{2,1,0:T(8,128)(2,1)S(1)}, u32[]{:S(2)}, u32[]{:S(2)}) collective-permute-start(bf16[4,48,512]{2,1,0:T(8,128)(2,1)S(1)} %get-tuple-element.122.refs_0_), channel_id=1, source_target_pairs={{0,2},{2,0},{1,3},{3,1},{4,6},{6,4},{5,7},{7,5},{8,10},{10,8},{9,1... | collective-permute-start | bytes 589832 | tf_op jit(solution)/shard_map/ppermute | solution.py:218
  9.8 8.5 %collective-permute-start.4 = (bf16[4,48,512]{2,1,0:T(8,128)(2,1)S(1)}, bf16[4,48,512]{2,1,0:T(8,128)(2,1)S(1)}, u32[]{:S(2)}, u32[]{:S(2)}) collective-permute-start(bf16[4,48,512]{2,1,0:T(8,128)(2,1)S(1)} %get-tuple-element.121.refs_1_), channel_id=1, source_target_pairs={{0,2},{2,0},{1,3},{3,1},{4,6},{6,4},{5,7},{7,5},{8,10},{10,8},{9,1... | collective-permute-start | bytes 589832 | tf_op jit(solution)/shard_map/ppermute | solution.py:218
  18.3 14.0 %collective-permute-start.5 = (bf16[8,32,512]{2,1,0:T(8,128)(2,1)S(1)}, bf16[8,32,512]{2,1,0:T(8,128)(2,1)S(1)}, u32[]{:S(2)}, u32[]{:S(2)}) collective-permute-start(bf16[8,32,512]{2,1,0:T(8,128)(2,1)S(1)} %get-tuple-element.66), channel_id=1, source_target_pairs={{0,12},{4,0},{8,4},{12,8},{1,13},{5,1},{9,5},{13,9},{2,14},{6,2},{... | collective-permute-start | bytes 786440 | tf_op jit(solution)/shard_map/ppermute | solution.py:215
  19.8 12.6 %collective-permute-start.6 = (bf16[8,32,512]{2,1,0:T(8,128)(2,1)S(1)}, bf16[8,32,512]{2,1,0:T(8,128)(2,1)S(1)}, u32[]{:S(2)}, u32[]{:S(2)}) collective-permute-start(bf16[8,32,512]{2,1,0:T(8,128)(2,1)S(1)} %get-tuple-element.67), channel_id=1, source_target_pairs={{0,4},{4,8},{8,12},{12,0},{1,5},{5,9},{9,13},{13,1},{2,6},{6,10},{... | collective-permute-start | bytes 786440 | tf_op jit(solution)/shard_map/ppermute | solution.py:215
  20.4 6.4 %collective-permute-start.7 = (bf16[8,16,512]{2,1,0:T(8,128)(2,1)S(1)}, bf16[8,16,512]{2,1,0:T(8,128)(2,1)S(1)}, u32[]{:S(2)}, u32[]{:S(2)}) collective-permute-start(bf16[8,16,512]{2,1,0:T(8,128)(2,1)S(1)} %collective-permute-done.refs_0_), channel_id=1, source_target_pairs={{0,2},{2,0},{1,3},{3,1},{4,6},{6,4},{5,7},{7,5},{8,10},{10,8},{9,1... | collective-permute-start | bytes 393224 | tf_op jit(solution)/shard_map/ppermute | solution.py:218
  21.9 7.3 %collective-permute-start.8 = (bf16[8,16,512]{2,1,0:T(8,128)(2,1)S(1)}, bf16[8,16,512]{2,1,0:T(8,128)(2,1)S(1)}, u32[]{:S(2)}, u32[]{:S(2)}) collective-permute-start(bf16[8,16,512]{2,1,0:T(8,128)(2,1)S(1)} %collective-permute-done.2.refs_0_), channel_id=1, source_target_pairs={{0,2},{2,0},{1,3},{3,1},{4,6},{6,4},{5,7},{7,5},{8,10},{10,8},{9,1... | collective-permute-start | bytes 393224 | tf_op jit(solution)/shard_map/ppermute | solution.py:218
  22.4 8.2 %collective-permute-start.9 = (bf16[8,16,512]{2,1,0:T(8,128)(2,1)S(1)}, bf16[8,16,512]{2,1,0:T(8,128)(2,1)S(1)}, u32[]{:S(2)}, u32[]{:S(2)}) collective-permute-start(bf16[8,16,512]{2,1,0:T(8,128)(2,1)S(1)} %collective-permute-done.1.refs_0_), channel_id=1, source_target_pairs={{0,2},{2,0},{1,3},{3,1},{4,6},{6,4},{5,7},{7,5},{8,10},{10,8},{9,1... | collective-permute-start | bytes 393224 | tf_op jit(solution)/shard_map/ppermute | solution.py:218
  32.4 10.6 %collective-permute-start.12 = (bf16[24,16,512]{2,1,0:T(8,128)(2,1)S(1)}, bf16[24,16,512]{2,1,0:T(8,128)(2,1)S(1)}, u32[]{:S(2)}, u32[]{:S(2)}) collective-permute-start(bf16[24,16,512]{2,1,0:T(8,128)(2,1)S(1)} %shard_map.69), channel_id=1, source_target_pairs={{0,1},{1,0},{2,3},{3,2},{4,5},{5,4},{6,7},{7,6},{8,9},{9,8},{10,11... | collective-permute-start | bytes 1179656 | tf_op jit(solution)/shard_map/ppermute | solution.py:252
  32.5 9.2 %collective-permute-start.13 = (bf16[8,32,512]{2,1,0:T(8,128)(2,1)S(1)}, bf16[8,32,512]{2,1,0:T(8,128)(2,1)S(1)}, u32[]{:S(2)}, u32[]{:S(2)}) collective-permute-start(bf16[8,32,512]{2,1,0:T(8,128)(2,1)S(1)} %collective-permute-done.6.refs_0_), channel_id=1, source_target_pairs={{0,2},{2,0},{1,3},{3,1},{4,6},{6,4},{5,7},{7,5},{8,10},{10,8},{9,1... | collective-permute-start | bytes 786440 | tf_op jit(solution)/shard_map/ppermute | solution.py:218
  34.0 12.8 %collective-permute-start.10 = (bf16[8,32,512]{2,1,0:T(8,128)(2,1)S(1)}, bf16[8,32,512]{2,1,0:T(8,128)(2,1)S(1)}, u32[]{:S(2)}, u32[]{:S(2)}) collective-permute-start(bf16[8,32,512]{2,1,0:T(8,128)(2,1)S(1)} %collective-permute-done.5.refs_0_), channel_id=1, source_target_pairs={{0,2},{2,0},{1,3},{3,1},{4,6},{6,4},{5,7},{7,5},{8,10},{10,8},{9,1... | collective-permute-start | bytes 786440 | tf_op jit(solution)/shard_map/ppermute | solution.py:218
  34.6 14.6 %collective-permute-start.11 = (bf16[8,32,512]{2,1,0:T(8,128)(2,1)S(1)}, bf16[8,32,512]{2,1,0:T(8,128)(2,1)S(1)}, u32[]{:S(2)}, u32[]{:S(2)}) collective-permute-start(bf16[8,32,512]{2,1,0:T(8,128)(2,1)S(1)} %get-tuple-element.86), channel_id=1, source_target_pairs={{0,8},{4,12},{8,0},{12,4},{1,9},{5,13},{9,1},{13,5},{2,10},{6,14},... | collective-permute-start | bytes 786440 | tf_op jit(solution)/shard_map/ppermute | solution.py:215
  49.2 7.9 %collective-permute-start.17 = (bf16[8,32,512]{2,1,0:T(8,128)(2,1)S(1)}, bf16[8,32,512]{2,1,0:T(8,128)(2,1)S(1)}, u32[]{:S(2)}, u32[]{:S(2)}) collective-permute-start(bf16[8,32,512]{2,1,0:T(8,128)(2,1)S(1)} %collective-permute-done.11.refs_0_), channel_id=1, source_target_pairs={{0,2},{2,0},{1,3},{3,1},{4,6},{6,4},{5,7},{7,5},{8,10},{10,8},{9,1... | collective-permute-start | bytes 786440 | tf_op jit(solution)/shard_map/ppermute | solution.py:218
  50.7 9.7 %collective-permute-start.14 = (bf16[8,16,512]{2,1,0:T(8,128)(2,1)S(1)}, bf16[8,16,512]{2,1,0:T(8,128)(2,1)S(1)}, u32[]{:S(2)}, u32[]{:S(2)}) collective-permute-start(bf16[8,16,512]{2,1,0:T(8,128)(2,1)S(1)} %get-tuple-element.98), channel_id=1, source_target_pairs={{0,12},{4,0},{8,4},{12,8},{1,13},{5,1},{9,5},{13,9},{2,14},{6,2},{... | collective-permute-start | bytes 393224 | tf_op jit(solution)/shard_map/ppermute | solution.py:215
  52.5 8.2 %collective-permute-start.15 = (bf16[8,16,512]{2,1,0:T(8,128)(2,1)S(1)}, bf16[8,16,512]{2,1,0:T(8,128)(2,1)S(1)}, u32[]{:S(2)}, u32[]{:S(2)}) collective-permute-start(bf16[8,16,512]{2,1,0:T(8,128)(2,1)S(1)} %get-tuple-element.99), channel_id=1, source_target_pairs={{0,4},{4,8},{8,12},{12,0},{1,5},{5,9},{9,13},{13,1},{2,6},{6,10},{... | collective-permute-start | bytes 393224 | tf_op jit(solution)/shard_map/ppermute | solution.py:215
  52.7 11.3 %collective-permute-start.16 = (bf16[8,16,512]{2,1,0:T(8,128)(2,1)S(1)}, bf16[8,16,512]{2,1,0:T(8,128)(2,1)S(1)}, u32[]{:S(2)}, u32[]{:S(2)}) collective-permute-start(bf16[8,16,512]{2,1,0:T(8,128)(2,1)S(1)} %get-tuple-element.100), channel_id=1, source_target_pairs={{0,8},{4,12},{8,0},{12,4},{1,9},{5,13},{9,1},{13,5},{2,10},{6,14},... | collective-permute-start | bytes 393224 | tf_op jit(solution)/shard_map/ppermute | solution.py:215
  64.0 2.3 %collective-permute-start.18 = (bf16[24,32,512]{2,1,0:T(8,128)(2,1)S(1)}, bf16[24,32,512]{2,1,0:T(8,128)(2,1)S(1)}, u32[]{:S(2)}, u32[]{:S(2)}) collective-permute-start(bf16[24,32,512]{2,1,0:T(8,128)(2,1)S(1)} %shard_map.76), channel_id=1, source_target_pairs={{0,1},{1,0},{2,3},{3,2},{4,5},{5,4},{6,7},{7,6},{8,9},{9,8},{10,11... | collective-permute-start | bytes 2359304 | tf_op jit(solution)/shard_map/ppermute | solution.py:262
  67.5 15.6 %collective-permute-start.21 = (bf16[8,32,512]{2,1,0:T(8,128)(2,1)S(1)}, bf16[8,32,512]{2,1,0:T(8,128)(2,1)S(1)}, u32[]{:S(2)}, u32[]{:S(2)}) collective-permute-start(bf16[8,32,512]{2,1,0:T(8,128)(2,1)S(1)} %get-tuple-element.116), channel_id=1, source_target_pairs={{0,12},{4,0},{8,4},{12,8},{1,13},{5,1},{9,5},{13,9},{2,14},{6,2},{... | collective-permute-start | bytes 786440 | tf_op jit(solution)/shard_map/ppermute | solution.py:215
  70.0 14.5 %collective-permute-start.19 = (bf16[8,32,512]{2,1,0:T(8,128)(2,1)S(1)}, bf16[8,32,512]{2,1,0:T(8,128)(2,1)S(1)}, u32[]{:S(2)}, u32[]{:S(2)}) collective-permute-start(bf16[8,32,512]{2,1,0:T(8,128)(2,1)S(1)} %get-tuple-element.113), channel_id=1, source_target_pairs={{0,4},{4,8},{8,12},{12,0},{1,5},{5,9},{9,13},{13,1},{2,6},{6,10},{... | collective-permute-start | bytes 786440 | tf_op jit(solution)/shard_map/ppermute | solution.py:215
  70.0 21.9 %collective-permute-start.20 = (bf16[8,32,512]{2,1,0:T(8,128)(2,1)S(1)}, bf16[8,32,512]{2,1,0:T(8,128)(2,1)S(1)}, u32[]{:S(2)}, u32[]{:S(2)}) collective-permute-start(bf16[8,32,512]{2,1,0:T(8,128)(2,1)S(1)} %get-tuple-element.114), channel_id=1, source_target_pairs={{0,8},{4,12},{8,0},{12,4},{1,9},{5,13},{9,1},{13,5},{2,10},{6,14},... | collective-permute-start | bytes 786440 | tf_op jit(solution)/shard_map/ppermute | solution.py:215
  (2 other events, 10.6 us)

commit v10 on v8

--- a/solution.py
+++ b/solution.py
@@ -261,11 +261,13 @@
     (first[2], first[3], first[1]), first[0], kept, gone = fence(
         ((first[2], first[3], first[1]), first[0], kept, gone)
     )
+    result_a = [first[j] for j in (1, 2, 3, 0)], spots
+    spots = [(1, 0, freqs), (2, 0, half), (3, 0, half), (2, half, freqs), (3, half, freqs), (0, 0, freqs)]
     outs = fence(restore(kept, lax.ppermute(gone, "pol", other), ratios, up, spots))
-    back = [along_z(outs[j - 1], j) for j in (1, 2, 3)]
-    result = place(where, [first[j] for j in (1, 2, 3, 0)], spots, 0, shape)
-    result = place(where, [outs[3], back[0]], [spots[3], spots[0]], ROWS, shape, into=result)
-    return place(where, back[1:], spots[1:3], ROWS, shape, into=result)
+    back = [along_z(part, j) for part, (j, _, _) in zip(outs[:-1], spots)] + [outs[-1]]
+    result = place(where, *result_a, 0, shape)
+    result = place(where, [back[5], back[0]], [spots[5], spots[0]], ROWS, shape, into=result)
+    return place(where, back[1:5], spots[1:5], ROWS, shape, into=result)
 
 
 def plain(visibility, beam_transfer, tile_mask, first_block, eigen_modes, signal_noise):

time: 92.1 us -> 93.2 us (1.012)
  waiting for transfers between devices: 38.7 us -> 36.3 us
  starting transfers between devices: 24.9 us -> 27.3 us
    ppermute x12 -> x14, waiting for transfers between devices: 25.6 us -> 23.1 us  [along_z(): return lax.ppermute(value, 'fm', [(i, i ^ j) for i in range(parts)])]
    ppermute x12 -> x14, starting transfers between devices: 15.6 us -> 18 us  [along_z(): return lax.ppermute(value, 'fm', [(i, i ^ j) for i in range(parts)])]
  transfers between devices with their start and end apart: 22 -> 24, of which waited for: 10 -> 12; matrix products, arithmetic and copies ran while one was open for 1% -> 1% of each run, Pallas kernels for 24% -> 24%
where the time goes in v10:
time: 93.2 us; the launch traced here: 92.3 us
  waiting for transfers between devices  36.3 us (39%)
  starting transfers between devices  27.3 us (29%)
  Pallas kernels  25.4 us (27%)
  local copies, waits for them, and re-layouts  2.39 us (3%)
    ppermute x14, waiting for transfers between devices, along_z(): return lax.ppermute(value, 'fm', [(i, i ^ j) for i in range(parts)])  23.1 us
    ppermute x14, starting transfers between devices, along_z(): return lax.ppermute(value, 'fm', [(i, i ^ j) for i in range(parts)])  18 us
    ppermute x8, waiting for transfers between devices, along_x(): return lax.ppermute(value, 'kl', other)  10.9 us
    pallas_call x7, Pallas kernels, project(): pl.pallas_call(functools.partial(project_kernel, piece=piece, blocks=bloc...  9.56 us
    ppermute x8, starting transfers between devices, along_x(): return lax.ppermute(value, 'kl', other)  9.19 us
    pallas_call x1, Pallas kernels, hold(): pl.pallas_call(hold_kernel, grid_spec=pltpu.PrefetchScalarGridSpec(num_sc...  7.04 us
    pallas_call x3, Pallas kernels, place(): pl.pallas_call(functools.partial(place_kernel, spots=spots, first=first),...  4.07 us
    pallas_call x4, Pallas kernels, reduce(): pl.pallas_call(reduce_kernel, grid=(rows // ROWS,), in_specs=[fixed(modes...  2.62 us
  transfers between devices with their start and end apart: 24, of which 12 were waited for; matrix products, arithmetic and copies ran while one was open for 1% of the time, Pallas kernels for 24%

profile of v10, /device:TPU:12, one launch (start us, length us, event | category | flops | bytes accessed | tf_op | source)
XLA Modules:
  0.0 92.3 jit_solution(15981180381066901625)
XLA Ops:
  1.1 1.6 %collective-permute-start = (bf16[8,16,512]{2,1,0:T(8,128)(2,1)S(1)}, bf16[8,16,512]{2,1,0:T(8,128)(2,1)S(1)}, u32[]{:S(2)}, u32[]{:S(2)}) collective-permute-start(bf16[8,16,512]{2,1,0:T(8,128)(2,1)S(1)} %get-tuple-element.132), channel_id=1, source_target_pairs={{0,12},{4,8},{8,4},{12,0},{1,13},{5,9},{9,5},{13,1},{2,14},{6,10},... | collective-permute-start | bytes 393224 | tf_op jit(solution)/shard_map/ppermute | solution.py:215
  6.3 1.6 %collective-permute-start.3 = (bf16[4,48,512]{2,1,0:T(8,128)(2,1)S(1)}, bf16[4,48,512]{2,1,0:T(8,128)(2,1)S(1)}, u32[]{:S(2)}, u32[]{:S(2)}) collective-permute-start(bf16[4,48,512]{2,1,0:T(8,128)(2,1)S(1)} %get-tuple-element.126.refs_0_), channel_id=1, source_target_pairs={{0,2},{2,0},{1,3},{3,1},{4,6},{6,4},{5,7},{7,5},{8,10},{10,8},{9,1... | collective-permute-start | bytes 589832 | tf_op jit(solution)/shard_map/ppermute | solution.py:218
  9.1 7.0 %shard_map.64 = (bf16[32,512,512]{2,1,0:T(8,128)(2,1)S(1)}, bf16[384,512]{1,0:T(8,128)(2,1)S(1)}, bf16[512,384]{1,0:T(8,128)(2,1)S(1)}) custom-call(s32[6]{0:T(128)S(1)} %compare_select_fusion.1.where, s32[4,4]{1,0:T(4,128)S(1)} %bitcast.27, s32[1]{0:T(128)S(6)} %copy.16.starts, bf16[32,512,512]{2,1,0:T(8,128)(2,1)} %bitcast.28, bf16[32,24]{1,0:T(8,128)(2,1)S(1)} %bitcast.26), custom_call_target="tpu_custom_call" | custom-call | flops 1024 | bytes 1024 | tf_op jit(solution)/shard_map/pallas_call | solution.py:63
  16.6 2.7 %collective-permute-start.5 = (bf16[8,32,512]{2,1,0:T(8,128)(2,1)S(1)}, bf16[8,32,512]{2,1,0:T(8,128)(2,1)S(1)}, u32[]{:S(2)}, u32[]{:S(2)}) collective-permute-start(bf16[8,32,512]{2,1,0:T(8,128)(2,1)S(1)} %get-tuple-element.68), channel_id=1, source_target_pairs={{0,8},{4,12},{8,0},{12,4},{1,9},{5,13},{9,1},{13,5},{2,10},{6,14},... | collective-permute-start | bytes 786440 | tf_op jit(solution)/shard_map/ppermute | solution.py:215
  19.6 1.5 %collective-permute-start.7 = (bf16[8,16,512]{2,1,0:T(8,128)(2,1)S(1)}, bf16[8,16,512]{2,1,0:T(8,128)(2,1)S(1)}, u32[]{:S(2)}, u32[]{:S(2)}) collective-permute-start(bf16[8,16,512]{2,1,0:T(8,128)(2,1)S(1)} %collective-permute-done.2.refs_0_), channel_id=1, source_target_pairs={{0,2},{2,0},{1,3},{3,1},{4,6},{6,4},{5,7},{7,5},{8,10},{10,8},{9,1... | collective-permute-start | bytes 393224 | tf_op jit(solution)/shard_map/ppermute | solution.py:218
  21.6 1.5 %collective-permute-start.9 = (bf16[8,16,512]{2,1,0:T(8,128)(2,1)S(1)}, bf16[8,16,512]{2,1,0:T(8,128)(2,1)S(1)}, u32[]{:S(2)}, u32[]{:S(2)}) collective-permute-start(bf16[8,16,512]{2,1,0:T(8,128)(2,1)S(1)} %collective-permute-done.refs_0_), channel_id=1, source_target_pairs={{0,2},{2,0},{1,3},{3,1},{4,6},{6,4},{5,7},{7,5},{8,10},{10,8},{9,1... | collective-permute-start | bytes 393224 | tf_op jit(solution)/shard_map/ppermute | solution.py:218
  30.3 1.6 %collective-permute-start.13 = (bf16[8,32,512]{2,1,0:T(8,128)(2,1)S(1)}, bf16[8,32,512]{2,1,0:T(8,128)(2,1)S(1)}, u32[]{:S(2)}, u32[]{:S(2)}) collective-permute-start(bf16[8,32,512]{2,1,0:T(8,128)(2,1)S(1)} %collective-permute-done.6.refs_0_), channel_id=1, source_target_pairs={{0,2},{2,0},{1,3},{3,1},{4,6},{6,4},{5,7},{7,5},{8,10},{10,8},{9,1... | collective-permute-start | bytes 786440 | tf_op jit(solution)/shard_map/ppermute | solution.py:218
  33.4 6.1 %collective-permute-done.13.refs_1_ = bf16[8,32,512]{2,1,0:T(8,128)(2,1)S(1)} collective-permute-done((bf16[8,32,512]{2,1,0:T(8,128)(2,1)S(1)}, bf16[8,32,512]{2,1,0:T(8,128)(2,1)S(1)}, u32[]{:S(2)}, u32[]{:S(2)}) %collective-permute-start.13) | collective-permute-done | bytes 262176 | tf_op jit(solution)/shard_map/ppermute | solution.py:218
  39.5 1.4 %shard_map.72 = (bf16[8,32,512]{2,1,0:T(8,128)(2,1)S(1)}, bf16[8,32,512]{2,1,0:T(8,128)(2,1)S(1)}) custom-call(s32[6]{0:T(128)S(1)} %compare_select_fusion.1.where, bf16[8,32,512]{2,1,0:T(8,128)(2,1)S(1)} %collective-permute-done.6.refs_0_, bf16[8,32,512]{2,1,0:T(8,128)(2,1)S(1)} %collective-permute-done.13.refs_1_, ...), custom_call_target="tpu_custom_call" | custom-call | flops 1024 | bytes 1024 | tf_op jit(solution)/shard_map/pallas_call | solution.py:102
  41.5 3.2 %collective-permute-done.10.refs_1_ = bf16[8,32,512]{2,1,0:T(8,128)(2,1)S(1)} collective-permute-done((bf16[8,32,512]{2,1,0:T(8,128)(2,1)S(1)}, bf16[8,32,512]{2,1,0:T(8,128)(2,1)S(1)}, u32[]{:S(2)}, u32[]{:S(2)}) %collective-permute-start.10) | collective-permute-done | bytes 262176 | tf_op jit(solution)/shard_map/ppermute | solution.py:218
  44.7 1.5 %collective-permute-done.11.refs_0_ = bf16[8,32,512]{2,1,0:T(8,128)(2,1)S(1)} collective-permute-done((bf16[8,32,512]{2,1,0:T(8,128)(2,1)S(1)}, bf16[8,32,512]{2,1,0:T(8,128)(2,1)S(1)}, u32[]{:S(2)}, u32[]{:S(2)}) %collective-permute-start.11) | collective-permute-done | bytes 262176 | tf_op jit(solution)/shard_map/ppermute | solution.py:215
  46.1 1.5 %collective-permute-start.17 = (bf16[8,32,512]{2,1,0:T(8,128)(2,1)S(1)}, bf16[8,32,512]{2,1,0:T(8,128)(2,1)S(1)}, u32[]{:S(2)}, u32[]{:S(2)}) collective-permute-start(bf16[8,32,512]{2,1,0:T(8,128)(2,1)S(1)} %collective-permute-done.11.refs_0_), channel_id=1, source_target_pairs={{0,2},{2,0},{1,3},{3,1},{4,6},{6,4},{5,7},{7,5},{8,10},{10,8},{9,1... | collective-permute-start | bytes 786440 | tf_op jit(solution)/shard_map/ppermute | solution.py:218
  49.4 2.6 %collective-permute-start.16 = (bf16[8,16,512]{2,1,0:T(8,128)(2,1)S(1)}, bf16[8,16,512]{2,1,0:T(8,128)(2,1)S(1)}, u32[]{:S(2)}, u32[]{:S(2)}) collective-permute-start(bf16[8,16,512]{2,1,0:T(8,128)(2,1)S(1)} %get-tuple-element.102), channel_id=1, source_target_pairs={{0,4},{4,0},{8,12},{12,8},{1,5},{5,1},{9,13},{13,9},{2,6},{6,2},{1... | collective-permute-start | bytes 393224 | tf_op jit(solution)/shard_map/ppermute | solution.py:215
  52.0 1.4 %shard_map.73 = (bf16[8,32,512]{2,1,0:T(8,128)(2,1)S(1)}, bf16[8,32,512]{2,1,0:T(8,128)(2,1)S(1)}) custom-call(s32[6]{0:T(128)S(1)} %compare_select_fusion.1.where, bf16[8,32,512]{2,1,0:T(8,128)(2,1)S(1)} %collective-permute-done.5.refs_0_, bf16[8,32,512]{2,1,0:T(8,128)(2,1)S(1)} %collective-permute-done.10.refs_1_, ...), custom_call_target="tpu_custom_call" | custom-call | flops 1024 | bytes 1024 | tf_op jit(solution)/shard_map/pallas_call | solution.py:102
  53.4 1.4 %shard_map.74 = (bf16[8,32,512]{2,1,0:T(8,128)(2,1)S(1)}, bf16[8,32,512]{2,1,0:T(8,128)(2,1)S(1)}) custom-call(s32[6]{0:T(128)S(1)} %compare_select_fusion.1.where, bf16[8,32,512]{2,1,0:T(8,128)(2,1)S(1)} %collective-permute-done.11.refs_0_, bf16[8,32,512]{2,1,0:T(8,128)(2,1)S(1)} %collective-permute-done.17.refs_1_, ...), custom_call_target="tpu_custom_call" | custom-call | flops 1024 | bytes 1024 | tf_op jit(solution)/shard_map/pallas_call | solution.py:102
  56.7 3.8 %collective-permute-done.15.refs_2_ = bf16[8,16,512]{2,1,0:T(8,128)(2,1)S(1)} collective-permute-done((bf16[8,16,512]{2,1,0:T(8,128)(2,1)S(1)}, bf16[8,16,512]{2,1,0:T(8,128)(2,1)S(1)}, u32[]{:S(2)}, u32[]{:S(2)}) %collective-permute-start.15) | collective-permute-done | bytes 131104 | tf_op jit(solution)/shard_map/ppermute | solution.py:215
  60.6 2.3 %collective-permute-done.18.came_ref = bf16[24,32,512]{2,1,0:T(8,128)(2,1)S(1)} collective-permute-done((bf16[24,32,512]{2,1,0:T(8,128)(2,1)S(1)}, bf16[24,32,512]{2,1,0:T(8,128)(2,1)S(1)}, u32[]{:S(2)}, u32[]{:S(2)}) %collective-permute-start.18) | collective-permute-done | bytes 786464 | tf_op jit(solution)/shard_map/ppermute | solution.py:266
  62.9 1.6 %shard_map.77 = (bf16[8,32,512]{2,1,0:T(8,128)(2,1)S(1)}, bf16[4,32,512]{2,1,0:T(8,128)(2,1)S(1)}, bf16[4,32,512]{2,1,0:T(8,128)(2,1)S(1)}, bf16[4,32,512]{2,1,0...) custom-call(bf16[512,384]{1,0:T(8,128)(2,1)S(1)} %get-tuple-element.67.up_ref, ...), custom_call_target="tpu_custom_call" | custom-call | flops 1024 | bytes 1024 | tf_op jit(solution)/shard_map/pallas_call | solution.py:161
  64.5 2.2 %collective-permute-start.19 = (bf16[4,32,512]{2,1,0:T(8,128)(2,1)S(1)}, bf16[4,32,512]{2,1,0:T(8,128)(2,1)S(1)}, u32[]{:S(2)}, u32[]{:S(2)}) collective-permute-start(bf16[4,32,512]{2,1,0:T(8,128)(2,1)S(1)} %get-tuple-element.115), channel_id=1, source_target_pairs={{0,8},{4,12},{8,0},{12,4},{1,9},{5,13},{9,1},{13,5},{2,10},{6,14},... | collective-permute-start | bytes 393224 | tf_op jit(solution)/shard_map/ppermute | solution.py:215
  71.8 1.9 %collective-permute-done.23.refs_1_ = bf16[8,32,512]{2,1,0:T(8,128)(2,1)S(1)} collective-permute-done((bf16[8,32,512]{2,1,0:T(8,128)(2,1)S(1)}, bf16[8,32,512]{2,1,0:T(8,128)(2,1)S(1)}, u32[]{:S(2)}, u32[]{:S(2)}) %collective-permute-start.23) | collective-permute-done | bytes 262176 | tf_op jit(solution)/shard_map/ppermute | solution.py:215
  75.0 1.7 %collective-permute-done.19.refs_0_ = bf16[4,32,512]{2,1,0:T(8,128)(2,1)S(1)} collective-permute-done((bf16[4,32,512]{2,1,0:T(8,128)(2,1)S(1)}, bf16[4,32,512]{2,1,0:T(8,128)(2,1)S(1)}, u32[]{:S(2)}, u32[]{:S(2)}) %collective-permute-start.19) | collective-permute-done | bytes 131104 | tf_op jit(solution)/shard_map/ppermute | solution.py:215
  76.7 9.7 %collective-permute-done.20.refs_1_ = bf16[4,32,512]{2,1,0:T(8,128)(2,1)S(1)} collective-permute-done((bf16[4,32,512]{2,1,0:T(8,128)(2,1)S(1)}, bf16[4,32,512]{2,1,0:T(8,128)(2,1)S(1)}, u32[]{:S(2)}, u32[]{:S(2)}) %collective-permute-start.20) | collective-permute-done | bytes 131104 | tf_op jit(solution)/shard_map/ppermute | solution.py:215
  87.4 3.5 %collective-permute-done.22.refs_3_ = bf16[4,32,512]{2,1,0:T(8,128)(2,1)S(1)} collective-permute-done((bf16[4,32,512]{2,1,0:T(8,128)(2,1)S(1)}, bf16[4,32,512]{2,1,0:T(8,128)(2,1)S(1)}, u32[]{:S(2)}, u32[]{:S(2)}) %collective-permute-start.22) | collective-permute-done | bytes 131104 | tf_op jit(solution)/shard_map/ppermute | solution.py:215
  90.9 1.4 %shard_map.80 = bf16[8,4,48,512]{3,2,1,0:T(8,128)(2,1)} custom-call(s32[6]{0:T(128)S(1)} %compare_select_fusion.1.where, bf16[4,32,512]{2,1,0:T(8,128)(2,1)S(1)} %collective-permute-done.19.refs_0_, bf16[4,32,512]{2,1,0:T(8,128)(2,1)S(1)} %collective-permute-done.20.refs_1_, ...), custom_call_target="tpu_custom_call", output_to_operand_aliasing={{}: (5, {})} | custom-call | flops 1024 | bytes 1024 | tf_op jit(solution)/shard_map/pallas_call | solution.py:190
  (56 shorter events, 27.0 us)
Async XLA Ops:
  1.1 15.2 %collective-permute-start = (bf16[8,16,512]{2,1,0:T(8,128)(2,1)S(1)}, bf16[8,16,512]{2,1,0:T(8,128)(2,1)S(1)}, u32[]{:S(2)}, u32[]{:S(2)}) collective-permute-start(bf16[8,16,512]{2,1,0:T(8,128)(2,1)S(1)} %get-tuple-element.132), channel_id=1, source_target_pairs={{0,12},{4,8},{8,4},{12,0},{1,13},{5,9},{9,5},{13,1},{2,14},{6,10},... | collective-permute-start | bytes 393224 | tf_op jit(solution)/shard_map/ppermute | solution.py:215
  2.7 13.5 %collective-permute-start.1 = (bf16[8,16,512]{2,1,0:T(8,128)(2,1)S(1)}, bf16[8,16,512]{2,1,0:T(8,128)(2,1)S(1)}, u32[]{:S(2)}, u32[]{:S(2)}) collective-permute-start(bf16[8,16,512]{2,1,0:T(8,128)(2,1)S(1)} %get-tuple-element.131), channel_id=1, source_target_pairs={{0,8},{4,12},{8,0},{12,4},{1,9},{5,13},{9,1},{13,5},{2,10},{6,14},... | collective-permute-start | bytes 393224 | tf_op jit(solution)/shard_map/ppermute | solution.py:215
  4.0 12.3 %collective-permute-start.2 = (bf16[8,16,512]{2,1,0:T(8,128)(2,1)S(1)}, bf16[8,16,512]{2,1,0:T(8,128)(2,1)S(1)}, u32[]{:S(2)}, u32[]{:S(2)}) collective-permute-start(bf16[8,16,512]{2,1,0:T(8,128)(2,1)S(1)} %get-tuple-element.130), channel_id=1, source_target_pairs={{0,4},{4,0},{8,12},{12,8},{1,5},{5,1},{9,13},{13,9},{2,6},{6,2},{1... | collective-permute-start | bytes 393224 | tf_op jit(solution)/shard_map/ppermute | solution.py:215
  6.3 10.0 %collective-permute-start.3 = (bf16[4,48,512]{2,1,0:T(8,128)(2,1)S(1)}, bf16[4,48,512]{2,1,0:T(8,128)(2,1)S(1)}, u32[]{:S(2)}, u32[]{:S(2)}) collective-permute-start(bf16[4,48,512]{2,1,0:T(8,128)(2,1)S(1)} %get-tuple-element.126.refs_0_), channel_id=1, source_target_pairs={{0,2},{2,0},{1,3},{3,1},{4,6},{6,4},{5,7},{7,5},{8,10},{10,8},{9,1... | collective-permute-start | bytes 589832 | tf_op jit(solution)/shard_map/ppermute | solution.py:218
  7.8 8.8 %collective-permute-start.4 = (bf16[4,48,512]{2,1,0:T(8,128)(2,1)S(1)}, bf16[4,48,512]{2,1,0:T(8,128)(2,1)S(1)}, u32[]{:S(2)}, u32[]{:S(2)}) collective-permute-start(bf16[4,48,512]{2,1,0:T(8,128)(2,1)S(1)} %get-tuple-element.125.refs_1_), channel_id=1, source_target_pairs={{0,2},{2,0},{1,3},{3,1},{4,6},{6,4},{5,7},{7,5},{8,10},{10,8},{9,1... | collective-permute-start | bytes 589832 | tf_op jit(solution)/shard_map/ppermute | solution.py:218
  16.6 13.6 %collective-permute-start.5 = (bf16[8,32,512]{2,1,0:T(8,128)(2,1)S(1)}, bf16[8,32,512]{2,1,0:T(8,128)(2,1)S(1)}, u32[]{:S(2)}, u32[]{:S(2)}) collective-permute-start(bf16[8,32,512]{2,1,0:T(8,128)(2,1)S(1)} %get-tuple-element.68), channel_id=1, source_target_pairs={{0,8},{4,12},{8,0},{12,4},{1,9},{5,13},{9,1},{13,5},{2,10},{6,14},... | collective-permute-start | bytes 786440 | tf_op jit(solution)/shard_map/ppermute | solution.py:215
  19.3 10.9 %collective-permute-start.6 = (bf16[8,32,512]{2,1,0:T(8,128)(2,1)S(1)}, bf16[8,32,512]{2,1,0:T(8,128)(2,1)S(1)}, u32[]{:S(2)}, u32[]{:S(2)}) collective-permute-start(bf16[8,32,512]{2,1,0:T(8,128)(2,1)S(1)} %get-tuple-element.69), channel_id=1, source_target_pairs={{0,4},{4,0},{8,12},{12,8},{1,5},{5,1},{9,13},{13,9},{2,6},{6,2},{1... | collective-permute-start | bytes 786440 | tf_op jit(solution)/shard_map/ppermute | solution.py:215
  19.6 6.1 %collective-permute-start.7 = (bf16[8,16,512]{2,1,0:T(8,128)(2,1)S(1)}, bf16[8,16,512]{2,1,0:T(8,128)(2,1)S(1)}, u32[]{:S(2)}, u32[]{:S(2)}) collective-permute-start(bf16[8,16,512]{2,1,0:T(8,128)(2,1)S(1)} %collective-permute-done.2.refs_0_), channel_id=1, source_target_pairs={{0,2},{2,0},{1,3},{3,1},{4,6},{6,4},{5,7},{7,5},{8,10},{10,8},{9,1... | collective-permute-start | bytes 393224 | tf_op jit(solution)/shard_map/ppermute | solution.py:218
  21.0 6.0 %collective-permute-start.8 = (bf16[8,16,512]{2,1,0:T(8,128)(2,1)S(1)}, bf16[8,16,512]{2,1,0:T(8,128)(2,1)S(1)}, u32[]{:S(2)}, u32[]{:S(2)}) collective-permute-start(bf16[8,16,512]{2,1,0:T(8,128)(2,1)S(1)} %collective-permute-done.1.refs_0_), channel_id=1, source_target_pairs={{0,2},{2,0},{1,3},{3,1},{4,6},{6,4},{5,7},{7,5},{8,10},{10,8},{9,1... | collective-permute-start | bytes 393224 | tf_op jit(solution)/shard_map/ppermute | solution.py:218
  21.6 6.9 %collective-permute-start.9 = (bf16[8,16,512]{2,1,0:T(8,128)(2,1)S(1)}, bf16[8,16,512]{2,1,0:T(8,128)(2,1)S(1)}, u32[]{:S(2)}, u32[]{:S(2)}) collective-permute-start(bf16[8,16,512]{2,1,0:T(8,128)(2,1)S(1)} %collective-permute-done.refs_0_), channel_id=1, source_target_pairs={{0,2},{2,0},{1,3},{3,1},{4,6},{6,4},{5,7},{7,5},{8,10},{10,8},{9,1... | collective-permute-start | bytes 393224 | tf_op jit(solution)/shard_map/ppermute | solution.py:218
  30.3 10.6 %collective-permute-start.12 = (bf16[24,16,512]{2,1,0:T(8,128)(2,1)S(1)}, bf16[24,16,512]{2,1,0:T(8,128)(2,1)S(1)}, u32[]{:S(2)}, u32[]{:S(2)}) collective-permute-start(bf16[24,16,512]{2,1,0:T(8,128)(2,1)S(1)} %shard_map.69), channel_id=1, source_target_pairs={{0,1},{1,0},{2,3},{3,2},{4,5},{5,4},{6,7},{7,6},{8,9},{9,8},{10,11... | collective-permute-start | bytes 1179656 | tf_op jit(solution)/shard_map/ppermute | solution.py:252
  30.3 9.2 %collective-permute-start.13 = (bf16[8,32,512]{2,1,0:T(8,128)(2,1)S(1)}, bf16[8,32,512]{2,1,0:T(8,128)(2,1)S(1)}, u32[]{:S(2)}, u32[]{:S(2)}) collective-permute-start(bf16[8,32,512]{2,1,0:T(8,128)(2,1)S(1)} %collective-permute-done.6.refs_0_), channel_id=1, source_target_pairs={{0,2},{2,0},{1,3},{3,1},{4,6},{6,4},{5,7},{7,5},{8,10},{10,8},{9,1... | collective-permute-start | bytes 786440 | tf_op jit(solution)/shard_map/ppermute | solution.py:218
  31.9 12.8 %collective-permute-start.10 = (bf16[8,32,512]{2,1,0:T(8,128)(2,1)S(1)}, bf16[8,32,512]{2,1,0:T(8,128)(2,1)S(1)}, u32[]{:S(2)}, u32[]{:S(2)}) collective-permute-start(bf16[8,32,512]{2,1,0:T(8,128)(2,1)S(1)} %collective-permute-done.5.refs_0_), channel_id=1, source_target_pairs={{0,2},{2,0},{1,3},{3,1},{4,6},{6,4},{5,7},{7,5},{8,10},{10,8},{9,1... | collective-permute-start | bytes 786440 | tf_op jit(solution)/shard_map/ppermute | solution.py:218
  32.4 13.7 %collective-permute-start.11 = (bf16[8,32,512]{2,1,0:T(8,128)(2,1)S(1)}, bf16[8,32,512]{2,1,0:T(8,128)(2,1)S(1)}, u32[]{:S(2)}, u32[]{:S(2)}) collective-permute-start(bf16[8,32,512]{2,1,0:T(8,128)(2,1)S(1)} %get-tuple-element.88), channel_id=1, source_target_pairs={{0,12},{4,8},{8,4},{12,0},{1,13},{5,9},{9,5},{13,1},{2,14},{6,10},... | collective-permute-start | bytes 786440 | tf_op jit(solution)/shard_map/ppermute | solution.py:215
  46.1 7.3 %collective-permute-start.17 = (bf16[8,32,512]{2,1,0:T(8,128)(2,1)S(1)}, bf16[8,32,512]{2,1,0:T(8,128)(2,1)S(1)}, u32[]{:S(2)}, u32[]{:S(2)}) collective-permute-start(bf16[8,32,512]{2,1,0:T(8,128)(2,1)S(1)} %collective-permute-done.11.refs_0_), channel_id=1, source_target_pairs={{0,2},{2,0},{1,3},{3,1},{4,6},{6,4},{5,7},{7,5},{8,10},{10,8},{9,1... | collective-permute-start | bytes 786440 | tf_op jit(solution)/shard_map/ppermute | solution.py:218
  47.6 9.1 %collective-permute-start.14 = (bf16[8,16,512]{2,1,0:T(8,128)(2,1)S(1)}, bf16[8,16,512]{2,1,0:T(8,128)(2,1)S(1)}, u32[]{:S(2)}, u32[]{:S(2)}) collective-permute-start(bf16[8,16,512]{2,1,0:T(8,128)(2,1)S(1)} %get-tuple-element.100), channel_id=1, source_target_pairs={{0,8},{4,12},{8,0},{12,4},{1,9},{5,13},{9,1},{13,5},{2,10},{6,14},... | collective-permute-start | bytes 393224 | tf_op jit(solution)/shard_map/ppermute | solution.py:215
  48.0 12.5 %collective-permute-start.15 = (bf16[8,16,512]{2,1,0:T(8,128)(2,1)S(1)}, bf16[8,16,512]{2,1,0:T(8,128)(2,1)S(1)}, u32[]{:S(2)}, u32[]{:S(2)}) collective-permute-start(bf16[8,16,512]{2,1,0:T(8,128)(2,1)S(1)} %get-tuple-element.101), channel_id=1, source_target_pairs={{0,12},{4,8},{8,4},{12,0},{1,13},{5,9},{9,5},{13,1},{2,14},{6,10},... | collective-permute-start | bytes 393224 | tf_op jit(solution)/shard_map/ppermute | solution.py:215
  49.4 11.2 %collective-permute-start.16 = (bf16[8,16,512]{2,1,0:T(8,128)(2,1)S(1)}, bf16[8,16,512]{2,1,0:T(8,128)(2,1)S(1)}, u32[]{:S(2)}, u32[]{:S(2)}) collective-permute-start(bf16[8,16,512]{2,1,0:T(8,128)(2,1)S(1)} %get-tuple-element.102), channel_id=1, source_target_pairs={{0,4},{4,0},{8,12},{12,8},{1,5},{5,1},{9,13},{13,9},{2,6},{6,2},{1... | collective-permute-start | bytes 393224 | tf_op jit(solution)/shard_map/ppermute | solution.py:215
  60.6 2.3 %collective-permute-start.18 = (bf16[24,32,512]{2,1,0:T(8,128)(2,1)S(1)}, bf16[24,32,512]{2,1,0:T(8,128)(2,1)S(1)}, u32[]{:S(2)}, u32[]{:S(2)}) collective-permute-start(bf16[24,32,512]{2,1,0:T(8,128)(2,1)S(1)} %shard_map.76), channel_id=1, source_target_pairs={{0,1},{1,0},{2,3},{3,2},{4,5},{5,4},{6,7},{7,6},{8,9},{9,8},{10,11... | collective-permute-start | bytes 2359304 | tf_op jit(solution)/shard_map/ppermute | solution.py:266
  64.4 9.2 %collective-permute-start.23 = (bf16[8,32,512]{2,1,0:T(8,128)(2,1)S(1)}, bf16[8,32,512]{2,1,0:T(8,128)(2,1)S(1)}, u32[]{:S(2)}, u32[]{:S(2)}) collective-permute-start(bf16[8,32,512]{2,1,0:T(8,128)(2,1)S(1)} %get-tuple-element.120), channel_id=1, source_target_pairs={{0,4},{4,0},{8,12},{12,8},{1,5},{5,1},{9,13},{13,9},{2,6},{6,2},{1... | collective-permute-start | bytes 786440 | tf_op jit(solution)/shard_map/ppermute | solution.py:215
  64.5 12.2 %collective-permute-start.19 = (bf16[4,32,512]{2,1,0:T(8,128)(2,1)S(1)}, bf16[4,32,512]{2,1,0:T(8,128)(2,1)S(1)}, u32[]{:S(2)}, u32[]{:S(2)}) collective-permute-start(bf16[4,32,512]{2,1,0:T(8,128)(2,1)S(1)} %get-tuple-element.115), channel_id=1, source_target_pairs={{0,8},{4,12},{8,0},{12,4},{1,9},{5,13},{9,1},{13,5},{2,10},{6,14},... | collective-permute-start | bytes 393224 | tf_op jit(solution)/shard_map/ppermute | solution.py:215
  66.7 19.7 %collective-permute-start.20 = (bf16[4,32,512]{2,1,0:T(8,128)(2,1)S(1)}, bf16[4,32,512]{2,1,0:T(8,128)(2,1)S(1)}, u32[]{:S(2)}, u32[]{:S(2)}) collective-permute-start(bf16[4,32,512]{2,1,0:T(8,128)(2,1)S(1)} %get-tuple-element.116), channel_id=1, source_target_pairs={{0,12},{4,8},{8,4},{12,0},{1,13},{5,9},{9,5},{13,1},{2,14},{6,10},... | collective-permute-start | bytes 393224 | tf_op jit(solution)/shard_map/ppermute | solution.py:215
  68.0 19.4 %collective-permute-start.21 = (bf16[4,32,512]{2,1,0:T(8,128)(2,1)S(1)}, bf16[4,32,512]{2,1,0:T(8,128)(2,1)S(1)}, u32[]{:S(2)}, u32[]{:S(2)}) collective-permute-start(bf16[4,32,512]{2,1,0:T(8,128)(2,1)S(1)} %get-tuple-element.117), channel_id=1, source_target_pairs={{0,8},{4,12},{8,0},{12,4},{1,9},{5,13},{9,1},{13,5},{2,10},{6,14},... | collective-permute-start | bytes 393224 | tf_op jit(solution)/shard_map/ppermute | solution.py:215
  69.1 21.8 %collective-permute-start.22 = (bf16[4,32,512]{2,1,0:T(8,128)(2,1)S(1)}, bf16[4,32,512]{2,1,0:T(8,128)(2,1)S(1)}, u32[]{:S(2)}, u32[]{:S(2)}) collective-permute-start(bf16[4,32,512]{2,1,0:T(8,128)(2,1)S(1)} %get-tuple-element.118), channel_id=1, source_target_pairs={{0,12},{4,8},{8,4},{12,0},{1,13},{5,9},{9,5},{13,1},{2,14},{6,10},... | collective-permute-start | bytes 393224 | tf_op jit(solution)/shard_map/ppermute | solution.py:215
  (4 other events, 28.4 us)

commit v11 on v8

--- a/solution.py
+++ b/solution.py
@@ -95,7 +95,7 @@
         leave_ref[f] = value[rows:]
 
 
-def project(where, mine, others, held, piece, blocks):
+def project(where, mine, others, held, piece, blocks, flops=1024):
     ell = held.shape[2]
     rows = sum(mine[n].shape[1] for n, _ in blocks[0])
     vmem = pl.BlockSpec(memory_space=pltpu.VMEM)
@@ -106,7 +106,7 @@
         ),
         out_shape=[jax.ShapeDtypeStruct((len(blocks), rows, ell), jnp.bfloat16)] * 2,
         compiler_params=pltpu.CompilerParams(vmem_limit_bytes=VMEM_LIMIT),
-        cost_estimate=pl.CostEstimate(flops=1024, bytes_accessed=1024, transcendentals=0),
+        cost_estimate=pl.CostEstimate(flops=flops, bytes_accessed=1024, transcendentals=0),
     )(where, *mine, *others, pltpu.with_memory_space_constraint(held, pltpu.VMEM))
 
 
@@ -203,6 +203,22 @@
     )(where, *pieces, *extra)
 
 
+def anchor_kernel(*refs):
+    del refs
+
+
+def anchor(values, flops):
+    anywhere = pl.BlockSpec(memory_space=pl.ANY)
+    return pl.pallas_call(
+        anchor_kernel,
+        in_specs=[anywhere] * len(values),
+        out_specs=[anywhere] * len(values),
+        out_shape=[jax.ShapeDtypeStruct(value.shape, value.dtype) for value in values],
+        input_output_aliases={n: n for n in range(len(values))},
+        cost_estimate=pl.CostEstimate(flops=flops, bytes_accessed=1024, transcendentals=0),
+    )(*values)
+
+
 def staged(visibility, beam_transfer, tile_mask, first_block, eigen_modes, signal_noise):
     freqs, parts, rows_all, base = visibility.shape
     _, freq_total, _, ell = beam_transfer.shape
@@ -236,17 +252,17 @@
     a = {j: along_z(cut(j, 0, ROWS), j) for j in (3, 2, 1)}
     mine = [cut(0, 0, rows_all)[n:n + half] for n in (0, half)]
     others = [along_x(part) for part in mine]
-    b = {j: cut(j, ROWS, most) for j in (1, 2, 3)}
+    b, far = {j: cut(j, ROWS, most) for j in (1, 2)}, cut(3, ROWS, most)
     held, down, up = hold(where, tile_mask[0], first_block, beam, eigen_modes[0])
     (a[3], a[2], a[1]), b, others, down, up = fence(((a[3], a[2], a[1]), b, others, down, up))
     b[1], b[2] = along_z(b[1], 1), along_z(b[2], 2)
-    own = project(where, mine, others, held, 0, halves)
-    skies = [own] + [project(where, [a[j]], [along_x(a[j])], held, j, blocks) for j in (1, 2, 3)]
+    own = project(where, mine, others, held, 0, halves, 200_000_000)
+    skies = [own] + [project(where, [a[j]], [along_x(a[j])], held, j, blocks, 200_000_000) for j in (1, 2, 3)]
     gone = reduce(down, [leave for _, leave in skies], (0, 0, 0, 0), n_modes)
     stay_a = [stay for stay, _ in skies]
-    (b[2], b[1]), b[3], stay_a, gone = fence(((b[2], b[1]), b[3], stay_a, gone))
-    x_2, x_1 = along_x(b[2]), along_x(b[1])
-    b[3] = along_z(b[3], 3)
+    b[2], stay_a, gone = fence((b[2], stay_a, gone))
+    x_2 = along_x(b[2])
+    x_1, b[3] = anchor([along_x(b[1]), along_z(far, 3)], 1_500_000_000)
     kept = reduce(down, stay_a, (0, 0, 0, 0), n_modes, jnp.float32)
     spots = [(j, 0, freqs) for j in (1, 2, 3, 0)]
     outs = restore(kept, lax.ppermute(gone, "pol", other), ratios, up, spots)

time: 92.1 us -> 98.7 us (1.072)
  local copies, waits for them, and re-layouts: 2.39 us -> 9.14 us
  waiting for transfers between devices: 38.7 us -> 34.3 us
  Pallas kernels: 25.1 us -> 28 us
    ppermute x8, waiting for transfers between devices: 10.9 us -> 1.12 us  [along_x(): return lax.ppermute(value, 'kl', other)]
    unnamed x9 -> x19, local copies, waits for them, and re-layouts: 0.1 us -> 6.85 us
    ppermute x12, waiting for transfers between devices: 25.6 us -> 30.9 us  [along_z(): return lax.ppermute(value, 'fm', [(i, i ^ j) for i in range(parts)])]
    pallas_call x7, Pallas kernels: 9.56 us -> 12.7 us  [project(): pl.pallas_call(functools.partial(project_kernel, piece=piece, blocks=bloc...]
    ppermute x8, starting transfers between devices: 9.19 us -> 10.2 us  [along_x(): return lax.ppermute(value, 'kl', other)]
  transfers between devices with their start and end apart: 22 -> 22, of which waited for: 10 -> 10; matrix products, arithmetic and copies ran while one was open for 1% -> 1% of each run, Pallas kernels for 24% -> 26%
where the time goes in v11:
time: 98.7 us; the launch traced here: 97.8 us
  waiting for transfers between devices  34.3 us (35%)
  Pallas kernels  28 us (28%)
  starting transfers between devices  25.4 us (26%)
  local copies, waits for them, and re-layouts  9.14 us (9%)
    ppermute x12, waiting for transfers between devices, along_z(): return lax.ppermute(value, 'fm', [(i, i ^ j) for i in range(parts)])  30.9 us
    ppermute x12, starting transfers between devices, along_z(): return lax.ppermute(value, 'fm', [(i, i ^ j) for i in range(parts)])  15.2 us
    pallas_call x7, Pallas kernels, project(): pl.pallas_call(functools.partial(project_kernel, piece=piece, blocks=bloc...  12.7 us
    ppermute x8, starting transfers between devices, along_x(): return lax.ppermute(value, 'kl', other)  10.2 us
    pallas_call x1, Pallas kernels, hold(): pl.pallas_call(hold_kernel, grid_spec=pltpu.PrefetchScalarGridSpec(num_sc...  7.04 us
    unnamed x19, local copies, waits for them, and re-layouts  6.85 us
    pallas_call x3, Pallas kernels, place(): pl.pallas_call(functools.partial(place_kernel, spots=spots, first=first),...  4.06 us
    pallas_call x4, Pallas kernels, reduce(): pl.pallas_call(reduce_kernel, grid=(rows // ROWS,), in_specs=[fixed(modes...  2.61 us
  transfers between devices with their start and end apart: 22, of which 10 were waited for; matrix products, arithmetic and copies ran while one was open for 1% of the time, Pallas kernels for 26%

profile of v11, /device:TPU:12, one launch (start us, length us, event | category | flops | bytes accessed | tf_op | source)
XLA Modules:
  0.0 97.8 jit_solution(3099050764852316300)
XLA Ops:
  1.1 1.6 %collective-permute-start.4 = (bf16[4,48,512]{2,1,0:T(8,128)(2,1)S(1)}, bf16[4,48,512]{2,1,0:T(8,128)(2,1)S(1)}, u32[]{:S(2)}, u32[]{:S(2)}) collective-permute-start(bf16[4,48,512]{2,1,0:T(8,128)(2,1)S(1)} %get-tuple-element.122.refs_1_), channel_id=1, source_target_pairs={{0,2},{2,0},{1,3},{3,1},{4,6},{6,4},{5,7},{7,5},{8,10},{10,8},{9,1... | collective-permute-start | bytes 589832 | tf_op jit(solution)/shard_map/ppermute | solution.py:234
  4.8 2.6 %collective-permute-start.1 = (bf16[8,16,512]{2,1,0:T(8,128)(2,1)S(1)}, bf16[8,16,512]{2,1,0:T(8,128)(2,1)S(1)}, u32[]{:S(2)}, u32[]{:S(2)}) collective-permute-start(bf16[8,16,512]{2,1,0:T(8,128)(2,1)S(1)} %get-tuple-element.125), channel_id=1, source_target_pairs={{0,8},{4,12},{8,0},{12,4},{1,9},{5,13},{9,1},{13,5},{2,10},{6,14},... | collective-permute-start | bytes 393224 | tf_op jit(solution)/shard_map/ppermute | solution.py:231
  8.6 7.0 %shard_map.64 = (bf16[32,512,512]{2,1,0:T(8,128)(2,1)S(1)}, bf16[384,512]{1,0:T(8,128)(2,1)S(1)}, bf16[512,384]{1,0:T(8,128)(2,1)S(1)}) custom-call(s32[6]{0:T(128)S(1)} %compare_select_fusion.1.where, s32[4,4]{1,0:T(4,128)S(1)} %bitcast.27, s32[1]{0:T(128)S(6)} %copy.20.starts, bf16[32,512,512]{2,1,0:T(8,128)(2,1)} %bitcast.28, bf16[32,24]{1,0:T(8,128)(2,1)S(1)} %bitcast.26), custom_call_target="tpu_custom_call" | custom-call | flops 1024 | bytes 1024 | tf_op jit(solution)/shard_map/pallas_call | solution.py:63
  16.3 2.3 %collective-permute-done.refs_0_ = bf16[8,16,512]{2,1,0:T(8,128)(2,1)S(1)} collective-permute-done((bf16[8,16,512]{2,1,0:T(8,128)(2,1)S(1)}, bf16[8,16,512]{2,1,0:T(8,128)(2,1)S(1)}, u32[]{:S(2)}, u32[]{:S(2)}) %collective-permute-start) | collective-permute-done | bytes 131104 | tf_op jit(solution)/shard_map/ppermute | solution.py:231
  18.8 2.9 %collective-permute-start.5 = (bf16[8,32,512]{2,1,0:T(8,128)(2,1)S(1)}, bf16[8,32,512]{2,1,0:T(8,128)(2,1)S(1)}, u32[]{:S(2)}, u32[]{:S(2)}) collective-permute-start(bf16[8,32,512]{2,1,0:T(8,128)(2,1)S(1)} %get-tuple-element.65), channel_id=1, source_target_pairs={{0,8},{4,12},{8,0},{12,4},{1,9},{5,13},{9,1},{13,5},{2,10},{6,14},... | collective-permute-start | bytes 786440 | tf_op jit(solution)/shard_map/ppermute | solution.py:231
  21.7 1.5 %collective-permute-start.6 = (bf16[8,16,512]{2,1,0:T(8,128)(2,1)S(1)}, bf16[8,16,512]{2,1,0:T(8,128)(2,1)S(1)}, u32[]{:S(2)}, u32[]{:S(2)}) collective-permute-start(bf16[8,16,512]{2,1,0:T(8,128)(2,1)S(1)} %collective-permute-done.2.refs_0_), channel_id=1, source_target_pairs={{0,2},{2,0},{1,3},{3,1},{4,6},{6,4},{5,7},{7,5},{8,10},{10,8},{9,1... | collective-permute-start | bytes 393224 | tf_op jit(solution)/shard_map/ppermute | solution.py:234
  23.7 1.5 %collective-permute-start.8 = (bf16[8,16,512]{2,1,0:T(8,128)(2,1)S(1)}, bf16[8,16,512]{2,1,0:T(8,128)(2,1)S(1)}, u32[]{:S(2)}, u32[]{:S(2)}) collective-permute-start(bf16[8,16,512]{2,1,0:T(8,128)(2,1)S(1)} %collective-permute-done.refs_0_), channel_id=1, source_target_pairs={{0,2},{2,0},{1,3},{3,1},{4,6},{6,4},{5,7},{7,5},{8,10},{10,8},{9,1... | collective-permute-start | bytes 393224 | tf_op jit(solution)/shard_map/ppermute | solution.py:234
  29.5 1.4 %shard_map.67 = (bf16[8,16,512]{2,1,0:T(8,128)(2,1)S(1)}, bf16[8,16,512]{2,1,0:T(8,128)(2,1)S(1)}) custom-call(s32[6]{0:T(128)S(1)} %compare_select_fusion.1.where, bf16[8,16,512]{2,1,0:T(8,128)(2,1)S(1)} %collective-permute-done.1.refs_0_, bf16[8,16,512]{2,1,0:T(8,128)(2,1)S(1)} %collective-permute-done.7.refs_1_, ...), custom_call_target="tpu_custom_call" | custom-call | flops 200000000 | bytes 1024 | tf_op jit(solution)/shard_map/pallas_call | solution.py:102
  30.9 1.6 %collective-permute-start.11 = (bf16[8,32,512]{2,1,0:T(8,128)(2,1)S(1)}, bf16[8,32,512]{2,1,0:T(8,128)(2,1)}, u32[]{:S(2)}, u32[]{:S(2)}) collective-permute-start(bf16[8,32,512]{2,1,0:T(8,128)(2,1)S(1)} %collective-permute-done.10.refs_0_), channel_id=1, source_target_pairs={{0,2},{2,0},{1,3},{3,1},{4,6},{6,4},{5,7},{7,5},{8,10},{10,8},{9,1... | collective-permute-start | bytes 786440 | tf_op jit(solution)/shard_map/ppermute | solution.py:234
  34.3 4.8 %collective-permute-done.5.refs_0_ = bf16[8,32,512]{2,1,0:T(8,128)(2,1)S(1)} collective-permute-done((bf16[8,32,512]{2,1,0:T(8,128)(2,1)S(1)}, bf16[8,32,512]{2,1,0:T(8,128)(2,1)S(1)}, u32[]{:S(2)}, u32[]{:S(2)}) %collective-permute-start.5) | collective-permute-done | bytes 262176 | tf_op jit(solution)/shard_map/ppermute | solution.py:231
  39.1 1.5 %collective-permute-start.9 = (bf16[8,32,512]{2,1,0:T(8,128)(2,1)S(1)}, bf16[8,32,512]{2,1,0:T(8,128)(2,1)}, u32[]{:S(2)}, u32[]{:S(2)}) collective-permute-start(bf16[8,32,512]{2,1,0:T(8,128)(2,1)S(1)} %collective-permute-done.5.refs_0_), channel_id=1, source_target_pairs={{0,2},{2,0},{1,3},{3,1},{4,6},{6,4},{5,7},{7,5},{8,10},{10,8},{9,1... | collective-permute-start | bytes 786440 | tf_op jit(solution)/shard_map/ppermute | solution.py:234
  40.9 2.5 %collective-permute-done.12.refs_1_ = bf16[8,32,512]{2,1,0:T(8,128)(2,1)} collective-permute-done((bf16[8,32,512]{2,1,0:T(8,128)(2,1)S(1)}, bf16[8,32,512]{2,1,0:T(8,128)(2,1)}, u32[]{:S(2)}, u32[]{:S(2)}) %collective-permute-start.12) | collective-permute-done | bytes 262176 | tf_op jit(solution)/shard_map/ppermute | solution.py:231
  43.4 5.8 %copy-done.1 = bf16[32,512,512]{2,1,0:T(8,128)(2,1)S(1)} copy-done((bf16[32,512,512]{2,1,0:T(8,128)(2,1)S(1)}, bf16[32,512,512]{2,1,0:T(8,128)(2,1)}, u32[]{:S(2)}) %copy-start.1) | copy-done | bytes 16777240
  50.1 2.6 %shard_map.73 = (bf16[8,32,512]{2,1,0:T(8,128)(2,1)S(1)}, bf16[8,32,512]{2,1,0:T(8,128)(2,1)S(1)}) custom-call(s32[6]{0:T(128)S(1)} %compare_select_fusion.1.where, bf16[8,32,512]{2,1,0:T(8,128)(2,1)S(1)} %copy-done.4, bf16[8,32,512]{2,1,0:T(8,128)(2,1)} %get-tuple-element.93.refs_1_, bf16[32,512,512]{2,1,0:T(8,128)(2,1)S(1)} %copy-done.1), custom_call_target="tpu_custom_call" | custom-call | flops 1024 | bytes 1024 | tf_op jit(solution)/shard_map/pallas_call | solution.py:102
  53.3 1.6 %collective-permute-start.17 = (bf16[8,32,512]{2,1,0:T(8,128)(2,1)}, bf16[8,32,512]{2,1,0:T(8,128)(2,1)S(1)}, u32[]{:S(2)}, u32[]{:S(2)}) collective-permute-start(bf16[8,32,512]{2,1,0:T(8,128)(2,1)} %get-tuple-element.104.refs_0_), channel_id=1, source_target_pairs={{0,2},{2,0},{1,3},{3,1},{4,6},{6,4},{5,7},{7,5},{8,10},{10,8},{9,1... | collective-permute-start | bytes 786440 | tf_op jit(solution)/shard_map/ppermute | solution.py:234
  54.9 1.5 %collective-permute-start.15 = (bf16[8,16,512]{2,1,0:T(8,128)(2,1)S(1)}, bf16[8,16,512]{2,1,0:T(8,128)(2,1)S(1)}, u32[]{:S(2)}, u32[]{:S(2)}) collective-permute-start(bf16[8,16,512]{2,1,0:T(8,128)(2,1)S(1)} %get-tuple-element.97), channel_id=1, source_target_pairs={{0,12},{4,8},{8,4},{12,0},{1,13},{5,9},{9,5},{13,1},{2,14},{6,10},... | collective-permute-start | bytes 393224 | tf_op jit(solution)/shard_map/ppermute | solution.py:231
  56.4 2.9 %collective-permute-start.16 = (bf16[8,16,512]{2,1,0:T(8,128)(2,1)S(1)}, bf16[8,16,512]{2,1,0:T(8,128)(2,1)S(1)}, u32[]{:S(2)}, u32[]{:S(2)}) collective-permute-start(bf16[8,16,512]{2,1,0:T(8,128)(2,1)S(1)} %get-tuple-element.98), channel_id=1, source_target_pairs={{0,4},{4,0},{8,12},{12,8},{1,5},{5,1},{9,13},{13,9},{2,6},{6,2},{1... | collective-permute-start | bytes 393224 | tf_op jit(solution)/shard_map/ppermute | solution.py:231
  59.2 2.3 %shard_map.74 = (bf16[8,32,512]{2,1,0:T(8,128)(2,1)S(1)}, bf16[8,32,512]{2,1,0:T(8,128)(2,1)S(1)}) custom-call(s32[6]{0:T(128)S(1)} %compare_select_fusion.1.where, bf16[8,32,512]{2,1,0:T(8,128)(2,1)S(1)} %collective-permute-done.5.refs_0_, bf16[8,32,512]{2,1,0:T(8,128)(2,1)} %collective-permute-done.9.refs_1_, bf16[32,512,512]{2,1,0:T(8,128)(2,1)S(1)} %copy-done.2), custom_call_target="tpu_custom_call" | custom-call | flops 1024 | bytes 1024 | tf_op jit(solution)/shard_map/pallas_call | solution.py:102
  61.6 2.3 %shard_map.75 = (bf16[8,32,512]{2,1,0:T(8,128)(2,1)S(1)}, bf16[8,32,512]{2,1,0:T(8,128)(2,1)S(1)}) custom-call(s32[6]{0:T(128)S(1)} %compare_select_fusion.1.where, bf16[8,32,512]{2,1,0:T(8,128)(2,1)} %get-tuple-element.104.refs_0_, bf16[8,32,512]{2,1,0:T(8,128)(2,1)S(1)} %collective-permute-done.17.refs_1_, bf16[32,512,512]{2,1,0:T(8,128)(2,1)S(1)} %copy-done.2), custom_call_target="tpu_custom_call" | custom-call | flops 1024 | bytes 1024 | tf_op jit(solution)/shard_map/pallas_call | solution.py:102
  66.5 2.3 %collective-permute-done.18.came_ref = bf16[24,32,512]{2,1,0:T(8,128)(2,1)S(1)} collective-permute-done((bf16[24,32,512]{2,1,0:T(8,128)(2,1)S(1)}, bf16[24,32,512]{2,1,0:T(8,128)(2,1)S(1)}, u32[]{:S(2)}, u32[]{:S(2)}) %collective-permute-start.18) | collective-permute-done | bytes 786464 | tf_op jit(solution)/shard_map/ppermute | solution.py:280
  70.2 3.5 %collective-permute-start.19 = (bf16[8,32,512]{2,1,0:T(8,128)(2,1)S(1)}, bf16[8,32,512]{2,1,0:T(8,128)(2,1)S(1)}, u32[]{:S(2)}, u32[]{:S(2)}) collective-permute-start(bf16[8,32,512]{2,1,0:T(8,128)(2,1)S(1)} %get-tuple-element.111), channel_id=1, source_target_pairs={{0,8},{4,12},{8,0},{12,4},{1,9},{5,13},{9,1},{13,5},{2,10},{6,14},... | collective-permute-start | bytes 786440 | tf_op jit(solution)/shard_map/ppermute | solution.py:231
  75.1 6.5 %collective-permute-done.21.refs_1_ = bf16[8,32,512]{2,1,0:T(8,128)(2,1)S(1)} collective-permute-done((bf16[8,32,512]{2,1,0:T(8,128)(2,1)S(1)}, bf16[8,32,512]{2,1,0:T(8,128)(2,1)S(1)}, u32[]{:S(2)}, u32[]{:S(2)}) %collective-permute-start.21) | collective-permute-done | bytes 262176 | tf_op jit(solution)/shard_map/ppermute | solution.py:231
  82.9 8.8 %collective-permute-done.19.refs_0_ = bf16[8,32,512]{2,1,0:T(8,128)(2,1)S(1)} collective-permute-done((bf16[8,32,512]{2,1,0:T(8,128)(2,1)S(1)}, bf16[8,32,512]{2,1,0:T(8,128)(2,1)S(1)}, u32[]{:S(2)}, u32[]{:S(2)}) %collective-permute-start.19) | collective-permute-done | bytes 262176 | tf_op jit(solution)/shard_map/ppermute | solution.py:231
  91.6 4.9 %collective-permute-done.20.refs_1_ = bf16[8,32,512]{2,1,0:T(8,128)(2,1)S(1)} collective-permute-done((bf16[8,32,512]{2,1,0:T(8,128)(2,1)S(1)}, bf16[8,32,512]{2,1,0:T(8,128)(2,1)S(1)}, u32[]{:S(2)}, u32[]{:S(2)}) %collective-permute-start.20) | collective-permute-done | bytes 262176 | tf_op jit(solution)/shard_map/ppermute | solution.py:231
  (63 shorter events, 21.0 us)
Async XLA Ops:
  1.1 17.6 %collective-permute-start.4 = (bf16[4,48,512]{2,1,0:T(8,128)(2,1)S(1)}, bf16[4,48,512]{2,1,0:T(8,128)(2,1)S(1)}, u32[]{:S(2)}, u32[]{:S(2)}) collective-permute-start(bf16[4,48,512]{2,1,0:T(8,128)(2,1)S(1)} %get-tuple-element.122.refs_1_), channel_id=1, source_target_pairs={{0,2},{2,0},{1,3},{3,1},{4,6},{6,4},{5,7},{7,5},{8,10},{10,8},{9,1... | collective-permute-start | bytes 589832 | tf_op jit(solution)/shard_map/ppermute | solution.py:234
  2.6 16.0 %collective-permute-start.3 = (bf16[4,48,512]{2,1,0:T(8,128)(2,1)S(1)}, bf16[4,48,512]{2,1,0:T(8,128)(2,1)S(1)}, u32[]{:S(2)}, u32[]{:S(2)}) collective-permute-start(bf16[4,48,512]{2,1,0:T(8,128)(2,1)S(1)} %get-tuple-element.123.refs_0_), channel_id=1, source_target_pairs={{0,2},{2,0},{1,3},{3,1},{4,6},{6,4},{5,7},{7,5},{8,10},{10,8},{9,1... | collective-permute-start | bytes 589832 | tf_op jit(solution)/shard_map/ppermute | solution.py:234
  4.2 11.5 %collective-permute-start.2 = (bf16[8,16,512]{2,1,0:T(8,128)(2,1)S(1)}, bf16[8,16,512]{2,1,0:T(8,128)(2,1)S(1)}, u32[]{:S(2)}, u32[]{:S(2)}) collective-permute-start(bf16[8,16,512]{2,1,0:T(8,128)(2,1)S(1)} %get-tuple-element.124), channel_id=1, source_target_pairs={{0,4},{4,0},{8,12},{12,8},{1,5},{5,1},{9,13},{13,9},{2,6},{6,2},{1... | collective-permute-start | bytes 393224 | tf_op jit(solution)/shard_map/ppermute | solution.py:231
  4.8 11.6 %collective-permute-start.1 = (bf16[8,16,512]{2,1,0:T(8,128)(2,1)S(1)}, bf16[8,16,512]{2,1,0:T(8,128)(2,1)S(1)}, u32[]{:S(2)}, u32[]{:S(2)}) collective-permute-start(bf16[8,16,512]{2,1,0:T(8,128)(2,1)S(1)} %get-tuple-element.125), channel_id=1, source_target_pairs={{0,8},{4,12},{8,0},{12,4},{1,9},{5,13},{9,1},{13,5},{2,10},{6,14},... | collective-permute-start | bytes 393224 | tf_op jit(solution)/shard_map/ppermute | solution.py:231
  7.3 11.3 %collective-permute-start = (bf16[8,16,512]{2,1,0:T(8,128)(2,1)S(1)}, bf16[8,16,512]{2,1,0:T(8,128)(2,1)S(1)}, u32[]{:S(2)}, u32[]{:S(2)}) collective-permute-start(bf16[8,16,512]{2,1,0:T(8,128)(2,1)S(1)} %get-tuple-element.126), channel_id=1, source_target_pairs={{0,12},{4,8},{8,4},{12,0},{1,13},{5,9},{9,5},{13,1},{2,14},{6,10},... | collective-permute-start | bytes 393224 | tf_op jit(solution)/shard_map/ppermute | solution.py:231
  15.6 16.9 %copy-start = (bf16[32,512,512]{2,1,0:T(8,128)(2,1)}, bf16[32,512,512]{2,1,0:T(8,128)(2,1)S(1)}, u32[]{:S(2)}) copy-start(bf16[32,512,512]{2,1,0:T(8,128)(2,1)S(1)} %get-tuple-element.68.refs_4_.refs_2_) | copy-start | bytes 50331652
  18.6 12.3 %collective-permute-start.10 = (bf16[8,32,512]{2,1,0:T(8,128)(2,1)S(1)}, bf16[8,32,512]{2,1,0:T(8,128)(2,1)S(1)}, u32[]{:S(2)}, u32[]{:S(2)}) collective-permute-start(bf16[8,32,512]{2,1,0:T(8,128)(2,1)S(1)} %get-tuple-element.82), channel_id=1, source_target_pairs={{0,4},{4,0},{8,12},{12,8},{1,5},{5,1},{9,13},{13,9},{2,6},{6,2},{1... | collective-permute-start | bytes 786440 | tf_op jit(solution)/shard_map/ppermute | solution.py:231
  18.8 20.3 %collective-permute-start.5 = (bf16[8,32,512]{2,1,0:T(8,128)(2,1)S(1)}, bf16[8,32,512]{2,1,0:T(8,128)(2,1)S(1)}, u32[]{:S(2)}, u32[]{:S(2)}) collective-permute-start(bf16[8,32,512]{2,1,0:T(8,128)(2,1)S(1)} %get-tuple-element.65), channel_id=1, source_target_pairs={{0,8},{4,12},{8,0},{12,4},{1,9},{5,13},{9,1},{13,5},{2,10},{6,14},... | collective-permute-start | bytes 786440 | tf_op jit(solution)/shard_map/ppermute | solution.py:231
  21.7 6.0 %collective-permute-start.6 = (bf16[8,16,512]{2,1,0:T(8,128)(2,1)S(1)}, bf16[8,16,512]{2,1,0:T(8,128)(2,1)S(1)}, u32[]{:S(2)}, u32[]{:S(2)}) collective-permute-start(bf16[8,16,512]{2,1,0:T(8,128)(2,1)S(1)} %collective-permute-done.2.refs_0_), channel_id=1, source_target_pairs={{0,2},{2,0},{1,3},{3,1},{4,6},{6,4},{5,7},{7,5},{8,10},{10,8},{9,1... | collective-permute-start | bytes 393224 | tf_op jit(solution)/shard_map/ppermute | solution.py:234
  23.2 6.3 %collective-permute-start.7 = (bf16[8,16,512]{2,1,0:T(8,128)(2,1)S(1)}, bf16[8,16,512]{2,1,0:T(8,128)(2,1)S(1)}, u32[]{:S(2)}, u32[]{:S(2)}) collective-permute-start(bf16[8,16,512]{2,1,0:T(8,128)(2,1)S(1)} %collective-permute-done.1.refs_0_), channel_id=1, source_target_pairs={{0,2},{2,0},{1,3},{3,1},{4,6},{6,4},{5,7},{7,5},{8,10},{10,8},{9,1... | collective-permute-start | bytes 393224 | tf_op jit(solution)/shard_map/ppermute | solution.py:234
  23.7 8.8 %collective-permute-start.8 = (bf16[8,16,512]{2,1,0:T(8,128)(2,1)S(1)}, bf16[8,16,512]{2,1,0:T(8,128)(2,1)S(1)}, u32[]{:S(2)}, u32[]{:S(2)}) collective-permute-start(bf16[8,16,512]{2,1,0:T(8,128)(2,1)S(1)} %collective-permute-done.refs_0_), channel_id=1, source_target_pairs={{0,2},{2,0},{1,3},{3,1},{4,6},{6,4},{5,7},{7,5},{8,10},{10,8},{9,1... | collective-permute-start | bytes 393224 | tf_op jit(solution)/shard_map/ppermute | solution.py:234
  27.7 15.8 %collective-permute-start.12 = (bf16[8,32,512]{2,1,0:T(8,128)(2,1)S(1)}, bf16[8,32,512]{2,1,0:T(8,128)(2,1)}, u32[]{:S(2)}, u32[]{:S(2)}) collective-permute-start(bf16[8,32,512]{2,1,0:T(8,128)(2,1)S(1)} %get-tuple-element.119), channel_id=1, source_target_pairs={{0,12},{4,8},{8,4},{12,0},{1,13},{5,9},{9,5},{13,1},{2,14},{6,10},... | collective-permute-start | bytes 786440 | tf_op jit(solution)/shard_map/ppermute | solution.py:231
  30.9 12.5 %collective-permute-start.11 = (bf16[8,32,512]{2,1,0:T(8,128)(2,1)S(1)}, bf16[8,32,512]{2,1,0:T(8,128)(2,1)}, u32[]{:S(2)}, u32[]{:S(2)}) collective-permute-start(bf16[8,32,512]{2,1,0:T(8,128)(2,1)S(1)} %collective-permute-done.10.refs_0_), channel_id=1, source_target_pairs={{0,2},{2,0},{1,3},{3,1},{4,6},{6,4},{5,7},{7,5},{8,10},{10,8},{9,1... | collective-permute-start | bytes 786440 | tf_op jit(solution)/shard_map/ppermute | solution.py:234
  39.1 13.6 %collective-permute-start.13 = (bf16[24,16,512]{2,1,0:T(8,128)(2,1)S(1)}, bf16[24,16,512]{2,1,0:T(8,128)(2,1)S(1)}, u32[]{:S(2)}, u32[]{:S(2)}) collective-permute-start(bf16[24,16,512]{2,1,0:T(8,128)(2,1)S(1)} %shard_map.69), channel_id=1, source_target_pairs={{0,1},{1,0},{2,3},{3,2},{4,5},{5,4},{6,7},{7,6},{8,9},{9,8},{10,11... | collective-permute-start | bytes 1179656 | tf_op jit(solution)/shard_map/ppermute | solution.py:268
  39.1 14.2 %collective-permute-start.9 = (bf16[8,32,512]{2,1,0:T(8,128)(2,1)S(1)}, bf16[8,32,512]{2,1,0:T(8,128)(2,1)}, u32[]{:S(2)}, u32[]{:S(2)}) collective-permute-start(bf16[8,32,512]{2,1,0:T(8,128)(2,1)S(1)} %collective-permute-done.5.refs_0_), channel_id=1, source_target_pairs={{0,2},{2,0},{1,3},{3,1},{4,6},{6,4},{5,7},{7,5},{8,10},{10,8},{9,1... | collective-permute-start | bytes 786440 | tf_op jit(solution)/shard_map/ppermute | solution.py:234
  50.1 9.1 %copy-start.2 = (bf16[32,512,512]{2,1,0:T(8,128)(2,1)S(1)}, bf16[32,512,512]{2,1,0:T(8,128)(2,1)}, u32[]{:S(2)}) copy-start(bf16[32,512,512]{2,1,0:T(8,128)(2,1)} %copy-done) | copy-start | bytes 50331652
  53.3 8.3 %collective-permute-start.17 = (bf16[8,32,512]{2,1,0:T(8,128)(2,1)}, bf16[8,32,512]{2,1,0:T(8,128)(2,1)S(1)}, u32[]{:S(2)}, u32[]{:S(2)}) collective-permute-start(bf16[8,32,512]{2,1,0:T(8,128)(2,1)} %get-tuple-element.104.refs_0_), channel_id=1, source_target_pairs={{0,2},{2,0},{1,3},{3,1},{4,6},{6,4},{5,7},{7,5},{8,10},{10,8},{9,1... | collective-permute-start | bytes 786440 | tf_op jit(solution)/shard_map/ppermute | solution.py:234
  54.9 11.0 %collective-permute-start.14 = (bf16[8,16,512]{2,1,0:T(8,128)(2,1)S(1)}, bf16[8,16,512]{2,1,0:T(8,128)(2,1)S(1)}, u32[]{:S(2)}, u32[]{:S(2)}) collective-permute-start(bf16[8,16,512]{2,1,0:T(8,128)(2,1)S(1)} %get-tuple-element.96), channel_id=1, source_target_pairs={{0,8},{4,12},{8,0},{12,4},{1,9},{5,13},{9,1},{13,5},{2,10},{6,14},... | collective-permute-start | bytes 393224 | tf_op jit(solution)/shard_map/ppermute | solution.py:231
  54.9 11.6 %collective-permute-start.15 = (bf16[8,16,512]{2,1,0:T(8,128)(2,1)S(1)}, bf16[8,16,512]{2,1,0:T(8,128)(2,1)S(1)}, u32[]{:S(2)}, u32[]{:S(2)}) collective-permute-start(bf16[8,16,512]{2,1,0:T(8,128)(2,1)S(1)} %get-tuple-element.97), channel_id=1, source_target_pairs={{0,12},{4,8},{8,4},{12,0},{1,13},{5,9},{9,5},{13,1},{2,14},{6,10},... | collective-permute-start | bytes 393224 | tf_op jit(solution)/shard_map/ppermute | solution.py:231
  56.4 10.1 %collective-permute-start.16 = (bf16[8,16,512]{2,1,0:T(8,128)(2,1)S(1)}, bf16[8,16,512]{2,1,0:T(8,128)(2,1)S(1)}, u32[]{:S(2)}, u32[]{:S(2)}) collective-permute-start(bf16[8,16,512]{2,1,0:T(8,128)(2,1)S(1)} %get-tuple-element.98), channel_id=1, source_target_pairs={{0,4},{4,0},{8,12},{12,8},{1,5},{5,1},{9,13},{13,9},{2,6},{6,2},{1... | collective-permute-start | bytes 393224 | tf_op jit(solution)/shard_map/ppermute | solution.py:231
  66.5 2.3 %collective-permute-start.18 = (bf16[24,32,512]{2,1,0:T(8,128)(2,1)S(1)}, bf16[24,32,512]{2,1,0:T(8,128)(2,1)S(1)}, u32[]{:S(2)}, u32[]{:S(2)}) collective-permute-start(bf16[24,32,512]{2,1,0:T(8,128)(2,1)S(1)} %shard_map.77), channel_id=1, source_target_pairs={{0,1},{1,0},{2,3},{3,2},{4,5},{5,4},{6,7},{7,6},{8,9},{9,8},{10,11... | collective-permute-start | bytes 2359304 | tf_op jit(solution)/shard_map/ppermute | solution.py:280
  70.0 11.5 %collective-permute-start.21 = (bf16[8,32,512]{2,1,0:T(8,128)(2,1)S(1)}, bf16[8,32,512]{2,1,0:T(8,128)(2,1)S(1)}, u32[]{:S(2)}, u32[]{:S(2)}) collective-permute-start(bf16[8,32,512]{2,1,0:T(8,128)(2,1)S(1)} %get-tuple-element.114), channel_id=1, source_target_pairs={{0,4},{4,0},{8,12},{12,8},{1,5},{5,1},{9,13},{13,9},{2,6},{6,2},{1... | collective-permute-start | bytes 786440 | tf_op jit(solution)/shard_map/ppermute | solution.py:231
  70.2 21.5 %collective-permute-start.19 = (bf16[8,32,512]{2,1,0:T(8,128)(2,1)S(1)}, bf16[8,32,512]{2,1,0:T(8,128)(2,1)S(1)}, u32[]{:S(2)}, u32[]{:S(2)}) collective-permute-start(bf16[8,32,512]{2,1,0:T(8,128)(2,1)S(1)} %get-tuple-element.111), channel_id=1, source_target_pairs={{0,8},{4,12},{8,0},{12,4},{1,9},{5,13},{9,1},{13,5},{2,10},{6,14},... | collective-permute-start | bytes 786440 | tf_op jit(solution)/shard_map/ppermute | solution.py:231
  73.7 22.8 %collective-permute-start.20 = (bf16[8,32,512]{2,1,0:T(8,128)(2,1)S(1)}, bf16[8,32,512]{2,1,0:T(8,128)(2,1)S(1)}, u32[]{:S(2)}, u32[]{:S(2)}) collective-permute-start(bf16[8,32,512]{2,1,0:T(8,128)(2,1)S(1)} %get-tuple-element.112), channel_id=1, source_target_pairs={{0,12},{4,8},{8,4},{12,0},{1,13},{5,9},{9,5},{13,1},{2,14},{6,10},... | collective-permute-start | bytes 786440 | tf_op jit(solution)/shard_map/ppermute | solution.py:231
  (7 other events, 40.4 us)

commit v12 on v11

--- a/solution.py
+++ b/solution.py
@@ -215,6 +215,7 @@
         out_specs=[anywhere] * len(values),
         out_shape=[jax.ShapeDtypeStruct(value.shape, value.dtype) for value in values],
         input_output_aliases={n: n for n in range(len(values))},
+        compiler_params=pltpu.CompilerParams(vmem_limit_bytes=1024 * 1024),
         cost_estimate=pl.CostEstimate(flops=flops, bytes_accessed=1024, transcendentals=0),
     )(*values)
 
@@ -252,26 +253,27 @@
     a = {j: along_z(cut(j, 0, ROWS), j) for j in (3, 2, 1)}
     mine = [cut(0, 0, rows_all)[n:n + half] for n in (0, half)]
     others = [along_x(part) for part in mine]
-    b, far = {j: cut(j, ROWS, most) for j in (1, 2)}, cut(3, ROWS, most)
+    b = {j: cut(j, ROWS, most) for j in (1, 2, 3)}
     held, down, up = hold(where, tile_mask[0], first_block, beam, eigen_modes[0])
-    (a[3], a[2], a[1]), b, others, down, up = fence(((a[3], a[2], a[1]), b, others, down, up))
-    b[1], b[2] = along_z(b[1], 1), along_z(b[2], 2)
+    (a[1], a[2], a[3]), b, others, down, up = fence(((a[1], a[2], a[3]), b, others, down, up))
+    b[1], b[3] = along_z(b[1], 1), along_z(b[3], 3)
     own = project(where, mine, others, held, 0, halves, 200_000_000)
     skies = [own] + [project(where, [a[j]], [along_x(a[j])], held, j, blocks, 200_000_000) for j in (1, 2, 3)]
     gone = reduce(down, [leave for _, leave in skies], (0, 0, 0, 0), n_modes)
     stay_a = [stay for stay, _ in skies]
-    b[2], stay_a, gone = fence((b[2], stay_a, gone))
-    x_2 = along_x(b[2])
-    x_1, b[3] = anchor([along_x(b[1]), along_z(far, 3)], 1_500_000_000)
+    b[3], stay_a, gone = fence((b[3], stay_a, gone))
+    x_3 = along_x(b[3])
+    x_1, b[2] = anchor([along_x(b[1]), along_z(b[2], 2)], 1_500_000_000)
     kept = reduce(down, stay_a, (0, 0, 0, 0), n_modes, jnp.float32)
     spots = [(j, 0, freqs) for j in (1, 2, 3, 0)]
     outs = restore(kept, lax.ppermute(gone, "pol", other), ratios, up, spots)
     near = project(where, [b[1]], [x_1], held, 1, blocks)
-    x_2, b, outs, near = fence((x_2, b, outs, near))
+    x_3, b, outs, near = fence((x_3, b, outs, near))
     first = {j: along_z(outs[j - 1], j) for j in (1, 2, 3)}
     first[0] = outs[3]
-    x_3 = along_x(b[3])
-    skies = [own, near] + [project(where, [b[j]], [x], held, j, blocks) for j, x in ((2, x_2), (3, x_3))]
+    x_2 = along_x(b[2])
+    last = project(where, [b[3]], [x_3], held, 3, blocks)
+    skies = [own, near, project(where, [b[2]], [x_2], held, 2, blocks), last]
     gone = reduce(down, [leave for _, leave in skies], (ROWS, 0, 0, 0), n_modes)
     kept = reduce(down, [stay for stay, _ in skies], (ROWS, 0, 0, 0), n_modes, jnp.float32)
     (first[2], first[3], first[1]), first[0], kept, gone = fence(

time: 98.7 us -> 92.8 us (0.940)
  local copies, waits for them, and re-layouts: 9.14 us -> 2.39 us
  Pallas kernels: 28 us -> 25.1 us
  starting transfers between devices: 25.4 us -> 27.7 us
  waiting for transfers between devices: 34.3 us -> 36.5 us
    unnamed x19 -> x9, local copies, waits for them, and re-layouts: 6.85 us -> 0.1 us
    ppermute x8, waiting for transfers between devices: 1.12 us -> 6.01 us  [along_x(): return lax.ppermute(value, 'kl', other)]
    pallas_call x7, Pallas kernels: 12.7 us -> 9.57 us  [project(): pl.pallas_call(functools.partial(project_kernel, piece=piece, blocks=bloc...]
    ppermute x12, waiting for transfers between devices: 30.9 us -> 28.2 us  [along_z(): return lax.ppermute(value, 'fm', [(i, i ^ j) for i in range(parts)])]
    ppermute x12, starting transfers between devices: 15.2 us -> 17.5 us  [along_z(): return lax.ppermute(value, 'fm', [(i, i ^ j) for i in range(parts)])]
  transfers between devices with their start and end apart: 22 -> 22, of which waited for: 10 -> 12; matrix products, arithmetic and copies ran while one was open for 1% -> 1% of each run, Pallas kernels for 26% -> 24%
where the time goes in v12:
time: 92.8 us; the launch traced here: 92.5 us
  waiting for transfers between devices  36.5 us (39%)
  starting transfers between devices  27.7 us (30%)
  Pallas kernels  25.1 us (27%)
  local copies, waits for them, and re-layouts  2.39 us (3%)
    ppermute x12, waiting for transfers between devices, along_z(): return lax.ppermute(value, 'fm', [(i, i ^ j) for i in range(parts)])  28.2 us
    ppermute x12, starting transfers between devices, along_z(): return lax.ppermute(value, 'fm', [(i, i ^ j) for i in range(parts)])  17.5 us
    ppermute x8, starting transfers between devices, along_x(): return lax.ppermute(value, 'kl', other)  10.1 us
    pallas_call x7, Pallas kernels, project(): pl.pallas_call(functools.partial(project_kernel, piece=piece, blocks=bloc...  9.57 us
    pallas_call x1, Pallas kernels, hold(): pl.pallas_call(hold_kernel, grid_spec=pltpu.PrefetchScalarGridSpec(num_sc...  7.04 us
    ppermute x8, waiting for transfers between devices, along_x(): return lax.ppermute(value, 'kl', other)  6.01 us
    pallas_call x3, Pallas kernels, place(): pl.pallas_call(functools.partial(place_kernel, spots=spots, first=first),...  4.06 us
    pallas_call x4, Pallas kernels, reduce(): pl.pallas_call(reduce_kernel, grid=(rows // ROWS,), in_specs=[fixed(modes...  2.62 us
  transfers between devices with their start and end apart: 22, of which 12 were waited for; matrix products, arithmetic and copies ran while one was open for 1% of the time, Pallas kernels for 24%

profile of v12, /device:TPU:12, one launch (start us, length us, event | category | flops | bytes accessed | tf_op | source)
XLA Modules:
  0.0 92.5 jit_solution(17218765633447726725)
XLA Ops:
  1.1 1.6 %collective-permute-start.4 = (bf16[4,48,512]{2,1,0:T(8,128)(2,1)S(1)}, bf16[4,48,512]{2,1,0:T(8,128)(2,1)S(1)}, u32[]{:S(2)}, u32[]{:S(2)}) collective-permute-start(bf16[4,48,512]{2,1,0:T(8,128)(2,1)S(1)} %get-tuple-element.121.refs_1_), channel_id=1, source_target_pairs={{0,2},{2,0},{1,3},{3,1},{4,6},{6,4},{5,7},{7,5},{8,10},{10,8},{9,1... | collective-permute-start | bytes 589832 | tf_op jit(solution)/shard_map/ppermute | solution.py:235
  4.2 1.6 %collective-permute-start.2 = (bf16[8,16,512]{2,1,0:T(8,128)(2,1)S(1)}, bf16[8,16,512]{2,1,0:T(8,128)(2,1)S(1)}, u32[]{:S(2)}, u32[]{:S(2)}) collective-permute-start(bf16[8,16,512]{2,1,0:T(8,128)(2,1)S(1)} %get-tuple-element.126), channel_id=1, source_target_pairs={{0,12},{4,8},{8,4},{12,0},{1,13},{5,9},{9,5},{13,1},{2,14},{6,10},... | collective-permute-start | bytes 393224 | tf_op jit(solution)/shard_map/ppermute | solution.py:232
  9.1 7.0 %shard_map.64 = (bf16[32,512,512]{2,1,0:T(8,128)(2,1)S(1)}, bf16[384,512]{1,0:T(8,128)(2,1)S(1)}, bf16[512,384]{1,0:T(8,128)(2,1)S(1)}) custom-call(s32[6]{0:T(128)S(1)} %compare_select_fusion.1.where, s32[4,4]{1,0:T(4,128)S(1)} %bitcast.27, s32[1]{0:T(128)S(6)} %copy.20.starts, bf16[32,512,512]{2,1,0:T(8,128)(2,1)} %bitcast.28, bf16[32,24]{1,0:T(8,128)(2,1)S(1)} %bitcast.26), custom_call_target="tpu_custom_call" | custom-call | flops 1024 | bytes 1024 | tf_op jit(solution)/shard_map/pallas_call | solution.py:63
  16.7 2.3 %collective-permute-start.10 = (bf16[8,32,512]{2,1,0:T(8,128)(2,1)S(1)}, bf16[8,32,512]{2,1,0:T(8,128)(2,1)S(1)}, u32[]{:S(2)}, u32[]{:S(2)}) collective-permute-start(bf16[8,32,512]{2,1,0:T(8,128)(2,1)S(1)} %get-tuple-element.83), channel_id=1, source_target_pairs={{0,4},{4,0},{8,12},{12,8},{1,5},{5,1},{9,13},{13,9},{2,6},{6,2},{1... | collective-permute-start | bytes 786440 | tf_op jit(solution)/shard_map/ppermute | solution.py:232
  18.9 1.6 %collective-permute-start.5 = (bf16[8,32,512]{2,1,0:T(8,128)(2,1)S(1)}, bf16[8,32,512]{2,1,0:T(8,128)(2,1)S(1)}, u32[]{:S(2)}, u32[]{:S(2)}) collective-permute-start(bf16[8,32,512]{2,1,0:T(8,128)(2,1)S(1)} %get-tuple-element.66), channel_id=1, source_target_pairs={{0,12},{4,8},{8,4},{12,0},{1,13},{5,9},{9,5},{13,1},{2,14},{6,10},... | collective-permute-start | bytes 786440 | tf_op jit(solution)/shard_map/ppermute | solution.py:232
  20.5 1.5 %collective-permute-start.6 = (bf16[8,16,512]{2,1,0:T(8,128)(2,1)S(1)}, bf16[8,16,512]{2,1,0:T(8,128)(2,1)S(1)}, u32[]{:S(2)}, u32[]{:S(2)}) collective-permute-start(bf16[8,16,512]{2,1,0:T(8,128)(2,1)S(1)} %collective-permute-done.refs_0_), channel_id=1, source_target_pairs={{0,2},{2,0},{1,3},{3,1},{4,6},{6,4},{5,7},{7,5},{8,10},{10,8},{9,1... | collective-permute-start | bytes 393224 | tf_op jit(solution)/shard_map/ppermute | solution.py:235
  22.6 1.5 %collective-permute-start.8 = (bf16[8,16,512]{2,1,0:T(8,128)(2,1)S(1)}, bf16[8,16,512]{2,1,0:T(8,128)(2,1)S(1)}, u32[]{:S(2)}, u32[]{:S(2)}) collective-permute-start(bf16[8,16,512]{2,1,0:T(8,128)(2,1)S(1)} %collective-permute-done.2.refs_0_), channel_id=1, source_target_pairs={{0,2},{2,0},{1,3},{3,1},{4,6},{6,4},{5,7},{7,5},{8,10},{10,8},{9,1... | collective-permute-start | bytes 393224 | tf_op jit(solution)/shard_map/ppermute | solution.py:235
  26.2 1.6 %collective-permute-start.12 = (bf16[8,32,512]{2,1,0:T(8,128)(2,1)S(1)}, bf16[8,32,512]{2,1,0:T(8,128)(2,1)S(1)}, u32[]{:S(2)}, u32[]{:S(2)}) collective-permute-start(bf16[8,32,512]{2,1,0:T(8,128)(2,1)S(1)} %get-tuple-element.84), channel_id=1, source_target_pairs={{0,8},{4,12},{8,0},{12,4},{1,9},{5,13},{9,1},{13,5},{2,10},{6,14},... | collective-permute-start | bytes 786440 | tf_op jit(solution)/shard_map/ppermute | solution.py:232
  29.2 1.4 %shard_map.67 = (bf16[8,16,512]{2,1,0:T(8,128)(2,1)S(1)}, bf16[8,16,512]{2,1,0:T(8,128)(2,1)S(1)}) custom-call(s32[6]{0:T(128)S(1)} %compare_select_fusion.1.where, bf16[8,16,512]{2,1,0:T(8,128)(2,1)S(1)} %collective-permute-done.1.refs_0_, bf16[8,16,512]{2,1,0:T(8,128)(2,1)S(1)} %collective-permute-done.7.refs_1_, ...), custom_call_target="tpu_custom_call" | custom-call | flops 200000000 | bytes 1024 | tf_op jit(solution)/shard_map/pallas_call | solution.py:102
  30.6 1.6 %collective-permute-start.11 = (bf16[8,32,512]{2,1,0:T(8,128)(2,1)S(1)}, bf16[8,32,512]{2,1,0:T(8,128)(2,1)S(1)}, u32[]{:S(2)}, u32[]{:S(2)}) collective-permute-start(bf16[8,32,512]{2,1,0:T(8,128)(2,1)S(1)} %collective-permute-done.10.refs_0_), channel_id=1, source_target_pairs={{0,2},{2,0},{1,3},{3,1},{4,6},{6,4},{5,7},{7,5},{8,10},{10,8},{9,1... | collective-permute-start | bytes 786440 | tf_op jit(solution)/shard_map/ppermute | solution.py:235
  33.9 5.2 %collective-permute-done.5.refs_0_ = bf16[8,32,512]{2,1,0:T(8,128)(2,1)S(1)} collective-permute-done((bf16[8,32,512]{2,1,0:T(8,128)(2,1)S(1)}, bf16[8,32,512]{2,1,0:T(8,128)(2,1)S(1)}, u32[]{:S(2)}, u32[]{:S(2)}) %collective-permute-start.5) | collective-permute-done | bytes 262176 | tf_op jit(solution)/shard_map/ppermute | solution.py:232
  39.1 1.5 %collective-permute-start.9 = (bf16[8,32,512]{2,1,0:T(8,128)(2,1)S(1)}, bf16[8,32,512]{2,1,0:T(8,128)(2,1)S(1)}, u32[]{:S(2)}, u32[]{:S(2)}) collective-permute-start(bf16[8,32,512]{2,1,0:T(8,128)(2,1)S(1)} %collective-permute-done.5.refs_0_), channel_id=1, source_target_pairs={{0,2},{2,0},{1,3},{3,1},{4,6},{6,4},{5,7},{7,5},{8,10},{10,8},{9,1... | collective-permute-start | bytes 786440 | tf_op jit(solution)/shard_map/ppermute | solution.py:235
  41.3 1.4 %shard_map.73 = (bf16[8,32,512]{2,1,0:T(8,128)(2,1)S(1)}, bf16[8,32,512]{2,1,0:T(8,128)(2,1)S(1)}) custom-call(s32[6]{0:T(128)S(1)} %compare_select_fusion.1.where, bf16[8,32,512]{2,1,0:T(8,128)(2,1)S(1)} %collective-permute-done.10.refs_0_, bf16[8,32,512]{2,1,0:T(8,128)(2,1)S(1)} %get-tuple-element.95.refs_1_, ...), custom_call_target="tpu_custom_call" | custom-call | flops 1024 | bytes 1024 | tf_op jit(solution)/shard_map/pallas_call | solution.py:102
  43.3 4.5 %collective-permute-done.9.refs_1_ = bf16[8,32,512]{2,1,0:T(8,128)(2,1)S(1)} collective-permute-done((bf16[8,32,512]{2,1,0:T(8,128)(2,1)S(1)}, bf16[8,32,512]{2,1,0:T(8,128)(2,1)S(1)}, u32[]{:S(2)}, u32[]{:S(2)}) %collective-permute-start.9) | collective-permute-done | bytes 262176 | tf_op jit(solution)/shard_map/ppermute | solution.py:235
  47.8 1.5 %collective-permute-start.17 = (bf16[8,32,512]{2,1,0:T(8,128)(2,1)S(1)}, bf16[8,32,512]{2,1,0:T(8,128)(2,1)S(1)}, u32[]{:S(2)}, u32[]{:S(2)}) collective-permute-start(bf16[8,32,512]{2,1,0:T(8,128)(2,1)S(1)} %get-tuple-element.103.refs_0_), channel_id=1, source_target_pairs={{0,2},{2,0},{1,3},{3,1},{4,6},{6,4},{5,7},{7,5},{8,10},{10,8},{9,1... | collective-permute-start | bytes 786440 | tf_op jit(solution)/shard_map/ppermute | solution.py:235
  49.6 4.1 %collective-permute-start.16 = (bf16[8,16,512]{2,1,0:T(8,128)(2,1)S(1)}, bf16[8,16,512]{2,1,0:T(8,128)(2,1)S(1)}, u32[]{:S(2)}, u32[]{:S(2)}) collective-permute-start(bf16[8,16,512]{2,1,0:T(8,128)(2,1)S(1)} %get-tuple-element.100), channel_id=1, source_target_pairs={{0,4},{4,0},{8,12},{12,8},{1,5},{5,1},{9,13},{13,9},{2,6},{6,2},{1... | collective-permute-start | bytes 393224 | tf_op jit(solution)/shard_map/ppermute | solution.py:232
  53.7 1.4 %shard_map.75 = (bf16[8,32,512]{2,1,0:T(8,128)(2,1)S(1)}, bf16[8,32,512]{2,1,0:T(8,128)(2,1)S(1)}) custom-call(s32[6]{0:T(128)S(1)} %compare_select_fusion.1.where, bf16[8,32,512]{2,1,0:T(8,128)(2,1)S(1)} %collective-permute-done.5.refs_0_, bf16[8,32,512]{2,1,0:T(8,128)(2,1)S(1)} %collective-permute-done.9.refs_1_, ...), custom_call_target="tpu_custom_call" | custom-call | flops 1024 | bytes 1024 | tf_op jit(solution)/shard_map/pallas_call | solution.py:102
  55.7 1.4 %shard_map.74 = (bf16[8,32,512]{2,1,0:T(8,128)(2,1)S(1)}, bf16[8,32,512]{2,1,0:T(8,128)(2,1)S(1)}) custom-call(s32[6]{0:T(128)S(1)} %compare_select_fusion.1.where, bf16[8,32,512]{2,1,0:T(8,128)(2,1)S(1)} %get-tuple-element.103.refs_0_, bf16[8,32,512]{2,1,0:T(8,128)(2,1)S(1)} %collective-permute-done.17.refs_1_, ...), custom_call_target="tpu_custom_call" | custom-call | flops 1024 | bytes 1024 | tf_op jit(solution)/shard_map/pallas_call | solution.py:102
  59.0 2.1 %collective-permute-done.15.refs_2_ = bf16[8,16,512]{2,1,0:T(8,128)(2,1)S(1)} collective-permute-done((bf16[8,16,512]{2,1,0:T(8,128)(2,1)S(1)}, bf16[8,16,512]{2,1,0:T(8,128)(2,1)S(1)}, u32[]{:S(2)}, u32[]{:S(2)}) %collective-permute-start.15) | collective-permute-done | bytes 131104 | tf_op jit(solution)/shard_map/ppermute | solution.py:232
  61.1 2.3 %collective-permute-done.18.came_ref = bf16[24,32,512]{2,1,0:T(8,128)(2,1)S(1)} collective-permute-done((bf16[24,32,512]{2,1,0:T(8,128)(2,1)S(1)}, bf16[24,32,512]{2,1,0:T(8,128)(2,1)S(1)}, u32[]{:S(2)}, u32[]{:S(2)}) %collective-permute-start.18) | collective-permute-done | bytes 786464 | tf_op jit(solution)/shard_map/ppermute | solution.py:282
  65.2 2.7 %collective-permute-start.19 = (bf16[8,32,512]{2,1,0:T(8,128)(2,1)S(1)}, bf16[8,32,512]{2,1,0:T(8,128)(2,1)S(1)}, u32[]{:S(2)}, u32[]{:S(2)}) collective-permute-start(bf16[8,32,512]{2,1,0:T(8,128)(2,1)S(1)} %get-tuple-element.113), channel_id=1, source_target_pairs={{0,8},{4,12},{8,0},{12,4},{1,9},{5,13},{9,1},{13,5},{2,10},{6,14},... | collective-permute-start | bytes 786440 | tf_op jit(solution)/shard_map/ppermute | solution.py:232
  69.6 6.6 %collective-permute-done.21.refs_1_ = bf16[8,32,512]{2,1,0:T(8,128)(2,1)S(1)} collective-permute-done((bf16[8,32,512]{2,1,0:T(8,128)(2,1)S(1)}, bf16[8,32,512]{2,1,0:T(8,128)(2,1)S(1)}, u32[]{:S(2)}, u32[]{:S(2)}) %collective-permute-start.21) | collective-permute-done | bytes 262176 | tf_op jit(solution)/shard_map/ppermute | solution.py:232
  77.5 8.3 %collective-permute-done.19.refs_0_ = bf16[8,32,512]{2,1,0:T(8,128)(2,1)S(1)} collective-permute-done((bf16[8,32,512]{2,1,0:T(8,128)(2,1)S(1)}, bf16[8,32,512]{2,1,0:T(8,128)(2,1)S(1)}, u32[]{:S(2)}, u32[]{:S(2)}) %collective-permute-start.19) | collective-permute-done | bytes 262176 | tf_op jit(solution)/shard_map/ppermute | solution.py:232
  85.9 5.3 %collective-permute-done.20.refs_1_ = bf16[8,32,512]{2,1,0:T(8,128)(2,1)S(1)} collective-permute-done((bf16[8,32,512]{2,1,0:T(8,128)(2,1)S(1)}, bf16[8,32,512]{2,1,0:T(8,128)(2,1)S(1)}, u32[]{:S(2)}, u32[]{:S(2)}) %collective-permute-start.20) | collective-permute-done | bytes 262176 | tf_op jit(solution)/shard_map/ppermute | solution.py:232
  (53 shorter events, 21.8 us)
Async XLA Ops:
  0.0 9.0 %copy-start.2 = (bf16[1,32,24]{1,2,0:T(8,128)(2,1)S(1)}, bf16[1,32,24]{1,2,0:T(8,128)(2,1)}, u32[]{:S(2)}) copy-start(bf16[1,32,24]{1,2,0:T(8,128)(2,1)} %param.10) | copy-start | bytes 4612
  0.0 9.1 %copy-start = (s32[1,4,4]{2,1,0:T(4,128)S(1)}, s32[1,4,4]{2,1,0:T(4,128)}, u32[]{:S(2)}) copy-start(s32[1,4,4]{2,1,0:T(4,128)} %param.8) | copy-start | bytes 196
  1.1 15.6 %collective-permute-start.4 = (bf16[4,48,512]{2,1,0:T(8,128)(2,1)S(1)}, bf16[4,48,512]{2,1,0:T(8,128)(2,1)S(1)}, u32[]{:S(2)}, u32[]{:S(2)}) collective-permute-start(bf16[4,48,512]{2,1,0:T(8,128)(2,1)S(1)} %get-tuple-element.121.refs_1_), channel_id=1, source_target_pairs={{0,2},{2,0},{1,3},{3,1},{4,6},{6,4},{5,7},{7,5},{8,10},{10,8},{9,1... | collective-permute-start | bytes 589832 | tf_op jit(solution)/shard_map/ppermute | solution.py:235
  2.6 14.0 %collective-permute-start.3 = (bf16[4,48,512]{2,1,0:T(8,128)(2,1)S(1)}, bf16[4,48,512]{2,1,0:T(8,128)(2,1)S(1)}, u32[]{:S(2)}, u32[]{:S(2)}) collective-permute-start(bf16[4,48,512]{2,1,0:T(8,128)(2,1)S(1)} %get-tuple-element.122.refs_0_), channel_id=1, source_target_pairs={{0,2},{2,0},{1,3},{3,1},{4,6},{6,4},{5,7},{7,5},{8,10},{10,8},{9,1... | collective-permute-start | bytes 589832 | tf_op jit(solution)/shard_map/ppermute | solution.py:235
  4.2 12.0 %collective-permute-start.2 = (bf16[8,16,512]{2,1,0:T(8,128)(2,1)S(1)}, bf16[8,16,512]{2,1,0:T(8,128)(2,1)S(1)}, u32[]{:S(2)}, u32[]{:S(2)}) collective-permute-start(bf16[8,16,512]{2,1,0:T(8,128)(2,1)S(1)} %get-tuple-element.126), channel_id=1, source_target_pairs={{0,12},{4,8},{8,4},{12,0},{1,13},{5,9},{9,5},{13,1},{2,14},{6,10},... | collective-permute-start | bytes 393224 | tf_op jit(solution)/shard_map/ppermute | solution.py:232
  5.9 10.6 %collective-permute-start.1 = (bf16[8,16,512]{2,1,0:T(8,128)(2,1)S(1)}, bf16[8,16,512]{2,1,0:T(8,128)(2,1)S(1)}, u32[]{:S(2)}, u32[]{:S(2)}) collective-permute-start(bf16[8,16,512]{2,1,0:T(8,128)(2,1)S(1)} %get-tuple-element.127), channel_id=1, source_target_pairs={{0,8},{4,12},{8,0},{12,4},{1,9},{5,13},{9,1},{13,5},{2,10},{6,14},... | collective-permute-start | bytes 393224 | tf_op jit(solution)/shard_map/ppermute | solution.py:232
  7.1 9.6 %collective-permute-start = (bf16[8,16,512]{2,1,0:T(8,128)(2,1)S(1)}, bf16[8,16,512]{2,1,0:T(8,128)(2,1)S(1)}, u32[]{:S(2)}, u32[]{:S(2)}) collective-permute-start(bf16[8,16,512]{2,1,0:T(8,128)(2,1)S(1)} %get-tuple-element.128), channel_id=1, source_target_pairs={{0,4},{4,0},{8,12},{12,8},{1,5},{5,1},{9,13},{13,9},{2,6},{6,2},{1... | collective-permute-start | bytes 393224 | tf_op jit(solution)/shard_map/ppermute | solution.py:232
  16.7 13.9 %collective-permute-start.10 = (bf16[8,32,512]{2,1,0:T(8,128)(2,1)S(1)}, bf16[8,32,512]{2,1,0:T(8,128)(2,1)S(1)}, u32[]{:S(2)}, u32[]{:S(2)}) collective-permute-start(bf16[8,32,512]{2,1,0:T(8,128)(2,1)S(1)} %get-tuple-element.83), channel_id=1, source_target_pairs={{0,4},{4,0},{8,12},{12,8},{1,5},{5,1},{9,13},{13,9},{2,6},{6,2},{1... | collective-permute-start | bytes 786440 | tf_op jit(solution)/shard_map/ppermute | solution.py:232
  18.9 20.1 %collective-permute-start.5 = (bf16[8,32,512]{2,1,0:T(8,128)(2,1)S(1)}, bf16[8,32,512]{2,1,0:T(8,128)(2,1)S(1)}, u32[]{:S(2)}, u32[]{:S(2)}) collective-permute-start(bf16[8,32,512]{2,1,0:T(8,128)(2,1)S(1)} %get-tuple-element.66), channel_id=1, source_target_pairs={{0,12},{4,8},{8,4},{12,0},{1,13},{5,9},{9,5},{13,1},{2,14},{6,10},... | collective-permute-start | bytes 786440 | tf_op jit(solution)/shard_map/ppermute | solution.py:232
  20.5 5.7 %collective-permute-start.6 = (bf16[8,16,512]{2,1,0:T(8,128)(2,1)S(1)}, bf16[8,16,512]{2,1,0:T(8,128)(2,1)S(1)}, u32[]{:S(2)}, u32[]{:S(2)}) collective-permute-start(bf16[8,16,512]{2,1,0:T(8,128)(2,1)S(1)} %collective-permute-done.refs_0_), channel_id=1, source_target_pairs={{0,2},{2,0},{1,3},{3,1},{4,6},{6,4},{5,7},{7,5},{8,10},{10,8},{9,1... | collective-permute-start | bytes 393224 | tf_op jit(solution)/shard_map/ppermute | solution.py:235
  22.0 7.2 %collective-permute-start.7 = (bf16[8,16,512]{2,1,0:T(8,128)(2,1)S(1)}, bf16[8,16,512]{2,1,0:T(8,128)(2,1)S(1)}, u32[]{:S(2)}, u32[]{:S(2)}) collective-permute-start(bf16[8,16,512]{2,1,0:T(8,128)(2,1)S(1)} %collective-permute-done.1.refs_0_), channel_id=1, source_target_pairs={{0,2},{2,0},{1,3},{3,1},{4,6},{6,4},{5,7},{7,5},{8,10},{10,8},{9,1... | collective-permute-start | bytes 393224 | tf_op jit(solution)/shard_map/ppermute | solution.py:235
  22.6 9.6 %collective-permute-start.8 = (bf16[8,16,512]{2,1,0:T(8,128)(2,1)S(1)}, bf16[8,16,512]{2,1,0:T(8,128)(2,1)S(1)}, u32[]{:S(2)}, u32[]{:S(2)}) collective-permute-start(bf16[8,16,512]{2,1,0:T(8,128)(2,1)S(1)} %collective-permute-done.2.refs_0_), channel_id=1, source_target_pairs={{0,2},{2,0},{1,3},{3,1},{4,6},{6,4},{5,7},{7,5},{8,10},{10,8},{9,1... | collective-permute-start | bytes 393224 | tf_op jit(solution)/shard_map/ppermute | solution.py:235
  26.2 15.0 %collective-permute-start.12 = (bf16[8,32,512]{2,1,0:T(8,128)(2,1)S(1)}, bf16[8,32,512]{2,1,0:T(8,128)(2,1)S(1)}, u32[]{:S(2)}, u32[]{:S(2)}) collective-permute-start(bf16[8,32,512]{2,1,0:T(8,128)(2,1)S(1)} %get-tuple-element.84), channel_id=1, source_target_pairs={{0,8},{4,12},{8,0},{12,4},{1,9},{5,13},{9,1},{13,5},{2,10},{6,14},... | collective-permute-start | bytes 786440 | tf_op jit(solution)/shard_map/ppermute | solution.py:232
  30.6 10.7 %collective-permute-start.11 = (bf16[8,32,512]{2,1,0:T(8,128)(2,1)S(1)}, bf16[8,32,512]{2,1,0:T(8,128)(2,1)S(1)}, u32[]{:S(2)}, u32[]{:S(2)}) collective-permute-start(bf16[8,32,512]{2,1,0:T(8,128)(2,1)S(1)} %collective-permute-done.10.refs_0_), channel_id=1, source_target_pairs={{0,2},{2,0},{1,3},{3,1},{4,6},{6,4},{5,7},{7,5},{8,10},{10,8},{9,1... | collective-permute-start | bytes 786440 | tf_op jit(solution)/shard_map/ppermute | solution.py:235
  39.1 3.6 %collective-permute-start.13 = (bf16[24,16,512]{2,1,0:T(8,128)(2,1)S(1)}, bf16[24,16,512]{2,1,0:T(8,128)(2,1)S(1)}, u32[]{:S(2)}, u32[]{:S(2)}) collective-permute-start(bf16[24,16,512]{2,1,0:T(8,128)(2,1)S(1)} %shard_map.69), channel_id=1, source_target_pairs={{0,1},{1,0},{2,3},{3,2},{4,5},{5,4},{6,7},{7,6},{8,9},{9,8},{10,11... | collective-permute-start | bytes 1179656 | tf_op jit(solution)/shard_map/ppermute | solution.py:269
  39.1 8.7 %collective-permute-start.9 = (bf16[8,32,512]{2,1,0:T(8,128)(2,1)S(1)}, bf16[8,32,512]{2,1,0:T(8,128)(2,1)S(1)}, u32[]{:S(2)}, u32[]{:S(2)}) collective-permute-start(bf16[8,32,512]{2,1,0:T(8,128)(2,1)S(1)} %collective-permute-done.5.refs_0_), channel_id=1, source_target_pairs={{0,2},{2,0},{1,3},{3,1},{4,6},{6,4},{5,7},{7,5},{8,10},{10,8},{9,1... | collective-permute-start | bytes 786440 | tf_op jit(solution)/shard_map/ppermute | solution.py:235
  47.8 7.9 %collective-permute-start.17 = (bf16[8,32,512]{2,1,0:T(8,128)(2,1)S(1)}, bf16[8,32,512]{2,1,0:T(8,128)(2,1)S(1)}, u32[]{:S(2)}, u32[]{:S(2)}) collective-permute-start(bf16[8,32,512]{2,1,0:T(8,128)(2,1)S(1)} %get-tuple-element.103.refs_0_), channel_id=1, source_target_pairs={{0,2},{2,0},{1,3},{3,1},{4,6},{6,4},{5,7},{7,5},{8,10},{10,8},{9,1... | collective-permute-start | bytes 786440 | tf_op jit(solution)/shard_map/ppermute | solution.py:235
  49.3 9.7 %collective-permute-start.14 = (bf16[8,16,512]{2,1,0:T(8,128)(2,1)S(1)}, bf16[8,16,512]{2,1,0:T(8,128)(2,1)S(1)}, u32[]{:S(2)}, u32[]{:S(2)}) collective-permute-start(bf16[8,16,512]{2,1,0:T(8,128)(2,1)S(1)} %get-tuple-element.98), channel_id=1, source_target_pairs={{0,8},{4,12},{8,0},{12,4},{1,9},{5,13},{9,1},{13,5},{2,10},{6,14},... | collective-permute-start | bytes 393224 | tf_op jit(solution)/shard_map/ppermute | solution.py:232
  49.3 11.8 %collective-permute-start.15 = (bf16[8,16,512]{2,1,0:T(8,128)(2,1)S(1)}, bf16[8,16,512]{2,1,0:T(8,128)(2,1)S(1)}, u32[]{:S(2)}, u32[]{:S(2)}) collective-permute-start(bf16[8,16,512]{2,1,0:T(8,128)(2,1)S(1)} %get-tuple-element.99), channel_id=1, source_target_pairs={{0,12},{4,8},{8,4},{12,0},{1,13},{5,9},{9,5},{13,1},{2,14},{6,10},... | collective-permute-start | bytes 393224 | tf_op jit(solution)/shard_map/ppermute | solution.py:232
  49.6 11.5 %collective-permute-start.16 = (bf16[8,16,512]{2,1,0:T(8,128)(2,1)S(1)}, bf16[8,16,512]{2,1,0:T(8,128)(2,1)S(1)}, u32[]{:S(2)}, u32[]{:S(2)}) collective-permute-start(bf16[8,16,512]{2,1,0:T(8,128)(2,1)S(1)} %get-tuple-element.100), channel_id=1, source_target_pairs={{0,4},{4,0},{8,12},{12,8},{1,5},{5,1},{9,13},{13,9},{2,6},{6,2},{1... | collective-permute-start | bytes 393224 | tf_op jit(solution)/shard_map/ppermute | solution.py:232
  61.1 2.3 %collective-permute-start.18 = (bf16[24,32,512]{2,1,0:T(8,128)(2,1)S(1)}, bf16[24,32,512]{2,1,0:T(8,128)(2,1)S(1)}, u32[]{:S(2)}, u32[]{:S(2)}) collective-permute-start(bf16[24,32,512]{2,1,0:T(8,128)(2,1)S(1)} %shard_map.77), channel_id=1, source_target_pairs={{0,1},{1,0},{2,3},{3,2},{4,5},{5,4},{6,7},{7,6},{8,9},{9,8},{10,11... | collective-permute-start | bytes 2359304 | tf_op jit(solution)/shard_map/ppermute | solution.py:282
  64.7 11.5 %collective-permute-start.21 = (bf16[8,32,512]{2,1,0:T(8,128)(2,1)S(1)}, bf16[8,32,512]{2,1,0:T(8,128)(2,1)S(1)}, u32[]{:S(2)}, u32[]{:S(2)}) collective-permute-start(bf16[8,32,512]{2,1,0:T(8,128)(2,1)S(1)} %get-tuple-element.116), channel_id=1, source_target_pairs={{0,4},{4,0},{8,12},{12,8},{1,5},{5,1},{9,13},{13,9},{2,6},{6,2},{1... | collective-permute-start | bytes 786440 | tf_op jit(solution)/shard_map/ppermute | solution.py:232
  65.2 20.7 %collective-permute-start.19 = (bf16[8,32,512]{2,1,0:T(8,128)(2,1)S(1)}, bf16[8,32,512]{2,1,0:T(8,128)(2,1)S(1)}, u32[]{:S(2)}, u32[]{:S(2)}) collective-permute-start(bf16[8,32,512]{2,1,0:T(8,128)(2,1)S(1)} %get-tuple-element.113), channel_id=1, source_target_pairs={{0,8},{4,12},{8,0},{12,4},{1,9},{5,13},{9,1},{13,5},{2,10},{6,14},... | collective-permute-start | bytes 786440 | tf_op jit(solution)/shard_map/ppermute | solution.py:232
  67.9 23.2 %collective-permute-start.20 = (bf16[8,32,512]{2,1,0:T(8,128)(2,1)S(1)}, bf16[8,32,512]{2,1,0:T(8,128)(2,1)S(1)}, u32[]{:S(2)}, u32[]{:S(2)}) collective-permute-start(bf16[8,32,512]{2,1,0:T(8,128)(2,1)S(1)} %get-tuple-element.114), channel_id=1, source_target_pairs={{0,12},{4,8},{8,4},{12,0},{1,13},{5,9},{9,5},{13,1},{2,14},{6,10},... | collective-permute-start | bytes 786440 | tf_op jit(solution)/shard_map/ppermute | solution.py:232
  (2 other events, 14.1 us)

commit v13 on v11

--- a/solution.py
+++ b/solution.py
@@ -215,6 +215,7 @@
         out_specs=[anywhere] * len(values),
         out_shape=[jax.ShapeDtypeStruct(value.shape, value.dtype) for value in values],
         input_output_aliases={n: n for n in range(len(values))},
+        compiler_params=pltpu.CompilerParams(vmem_limit_bytes=1024 * 1024),
         cost_estimate=pl.CostEstimate(flops=flops, bytes_accessed=1024, transcendentals=0),
     )(*values)
 
@@ -252,17 +253,18 @@
     a = {j: along_z(cut(j, 0, ROWS), j) for j in (3, 2, 1)}
     mine = [cut(0, 0, rows_all)[n:n + half] for n in (0, half)]
     others = [along_x(part) for part in mine]
-    b, far = {j: cut(j, ROWS, most) for j in (1, 2)}, cut(3, ROWS, most)
+    b = {j: cut(j, ROWS, most) for j in (1, 2, 3)}
     held, down, up = hold(where, tile_mask[0], first_block, beam, eigen_modes[0])
     (a[3], a[2], a[1]), b, others, down, up = fence(((a[3], a[2], a[1]), b, others, down, up))
     b[1], b[2] = along_z(b[1], 1), along_z(b[2], 2)
-    own = project(where, mine, others, held, 0, halves, 200_000_000)
-    skies = [own] + [project(where, [a[j]], [along_x(a[j])], held, j, blocks, 200_000_000) for j in (1, 2, 3)]
+    own = project(where, mine, others, held, 0, halves, 400_000_000)
+    skies = [own] + [project(where, [a[j]], [along_x(a[j])], held, j, blocks, 400_000_000) for j in (1, 2, 3)]
     gone = reduce(down, [leave for _, leave in skies], (0, 0, 0, 0), n_modes)
     stay_a = [stay for stay, _ in skies]
-    b[2], stay_a, gone = fence((b[2], stay_a, gone))
+    b[2], b[3], stay_a, gone = fence((b[2], b[3], stay_a, gone))
     x_2 = along_x(b[2])
-    x_1, b[3] = anchor([along_x(b[1]), along_z(far, 3)], 1_500_000_000)
+    x_1, = anchor([along_x(b[1])], 2_500_000_000)
+    b[3] = along_z(b[3], 3)
     kept = reduce(down, stay_a, (0, 0, 0, 0), n_modes, jnp.float32)
     spots = [(j, 0, freqs) for j in (1, 2, 3, 0)]
     outs = restore(kept, lax.ppermute(gone, "pol", other), ratios, up, spots)

time: 98.7 us -> 89.8 us (0.910)
  local copies, waits for them, and re-layouts: 9.14 us -> 2.39 us
  Pallas kernels: 28 us -> 25.1 us
    unnamed x19 -> x9, local copies, waits for them, and re-layouts: 6.85 us -> 0.1 us
    ppermute x8, waiting for transfers between devices: 1.12 us -> 5.8 us  [along_x(): return lax.ppermute(value, 'kl', other)]
    ppermute x12, waiting for transfers between devices: 30.9 us -> 26.9 us  [along_z(): return lax.ppermute(value, 'fm', [(i, i ^ j) for i in range(parts)])]
    pallas_call x7, Pallas kernels: 12.7 us -> 9.57 us  [project(): pl.pallas_call(functools.partial(project_kernel, piece=piece, blocks=bloc...]
  transfers between devices with their start and end apart: 22 -> 22, of which waited for: 10 -> 9; matrix products, arithmetic and copies ran while one was open for 1% -> 1% of each run, Pallas kernels for 26% -> 25%
where the time goes in v13:
time: 89.8 us; the launch traced here: 89.5 us
  waiting for transfers between devices  35 us (39%)
  starting transfers between devices  26.1 us (29%)
  Pallas kernels  25.1 us (28%)
  local copies, waits for them, and re-layouts  2.39 us (3%)
  between operations  0.94 us (1%)
    ppermute x12, waiting for transfers between devices, along_z(): return lax.ppermute(value, 'fm', [(i, i ^ j) for i in range(parts)])  26.9 us
    ppermute x12, starting transfers between devices, along_z(): return lax.ppermute(value, 'fm', [(i, i ^ j) for i in range(parts)])  15 us
    ppermute x8, starting transfers between devices, along_x(): return lax.ppermute(value, 'kl', other)  11 us
    pallas_call x7, Pallas kernels, project(): pl.pallas_call(functools.partial(project_kernel, piece=piece, blocks=bloc...  9.57 us
    pallas_call x1, Pallas kernels, hold(): pl.pallas_call(hold_kernel, grid_spec=pltpu.PrefetchScalarGridSpec(num_sc...  7.04 us
    ppermute x8, waiting for transfers between devices, along_x(): return lax.ppermute(value, 'kl', other)  5.8 us
    pallas_call x3, Pallas kernels, place(): pl.pallas_call(functools.partial(place_kernel, spots=spots, first=first),...  4.06 us
    pallas_call x4, Pallas kernels, reduce(): pl.pallas_call(reduce_kernel, grid=(rows // ROWS,), in_specs=[fixed(modes...  2.62 us
  transfers between devices with their start and end apart: 22, of which 9 were waited for; matrix products, arithmetic and copies ran while one was open for 1% of the time, Pallas kernels for 25%

profile of v13, /device:TPU:12, one launch (start us, length us, event | category | flops | bytes accessed | tf_op | source)
XLA Modules:
  0.0 89.5 jit_solution(8690767988987552962)
XLA Ops:
  1.1 1.6 %collective-permute-start = (bf16[8,16,512]{2,1,0:T(8,128)(2,1)S(1)}, bf16[8,16,512]{2,1,0:T(8,128)(2,1)S(1)}, u32[]{:S(2)}, u32[]{:S(2)}) collective-permute-start(bf16[8,16,512]{2,1,0:T(8,128)(2,1)S(1)} %get-tuple-element.126), channel_id=1, source_target_pairs={{0,12},{4,8},{8,4},{12,0},{1,13},{5,9},{9,5},{13,1},{2,14},{6,10},... | collective-permute-start | bytes 393224 | tf_op jit(solution)/shard_map/ppermute | solution.py:232
  6.3 1.6 %collective-permute-start.3 = (bf16[4,48,512]{2,1,0:T(8,128)(2,1)S(1)}, bf16[4,48,512]{2,1,0:T(8,128)(2,1)S(1)}, u32[]{:S(2)}, u32[]{:S(2)}) collective-permute-start(bf16[4,48,512]{2,1,0:T(8,128)(2,1)S(1)} %get-tuple-element.120.refs_0_), channel_id=1, source_target_pairs={{0,2},{2,0},{1,3},{3,1},{4,6},{6,4},{5,7},{7,5},{8,10},{10,8},{9,1... | collective-permute-start | bytes 589832 | tf_op jit(solution)/shard_map/ppermute | solution.py:235
  9.1 7.0 %shard_map.64 = (bf16[32,512,512]{2,1,0:T(8,128)(2,1)S(1)}, bf16[384,512]{1,0:T(8,128)(2,1)S(1)}, bf16[512,384]{1,0:T(8,128)(2,1)S(1)}) custom-call(s32[6]{0:T(128)S(1)} %compare_select_fusion.1.where, s32[4,4]{1,0:T(4,128)S(1)} %bitcast.27, s32[1]{0:T(128)S(6)} %copy.18.starts, bf16[32,512,512]{2,1,0:T(8,128)(2,1)} %bitcast.28, bf16[32,24]{1,0:T(8,128)(2,1)S(1)} %bitcast.26), custom_call_target="tpu_custom_call" | custom-call | flops 1024 | bytes 1024 | tf_op jit(solution)/shard_map/pallas_call | solution.py:63
  17.3 2.3 %collective-permute-start.5 = (bf16[8,32,512]{2,1,0:T(8,128)(2,1)S(1)}, bf16[8,32,512]{2,1,0:T(8,128)(2,1)S(1)}, u32[]{:S(2)}, u32[]{:S(2)}) collective-permute-start(bf16[8,32,512]{2,1,0:T(8,128)(2,1)S(1)} %get-tuple-element.65), channel_id=1, source_target_pairs={{0,8},{4,12},{8,0},{12,4},{1,9},{5,13},{9,1},{13,5},{2,10},{6,14},... | collective-permute-start | bytes 786440 | tf_op jit(solution)/shard_map/ppermute | solution.py:232
  19.6 1.5 %collective-permute-start.6 = (bf16[8,16,512]{2,1,0:T(8,128)(2,1)S(1)}, bf16[8,16,512]{2,1,0:T(8,128)(2,1)S(1)}, u32[]{:S(2)}, u32[]{:S(2)}) collective-permute-start(bf16[8,16,512]{2,1,0:T(8,128)(2,1)S(1)} %collective-permute-done.2.refs_0_), channel_id=1, source_target_pairs={{0,2},{2,0},{1,3},{3,1},{4,6},{6,4},{5,7},{7,5},{8,10},{10,8},{9,1... | collective-permute-start | bytes 393224 | tf_op jit(solution)/shard_map/ppermute | solution.py:235
  21.6 1.5 %collective-permute-start.8 = (bf16[8,16,512]{2,1,0:T(8,128)(2,1)S(1)}, bf16[8,16,512]{2,1,0:T(8,128)(2,1)S(1)}, u32[]{:S(2)}, u32[]{:S(2)}) collective-permute-start(bf16[8,16,512]{2,1,0:T(8,128)(2,1)S(1)} %collective-permute-done.refs_0_), channel_id=1, source_target_pairs={{0,2},{2,0},{1,3},{3,1},{4,6},{6,4},{5,7},{7,5},{8,10},{10,8},{9,1... | collective-permute-start | bytes 393224 | tf_op jit(solution)/shard_map/ppermute | solution.py:235
  27.2 1.4 %shard_map.67 = (bf16[8,16,512]{2,1,0:T(8,128)(2,1)S(1)}, bf16[8,16,512]{2,1,0:T(8,128)(2,1)S(1)}) custom-call(s32[6]{0:T(128)S(1)} %compare_select_fusion.1.where, bf16[8,16,512]{2,1,0:T(8,128)(2,1)S(1)} %collective-permute-done.1.refs_0_, bf16[8,16,512]{2,1,0:T(8,128)(2,1)S(1)} %collective-permute-done.7.refs_1_, ...), custom_call_target="tpu_custom_call" | custom-call | flops 400000000 | bytes 1024 | tf_op jit(solution)/shard_map/pallas_call | solution.py:102
  28.5 1.6 %collective-permute-start.13 = (bf16[8,32,512]{2,1,0:T(8,128)(2,1)S(1)}, bf16[8,32,512]{2,1,0:T(8,128)(2,1)S(1)}, u32[]{:S(2)}, u32[]{:S(2)}) collective-permute-start(bf16[8,32,512]{2,1,0:T(8,128)(2,1)S(1)} %collective-permute-done.10.refs_0_), channel_id=1, source_target_pairs={{0,2},{2,0},{1,3},{3,1},{4,6},{6,4},{5,7},{7,5},{8,10},{10,8},{9,1... | collective-permute-start | bytes 786440 | tf_op jit(solution)/shard_map/ppermute | solution.py:235
  31.8 1.4 %collective-permute-start.9 = (bf16[8,32,512]{2,1,0:T(8,128)(2,1)S(1)}, bf16[8,32,512]{2,1,0:T(8,128)(2,1)S(1)}, u32[]{:S(2)}, u32[]{:S(2)}) collective-permute-start(bf16[8,32,512]{2,1,0:T(8,128)(2,1)S(1)} %collective-permute-done.5.refs_0_), channel_id=1, source_target_pairs={{0,2},{2,0},{1,3},{3,1},{4,6},{6,4},{5,7},{7,5},{8,10},{10,8},{9,1... | collective-permute-start | bytes 786440 | tf_op jit(solution)/shard_map/ppermute | solution.py:235
  33.3 3.7 %collective-permute-done.13.refs_0_ = bf16[8,32,512]{2,1,0:T(8,128)(2,1)S(1)} collective-permute-done((bf16[8,32,512]{2,1,0:T(8,128)(2,1)S(1)}, bf16[8,32,512]{2,1,0:T(8,128)(2,1)S(1)}, u32[]{:S(2)}, u32[]{:S(2)}) %collective-permute-start.13) | collective-permute-done | bytes 262176 | tf_op jit(solution)/shard_map/ppermute | solution.py:235
  37.4 1.4 %shard_map.73 = (bf16[8,32,512]{2,1,0:T(8,128)(2,1)S(1)}, bf16[8,32,512]{2,1,0:T(8,128)(2,1)S(1)}) custom-call(s32[6]{0:T(128)S(1)} %compare_select_fusion.1.where, bf16[8,32,512]{2,1,0:T(8,128)(2,1)S(1)} %collective-permute-done.10.refs_0_, bf16[8,32,512]{2,1,0:T(8,128)(2,1)S(1)} %shard_map.72.refs_1_, ...), custom_call_target="tpu_custom_call" | custom-call | flops 1024 | bytes 1024 | tf_op jit(solution)/shard_map/pallas_call | solution.py:102
  39.8 6.7 %collective-permute-done.11.refs_0_ = bf16[8,32,512]{2,1,0:T(8,128)(2,1)S(1)} collective-permute-done((bf16[8,32,512]{2,1,0:T(8,128)(2,1)S(1)}, bf16[8,32,512]{2,1,0:T(8,128)(2,1)S(1)}, u32[]{:S(2)}, u32[]{:S(2)}) %collective-permute-start.11) | collective-permute-done | bytes 262176 | tf_op jit(solution)/shard_map/ppermute | solution.py:232
  46.5 2.4 %collective-permute-start.17 = (bf16[8,32,512]{2,1,0:T(8,128)(2,1)S(1)}, bf16[8,32,512]{2,1,0:T(8,128)(2,1)S(1)}, u32[]{:S(2)}, u32[]{:S(2)}) collective-permute-start(bf16[8,32,512]{2,1,0:T(8,128)(2,1)S(1)} %collective-permute-done.11.refs_0_), channel_id=1, source_target_pairs={{0,2},{2,0},{1,3},{3,1},{4,6},{6,4},{5,7},{7,5},{8,10},{10,8},{9,1... | collective-permute-start | bytes 786440 | tf_op jit(solution)/shard_map/ppermute | solution.py:235
  48.9 1.8 %collective-permute-start.15 = (bf16[8,16,512]{2,1,0:T(8,128)(2,1)S(1)}, bf16[8,16,512]{2,1,0:T(8,128)(2,1)S(1)}, u32[]{:S(2)}, u32[]{:S(2)}) collective-permute-start(bf16[8,16,512]{2,1,0:T(8,128)(2,1)S(1)} %get-tuple-element.97), channel_id=1, source_target_pairs={{0,12},{4,8},{8,4},{12,0},{1,13},{5,9},{9,5},{13,1},{2,14},{6,10},... | collective-permute-start | bytes 393224 | tf_op jit(solution)/shard_map/ppermute | solution.py:232
  50.7 2.6 %collective-permute-start.16 = (bf16[8,16,512]{2,1,0:T(8,128)(2,1)S(1)}, bf16[8,16,512]{2,1,0:T(8,128)(2,1)S(1)}, u32[]{:S(2)}, u32[]{:S(2)}) collective-permute-start(bf16[8,16,512]{2,1,0:T(8,128)(2,1)S(1)} %get-tuple-element.98), channel_id=1, source_target_pairs={{0,4},{4,0},{8,12},{12,8},{1,5},{5,1},{9,13},{13,9},{2,6},{6,2},{1... | collective-permute-start | bytes 393224 | tf_op jit(solution)/shard_map/ppermute | solution.py:232
  53.3 1.4 %shard_map.74 = (bf16[8,32,512]{2,1,0:T(8,128)(2,1)S(1)}, bf16[8,32,512]{2,1,0:T(8,128)(2,1)S(1)}) custom-call(s32[6]{0:T(128)S(1)} %compare_select_fusion.1.where, bf16[8,32,512]{2,1,0:T(8,128)(2,1)S(1)} %collective-permute-done.5.refs_0_, bf16[8,32,512]{2,1,0:T(8,128)(2,1)S(1)} %collective-permute-done.9.refs_1_, ...), custom_call_target="tpu_custom_call" | custom-call | flops 1024 | bytes 1024 | tf_op jit(solution)/shard_map/pallas_call | solution.py:102
  54.7 1.4 %shard_map.75 = (bf16[8,32,512]{2,1,0:T(8,128)(2,1)S(1)}, bf16[8,32,512]{2,1,0:T(8,128)(2,1)S(1)}) custom-call(s32[6]{0:T(128)S(1)} %compare_select_fusion.1.where, bf16[8,32,512]{2,1,0:T(8,128)(2,1)S(1)} %collective-permute-done.11.refs_0_, bf16[8,32,512]{2,1,0:T(8,128)(2,1)S(1)} %collective-permute-done.17.refs_1_, ...), custom_call_target="tpu_custom_call" | custom-call | flops 1024 | bytes 1024 | tf_op jit(solution)/shard_map/pallas_call | solution.py:102
  58.1 2.3 %collective-permute-done.18.came_ref = bf16[24,32,512]{2,1,0:T(8,128)(2,1)S(1)} collective-permute-done((bf16[24,32,512]{2,1,0:T(8,128)(2,1)S(1)}, bf16[24,32,512]{2,1,0:T(8,128)(2,1)S(1)}, u32[]{:S(2)}, u32[]{:S(2)}) %collective-permute-start.18) | collective-permute-done | bytes 786464 | tf_op jit(solution)/shard_map/ppermute | solution.py:282
  61.6 1.7 %collective-permute-start.21 = (bf16[8,32,512]{2,1,0:T(8,128)(2,1)S(1)}, bf16[8,32,512]{2,1,0:T(8,128)(2,1)S(1)}, u32[]{:S(2)}, u32[]{:S(2)}) collective-permute-start(bf16[8,32,512]{2,1,0:T(8,128)(2,1)S(1)} %get-tuple-element.114), channel_id=1, source_target_pairs={{0,4},{4,0},{8,12},{12,8},{1,5},{5,1},{9,13},{13,9},{2,6},{6,2},{1... | collective-permute-start | bytes 786440 | tf_op jit(solution)/shard_map/ppermute | solution.py:232
  63.3 1.6 %collective-permute-start.19 = (bf16[8,32,512]{2,1,0:T(8,128)(2,1)S(1)}, bf16[8,32,512]{2,1,0:T(8,128)(2,1)S(1)}, u32[]{:S(2)}, u32[]{:S(2)}) collective-permute-start(bf16[8,32,512]{2,1,0:T(8,128)(2,1)S(1)} %get-tuple-element.111), channel_id=1, source_target_pairs={{0,8},{4,12},{8,0},{12,4},{1,9},{5,13},{9,1},{13,5},{2,10},{6,14},... | collective-permute-start | bytes 786440 | tf_op jit(solution)/shard_map/ppermute | solution.py:232
  65.2 1.4 %shard_map.79.refs_2_ = bf16[8,4,48,512]{3,2,1,0:T(8,128)(2,1)} custom-call(s32[6]{0:T(128)S(1)} %compare_select_fusion.1.where, bf16[8,16,512]{2,1,0:T(8,128)(2,1)S(1)} %collective-permute-done.16.refs_0_, bf16[8,16,512]{2,1,0:T(8,128)(2,1)S(1)} %collective-permute-done.14.refs_1_, bf16[8,16,512]{2,1,0:T(8,128)(2,1)S(1)} %collective-permute-done.15.refs_2_, ...), custom_call_target="tpu_custom_call" | custom-call | flops 1024 | bytes 1024 | tf_op jit(solution)/shard_map/pallas_call | solution.py:190
  66.5 7.7 %collective-permute-done.21.refs_1_ = bf16[8,32,512]{2,1,0:T(8,128)(2,1)S(1)} collective-permute-done((bf16[8,32,512]{2,1,0:T(8,128)(2,1)S(1)}, bf16[8,32,512]{2,1,0:T(8,128)(2,1)S(1)}, u32[]{:S(2)}, u32[]{:S(2)}) %collective-permute-start.21) | collective-permute-done | bytes 262176 | tf_op jit(solution)/shard_map/ppermute | solution.py:232
  75.6 7.2 %collective-permute-done.19.refs_0_ = bf16[8,32,512]{2,1,0:T(8,128)(2,1)S(1)} collective-permute-done((bf16[8,32,512]{2,1,0:T(8,128)(2,1)S(1)}, bf16[8,32,512]{2,1,0:T(8,128)(2,1)S(1)}, u32[]{:S(2)}, u32[]{:S(2)}) %collective-permute-start.19) | collective-permute-done | bytes 262176 | tf_op jit(solution)/shard_map/ppermute | solution.py:232
  82.9 5.3 %collective-permute-done.20.refs_1_ = bf16[8,32,512]{2,1,0:T(8,128)(2,1)S(1)} collective-permute-done((bf16[8,32,512]{2,1,0:T(8,128)(2,1)S(1)}, bf16[8,32,512]{2,1,0:T(8,128)(2,1)S(1)}, u32[]{:S(2)}, u32[]{:S(2)}) %collective-permute-start.20) | collective-permute-done | bytes 262176 | tf_op jit(solution)/shard_map/ppermute | solution.py:232
  (53 shorter events, 20.2 us)
Async XLA Ops:
  0.0 9.0 %copy-start.2 = (bf16[1,32,24]{1,2,0:T(8,128)(2,1)S(1)}, bf16[1,32,24]{1,2,0:T(8,128)(2,1)}, u32[]{:S(2)}) copy-start(bf16[1,32,24]{1,2,0:T(8,128)(2,1)} %param.10) | copy-start | bytes 4612
  0.0 9.1 %copy-start = (s32[1,4,4]{2,1,0:T(4,128)S(1)}, s32[1,4,4]{2,1,0:T(4,128)}, u32[]{:S(2)}) copy-start(s32[1,4,4]{2,1,0:T(4,128)} %param.8) | copy-start | bytes 196
  1.1 15.2 %collective-permute-start = (bf16[8,16,512]{2,1,0:T(8,128)(2,1)S(1)}, bf16[8,16,512]{2,1,0:T(8,128)(2,1)S(1)}, u32[]{:S(2)}, u32[]{:S(2)}) collective-permute-start(bf16[8,16,512]{2,1,0:T(8,128)(2,1)S(1)} %get-tuple-element.126), channel_id=1, source_target_pairs={{0,12},{4,8},{8,4},{12,0},{1,13},{5,9},{9,5},{13,1},{2,14},{6,10},... | collective-permute-start | bytes 393224 | tf_op jit(solution)/shard_map/ppermute | solution.py:232
  2.7 13.5 %collective-permute-start.1 = (bf16[8,16,512]{2,1,0:T(8,128)(2,1)S(1)}, bf16[8,16,512]{2,1,0:T(8,128)(2,1)S(1)}, u32[]{:S(2)}, u32[]{:S(2)}) collective-permute-start(bf16[8,16,512]{2,1,0:T(8,128)(2,1)S(1)} %get-tuple-element.125), channel_id=1, source_target_pairs={{0,8},{4,12},{8,0},{12,4},{1,9},{5,13},{9,1},{13,5},{2,10},{6,14},... | collective-permute-start | bytes 393224 | tf_op jit(solution)/shard_map/ppermute | solution.py:232
  4.0 12.3 %collective-permute-start.2 = (bf16[8,16,512]{2,1,0:T(8,128)(2,1)S(1)}, bf16[8,16,512]{2,1,0:T(8,128)(2,1)S(1)}, u32[]{:S(2)}, u32[]{:S(2)}) collective-permute-start(bf16[8,16,512]{2,1,0:T(8,128)(2,1)S(1)} %get-tuple-element.124), channel_id=1, source_target_pairs={{0,4},{4,0},{8,12},{12,8},{1,5},{5,1},{9,13},{13,9},{2,6},{6,2},{1... | collective-permute-start | bytes 393224 | tf_op jit(solution)/shard_map/ppermute | solution.py:232
  6.3 10.0 %collective-permute-start.3 = (bf16[4,48,512]{2,1,0:T(8,128)(2,1)S(1)}, bf16[4,48,512]{2,1,0:T(8,128)(2,1)S(1)}, u32[]{:S(2)}, u32[]{:S(2)}) collective-permute-start(bf16[4,48,512]{2,1,0:T(8,128)(2,1)S(1)} %get-tuple-element.120.refs_0_), channel_id=1, source_target_pairs={{0,2},{2,0},{1,3},{3,1},{4,6},{6,4},{5,7},{7,5},{8,10},{10,8},{9,1... | collective-permute-start | bytes 589832 | tf_op jit(solution)/shard_map/ppermute | solution.py:235
  7.8 8.8 %collective-permute-start.4 = (bf16[4,48,512]{2,1,0:T(8,128)(2,1)S(1)}, bf16[4,48,512]{2,1,0:T(8,128)(2,1)S(1)}, u32[]{:S(2)}, u32[]{:S(2)}) collective-permute-start(bf16[4,48,512]{2,1,0:T(8,128)(2,1)S(1)} %get-tuple-element.119.refs_1_), channel_id=1, source_target_pairs={{0,2},{2,0},{1,3},{3,1},{4,6},{6,4},{5,7},{7,5},{8,10},{10,8},{9,1... | collective-permute-start | bytes 589832 | tf_op jit(solution)/shard_map/ppermute | solution.py:235
  16.6 11.9 %collective-permute-start.10 = (bf16[8,32,512]{2,1,0:T(8,128)(2,1)S(1)}, bf16[8,32,512]{2,1,0:T(8,128)(2,1)S(1)}, u32[]{:S(2)}, u32[]{:S(2)}) collective-permute-start(bf16[8,32,512]{2,1,0:T(8,128)(2,1)S(1)} %get-tuple-element.83), channel_id=1, source_target_pairs={{0,4},{4,0},{8,12},{12,8},{1,5},{5,1},{9,13},{13,9},{2,6},{6,2},{1... | collective-permute-start | bytes 786440 | tf_op jit(solution)/shard_map/ppermute | solution.py:232
  17.3 14.6 %collective-permute-start.5 = (bf16[8,32,512]{2,1,0:T(8,128)(2,1)S(1)}, bf16[8,32,512]{2,1,0:T(8,128)(2,1)S(1)}, u32[]{:S(2)}, u32[]{:S(2)}) collective-permute-start(bf16[8,32,512]{2,1,0:T(8,128)(2,1)S(1)} %get-tuple-element.65), channel_id=1, source_target_pairs={{0,8},{4,12},{8,0},{12,4},{1,9},{5,13},{9,1},{13,5},{2,10},{6,14},... | collective-permute-start | bytes 786440 | tf_op jit(solution)/shard_map/ppermute | solution.py:232
  19.6 6.2 %collective-permute-start.6 = (bf16[8,16,512]{2,1,0:T(8,128)(2,1)S(1)}, bf16[8,16,512]{2,1,0:T(8,128)(2,1)S(1)}, u32[]{:S(2)}, u32[]{:S(2)}) collective-permute-start(bf16[8,16,512]{2,1,0:T(8,128)(2,1)S(1)} %collective-permute-done.2.refs_0_), channel_id=1, source_target_pairs={{0,2},{2,0},{1,3},{3,1},{4,6},{6,4},{5,7},{7,5},{8,10},{10,8},{9,1... | collective-permute-start | bytes 393224 | tf_op jit(solution)/shard_map/ppermute | solution.py:235
  21.0 6.1 %collective-permute-start.7 = (bf16[8,16,512]{2,1,0:T(8,128)(2,1)S(1)}, bf16[8,16,512]{2,1,0:T(8,128)(2,1)S(1)}, u32[]{:S(2)}, u32[]{:S(2)}) collective-permute-start(bf16[8,16,512]{2,1,0:T(8,128)(2,1)S(1)} %collective-permute-done.1.refs_0_), channel_id=1, source_target_pairs={{0,2},{2,0},{1,3},{3,1},{4,6},{6,4},{5,7},{7,5},{8,10},{10,8},{9,1... | collective-permute-start | bytes 393224 | tf_op jit(solution)/shard_map/ppermute | solution.py:235
  21.6 8.5 %collective-permute-start.8 = (bf16[8,16,512]{2,1,0:T(8,128)(2,1)S(1)}, bf16[8,16,512]{2,1,0:T(8,128)(2,1)S(1)}, u32[]{:S(2)}, u32[]{:S(2)}) collective-permute-start(bf16[8,16,512]{2,1,0:T(8,128)(2,1)S(1)} %collective-permute-done.refs_0_), channel_id=1, source_target_pairs={{0,2},{2,0},{1,3},{3,1},{4,6},{6,4},{5,7},{7,5},{8,10},{10,8},{9,1... | collective-permute-start | bytes 393224 | tf_op jit(solution)/shard_map/ppermute | solution.py:235
  28.5 8.5 %collective-permute-start.13 = (bf16[8,32,512]{2,1,0:T(8,128)(2,1)S(1)}, bf16[8,32,512]{2,1,0:T(8,128)(2,1)S(1)}, u32[]{:S(2)}, u32[]{:S(2)}) collective-permute-start(bf16[8,32,512]{2,1,0:T(8,128)(2,1)S(1)} %collective-permute-done.10.refs_0_), channel_id=1, source_target_pairs={{0,2},{2,0},{1,3},{3,1},{4,6},{6,4},{5,7},{7,5},{8,10},{10,8},{9,1... | collective-permute-start | bytes 786440 | tf_op jit(solution)/shard_map/ppermute | solution.py:235
  31.8 7.9 %collective-permute-start.9 = (bf16[8,32,512]{2,1,0:T(8,128)(2,1)S(1)}, bf16[8,32,512]{2,1,0:T(8,128)(2,1)S(1)}, u32[]{:S(2)}, u32[]{:S(2)}) collective-permute-start(bf16[8,32,512]{2,1,0:T(8,128)(2,1)S(1)} %collective-permute-done.5.refs_0_), channel_id=1, source_target_pairs={{0,2},{2,0},{1,3},{3,1},{4,6},{6,4},{5,7},{7,5},{8,10},{10,8},{9,1... | collective-permute-start | bytes 786440 | tf_op jit(solution)/shard_map/ppermute | solution.py:235
  33.3 13.2 %collective-permute-start.11 = (bf16[8,32,512]{2,1,0:T(8,128)(2,1)S(1)}, bf16[8,32,512]{2,1,0:T(8,128)(2,1)S(1)}, u32[]{:S(2)}, u32[]{:S(2)}) collective-permute-start(bf16[8,32,512]{2,1,0:T(8,128)(2,1)S(1)} %get-tuple-element.84), channel_id=1, source_target_pairs={{0,12},{4,8},{8,4},{12,0},{1,13},{5,9},{9,5},{13,1},{2,14},{6,10},... | collective-permute-start | bytes 786440 | tf_op jit(solution)/shard_map/ppermute | solution.py:232
  33.3 5.5 %collective-permute-start.12 = (bf16[24,16,512]{2,1,0:T(8,128)(2,1)S(1)}, bf16[24,16,512]{2,1,0:T(8,128)(2,1)S(1)}, u32[]{:S(2)}, u32[]{:S(2)}) collective-permute-start(bf16[24,16,512]{2,1,0:T(8,128)(2,1)S(1)} %shard_map.69), channel_id=1, source_target_pairs={{0,1},{1,0},{2,3},{3,2},{4,5},{5,4},{6,7},{7,6},{8,9},{9,8},{10,11... | collective-permute-start | bytes 1179656 | tf_op jit(solution)/shard_map/ppermute | solution.py:270
  46.5 8.2 %collective-permute-start.17 = (bf16[8,32,512]{2,1,0:T(8,128)(2,1)S(1)}, bf16[8,32,512]{2,1,0:T(8,128)(2,1)S(1)}, u32[]{:S(2)}, u32[]{:S(2)}) collective-permute-start(bf16[8,32,512]{2,1,0:T(8,128)(2,1)S(1)} %collective-permute-done.11.refs_0_), channel_id=1, source_target_pairs={{0,2},{2,0},{1,3},{3,1},{4,6},{6,4},{5,7},{7,5},{8,10},{10,8},{9,1... | collective-permute-start | bytes 786440 | tf_op jit(solution)/shard_map/ppermute | solution.py:235
  48.9 9.1 %collective-permute-start.14 = (bf16[8,16,512]{2,1,0:T(8,128)(2,1)S(1)}, bf16[8,16,512]{2,1,0:T(8,128)(2,1)S(1)}, u32[]{:S(2)}, u32[]{:S(2)}) collective-permute-start(bf16[8,16,512]{2,1,0:T(8,128)(2,1)S(1)} %get-tuple-element.96), channel_id=1, source_target_pairs={{0,8},{4,12},{8,0},{12,4},{1,9},{5,13},{9,1},{13,5},{2,10},{6,14},... | collective-permute-start | bytes 393224 | tf_op jit(solution)/shard_map/ppermute | solution.py:232
  48.9 9.1 %collective-permute-start.15 = (bf16[8,16,512]{2,1,0:T(8,128)(2,1)S(1)}, bf16[8,16,512]{2,1,0:T(8,128)(2,1)S(1)}, u32[]{:S(2)}, u32[]{:S(2)}) collective-permute-start(bf16[8,16,512]{2,1,0:T(8,128)(2,1)S(1)} %get-tuple-element.97), channel_id=1, source_target_pairs={{0,12},{4,8},{8,4},{12,0},{1,13},{5,9},{9,5},{13,1},{2,14},{6,10},... | collective-permute-start | bytes 393224 | tf_op jit(solution)/shard_map/ppermute | solution.py:232
  50.7 7.3 %collective-permute-start.16 = (bf16[8,16,512]{2,1,0:T(8,128)(2,1)S(1)}, bf16[8,16,512]{2,1,0:T(8,128)(2,1)S(1)}, u32[]{:S(2)}, u32[]{:S(2)}) collective-permute-start(bf16[8,16,512]{2,1,0:T(8,128)(2,1)S(1)} %get-tuple-element.98), channel_id=1, source_target_pairs={{0,4},{4,0},{8,12},{12,8},{1,5},{5,1},{9,13},{13,9},{2,6},{6,2},{1... | collective-permute-start | bytes 393224 | tf_op jit(solution)/shard_map/ppermute | solution.py:232
  58.0 2.4 %collective-permute-start.18 = (bf16[24,32,512]{2,1,0:T(8,128)(2,1)S(1)}, bf16[24,32,512]{2,1,0:T(8,128)(2,1)S(1)}, u32[]{:S(2)}, u32[]{:S(2)}) collective-permute-start(bf16[24,32,512]{2,1,0:T(8,128)(2,1)S(1)} %shard_map.77), channel_id=1, source_target_pairs={{0,1},{1,0},{2,3},{3,2},{4,5},{5,4},{6,7},{7,6},{8,9},{9,8},{10,11... | collective-permute-start | bytes 2359304 | tf_op jit(solution)/shard_map/ppermute | solution.py:282
  61.6 12.6 %collective-permute-start.21 = (bf16[8,32,512]{2,1,0:T(8,128)(2,1)S(1)}, bf16[8,32,512]{2,1,0:T(8,128)(2,1)S(1)}, u32[]{:S(2)}, u32[]{:S(2)}) collective-permute-start(bf16[8,32,512]{2,1,0:T(8,128)(2,1)S(1)} %get-tuple-element.114), channel_id=1, source_target_pairs={{0,4},{4,0},{8,12},{12,8},{1,5},{5,1},{9,13},{13,9},{2,6},{6,2},{1... | collective-permute-start | bytes 786440 | tf_op jit(solution)/shard_map/ppermute | solution.py:232
  63.3 19.6 %collective-permute-start.19 = (bf16[8,32,512]{2,1,0:T(8,128)(2,1)S(1)}, bf16[8,32,512]{2,1,0:T(8,128)(2,1)S(1)}, u32[]{:S(2)}, u32[]{:S(2)}) collective-permute-start(bf16[8,32,512]{2,1,0:T(8,128)(2,1)S(1)} %get-tuple-element.111), channel_id=1, source_target_pairs={{0,8},{4,12},{8,0},{12,4},{1,9},{5,13},{9,1},{13,5},{2,10},{6,14},... | collective-permute-start | bytes 786440 | tf_op jit(solution)/shard_map/ppermute | solution.py:232
  64.9 23.2 %collective-permute-start.20 = (bf16[8,32,512]{2,1,0:T(8,128)(2,1)S(1)}, bf16[8,32,512]{2,1,0:T(8,128)(2,1)S(1)}, u32[]{:S(2)}, u32[]{:S(2)}) collective-permute-start(bf16[8,32,512]{2,1,0:T(8,128)(2,1)S(1)} %get-tuple-element.112), channel_id=1, source_target_pairs={{0,12},{4,8},{8,4},{12,0},{1,13},{5,9},{9,5},{13,1},{2,14},{6,10},... | collective-permute-start | bytes 786440 | tf_op jit(solution)/shard_map/ppermute | solution.py:232
  (2 other events, 8.9 us)

commit v14 on v13

--- a/solution.py
+++ b/solution.py
@@ -257,13 +257,13 @@
     held, down, up = hold(where, tile_mask[0], first_block, beam, eigen_modes[0])
     (a[3], a[2], a[1]), b, others, down, up = fence(((a[3], a[2], a[1]), b, others, down, up))
     b[1], b[2] = along_z(b[1], 1), along_z(b[2], 2)
-    own = project(where, mine, others, held, 0, halves, 400_000_000)
-    skies = [own] + [project(where, [a[j]], [along_x(a[j])], held, j, blocks, 400_000_000) for j in (1, 2, 3)]
+    own = project(where, mine, others, held, 0, halves, 200_000_000)
+    skies = [own] + [project(where, [a[j]], [along_x(a[j])], held, j, blocks, 200_000_000) for j in (1, 2, 3)]
     gone = reduce(down, [leave for _, leave in skies], (0, 0, 0, 0), n_modes)
     stay_a = [stay for stay, _ in skies]
     b[2], b[3], stay_a, gone = fence((b[2], b[3], stay_a, gone))
     x_2 = along_x(b[2])
-    x_1, = anchor([along_x(b[1])], 2_500_000_000)
+    x_1, = anchor([along_x(b[1])], 1_500_000_000)
     b[3] = along_z(b[3], 3)
     kept = reduce(down, stay_a, (0, 0, 0, 0), n_modes, jnp.float32)
     spots = [(j, 0, freqs) for j in (1, 2, 3, 0)]

time: 89.8 us -> 91.2 us (1.016)
  waiting for transfers between devices: 35 us -> 38.4 us
  starting transfers between devices: 26.1 us -> 24.3 us
    ppermute x8, waiting for transfers between devices: 5.8 us -> 7.69 us  [along_x(): return lax.ppermute(value, 'kl', other)]
    ppermute x8, starting transfers between devices: 11 us -> 9.26 us  [along_x(): return lax.ppermute(value, 'kl', other)]
    ppermute x12, waiting for transfers between devices: 26.9 us -> 28.4 us  [along_z(): return lax.ppermute(value, 'fm', [(i, i ^ j) for i in range(parts)])]
  transfers between devices with their start and end apart: 22 -> 22, of which waited for: 9 -> 11; matrix products, arithmetic and copies ran while one was open for 1% -> 1% of each run, Pallas kernels for 25% -> 25%
where the time goes in v14:
time: 91.2 us; the launch traced here: 91.1 us
  waiting for transfers between devices  38.4 us (42%)
  Pallas kernels  25.1 us (28%)
  starting transfers between devices  24.3 us (27%)
  local copies, waits for them, and re-layouts  2.39 us (3%)
    ppermute x12, waiting for transfers between devices, along_z(): return lax.ppermute(value, 'fm', [(i, i ^ j) for i in range(parts)])  28.4 us
    ppermute x12, starting transfers between devices, along_z(): return lax.ppermute(value, 'fm', [(i, i ^ j) for i in range(parts)])  15 us
    pallas_call x7, Pallas kernels, project(): pl.pallas_call(functools.partial(project_kernel, piece=piece, blocks=bloc...  9.57 us
    ppermute x8, starting transfers between devices, along_x(): return lax.ppermute(value, 'kl', other)  9.26 us
    ppermute x8, waiting for transfers between devices, along_x(): return lax.ppermute(value, 'kl', other)  7.69 us
    pallas_call x1, Pallas kernels, hold(): pl.pallas_call(hold_kernel, grid_spec=pltpu.PrefetchScalarGridSpec(num_sc...  7.04 us
    pallas_call x3, Pallas kernels, place(): pl.pallas_call(functools.partial(place_kernel, spots=spots, first=first),...  4.06 us
    pallas_call x4, Pallas kernels, reduce(): pl.pallas_call(reduce_kernel, grid=(rows // ROWS,), in_specs=[fixed(modes...  2.62 us
  transfers between devices with their start and end apart: 22, of which 11 were waited for; matrix products, arithmetic and copies ran while one was open for 1% of the time, Pallas kernels for 25%

profile of v14, /device:TPU:12, one launch (start us, length us, event | category | flops | bytes accessed | tf_op | source)
XLA Modules:
  0.0 91.1 jit_solution(14834956255381343593)
XLA Ops:
  1.1 1.6 %collective-permute-start = (bf16[8,16,512]{2,1,0:T(8,128)(2,1)S(1)}, bf16[8,16,512]{2,1,0:T(8,128)(2,1)S(1)}, u32[]{:S(2)}, u32[]{:S(2)}) collective-permute-start(bf16[8,16,512]{2,1,0:T(8,128)(2,1)S(1)} %get-tuple-element.126), channel_id=1, source_target_pairs={{0,12},{4,8},{8,4},{12,0},{1,13},{5,9},{9,5},{13,1},{2,14},{6,10},... | collective-permute-start | bytes 393224 | tf_op jit(solution)/shard_map/ppermute | solution.py:232
  6.3 1.6 %collective-permute-start.3 = (bf16[4,48,512]{2,1,0:T(8,128)(2,1)S(1)}, bf16[4,48,512]{2,1,0:T(8,128)(2,1)S(1)}, u32[]{:S(2)}, u32[]{:S(2)}) collective-permute-start(bf16[4,48,512]{2,1,0:T(8,128)(2,1)S(1)} %get-tuple-element.120.refs_0_), channel_id=1, source_target_pairs={{0,2},{2,0},{1,3},{3,1},{4,6},{6,4},{5,7},{7,5},{8,10},{10,8},{9,1... | collective-permute-start | bytes 589832 | tf_op jit(solution)/shard_map/ppermute | solution.py:235
  9.1 7.0 %shard_map.64 = (bf16[32,512,512]{2,1,0:T(8,128)(2,1)S(1)}, bf16[384,512]{1,0:T(8,128)(2,1)S(1)}, bf16[512,384]{1,0:T(8,128)(2,1)S(1)}) custom-call(s32[6]{0:T(128)S(1)} %compare_select_fusion.1.where, s32[4,4]{1,0:T(4,128)S(1)} %bitcast.27, s32[1]{0:T(128)S(6)} %copy.18.starts, bf16[32,512,512]{2,1,0:T(8,128)(2,1)} %bitcast.28, bf16[32,24]{1,0:T(8,128)(2,1)S(1)} %bitcast.26), custom_call_target="tpu_custom_call" | custom-call | flops 1024 | bytes 1024 | tf_op jit(solution)/shard_map/pallas_call | solution.py:63
  17.3 2.3 %collective-permute-start.5 = (bf16[8,32,512]{2,1,0:T(8,128)(2,1)S(1)}, bf16[8,32,512]{2,1,0:T(8,128)(2,1)S(1)}, u32[]{:S(2)}, u32[]{:S(2)}) collective-permute-start(bf16[8,32,512]{2,1,0:T(8,128)(2,1)S(1)} %get-tuple-element.65), channel_id=1, source_target_pairs={{0,8},{4,12},{8,0},{12,4},{1,9},{5,13},{9,1},{13,5},{2,10},{6,14},... | collective-permute-start | bytes 786440 | tf_op jit(solution)/shard_map/ppermute | solution.py:232
  19.6 1.5 %collective-permute-start.6 = (bf16[8,16,512]{2,1,0:T(8,128)(2,1)S(1)}, bf16[8,16,512]{2,1,0:T(8,128)(2,1)S(1)}, u32[]{:S(2)}, u32[]{:S(2)}) collective-permute-start(bf16[8,16,512]{2,1,0:T(8,128)(2,1)S(1)} %collective-permute-done.2.refs_0_), channel_id=1, source_target_pairs={{0,2},{2,0},{1,3},{3,1},{4,6},{6,4},{5,7},{7,5},{8,10},{10,8},{9,1... | collective-permute-start | bytes 393224 | tf_op jit(solution)/shard_map/ppermute | solution.py:235
  21.6 1.5 %collective-permute-start.8 = (bf16[8,16,512]{2,1,0:T(8,128)(2,1)S(1)}, bf16[8,16,512]{2,1,0:T(8,128)(2,1)S(1)}, u32[]{:S(2)}, u32[]{:S(2)}) collective-permute-start(bf16[8,16,512]{2,1,0:T(8,128)(2,1)S(1)} %collective-permute-done.refs_0_), channel_id=1, source_target_pairs={{0,2},{2,0},{1,3},{3,1},{4,6},{6,4},{5,7},{7,5},{8,10},{10,8},{9,1... | collective-permute-start | bytes 393224 | tf_op jit(solution)/shard_map/ppermute | solution.py:235
  23.1 1.4 %shard_map.65 = (bf16[8,48,512]{2,1,0:T(8,128)(2,1)S(1)}, bf16[8,48,512]{2,1,0:T(8,128)(2,1)S(1)}) custom-call(s32[6]{0:T(128)S(1)} %compare_select_fusion.1.where, bf16[4,48,512]{2,1,0:T(8,128)(2,1)S(1)} %get-tuple-element.120.refs_0_, bf16[4,48,512]{2,1,0:T(8,128)(2,1)S(1)} %get-tuple-element.119.refs_1_, ...), custom_call_target="tpu_custom_call" | custom-call | flops 200000000 | bytes 1024 | tf_op jit(solution)/shard_map/pallas_call | solution.py:102
  27.2 1.4 %shard_map.67 = (bf16[8,16,512]{2,1,0:T(8,128)(2,1)S(1)}, bf16[8,16,512]{2,1,0:T(8,128)(2,1)S(1)}) custom-call(s32[6]{0:T(128)S(1)} %compare_select_fusion.1.where, bf16[8,16,512]{2,1,0:T(8,128)(2,1)S(1)} %collective-permute-done.1.refs_0_, bf16[8,16,512]{2,1,0:T(8,128)(2,1)S(1)} %collective-permute-done.7.refs_1_, ...), custom_call_target="tpu_custom_call" | custom-call | flops 200000000 | bytes 1024 | tf_op jit(solution)/shard_map/pallas_call | solution.py:102
  28.5 1.6 %collective-permute-start.13 = (bf16[8,32,512]{2,1,0:T(8,128)(2,1)S(1)}, bf16[8,32,512]{2,1,0:T(8,128)(2,1)S(1)}, u32[]{:S(2)}, u32[]{:S(2)}) collective-permute-start(bf16[8,32,512]{2,1,0:T(8,128)(2,1)S(1)} %collective-permute-done.10.refs_0_), channel_id=1, source_target_pairs={{0,2},{2,0},{1,3},{3,1},{4,6},{6,4},{5,7},{7,5},{8,10},{10,8},{9,1... | collective-permute-start | bytes 786440 | tf_op jit(solution)/shard_map/ppermute | solution.py:235
  31.9 1.4 %collective-permute-start.9 = (bf16[8,32,512]{2,1,0:T(8,128)(2,1)S(1)}, bf16[8,32,512]{2,1,0:T(8,128)(2,1)S(1)}, u32[]{:S(2)}, u32[]{:S(2)}) collective-permute-start(bf16[8,32,512]{2,1,0:T(8,128)(2,1)S(1)} %collective-permute-done.5.refs_0_), channel_id=1, source_target_pairs={{0,2},{2,0},{1,3},{3,1},{4,6},{6,4},{5,7},{7,5},{8,10},{10,8},{9,1... | collective-permute-start | bytes 786440 | tf_op jit(solution)/shard_map/ppermute | solution.py:235
  33.4 1.6 %collective-permute-done.13.refs_0_ = bf16[8,32,512]{2,1,0:T(8,128)(2,1)S(1)} collective-permute-done((bf16[8,32,512]{2,1,0:T(8,128)(2,1)S(1)}, bf16[8,32,512]{2,1,0:T(8,128)(2,1)S(1)}, u32[]{:S(2)}, u32[]{:S(2)}) %collective-permute-start.13) | collective-permute-done | bytes 262176 | tf_op jit(solution)/shard_map/ppermute | solution.py:235
  35.3 1.4 %shard_map.73 = (bf16[8,32,512]{2,1,0:T(8,128)(2,1)S(1)}, bf16[8,32,512]{2,1,0:T(8,128)(2,1)S(1)}) custom-call(s32[6]{0:T(128)S(1)} %compare_select_fusion.1.where, bf16[8,32,512]{2,1,0:T(8,128)(2,1)S(1)} %collective-permute-done.10.refs_0_, bf16[8,32,512]{2,1,0:T(8,128)(2,1)S(1)} %shard_map.72.refs_1_, ...), custom_call_target="tpu_custom_call" | custom-call | flops 1024 | bytes 1024 | tf_op jit(solution)/shard_map/pallas_call | solution.py:102
  37.3 3.3 %collective-permute-done.9.refs_1_ = bf16[8,32,512]{2,1,0:T(8,128)(2,1)S(1)} collective-permute-done((bf16[8,32,512]{2,1,0:T(8,128)(2,1)S(1)}, bf16[8,32,512]{2,1,0:T(8,128)(2,1)S(1)}, u32[]{:S(2)}, u32[]{:S(2)}) %collective-permute-start.9) | collective-permute-done | bytes 262176 | tf_op jit(solution)/shard_map/ppermute | solution.py:235
  40.6 6.7 %collective-permute-done.11.refs_0_ = bf16[8,32,512]{2,1,0:T(8,128)(2,1)S(1)} collective-permute-done((bf16[8,32,512]{2,1,0:T(8,128)(2,1)S(1)}, bf16[8,32,512]{2,1,0:T(8,128)(2,1)S(1)}, u32[]{:S(2)}, u32[]{:S(2)}) %collective-permute-start.11) | collective-permute-done | bytes 262176 | tf_op jit(solution)/shard_map/ppermute | solution.py:232
  48.5 3.9 %collective-permute-start.16 = (bf16[8,16,512]{2,1,0:T(8,128)(2,1)S(1)}, bf16[8,16,512]{2,1,0:T(8,128)(2,1)S(1)}, u32[]{:S(2)}, u32[]{:S(2)}) collective-permute-start(bf16[8,16,512]{2,1,0:T(8,128)(2,1)S(1)} %get-tuple-element.98), channel_id=1, source_target_pairs={{0,4},{4,0},{8,12},{12,8},{1,5},{5,1},{9,13},{13,9},{2,6},{6,2},{1... | collective-permute-start | bytes 393224 | tf_op jit(solution)/shard_map/ppermute | solution.py:232
  52.4 1.4 %shard_map.74 = (bf16[8,32,512]{2,1,0:T(8,128)(2,1)S(1)}, bf16[8,32,512]{2,1,0:T(8,128)(2,1)S(1)}) custom-call(s32[6]{0:T(128)S(1)} %compare_select_fusion.1.where, bf16[8,32,512]{2,1,0:T(8,128)(2,1)S(1)} %collective-permute-done.5.refs_0_, bf16[8,32,512]{2,1,0:T(8,128)(2,1)S(1)} %collective-permute-done.9.refs_1_, ...), custom_call_target="tpu_custom_call" | custom-call | flops 1024 | bytes 1024 | tf_op jit(solution)/shard_map/pallas_call | solution.py:102
  54.9 1.4 %shard_map.75 = (bf16[8,32,512]{2,1,0:T(8,128)(2,1)S(1)}, bf16[8,32,512]{2,1,0:T(8,128)(2,1)S(1)}) custom-call(s32[6]{0:T(128)S(1)} %compare_select_fusion.1.where, bf16[8,32,512]{2,1,0:T(8,128)(2,1)S(1)} %collective-permute-done.11.refs_0_, bf16[8,32,512]{2,1,0:T(8,128)(2,1)S(1)} %collective-permute-done.17.refs_1_, ...), custom_call_target="tpu_custom_call" | custom-call | flops 1024 | bytes 1024 | tf_op jit(solution)/shard_map/pallas_call | solution.py:102
  58.2 1.5 %collective-permute-done.15.refs_2_ = bf16[8,16,512]{2,1,0:T(8,128)(2,1)S(1)} collective-permute-done((bf16[8,16,512]{2,1,0:T(8,128)(2,1)S(1)}, bf16[8,16,512]{2,1,0:T(8,128)(2,1)S(1)}, u32[]{:S(2)}, u32[]{:S(2)}) %collective-permute-start.15) | collective-permute-done | bytes 131104 | tf_op jit(solution)/shard_map/ppermute | solution.py:232
  59.7 2.3 %collective-permute-done.18.came_ref = bf16[24,32,512]{2,1,0:T(8,128)(2,1)S(1)} collective-permute-done((bf16[24,32,512]{2,1,0:T(8,128)(2,1)S(1)}, bf16[24,32,512]{2,1,0:T(8,128)(2,1)S(1)}, u32[]{:S(2)}, u32[]{:S(2)}) %collective-permute-start.18) | collective-permute-done | bytes 786464 | tf_op jit(solution)/shard_map/ppermute | solution.py:282
  63.9 2.4 %collective-permute-start.19 = (bf16[8,32,512]{2,1,0:T(8,128)(2,1)S(1)}, bf16[8,32,512]{2,1,0:T(8,128)(2,1)S(1)}, u32[]{:S(2)}, u32[]{:S(2)}) collective-permute-start(bf16[8,32,512]{2,1,0:T(8,128)(2,1)S(1)} %get-tuple-element.111), channel_id=1, source_target_pairs={{0,8},{4,12},{8,0},{12,4},{1,9},{5,13},{9,1},{13,5},{2,10},{6,14},... | collective-permute-start | bytes 786440 | tf_op jit(solution)/shard_map/ppermute | solution.py:232
  66.8 1.4 %shard_map.79.refs_2_ = bf16[8,4,48,512]{3,2,1,0:T(8,128)(2,1)} custom-call(s32[6]{0:T(128)S(1)} %compare_select_fusion.1.where, bf16[8,16,512]{2,1,0:T(8,128)(2,1)S(1)} %collective-permute-done.16.refs_0_, bf16[8,16,512]{2,1,0:T(8,128)(2,1)S(1)} %collective-permute-done.14.refs_1_, bf16[8,16,512]{2,1,0:T(8,128)(2,1)S(1)} %collective-permute-done.15.refs_2_, ...), custom_call_target="tpu_custom_call" | custom-call | flops 1024 | bytes 1024 | tf_op jit(solution)/shard_map/pallas_call | solution.py:190
  68.1 6.6 %collective-permute-done.21.refs_1_ = bf16[8,32,512]{2,1,0:T(8,128)(2,1)S(1)} collective-permute-done((bf16[8,32,512]{2,1,0:T(8,128)(2,1)S(1)}, bf16[8,32,512]{2,1,0:T(8,128)(2,1)S(1)}, u32[]{:S(2)}, u32[]{:S(2)}) %collective-permute-start.21) | collective-permute-done | bytes 262176 | tf_op jit(solution)/shard_map/ppermute | solution.py:232
  76.1 8.2 %collective-permute-done.19.refs_0_ = bf16[8,32,512]{2,1,0:T(8,128)(2,1)S(1)} collective-permute-done((bf16[8,32,512]{2,1,0:T(8,128)(2,1)S(1)}, bf16[8,32,512]{2,1,0:T(8,128)(2,1)S(1)}, u32[]{:S(2)}, u32[]{:S(2)}) %collective-permute-start.19) | collective-permute-done | bytes 262176 | tf_op jit(solution)/shard_map/ppermute | solution.py:232
  84.2 5.5 %collective-permute-done.20.refs_1_ = bf16[8,32,512]{2,1,0:T(8,128)(2,1)S(1)} collective-permute-done((bf16[8,32,512]{2,1,0:T(8,128)(2,1)S(1)}, bf16[8,32,512]{2,1,0:T(8,128)(2,1)S(1)}, u32[]{:S(2)}, u32[]{:S(2)}) %collective-permute-start.20) | collective-permute-done | bytes 262176 | tf_op jit(solution)/shard_map/ppermute | solution.py:232
  (53 shorter events, 21.6 us)
Async XLA Ops:
  0.0 9.0 %copy-start.2 = (bf16[1,32,24]{1,2,0:T(8,128)(2,1)S(1)}, bf16[1,32,24]{1,2,0:T(8,128)(2,1)}, u32[]{:S(2)}) copy-start(bf16[1,32,24]{1,2,0:T(8,128)(2,1)} %param.10) | copy-start | bytes 4612
  0.0 9.1 %copy-start = (s32[1,4,4]{2,1,0:T(4,128)S(1)}, s32[1,4,4]{2,1,0:T(4,128)}, u32[]{:S(2)}) copy-start(s32[1,4,4]{2,1,0:T(4,128)} %param.8) | copy-start | bytes 196
  1.1 15.2 %collective-permute-start = (bf16[8,16,512]{2,1,0:T(8,128)(2,1)S(1)}, bf16[8,16,512]{2,1,0:T(8,128)(2,1)S(1)}, u32[]{:S(2)}, u32[]{:S(2)}) collective-permute-start(bf16[8,16,512]{2,1,0:T(8,128)(2,1)S(1)} %get-tuple-element.126), channel_id=1, source_target_pairs={{0,12},{4,8},{8,4},{12,0},{1,13},{5,9},{9,5},{13,1},{2,14},{6,10},... | collective-permute-start | bytes 393224 | tf_op jit(solution)/shard_map/ppermute | solution.py:232
  2.7 13.5 %collective-permute-start.1 = (bf16[8,16,512]{2,1,0:T(8,128)(2,1)S(1)}, bf16[8,16,512]{2,1,0:T(8,128)(2,1)S(1)}, u32[]{:S(2)}, u32[]{:S(2)}) collective-permute-start(bf16[8,16,512]{2,1,0:T(8,128)(2,1)S(1)} %get-tuple-element.125), channel_id=1, source_target_pairs={{0,8},{4,12},{8,0},{12,4},{1,9},{5,13},{9,1},{13,5},{2,10},{6,14},... | collective-permute-start | bytes 393224 | tf_op jit(solution)/shard_map/ppermute | solution.py:232
  4.0 12.3 %collective-permute-start.2 = (bf16[8,16,512]{2,1,0:T(8,128)(2,1)S(1)}, bf16[8,16,512]{2,1,0:T(8,128)(2,1)S(1)}, u32[]{:S(2)}, u32[]{:S(2)}) collective-permute-start(bf16[8,16,512]{2,1,0:T(8,128)(2,1)S(1)} %get-tuple-element.124), channel_id=1, source_target_pairs={{0,4},{4,0},{8,12},{12,8},{1,5},{5,1},{9,13},{13,9},{2,6},{6,2},{1... | collective-permute-start | bytes 393224 | tf_op jit(solution)/shard_map/ppermute | solution.py:232
  6.3 10.0 %collective-permute-start.3 = (bf16[4,48,512]{2,1,0:T(8,128)(2,1)S(1)}, bf16[4,48,512]{2,1,0:T(8,128)(2,1)S(1)}, u32[]{:S(2)}, u32[]{:S(2)}) collective-permute-start(bf16[4,48,512]{2,1,0:T(8,128)(2,1)S(1)} %get-tuple-element.120.refs_0_), channel_id=1, source_target_pairs={{0,2},{2,0},{1,3},{3,1},{4,6},{6,4},{5,7},{7,5},{8,10},{10,8},{9,1... | collective-permute-start | bytes 589832 | tf_op jit(solution)/shard_map/ppermute | solution.py:235
  7.8 8.8 %collective-permute-start.4 = (bf16[4,48,512]{2,1,0:T(8,128)(2,1)S(1)}, bf16[4,48,512]{2,1,0:T(8,128)(2,1)S(1)}, u32[]{:S(2)}, u32[]{:S(2)}) collective-permute-start(bf16[4,48,512]{2,1,0:T(8,128)(2,1)S(1)} %get-tuple-element.119.refs_1_), channel_id=1, source_target_pairs={{0,2},{2,0},{1,3},{3,1},{4,6},{6,4},{5,7},{7,5},{8,10},{10,8},{9,1... | collective-permute-start | bytes 589832 | tf_op jit(solution)/shard_map/ppermute | solution.py:235
  16.6 11.9 %collective-permute-start.10 = (bf16[8,32,512]{2,1,0:T(8,128)(2,1)S(1)}, bf16[8,32,512]{2,1,0:T(8,128)(2,1)S(1)}, u32[]{:S(2)}, u32[]{:S(2)}) collective-permute-start(bf16[8,32,512]{2,1,0:T(8,128)(2,1)S(1)} %get-tuple-element.83), channel_id=1, source_target_pairs={{0,4},{4,0},{8,12},{12,8},{1,5},{5,1},{9,13},{13,9},{2,6},{6,2},{1... | collective-permute-start | bytes 786440 | tf_op jit(solution)/shard_map/ppermute | solution.py:232
  17.3 14.6 %collective-permute-start.5 = (bf16[8,32,512]{2,1,0:T(8,128)(2,1)S(1)}, bf16[8,32,512]{2,1,0:T(8,128)(2,1)S(1)}, u32[]{:S(2)}, u32[]{:S(2)}) collective-permute-start(bf16[8,32,512]{2,1,0:T(8,128)(2,1)S(1)} %get-tuple-element.65), channel_id=1, source_target_pairs={{0,8},{4,12},{8,0},{12,4},{1,9},{5,13},{9,1},{13,5},{2,10},{6,14},... | collective-permute-start | bytes 786440 | tf_op jit(solution)/shard_map/ppermute | solution.py:232
  19.6 6.2 %collective-permute-start.6 = (bf16[8,16,512]{2,1,0:T(8,128)(2,1)S(1)}, bf16[8,16,512]{2,1,0:T(8,128)(2,1)S(1)}, u32[]{:S(2)}, u32[]{:S(2)}) collective-permute-start(bf16[8,16,512]{2,1,0:T(8,128)(2,1)S(1)} %collective-permute-done.2.refs_0_), channel_id=1, source_target_pairs={{0,2},{2,0},{1,3},{3,1},{4,6},{6,4},{5,7},{7,5},{8,10},{10,8},{9,1... | collective-permute-start | bytes 393224 | tf_op jit(solution)/shard_map/ppermute | solution.py:235
  21.0 6.1 %collective-permute-start.7 = (bf16[8,16,512]{2,1,0:T(8,128)(2,1)S(1)}, bf16[8,16,512]{2,1,0:T(8,128)(2,1)S(1)}, u32[]{:S(2)}, u32[]{:S(2)}) collective-permute-start(bf16[8,16,512]{2,1,0:T(8,128)(2,1)S(1)} %collective-permute-done.1.refs_0_), channel_id=1, source_target_pairs={{0,2},{2,0},{1,3},{3,1},{4,6},{6,4},{5,7},{7,5},{8,10},{10,8},{9,1... | collective-permute-start | bytes 393224 | tf_op jit(solution)/shard_map/ppermute | solution.py:235
  21.6 8.5 %collective-permute-start.8 = (bf16[8,16,512]{2,1,0:T(8,128)(2,1)S(1)}, bf16[8,16,512]{2,1,0:T(8,128)(2,1)S(1)}, u32[]{:S(2)}, u32[]{:S(2)}) collective-permute-start(bf16[8,16,512]{2,1,0:T(8,128)(2,1)S(1)} %collective-permute-done.refs_0_), channel_id=1, source_target_pairs={{0,2},{2,0},{1,3},{3,1},{4,6},{6,4},{5,7},{7,5},{8,10},{10,8},{9,1... | collective-permute-start | bytes 393224 | tf_op jit(solution)/shard_map/ppermute | solution.py:235
  28.5 6.4 %collective-permute-start.13 = (bf16[8,32,512]{2,1,0:T(8,128)(2,1)S(1)}, bf16[8,32,512]{2,1,0:T(8,128)(2,1)S(1)}, u32[]{:S(2)}, u32[]{:S(2)}) collective-permute-start(bf16[8,32,512]{2,1,0:T(8,128)(2,1)S(1)} %collective-permute-done.10.refs_0_), channel_id=1, source_target_pairs={{0,2},{2,0},{1,3},{3,1},{4,6},{6,4},{5,7},{7,5},{8,10},{10,8},{9,1... | collective-permute-start | bytes 786440 | tf_op jit(solution)/shard_map/ppermute | solution.py:235
  31.8 4.9 %collective-permute-start.12 = (bf16[24,16,512]{2,1,0:T(8,128)(2,1)S(1)}, bf16[24,16,512]{2,1,0:T(8,128)(2,1)S(1)}, u32[]{:S(2)}, u32[]{:S(2)}) collective-permute-start(bf16[24,16,512]{2,1,0:T(8,128)(2,1)S(1)} %shard_map.69), channel_id=1, source_target_pairs={{0,1},{1,0},{2,3},{3,2},{4,5},{5,4},{6,7},{7,6},{8,9},{9,8},{10,11... | collective-permute-start | bytes 1179656 | tf_op jit(solution)/shard_map/ppermute | solution.py:270
  31.9 8.7 %collective-permute-start.9 = (bf16[8,32,512]{2,1,0:T(8,128)(2,1)S(1)}, bf16[8,32,512]{2,1,0:T(8,128)(2,1)S(1)}, u32[]{:S(2)}, u32[]{:S(2)}) collective-permute-start(bf16[8,32,512]{2,1,0:T(8,128)(2,1)S(1)} %collective-permute-done.5.refs_0_), channel_id=1, source_target_pairs={{0,2},{2,0},{1,3},{3,1},{4,6},{6,4},{5,7},{7,5},{8,10},{10,8},{9,1... | collective-permute-start | bytes 786440 | tf_op jit(solution)/shard_map/ppermute | solution.py:235
  33.4 14.0 %collective-permute-start.11 = (bf16[8,32,512]{2,1,0:T(8,128)(2,1)S(1)}, bf16[8,32,512]{2,1,0:T(8,128)(2,1)S(1)}, u32[]{:S(2)}, u32[]{:S(2)}) collective-permute-start(bf16[8,32,512]{2,1,0:T(8,128)(2,1)S(1)} %get-tuple-element.84), channel_id=1, source_target_pairs={{0,12},{4,8},{8,4},{12,0},{1,13},{5,9},{9,5},{13,1},{2,14},{6,10},... | collective-permute-start | bytes 786440 | tf_op jit(solution)/shard_map/ppermute | solution.py:232
  47.4 7.5 %collective-permute-start.17 = (bf16[8,32,512]{2,1,0:T(8,128)(2,1)S(1)}, bf16[8,32,512]{2,1,0:T(8,128)(2,1)S(1)}, u32[]{:S(2)}, u32[]{:S(2)}) collective-permute-start(bf16[8,32,512]{2,1,0:T(8,128)(2,1)S(1)} %collective-permute-done.11.refs_0_), channel_id=1, source_target_pairs={{0,2},{2,0},{1,3},{3,1},{4,6},{6,4},{5,7},{7,5},{8,10},{10,8},{9,1... | collective-permute-start | bytes 786440 | tf_op jit(solution)/shard_map/ppermute | solution.py:235
  48.0 10.2 %collective-permute-start.14 = (bf16[8,16,512]{2,1,0:T(8,128)(2,1)S(1)}, bf16[8,16,512]{2,1,0:T(8,128)(2,1)S(1)}, u32[]{:S(2)}, u32[]{:S(2)}) collective-permute-start(bf16[8,16,512]{2,1,0:T(8,128)(2,1)S(1)} %get-tuple-element.96), channel_id=1, source_target_pairs={{0,8},{4,12},{8,0},{12,4},{1,9},{5,13},{9,1},{13,5},{2,10},{6,14},... | collective-permute-start | bytes 393224 | tf_op jit(solution)/shard_map/ppermute | solution.py:232
  48.0 11.6 %collective-permute-start.15 = (bf16[8,16,512]{2,1,0:T(8,128)(2,1)S(1)}, bf16[8,16,512]{2,1,0:T(8,128)(2,1)S(1)}, u32[]{:S(2)}, u32[]{:S(2)}) collective-permute-start(bf16[8,16,512]{2,1,0:T(8,128)(2,1)S(1)} %get-tuple-element.97), channel_id=1, source_target_pairs={{0,12},{4,8},{8,4},{12,0},{1,13},{5,9},{9,5},{13,1},{2,14},{6,10},... | collective-permute-start | bytes 393224 | tf_op jit(solution)/shard_map/ppermute | solution.py:232
  48.5 11.1 %collective-permute-start.16 = (bf16[8,16,512]{2,1,0:T(8,128)(2,1)S(1)}, bf16[8,16,512]{2,1,0:T(8,128)(2,1)S(1)}, u32[]{:S(2)}, u32[]{:S(2)}) collective-permute-start(bf16[8,16,512]{2,1,0:T(8,128)(2,1)S(1)} %get-tuple-element.98), channel_id=1, source_target_pairs={{0,4},{4,0},{8,12},{12,8},{1,5},{5,1},{9,13},{13,9},{2,6},{6,2},{1... | collective-permute-start | bytes 393224 | tf_op jit(solution)/shard_map/ppermute | solution.py:232
  59.6 2.3 %collective-permute-start.18 = (bf16[24,32,512]{2,1,0:T(8,128)(2,1)S(1)}, bf16[24,32,512]{2,1,0:T(8,128)(2,1)S(1)}, u32[]{:S(2)}, u32[]{:S(2)}) collective-permute-start(bf16[24,32,512]{2,1,0:T(8,128)(2,1)S(1)} %shard_map.77), channel_id=1, source_target_pairs={{0,1},{1,0},{2,3},{3,2},{4,5},{5,4},{6,7},{7,6},{8,9},{9,8},{10,11... | collective-permute-start | bytes 2359304 | tf_op jit(solution)/shard_map/ppermute | solution.py:282
  63.2 11.5 %collective-permute-start.21 = (bf16[8,32,512]{2,1,0:T(8,128)(2,1)S(1)}, bf16[8,32,512]{2,1,0:T(8,128)(2,1)S(1)}, u32[]{:S(2)}, u32[]{:S(2)}) collective-permute-start(bf16[8,32,512]{2,1,0:T(8,128)(2,1)S(1)} %get-tuple-element.114), channel_id=1, source_target_pairs={{0,4},{4,0},{8,12},{12,8},{1,5},{5,1},{9,13},{13,9},{2,6},{6,2},{1... | collective-permute-start | bytes 786440 | tf_op jit(solution)/shard_map/ppermute | solution.py:232
  63.9 20.4 %collective-permute-start.19 = (bf16[8,32,512]{2,1,0:T(8,128)(2,1)S(1)}, bf16[8,32,512]{2,1,0:T(8,128)(2,1)S(1)}, u32[]{:S(2)}, u32[]{:S(2)}) collective-permute-start(bf16[8,32,512]{2,1,0:T(8,128)(2,1)S(1)} %get-tuple-element.111), channel_id=1, source_target_pairs={{0,8},{4,12},{8,0},{12,4},{1,9},{5,13},{9,1},{13,5},{2,10},{6,14},... | collective-permute-start | bytes 786440 | tf_op jit(solution)/shard_map/ppermute | solution.py:232
  66.3 23.4 %collective-permute-start.20 = (bf16[8,32,512]{2,1,0:T(8,128)(2,1)S(1)}, bf16[8,32,512]{2,1,0:T(8,128)(2,1)S(1)}, u32[]{:S(2)}, u32[]{:S(2)}) collective-permute-start(bf16[8,32,512]{2,1,0:T(8,128)(2,1)S(1)} %get-tuple-element.112), channel_id=1, source_target_pairs={{0,12},{4,8},{8,4},{12,0},{1,13},{5,9},{9,5},{13,1},{2,14},{6,10},... | collective-permute-start | bytes 786440 | tf_op jit(solution)/shard_map/ppermute | solution.py:232
  (2 other events, 9.0 us)

commit v15 on v13

--- a/solution.py
+++ b/solution.py
@@ -275,11 +275,13 @@
     x_3 = along_x(b[3])
     skies = [own, near] + [project(where, [b[j]], [x], held, j, blocks) for j, x in ((2, x_2), (3, x_3))]
     gone = reduce(down, [leave for _, leave in skies], (ROWS, 0, 0, 0), n_modes)
-    kept = reduce(down, [stay for stay, _ in skies], (ROWS, 0, 0, 0), n_modes, jnp.float32)
-    (first[2], first[3], first[1]), first[0], kept, gone = fence(
-        ((first[2], first[3], first[1]), first[0], kept, gone)
-    )
-    outs = fence(restore(kept, lax.ppermute(gone, "pol", other), ratios, up, spots))
+    stays = [stay for stay, _ in skies]
+    first[2], first[1], here, stays, gone = fence((first[2], first[1], first[0], stays, gone))
+    came = lax.ppermute(gone, "pol", other)
+    kept = reduce(down, stays, (ROWS, 0, 0, 0), n_modes, jnp.float32)
+    first[3], = anchor([first[3]], 20_000_000_000)
+    outs, first[3] = fence((restore(kept, came, ratios, up, spots), first[3]))
+    first[0] = here
     back = [along_z(outs[j - 1], j) for j in (1, 2, 3)]
     result = place(where, [first[j] for j in (1, 2, 3, 0)], spots, 0, shape)
     result = place(where, [outs[3], back[0]], [spots[3], spots[0]], ROWS, shape, into=result)

time: 89.8 us -> 89.2 us (level)
    ppermute x1, waiting for transfers between devices: 2.27 us -> 0.01 us  [staged(): came = lax.ppermute(gone, 'pol', other)]
    ppermute x12, waiting for transfers between devices: 26.9 us -> 28.4 us  [along_z(): return lax.ppermute(value, 'fm', [(i, i ^ j) for i in range(parts)])]
  transfers between devices with their start and end apart: 22 -> 22, of which waited for: 9 -> 10; matrix products, arithmetic and copies ran while one was open for 1% -> 1% of each run, Pallas kernels for 25% -> 25%
where the time goes in v15:
time: 89.2 us; the launch traced here: 89 us
  waiting for transfers between devices  34.2 us (38%)
  starting transfers between devices  26.5 us (30%)
  Pallas kernels  25 us (28%)
  local copies, waits for them, and re-layouts  2.39 us (3%)
  between operations  0.92 us (1%)
    ppermute x12, waiting for transfers between devices, along_z(): return lax.ppermute(value, 'fm', [(i, i ^ j) for i in range(parts)])  28.4 us
    ppermute x12, starting transfers between devices, along_z(): return lax.ppermute(value, 'fm', [(i, i ^ j) for i in range(parts)])  14.7 us
    ppermute x8, starting transfers between devices, along_x(): return lax.ppermute(value, 'kl', other)  11.7 us
    pallas_call x7, Pallas kernels, project(): pl.pallas_call(functools.partial(project_kernel, piece=piece, blocks=bloc...  9.57 us
    pallas_call x1, Pallas kernels, hold(): pl.pallas_call(hold_kernel, grid_spec=pltpu.PrefetchScalarGridSpec(num_sc...  7.04 us
    ppermute x8, waiting for transfers between devices, along_x(): return lax.ppermute(value, 'kl', other)  5.8 us
    pallas_call x3, Pallas kernels, place(): pl.pallas_call(functools.partial(place_kernel, spots=spots, first=first),...  4.06 us
    pallas_call x4, Pallas kernels, reduce(): pl.pallas_call(reduce_kernel, grid=(rows // ROWS,), in_specs=[fixed(modes...  2.6 us
  transfers between devices with their start and end apart: 22, of which 10 were waited for; matrix products, arithmetic and copies ran while one was open for 1% of the time, Pallas kernels for 25%

profile of v15, /device:TPU:12, one launch (start us, length us, event | category | flops | bytes accessed | tf_op | source)
XLA Modules:
  0.0 89.0 jit_solution(3338322670154890643)
XLA Ops:
  1.1 1.6 %collective-permute-start = (bf16[8,16,512]{2,1,0:T(8,128)(2,1)S(1)}, bf16[8,16,512]{2,1,0:T(8,128)(2,1)S(1)}, u32[]{:S(2)}, u32[]{:S(2)}) collective-permute-start(bf16[8,16,512]{2,1,0:T(8,128)(2,1)S(1)} %get-tuple-element.140), channel_id=1, source_target_pairs={{0,12},{4,8},{8,4},{12,0},{1,13},{5,9},{9,5},{13,1},{2,14},{6,10},... | collective-permute-start | bytes 393224 | tf_op jit(solution)/shard_map/ppermute | solution.py:232
  6.3 1.6 %collective-permute-start.3 = (bf16[4,48,512]{2,1,0:T(8,128)(2,1)S(1)}, bf16[4,48,512]{2,1,0:T(8,128)(2,1)S(1)}, u32[]{:S(2)}, u32[]{:S(2)}) collective-permute-start(bf16[4,48,512]{2,1,0:T(8,128)(2,1)S(1)} %get-tuple-element.134.refs_0_), channel_id=1, source_target_pairs={{0,2},{2,0},{1,3},{3,1},{4,6},{6,4},{5,7},{7,5},{8,10},{10,8},{9,1... | collective-permute-start | bytes 589832 | tf_op jit(solution)/shard_map/ppermute | solution.py:235
  9.1 7.0 %shard_map.64 = (bf16[32,512,512]{2,1,0:T(8,128)(2,1)S(1)}, bf16[384,512]{1,0:T(8,128)(2,1)S(1)}, bf16[512,384]{1,0:T(8,128)(2,1)S(1)}) custom-call(s32[6]{0:T(128)S(1)} %compare_select_fusion.1.where, s32[4,4]{1,0:T(4,128)S(1)} %bitcast.27, s32[1]{0:T(128)S(6)} %copy.20.starts, bf16[32,512,512]{2,1,0:T(8,128)(2,1)} %bitcast.28, bf16[32,24]{1,0:T(8,128)(2,1)S(1)} %bitcast.26), custom_call_target="tpu_custom_call" | custom-call | flops 1024 | bytes 1024 | tf_op jit(solution)/shard_map/pallas_call | solution.py:63
  17.3 2.3 %collective-permute-start.5 = (bf16[8,32,512]{2,1,0:T(8,128)(2,1)S(1)}, bf16[8,32,512]{2,1,0:T(8,128)(2,1)S(1)}, u32[]{:S(2)}, u32[]{:S(2)}) collective-permute-start(bf16[8,32,512]{2,1,0:T(8,128)(2,1)S(1)} %get-tuple-element.73), channel_id=1, source_target_pairs={{0,8},{4,12},{8,0},{12,4},{1,9},{5,13},{9,1},{13,5},{2,10},{6,14},... | collective-permute-start | bytes 786440 | tf_op jit(solution)/shard_map/ppermute | solution.py:232
  19.6 1.5 %collective-permute-start.6 = (bf16[8,16,512]{2,1,0:T(8,128)(2,1)S(1)}, bf16[8,16,512]{2,1,0:T(8,128)(2,1)S(1)}, u32[]{:S(2)}, u32[]{:S(2)}) collective-permute-start(bf16[8,16,512]{2,1,0:T(8,128)(2,1)S(1)} %collective-permute-done.2.refs_0_), channel_id=1, source_target_pairs={{0,2},{2,0},{1,3},{3,1},{4,6},{6,4},{5,7},{7,5},{8,10},{10,8},{9,1... | collective-permute-start | bytes 393224 | tf_op jit(solution)/shard_map/ppermute | solution.py:235
  21.6 1.5 %collective-permute-start.8 = (bf16[8,16,512]{2,1,0:T(8,128)(2,1)S(1)}, bf16[8,16,512]{2,1,0:T(8,128)(2,1)S(1)}, u32[]{:S(2)}, u32[]{:S(2)}) collective-permute-start(bf16[8,16,512]{2,1,0:T(8,128)(2,1)S(1)} %collective-permute-done.refs_0_), channel_id=1, source_target_pairs={{0,2},{2,0},{1,3},{3,1},{4,6},{6,4},{5,7},{7,5},{8,10},{10,8},{9,1... | collective-permute-start | bytes 393224 | tf_op jit(solution)/shard_map/ppermute | solution.py:235
  27.2 1.4 %shard_map.67 = (bf16[8,16,512]{2,1,0:T(8,128)(2,1)S(1)}, bf16[8,16,512]{2,1,0:T(8,128)(2,1)S(1)}) custom-call(s32[6]{0:T(128)S(1)} %compare_select_fusion.1.where, bf16[8,16,512]{2,1,0:T(8,128)(2,1)S(1)} %collective-permute-done.1.refs_0_, bf16[8,16,512]{2,1,0:T(8,128)(2,1)S(1)} %collective-permute-done.7.refs_1_, ...), custom_call_target="tpu_custom_call" | custom-call | flops 400000000 | bytes 1024 | tf_op jit(solution)/shard_map/pallas_call | solution.py:102
  28.5 1.6 %collective-permute-start.13 = (bf16[8,32,512]{2,1,0:T(8,128)(2,1)S(1)}, bf16[8,32,512]{2,1,0:T(8,128)(2,1)S(1)}, u32[]{:S(2)}, u32[]{:S(2)}) collective-permute-start(bf16[8,32,512]{2,1,0:T(8,128)(2,1)S(1)} %collective-permute-done.10.refs_0_), channel_id=1, source_target_pairs={{0,2},{2,0},{1,3},{3,1},{4,6},{6,4},{5,7},{7,5},{8,10},{10,8},{9,1... | collective-permute-start | bytes 786440 | tf_op jit(solution)/shard_map/ppermute | solution.py:235
  30.1 1.4 %shard_map.68 = (bf16[8,16,512]{2,1,0:T(8,128)(2,1)S(1)}, bf16[8,16,512]{2,1,0:T(8,128)(2,1)S(1)}) custom-call(s32[6]{0:T(128)S(1)} %compare_select_fusion.1.where, bf16[8,16,512]{2,1,0:T(8,128)(2,1)S(1)} %collective-permute-done.refs_0_, bf16[8,16,512]{2,1,0:T(8,128)(2,1)S(1)} %collective-permute-done.8.refs_1_, ...), custom_call_target="tpu_custom_call" | custom-call | flops 400000000 | bytes 1024 | tf_op jit(solution)/shard_map/pallas_call | solution.py:102
  31.8 1.4 %collective-permute-start.9 = (bf16[8,32,512]{2,1,0:T(8,128)(2,1)S(1)}, bf16[8,32,512]{2,1,0:T(8,128)(2,1)S(1)}, u32[]{:S(2)}, u32[]{:S(2)}) collective-permute-start(bf16[8,32,512]{2,1,0:T(8,128)(2,1)S(1)} %collective-permute-done.5.refs_0_), channel_id=1, source_target_pairs={{0,2},{2,0},{1,3},{3,1},{4,6},{6,4},{5,7},{7,5},{8,10},{10,8},{9,1... | collective-permute-start | bytes 786440 | tf_op jit(solution)/shard_map/ppermute | solution.py:235
  33.3 3.7 %collective-permute-done.13.refs_0_ = bf16[8,32,512]{2,1,0:T(8,128)(2,1)S(1)} collective-permute-done((bf16[8,32,512]{2,1,0:T(8,128)(2,1)S(1)}, bf16[8,32,512]{2,1,0:T(8,128)(2,1)S(1)}, u32[]{:S(2)}, u32[]{:S(2)}) %collective-permute-start.13) | collective-permute-done | bytes 262176 | tf_op jit(solution)/shard_map/ppermute | solution.py:235
  37.4 1.4 %shard_map.73 = (bf16[8,32,512]{2,1,0:T(8,128)(2,1)S(1)}, bf16[8,32,512]{2,1,0:T(8,128)(2,1)S(1)}) custom-call(s32[6]{0:T(128)S(1)} %compare_select_fusion.1.where, bf16[8,32,512]{2,1,0:T(8,128)(2,1)S(1)} %collective-permute-done.10.refs_0_, bf16[8,32,512]{2,1,0:T(8,128)(2,1)S(1)} %shard_map.72.refs_1_, ...), custom_call_target="tpu_custom_call" | custom-call | flops 1024 | bytes 1024 | tf_op jit(solution)/shard_map/pallas_call | solution.py:102
  39.8 5.2 %collective-permute-done.11.refs_0_ = bf16[8,32,512]{2,1,0:T(8,128)(2,1)S(1)} collective-permute-done((bf16[8,32,512]{2,1,0:T(8,128)(2,1)S(1)}, bf16[8,32,512]{2,1,0:T(8,128)(2,1)S(1)}, u32[]{:S(2)}, u32[]{:S(2)}) %collective-permute-start.11) | collective-permute-done | bytes 262176 | tf_op jit(solution)/shard_map/ppermute | solution.py:232
  45.0 3.1 %collective-permute-start.16 = (bf16[8,32,512]{2,1,0:T(8,128)(2,1)S(1)}, bf16[8,32,512]{2,1,0:T(8,128)(2,1)S(1)}, u32[]{:S(2)}, u32[]{:S(2)}) collective-permute-start(bf16[8,32,512]{2,1,0:T(8,128)(2,1)S(1)} %collective-permute-done.11.refs_0_), channel_id=1, source_target_pairs={{0,2},{2,0},{1,3},{3,1},{4,6},{6,4},{5,7},{7,5},{8,10},{10,8},{9,1... | collective-permute-start | bytes 786440 | tf_op jit(solution)/shard_map/ppermute | solution.py:235
  48.2 3.9 %collective-permute-start.15 = (bf16[8,16,512]{2,1,0:T(8,128)(2,1)S(1)}, bf16[8,16,512]{2,1,0:T(8,128)(2,1)S(1)}, u32[]{:S(2)}, u32[]{:S(2)}) collective-permute-start(bf16[8,16,512]{2,1,0:T(8,128)(2,1)S(1)} %get-tuple-element.104), channel_id=1, source_target_pairs={{0,4},{4,0},{8,12},{12,8},{1,5},{5,1},{9,13},{13,9},{2,6},{6,2},{1... | collective-permute-start | bytes 393224 | tf_op jit(solution)/shard_map/ppermute | solution.py:232
  52.1 1.4 %shard_map.74 = (bf16[8,32,512]{2,1,0:T(8,128)(2,1)S(1)}, bf16[8,32,512]{2,1,0:T(8,128)(2,1)S(1)}) custom-call(s32[6]{0:T(128)S(1)} %compare_select_fusion.1.where, bf16[8,32,512]{2,1,0:T(8,128)(2,1)S(1)} %collective-permute-done.5.refs_0_, bf16[8,32,512]{2,1,0:T(8,128)(2,1)S(1)} %collective-permute-done.9.refs_1_, ...), custom_call_target="tpu_custom_call" | custom-call | flops 1024 | bytes 1024 | tf_op jit(solution)/shard_map/pallas_call | solution.py:102
  53.5 1.4 %shard_map.75 = (bf16[8,32,512]{2,1,0:T(8,128)(2,1)S(1)}, bf16[8,32,512]{2,1,0:T(8,128)(2,1)S(1)}) custom-call(s32[6]{0:T(128)S(1)} %compare_select_fusion.1.where, bf16[8,32,512]{2,1,0:T(8,128)(2,1)S(1)} %collective-permute-done.11.refs_0_, bf16[8,32,512]{2,1,0:T(8,128)(2,1)S(1)} %collective-permute-done.16.refs_1_, ...), custom_call_target="tpu_custom_call" | custom-call | flops 1024 | bytes 1024 | tf_op jit(solution)/shard_map/pallas_call | solution.py:102
  56.8 1.7 %collective-permute-done.18.refs_0_ = bf16[8,16,512]{2,1,0:T(8,128)(2,1)S(1)} collective-permute-done((bf16[8,16,512]{2,1,0:T(8,128)(2,1)S(1)}, bf16[8,16,512]{2,1,0:T(8,128)(2,1)S(1)}, u32[]{:S(2)}, u32[]{:S(2)}) %collective-permute-start.18) | collective-permute-done | bytes 131104 | tf_op jit(solution)/shard_map/ppermute | solution.py:232
  60.7 2.2 %collective-permute-start.21 = (bf16[8,32,512]{2,1,0:T(8,128)(2,1)S(1)}, bf16[8,32,512]{2,1,0:T(8,128)(2,1)S(1)}, u32[]{:S(2)}, u32[]{:S(2)}) collective-permute-start(bf16[8,32,512]{2,1,0:T(8,128)(2,1)S(1)} %get-tuple-element.128), channel_id=1, source_target_pairs={{0,4},{4,0},{8,12},{12,8},{1,5},{5,1},{9,13},{13,9},{2,6},{6,2},{1... | collective-permute-start | bytes 786440 | tf_op jit(solution)/shard_map/ppermute | solution.py:232
  63.0 1.4 %collective-permute-start.20 = (bf16[8,32,512]{2,1,0:T(8,128)(2,1)S(1)}, bf16[8,32,512]{2,1,0:T(8,128)(2,1)S(1)}, u32[]{:S(2)}, u32[]{:S(2)}) collective-permute-start(bf16[8,32,512]{2,1,0:T(8,128)(2,1)S(1)} %get-tuple-element.126), channel_id=1, source_target_pairs={{0,12},{4,8},{8,4},{12,0},{1,13},{5,9},{9,5},{13,1},{2,14},{6,10},... | collective-permute-start | bytes 786440 | tf_op jit(solution)/shard_map/ppermute | solution.py:232
  64.5 1.4 %shard_map.80.refs_2_ = bf16[8,4,48,512]{3,2,1,0:T(8,128)(2,1)} custom-call(s32[6]{0:T(128)S(1)} %compare_select_fusion.1.where, bf16[8,16,512]{2,1,0:T(8,128)(2,1)S(1)} %collective-permute-done.15.refs_0_, bf16[8,16,512]{2,1,0:T(8,128)(2,1)S(1)} %collective-permute-done.14.refs_1_, bf16[8,16,512]{2,1,0:T(8,128)(2,1)S(1)} %shard_map.79.refs_2_, ...), custom_call_target="tpu_custom_call" | custom-call | flops 1024 | bytes 1024 | tf_op jit(solution)/shard_map/pallas_call | solution.py:190
  65.8 7.2 %collective-permute-done.21.refs_1_ = bf16[8,32,512]{2,1,0:T(8,128)(2,1)S(1)} collective-permute-done((bf16[8,32,512]{2,1,0:T(8,128)(2,1)S(1)}, bf16[8,32,512]{2,1,0:T(8,128)(2,1)S(1)}, u32[]{:S(2)}, u32[]{:S(2)}) %collective-permute-start.21) | collective-permute-done | bytes 262176 | tf_op jit(solution)/shard_map/ppermute | solution.py:232
  74.4 6.6 %collective-permute-done.19.refs_0_ = bf16[8,32,512]{2,1,0:T(8,128)(2,1)S(1)} collective-permute-done((bf16[8,32,512]{2,1,0:T(8,128)(2,1)S(1)}, bf16[8,32,512]{2,1,0:T(8,128)(2,1)S(1)}, u32[]{:S(2)}, u32[]{:S(2)}) %collective-permute-start.19) | collective-permute-done | bytes 262176 | tf_op jit(solution)/shard_map/ppermute | solution.py:232
  81.0 6.7 %collective-permute-done.20.refs_1_ = bf16[8,32,512]{2,1,0:T(8,128)(2,1)S(1)} collective-permute-done((bf16[8,32,512]{2,1,0:T(8,128)(2,1)S(1)}, bf16[8,32,512]{2,1,0:T(8,128)(2,1)S(1)}, u32[]{:S(2)}, u32[]{:S(2)}) %collective-permute-start.20) | collective-permute-done | bytes 262176 | tf_op jit(solution)/shard_map/ppermute | solution.py:232
  (54 shorter events, 19.6 us)
Async XLA Ops:
  0.0 9.0 %copy-start.2 = (bf16[1,32,24]{1,2,0:T(8,128)(2,1)S(1)}, bf16[1,32,24]{1,2,0:T(8,128)(2,1)}, u32[]{:S(2)}) copy-start(bf16[1,32,24]{1,2,0:T(8,128)(2,1)} %param.10) | copy-start | bytes 4612
  0.0 9.1 %copy-start = (s32[1,4,4]{2,1,0:T(4,128)S(1)}, s32[1,4,4]{2,1,0:T(4,128)}, u32[]{:S(2)}) copy-start(s32[1,4,4]{2,1,0:T(4,128)} %param.8) | copy-start | bytes 196
  1.1 15.2 %collective-permute-start = (bf16[8,16,512]{2,1,0:T(8,128)(2,1)S(1)}, bf16[8,16,512]{2,1,0:T(8,128)(2,1)S(1)}, u32[]{:S(2)}, u32[]{:S(2)}) collective-permute-start(bf16[8,16,512]{2,1,0:T(8,128)(2,1)S(1)} %get-tuple-element.140), channel_id=1, source_target_pairs={{0,12},{4,8},{8,4},{12,0},{1,13},{5,9},{9,5},{13,1},{2,14},{6,10},... | collective-permute-start | bytes 393224 | tf_op jit(solution)/shard_map/ppermute | solution.py:232
  2.7 13.5 %collective-permute-start.1 = (bf16[8,16,512]{2,1,0:T(8,128)(2,1)S(1)}, bf16[8,16,512]{2,1,0:T(8,128)(2,1)S(1)}, u32[]{:S(2)}, u32[]{:S(2)}) collective-permute-start(bf16[8,16,512]{2,1,0:T(8,128)(2,1)S(1)} %get-tuple-element.139), channel_id=1, source_target_pairs={{0,8},{4,12},{8,0},{12,4},{1,9},{5,13},{9,1},{13,5},{2,10},{6,14},... | collective-permute-start | bytes 393224 | tf_op jit(solution)/shard_map/ppermute | solution.py:232
  4.0 12.3 %collective-permute-start.2 = (bf16[8,16,512]{2,1,0:T(8,128)(2,1)S(1)}, bf16[8,16,512]{2,1,0:T(8,128)(2,1)S(1)}, u32[]{:S(2)}, u32[]{:S(2)}) collective-permute-start(bf16[8,16,512]{2,1,0:T(8,128)(2,1)S(1)} %get-tuple-element.138), channel_id=1, source_target_pairs={{0,4},{4,0},{8,12},{12,8},{1,5},{5,1},{9,13},{13,9},{2,6},{6,2},{1... | collective-permute-start | bytes 393224 | tf_op jit(solution)/shard_map/ppermute | solution.py:232
  6.3 10.0 %collective-permute-start.3 = (bf16[4,48,512]{2,1,0:T(8,128)(2,1)S(1)}, bf16[4,48,512]{2,1,0:T(8,128)(2,1)S(1)}, u32[]{:S(2)}, u32[]{:S(2)}) collective-permute-start(bf16[4,48,512]{2,1,0:T(8,128)(2,1)S(1)} %get-tuple-element.134.refs_0_), channel_id=1, source_target_pairs={{0,2},{2,0},{1,3},{3,1},{4,6},{6,4},{5,7},{7,5},{8,10},{10,8},{9,1... | collective-permute-start | bytes 589832 | tf_op jit(solution)/shard_map/ppermute | solution.py:235
  7.8 8.8 %collective-permute-start.4 = (bf16[4,48,512]{2,1,0:T(8,128)(2,1)S(1)}, bf16[4,48,512]{2,1,0:T(8,128)(2,1)S(1)}, u32[]{:S(2)}, u32[]{:S(2)}) collective-permute-start(bf16[4,48,512]{2,1,0:T(8,128)(2,1)S(1)} %get-tuple-element.133.refs_1_), channel_id=1, source_target_pairs={{0,2},{2,0},{1,3},{3,1},{4,6},{6,4},{5,7},{7,5},{8,10},{10,8},{9,1... | collective-permute-start | bytes 589832 | tf_op jit(solution)/shard_map/ppermute | solution.py:235
  16.6 11.9 %collective-permute-start.10 = (bf16[8,32,512]{2,1,0:T(8,128)(2,1)S(1)}, bf16[8,32,512]{2,1,0:T(8,128)(2,1)S(1)}, u32[]{:S(2)}, u32[]{:S(2)}) collective-permute-start(bf16[8,32,512]{2,1,0:T(8,128)(2,1)S(1)} %get-tuple-element.90), channel_id=1, source_target_pairs={{0,4},{4,0},{8,12},{12,8},{1,5},{5,1},{9,13},{13,9},{2,6},{6,2},{1... | collective-permute-start | bytes 786440 | tf_op jit(solution)/shard_map/ppermute | solution.py:232
  17.3 14.6 %collective-permute-start.5 = (bf16[8,32,512]{2,1,0:T(8,128)(2,1)S(1)}, bf16[8,32,512]{2,1,0:T(8,128)(2,1)S(1)}, u32[]{:S(2)}, u32[]{:S(2)}) collective-permute-start(bf16[8,32,512]{2,1,0:T(8,128)(2,1)S(1)} %get-tuple-element.73), channel_id=1, source_target_pairs={{0,8},{4,12},{8,0},{12,4},{1,9},{5,13},{9,1},{13,5},{2,10},{6,14},... | collective-permute-start | bytes 786440 | tf_op jit(solution)/shard_map/ppermute | solution.py:232
  19.6 6.2 %collective-permute-start.6 = (bf16[8,16,512]{2,1,0:T(8,128)(2,1)S(1)}, bf16[8,16,512]{2,1,0:T(8,128)(2,1)S(1)}, u32[]{:S(2)}, u32[]{:S(2)}) collective-permute-start(bf16[8,16,512]{2,1,0:T(8,128)(2,1)S(1)} %collective-permute-done.2.refs_0_), channel_id=1, source_target_pairs={{0,2},{2,0},{1,3},{3,1},{4,6},{6,4},{5,7},{7,5},{8,10},{10,8},{9,1... | collective-permute-start | bytes 393224 | tf_op jit(solution)/shard_map/ppermute | solution.py:235
  21.0 6.1 %collective-permute-start.7 = (bf16[8,16,512]{2,1,0:T(8,128)(2,1)S(1)}, bf16[8,16,512]{2,1,0:T(8,128)(2,1)S(1)}, u32[]{:S(2)}, u32[]{:S(2)}) collective-permute-start(bf16[8,16,512]{2,1,0:T(8,128)(2,1)S(1)} %collective-permute-done.1.refs_0_), channel_id=1, source_target_pairs={{0,2},{2,0},{1,3},{3,1},{4,6},{6,4},{5,7},{7,5},{8,10},{10,8},{9,1... | collective-permute-start | bytes 393224 | tf_op jit(solution)/shard_map/ppermute | solution.py:235
  21.6 8.5 %collective-permute-start.8 = (bf16[8,16,512]{2,1,0:T(8,128)(2,1)S(1)}, bf16[8,16,512]{2,1,0:T(8,128)(2,1)S(1)}, u32[]{:S(2)}, u32[]{:S(2)}) collective-permute-start(bf16[8,16,512]{2,1,0:T(8,128)(2,1)S(1)} %collective-permute-done.refs_0_), channel_id=1, source_target_pairs={{0,2},{2,0},{1,3},{3,1},{4,6},{6,4},{5,7},{7,5},{8,10},{10,8},{9,1... | collective-permute-start | bytes 393224 | tf_op jit(solution)/shard_map/ppermute | solution.py:235
  28.5 8.5 %collective-permute-start.13 = (bf16[8,32,512]{2,1,0:T(8,128)(2,1)S(1)}, bf16[8,32,512]{2,1,0:T(8,128)(2,1)S(1)}, u32[]{:S(2)}, u32[]{:S(2)}) collective-permute-start(bf16[8,32,512]{2,1,0:T(8,128)(2,1)S(1)} %collective-permute-done.10.refs_0_), channel_id=1, source_target_pairs={{0,2},{2,0},{1,3},{3,1},{4,6},{6,4},{5,7},{7,5},{8,10},{10,8},{9,1... | collective-permute-start | bytes 786440 | tf_op jit(solution)/shard_map/ppermute | solution.py:235
  31.8 7.9 %collective-permute-start.9 = (bf16[8,32,512]{2,1,0:T(8,128)(2,1)S(1)}, bf16[8,32,512]{2,1,0:T(8,128)(2,1)S(1)}, u32[]{:S(2)}, u32[]{:S(2)}) collective-permute-start(bf16[8,32,512]{2,1,0:T(8,128)(2,1)S(1)} %collective-permute-done.5.refs_0_), channel_id=1, source_target_pairs={{0,2},{2,0},{1,3},{3,1},{4,6},{6,4},{5,7},{7,5},{8,10},{10,8},{9,1... | collective-permute-start | bytes 786440 | tf_op jit(solution)/shard_map/ppermute | solution.py:235
  33.3 11.8 %collective-permute-start.11 = (bf16[8,32,512]{2,1,0:T(8,128)(2,1)S(1)}, bf16[8,32,512]{2,1,0:T(8,128)(2,1)S(1)}, u32[]{:S(2)}, u32[]{:S(2)}) collective-permute-start(bf16[8,32,512]{2,1,0:T(8,128)(2,1)S(1)} %get-tuple-element.91), channel_id=1, source_target_pairs={{0,12},{4,8},{8,4},{12,0},{1,13},{5,9},{9,5},{13,1},{2,14},{6,10},... | collective-permute-start | bytes 786440 | tf_op jit(solution)/shard_map/ppermute | solution.py:232
  33.3 5.5 %collective-permute-start.12 = (bf16[24,16,512]{2,1,0:T(8,128)(2,1)S(1)}, bf16[24,16,512]{2,1,0:T(8,128)(2,1)S(1)}, u32[]{:S(2)}, u32[]{:S(2)}) collective-permute-start(bf16[24,16,512]{2,1,0:T(8,128)(2,1)S(1)} %shard_map.69), channel_id=1, source_target_pairs={{0,1},{1,0},{2,3},{3,2},{4,5},{5,4},{6,7},{7,6},{8,9},{9,8},{10,11... | collective-permute-start | bytes 1179656 | tf_op jit(solution)/shard_map/ppermute | solution.py:270
  45.0 8.5 %collective-permute-start.16 = (bf16[8,32,512]{2,1,0:T(8,128)(2,1)S(1)}, bf16[8,32,512]{2,1,0:T(8,128)(2,1)S(1)}, u32[]{:S(2)}, u32[]{:S(2)}) collective-permute-start(bf16[8,32,512]{2,1,0:T(8,128)(2,1)S(1)} %collective-permute-done.11.refs_0_), channel_id=1, source_target_pairs={{0,2},{2,0},{1,3},{3,1},{4,6},{6,4},{5,7},{7,5},{8,10},{10,8},{9,1... | collective-permute-start | bytes 786440 | tf_op jit(solution)/shard_map/ppermute | solution.py:235
  48.2 7.7 %collective-permute-start.14 = (bf16[8,16,512]{2,1,0:T(8,128)(2,1)S(1)}, bf16[8,16,512]{2,1,0:T(8,128)(2,1)S(1)}, u32[]{:S(2)}, u32[]{:S(2)}) collective-permute-start(bf16[8,16,512]{2,1,0:T(8,128)(2,1)S(1)} %get-tuple-element.103), channel_id=1, source_target_pairs={{0,8},{4,12},{8,0},{12,4},{1,9},{5,13},{9,1},{13,5},{2,10},{6,14},... | collective-permute-start | bytes 393224 | tf_op jit(solution)/shard_map/ppermute | solution.py:232
  48.2 8.7 %collective-permute-start.15 = (bf16[8,16,512]{2,1,0:T(8,128)(2,1)S(1)}, bf16[8,16,512]{2,1,0:T(8,128)(2,1)S(1)}, u32[]{:S(2)}, u32[]{:S(2)}) collective-permute-start(bf16[8,16,512]{2,1,0:T(8,128)(2,1)S(1)} %get-tuple-element.104), channel_id=1, source_target_pairs={{0,4},{4,0},{8,12},{12,8},{1,5},{5,1},{9,13},{13,9},{2,6},{6,2},{1... | collective-permute-start | bytes 393224 | tf_op jit(solution)/shard_map/ppermute | solution.py:232
  52.1 6.4 %collective-permute-start.18 = (bf16[8,16,512]{2,1,0:T(8,128)(2,1)S(1)}, bf16[8,16,512]{2,1,0:T(8,128)(2,1)S(1)}, u32[]{:S(2)}, u32[]{:S(2)}) collective-permute-start(bf16[8,16,512]{2,1,0:T(8,128)(2,1)S(1)} %get-tuple-element.124), channel_id=1, source_target_pairs={{0,12},{4,8},{8,4},{12,0},{1,13},{5,9},{9,5},{13,1},{2,14},{6,10},... | collective-permute-start | bytes 393224 | tf_op jit(solution)/shard_map/ppermute | solution.py:232
  56.8 2.6 %collective-permute-start.17 = (bf16[24,32,512]{2,1,0:T(8,128)(2,1)S(1)}, bf16[24,32,512]{2,1,0:T(8,128)(2,1)S(1)}, u32[]{:S(2)}, u32[]{:S(2)}) collective-permute-start(bf16[24,32,512]{2,1,0:T(8,128)(2,1)S(1)} %shard_map.76), channel_id=1, source_target_pairs={{0,1},{1,0},{2,3},{3,2},{4,5},{5,4},{6,7},{7,6},{8,9},{9,8},{10,11... | collective-permute-start | bytes 2359304 | tf_op jit(solution)/shard_map/ppermute | solution.py:280
  60.7 12.3 %collective-permute-start.21 = (bf16[8,32,512]{2,1,0:T(8,128)(2,1)S(1)}, bf16[8,32,512]{2,1,0:T(8,128)(2,1)S(1)}, u32[]{:S(2)}, u32[]{:S(2)}) collective-permute-start(bf16[8,32,512]{2,1,0:T(8,128)(2,1)S(1)} %get-tuple-element.128), channel_id=1, source_target_pairs={{0,4},{4,0},{8,12},{12,8},{1,5},{5,1},{9,13},{13,9},{2,6},{6,2},{1... | collective-permute-start | bytes 786440 | tf_op jit(solution)/shard_map/ppermute | solution.py:232
  62.9 18.1 %collective-permute-start.19 = (bf16[8,32,512]{2,1,0:T(8,128)(2,1)S(1)}, bf16[8,32,512]{2,1,0:T(8,128)(2,1)S(1)}, u32[]{:S(2)}, u32[]{:S(2)}) collective-permute-start(bf16[8,32,512]{2,1,0:T(8,128)(2,1)S(1)} %get-tuple-element.125), channel_id=1, source_target_pairs={{0,8},{4,12},{8,0},{12,4},{1,9},{5,13},{9,1},{13,5},{2,10},{6,14},... | collective-permute-start | bytes 786440 | tf_op jit(solution)/shard_map/ppermute | solution.py:232
  63.0 24.6 %collective-permute-start.20 = (bf16[8,32,512]{2,1,0:T(8,128)(2,1)S(1)}, bf16[8,32,512]{2,1,0:T(8,128)(2,1)S(1)}, u32[]{:S(2)}, u32[]{:S(2)}) collective-permute-start(bf16[8,32,512]{2,1,0:T(8,128)(2,1)S(1)} %get-tuple-element.126), channel_id=1, source_target_pairs={{0,12},{4,8},{8,4},{12,0},{1,13},{5,9},{9,5},{13,1},{2,14},{6,10},... | collective-permute-start | bytes 786440 | tf_op jit(solution)/shard_map/ppermute | solution.py:232
  (2 other events, 8.9 us)

commit v16 on v15

--- a/solution.py
+++ b/solution.py
@@ -282,10 +282,10 @@
     first[3], = anchor([first[3]], 20_000_000_000)
     outs, first[3] = fence((restore(kept, came, ratios, up, spots), first[3]))
     first[0] = here
-    back = [along_z(outs[j - 1], j) for j in (1, 2, 3)]
+    back = [along_z(outs[j - 1], j) for j in (3, 1, 2)]
     result = place(where, [first[j] for j in (1, 2, 3, 0)], spots, 0, shape)
-    result = place(where, [outs[3], back[0]], [spots[3], spots[0]], ROWS, shape, into=result)
-    return place(where, back[1:], spots[1:3], ROWS, shape, into=result)
+    result = place(where, [outs[3]], [spots[3]], ROWS, shape, into=result)
+    return place(where, back, [spots[2], spots[0], spots[1]], ROWS, shape, into=result)
 
 
 def plain(visibility, beam_transfer, tile_mask, first_block, eigen_modes, signal_noise):

time: 89.2 us -> 89.7 us (level)
  the two profiles are of different devices: /device:TPU:12 before, /device:TPU:0 now
where the time goes in v16:
time: 89.7 us; the launch traced here: 89.6 us
  starting transfers between devices  34 us (38%)
  waiting for transfers between devices  27.2 us (30%)
  Pallas kernels  25.1 us (28%)
  local copies, waits for them, and re-layouts  2.39 us (3%)
  between operations  0.91 us (1%)
    ppermute x12, starting transfers between devices, along_z(): return lax.ppermute(value, 'fm', [(i, i ^ j) for i in range(parts)])  24.7 us
    ppermute x12, waiting for transfers between devices, along_z(): return lax.ppermute(value, 'fm', [(i, i ^ j) for i in range(parts)])  20.8 us
    pallas_call x7, Pallas kernels, project(): pl.pallas_call(functools.partial(project_kernel, piece=piece, blocks=bloc...  9.57 us
    ppermute x8, starting transfers between devices, along_x(): return lax.ppermute(value, 'kl', other)  9.26 us
    pallas_call x1, Pallas kernels, hold(): pl.pallas_call(hold_kernel, grid_spec=pltpu.PrefetchScalarGridSpec(num_sc...  7.04 us
    ppermute x8, waiting for transfers between devices, along_x(): return lax.ppermute(value, 'kl', other)  5.08 us
    pallas_call x3, Pallas kernels, place(): pl.pallas_call(functools.partial(place_kernel, spots=spots, first=first),...  4.06 us
    pallas_call x4, Pallas kernels, reduce(): pl.pallas_call(reduce_kernel, grid=(rows // ROWS,), in_specs=[fixed(modes...  2.61 us
  transfers between devices with their start and end apart: 22, of which 10 were waited for; matrix products, arithmetic and copies ran while one was open for 1% of the time, Pallas kernels for 25%

profile of v16, /device:TPU:0, one launch (start us, length us, event | category | flops | bytes accessed | tf_op | source)
XLA Modules:
  0.0 89.6 jit_solution(8624309323519975728)
XLA Ops:
  1.1 5.1 %collective-permute-start = (bf16[8,16,512]{2,1,0:T(8,128)(2,1)S(1)}, bf16[8,16,512]{2,1,0:T(8,128)(2,1)S(1)}, u32[]{:S(2)}, u32[]{:S(2)}) collective-permute-start(bf16[8,16,512]{2,1,0:T(8,128)(2,1)S(1)} %get-tuple-element.140), channel_id=1, source_target_pairs={{0,12},{4,8},{8,4},{12,0},{1,13},{5,9},{9,5},{13,1},{2,14},{6,10},... | collective-permute-start | bytes 393224 | tf_op jit(solution)/shard_map/ppermute | solution.py:232
  7.9 1.7 %collective-permute-start.3 = (bf16[4,48,512]{2,1,0:T(8,128)(2,1)S(1)}, bf16[4,48,512]{2,1,0:T(8,128)(2,1)S(1)}, u32[]{:S(2)}, u32[]{:S(2)}) collective-permute-start(bf16[4,48,512]{2,1,0:T(8,128)(2,1)S(1)} %get-tuple-element.134.refs_0_), channel_id=1, source_target_pairs={{0,2},{2,0},{1,3},{3,1},{4,6},{6,4},{5,7},{7,5},{8,10},{10,8},{9,1... | collective-permute-start | bytes 589832 | tf_op jit(solution)/shard_map/ppermute | solution.py:235
  10.8 7.0 %shard_map.64 = (bf16[32,512,512]{2,1,0:T(8,128)(2,1)S(1)}, bf16[384,512]{1,0:T(8,128)(2,1)S(1)}, bf16[512,384]{1,0:T(8,128)(2,1)S(1)}) custom-call(s32[6]{0:T(128)S(1)} %compare_select_fusion.1.where, s32[4,4]{1,0:T(4,128)S(1)} %bitcast.27, s32[1]{0:T(128)S(6)} %copy.20.starts, bf16[32,512,512]{2,1,0:T(8,128)(2,1)} %bitcast.28, bf16[32,24]{1,0:T(8,128)(2,1)S(1)} %bitcast.26), custom_call_target="tpu_custom_call" | custom-call | flops 1024 | bytes 1024 | tf_op jit(solution)/shard_map/pallas_call | solution.py:63
  18.3 1.4 %collective-permute-start.10 = (bf16[8,32,512]{2,1,0:T(8,128)(2,1)S(1)}, bf16[8,32,512]{2,1,0:T(8,128)(2,1)S(1)}, u32[]{:S(2)}, u32[]{:S(2)}) collective-permute-start(bf16[8,32,512]{2,1,0:T(8,128)(2,1)S(1)} %get-tuple-element.90), channel_id=1, source_target_pairs={{0,4},{4,0},{8,12},{12,8},{1,5},{5,1},{9,13},{13,9},{2,6},{6,2},{1... | collective-permute-start | bytes 786440 | tf_op jit(solution)/shard_map/ppermute | solution.py:232
  19.7 2.7 %collective-permute-start.5 = (bf16[8,32,512]{2,1,0:T(8,128)(2,1)S(1)}, bf16[8,32,512]{2,1,0:T(8,128)(2,1)S(1)}, u32[]{:S(2)}, u32[]{:S(2)}) collective-permute-start(bf16[8,32,512]{2,1,0:T(8,128)(2,1)S(1)} %get-tuple-element.73), channel_id=1, source_target_pairs={{0,8},{4,12},{8,0},{12,4},{1,9},{5,13},{9,1},{13,5},{2,10},{6,14},... | collective-permute-start | bytes 786440 | tf_op jit(solution)/shard_map/ppermute | solution.py:232
  22.3 1.5 %collective-permute-start.6 = (bf16[8,16,512]{2,1,0:T(8,128)(2,1)S(1)}, bf16[8,16,512]{2,1,0:T(8,128)(2,1)S(1)}, u32[]{:S(2)}, u32[]{:S(2)}) collective-permute-start(bf16[8,16,512]{2,1,0:T(8,128)(2,1)S(1)} %collective-permute-done.2.refs_0_), channel_id=1, source_target_pairs={{0,2},{2,0},{1,3},{3,1},{4,6},{6,4},{5,7},{7,5},{8,10},{10,8},{9,1... | collective-permute-start | bytes 393224 | tf_op jit(solution)/shard_map/ppermute | solution.py:235
  24.4 1.5 %collective-permute-start.8 = (bf16[8,16,512]{2,1,0:T(8,128)(2,1)S(1)}, bf16[8,16,512]{2,1,0:T(8,128)(2,1)S(1)}, u32[]{:S(2)}, u32[]{:S(2)}) collective-permute-start(bf16[8,16,512]{2,1,0:T(8,128)(2,1)S(1)} %collective-permute-done.refs_0_), channel_id=1, source_target_pairs={{0,2},{2,0},{1,3},{3,1},{4,6},{6,4},{5,7},{7,5},{8,10},{10,8},{9,1... | collective-permute-start | bytes 393224 | tf_op jit(solution)/shard_map/ppermute | solution.py:235
  25.8 1.4 %shard_map.65 = (bf16[8,48,512]{2,1,0:T(8,128)(2,1)S(1)}, bf16[8,48,512]{2,1,0:T(8,128)(2,1)S(1)}) custom-call(s32[6]{0:T(128)S(1)} %compare_select_fusion.1.where, bf16[4,48,512]{2,1,0:T(8,128)(2,1)S(1)} %get-tuple-element.134.refs_0_, bf16[4,48,512]{2,1,0:T(8,128)(2,1)S(1)} %get-tuple-element.133.refs_1_, ...), custom_call_target="tpu_custom_call" | custom-call | flops 400000000 | bytes 1024 | tf_op jit(solution)/shard_map/pallas_call | solution.py:102
  31.2 1.6 %collective-permute-start.13 = (bf16[8,32,512]{2,1,0:T(8,128)(2,1)S(1)}, bf16[8,32,512]{2,1,0:T(8,128)(2,1)S(1)}, u32[]{:S(2)}, u32[]{:S(2)}) collective-permute-start(bf16[8,32,512]{2,1,0:T(8,128)(2,1)S(1)} %collective-permute-done.10.refs_0_), channel_id=1, source_target_pairs={{0,2},{2,0},{1,3},{3,1},{4,6},{6,4},{5,7},{7,5},{8,10},{10,8},{9,1... | collective-permute-start | bytes 786440 | tf_op jit(solution)/shard_map/ppermute | solution.py:235
  34.5 1.4 %collective-permute-start.9 = (bf16[8,32,512]{2,1,0:T(8,128)(2,1)S(1)}, bf16[8,32,512]{2,1,0:T(8,128)(2,1)S(1)}, u32[]{:S(2)}, u32[]{:S(2)}) collective-permute-start(bf16[8,32,512]{2,1,0:T(8,128)(2,1)S(1)} %collective-permute-done.5.refs_0_), channel_id=1, source_target_pairs={{0,2},{2,0},{1,3},{3,1},{4,6},{6,4},{5,7},{7,5},{8,10},{10,8},{9,1... | collective-permute-start | bytes 786440 | tf_op jit(solution)/shard_map/ppermute | solution.py:235
  36.7 3.0 %collective-permute-done.13.refs_0_ = bf16[8,32,512]{2,1,0:T(8,128)(2,1)S(1)} collective-permute-done((bf16[8,32,512]{2,1,0:T(8,128)(2,1)S(1)}, bf16[8,32,512]{2,1,0:T(8,128)(2,1)S(1)}, u32[]{:S(2)}, u32[]{:S(2)}) %collective-permute-start.13) | collective-permute-done | bytes 262176 | tf_op jit(solution)/shard_map/ppermute | solution.py:235
  40.0 1.4 %shard_map.73 = (bf16[8,32,512]{2,1,0:T(8,128)(2,1)S(1)}, bf16[8,32,512]{2,1,0:T(8,128)(2,1)S(1)}) custom-call(s32[6]{0:T(128)S(1)} %compare_select_fusion.1.where, bf16[8,32,512]{2,1,0:T(8,128)(2,1)S(1)} %collective-permute-done.10.refs_0_, bf16[8,32,512]{2,1,0:T(8,128)(2,1)S(1)} %shard_map.72.refs_1_, ...), custom_call_target="tpu_custom_call" | custom-call | flops 1024 | bytes 1024 | tf_op jit(solution)/shard_map/pallas_call | solution.py:102
  42.6 1.7 %collective-permute-done.11.refs_0_ = bf16[8,32,512]{2,1,0:T(8,128)(2,1)S(1)} collective-permute-done((bf16[8,32,512]{2,1,0:T(8,128)(2,1)S(1)}, bf16[8,32,512]{2,1,0:T(8,128)(2,1)S(1)}, u32[]{:S(2)}, u32[]{:S(2)}) %collective-permute-start.11) | collective-permute-done | bytes 262176 | tf_op jit(solution)/shard_map/ppermute | solution.py:232
  44.9 8.2 %collective-permute-start.14 = (bf16[8,16,512]{2,1,0:T(8,128)(2,1)S(1)}, bf16[8,16,512]{2,1,0:T(8,128)(2,1)S(1)}, u32[]{:S(2)}, u32[]{:S(2)}) collective-permute-start(bf16[8,16,512]{2,1,0:T(8,128)(2,1)S(1)} %get-tuple-element.103), channel_id=1, source_target_pairs={{0,8},{4,12},{8,0},{12,4},{1,9},{5,13},{9,1},{13,5},{2,10},{6,14},... | collective-permute-start | bytes 393224 | tf_op jit(solution)/shard_map/ppermute | solution.py:232
  53.1 1.5 %collective-permute-start.18 = (bf16[8,16,512]{2,1,0:T(8,128)(2,1)S(1)}, bf16[8,16,512]{2,1,0:T(8,128)(2,1)S(1)}, u32[]{:S(2)}, u32[]{:S(2)}) collective-permute-start(bf16[8,16,512]{2,1,0:T(8,128)(2,1)S(1)} %get-tuple-element.124), channel_id=1, source_target_pairs={{0,12},{4,8},{8,4},{12,0},{1,13},{5,9},{9,5},{13,1},{2,14},{6,10},... | collective-permute-start | bytes 393224 | tf_op jit(solution)/shard_map/ppermute | solution.py:232
  54.6 1.4 %shard_map.74 = (bf16[8,32,512]{2,1,0:T(8,128)(2,1)S(1)}, bf16[8,32,512]{2,1,0:T(8,128)(2,1)S(1)}) custom-call(s32[6]{0:T(128)S(1)} %compare_select_fusion.1.where, bf16[8,32,512]{2,1,0:T(8,128)(2,1)S(1)} %collective-permute-done.5.refs_0_, bf16[8,32,512]{2,1,0:T(8,128)(2,1)S(1)} %collective-permute-done.9.refs_1_, ...), custom_call_target="tpu_custom_call" | custom-call | flops 1024 | bytes 1024 | tf_op jit(solution)/shard_map/pallas_call | solution.py:102
  56.0 1.4 %shard_map.75 = (bf16[8,32,512]{2,1,0:T(8,128)(2,1)S(1)}, bf16[8,32,512]{2,1,0:T(8,128)(2,1)S(1)}) custom-call(s32[6]{0:T(128)S(1)} %compare_select_fusion.1.where, bf16[8,32,512]{2,1,0:T(8,128)(2,1)S(1)} %collective-permute-done.11.refs_0_, bf16[8,32,512]{2,1,0:T(8,128)(2,1)S(1)} %collective-permute-done.16.refs_1_, ...), custom_call_target="tpu_custom_call" | custom-call | flops 1024 | bytes 1024 | tf_op jit(solution)/shard_map/pallas_call | solution.py:102
  58.3 2.0 %collective-permute-done.15.refs_0_ = bf16[8,16,512]{2,1,0:T(8,128)(2,1)S(1)} collective-permute-done((bf16[8,16,512]{2,1,0:T(8,128)(2,1)S(1)}, bf16[8,16,512]{2,1,0:T(8,128)(2,1)S(1)}, u32[]{:S(2)}, u32[]{:S(2)}) %collective-permute-start.15) | collective-permute-done | bytes 131104 | tf_op jit(solution)/shard_map/ppermute | solution.py:232
  65.0 3.3 %collective-permute-start.21 = (bf16[8,32,512]{2,1,0:T(8,128)(2,1)S(1)}, bf16[8,32,512]{2,1,0:T(8,128)(2,1)S(1)}, u32[]{:S(2)}, u32[]{:S(2)}) collective-permute-start(bf16[8,32,512]{2,1,0:T(8,128)(2,1)S(1)} %get-tuple-element.127), channel_id=1, source_target_pairs={{0,8},{4,12},{8,0},{12,4},{1,9},{5,13},{9,1},{13,5},{2,10},{6,14},... | collective-permute-start | bytes 786440 | tf_op jit(solution)/shard_map/ppermute | solution.py:232
  68.3 1.4 %shard_map.80.refs_1_ = bf16[8,4,48,512]{3,2,1,0:T(8,128)(2,1)} custom-call(s32[6]{0:T(128)S(1)} %compare_select_fusion.1.where, bf16[8,16,512]{2,1,0:T(8,128)(2,1)S(1)} %collective-permute-done.15.refs_0_, bf16[8,16,512]{2,1,0:T(8,128)(2,1)S(1)} %collective-permute-done.14.refs_1_, bf16[8,16,512]{2,1,0:T(8,128)(2,1)S(1)} %shard_map.79.refs_2_, ...), custom_call_target="tpu_custom_call" | custom-call | flops 1024 | bytes 1024 | tf_op jit(solution)/shard_map/pallas_call | solution.py:190
  70.9 4.0 %collective-permute-done.19.refs_0_ = bf16[8,32,512]{2,1,0:T(8,128)(2,1)S(1)} collective-permute-done((bf16[8,32,512]{2,1,0:T(8,128)(2,1)S(1)}, bf16[8,32,512]{2,1,0:T(8,128)(2,1)S(1)}, u32[]{:S(2)}, u32[]{:S(2)}) %collective-permute-start.19) | collective-permute-done | bytes 262176 | tf_op jit(solution)/shard_map/ppermute | solution.py:232
  74.9 6.1 %collective-permute-done.20.refs_1_ = bf16[8,32,512]{2,1,0:T(8,128)(2,1)S(1)} collective-permute-done((bf16[8,32,512]{2,1,0:T(8,128)(2,1)S(1)}, bf16[8,32,512]{2,1,0:T(8,128)(2,1)S(1)}, u32[]{:S(2)}, u32[]{:S(2)}) %collective-permute-start.20) | collective-permute-done | bytes 262176 | tf_op jit(solution)/shard_map/ppermute | solution.py:232
  81.0 7.1 %collective-permute-done.21.refs_2_ = bf16[8,32,512]{2,1,0:T(8,128)(2,1)S(1)} collective-permute-done((bf16[8,32,512]{2,1,0:T(8,128)(2,1)S(1)}, bf16[8,32,512]{2,1,0:T(8,128)(2,1)S(1)}, u32[]{:S(2)}, u32[]{:S(2)}) %collective-permute-start.21) | collective-permute-done | bytes 262176 | tf_op jit(solution)/shard_map/ppermute | solution.py:232
  88.1 1.4 %shard_map.82 = bf16[8,4,48,512]{3,2,1,0:T(8,128)(2,1)} custom-call(s32[6]{0:T(128)S(1)} %compare_select_fusion.1.where, bf16[8,32,512]{2,1,0:T(8,128)(2,1)S(1)} %collective-permute-done.19.refs_0_, bf16[8,32,512]{2,1,0:T(8,128)(2,1)S(1)} %collective-permute-done.20.refs_1_, ...), custom_call_target="tpu_custom_call", output_to_operand_aliasing={{}: (4, {})} | custom-call | flops 1024 | bytes 1024 | tf_op jit(solution)/shard_map/pallas_call | solution.py:190
  (54 shorter events, 19.7 us)
Async XLA Ops:
  0.0 10.6 %copy-start.2 = (bf16[1,32,24]{1,2,0:T(8,128)(2,1)S(1)}, bf16[1,32,24]{1,2,0:T(8,128)(2,1)}, u32[]{:S(2)}) copy-start(bf16[1,32,24]{1,2,0:T(8,128)(2,1)} %param.10) | copy-start | bytes 4612
  0.0 10.7 %copy-start = (s32[1,4,4]{2,1,0:T(4,128)S(1)}, s32[1,4,4]{2,1,0:T(4,128)}, u32[]{:S(2)}) copy-start(s32[1,4,4]{2,1,0:T(4,128)} %param.8) | copy-start | bytes 196
  1.1 16.8 %collective-permute-start = (bf16[8,16,512]{2,1,0:T(8,128)(2,1)S(1)}, bf16[8,16,512]{2,1,0:T(8,128)(2,1)S(1)}, u32[]{:S(2)}, u32[]{:S(2)}) collective-permute-start(bf16[8,16,512]{2,1,0:T(8,128)(2,1)S(1)} %get-tuple-element.140), channel_id=1, source_target_pairs={{0,12},{4,8},{8,4},{12,0},{1,13},{5,9},{9,5},{13,1},{2,14},{6,10},... | collective-permute-start | bytes 393224 | tf_op jit(solution)/shard_map/ppermute | solution.py:232
  6.2 11.7 %collective-permute-start.1 = (bf16[8,16,512]{2,1,0:T(8,128)(2,1)S(1)}, bf16[8,16,512]{2,1,0:T(8,128)(2,1)S(1)}, u32[]{:S(2)}, u32[]{:S(2)}) collective-permute-start(bf16[8,16,512]{2,1,0:T(8,128)(2,1)S(1)} %get-tuple-element.139), channel_id=1, source_target_pairs={{0,8},{4,12},{8,0},{12,4},{1,9},{5,13},{9,1},{13,5},{2,10},{6,14},... | collective-permute-start | bytes 393224 | tf_op jit(solution)/shard_map/ppermute | solution.py:232
  6.2 11.7 %collective-permute-start.2 = (bf16[8,16,512]{2,1,0:T(8,128)(2,1)S(1)}, bf16[8,16,512]{2,1,0:T(8,128)(2,1)S(1)}, u32[]{:S(2)}, u32[]{:S(2)}) collective-permute-start(bf16[8,16,512]{2,1,0:T(8,128)(2,1)S(1)} %get-tuple-element.138), channel_id=1, source_target_pairs={{0,4},{4,0},{8,12},{12,8},{1,5},{5,1},{9,13},{13,9},{2,6},{6,2},{1... | collective-permute-start | bytes 393224 | tf_op jit(solution)/shard_map/ppermute | solution.py:232
  7.9 10.0 %collective-permute-start.3 = (bf16[4,48,512]{2,1,0:T(8,128)(2,1)S(1)}, bf16[4,48,512]{2,1,0:T(8,128)(2,1)S(1)}, u32[]{:S(2)}, u32[]{:S(2)}) collective-permute-start(bf16[4,48,512]{2,1,0:T(8,128)(2,1)S(1)} %get-tuple-element.134.refs_0_), channel_id=1, source_target_pairs={{0,2},{2,0},{1,3},{3,1},{4,6},{6,4},{5,7},{7,5},{8,10},{10,8},{9,1... | collective-permute-start | bytes 589832 | tf_op jit(solution)/shard_map/ppermute | solution.py:235
  9.6 8.7 %collective-permute-start.4 = (bf16[4,48,512]{2,1,0:T(8,128)(2,1)S(1)}, bf16[4,48,512]{2,1,0:T(8,128)(2,1)S(1)}, u32[]{:S(2)}, u32[]{:S(2)}) collective-permute-start(bf16[4,48,512]{2,1,0:T(8,128)(2,1)S(1)} %get-tuple-element.133.refs_1_), channel_id=1, source_target_pairs={{0,2},{2,0},{1,3},{3,1},{4,6},{6,4},{5,7},{7,5},{8,10},{10,8},{9,1... | collective-permute-start | bytes 589832 | tf_op jit(solution)/shard_map/ppermute | solution.py:235
  18.3 12.9 %collective-permute-start.10 = (bf16[8,32,512]{2,1,0:T(8,128)(2,1)S(1)}, bf16[8,32,512]{2,1,0:T(8,128)(2,1)S(1)}, u32[]{:S(2)}, u32[]{:S(2)}) collective-permute-start(bf16[8,32,512]{2,1,0:T(8,128)(2,1)S(1)} %get-tuple-element.90), channel_id=1, source_target_pairs={{0,4},{4,0},{8,12},{12,8},{1,5},{5,1},{9,13},{13,9},{2,6},{6,2},{1... | collective-permute-start | bytes 786440 | tf_op jit(solution)/shard_map/ppermute | solution.py:232
  19.7 14.8 %collective-permute-start.5 = (bf16[8,32,512]{2,1,0:T(8,128)(2,1)S(1)}, bf16[8,32,512]{2,1,0:T(8,128)(2,1)S(1)}, u32[]{:S(2)}, u32[]{:S(2)}) collective-permute-start(bf16[8,32,512]{2,1,0:T(8,128)(2,1)S(1)} %get-tuple-element.73), channel_id=1, source_target_pairs={{0,8},{4,12},{8,0},{12,4},{1,9},{5,13},{9,1},{13,5},{2,10},{6,14},... | collective-permute-start | bytes 786440 | tf_op jit(solution)/shard_map/ppermute | solution.py:232
  22.3 6.1 %collective-permute-start.6 = (bf16[8,16,512]{2,1,0:T(8,128)(2,1)S(1)}, bf16[8,16,512]{2,1,0:T(8,128)(2,1)S(1)}, u32[]{:S(2)}, u32[]{:S(2)}) collective-permute-start(bf16[8,16,512]{2,1,0:T(8,128)(2,1)S(1)} %collective-permute-done.2.refs_0_), channel_id=1, source_target_pairs={{0,2},{2,0},{1,3},{3,1},{4,6},{6,4},{5,7},{7,5},{8,10},{10,8},{9,1... | collective-permute-start | bytes 393224 | tf_op jit(solution)/shard_map/ppermute | solution.py:235
  23.8 6.0 %collective-permute-start.7 = (bf16[8,16,512]{2,1,0:T(8,128)(2,1)S(1)}, bf16[8,16,512]{2,1,0:T(8,128)(2,1)S(1)}, u32[]{:S(2)}, u32[]{:S(2)}) collective-permute-start(bf16[8,16,512]{2,1,0:T(8,128)(2,1)S(1)} %collective-permute-done.1.refs_0_), channel_id=1, source_target_pairs={{0,2},{2,0},{1,3},{3,1},{4,6},{6,4},{5,7},{7,5},{8,10},{10,8},{9,1... | collective-permute-start | bytes 393224 | tf_op jit(solution)/shard_map/ppermute | solution.py:235
  24.4 8.4 %collective-permute-start.8 = (bf16[8,16,512]{2,1,0:T(8,128)(2,1)S(1)}, bf16[8,16,512]{2,1,0:T(8,128)(2,1)S(1)}, u32[]{:S(2)}, u32[]{:S(2)}) collective-permute-start(bf16[8,16,512]{2,1,0:T(8,128)(2,1)S(1)} %collective-permute-done.refs_0_), channel_id=1, source_target_pairs={{0,2},{2,0},{1,3},{3,1},{4,6},{6,4},{5,7},{7,5},{8,10},{10,8},{9,1... | collective-permute-start | bytes 393224 | tf_op jit(solution)/shard_map/ppermute | solution.py:235
  31.2 8.5 %collective-permute-start.13 = (bf16[8,32,512]{2,1,0:T(8,128)(2,1)S(1)}, bf16[8,32,512]{2,1,0:T(8,128)(2,1)S(1)}, u32[]{:S(2)}, u32[]{:S(2)}) collective-permute-start(bf16[8,32,512]{2,1,0:T(8,128)(2,1)S(1)} %collective-permute-done.10.refs_0_), channel_id=1, source_target_pairs={{0,2},{2,0},{1,3},{3,1},{4,6},{6,4},{5,7},{7,5},{8,10},{10,8},{9,1... | collective-permute-start | bytes 786440 | tf_op jit(solution)/shard_map/ppermute | solution.py:235
  34.5 8.1 %collective-permute-start.9 = (bf16[8,32,512]{2,1,0:T(8,128)(2,1)S(1)}, bf16[8,32,512]{2,1,0:T(8,128)(2,1)S(1)}, u32[]{:S(2)}, u32[]{:S(2)}) collective-permute-start(bf16[8,32,512]{2,1,0:T(8,128)(2,1)S(1)} %collective-permute-done.5.refs_0_), channel_id=1, source_target_pairs={{0,2},{2,0},{1,3},{3,1},{4,6},{6,4},{5,7},{7,5},{8,10},{10,8},{9,1... | collective-permute-start | bytes 786440 | tf_op jit(solution)/shard_map/ppermute | solution.py:235
  35.9 8.3 %collective-permute-start.11 = (bf16[8,32,512]{2,1,0:T(8,128)(2,1)S(1)}, bf16[8,32,512]{2,1,0:T(8,128)(2,1)S(1)}, u32[]{:S(2)}, u32[]{:S(2)}) collective-permute-start(bf16[8,32,512]{2,1,0:T(8,128)(2,1)S(1)} %get-tuple-element.91), channel_id=1, source_target_pairs={{0,12},{4,8},{8,4},{12,0},{1,13},{5,9},{9,5},{13,1},{2,14},{6,10},... | collective-permute-start | bytes 786440 | tf_op jit(solution)/shard_map/ppermute | solution.py:232
  36.7 4.7 %collective-permute-start.12 = (bf16[24,16,512]{2,1,0:T(8,128)(2,1)S(1)}, bf16[24,16,512]{2,1,0:T(8,128)(2,1)S(1)}, u32[]{:S(2)}, u32[]{:S(2)}) collective-permute-start(bf16[24,16,512]{2,1,0:T(8,128)(2,1)S(1)} %shard_map.69), channel_id=1, source_target_pairs={{0,1},{1,0},{2,3},{3,2},{4,5},{5,4},{6,7},{7,6},{8,9},{9,8},{10,11... | collective-permute-start | bytes 1179656 | tf_op jit(solution)/shard_map/ppermute | solution.py:270
  44.2 11.8 %collective-permute-start.16 = (bf16[8,32,512]{2,1,0:T(8,128)(2,1)S(1)}, bf16[8,32,512]{2,1,0:T(8,128)(2,1)S(1)}, u32[]{:S(2)}, u32[]{:S(2)}) collective-permute-start(bf16[8,32,512]{2,1,0:T(8,128)(2,1)S(1)} %collective-permute-done.11.refs_0_), channel_id=1, source_target_pairs={{0,2},{2,0},{1,3},{3,1},{4,6},{6,4},{5,7},{7,5},{8,10},{10,8},{9,1... | collective-permute-start | bytes 786440 | tf_op jit(solution)/shard_map/ppermute | solution.py:235
  44.9 13.4 %collective-permute-start.14 = (bf16[8,16,512]{2,1,0:T(8,128)(2,1)S(1)}, bf16[8,16,512]{2,1,0:T(8,128)(2,1)S(1)}, u32[]{:S(2)}, u32[]{:S(2)}) collective-permute-start(bf16[8,16,512]{2,1,0:T(8,128)(2,1)S(1)} %get-tuple-element.103), channel_id=1, source_target_pairs={{0,8},{4,12},{8,0},{12,4},{1,9},{5,13},{9,1},{13,5},{2,10},{6,14},... | collective-permute-start | bytes 393224 | tf_op jit(solution)/shard_map/ppermute | solution.py:232
  53.1 7.2 %collective-permute-start.15 = (bf16[8,16,512]{2,1,0:T(8,128)(2,1)S(1)}, bf16[8,16,512]{2,1,0:T(8,128)(2,1)S(1)}, u32[]{:S(2)}, u32[]{:S(2)}) collective-permute-start(bf16[8,16,512]{2,1,0:T(8,128)(2,1)S(1)} %get-tuple-element.104), channel_id=1, source_target_pairs={{0,4},{4,0},{8,12},{12,8},{1,5},{5,1},{9,13},{13,9},{2,6},{6,2},{1... | collective-permute-start | bytes 393224 | tf_op jit(solution)/shard_map/ppermute | solution.py:232
  53.1 7.2 %collective-permute-start.18 = (bf16[8,16,512]{2,1,0:T(8,128)(2,1)S(1)}, bf16[8,16,512]{2,1,0:T(8,128)(2,1)S(1)}, u32[]{:S(2)}, u32[]{:S(2)}) collective-permute-start(bf16[8,16,512]{2,1,0:T(8,128)(2,1)S(1)} %get-tuple-element.124), channel_id=1, source_target_pairs={{0,12},{4,8},{8,4},{12,0},{1,13},{5,9},{9,5},{13,1},{2,14},{6,10},... | collective-permute-start | bytes 393224 | tf_op jit(solution)/shard_map/ppermute | solution.py:232
  60.3 2.3 %collective-permute-start.17 = (bf16[24,32,512]{2,1,0:T(8,128)(2,1)S(1)}, bf16[24,32,512]{2,1,0:T(8,128)(2,1)S(1)}, u32[]{:S(2)}, u32[]{:S(2)}) collective-permute-start(bf16[24,32,512]{2,1,0:T(8,128)(2,1)S(1)} %shard_map.76), channel_id=1, source_target_pairs={{0,1},{1,0},{2,3},{3,2},{4,5},{5,4},{6,7},{7,6},{8,9},{9,8},{10,11... | collective-permute-start | bytes 2359304 | tf_op jit(solution)/shard_map/ppermute | solution.py:280
  63.8 11.1 %collective-permute-start.19 = (bf16[8,32,512]{2,1,0:T(8,128)(2,1)S(1)}, bf16[8,32,512]{2,1,0:T(8,128)(2,1)S(1)}, u32[]{:S(2)}, u32[]{:S(2)}) collective-permute-start(bf16[8,32,512]{2,1,0:T(8,128)(2,1)S(1)} %get-tuple-element.125), channel_id=1, source_target_pairs={{0,12},{4,8},{8,4},{12,0},{1,13},{5,9},{9,5},{13,1},{2,14},{6,10},... | collective-permute-start | bytes 786440 | tf_op jit(solution)/shard_map/ppermute | solution.py:232
  65.0 16.0 %collective-permute-start.20 = (bf16[8,32,512]{2,1,0:T(8,128)(2,1)S(1)}, bf16[8,32,512]{2,1,0:T(8,128)(2,1)S(1)}, u32[]{:S(2)}, u32[]{:S(2)}) collective-permute-start(bf16[8,32,512]{2,1,0:T(8,128)(2,1)S(1)} %get-tuple-element.126), channel_id=1, source_target_pairs={{0,4},{4,0},{8,12},{12,8},{1,5},{5,1},{9,13},{13,9},{2,6},{6,2},{1... | collective-permute-start | bytes 786440 | tf_op jit(solution)/shard_map/ppermute | solution.py:232
  65.0 23.1 %collective-permute-start.21 = (bf16[8,32,512]{2,1,0:T(8,128)(2,1)S(1)}, bf16[8,32,512]{2,1,0:T(8,128)(2,1)S(1)}, u32[]{:S(2)}, u32[]{:S(2)}) collective-permute-start(bf16[8,32,512]{2,1,0:T(8,128)(2,1)S(1)} %get-tuple-element.127), channel_id=1, source_target_pairs={{0,8},{4,12},{8,0},{12,4},{1,9},{5,13},{9,1},{13,5},{2,10},{6,14},... | collective-permute-start | bytes 786440 | tf_op jit(solution)/shard_map/ppermute | solution.py:232
  (2 other events, 9.6 us)

commit v17 on v16

--- a/solution.py
+++ b/solution.py
@@ -282,10 +282,10 @@
     first[3], = anchor([first[3]], 20_000_000_000)
     outs, first[3] = fence((restore(kept, came, ratios, up, spots), first[3]))
     first[0] = here
-    back = [along_z(outs[j - 1], j) for j in (3, 1, 2)]
+    back = [along_z(outs[j - 1], j) for j in (1, 3, 2)]
     result = place(where, [first[j] for j in (1, 2, 3, 0)], spots, 0, shape)
     result = place(where, [outs[3]], [spots[3]], ROWS, shape, into=result)
-    return place(where, back, [spots[2], spots[0], spots[1]], ROWS, shape, into=result)
+    return place(where, back, [spots[0], spots[2], spots[1]], ROWS, shape, into=result)
 
 
 def plain(visibility, beam_transfer, tile_mask, first_block, eigen_modes, signal_noise):

time: 89.7 us -> 91.9 us (1.025)
  waiting for transfers between devices: 27.2 us -> 30.3 us
    ppermute x12, waiting for transfers between devices: 20.8 us -> 23.9 us  [along_z(): return lax.ppermute(value, 'fm', [(i, i ^ j) for i in range(parts)])]
  transfers between devices with their start and end apart: 22 -> 22, of which waited for: 10 -> 10; matrix products, arithmetic and copies ran while one was open for 1% -> 1% of each run, Pallas kernels for 25% -> 24%
where the time goes in v17:
time: 91.9 us; the launch traced here: 91.7 us
  starting transfers between devices  33.1 us (36%)
  waiting for transfers between devices  30.3 us (33%)
  Pallas kernels  25.1 us (27%)
  local copies, waits for them, and re-layouts  2.39 us (3%)
  between operations  0.92 us (1%)
    ppermute x12, waiting for transfers between devices, along_z(): return lax.ppermute(value, 'fm', [(i, i ^ j) for i in range(parts)])  23.9 us
    ppermute x12, starting transfers between devices, along_z(): return lax.ppermute(value, 'fm', [(i, i ^ j) for i in range(parts)])  23.8 us
    pallas_call x7, Pallas kernels, project(): pl.pallas_call(functools.partial(project_kernel, piece=piece, blocks=bloc...  9.57 us
    ppermute x8, starting transfers between devices, along_x(): return lax.ppermute(value, 'kl', other)  9.26 us
    pallas_call x1, Pallas kernels, hold(): pl.pallas_call(hold_kernel, grid_spec=pltpu.PrefetchScalarGridSpec(num_sc...  7.04 us
    ppermute x8, waiting for transfers between devices, along_x(): return lax.ppermute(value, 'kl', other)  5.08 us
    pallas_call x3, Pallas kernels, place(): pl.pallas_call(functools.partial(place_kernel, spots=spots, first=first),...  4.06 us
    pallas_call x4, Pallas kernels, reduce(): pl.pallas_call(reduce_kernel, grid=(rows // ROWS,), in_specs=[fixed(modes...  2.61 us
  transfers between devices with their start and end apart: 22, of which 10 were waited for; matrix products, arithmetic and copies ran while one was open for 1% of the time, Pallas kernels for 24%

profile of v17, /device:TPU:0, one launch (start us, length us, event | category | flops | bytes accessed | tf_op | source)
XLA Modules:
  0.0 91.7 jit_solution(17226791177472172130)
XLA Ops:
  1.1 5.1 %collective-permute-start = (bf16[8,16,512]{2,1,0:T(8,128)(2,1)S(1)}, bf16[8,16,512]{2,1,0:T(8,128)(2,1)S(1)}, u32[]{:S(2)}, u32[]{:S(2)}) collective-permute-start(bf16[8,16,512]{2,1,0:T(8,128)(2,1)S(1)} %get-tuple-element.140), channel_id=1, source_target_pairs={{0,12},{4,8},{8,4},{12,0},{1,13},{5,9},{9,5},{13,1},{2,14},{6,10},... | collective-permute-start | bytes 393224 | tf_op jit(solution)/shard_map/ppermute | solution.py:232
  7.9 1.7 %collective-permute-start.3 = (bf16[4,48,512]{2,1,0:T(8,128)(2,1)S(1)}, bf16[4,48,512]{2,1,0:T(8,128)(2,1)S(1)}, u32[]{:S(2)}, u32[]{:S(2)}) collective-permute-start(bf16[4,48,512]{2,1,0:T(8,128)(2,1)S(1)} %get-tuple-element.134.refs_0_), channel_id=1, source_target_pairs={{0,2},{2,0},{1,3},{3,1},{4,6},{6,4},{5,7},{7,5},{8,10},{10,8},{9,1... | collective-permute-start | bytes 589832 | tf_op jit(solution)/shard_map/ppermute | solution.py:235
  10.8 7.0 %shard_map.64 = (bf16[32,512,512]{2,1,0:T(8,128)(2,1)S(1)}, bf16[384,512]{1,0:T(8,128)(2,1)S(1)}, bf16[512,384]{1,0:T(8,128)(2,1)S(1)}) custom-call(s32[6]{0:T(128)S(1)} %compare_select_fusion.1.where, s32[4,4]{1,0:T(4,128)S(1)} %bitcast.27, s32[1]{0:T(128)S(6)} %copy.20.starts, bf16[32,512,512]{2,1,0:T(8,128)(2,1)} %bitcast.28, bf16[32,24]{1,0:T(8,128)(2,1)S(1)} %bitcast.26), custom_call_target="tpu_custom_call" | custom-call | flops 1024 | bytes 1024 | tf_op jit(solution)/shard_map/pallas_call | solution.py:63
  18.3 1.4 %collective-permute-start.10 = (bf16[8,32,512]{2,1,0:T(8,128)(2,1)S(1)}, bf16[8,32,512]{2,1,0:T(8,128)(2,1)S(1)}, u32[]{:S(2)}, u32[]{:S(2)}) collective-permute-start(bf16[8,32,512]{2,1,0:T(8,128)(2,1)S(1)} %get-tuple-element.90), channel_id=1, source_target_pairs={{0,4},{4,0},{8,12},{12,8},{1,5},{5,1},{9,13},{13,9},{2,6},{6,2},{1... | collective-permute-start | bytes 786440 | tf_op jit(solution)/shard_map/ppermute | solution.py:232
  19.7 2.7 %collective-permute-start.5 = (bf16[8,32,512]{2,1,0:T(8,128)(2,1)S(1)}, bf16[8,32,512]{2,1,0:T(8,128)(2,1)S(1)}, u32[]{:S(2)}, u32[]{:S(2)}) collective-permute-start(bf16[8,32,512]{2,1,0:T(8,128)(2,1)S(1)} %get-tuple-element.73), channel_id=1, source_target_pairs={{0,8},{4,12},{8,0},{12,4},{1,9},{5,13},{9,1},{13,5},{2,10},{6,14},... | collective-permute-start | bytes 786440 | tf_op jit(solution)/shard_map/ppermute | solution.py:232
  22.3 1.5 %collective-permute-start.6 = (bf16[8,16,512]{2,1,0:T(8,128)(2,1)S(1)}, bf16[8,16,512]{2,1,0:T(8,128)(2,1)S(1)}, u32[]{:S(2)}, u32[]{:S(2)}) collective-permute-start(bf16[8,16,512]{2,1,0:T(8,128)(2,1)S(1)} %collective-permute-done.2.refs_0_), channel_id=1, source_target_pairs={{0,2},{2,0},{1,3},{3,1},{4,6},{6,4},{5,7},{7,5},{8,10},{10,8},{9,1... | collective-permute-start | bytes 393224 | tf_op jit(solution)/shard_map/ppermute | solution.py:235
  24.4 1.5 %collective-permute-start.8 = (bf16[8,16,512]{2,1,0:T(8,128)(2,1)S(1)}, bf16[8,16,512]{2,1,0:T(8,128)(2,1)S(1)}, u32[]{:S(2)}, u32[]{:S(2)}) collective-permute-start(bf16[8,16,512]{2,1,0:T(8,128)(2,1)S(1)} %collective-permute-done.refs_0_), channel_id=1, source_target_pairs={{0,2},{2,0},{1,3},{3,1},{4,6},{6,4},{5,7},{7,5},{8,10},{10,8},{9,1... | collective-permute-start | bytes 393224 | tf_op jit(solution)/shard_map/ppermute | solution.py:235
  25.8 1.4 %shard_map.65 = (bf16[8,48,512]{2,1,0:T(8,128)(2,1)S(1)}, bf16[8,48,512]{2,1,0:T(8,128)(2,1)S(1)}) custom-call(s32[6]{0:T(128)S(1)} %compare_select_fusion.1.where, bf16[4,48,512]{2,1,0:T(8,128)(2,1)S(1)} %get-tuple-element.134.refs_0_, bf16[4,48,512]{2,1,0:T(8,128)(2,1)S(1)} %get-tuple-element.133.refs_1_, ...), custom_call_target="tpu_custom_call" | custom-call | flops 400000000 | bytes 1024 | tf_op jit(solution)/shard_map/pallas_call | solution.py:102
  31.2 1.6 %collective-permute-start.13 = (bf16[8,32,512]{2,1,0:T(8,128)(2,1)S(1)}, bf16[8,32,512]{2,1,0:T(8,128)(2,1)S(1)}, u32[]{:S(2)}, u32[]{:S(2)}) collective-permute-start(bf16[8,32,512]{2,1,0:T(8,128)(2,1)S(1)} %collective-permute-done.10.refs_0_), channel_id=1, source_target_pairs={{0,2},{2,0},{1,3},{3,1},{4,6},{6,4},{5,7},{7,5},{8,10},{10,8},{9,1... | collective-permute-start | bytes 786440 | tf_op jit(solution)/shard_map/ppermute | solution.py:235
  34.5 1.4 %collective-permute-start.9 = (bf16[8,32,512]{2,1,0:T(8,128)(2,1)S(1)}, bf16[8,32,512]{2,1,0:T(8,128)(2,1)S(1)}, u32[]{:S(2)}, u32[]{:S(2)}) collective-permute-start(bf16[8,32,512]{2,1,0:T(8,128)(2,1)S(1)} %collective-permute-done.5.refs_0_), channel_id=1, source_target_pairs={{0,2},{2,0},{1,3},{3,1},{4,6},{6,4},{5,7},{7,5},{8,10},{10,8},{9,1... | collective-permute-start | bytes 786440 | tf_op jit(solution)/shard_map/ppermute | solution.py:235
  36.7 3.0 %collective-permute-done.13.refs_0_ = bf16[8,32,512]{2,1,0:T(8,128)(2,1)S(1)} collective-permute-done((bf16[8,32,512]{2,1,0:T(8,128)(2,1)S(1)}, bf16[8,32,512]{2,1,0:T(8,128)(2,1)S(1)}, u32[]{:S(2)}, u32[]{:S(2)}) %collective-permute-start.13) | collective-permute-done | bytes 262176 | tf_op jit(solution)/shard_map/ppermute | solution.py:235
  40.0 1.4 %shard_map.73 = (bf16[8,32,512]{2,1,0:T(8,128)(2,1)S(1)}, bf16[8,32,512]{2,1,0:T(8,128)(2,1)S(1)}) custom-call(s32[6]{0:T(128)S(1)} %compare_select_fusion.1.where, bf16[8,32,512]{2,1,0:T(8,128)(2,1)S(1)} %collective-permute-done.10.refs_0_, bf16[8,32,512]{2,1,0:T(8,128)(2,1)S(1)} %shard_map.72.refs_1_, ...), custom_call_target="tpu_custom_call" | custom-call | flops 1024 | bytes 1024 | tf_op jit(solution)/shard_map/pallas_call | solution.py:102
  42.6 1.7 %collective-permute-done.11.refs_0_ = bf16[8,32,512]{2,1,0:T(8,128)(2,1)S(1)} collective-permute-done((bf16[8,32,512]{2,1,0:T(8,128)(2,1)S(1)}, bf16[8,32,512]{2,1,0:T(8,128)(2,1)S(1)}, u32[]{:S(2)}, u32[]{:S(2)}) %collective-permute-start.11) | collective-permute-done | bytes 262176 | tf_op jit(solution)/shard_map/ppermute | solution.py:232
  44.9 8.2 %collective-permute-start.14 = (bf16[8,16,512]{2,1,0:T(8,128)(2,1)S(1)}, bf16[8,16,512]{2,1,0:T(8,128)(2,1)S(1)}, u32[]{:S(2)}, u32[]{:S(2)}) collective-permute-start(bf16[8,16,512]{2,1,0:T(8,128)(2,1)S(1)} %get-tuple-element.103), channel_id=1, source_target_pairs={{0,8},{4,12},{8,0},{12,4},{1,9},{5,13},{9,1},{13,5},{2,10},{6,14},... | collective-permute-start | bytes 393224 | tf_op jit(solution)/shard_map/ppermute | solution.py:232
  53.1 1.5 %collective-permute-start.18 = (bf16[8,16,512]{2,1,0:T(8,128)(2,1)S(1)}, bf16[8,16,512]{2,1,0:T(8,128)(2,1)S(1)}, u32[]{:S(2)}, u32[]{:S(2)}) collective-permute-start(bf16[8,16,512]{2,1,0:T(8,128)(2,1)S(1)} %get-tuple-element.124), channel_id=1, source_target_pairs={{0,12},{4,8},{8,4},{12,0},{1,13},{5,9},{9,5},{13,1},{2,14},{6,10},... | collective-permute-start | bytes 393224 | tf_op jit(solution)/shard_map/ppermute | solution.py:232
  54.6 1.4 %shard_map.74 = (bf16[8,32,512]{2,1,0:T(8,128)(2,1)S(1)}, bf16[8,32,512]{2,1,0:T(8,128)(2,1)S(1)}) custom-call(s32[6]{0:T(128)S(1)} %compare_select_fusion.1.where, bf16[8,32,512]{2,1,0:T(8,128)(2,1)S(1)} %collective-permute-done.5.refs_0_, bf16[8,32,512]{2,1,0:T(8,128)(2,1)S(1)} %collective-permute-done.9.refs_1_, ...), custom_call_target="tpu_custom_call" | custom-call | flops 1024 | bytes 1024 | tf_op jit(solution)/shard_map/pallas_call | solution.py:102
  56.0 1.4 %shard_map.75 = (bf16[8,32,512]{2,1,0:T(8,128)(2,1)S(1)}, bf16[8,32,512]{2,1,0:T(8,128)(2,1)S(1)}) custom-call(s32[6]{0:T(128)S(1)} %compare_select_fusion.1.where, bf16[8,32,512]{2,1,0:T(8,128)(2,1)S(1)} %collective-permute-done.11.refs_0_, bf16[8,32,512]{2,1,0:T(8,128)(2,1)S(1)} %collective-permute-done.16.refs_1_, ...), custom_call_target="tpu_custom_call" | custom-call | flops 1024 | bytes 1024 | tf_op jit(solution)/shard_map/pallas_call | solution.py:102
  58.3 2.0 %collective-permute-done.15.refs_0_ = bf16[8,16,512]{2,1,0:T(8,128)(2,1)S(1)} collective-permute-done((bf16[8,16,512]{2,1,0:T(8,128)(2,1)S(1)}, bf16[8,16,512]{2,1,0:T(8,128)(2,1)S(1)}, u32[]{:S(2)}, u32[]{:S(2)}) %collective-permute-start.15) | collective-permute-done | bytes 131104 | tf_op jit(solution)/shard_map/ppermute | solution.py:232
  63.9 1.6 %collective-permute-start.20 = (bf16[8,32,512]{2,1,0:T(8,128)(2,1)S(1)}, bf16[8,32,512]{2,1,0:T(8,128)(2,1)S(1)}, u32[]{:S(2)}, u32[]{:S(2)}) collective-permute-start(bf16[8,32,512]{2,1,0:T(8,128)(2,1)S(1)} %get-tuple-element.126), channel_id=1, source_target_pairs={{0,12},{4,8},{8,4},{12,0},{1,13},{5,9},{9,5},{13,1},{2,14},{6,10},... | collective-permute-start | bytes 786440 | tf_op jit(solution)/shard_map/ppermute | solution.py:232
  65.5 1.9 %collective-permute-start.21 = (bf16[8,32,512]{2,1,0:T(8,128)(2,1)S(1)}, bf16[8,32,512]{2,1,0:T(8,128)(2,1)S(1)}, u32[]{:S(2)}, u32[]{:S(2)}) collective-permute-start(bf16[8,32,512]{2,1,0:T(8,128)(2,1)S(1)} %get-tuple-element.127), channel_id=1, source_target_pairs={{0,8},{4,12},{8,0},{12,4},{1,9},{5,13},{9,1},{13,5},{2,10},{6,14},... | collective-permute-start | bytes 786440 | tf_op jit(solution)/shard_map/ppermute | solution.py:232
  67.4 1.4 %shard_map.80.refs_1_ = bf16[8,4,48,512]{3,2,1,0:T(8,128)(2,1)} custom-call(s32[6]{0:T(128)S(1)} %compare_select_fusion.1.where, bf16[8,16,512]{2,1,0:T(8,128)(2,1)S(1)} %collective-permute-done.15.refs_0_, bf16[8,16,512]{2,1,0:T(8,128)(2,1)S(1)} %collective-permute-done.14.refs_1_, bf16[8,16,512]{2,1,0:T(8,128)(2,1)S(1)} %shard_map.79.refs_2_, ...), custom_call_target="tpu_custom_call" | custom-call | flops 1024 | bytes 1024 | tf_op jit(solution)/shard_map/pallas_call | solution.py:190
  70.0 7.4 %collective-permute-done.19.refs_0_ = bf16[8,32,512]{2,1,0:T(8,128)(2,1)S(1)} collective-permute-done((bf16[8,32,512]{2,1,0:T(8,128)(2,1)S(1)}, bf16[8,32,512]{2,1,0:T(8,128)(2,1)S(1)}, u32[]{:S(2)}, u32[]{:S(2)}) %collective-permute-start.19) | collective-permute-done | bytes 262176 | tf_op jit(solution)/shard_map/ppermute | solution.py:232
  78.3 12.0 %collective-permute-done.21.refs_2_ = bf16[8,32,512]{2,1,0:T(8,128)(2,1)S(1)} collective-permute-done((bf16[8,32,512]{2,1,0:T(8,128)(2,1)S(1)}, bf16[8,32,512]{2,1,0:T(8,128)(2,1)S(1)}, u32[]{:S(2)}, u32[]{:S(2)}) %collective-permute-start.21) | collective-permute-done | bytes 262176 | tf_op jit(solution)/shard_map/ppermute | solution.py:232
  90.3 1.4 %shard_map.82 = bf16[8,4,48,512]{3,2,1,0:T(8,128)(2,1)} custom-call(s32[6]{0:T(128)S(1)} %compare_select_fusion.1.where, bf16[8,32,512]{2,1,0:T(8,128)(2,1)S(1)} %collective-permute-done.19.refs_0_, bf16[8,32,512]{2,1,0:T(8,128)(2,1)S(1)} %collective-permute-done.20.refs_1_, ...), custom_call_target="tpu_custom_call", output_to_operand_aliasing={{}: (4, {})} | custom-call | flops 1024 | bytes 1024 | tf_op jit(solution)/shard_map/pallas_call | solution.py:190
  (54 shorter events, 19.5 us)
Async XLA Ops:
  0.0 10.6 %copy-start.2 = (bf16[1,32,24]{1,2,0:T(8,128)(2,1)S(1)}, bf16[1,32,24]{1,2,0:T(8,128)(2,1)}, u32[]{:S(2)}) copy-start(bf16[1,32,24]{1,2,0:T(8,128)(2,1)} %param.10) | copy-start | bytes 4612
  0.0 10.7 %copy-start = (s32[1,4,4]{2,1,0:T(4,128)S(1)}, s32[1,4,4]{2,1,0:T(4,128)}, u32[]{:S(2)}) copy-start(s32[1,4,4]{2,1,0:T(4,128)} %param.8) | copy-start | bytes 196
  1.1 16.8 %collective-permute-start = (bf16[8,16,512]{2,1,0:T(8,128)(2,1)S(1)}, bf16[8,16,512]{2,1,0:T(8,128)(2,1)S(1)}, u32[]{:S(2)}, u32[]{:S(2)}) collective-permute-start(bf16[8,16,512]{2,1,0:T(8,128)(2,1)S(1)} %get-tuple-element.140), channel_id=1, source_target_pairs={{0,12},{4,8},{8,4},{12,0},{1,13},{5,9},{9,5},{13,1},{2,14},{6,10},... | collective-permute-start | bytes 393224 | tf_op jit(solution)/shard_map/ppermute | solution.py:232
  6.2 11.7 %collective-permute-start.1 = (bf16[8,16,512]{2,1,0:T(8,128)(2,1)S(1)}, bf16[8,16,512]{2,1,0:T(8,128)(2,1)S(1)}, u32[]{:S(2)}, u32[]{:S(2)}) collective-permute-start(bf16[8,16,512]{2,1,0:T(8,128)(2,1)S(1)} %get-tuple-element.139), channel_id=1, source_target_pairs={{0,8},{4,12},{8,0},{12,4},{1,9},{5,13},{9,1},{13,5},{2,10},{6,14},... | collective-permute-start | bytes 393224 | tf_op jit(solution)/shard_map/ppermute | solution.py:232
  6.2 11.7 %collective-permute-start.2 = (bf16[8,16,512]{2,1,0:T(8,128)(2,1)S(1)}, bf16[8,16,512]{2,1,0:T(8,128)(2,1)S(1)}, u32[]{:S(2)}, u32[]{:S(2)}) collective-permute-start(bf16[8,16,512]{2,1,0:T(8,128)(2,1)S(1)} %get-tuple-element.138), channel_id=1, source_target_pairs={{0,4},{4,0},{8,12},{12,8},{1,5},{5,1},{9,13},{13,9},{2,6},{6,2},{1... | collective-permute-start | bytes 393224 | tf_op jit(solution)/shard_map/ppermute | solution.py:232
  7.9 10.0 %collective-permute-start.3 = (bf16[4,48,512]{2,1,0:T(8,128)(2,1)S(1)}, bf16[4,48,512]{2,1,0:T(8,128)(2,1)S(1)}, u32[]{:S(2)}, u32[]{:S(2)}) collective-permute-start(bf16[4,48,512]{2,1,0:T(8,128)(2,1)S(1)} %get-tuple-element.134.refs_0_), channel_id=1, source_target_pairs={{0,2},{2,0},{1,3},{3,1},{4,6},{6,4},{5,7},{7,5},{8,10},{10,8},{9,1... | collective-permute-start | bytes 589832 | tf_op jit(solution)/shard_map/ppermute | solution.py:235
  9.6 8.7 %collective-permute-start.4 = (bf16[4,48,512]{2,1,0:T(8,128)(2,1)S(1)}, bf16[4,48,512]{2,1,0:T(8,128)(2,1)S(1)}, u32[]{:S(2)}, u32[]{:S(2)}) collective-permute-start(bf16[4,48,512]{2,1,0:T(8,128)(2,1)S(1)} %get-tuple-element.133.refs_1_), channel_id=1, source_target_pairs={{0,2},{2,0},{1,3},{3,1},{4,6},{6,4},{5,7},{7,5},{8,10},{10,8},{9,1... | collective-permute-start | bytes 589832 | tf_op jit(solution)/shard_map/ppermute | solution.py:235
  18.3 12.9 %collective-permute-start.10 = (bf16[8,32,512]{2,1,0:T(8,128)(2,1)S(1)}, bf16[8,32,512]{2,1,0:T(8,128)(2,1)S(1)}, u32[]{:S(2)}, u32[]{:S(2)}) collective-permute-start(bf16[8,32,512]{2,1,0:T(8,128)(2,1)S(1)} %get-tuple-element.90), channel_id=1, source_target_pairs={{0,4},{4,0},{8,12},{12,8},{1,5},{5,1},{9,13},{13,9},{2,6},{6,2},{1... | collective-permute-start | bytes 786440 | tf_op jit(solution)/shard_map/ppermute | solution.py:232
  19.7 14.8 %collective-permute-start.5 = (bf16[8,32,512]{2,1,0:T(8,128)(2,1)S(1)}, bf16[8,32,512]{2,1,0:T(8,128)(2,1)S(1)}, u32[]{:S(2)}, u32[]{:S(2)}) collective-permute-start(bf16[8,32,512]{2,1,0:T(8,128)(2,1)S(1)} %get-tuple-element.73), channel_id=1, source_target_pairs={{0,8},{4,12},{8,0},{12,4},{1,9},{5,13},{9,1},{13,5},{2,10},{6,14},... | collective-permute-start | bytes 786440 | tf_op jit(solution)/shard_map/ppermute | solution.py:232
  22.3 6.1 %collective-permute-start.6 = (bf16[8,16,512]{2,1,0:T(8,128)(2,1)S(1)}, bf16[8,16,512]{2,1,0:T(8,128)(2,1)S(1)}, u32[]{:S(2)}, u32[]{:S(2)}) collective-permute-start(bf16[8,16,512]{2,1,0:T(8,128)(2,1)S(1)} %collective-permute-done.2.refs_0_), channel_id=1, source_target_pairs={{0,2},{2,0},{1,3},{3,1},{4,6},{6,4},{5,7},{7,5},{8,10},{10,8},{9,1... | collective-permute-start | bytes 393224 | tf_op jit(solution)/shard_map/ppermute | solution.py:235
  23.8 6.0 %collective-permute-start.7 = (bf16[8,16,512]{2,1,0:T(8,128)(2,1)S(1)}, bf16[8,16,512]{2,1,0:T(8,128)(2,1)S(1)}, u32[]{:S(2)}, u32[]{:S(2)}) collective-permute-start(bf16[8,16,512]{2,1,0:T(8,128)(2,1)S(1)} %collective-permute-done.1.refs_0_), channel_id=1, source_target_pairs={{0,2},{2,0},{1,3},{3,1},{4,6},{6,4},{5,7},{7,5},{8,10},{10,8},{9,1... | collective-permute-start | bytes 393224 | tf_op jit(solution)/shard_map/ppermute | solution.py:235
  24.4 8.4 %collective-permute-start.8 = (bf16[8,16,512]{2,1,0:T(8,128)(2,1)S(1)}, bf16[8,16,512]{2,1,0:T(8,128)(2,1)S(1)}, u32[]{:S(2)}, u32[]{:S(2)}) collective-permute-start(bf16[8,16,512]{2,1,0:T(8,128)(2,1)S(1)} %collective-permute-done.refs_0_), channel_id=1, source_target_pairs={{0,2},{2,0},{1,3},{3,1},{4,6},{6,4},{5,7},{7,5},{8,10},{10,8},{9,1... | collective-permute-start | bytes 393224 | tf_op jit(solution)/shard_map/ppermute | solution.py:235
  31.2 8.5 %collective-permute-start.13 = (bf16[8,32,512]{2,1,0:T(8,128)(2,1)S(1)}, bf16[8,32,512]{2,1,0:T(8,128)(2,1)S(1)}, u32[]{:S(2)}, u32[]{:S(2)}) collective-permute-start(bf16[8,32,512]{2,1,0:T(8,128)(2,1)S(1)} %collective-permute-done.10.refs_0_), channel_id=1, source_target_pairs={{0,2},{2,0},{1,3},{3,1},{4,6},{6,4},{5,7},{7,5},{8,10},{10,8},{9,1... | collective-permute-start | bytes 786440 | tf_op jit(solution)/shard_map/ppermute | solution.py:235
  34.5 8.1 %collective-permute-start.9 = (bf16[8,32,512]{2,1,0:T(8,128)(2,1)S(1)}, bf16[8,32,512]{2,1,0:T(8,128)(2,1)S(1)}, u32[]{:S(2)}, u32[]{:S(2)}) collective-permute-start(bf16[8,32,512]{2,1,0:T(8,128)(2,1)S(1)} %collective-permute-done.5.refs_0_), channel_id=1, source_target_pairs={{0,2},{2,0},{1,3},{3,1},{4,6},{6,4},{5,7},{7,5},{8,10},{10,8},{9,1... | collective-permute-start | bytes 786440 | tf_op jit(solution)/shard_map/ppermute | solution.py:235
  35.9 8.3 %collective-permute-start.11 = (bf16[8,32,512]{2,1,0:T(8,128)(2,1)S(1)}, bf16[8,32,512]{2,1,0:T(8,128)(2,1)S(1)}, u32[]{:S(2)}, u32[]{:S(2)}) collective-permute-start(bf16[8,32,512]{2,1,0:T(8,128)(2,1)S(1)} %get-tuple-element.91), channel_id=1, source_target_pairs={{0,12},{4,8},{8,4},{12,0},{1,13},{5,9},{9,5},{13,1},{2,14},{6,10},... | collective-permute-start | bytes 786440 | tf_op jit(solution)/shard_map/ppermute | solution.py:232
  36.7 4.7 %collective-permute-start.12 = (bf16[24,16,512]{2,1,0:T(8,128)(2,1)S(1)}, bf16[24,16,512]{2,1,0:T(8,128)(2,1)S(1)}, u32[]{:S(2)}, u32[]{:S(2)}) collective-permute-start(bf16[24,16,512]{2,1,0:T(8,128)(2,1)S(1)} %shard_map.69), channel_id=1, source_target_pairs={{0,1},{1,0},{2,3},{3,2},{4,5},{5,4},{6,7},{7,6},{8,9},{9,8},{10,11... | collective-permute-start | bytes 1179656 | tf_op jit(solution)/shard_map/ppermute | solution.py:270
  44.2 11.8 %collective-permute-start.16 = (bf16[8,32,512]{2,1,0:T(8,128)(2,1)S(1)}, bf16[8,32,512]{2,1,0:T(8,128)(2,1)S(1)}, u32[]{:S(2)}, u32[]{:S(2)}) collective-permute-start(bf16[8,32,512]{2,1,0:T(8,128)(2,1)S(1)} %collective-permute-done.11.refs_0_), channel_id=1, source_target_pairs={{0,2},{2,0},{1,3},{3,1},{4,6},{6,4},{5,7},{7,5},{8,10},{10,8},{9,1... | collective-permute-start | bytes 786440 | tf_op jit(solution)/shard_map/ppermute | solution.py:235
  44.9 13.4 %collective-permute-start.14 = (bf16[8,16,512]{2,1,0:T(8,128)(2,1)S(1)}, bf16[8,16,512]{2,1,0:T(8,128)(2,1)S(1)}, u32[]{:S(2)}, u32[]{:S(2)}) collective-permute-start(bf16[8,16,512]{2,1,0:T(8,128)(2,1)S(1)} %get-tuple-element.103), channel_id=1, source_target_pairs={{0,8},{4,12},{8,0},{12,4},{1,9},{5,13},{9,1},{13,5},{2,10},{6,14},... | collective-permute-start | bytes 393224 | tf_op jit(solution)/shard_map/ppermute | solution.py:232
  53.1 7.2 %collective-permute-start.15 = (bf16[8,16,512]{2,1,0:T(8,128)(2,1)S(1)}, bf16[8,16,512]{2,1,0:T(8,128)(2,1)S(1)}, u32[]{:S(2)}, u32[]{:S(2)}) collective-permute-start(bf16[8,16,512]{2,1,0:T(8,128)(2,1)S(1)} %get-tuple-element.104), channel_id=1, source_target_pairs={{0,4},{4,0},{8,12},{12,8},{1,5},{5,1},{9,13},{13,9},{2,6},{6,2},{1... | collective-permute-start | bytes 393224 | tf_op jit(solution)/shard_map/ppermute | solution.py:232
  53.1 7.2 %collective-permute-start.18 = (bf16[8,16,512]{2,1,0:T(8,128)(2,1)S(1)}, bf16[8,16,512]{2,1,0:T(8,128)(2,1)S(1)}, u32[]{:S(2)}, u32[]{:S(2)}) collective-permute-start(bf16[8,16,512]{2,1,0:T(8,128)(2,1)S(1)} %get-tuple-element.124), channel_id=1, source_target_pairs={{0,12},{4,8},{8,4},{12,0},{1,13},{5,9},{9,5},{13,1},{2,14},{6,10},... | collective-permute-start | bytes 393224 | tf_op jit(solution)/shard_map/ppermute | solution.py:232
  60.3 2.3 %collective-permute-start.17 = (bf16[24,32,512]{2,1,0:T(8,128)(2,1)S(1)}, bf16[24,32,512]{2,1,0:T(8,128)(2,1)S(1)}, u32[]{:S(2)}, u32[]{:S(2)}) collective-permute-start(bf16[24,32,512]{2,1,0:T(8,128)(2,1)S(1)} %shard_map.76), channel_id=1, source_target_pairs={{0,1},{1,0},{2,3},{3,2},{4,5},{5,4},{6,7},{7,6},{8,9},{9,8},{10,11... | collective-permute-start | bytes 2359304 | tf_op jit(solution)/shard_map/ppermute | solution.py:280
  63.8 13.6 %collective-permute-start.19 = (bf16[8,32,512]{2,1,0:T(8,128)(2,1)S(1)}, bf16[8,32,512]{2,1,0:T(8,128)(2,1)S(1)}, u32[]{:S(2)}, u32[]{:S(2)}) collective-permute-start(bf16[8,32,512]{2,1,0:T(8,128)(2,1)S(1)} %get-tuple-element.125), channel_id=1, source_target_pairs={{0,4},{4,0},{8,12},{12,8},{1,5},{5,1},{9,13},{13,9},{2,6},{6,2},{1... | collective-permute-start | bytes 786440 | tf_op jit(solution)/shard_map/ppermute | solution.py:232
  63.9 14.4 %collective-permute-start.20 = (bf16[8,32,512]{2,1,0:T(8,128)(2,1)S(1)}, bf16[8,32,512]{2,1,0:T(8,128)(2,1)S(1)}, u32[]{:S(2)}, u32[]{:S(2)}) collective-permute-start(bf16[8,32,512]{2,1,0:T(8,128)(2,1)S(1)} %get-tuple-element.126), channel_id=1, source_target_pairs={{0,12},{4,8},{8,4},{12,0},{1,13},{5,9},{9,5},{13,1},{2,14},{6,10},... | collective-permute-start | bytes 786440 | tf_op jit(solution)/shard_map/ppermute | solution.py:232
  65.5 24.8 %collective-permute-start.21 = (bf16[8,32,512]{2,1,0:T(8,128)(2,1)S(1)}, bf16[8,32,512]{2,1,0:T(8,128)(2,1)S(1)}, u32[]{:S(2)}, u32[]{:S(2)}) collective-permute-start(bf16[8,32,512]{2,1,0:T(8,128)(2,1)S(1)} %get-tuple-element.127), channel_id=1, source_target_pairs={{0,8},{4,12},{8,0},{12,4},{1,9},{5,13},{9,1},{13,5},{2,10},{6,14},... | collective-permute-start | bytes 786440 | tf_op jit(solution)/shard_map/ppermute | solution.py:232
  (2 other events, 9.6 us)

commit v18 on v15

--- a/solution.py
+++ b/solution.py
@@ -27,14 +27,14 @@
             ).astype(jnp.bfloat16)
     modes = modes_ref[...]
 
-    def pick(shape, axis):
+    def pick(shape, axis, orders=0):
         big = lax.broadcasted_iota(jnp.int32, shape, axis) // ROWS
         small = lax.broadcasted_iota(jnp.int32, shape, 1 - axis)
         if freq in shape:
             piece, within = big // freqs, big % freqs
             big = within
             for j in range(PARTS):
-                big = jnp.where(piece == j, where[j] * freqs + within, big)
+                big = jnp.where(piece == j, where[orders + j] * freqs + within, big)
         return jnp.where(big == small, 1.0, 0.0).astype(jnp.bfloat16)
 
     def lane(shape):
@@ -48,7 +48,7 @@
     tall = dot(pick((n_modes * ROWS, n_modes), 0), modes, ((1,), (1,))).astype(jnp.bfloat16)
     value = dot(tall, pick((freq, freq * ROWS), 1), ((1,), (0,)))
     down_ref[...] = jnp.where(lane(value.shape), value, 0.0).astype(jnp.bfloat16)
-    tall = dot(pick((freq * ROWS, freq), 0), modes, ((1,), (0,))).astype(jnp.bfloat16)
+    tall = dot(pick((freq * ROWS, freq), 0, PARTS + 2), modes, ((1,), (0,))).astype(jnp.bfloat16)
     value = dot(tall, pick((n_modes, n_modes * ROWS), 1), ((1,), (0,)))
     up_ref[...] = jnp.where(lane(value.shape), value, 0.0).astype(jnp.bfloat16)
     for f, copy in enumerate(copies):
@@ -174,7 +174,7 @@
     pieces, out, sems = refs[:count], refs[-2], refs[-1]
     rows = pieces[0].shape[1]
     copies = [
-        pltpu.make_async_copy(pieces[n], out.at[low:high, where[j], first:first + rows, :], sems.at[n])
+        pltpu.make_async_copy(pieces[n], out.at[low:high, where[PARTS + 2 + j], first:first + rows, :], sems.at[n])
         for n, (j, low, high) in enumerate(spots)
     ]
     for copy in copies:
@@ -228,19 +228,22 @@
     z, x, p = lax.axis_index("fm"), lax.axis_index("kl"), lax.axis_index("pol")
     other = [(0, 1), (1, 0)]
 
-    def along_z(value, j):
+    def shift_z(value, j):
+        return lax.ppermute(value, "fm", [(i, (i + j) % parts) for i in range(parts)])
+
+    def swap_z(value, j):
         return lax.ppermute(value, "fm", [(i, i ^ j) for i in range(parts)])
 
     def along_x(value):
         return lax.ppermute(value, "kl", other)
 
     def cut(j, first, rows):
-        return lax.dynamic_slice(visibility, (0, z ^ j, first, 0), (freqs, 1, rows, base)).reshape(freqs, rows, base)
-
-    index = jnp.arange(parts + 2, dtype=jnp.int32)
-    where = jnp.where(
-        index < parts, z ^ index, jnp.where(index == parts, (x == p).astype(jnp.int32), x * ell_tiles)
-    ).astype(jnp.int32)
+        return lax.dynamic_slice(visibility, (0, (z + j) % parts, first, 0), (freqs, 1, rows, base)).reshape(freqs, rows, base)
+
+    index = jnp.arange(2 * parts + 2, dtype=jnp.int32)
+    where = jnp.where(index < parts, (z - index) % parts, z ^ (index - parts - 2))
+    where = jnp.where(index == parts, (x == p).astype(jnp.int32), where)
+    where = jnp.where(index == parts + 1, x * ell_tiles, where).astype(jnp.int32)
     ratio = signal_noise[0] / (1.0 + signal_noise[0])
     ratios = jnp.broadcast_to(ratio[:, None, None], (n_modes, 1, ell))
     beam = beam_transfer.reshape(freq_total, base, ell)
@@ -250,30 +253,31 @@
     most, half = rows_all - ROWS, freqs // 2
     blocks = [[(0, f)] for f in range(freqs)]
     halves = [[(f // half, f % half)] for f in range(freqs)]
-    a = {j: along_z(cut(j, 0, ROWS), j) for j in (3, 2, 1)}
+    a = {j: shift_z(cut(j, 0, ROWS), j) for j in (1, 3, 2)}
     mine = [cut(0, 0, rows_all)[n:n + half] for n in (0, half)]
     others = [along_x(part) for part in mine]
     b = {j: cut(j, ROWS, most) for j in (1, 2, 3)}
     held, down, up = hold(where, tile_mask[0], first_block, beam, eigen_modes[0])
-    (a[3], a[2], a[1]), b, others, down, up = fence(((a[3], a[2], a[1]), b, others, down, up))
-    b[1], b[2] = along_z(b[1], 1), along_z(b[2], 2)
+    (a[1], a[3], a[2]), b, others, down, up = fence(((a[1], a[3], a[2]), b, others, down, up))
+    b[1], b[3] = shift_z(b[1], 1), shift_z(b[3], 3)
     own = project(where, mine, others, held, 0, halves, 400_000_000)
     skies = [own] + [project(where, [a[j]], [along_x(a[j])], held, j, blocks, 400_000_000) for j in (1, 2, 3)]
     gone = reduce(down, [leave for _, leave in skies], (0, 0, 0, 0), n_modes)
     stay_a = [stay for stay, _ in skies]
-    b[2], b[3], stay_a, gone = fence((b[2], b[3], stay_a, gone))
-    x_2 = along_x(b[2])
+    b[3], b[2], stay_a, gone = fence((b[3], b[2], stay_a, gone))
+    x_3 = along_x(b[3])
     x_1, = anchor([along_x(b[1])], 2_500_000_000)
-    b[3] = along_z(b[3], 3)
+    b[2] = shift_z(b[2], 2)
     kept = reduce(down, stay_a, (0, 0, 0, 0), n_modes, jnp.float32)
     spots = [(j, 0, freqs) for j in (1, 2, 3, 0)]
     outs = restore(kept, lax.ppermute(gone, "pol", other), ratios, up, spots)
     near = project(where, [b[1]], [x_1], held, 1, blocks)
-    x_2, b, outs, near = fence((x_2, b, outs, near))
-    first = {j: along_z(outs[j - 1], j) for j in (1, 2, 3)}
+    x_3, b, outs, near = fence((x_3, b, outs, near))
+    first = {j: swap_z(outs[j - 1], j) for j in (1, 2, 3)}
     first[0] = outs[3]
-    x_3 = along_x(b[3])
-    skies = [own, near] + [project(where, [b[j]], [x], held, j, blocks) for j, x in ((2, x_2), (3, x_3))]
+    x_2 = along_x(b[2])
+    last = project(where, [b[3]], [x_3], held, 3, blocks)
+    skies = [own, near, project(where, [b[2]], [x_2], held, 2, blocks), last]
     gone = reduce(down, [leave for _, leave in skies], (ROWS, 0, 0, 0), n_modes)
     stays = [stay for stay, _ in skies]
     first[2], first[1], here, stays, gone = fence((first[2], first[1], first[0], stays, gone))
@@ -282,7 +286,7 @@
     first[3], = anchor([first[3]], 20_000_000_000)
     outs, first[3] = fence((restore(kept, came, ratios, up, spots), first[3]))
     first[0] = here
-    back = [along_z(outs[j - 1], j) for j in (1, 2, 3)]
+    back = [swap_z(outs[j - 1], j) for j in (1, 2, 3)]
     result = place(where, [first[j] for j in (1, 2, 3, 0)], spots, 0, shape)
     result = place(where, [outs[3], back[0]], [spots[3], spots[0]], ROWS, shape, into=result)
     return place(where, back[1:], spots[1:3], ROWS, shape, into=result)

time: 89.2 us -> 87.6 us (0.982)
  starting transfers between devices: 26.5 us -> 25.5 us
    ppermute x8, starting transfers between devices: 11.7 us -> 9.13 us  [along_x(): return lax.ppermute(value, 'kl', other)]
    ppermute x12, starting transfers between devices: 14.7 us -> 16.4 us  [the longest x6 8.2 us: shift_z(): lax.ppermute(value, 'fm', [(i, (i + j) % parts) for i in range(parts)])]
  transfers between devices with their start and end apart: 22 -> 22, of which waited for: 10 -> 10; matrix products, arithmetic and copies ran while one was open for 1% -> 1% of each run, Pallas kernels for 25% -> 26%
where the time goes in v18:
time: 87.6 us; the launch traced here: 87.4 us
  waiting for transfers between devices  33.5 us (38%)
  starting transfers between devices  25.5 us (29%)
  Pallas kernels  25 us (29%)
  local copies, waits for them, and re-layouts  2.39 us (3%)
  between operations  0.91 us (1%)
    ppermute x6, waiting for transfers between devices, swap_z(): return lax.ppermute(value, 'fm', [(i, i ^ j) for i in range(parts)])  25 us
    pallas_call x7, Pallas kernels, project(): pl.pallas_call(functools.partial(project_kernel, piece=piece, blocks=bloc...  9.56 us
    ppermute x8, starting transfers between devices, along_x(): return lax.ppermute(value, 'kl', other)  9.13 us
    ppermute x6, starting transfers between devices, shift_z(): lax.ppermute(value, 'fm', [(i, (i + j) % parts) for i in range(parts)])  8.2 us
    ppermute x6, starting transfers between devices, swap_z(): return lax.ppermute(value, 'fm', [(i, i ^ j) for i in range(parts)])  8.18 us
    pallas_call x1, Pallas kernels, hold(): pl.pallas_call(hold_kernel, grid_spec=pltpu.PrefetchScalarGridSpec(num_sc...  7.04 us
    ppermute x8, waiting for transfers between devices, along_x(): return lax.ppermute(value, 'kl', other)  5.31 us
    pallas_call x3, Pallas kernels, place(): pl.pallas_call(functools.partial(place_kernel, spots=spots, first=first),...  4.06 us
  transfers between devices with their start and end apart: 22, of which 10 were waited for; matrix products, arithmetic and copies ran while one was open for 1% of the time, Pallas kernels for 26%

profile of v18, /device:TPU:12, one launch (start us, length us, event | category | flops | bytes accessed | tf_op | source)
XLA Modules:
  0.0 87.4 jit_solution(6173099654952707407)
XLA Ops:
  1.1 1.6 %collective-permute-start = (bf16[8,16,512]{2,1,0:T(8,128)(2,1)S(1)}, bf16[8,16,512]{2,1,0:T(8,128)(2,1)S(1)}, u32[]{:S(2)}, u32[]{:S(2)}) collective-permute-start(bf16[8,16,512]{2,1,0:T(8,128)(2,1)S(1)} %get-tuple-element.140), channel_id=1, source_target_pairs={{0,4},{4,8},{8,12},{12,0},{1,5},{5,9},{9,13},{13,1},{2,6},{6,10},{... | collective-permute-start | bytes 393224 | tf_op jit(solution)/shard_map/ppermute | solution.py:232
  3.2 2.6 %collective-permute-start.2 = (bf16[8,16,512]{2,1,0:T(8,128)(2,1)S(1)}, bf16[8,16,512]{2,1,0:T(8,128)(2,1)S(1)}, u32[]{:S(2)}, u32[]{:S(2)}) collective-permute-start(bf16[8,16,512]{2,1,0:T(8,128)(2,1)S(1)} %get-tuple-element.138), channel_id=1, source_target_pairs={{0,8},{4,12},{8,0},{12,4},{1,9},{5,13},{9,1},{13,5},{2,10},{6,14},... | collective-permute-start | bytes 393224 | tf_op jit(solution)/shard_map/ppermute | solution.py:232
  6.8 1.6 %collective-permute-start.3 = (bf16[4,48,512]{2,1,0:T(8,128)(2,1)S(1)}, bf16[4,48,512]{2,1,0:T(8,128)(2,1)S(1)}, u32[]{:S(2)}, u32[]{:S(2)}) collective-permute-start(bf16[4,48,512]{2,1,0:T(8,128)(2,1)S(1)} %get-tuple-element.134.refs_0_), channel_id=1, source_target_pairs={{0,2},{2,0},{1,3},{3,1},{4,6},{6,4},{5,7},{7,5},{8,10},{10,8},{9,1... | collective-permute-start | bytes 589832 | tf_op jit(solution)/shard_map/ppermute | solution.py:238
  9.7 7.0 %shard_map.64 = (bf16[32,512,512]{2,1,0:T(8,128)(2,1)S(1)}, bf16[384,512]{1,0:T(8,128)(2,1)S(1)}, bf16[512,384]{1,0:T(8,128)(2,1)S(1)}) custom-call(s32[10]{0:T(128)S(1)} %compare_select_fusion.4.where, s32[4,4]{1,0:T(4,128)S(1)} %bitcast.27, s32[1]{0:T(128)S(6)} %copy.20.starts, bf16[32,512,512]{2,1,0:T(8,128)(2,1)} %bitcast.28, bf16[32,24]{1,0:T(8,128)(2,1)S(1)} %bitcast.26), custom_call_target="tpu_custom_call" | custom-call | flops 1024 | bytes 1024 | tf_op jit(solution)/shard_map/pallas_call | solution.py:63
  19.0 1.5 %collective-permute-start.6 = (bf16[8,16,512]{2,1,0:T(8,128)(2,1)S(1)}, bf16[8,16,512]{2,1,0:T(8,128)(2,1)S(1)}, u32[]{:S(2)}, u32[]{:S(2)}) collective-permute-start(bf16[8,16,512]{2,1,0:T(8,128)(2,1)S(1)} %collective-permute-done.refs_0_), channel_id=1, source_target_pairs={{0,2},{2,0},{1,3},{3,1},{4,6},{6,4},{5,7},{7,5},{8,10},{10,8},{9,1... | collective-permute-start | bytes 393224 | tf_op jit(solution)/shard_map/ppermute | solution.py:238
  21.0 1.5 %collective-permute-start.8 = (bf16[8,16,512]{2,1,0:T(8,128)(2,1)S(1)}, bf16[8,16,512]{2,1,0:T(8,128)(2,1)S(1)}, u32[]{:S(2)}, u32[]{:S(2)}) collective-permute-start(bf16[8,16,512]{2,1,0:T(8,128)(2,1)S(1)} %collective-permute-done.1.refs_0_), channel_id=1, source_target_pairs={{0,2},{2,0},{1,3},{3,1},{4,6},{6,4},{5,7},{7,5},{8,10},{10,8},{9,1... | collective-permute-start | bytes 393224 | tf_op jit(solution)/shard_map/ppermute | solution.py:238
  22.5 1.4 %shard_map.65 = (bf16[8,48,512]{2,1,0:T(8,128)(2,1)S(1)}, bf16[8,48,512]{2,1,0:T(8,128)(2,1)S(1)}) custom-call(s32[10]{0:T(128)S(1)} %compare_select_fusion.4.where, bf16[4,48,512]{2,1,0:T(8,128)(2,1)S(1)} %get-tuple-element.134.refs_0_, bf16[4,48,512]{2,1,0:T(8,128)(2,1)S(1)} %get-tuple-element.133.refs_1_, ...), custom_call_target="tpu_custom_call" | custom-call | flops 400000000 | bytes 1024 | tf_op jit(solution)/shard_map/pallas_call | solution.py:102
  27.9 1.6 %collective-permute-start.13 = (bf16[8,32,512]{2,1,0:T(8,128)(2,1)S(1)}, bf16[8,32,512]{2,1,0:T(8,128)(2,1)S(1)}, u32[]{:S(2)}, u32[]{:S(2)}) collective-permute-start(bf16[8,32,512]{2,1,0:T(8,128)(2,1)S(1)} %collective-permute-done.10.refs_0_), channel_id=1, source_target_pairs={{0,2},{2,0},{1,3},{3,1},{4,6},{6,4},{5,7},{7,5},{8,10},{10,8},{9,1... | collective-permute-start | bytes 786440 | tf_op jit(solution)/shard_map/ppermute | solution.py:238
  31.2 1.4 %collective-permute-start.9 = (bf16[8,32,512]{2,1,0:T(8,128)(2,1)S(1)}, bf16[8,32,512]{2,1,0:T(8,128)(2,1)S(1)}, u32[]{:S(2)}, u32[]{:S(2)}) collective-permute-start(bf16[8,32,512]{2,1,0:T(8,128)(2,1)S(1)} %collective-permute-done.5.refs_0_), channel_id=1, source_target_pairs={{0,2},{2,0},{1,3},{3,1},{4,6},{6,4},{5,7},{7,5},{8,10},{10,8},{9,1... | collective-permute-start | bytes 786440 | tf_op jit(solution)/shard_map/ppermute | solution.py:238
  32.7 1.5 %collective-permute-start.11 = (bf16[8,32,512]{2,1,0:T(8,128)(2,1)S(1)}, bf16[8,32,512]{2,1,0:T(8,128)(2,1)S(1)}, u32[]{:S(2)}, u32[]{:S(2)}) collective-permute-start(bf16[8,32,512]{2,1,0:T(8,128)(2,1)S(1)} %get-tuple-element.91), channel_id=1, source_target_pairs={{0,8},{4,12},{8,0},{12,4},{1,9},{5,13},{9,1},{13,5},{2,10},{6,14},... | collective-permute-start | bytes 786440 | tf_op jit(solution)/shard_map/ppermute | solution.py:232
  34.2 3.0 %collective-permute-done.13.refs_0_ = bf16[8,32,512]{2,1,0:T(8,128)(2,1)S(1)} collective-permute-done((bf16[8,32,512]{2,1,0:T(8,128)(2,1)S(1)}, bf16[8,32,512]{2,1,0:T(8,128)(2,1)S(1)}, u32[]{:S(2)}, u32[]{:S(2)}) %collective-permute-start.13) | collective-permute-done | bytes 262176 | tf_op jit(solution)/shard_map/ppermute | solution.py:238
  37.5 1.4 %shard_map.73 = (bf16[8,32,512]{2,1,0:T(8,128)(2,1)S(1)}, bf16[8,32,512]{2,1,0:T(8,128)(2,1)S(1)}) custom-call(s32[10]{0:T(128)S(1)} %compare_select_fusion.4.where, bf16[8,32,512]{2,1,0:T(8,128)(2,1)S(1)} %collective-permute-done.10.refs_0_, bf16[8,32,512]{2,1,0:T(8,128)(2,1)S(1)} %shard_map.72.refs_1_, ...), custom_call_target="tpu_custom_call" | custom-call | flops 1024 | bytes 1024 | tf_op jit(solution)/shard_map/pallas_call | solution.py:102
  40.0 3.2 %collective-permute-done.11.refs_0_ = bf16[8,32,512]{2,1,0:T(8,128)(2,1)S(1)} collective-permute-done((bf16[8,32,512]{2,1,0:T(8,128)(2,1)S(1)}, bf16[8,32,512]{2,1,0:T(8,128)(2,1)S(1)}, u32[]{:S(2)}, u32[]{:S(2)}) %collective-permute-start.11) | collective-permute-done | bytes 262176 | tf_op jit(solution)/shard_map/ppermute | solution.py:232
  43.7 3.4 %collective-permute-start.14 = (bf16[8,16,512]{2,1,0:T(8,128)(2,1)S(1)}, bf16[8,16,512]{2,1,0:T(8,128)(2,1)S(1)}, u32[]{:S(2)}, u32[]{:S(2)}) collective-permute-start(bf16[8,16,512]{2,1,0:T(8,128)(2,1)S(1)} %get-tuple-element.103), channel_id=1, source_target_pairs={{0,8},{4,12},{8,0},{12,4},{1,9},{5,13},{9,1},{13,5},{2,10},{6,14},... | collective-permute-start | bytes 393224 | tf_op jit(solution)/shard_map/ppermute | solution.py:235
  48.4 1.4 %shard_map.75 = (bf16[8,32,512]{2,1,0:T(8,128)(2,1)S(1)}, bf16[8,32,512]{2,1,0:T(8,128)(2,1)S(1)}) custom-call(s32[10]{0:T(128)S(1)} %compare_select_fusion.4.where, bf16[8,32,512]{2,1,0:T(8,128)(2,1)S(1)} %collective-permute-done.5.refs_0_, bf16[8,32,512]{2,1,0:T(8,128)(2,1)S(1)} %collective-permute-done.9.refs_1_, ...), custom_call_target="tpu_custom_call" | custom-call | flops 1024 | bytes 1024 | tf_op jit(solution)/shard_map/pallas_call | solution.py:102
  50.3 1.4 %shard_map.74 = (bf16[8,32,512]{2,1,0:T(8,128)(2,1)S(1)}, bf16[8,32,512]{2,1,0:T(8,128)(2,1)S(1)}) custom-call(s32[10]{0:T(128)S(1)} %compare_select_fusion.4.where, bf16[8,32,512]{2,1,0:T(8,128)(2,1)S(1)} %collective-permute-done.11.refs_0_, bf16[8,32,512]{2,1,0:T(8,128)(2,1)S(1)} %collective-permute-done.16.refs_1_, ...), custom_call_target="tpu_custom_call" | custom-call | flops 1024 | bytes 1024 | tf_op jit(solution)/shard_map/pallas_call | solution.py:102
  52.6 2.4 %collective-permute-done.14.refs_1_ = bf16[8,16,512]{2,1,0:T(8,128)(2,1)S(1)} collective-permute-done((bf16[8,16,512]{2,1,0:T(8,128)(2,1)S(1)}, bf16[8,16,512]{2,1,0:T(8,128)(2,1)S(1)}, u32[]{:S(2)}, u32[]{:S(2)}) %collective-permute-start.14) | collective-permute-done | bytes 131104 | tf_op jit(solution)/shard_map/ppermute | solution.py:235
  54.9 2.7 %collective-permute-done.18.refs_0_ = bf16[8,16,512]{2,1,0:T(8,128)(2,1)S(1)} collective-permute-done((bf16[8,16,512]{2,1,0:T(8,128)(2,1)S(1)}, bf16[8,16,512]{2,1,0:T(8,128)(2,1)S(1)}, u32[]{:S(2)}, u32[]{:S(2)}) %collective-permute-start.18) | collective-permute-done | bytes 131104 | tf_op jit(solution)/shard_map/ppermute | solution.py:235
  59.9 1.4 %collective-permute-start.21 = (bf16[8,32,512]{2,1,0:T(8,128)(2,1)S(1)}, bf16[8,32,512]{2,1,0:T(8,128)(2,1)S(1)}, u32[]{:S(2)}, u32[]{:S(2)}) collective-permute-start(bf16[8,32,512]{2,1,0:T(8,128)(2,1)S(1)} %get-tuple-element.128), channel_id=1, source_target_pairs={{0,4},{4,0},{8,12},{12,8},{1,5},{5,1},{9,13},{13,9},{2,6},{6,2},{1... | collective-permute-start | bytes 786440 | tf_op jit(solution)/shard_map/ppermute | solution.py:235
  61.3 1.8 %collective-permute-start.19 = (bf16[8,32,512]{2,1,0:T(8,128)(2,1)S(1)}, bf16[8,32,512]{2,1,0:T(8,128)(2,1)S(1)}, u32[]{:S(2)}, u32[]{:S(2)}) collective-permute-start(bf16[8,32,512]{2,1,0:T(8,128)(2,1)S(1)} %get-tuple-element.125), channel_id=1, source_target_pairs={{0,8},{4,12},{8,0},{12,4},{1,9},{5,13},{9,1},{13,5},{2,10},{6,14},... | collective-permute-start | bytes 786440 | tf_op jit(solution)/shard_map/ppermute | solution.py:235
  63.4 1.4 %shard_map.80.refs_2_ = bf16[8,4,48,512]{3,2,1,0:T(8,128)(2,1)} custom-call(s32[10]{0:T(128)S(1)} %compare_select_fusion.4.where, bf16[8,16,512]{2,1,0:T(8,128)(2,1)S(1)} %collective-permute-done.15.refs_0_, bf16[8,16,512]{2,1,0:T(8,128)(2,1)S(1)} %collective-permute-done.14.refs_1_, bf16[8,16,512]{2,1,0:T(8,128)(2,1)S(1)} %shard_map.79.refs_2_, ...), custom_call_target="tpu_custom_call" | custom-call | flops 1024 | bytes 1024 | tf_op jit(solution)/shard_map/pallas_call | solution.py:190
  64.8 7.1 %collective-permute-done.21.refs_1_ = bf16[8,32,512]{2,1,0:T(8,128)(2,1)S(1)} collective-permute-done((bf16[8,32,512]{2,1,0:T(8,128)(2,1)S(1)}, bf16[8,32,512]{2,1,0:T(8,128)(2,1)S(1)}, u32[]{:S(2)}, u32[]{:S(2)}) %collective-permute-start.21) | collective-permute-done | bytes 262176 | tf_op jit(solution)/shard_map/ppermute | solution.py:235
  73.2 7.8 %collective-permute-done.19.refs_0_ = bf16[8,32,512]{2,1,0:T(8,128)(2,1)S(1)} collective-permute-done((bf16[8,32,512]{2,1,0:T(8,128)(2,1)S(1)}, bf16[8,32,512]{2,1,0:T(8,128)(2,1)S(1)}, u32[]{:S(2)}, u32[]{:S(2)}) %collective-permute-start.19) | collective-permute-done | bytes 262176 | tf_op jit(solution)/shard_map/ppermute | solution.py:235
  81.1 5.0 %collective-permute-done.20.refs_1_ = bf16[8,32,512]{2,1,0:T(8,128)(2,1)S(1)} collective-permute-done((bf16[8,32,512]{2,1,0:T(8,128)(2,1)S(1)}, bf16[8,32,512]{2,1,0:T(8,128)(2,1)S(1)}, u32[]{:S(2)}, u32[]{:S(2)}) %collective-permute-start.20) | collective-permute-done | bytes 262176 | tf_op jit(solution)/shard_map/ppermute | solution.py:235
  (54 shorter events, 21.6 us)
Async XLA Ops:
  0.0 9.6 %copy-start.2 = (bf16[1,32,24]{1,2,0:T(8,128)(2,1)S(1)}, bf16[1,32,24]{1,2,0:T(8,128)(2,1)}, u32[]{:S(2)}) copy-start(bf16[1,32,24]{1,2,0:T(8,128)(2,1)} %param.10) | copy-start | bytes 4612
  0.0 9.7 %copy-start = (s32[1,4,4]{2,1,0:T(4,128)S(1)}, s32[1,4,4]{2,1,0:T(4,128)}, u32[]{:S(2)}) copy-start(s32[1,4,4]{2,1,0:T(4,128)} %param.8) | copy-start | bytes 196
  1.1 15.7 %collective-permute-start = (bf16[8,16,512]{2,1,0:T(8,128)(2,1)S(1)}, bf16[8,16,512]{2,1,0:T(8,128)(2,1)S(1)}, u32[]{:S(2)}, u32[]{:S(2)}) collective-permute-start(bf16[8,16,512]{2,1,0:T(8,128)(2,1)S(1)} %get-tuple-element.140), channel_id=1, source_target_pairs={{0,4},{4,8},{8,12},{12,0},{1,5},{5,9},{9,13},{13,1},{2,6},{6,10},{... | collective-permute-start | bytes 393224 | tf_op jit(solution)/shard_map/ppermute | solution.py:232
  2.7 14.1 %collective-permute-start.1 = (bf16[8,16,512]{2,1,0:T(8,128)(2,1)S(1)}, bf16[8,16,512]{2,1,0:T(8,128)(2,1)S(1)}, u32[]{:S(2)}, u32[]{:S(2)}) collective-permute-start(bf16[8,16,512]{2,1,0:T(8,128)(2,1)S(1)} %get-tuple-element.139), channel_id=1, source_target_pairs={{0,12},{4,0},{8,4},{12,8},{1,13},{5,1},{9,5},{13,9},{2,14},{6,2},{... | collective-permute-start | bytes 393224 | tf_op jit(solution)/shard_map/ppermute | solution.py:232
  3.2 13.7 %collective-permute-start.2 = (bf16[8,16,512]{2,1,0:T(8,128)(2,1)S(1)}, bf16[8,16,512]{2,1,0:T(8,128)(2,1)S(1)}, u32[]{:S(2)}, u32[]{:S(2)}) collective-permute-start(bf16[8,16,512]{2,1,0:T(8,128)(2,1)S(1)} %get-tuple-element.138), channel_id=1, source_target_pairs={{0,8},{4,12},{8,0},{12,4},{1,9},{5,13},{9,1},{13,5},{2,10},{6,14},... | collective-permute-start | bytes 393224 | tf_op jit(solution)/shard_map/ppermute | solution.py:232
  6.8 10.0 %collective-permute-start.3 = (bf16[4,48,512]{2,1,0:T(8,128)(2,1)S(1)}, bf16[4,48,512]{2,1,0:T(8,128)(2,1)S(1)}, u32[]{:S(2)}, u32[]{:S(2)}) collective-permute-start(bf16[4,48,512]{2,1,0:T(8,128)(2,1)S(1)} %get-tuple-element.134.refs_0_), channel_id=1, source_target_pairs={{0,2},{2,0},{1,3},{3,1},{4,6},{6,4},{5,7},{7,5},{8,10},{10,8},{9,1... | collective-permute-start | bytes 589832 | tf_op jit(solution)/shard_map/ppermute | solution.py:238
  8.4 8.5 %collective-permute-start.4 = (bf16[4,48,512]{2,1,0:T(8,128)(2,1)S(1)}, bf16[4,48,512]{2,1,0:T(8,128)(2,1)S(1)}, u32[]{:S(2)}, u32[]{:S(2)}) collective-permute-start(bf16[4,48,512]{2,1,0:T(8,128)(2,1)S(1)} %get-tuple-element.133.refs_1_), channel_id=1, source_target_pairs={{0,2},{2,0},{1,3},{3,1},{4,6},{6,4},{5,7},{7,5},{8,10},{10,8},{9,1... | collective-permute-start | bytes 589832 | tf_op jit(solution)/shard_map/ppermute | solution.py:238
  16.9 11.0 %collective-permute-start.10 = (bf16[8,32,512]{2,1,0:T(8,128)(2,1)S(1)}, bf16[8,32,512]{2,1,0:T(8,128)(2,1)S(1)}, u32[]{:S(2)}, u32[]{:S(2)}) collective-permute-start(bf16[8,32,512]{2,1,0:T(8,128)(2,1)S(1)} %get-tuple-element.90), channel_id=1, source_target_pairs={{0,4},{4,8},{8,12},{12,0},{1,5},{5,9},{9,13},{13,1},{2,6},{6,10},{... | collective-permute-start | bytes 786440 | tf_op jit(solution)/shard_map/ppermute | solution.py:232
  18.1 13.1 %collective-permute-start.5 = (bf16[8,32,512]{2,1,0:T(8,128)(2,1)S(1)}, bf16[8,32,512]{2,1,0:T(8,128)(2,1)S(1)}, u32[]{:S(2)}, u32[]{:S(2)}) collective-permute-start(bf16[8,32,512]{2,1,0:T(8,128)(2,1)S(1)} %get-tuple-element.73), channel_id=1, source_target_pairs={{0,12},{4,0},{8,4},{12,8},{1,13},{5,1},{9,5},{13,9},{2,14},{6,2},{... | collective-permute-start | bytes 786440 | tf_op jit(solution)/shard_map/ppermute | solution.py:232
  19.0 6.2 %collective-permute-start.6 = (bf16[8,16,512]{2,1,0:T(8,128)(2,1)S(1)}, bf16[8,16,512]{2,1,0:T(8,128)(2,1)S(1)}, u32[]{:S(2)}, u32[]{:S(2)}) collective-permute-start(bf16[8,16,512]{2,1,0:T(8,128)(2,1)S(1)} %collective-permute-done.refs_0_), channel_id=1, source_target_pairs={{0,2},{2,0},{1,3},{3,1},{4,6},{6,4},{5,7},{7,5},{8,10},{10,8},{9,1... | collective-permute-start | bytes 393224 | tf_op jit(solution)/shard_map/ppermute | solution.py:238
  20.5 6.1 %collective-permute-start.7 = (bf16[8,16,512]{2,1,0:T(8,128)(2,1)S(1)}, bf16[8,16,512]{2,1,0:T(8,128)(2,1)S(1)}, u32[]{:S(2)}, u32[]{:S(2)}) collective-permute-start(bf16[8,16,512]{2,1,0:T(8,128)(2,1)S(1)} %collective-permute-done.2.refs_0_), channel_id=1, source_target_pairs={{0,2},{2,0},{1,3},{3,1},{4,6},{6,4},{5,7},{7,5},{8,10},{10,8},{9,1... | collective-permute-start | bytes 393224 | tf_op jit(solution)/shard_map/ppermute | solution.py:238
  21.0 8.5 %collective-permute-start.8 = (bf16[8,16,512]{2,1,0:T(8,128)(2,1)S(1)}, bf16[8,16,512]{2,1,0:T(8,128)(2,1)S(1)}, u32[]{:S(2)}, u32[]{:S(2)}) collective-permute-start(bf16[8,16,512]{2,1,0:T(8,128)(2,1)S(1)} %collective-permute-done.1.refs_0_), channel_id=1, source_target_pairs={{0,2},{2,0},{1,3},{3,1},{4,6},{6,4},{5,7},{7,5},{8,10},{10,8},{9,1... | collective-permute-start | bytes 393224 | tf_op jit(solution)/shard_map/ppermute | solution.py:238
  27.9 9.2 %collective-permute-start.13 = (bf16[8,32,512]{2,1,0:T(8,128)(2,1)S(1)}, bf16[8,32,512]{2,1,0:T(8,128)(2,1)S(1)}, u32[]{:S(2)}, u32[]{:S(2)}) collective-permute-start(bf16[8,32,512]{2,1,0:T(8,128)(2,1)S(1)} %collective-permute-done.10.refs_0_), channel_id=1, source_target_pairs={{0,2},{2,0},{1,3},{3,1},{4,6},{6,4},{5,7},{7,5},{8,10},{10,8},{9,1... | collective-permute-start | bytes 786440 | tf_op jit(solution)/shard_map/ppermute | solution.py:238
  31.2 8.7 %collective-permute-start.9 = (bf16[8,32,512]{2,1,0:T(8,128)(2,1)S(1)}, bf16[8,32,512]{2,1,0:T(8,128)(2,1)S(1)}, u32[]{:S(2)}, u32[]{:S(2)}) collective-permute-start(bf16[8,32,512]{2,1,0:T(8,128)(2,1)S(1)} %collective-permute-done.5.refs_0_), channel_id=1, source_target_pairs={{0,2},{2,0},{1,3},{3,1},{4,6},{6,4},{5,7},{7,5},{8,10},{10,8},{9,1... | collective-permute-start | bytes 786440 | tf_op jit(solution)/shard_map/ppermute | solution.py:238
  32.7 10.5 %collective-permute-start.11 = (bf16[8,32,512]{2,1,0:T(8,128)(2,1)S(1)}, bf16[8,32,512]{2,1,0:T(8,128)(2,1)S(1)}, u32[]{:S(2)}, u32[]{:S(2)}) collective-permute-start(bf16[8,32,512]{2,1,0:T(8,128)(2,1)S(1)} %get-tuple-element.91), channel_id=1, source_target_pairs={{0,8},{4,12},{8,0},{12,4},{1,9},{5,13},{9,1},{13,5},{2,10},{6,14},... | collective-permute-start | bytes 786440 | tf_op jit(solution)/shard_map/ppermute | solution.py:232
  34.1 4.8 %collective-permute-start.12 = (bf16[24,16,512]{2,1,0:T(8,128)(2,1)S(1)}, bf16[24,16,512]{2,1,0:T(8,128)(2,1)S(1)}, u32[]{:S(2)}, u32[]{:S(2)}) collective-permute-start(bf16[24,16,512]{2,1,0:T(8,128)(2,1)S(1)} %shard_map.69), channel_id=1, source_target_pairs={{0,1},{1,0},{2,3},{3,2},{4,5},{5,4},{6,7},{7,6},{8,9},{9,8},{10,11... | collective-permute-start | bytes 1179656 | tf_op jit(solution)/shard_map/ppermute | solution.py:273
  43.2 7.1 %collective-permute-start.16 = (bf16[8,32,512]{2,1,0:T(8,128)(2,1)S(1)}, bf16[8,32,512]{2,1,0:T(8,128)(2,1)S(1)}, u32[]{:S(2)}, u32[]{:S(2)}) collective-permute-start(bf16[8,32,512]{2,1,0:T(8,128)(2,1)S(1)} %collective-permute-done.11.refs_0_), channel_id=1, source_target_pairs={{0,2},{2,0},{1,3},{3,1},{4,6},{6,4},{5,7},{7,5},{8,10},{10,8},{9,1... | collective-permute-start | bytes 786440 | tf_op jit(solution)/shard_map/ppermute | solution.py:238
  43.7 11.2 %collective-permute-start.14 = (bf16[8,16,512]{2,1,0:T(8,128)(2,1)S(1)}, bf16[8,16,512]{2,1,0:T(8,128)(2,1)S(1)}, u32[]{:S(2)}, u32[]{:S(2)}) collective-permute-start(bf16[8,16,512]{2,1,0:T(8,128)(2,1)S(1)} %get-tuple-element.103), channel_id=1, source_target_pairs={{0,8},{4,12},{8,0},{12,4},{1,9},{5,13},{9,1},{13,5},{2,10},{6,14},... | collective-permute-start | bytes 393224 | tf_op jit(solution)/shard_map/ppermute | solution.py:235
  47.1 7.8 %collective-permute-start.15 = (bf16[8,16,512]{2,1,0:T(8,128)(2,1)S(1)}, bf16[8,16,512]{2,1,0:T(8,128)(2,1)S(1)}, u32[]{:S(2)}, u32[]{:S(2)}) collective-permute-start(bf16[8,16,512]{2,1,0:T(8,128)(2,1)S(1)} %get-tuple-element.104), channel_id=1, source_target_pairs={{0,4},{4,0},{8,12},{12,8},{1,5},{5,1},{9,13},{13,9},{2,6},{6,2},{1... | collective-permute-start | bytes 393224 | tf_op jit(solution)/shard_map/ppermute | solution.py:235
  47.1 10.5 %collective-permute-start.18 = (bf16[8,16,512]{2,1,0:T(8,128)(2,1)S(1)}, bf16[8,16,512]{2,1,0:T(8,128)(2,1)S(1)}, u32[]{:S(2)}, u32[]{:S(2)}) collective-permute-start(bf16[8,16,512]{2,1,0:T(8,128)(2,1)S(1)} %get-tuple-element.124), channel_id=1, source_target_pairs={{0,12},{4,8},{8,4},{12,0},{1,13},{5,9},{9,5},{13,1},{2,14},{6,10},... | collective-permute-start | bytes 393224 | tf_op jit(solution)/shard_map/ppermute | solution.py:235
  54.9 3.7 %collective-permute-start.17 = (bf16[24,32,512]{2,1,0:T(8,128)(2,1)S(1)}, bf16[24,32,512]{2,1,0:T(8,128)(2,1)S(1)}, u32[]{:S(2)}, u32[]{:S(2)}) collective-permute-start(bf16[24,32,512]{2,1,0:T(8,128)(2,1)S(1)} %shard_map.76), channel_id=1, source_target_pairs={{0,1},{1,0},{2,3},{3,2},{4,5},{5,4},{6,7},{7,6},{8,9},{9,8},{10,11... | collective-permute-start | bytes 2359304 | tf_op jit(solution)/shard_map/ppermute | solution.py:284
  59.9 12.0 %collective-permute-start.21 = (bf16[8,32,512]{2,1,0:T(8,128)(2,1)S(1)}, bf16[8,32,512]{2,1,0:T(8,128)(2,1)S(1)}, u32[]{:S(2)}, u32[]{:S(2)}) collective-permute-start(bf16[8,32,512]{2,1,0:T(8,128)(2,1)S(1)} %get-tuple-element.128), channel_id=1, source_target_pairs={{0,4},{4,0},{8,12},{12,8},{1,5},{5,1},{9,13},{13,9},{2,6},{6,2},{1... | collective-permute-start | bytes 786440 | tf_op jit(solution)/shard_map/ppermute | solution.py:235
  61.3 19.8 %collective-permute-start.19 = (bf16[8,32,512]{2,1,0:T(8,128)(2,1)S(1)}, bf16[8,32,512]{2,1,0:T(8,128)(2,1)S(1)}, u32[]{:S(2)}, u32[]{:S(2)}) collective-permute-start(bf16[8,32,512]{2,1,0:T(8,128)(2,1)S(1)} %get-tuple-element.125), channel_id=1, source_target_pairs={{0,8},{4,12},{8,0},{12,4},{1,9},{5,13},{9,1},{13,5},{2,10},{6,14},... | collective-permute-start | bytes 786440 | tf_op jit(solution)/shard_map/ppermute | solution.py:235
  63.1 23.0 %collective-permute-start.20 = (bf16[8,32,512]{2,1,0:T(8,128)(2,1)S(1)}, bf16[8,32,512]{2,1,0:T(8,128)(2,1)S(1)}, u32[]{:S(2)}, u32[]{:S(2)}) collective-permute-start(bf16[8,32,512]{2,1,0:T(8,128)(2,1)S(1)} %get-tuple-element.126), channel_id=1, source_target_pairs={{0,12},{4,8},{8,4},{12,0},{1,13},{5,9},{9,5},{13,1},{2,14},{6,10},... | collective-permute-start | bytes 786440 | tf_op jit(solution)/shard_map/ppermute | solution.py:235
  (2 other events, 10.4 us)

commit v19 on v18

--- a/solution.py
+++ b/solution.py
@@ -280,11 +280,12 @@
     skies = [own, near, project(where, [b[2]], [x_2], held, 2, blocks), last]
     gone = reduce(down, [leave for _, leave in skies], (ROWS, 0, 0, 0), n_modes)
     stays = [stay for stay, _ in skies]
-    first[2], first[1], here, stays, gone = fence((first[2], first[1], first[0], stays, gone))
+    here, stays, gone = fence((first[0], stays, gone))
     came = lax.ppermute(gone, "pol", other)
     kept = reduce(down, stays, (ROWS, 0, 0, 0), n_modes, jnp.float32)
-    first[3], = anchor([first[3]], 20_000_000_000)
-    outs, first[3] = fence((restore(kept, came, ratios, up, spots), first[3]))
+    first[3], first[2], first[1], kept = fence((first[3], first[2], first[1], kept))
+    first[3], first[2], first[1] = anchor([first[3], first[2], first[1]], 7_500_000_000)
+    outs, first[3], first[2], first[1] = fence((restore(kept, came, ratios, up, spots), first[3], first[2], first[1]))
     first[0] = here
     back = [swap_z(outs[j - 1], j) for j in (1, 2, 3)]
     result = place(where, [first[j] for j in (1, 2, 3, 0)], spots, 0, shape)

time: 87.6 us -> 86.3 us (0.985)
  waiting for transfers between devices: 33.5 us -> 30.4 us
  starting transfers between devices: 25.5 us -> 27.3 us
    ppermute x6, waiting for transfers between devices: 25 us -> 22.3 us  [swap_z(): return lax.ppermute(value, 'fm', [(i, i ^ j) for i in range(parts)])]
    ppermute x6, starting transfers between devices: 8.18 us -> 9.85 us  [swap_z(): return lax.ppermute(value, 'fm', [(i, i ^ j) for i in range(parts)])]
  transfers between devices with their start and end apart: 22 -> 22, of which waited for: 10 -> 8; matrix products, arithmetic and copies ran while one was open for 1% -> 2% of each run, Pallas kernels for 26% -> 26%
where the time goes in v19:
time: 86.3 us; the launch traced here: 86 us
  waiting for transfers between devices  30.4 us (35%)
  starting transfers between devices  27.3 us (32%)
  Pallas kernels  25 us (29%)
  local copies, waits for them, and re-layouts  2.39 us (3%)
  between operations  0.92 us (1%)
    ppermute x6, waiting for transfers between devices, swap_z(): return lax.ppermute(value, 'fm', [(i, i ^ j) for i in range(parts)])  22.3 us
    ppermute x6, starting transfers between devices, swap_z(): return lax.ppermute(value, 'fm', [(i, i ^ j) for i in range(parts)])  9.85 us
    pallas_call x7, Pallas kernels, project(): pl.pallas_call(functools.partial(project_kernel, piece=piece, blocks=bloc...  9.57 us
    ppermute x8, starting transfers between devices, along_x(): return lax.ppermute(value, 'kl', other)  9.13 us
    ppermute x6, starting transfers between devices, shift_z(): lax.ppermute(value, 'fm', [(i, (i + j) % parts) for i in range(parts)])  8.2 us
    pallas_call x1, Pallas kernels, hold(): pl.pallas_call(hold_kernel, grid_spec=pltpu.PrefetchScalarGridSpec(num_sc...  7.04 us
    ppermute x8, waiting for transfers between devices, along_x(): return lax.ppermute(value, 'kl', other)  4.81 us
    pallas_call x3, Pallas kernels, place(): pl.pallas_call(functools.partial(place_kernel, spots=spots, first=first),...  4.06 us
  transfers between devices with their start and end apart: 22, of which 8 were waited for; matrix products, arithmetic and copies ran while one was open for 2% of the time, Pallas kernels for 26%

profile of v19, /device:TPU:12, one launch (start us, length us, event | category | flops | bytes accessed | tf_op | source)
XLA Modules:
  0.0 86.0 jit_solution(5099508090018721664)
XLA Ops:
  1.1 1.6 %collective-permute-start = (bf16[8,16,512]{2,1,0:T(8,128)(2,1)S(1)}, bf16[8,16,512]{2,1,0:T(8,128)(2,1)S(1)}, u32[]{:S(2)}, u32[]{:S(2)}) collective-permute-start(bf16[8,16,512]{2,1,0:T(8,128)(2,1)S(1)} %get-tuple-element.154), channel_id=1, source_target_pairs={{0,4},{4,8},{8,12},{12,0},{1,5},{5,9},{9,13},{13,1},{2,6},{6,10},{... | collective-permute-start | bytes 393224 | tf_op jit(solution)/shard_map/ppermute | solution.py:232
  3.2 2.6 %collective-permute-start.2 = (bf16[8,16,512]{2,1,0:T(8,128)(2,1)S(1)}, bf16[8,16,512]{2,1,0:T(8,128)(2,1)S(1)}, u32[]{:S(2)}, u32[]{:S(2)}) collective-permute-start(bf16[8,16,512]{2,1,0:T(8,128)(2,1)S(1)} %get-tuple-element.152), channel_id=1, source_target_pairs={{0,8},{4,12},{8,0},{12,4},{1,9},{5,13},{9,1},{13,5},{2,10},{6,14},... | collective-permute-start | bytes 393224 | tf_op jit(solution)/shard_map/ppermute | solution.py:232
  6.8 1.6 %collective-permute-start.3 = (bf16[4,48,512]{2,1,0:T(8,128)(2,1)S(1)}, bf16[4,48,512]{2,1,0:T(8,128)(2,1)S(1)}, u32[]{:S(2)}, u32[]{:S(2)}) collective-permute-start(bf16[4,48,512]{2,1,0:T(8,128)(2,1)S(1)} %get-tuple-element.148.refs_0_), channel_id=1, source_target_pairs={{0,2},{2,0},{1,3},{3,1},{4,6},{6,4},{5,7},{7,5},{8,10},{10,8},{9,1... | collective-permute-start | bytes 589832 | tf_op jit(solution)/shard_map/ppermute | solution.py:238
  9.7 7.0 %shard_map.64 = (bf16[32,512,512]{2,1,0:T(8,128)(2,1)S(1)}, bf16[384,512]{1,0:T(8,128)(2,1)S(1)}, bf16[512,384]{1,0:T(8,128)(2,1)S(1)}) custom-call(s32[10]{0:T(128)S(1)} %compare_select_fusion.4.where, s32[4,4]{1,0:T(4,128)S(1)} %bitcast.27, s32[1]{0:T(128)S(6)} %copy.24.starts, bf16[32,512,512]{2,1,0:T(8,128)(2,1)} %bitcast.28, bf16[32,24]{1,0:T(8,128)(2,1)S(1)} %bitcast.26), custom_call_target="tpu_custom_call" | custom-call | flops 1024 | bytes 1024 | tf_op jit(solution)/shard_map/pallas_call | solution.py:63
  19.0 1.5 %collective-permute-start.6 = (bf16[8,16,512]{2,1,0:T(8,128)(2,1)S(1)}, bf16[8,16,512]{2,1,0:T(8,128)(2,1)S(1)}, u32[]{:S(2)}, u32[]{:S(2)}) collective-permute-start(bf16[8,16,512]{2,1,0:T(8,128)(2,1)S(1)} %collective-permute-done.refs_0_), channel_id=1, source_target_pairs={{0,2},{2,0},{1,3},{3,1},{4,6},{6,4},{5,7},{7,5},{8,10},{10,8},{9,1... | collective-permute-start | bytes 393224 | tf_op jit(solution)/shard_map/ppermute | solution.py:238
  21.0 1.5 %collective-permute-start.8 = (bf16[8,16,512]{2,1,0:T(8,128)(2,1)S(1)}, bf16[8,16,512]{2,1,0:T(8,128)(2,1)S(1)}, u32[]{:S(2)}, u32[]{:S(2)}) collective-permute-start(bf16[8,16,512]{2,1,0:T(8,128)(2,1)S(1)} %collective-permute-done.1.refs_0_), channel_id=1, source_target_pairs={{0,2},{2,0},{1,3},{3,1},{4,6},{6,4},{5,7},{7,5},{8,10},{10,8},{9,1... | collective-permute-start | bytes 393224 | tf_op jit(solution)/shard_map/ppermute | solution.py:238
  22.5 1.4 %shard_map.65 = (bf16[8,48,512]{2,1,0:T(8,128)(2,1)S(1)}, bf16[8,48,512]{2,1,0:T(8,128)(2,1)S(1)}) custom-call(s32[10]{0:T(128)S(1)} %compare_select_fusion.4.where, bf16[4,48,512]{2,1,0:T(8,128)(2,1)S(1)} %get-tuple-element.148.refs_0_, bf16[4,48,512]{2,1,0:T(8,128)(2,1)S(1)} %get-tuple-element.147.refs_1_, ...), custom_call_target="tpu_custom_call" | custom-call | flops 400000000 | bytes 1024 | tf_op jit(solution)/shard_map/pallas_call | solution.py:102
  25.1 1.4 %shard_map.66 = (bf16[8,16,512]{2,1,0:T(8,128)(2,1)S(1)}, bf16[8,16,512]{2,1,0:T(8,128)(2,1)S(1)}) custom-call(s32[10]{0:T(128)S(1)} %compare_select_fusion.4.where, bf16[8,16,512]{2,1,0:T(8,128)(2,1)S(1)} %collective-permute-done.refs_0_, bf16[8,16,512]{2,1,0:T(8,128)(2,1)S(1)} %collective-permute-done.6.refs_1_, ...), custom_call_target="tpu_custom_call" | custom-call | flops 400000000 | bytes 1024 | tf_op jit(solution)/shard_map/pallas_call | solution.py:102
  26.5 1.4 %shard_map.67 = (bf16[8,16,512]{2,1,0:T(8,128)(2,1)S(1)}, bf16[8,16,512]{2,1,0:T(8,128)(2,1)S(1)}) custom-call(s32[10]{0:T(128)S(1)} %compare_select_fusion.4.where, bf16[8,16,512]{2,1,0:T(8,128)(2,1)S(1)} %collective-permute-done.2.refs_0_, bf16[8,16,512]{2,1,0:T(8,128)(2,1)S(1)} %collective-permute-done.7.refs_1_, ...), custom_call_target="tpu_custom_call" | custom-call | flops 400000000 | bytes 1024 | tf_op jit(solution)/shard_map/pallas_call | solution.py:102
  27.9 1.6 %collective-permute-start.13 = (bf16[8,32,512]{2,1,0:T(8,128)(2,1)S(1)}, bf16[8,32,512]{2,1,0:T(8,128)(2,1)S(1)}, u32[]{:S(2)}, u32[]{:S(2)}) collective-permute-start(bf16[8,32,512]{2,1,0:T(8,128)(2,1)S(1)} %collective-permute-done.10.refs_0_), channel_id=1, source_target_pairs={{0,2},{2,0},{1,3},{3,1},{4,6},{6,4},{5,7},{7,5},{8,10},{10,8},{9,1... | collective-permute-start | bytes 786440 | tf_op jit(solution)/shard_map/ppermute | solution.py:238
  31.2 1.4 %collective-permute-start.9 = (bf16[8,32,512]{2,1,0:T(8,128)(2,1)S(1)}, bf16[8,32,512]{2,1,0:T(8,128)(2,1)S(1)}, u32[]{:S(2)}, u32[]{:S(2)}) collective-permute-start(bf16[8,32,512]{2,1,0:T(8,128)(2,1)S(1)} %collective-permute-done.5.refs_0_), channel_id=1, source_target_pairs={{0,2},{2,0},{1,3},{3,1},{4,6},{6,4},{5,7},{7,5},{8,10},{10,8},{9,1... | collective-permute-start | bytes 786440 | tf_op jit(solution)/shard_map/ppermute | solution.py:238
  32.7 1.5 %collective-permute-start.11 = (bf16[8,32,512]{2,1,0:T(8,128)(2,1)S(1)}, bf16[8,32,512]{2,1,0:T(8,128)(2,1)S(1)}, u32[]{:S(2)}, u32[]{:S(2)}) collective-permute-start(bf16[8,32,512]{2,1,0:T(8,128)(2,1)S(1)} %get-tuple-element.98), channel_id=1, source_target_pairs={{0,8},{4,12},{8,0},{12,4},{1,9},{5,13},{9,1},{13,5},{2,10},{6,14},... | collective-permute-start | bytes 786440 | tf_op jit(solution)/shard_map/ppermute | solution.py:232
  34.2 3.0 %collective-permute-done.13.refs_0_ = bf16[8,32,512]{2,1,0:T(8,128)(2,1)S(1)} collective-permute-done((bf16[8,32,512]{2,1,0:T(8,128)(2,1)S(1)}, bf16[8,32,512]{2,1,0:T(8,128)(2,1)S(1)}, u32[]{:S(2)}, u32[]{:S(2)}) %collective-permute-start.13) | collective-permute-done | bytes 262176 | tf_op jit(solution)/shard_map/ppermute | solution.py:238
  37.5 1.4 %shard_map.73 = (bf16[8,32,512]{2,1,0:T(8,128)(2,1)S(1)}, bf16[8,32,512]{2,1,0:T(8,128)(2,1)S(1)}) custom-call(s32[10]{0:T(128)S(1)} %compare_select_fusion.4.where, bf16[8,32,512]{2,1,0:T(8,128)(2,1)S(1)} %collective-permute-done.10.refs_0_, bf16[8,32,512]{2,1,0:T(8,128)(2,1)S(1)} %shard_map.72.refs_1_, ...), custom_call_target="tpu_custom_call" | custom-call | flops 1024 | bytes 1024 | tf_op jit(solution)/shard_map/pallas_call | solution.py:102
  40.0 3.2 %collective-permute-done.11.refs_0_ = bf16[8,32,512]{2,1,0:T(8,128)(2,1)S(1)} collective-permute-done((bf16[8,32,512]{2,1,0:T(8,128)(2,1)S(1)}, bf16[8,32,512]{2,1,0:T(8,128)(2,1)S(1)}, u32[]{:S(2)}, u32[]{:S(2)}) %collective-permute-start.11) | collective-permute-done | bytes 262176 | tf_op jit(solution)/shard_map/ppermute | solution.py:232
  45.0 4.3 %collective-permute-start.15 = (bf16[8,16,512]{2,1,0:T(8,128)(2,1)S(1)}, bf16[8,16,512]{2,1,0:T(8,128)(2,1)S(1)}, u32[]{:S(2)}, u32[]{:S(2)}) collective-permute-start(bf16[8,16,512]{2,1,0:T(8,128)(2,1)S(1)} %get-tuple-element.111), channel_id=1, source_target_pairs={{0,8},{4,12},{8,0},{12,4},{1,9},{5,13},{9,1},{13,5},{2,10},{6,14},... | collective-permute-start | bytes 393224 | tf_op jit(solution)/shard_map/ppermute | solution.py:235
  49.3 1.4 %shard_map.75 = (bf16[8,32,512]{2,1,0:T(8,128)(2,1)S(1)}, bf16[8,32,512]{2,1,0:T(8,128)(2,1)S(1)}) custom-call(s32[10]{0:T(128)S(1)} %compare_select_fusion.4.where, bf16[8,32,512]{2,1,0:T(8,128)(2,1)S(1)} %collective-permute-done.5.refs_0_, bf16[8,32,512]{2,1,0:T(8,128)(2,1)S(1)} %collective-permute-done.9.refs_1_, ...), custom_call_target="tpu_custom_call" | custom-call | flops 1024 | bytes 1024 | tf_op jit(solution)/shard_map/pallas_call | solution.py:102
  50.7 1.4 %shard_map.74 = (bf16[8,32,512]{2,1,0:T(8,128)(2,1)S(1)}, bf16[8,32,512]{2,1,0:T(8,128)(2,1)S(1)}) custom-call(s32[10]{0:T(128)S(1)} %compare_select_fusion.4.where, bf16[8,32,512]{2,1,0:T(8,128)(2,1)S(1)} %collective-permute-done.11.refs_0_, bf16[8,32,512]{2,1,0:T(8,128)(2,1)S(1)} %collective-permute-done.17.refs_1_, ...), custom_call_target="tpu_custom_call" | custom-call | flops 1024 | bytes 1024 | tf_op jit(solution)/shard_map/pallas_call | solution.py:102
  54.0 1.9 %collective-permute-done.15.refs_1_ = bf16[8,16,512]{2,1,0:T(8,128)(2,1)S(1)} collective-permute-done((bf16[8,16,512]{2,1,0:T(8,128)(2,1)S(1)}, bf16[8,16,512]{2,1,0:T(8,128)(2,1)S(1)}, u32[]{:S(2)}, u32[]{:S(2)}) %collective-permute-start.15) | collective-permute-done | bytes 131104 | tf_op jit(solution)/shard_map/ppermute | solution.py:235
  57.2 2.8 %collective-permute-start.21 = (bf16[8,32,512]{2,1,0:T(8,128)(2,1)S(1)}, bf16[8,32,512]{2,1,0:T(8,128)(2,1)S(1)}, u32[]{:S(2)}, u32[]{:S(2)}) collective-permute-start(bf16[8,32,512]{2,1,0:T(8,128)(2,1)S(1)} %get-tuple-element.142), channel_id=1, source_target_pairs={{0,4},{4,0},{8,12},{12,8},{1,5},{5,1},{9,13},{13,9},{2,6},{6,2},{1... | collective-permute-start | bytes 786440 | tf_op jit(solution)/shard_map/ppermute | solution.py:235
  61.5 1.4 %shard_map.80.refs_2_ = bf16[8,4,48,512]{3,2,1,0:T(8,128)(2,1)} custom-call(s32[10]{0:T(128)S(1)} %compare_select_fusion.4.where, bf16[8,16,512]{2,1,0:T(8,128)(2,1)S(1)} %get-tuple-element.143.refs_0_, bf16[8,16,512]{2,1,0:T(8,128)(2,1)S(1)} %get-tuple-element.144.refs_1_, bf16[8,16,512]{2,1,0:T(8,128)(2,1)S(1)} %get-tuple-element.145.refs_2_, ...), custom_call_target="tpu_custom_call" | custom-call | flops 1024 | bytes 1024 | tf_op jit(solution)/shard_map/pallas_call | solution.py:190
  62.9 7.5 %collective-permute-done.21.refs_1_ = bf16[8,32,512]{2,1,0:T(8,128)(2,1)S(1)} collective-permute-done((bf16[8,32,512]{2,1,0:T(8,128)(2,1)S(1)}, bf16[8,32,512]{2,1,0:T(8,128)(2,1)S(1)}, u32[]{:S(2)}, u32[]{:S(2)}) %collective-permute-start.21) | collective-permute-done | bytes 262176 | tf_op jit(solution)/shard_map/ppermute | solution.py:235
  71.7 7.0 %collective-permute-done.19.refs_0_ = bf16[8,32,512]{2,1,0:T(8,128)(2,1)S(1)} collective-permute-done((bf16[8,32,512]{2,1,0:T(8,128)(2,1)S(1)}, bf16[8,32,512]{2,1,0:T(8,128)(2,1)S(1)}, u32[]{:S(2)}, u32[]{:S(2)}) %collective-permute-start.19) | collective-permute-done | bytes 262176 | tf_op jit(solution)/shard_map/ppermute | solution.py:235
  78.7 5.9 %collective-permute-done.20.refs_1_ = bf16[8,32,512]{2,1,0:T(8,128)(2,1)S(1)} collective-permute-done((bf16[8,32,512]{2,1,0:T(8,128)(2,1)S(1)}, bf16[8,32,512]{2,1,0:T(8,128)(2,1)S(1)}, u32[]{:S(2)}, u32[]{:S(2)}) %collective-permute-start.20) | collective-permute-done | bytes 262176 | tf_op jit(solution)/shard_map/ppermute | solution.py:235
  (54 shorter events, 19.8 us)
Async XLA Ops:
  0.0 9.6 %copy-start.2 = (bf16[1,32,24]{1,2,0:T(8,128)(2,1)S(1)}, bf16[1,32,24]{1,2,0:T(8,128)(2,1)}, u32[]{:S(2)}) copy-start(bf16[1,32,24]{1,2,0:T(8,128)(2,1)} %param.10) | copy-start | bytes 4612
  0.0 9.7 %copy-start = (s32[1,4,4]{2,1,0:T(4,128)S(1)}, s32[1,4,4]{2,1,0:T(4,128)}, u32[]{:S(2)}) copy-start(s32[1,4,4]{2,1,0:T(4,128)} %param.8) | copy-start | bytes 196
  1.1 15.7 %collective-permute-start = (bf16[8,16,512]{2,1,0:T(8,128)(2,1)S(1)}, bf16[8,16,512]{2,1,0:T(8,128)(2,1)S(1)}, u32[]{:S(2)}, u32[]{:S(2)}) collective-permute-start(bf16[8,16,512]{2,1,0:T(8,128)(2,1)S(1)} %get-tuple-element.154), channel_id=1, source_target_pairs={{0,4},{4,8},{8,12},{12,0},{1,5},{5,9},{9,13},{13,1},{2,6},{6,10},{... | collective-permute-start | bytes 393224 | tf_op jit(solution)/shard_map/ppermute | solution.py:232
  2.7 14.1 %collective-permute-start.1 = (bf16[8,16,512]{2,1,0:T(8,128)(2,1)S(1)}, bf16[8,16,512]{2,1,0:T(8,128)(2,1)S(1)}, u32[]{:S(2)}, u32[]{:S(2)}) collective-permute-start(bf16[8,16,512]{2,1,0:T(8,128)(2,1)S(1)} %get-tuple-element.153), channel_id=1, source_target_pairs={{0,12},{4,0},{8,4},{12,8},{1,13},{5,1},{9,5},{13,9},{2,14},{6,2},{... | collective-permute-start | bytes 393224 | tf_op jit(solution)/shard_map/ppermute | solution.py:232
  3.2 13.7 %collective-permute-start.2 = (bf16[8,16,512]{2,1,0:T(8,128)(2,1)S(1)}, bf16[8,16,512]{2,1,0:T(8,128)(2,1)S(1)}, u32[]{:S(2)}, u32[]{:S(2)}) collective-permute-start(bf16[8,16,512]{2,1,0:T(8,128)(2,1)S(1)} %get-tuple-element.152), channel_id=1, source_target_pairs={{0,8},{4,12},{8,0},{12,4},{1,9},{5,13},{9,1},{13,5},{2,10},{6,14},... | collective-permute-start | bytes 393224 | tf_op jit(solution)/shard_map/ppermute | solution.py:232
  6.8 10.0 %collective-permute-start.3 = (bf16[4,48,512]{2,1,0:T(8,128)(2,1)S(1)}, bf16[4,48,512]{2,1,0:T(8,128)(2,1)S(1)}, u32[]{:S(2)}, u32[]{:S(2)}) collective-permute-start(bf16[4,48,512]{2,1,0:T(8,128)(2,1)S(1)} %get-tuple-element.148.refs_0_), channel_id=1, source_target_pairs={{0,2},{2,0},{1,3},{3,1},{4,6},{6,4},{5,7},{7,5},{8,10},{10,8},{9,1... | collective-permute-start | bytes 589832 | tf_op jit(solution)/shard_map/ppermute | solution.py:238
  8.4 8.5 %collective-permute-start.4 = (bf16[4,48,512]{2,1,0:T(8,128)(2,1)S(1)}, bf16[4,48,512]{2,1,0:T(8,128)(2,1)S(1)}, u32[]{:S(2)}, u32[]{:S(2)}) collective-permute-start(bf16[4,48,512]{2,1,0:T(8,128)(2,1)S(1)} %get-tuple-element.147.refs_1_), channel_id=1, source_target_pairs={{0,2},{2,0},{1,3},{3,1},{4,6},{6,4},{5,7},{7,5},{8,10},{10,8},{9,1... | collective-permute-start | bytes 589832 | tf_op jit(solution)/shard_map/ppermute | solution.py:238
  16.9 11.0 %collective-permute-start.10 = (bf16[8,32,512]{2,1,0:T(8,128)(2,1)S(1)}, bf16[8,32,512]{2,1,0:T(8,128)(2,1)S(1)}, u32[]{:S(2)}, u32[]{:S(2)}) collective-permute-start(bf16[8,32,512]{2,1,0:T(8,128)(2,1)S(1)} %get-tuple-element.97), channel_id=1, source_target_pairs={{0,4},{4,8},{8,12},{12,0},{1,5},{5,9},{9,13},{13,1},{2,6},{6,10},{... | collective-permute-start | bytes 786440 | tf_op jit(solution)/shard_map/ppermute | solution.py:232
  18.1 13.1 %collective-permute-start.5 = (bf16[8,32,512]{2,1,0:T(8,128)(2,1)S(1)}, bf16[8,32,512]{2,1,0:T(8,128)(2,1)S(1)}, u32[]{:S(2)}, u32[]{:S(2)}) collective-permute-start(bf16[8,32,512]{2,1,0:T(8,128)(2,1)S(1)} %get-tuple-element.79), channel_id=1, source_target_pairs={{0,12},{4,0},{8,4},{12,8},{1,13},{5,1},{9,5},{13,9},{2,14},{6,2},{... | collective-permute-start | bytes 786440 | tf_op jit(solution)/shard_map/ppermute | solution.py:232
  19.0 6.2 %collective-permute-start.6 = (bf16[8,16,512]{2,1,0:T(8,128)(2,1)S(1)}, bf16[8,16,512]{2,1,0:T(8,128)(2,1)S(1)}, u32[]{:S(2)}, u32[]{:S(2)}) collective-permute-start(bf16[8,16,512]{2,1,0:T(8,128)(2,1)S(1)} %collective-permute-done.refs_0_), channel_id=1, source_target_pairs={{0,2},{2,0},{1,3},{3,1},{4,6},{6,4},{5,7},{7,5},{8,10},{10,8},{9,1... | collective-permute-start | bytes 393224 | tf_op jit(solution)/shard_map/ppermute | solution.py:238
  20.5 6.1 %collective-permute-start.7 = (bf16[8,16,512]{2,1,0:T(8,128)(2,1)S(1)}, bf16[8,16,512]{2,1,0:T(8,128)(2,1)S(1)}, u32[]{:S(2)}, u32[]{:S(2)}) collective-permute-start(bf16[8,16,512]{2,1,0:T(8,128)(2,1)S(1)} %collective-permute-done.2.refs_0_), channel_id=1, source_target_pairs={{0,2},{2,0},{1,3},{3,1},{4,6},{6,4},{5,7},{7,5},{8,10},{10,8},{9,1... | collective-permute-start | bytes 393224 | tf_op jit(solution)/shard_map/ppermute | solution.py:238
  21.0 8.5 %collective-permute-start.8 = (bf16[8,16,512]{2,1,0:T(8,128)(2,1)S(1)}, bf16[8,16,512]{2,1,0:T(8,128)(2,1)S(1)}, u32[]{:S(2)}, u32[]{:S(2)}) collective-permute-start(bf16[8,16,512]{2,1,0:T(8,128)(2,1)S(1)} %collective-permute-done.1.refs_0_), channel_id=1, source_target_pairs={{0,2},{2,0},{1,3},{3,1},{4,6},{6,4},{5,7},{7,5},{8,10},{10,8},{9,1... | collective-permute-start | bytes 393224 | tf_op jit(solution)/shard_map/ppermute | solution.py:238
  27.9 9.2 %collective-permute-start.13 = (bf16[8,32,512]{2,1,0:T(8,128)(2,1)S(1)}, bf16[8,32,512]{2,1,0:T(8,128)(2,1)S(1)}, u32[]{:S(2)}, u32[]{:S(2)}) collective-permute-start(bf16[8,32,512]{2,1,0:T(8,128)(2,1)S(1)} %collective-permute-done.10.refs_0_), channel_id=1, source_target_pairs={{0,2},{2,0},{1,3},{3,1},{4,6},{6,4},{5,7},{7,5},{8,10},{10,8},{9,1... | collective-permute-start | bytes 786440 | tf_op jit(solution)/shard_map/ppermute | solution.py:238
  31.2 8.7 %collective-permute-start.9 = (bf16[8,32,512]{2,1,0:T(8,128)(2,1)S(1)}, bf16[8,32,512]{2,1,0:T(8,128)(2,1)S(1)}, u32[]{:S(2)}, u32[]{:S(2)}) collective-permute-start(bf16[8,32,512]{2,1,0:T(8,128)(2,1)S(1)} %collective-permute-done.5.refs_0_), channel_id=1, source_target_pairs={{0,2},{2,0},{1,3},{3,1},{4,6},{6,4},{5,7},{7,5},{8,10},{10,8},{9,1... | collective-permute-start | bytes 786440 | tf_op jit(solution)/shard_map/ppermute | solution.py:238
  32.7 10.5 %collective-permute-start.11 = (bf16[8,32,512]{2,1,0:T(8,128)(2,1)S(1)}, bf16[8,32,512]{2,1,0:T(8,128)(2,1)S(1)}, u32[]{:S(2)}, u32[]{:S(2)}) collective-permute-start(bf16[8,32,512]{2,1,0:T(8,128)(2,1)S(1)} %get-tuple-element.98), channel_id=1, source_target_pairs={{0,8},{4,12},{8,0},{12,4},{1,9},{5,13},{9,1},{13,5},{2,10},{6,14},... | collective-permute-start | bytes 786440 | tf_op jit(solution)/shard_map/ppermute | solution.py:232
  34.1 4.8 %collective-permute-start.12 = (bf16[24,16,512]{2,1,0:T(8,128)(2,1)S(1)}, bf16[24,16,512]{2,1,0:T(8,128)(2,1)S(1)}, u32[]{:S(2)}, u32[]{:S(2)}) collective-permute-start(bf16[24,16,512]{2,1,0:T(8,128)(2,1)S(1)} %shard_map.69), channel_id=1, source_target_pairs={{0,1},{1,0},{2,3},{3,2},{4,5},{5,4},{6,7},{7,6},{8,9},{9,8},{10,11... | collective-permute-start | bytes 1179656 | tf_op jit(solution)/shard_map/ppermute | solution.py:273
  43.2 7.5 %collective-permute-start.17 = (bf16[8,32,512]{2,1,0:T(8,128)(2,1)S(1)}, bf16[8,32,512]{2,1,0:T(8,128)(2,1)S(1)}, u32[]{:S(2)}, u32[]{:S(2)}) collective-permute-start(bf16[8,32,512]{2,1,0:T(8,128)(2,1)S(1)} %collective-permute-done.11.refs_0_), channel_id=1, source_target_pairs={{0,2},{2,0},{1,3},{3,1},{4,6},{6,4},{5,7},{7,5},{8,10},{10,8},{9,1... | collective-permute-start | bytes 786440 | tf_op jit(solution)/shard_map/ppermute | solution.py:238
  43.7 10.3 %collective-permute-start.14 = (bf16[8,16,512]{2,1,0:T(8,128)(2,1)S(1)}, bf16[8,16,512]{2,1,0:T(8,128)(2,1)S(1)}, u32[]{:S(2)}, u32[]{:S(2)}) collective-permute-start(bf16[8,16,512]{2,1,0:T(8,128)(2,1)S(1)} %get-tuple-element.110), channel_id=1, source_target_pairs={{0,12},{4,8},{8,4},{12,0},{1,13},{5,9},{9,5},{13,1},{2,14},{6,10},... | collective-permute-start | bytes 393224 | tf_op jit(solution)/shard_map/ppermute | solution.py:235
  45.0 10.9 %collective-permute-start.15 = (bf16[8,16,512]{2,1,0:T(8,128)(2,1)S(1)}, bf16[8,16,512]{2,1,0:T(8,128)(2,1)S(1)}, u32[]{:S(2)}, u32[]{:S(2)}) collective-permute-start(bf16[8,16,512]{2,1,0:T(8,128)(2,1)S(1)} %get-tuple-element.111), channel_id=1, source_target_pairs={{0,8},{4,12},{8,0},{12,4},{1,9},{5,13},{9,1},{13,5},{2,10},{6,14},... | collective-permute-start | bytes 393224 | tf_op jit(solution)/shard_map/ppermute | solution.py:235
  49.3 6.7 %collective-permute-start.16 = (bf16[8,16,512]{2,1,0:T(8,128)(2,1)S(1)}, bf16[8,16,512]{2,1,0:T(8,128)(2,1)S(1)}, u32[]{:S(2)}, u32[]{:S(2)}) collective-permute-start(bf16[8,16,512]{2,1,0:T(8,128)(2,1)S(1)} %get-tuple-element.112), channel_id=1, source_target_pairs={{0,4},{4,0},{8,12},{12,8},{1,5},{5,1},{9,13},{13,9},{2,6},{6,2},{1... | collective-permute-start | bytes 393224 | tf_op jit(solution)/shard_map/ppermute | solution.py:235
  53.0 3.0 %collective-permute-start.18 = (bf16[24,32,512]{2,1,0:T(8,128)(2,1)S(1)}, bf16[24,32,512]{2,1,0:T(8,128)(2,1)S(1)}, u32[]{:S(2)}, u32[]{:S(2)}) collective-permute-start(bf16[24,32,512]{2,1,0:T(8,128)(2,1)S(1)} %shard_map.76), channel_id=1, source_target_pairs={{0,1},{1,0},{2,3},{3,2},{4,5},{5,4},{6,7},{7,6},{8,9},{9,8},{10,11... | collective-permute-start | bytes 2359304 | tf_op jit(solution)/shard_map/ppermute | solution.py:284
  57.2 13.1 %collective-permute-start.21 = (bf16[8,32,512]{2,1,0:T(8,128)(2,1)S(1)}, bf16[8,32,512]{2,1,0:T(8,128)(2,1)S(1)}, u32[]{:S(2)}, u32[]{:S(2)}) collective-permute-start(bf16[8,32,512]{2,1,0:T(8,128)(2,1)S(1)} %get-tuple-element.142), channel_id=1, source_target_pairs={{0,4},{4,0},{8,12},{12,8},{1,5},{5,1},{9,13},{13,9},{2,6},{6,2},{1... | collective-permute-start | bytes 786440 | tf_op jit(solution)/shard_map/ppermute | solution.py:235
  60.0 18.7 %collective-permute-start.19 = (bf16[8,32,512]{2,1,0:T(8,128)(2,1)S(1)}, bf16[8,32,512]{2,1,0:T(8,128)(2,1)S(1)}, u32[]{:S(2)}, u32[]{:S(2)}) collective-permute-start(bf16[8,32,512]{2,1,0:T(8,128)(2,1)S(1)} %get-tuple-element.139), channel_id=1, source_target_pairs={{0,8},{4,12},{8,0},{12,4},{1,9},{5,13},{9,1},{13,5},{2,10},{6,14},... | collective-permute-start | bytes 786440 | tf_op jit(solution)/shard_map/ppermute | solution.py:235
  60.7 23.9 %collective-permute-start.20 = (bf16[8,32,512]{2,1,0:T(8,128)(2,1)S(1)}, bf16[8,32,512]{2,1,0:T(8,128)(2,1)S(1)}, u32[]{:S(2)}, u32[]{:S(2)}) collective-permute-start(bf16[8,32,512]{2,1,0:T(8,128)(2,1)S(1)} %get-tuple-element.140), channel_id=1, source_target_pairs={{0,12},{4,8},{8,4},{12,0},{1,13},{5,9},{9,5},{13,1},{2,14},{6,10},... | collective-permute-start | bytes 786440 | tf_op jit(solution)/shard_map/ppermute | solution.py:235
  (2 other events, 10.4 us)

commit v20 on v19

--- a/solution.py
+++ b/solution.py
@@ -267,7 +267,7 @@
     b[3], b[2], stay_a, gone = fence((b[3], b[2], stay_a, gone))
     x_3 = along_x(b[3])
     x_1, = anchor([along_x(b[1])], 2_500_000_000)
-    b[2] = shift_z(b[2], 2)
+    b[2], = anchor([shift_z(b[2], 2)], 2_000_000_000)
     kept = reduce(down, stay_a, (0, 0, 0, 0), n_modes, jnp.float32)
     spots = [(j, 0, freqs) for j in (1, 2, 3, 0)]
     outs = restore(kept, lax.ppermute(gone, "pol", other), ratios, up, spots)

time: 86.3 us -> 86.3 us (level)
    ppermute x8, waiting for transfers between devices: 4.81 us -> 2.91 us  [along_x(): return lax.ppermute(value, 'kl', other)]
    ppermute x6, waiting for transfers between devices: 3.23 us -> 4.54 us  [shift_z(): lax.ppermute(value, 'fm', [(i, (i + j) % parts) for i in range(parts)])]
    ppermute x6, starting transfers between devices: 8.2 us -> 9.1 us  [shift_z(): lax.ppermute(value, 'fm', [(i, (i + j) % parts) for i in range(parts)])]
  transfers between devices with their start and end apart: 22 -> 22, of which waited for: 8 -> 7; matrix products, arithmetic and copies ran while one was open for 2% -> 2% of each run, Pallas kernels for 26% -> 26%
where the time goes in v20:
time: 86.3 us; the launch traced here: 86.1 us
  waiting for transfers between devices  29.7 us (34%)
  starting transfers between devices  28 us (32%)
  Pallas kernels  25.1 us (29%)
  local copies, waits for them, and re-layouts  2.39 us (3%)
  between operations  0.92 us (1%)
    ppermute x6, waiting for transfers between devices, swap_z(): return lax.ppermute(value, 'fm', [(i, i ^ j) for i in range(parts)])  22.2 us
    ppermute x6, starting transfers between devices, swap_z(): return lax.ppermute(value, 'fm', [(i, i ^ j) for i in range(parts)])  9.61 us
    pallas_call x7, Pallas kernels, project(): pl.pallas_call(functools.partial(project_kernel, piece=piece, blocks=bloc...  9.57 us
    ppermute x8, starting transfers between devices, along_x(): return lax.ppermute(value, 'kl', other)  9.26 us
    ppermute x6, starting transfers between devices, shift_z(): lax.ppermute(value, 'fm', [(i, (i + j) % parts) for i in range(parts)])  9.1 us
    pallas_call x1, Pallas kernels, hold(): pl.pallas_call(hold_kernel, grid_spec=pltpu.PrefetchScalarGridSpec(num_sc...  7.04 us
    ppermute x6, waiting for transfers between devices, shift_z(): lax.ppermute(value, 'fm', [(i, (i + j) % parts) for i in range(parts)])  4.54 us
    pallas_call x3, Pallas kernels, place(): pl.pallas_call(functools.partial(place_kernel, spots=spots, first=first),...  4.06 us
  transfers between devices with their start and end apart: 22, of which 7 were waited for; matrix products, arithmetic and copies ran while one was open for 2% of the time, Pallas kernels for 26%

profile of v20, /device:TPU:12, one launch (start us, length us, event | category | flops | bytes accessed | tf_op | source)
XLA Modules:
  0.0 86.1 jit_solution(9035087799944726064)
XLA Ops:
  1.1 1.6 %collective-permute-start = (bf16[8,16,512]{2,1,0:T(8,128)(2,1)S(1)}, bf16[8,16,512]{2,1,0:T(8,128)(2,1)S(1)}, u32[]{:S(2)}, u32[]{:S(2)}) collective-permute-start(bf16[8,16,512]{2,1,0:T(8,128)(2,1)S(1)} %get-tuple-element.154), channel_id=1, source_target_pairs={{0,4},{4,8},{8,12},{12,0},{1,5},{5,9},{9,13},{13,1},{2,6},{6,10},{... | collective-permute-start | bytes 393224 | tf_op jit(solution)/shard_map/ppermute | solution.py:232
  3.2 2.6 %collective-permute-start.2 = (bf16[8,16,512]{2,1,0:T(8,128)(2,1)S(1)}, bf16[8,16,512]{2,1,0:T(8,128)(2,1)S(1)}, u32[]{:S(2)}, u32[]{:S(2)}) collective-permute-start(bf16[8,16,512]{2,1,0:T(8,128)(2,1)S(1)} %get-tuple-element.152), channel_id=1, source_target_pairs={{0,8},{4,12},{8,0},{12,4},{1,9},{5,13},{9,1},{13,5},{2,10},{6,14},... | collective-permute-start | bytes 393224 | tf_op jit(solution)/shard_map/ppermute | solution.py:232
  6.8 1.6 %collective-permute-start.3 = (bf16[4,48,512]{2,1,0:T(8,128)(2,1)S(1)}, bf16[4,48,512]{2,1,0:T(8,128)(2,1)S(1)}, u32[]{:S(2)}, u32[]{:S(2)}) collective-permute-start(bf16[4,48,512]{2,1,0:T(8,128)(2,1)S(1)} %get-tuple-element.148.refs_0_), channel_id=1, source_target_pairs={{0,2},{2,0},{1,3},{3,1},{4,6},{6,4},{5,7},{7,5},{8,10},{10,8},{9,1... | collective-permute-start | bytes 589832 | tf_op jit(solution)/shard_map/ppermute | solution.py:238
  9.7 7.0 %shard_map.64 = (bf16[32,512,512]{2,1,0:T(8,128)(2,1)S(1)}, bf16[384,512]{1,0:T(8,128)(2,1)S(1)}, bf16[512,384]{1,0:T(8,128)(2,1)S(1)}) custom-call(s32[10]{0:T(128)S(1)} %compare_select_fusion.4.where, s32[4,4]{1,0:T(4,128)S(1)} %bitcast.27, s32[1]{0:T(128)S(6)} %copy.26.starts, bf16[32,512,512]{2,1,0:T(8,128)(2,1)} %bitcast.28, bf16[32,24]{1,0:T(8,128)(2,1)S(1)} %bitcast.26), custom_call_target="tpu_custom_call" | custom-call | flops 1024 | bytes 1024 | tf_op jit(solution)/shard_map/pallas_call | solution.py:63
  19.0 1.5 %collective-permute-start.6 = (bf16[8,16,512]{2,1,0:T(8,128)(2,1)S(1)}, bf16[8,16,512]{2,1,0:T(8,128)(2,1)S(1)}, u32[]{:S(2)}, u32[]{:S(2)}) collective-permute-start(bf16[8,16,512]{2,1,0:T(8,128)(2,1)S(1)} %collective-permute-done.refs_0_), channel_id=1, source_target_pairs={{0,2},{2,0},{1,3},{3,1},{4,6},{6,4},{5,7},{7,5},{8,10},{10,8},{9,1... | collective-permute-start | bytes 393224 | tf_op jit(solution)/shard_map/ppermute | solution.py:238
  21.0 1.5 %collective-permute-start.8 = (bf16[8,16,512]{2,1,0:T(8,128)(2,1)S(1)}, bf16[8,16,512]{2,1,0:T(8,128)(2,1)S(1)}, u32[]{:S(2)}, u32[]{:S(2)}) collective-permute-start(bf16[8,16,512]{2,1,0:T(8,128)(2,1)S(1)} %collective-permute-done.1.refs_0_), channel_id=1, source_target_pairs={{0,2},{2,0},{1,3},{3,1},{4,6},{6,4},{5,7},{7,5},{8,10},{10,8},{9,1... | collective-permute-start | bytes 393224 | tf_op jit(solution)/shard_map/ppermute | solution.py:238
  22.5 1.4 %shard_map.65 = (bf16[8,48,512]{2,1,0:T(8,128)(2,1)S(1)}, bf16[8,48,512]{2,1,0:T(8,128)(2,1)S(1)}) custom-call(s32[10]{0:T(128)S(1)} %compare_select_fusion.4.where, bf16[4,48,512]{2,1,0:T(8,128)(2,1)S(1)} %get-tuple-element.148.refs_0_, bf16[4,48,512]{2,1,0:T(8,128)(2,1)S(1)} %get-tuple-element.147.refs_1_, ...), custom_call_target="tpu_custom_call" | custom-call | flops 400000000 | bytes 1024 | tf_op jit(solution)/shard_map/pallas_call | solution.py:102
  25.1 1.4 %shard_map.66 = (bf16[8,16,512]{2,1,0:T(8,128)(2,1)S(1)}, bf16[8,16,512]{2,1,0:T(8,128)(2,1)S(1)}) custom-call(s32[10]{0:T(128)S(1)} %compare_select_fusion.4.where, bf16[8,16,512]{2,1,0:T(8,128)(2,1)S(1)} %collective-permute-done.refs_0_, bf16[8,16,512]{2,1,0:T(8,128)(2,1)S(1)} %collective-permute-done.6.refs_1_, ...), custom_call_target="tpu_custom_call" | custom-call | flops 400000000 | bytes 1024 | tf_op jit(solution)/shard_map/pallas_call | solution.py:102
  26.5 1.4 %shard_map.67 = (bf16[8,16,512]{2,1,0:T(8,128)(2,1)S(1)}, bf16[8,16,512]{2,1,0:T(8,128)(2,1)S(1)}) custom-call(s32[10]{0:T(128)S(1)} %compare_select_fusion.4.where, bf16[8,16,512]{2,1,0:T(8,128)(2,1)S(1)} %collective-permute-done.2.refs_0_, bf16[8,16,512]{2,1,0:T(8,128)(2,1)S(1)} %collective-permute-done.7.refs_1_, ...), custom_call_target="tpu_custom_call" | custom-call | flops 400000000 | bytes 1024 | tf_op jit(solution)/shard_map/pallas_call | solution.py:102
  27.9 1.6 %collective-permute-start.13 = (bf16[8,32,512]{2,1,0:T(8,128)(2,1)S(1)}, bf16[8,32,512]{2,1,0:T(8,128)(2,1)S(1)}, u32[]{:S(2)}, u32[]{:S(2)}) collective-permute-start(bf16[8,32,512]{2,1,0:T(8,128)(2,1)S(1)} %collective-permute-done.10.refs_0_), channel_id=1, source_target_pairs={{0,2},{2,0},{1,3},{3,1},{4,6},{6,4},{5,7},{7,5},{8,10},{10,8},{9,1... | collective-permute-start | bytes 786440 | tf_op jit(solution)/shard_map/ppermute | solution.py:238
  31.2 2.4 %collective-permute-start.11 = (bf16[8,32,512]{2,1,0:T(8,128)(2,1)S(1)}, bf16[8,32,512]{2,1,0:T(8,128)(2,1)S(1)}, u32[]{:S(2)}, u32[]{:S(2)}) collective-permute-start(bf16[8,32,512]{2,1,0:T(8,128)(2,1)S(1)} %get-tuple-element.98), channel_id=1, source_target_pairs={{0,8},{4,12},{8,0},{12,4},{1,9},{5,13},{9,1},{13,5},{2,10},{6,14},... | collective-permute-start | bytes 786440 | tf_op jit(solution)/shard_map/ppermute | solution.py:232
  34.2 1.5 %collective-permute-done.13.refs_0_ = bf16[8,32,512]{2,1,0:T(8,128)(2,1)S(1)} collective-permute-done((bf16[8,32,512]{2,1,0:T(8,128)(2,1)S(1)}, bf16[8,32,512]{2,1,0:T(8,128)(2,1)S(1)}, u32[]{:S(2)}, u32[]{:S(2)}) %collective-permute-start.13) | collective-permute-done | bytes 262176 | tf_op jit(solution)/shard_map/ppermute | solution.py:238
  36.1 1.4 %shard_map.74 = (bf16[8,32,512]{2,1,0:T(8,128)(2,1)S(1)}, bf16[8,32,512]{2,1,0:T(8,128)(2,1)S(1)}) custom-call(s32[10]{0:T(128)S(1)} %compare_select_fusion.4.where, bf16[8,32,512]{2,1,0:T(8,128)(2,1)S(1)} %collective-permute-done.10.refs_0_, bf16[8,32,512]{2,1,0:T(8,128)(2,1)S(1)} %shard_map.73.refs_1_, ...), custom_call_target="tpu_custom_call" | custom-call | flops 1024 | bytes 1024 | tf_op jit(solution)/shard_map/pallas_call | solution.py:102
  37.5 4.5 %collective-permute-done.11.refs_0_ = bf16[8,32,512]{2,1,0:T(8,128)(2,1)S(1)} collective-permute-done((bf16[8,32,512]{2,1,0:T(8,128)(2,1)S(1)}, bf16[8,32,512]{2,1,0:T(8,128)(2,1)S(1)}, u32[]{:S(2)}, u32[]{:S(2)}) %collective-permute-start.11) | collective-permute-done | bytes 262176 | tf_op jit(solution)/shard_map/ppermute | solution.py:232
  42.6 1.6 %collective-permute-start.17 = (bf16[8,32,512]{2,1,0:T(8,128)(2,1)S(1)}, bf16[8,32,512]{2,1,0:T(8,128)(2,1)S(1)}, u32[]{:S(2)}, u32[]{:S(2)}) collective-permute-start(bf16[8,32,512]{2,1,0:T(8,128)(2,1)S(1)} %shard_map.70.refs_0_), channel_id=1, source_target_pairs={{0,2},{2,0},{1,3},{3,1},{4,6},{6,4},{5,7},{7,5},{8,10},{10,8},{9,1... | collective-permute-start | bytes 786440 | tf_op jit(solution)/shard_map/ppermute | solution.py:238
  45.4 4.3 %collective-permute-start.15 = (bf16[8,16,512]{2,1,0:T(8,128)(2,1)S(1)}, bf16[8,16,512]{2,1,0:T(8,128)(2,1)S(1)}, u32[]{:S(2)}, u32[]{:S(2)}) collective-permute-start(bf16[8,16,512]{2,1,0:T(8,128)(2,1)S(1)} %get-tuple-element.111), channel_id=1, source_target_pairs={{0,8},{4,12},{8,0},{12,4},{1,9},{5,13},{9,1},{13,5},{2,10},{6,14},... | collective-permute-start | bytes 393224 | tf_op jit(solution)/shard_map/ppermute | solution.py:235
  49.7 1.4 %shard_map.76 = (bf16[8,32,512]{2,1,0:T(8,128)(2,1)S(1)}, bf16[8,32,512]{2,1,0:T(8,128)(2,1)S(1)}) custom-call(s32[10]{0:T(128)S(1)} %compare_select_fusion.4.where, bf16[8,32,512]{2,1,0:T(8,128)(2,1)S(1)} %collective-permute-done.5.refs_0_, bf16[8,32,512]{2,1,0:T(8,128)(2,1)S(1)} %collective-permute-done.9.refs_1_, ...), custom_call_target="tpu_custom_call" | custom-call | flops 1024 | bytes 1024 | tf_op jit(solution)/shard_map/pallas_call | solution.py:102
  51.1 1.4 %shard_map.75 = (bf16[8,32,512]{2,1,0:T(8,128)(2,1)S(1)}, bf16[8,32,512]{2,1,0:T(8,128)(2,1)S(1)}) custom-call(s32[10]{0:T(128)S(1)} %compare_select_fusion.4.where, bf16[8,32,512]{2,1,0:T(8,128)(2,1)S(1)} %shard_map.70.refs_0_, bf16[8,32,512]{2,1,0:T(8,128)(2,1)S(1)} %collective-permute-done.17.refs_1_, ...), custom_call_target="tpu_custom_call" | custom-call | flops 1024 | bytes 1024 | tf_op jit(solution)/shard_map/pallas_call | solution.py:102
  54.5 2.3 %collective-permute-done.15.refs_1_ = bf16[8,16,512]{2,1,0:T(8,128)(2,1)S(1)} collective-permute-done((bf16[8,16,512]{2,1,0:T(8,128)(2,1)S(1)}, bf16[8,16,512]{2,1,0:T(8,128)(2,1)S(1)}, u32[]{:S(2)}, u32[]{:S(2)}) %collective-permute-start.15) | collective-permute-done | bytes 131104 | tf_op jit(solution)/shard_map/ppermute | solution.py:235
  58.0 2.5 %collective-permute-start.21 = (bf16[8,32,512]{2,1,0:T(8,128)(2,1)S(1)}, bf16[8,32,512]{2,1,0:T(8,128)(2,1)S(1)}, u32[]{:S(2)}, u32[]{:S(2)}) collective-permute-start(bf16[8,32,512]{2,1,0:T(8,128)(2,1)S(1)} %get-tuple-element.142), channel_id=1, source_target_pairs={{0,4},{4,0},{8,12},{12,8},{1,5},{5,1},{9,13},{13,9},{2,6},{6,2},{1... | collective-permute-start | bytes 786440 | tf_op jit(solution)/shard_map/ppermute | solution.py:235
  62.1 1.4 %shard_map.81.refs_2_ = bf16[8,4,48,512]{3,2,1,0:T(8,128)(2,1)} custom-call(s32[10]{0:T(128)S(1)} %compare_select_fusion.4.where, bf16[8,16,512]{2,1,0:T(8,128)(2,1)S(1)} %get-tuple-element.143.refs_0_, bf16[8,16,512]{2,1,0:T(8,128)(2,1)S(1)} %get-tuple-element.144.refs_1_, bf16[8,16,512]{2,1,0:T(8,128)(2,1)S(1)} %get-tuple-element.145.refs_2_, ...), custom_call_target="tpu_custom_call" | custom-call | flops 1024 | bytes 1024 | tf_op jit(solution)/shard_map/pallas_call | solution.py:190
  63.5 7.2 %collective-permute-done.21.refs_1_ = bf16[8,32,512]{2,1,0:T(8,128)(2,1)S(1)} collective-permute-done((bf16[8,32,512]{2,1,0:T(8,128)(2,1)S(1)}, bf16[8,32,512]{2,1,0:T(8,128)(2,1)S(1)}, u32[]{:S(2)}, u32[]{:S(2)}) %collective-permute-start.21) | collective-permute-done | bytes 262176 | tf_op jit(solution)/shard_map/ppermute | solution.py:235
  72.0 7.5 %collective-permute-done.19.refs_0_ = bf16[8,32,512]{2,1,0:T(8,128)(2,1)S(1)} collective-permute-done((bf16[8,32,512]{2,1,0:T(8,128)(2,1)S(1)}, bf16[8,32,512]{2,1,0:T(8,128)(2,1)S(1)}, u32[]{:S(2)}, u32[]{:S(2)}) %collective-permute-start.19) | collective-permute-done | bytes 262176 | tf_op jit(solution)/shard_map/ppermute | solution.py:235
  79.5 5.2 %collective-permute-done.20.refs_1_ = bf16[8,32,512]{2,1,0:T(8,128)(2,1)S(1)} collective-permute-done((bf16[8,32,512]{2,1,0:T(8,128)(2,1)S(1)}, bf16[8,32,512]{2,1,0:T(8,128)(2,1)S(1)}, u32[]{:S(2)}, u32[]{:S(2)}) %collective-permute-start.20) | collective-permute-done | bytes 262176 | tf_op jit(solution)/shard_map/ppermute | solution.py:235
  (55 shorter events, 19.3 us)
Async XLA Ops:
  0.0 9.6 %copy-start.2 = (bf16[1,32,24]{1,2,0:T(8,128)(2,1)S(1)}, bf16[1,32,24]{1,2,0:T(8,128)(2,1)}, u32[]{:S(2)}) copy-start(bf16[1,32,24]{1,2,0:T(8,128)(2,1)} %param.10) | copy-start | bytes 4612
  0.0 9.7 %copy-start = (s32[1,4,4]{2,1,0:T(4,128)S(1)}, s32[1,4,4]{2,1,0:T(4,128)}, u32[]{:S(2)}) copy-start(s32[1,4,4]{2,1,0:T(4,128)} %param.8) | copy-start | bytes 196
  1.1 15.7 %collective-permute-start = (bf16[8,16,512]{2,1,0:T(8,128)(2,1)S(1)}, bf16[8,16,512]{2,1,0:T(8,128)(2,1)S(1)}, u32[]{:S(2)}, u32[]{:S(2)}) collective-permute-start(bf16[8,16,512]{2,1,0:T(8,128)(2,1)S(1)} %get-tuple-element.154), channel_id=1, source_target_pairs={{0,4},{4,8},{8,12},{12,0},{1,5},{5,9},{9,13},{13,1},{2,6},{6,10},{... | collective-permute-start | bytes 393224 | tf_op jit(solution)/shard_map/ppermute | solution.py:232
  2.7 14.1 %collective-permute-start.1 = (bf16[8,16,512]{2,1,0:T(8,128)(2,1)S(1)}, bf16[8,16,512]{2,1,0:T(8,128)(2,1)S(1)}, u32[]{:S(2)}, u32[]{:S(2)}) collective-permute-start(bf16[8,16,512]{2,1,0:T(8,128)(2,1)S(1)} %get-tuple-element.153), channel_id=1, source_target_pairs={{0,12},{4,0},{8,4},{12,8},{1,13},{5,1},{9,5},{13,9},{2,14},{6,2},{... | collective-permute-start | bytes 393224 | tf_op jit(solution)/shard_map/ppermute | solution.py:232
  3.2 13.7 %collective-permute-start.2 = (bf16[8,16,512]{2,1,0:T(8,128)(2,1)S(1)}, bf16[8,16,512]{2,1,0:T(8,128)(2,1)S(1)}, u32[]{:S(2)}, u32[]{:S(2)}) collective-permute-start(bf16[8,16,512]{2,1,0:T(8,128)(2,1)S(1)} %get-tuple-element.152), channel_id=1, source_target_pairs={{0,8},{4,12},{8,0},{12,4},{1,9},{5,13},{9,1},{13,5},{2,10},{6,14},... | collective-permute-start | bytes 393224 | tf_op jit(solution)/shard_map/ppermute | solution.py:232
  6.8 10.0 %collective-permute-start.3 = (bf16[4,48,512]{2,1,0:T(8,128)(2,1)S(1)}, bf16[4,48,512]{2,1,0:T(8,128)(2,1)S(1)}, u32[]{:S(2)}, u32[]{:S(2)}) collective-permute-start(bf16[4,48,512]{2,1,0:T(8,128)(2,1)S(1)} %get-tuple-element.148.refs_0_), channel_id=1, source_target_pairs={{0,2},{2,0},{1,3},{3,1},{4,6},{6,4},{5,7},{7,5},{8,10},{10,8},{9,1... | collective-permute-start | bytes 589832 | tf_op jit(solution)/shard_map/ppermute | solution.py:238
  8.4 8.5 %collective-permute-start.4 = (bf16[4,48,512]{2,1,0:T(8,128)(2,1)S(1)}, bf16[4,48,512]{2,1,0:T(8,128)(2,1)S(1)}, u32[]{:S(2)}, u32[]{:S(2)}) collective-permute-start(bf16[4,48,512]{2,1,0:T(8,128)(2,1)S(1)} %get-tuple-element.147.refs_1_), channel_id=1, source_target_pairs={{0,2},{2,0},{1,3},{3,1},{4,6},{6,4},{5,7},{7,5},{8,10},{10,8},{9,1... | collective-permute-start | bytes 589832 | tf_op jit(solution)/shard_map/ppermute | solution.py:238
  16.9 11.0 %collective-permute-start.10 = (bf16[8,32,512]{2,1,0:T(8,128)(2,1)S(1)}, bf16[8,32,512]{2,1,0:T(8,128)(2,1)S(1)}, u32[]{:S(2)}, u32[]{:S(2)}) collective-permute-start(bf16[8,32,512]{2,1,0:T(8,128)(2,1)S(1)} %get-tuple-element.97), channel_id=1, source_target_pairs={{0,4},{4,8},{8,12},{12,0},{1,5},{5,9},{9,13},{13,1},{2,6},{6,10},{... | collective-permute-start | bytes 786440 | tf_op jit(solution)/shard_map/ppermute | solution.py:232
  18.1 13.1 %collective-permute-start.5 = (bf16[8,32,512]{2,1,0:T(8,128)(2,1)S(1)}, bf16[8,32,512]{2,1,0:T(8,128)(2,1)S(1)}, u32[]{:S(2)}, u32[]{:S(2)}) collective-permute-start(bf16[8,32,512]{2,1,0:T(8,128)(2,1)S(1)} %get-tuple-element.79), channel_id=1, source_target_pairs={{0,12},{4,0},{8,4},{12,8},{1,13},{5,1},{9,5},{13,9},{2,14},{6,2},{... | collective-permute-start | bytes 786440 | tf_op jit(solution)/shard_map/ppermute | solution.py:232
  19.0 6.2 %collective-permute-start.6 = (bf16[8,16,512]{2,1,0:T(8,128)(2,1)S(1)}, bf16[8,16,512]{2,1,0:T(8,128)(2,1)S(1)}, u32[]{:S(2)}, u32[]{:S(2)}) collective-permute-start(bf16[8,16,512]{2,1,0:T(8,128)(2,1)S(1)} %collective-permute-done.refs_0_), channel_id=1, source_target_pairs={{0,2},{2,0},{1,3},{3,1},{4,6},{6,4},{5,7},{7,5},{8,10},{10,8},{9,1... | collective-permute-start | bytes 393224 | tf_op jit(solution)/shard_map/ppermute | solution.py:238
  20.5 6.1 %collective-permute-start.7 = (bf16[8,16,512]{2,1,0:T(8,128)(2,1)S(1)}, bf16[8,16,512]{2,1,0:T(8,128)(2,1)S(1)}, u32[]{:S(2)}, u32[]{:S(2)}) collective-permute-start(bf16[8,16,512]{2,1,0:T(8,128)(2,1)S(1)} %collective-permute-done.2.refs_0_), channel_id=1, source_target_pairs={{0,2},{2,0},{1,3},{3,1},{4,6},{6,4},{5,7},{7,5},{8,10},{10,8},{9,1... | collective-permute-start | bytes 393224 | tf_op jit(solution)/shard_map/ppermute | solution.py:238
  21.0 8.5 %collective-permute-start.8 = (bf16[8,16,512]{2,1,0:T(8,128)(2,1)S(1)}, bf16[8,16,512]{2,1,0:T(8,128)(2,1)S(1)}, u32[]{:S(2)}, u32[]{:S(2)}) collective-permute-start(bf16[8,16,512]{2,1,0:T(8,128)(2,1)S(1)} %collective-permute-done.1.refs_0_), channel_id=1, source_target_pairs={{0,2},{2,0},{1,3},{3,1},{4,6},{6,4},{5,7},{7,5},{8,10},{10,8},{9,1... | collective-permute-start | bytes 393224 | tf_op jit(solution)/shard_map/ppermute | solution.py:238
  27.9 7.8 %collective-permute-start.13 = (bf16[8,32,512]{2,1,0:T(8,128)(2,1)S(1)}, bf16[8,32,512]{2,1,0:T(8,128)(2,1)S(1)}, u32[]{:S(2)}, u32[]{:S(2)}) collective-permute-start(bf16[8,32,512]{2,1,0:T(8,128)(2,1)S(1)} %collective-permute-done.10.refs_0_), channel_id=1, source_target_pairs={{0,2},{2,0},{1,3},{3,1},{4,6},{6,4},{5,7},{7,5},{8,10},{10,8},{9,1... | collective-permute-start | bytes 786440 | tf_op jit(solution)/shard_map/ppermute | solution.py:238
  31.2 10.7 %collective-permute-start.11 = (bf16[8,32,512]{2,1,0:T(8,128)(2,1)S(1)}, bf16[8,32,512]{2,1,0:T(8,128)(2,1)S(1)}, u32[]{:S(2)}, u32[]{:S(2)}) collective-permute-start(bf16[8,32,512]{2,1,0:T(8,128)(2,1)S(1)} %get-tuple-element.98), channel_id=1, source_target_pairs={{0,8},{4,12},{8,0},{12,4},{1,9},{5,13},{9,1},{13,5},{2,10},{6,14},... | collective-permute-start | bytes 786440 | tf_op jit(solution)/shard_map/ppermute | solution.py:232
  33.6 9.0 %collective-permute-start.9 = (bf16[8,32,512]{2,1,0:T(8,128)(2,1)S(1)}, bf16[8,32,512]{2,1,0:T(8,128)(2,1)S(1)}, u32[]{:S(2)}, u32[]{:S(2)}) collective-permute-start(bf16[8,32,512]{2,1,0:T(8,128)(2,1)S(1)} %collective-permute-done.5.refs_0_), channel_id=1, source_target_pairs={{0,2},{2,0},{1,3},{3,1},{4,6},{6,4},{5,7},{7,5},{8,10},{10,8},{9,1... | collective-permute-start | bytes 786440 | tf_op jit(solution)/shard_map/ppermute | solution.py:238
  34.2 7.8 %collective-permute-start.12 = (bf16[24,16,512]{2,1,0:T(8,128)(2,1)S(1)}, bf16[24,16,512]{2,1,0:T(8,128)(2,1)S(1)}, u32[]{:S(2)}, u32[]{:S(2)}) collective-permute-start(bf16[24,16,512]{2,1,0:T(8,128)(2,1)S(1)} %shard_map.69), channel_id=1, source_target_pairs={{0,1},{1,0},{2,3},{3,2},{4,5},{5,4},{6,7},{7,6},{8,9},{9,8},{10,11... | collective-permute-start | bytes 1179656 | tf_op jit(solution)/shard_map/ppermute | solution.py:273
  42.6 8.5 %collective-permute-start.17 = (bf16[8,32,512]{2,1,0:T(8,128)(2,1)S(1)}, bf16[8,32,512]{2,1,0:T(8,128)(2,1)S(1)}, u32[]{:S(2)}, u32[]{:S(2)}) collective-permute-start(bf16[8,32,512]{2,1,0:T(8,128)(2,1)S(1)} %shard_map.70.refs_0_), channel_id=1, source_target_pairs={{0,2},{2,0},{1,3},{3,1},{4,6},{6,4},{5,7},{7,5},{8,10},{10,8},{9,1... | collective-permute-start | bytes 786440 | tf_op jit(solution)/shard_map/ppermute | solution.py:238
  44.2 10.3 %collective-permute-start.14 = (bf16[8,16,512]{2,1,0:T(8,128)(2,1)S(1)}, bf16[8,16,512]{2,1,0:T(8,128)(2,1)S(1)}, u32[]{:S(2)}, u32[]{:S(2)}) collective-permute-start(bf16[8,16,512]{2,1,0:T(8,128)(2,1)S(1)} %get-tuple-element.110), channel_id=1, source_target_pairs={{0,12},{4,8},{8,4},{12,0},{1,13},{5,9},{9,5},{13,1},{2,14},{6,10},... | collective-permute-start | bytes 393224 | tf_op jit(solution)/shard_map/ppermute | solution.py:235
  45.4 11.3 %collective-permute-start.15 = (bf16[8,16,512]{2,1,0:T(8,128)(2,1)S(1)}, bf16[8,16,512]{2,1,0:T(8,128)(2,1)S(1)}, u32[]{:S(2)}, u32[]{:S(2)}) collective-permute-start(bf16[8,16,512]{2,1,0:T(8,128)(2,1)S(1)} %get-tuple-element.111), channel_id=1, source_target_pairs={{0,8},{4,12},{8,0},{12,4},{1,9},{5,13},{9,1},{13,5},{2,10},{6,14},... | collective-permute-start | bytes 393224 | tf_op jit(solution)/shard_map/ppermute | solution.py:235
  49.7 7.0 %collective-permute-start.16 = (bf16[8,16,512]{2,1,0:T(8,128)(2,1)S(1)}, bf16[8,16,512]{2,1,0:T(8,128)(2,1)S(1)}, u32[]{:S(2)}, u32[]{:S(2)}) collective-permute-start(bf16[8,16,512]{2,1,0:T(8,128)(2,1)S(1)} %get-tuple-element.112), channel_id=1, source_target_pairs={{0,4},{4,0},{8,12},{12,8},{1,5},{5,1},{9,13},{13,9},{2,6},{6,2},{1... | collective-permute-start | bytes 393224 | tf_op jit(solution)/shard_map/ppermute | solution.py:235
  53.4 3.3 %collective-permute-start.18 = (bf16[24,32,512]{2,1,0:T(8,128)(2,1)S(1)}, bf16[24,32,512]{2,1,0:T(8,128)(2,1)S(1)}, u32[]{:S(2)}, u32[]{:S(2)}) collective-permute-start(bf16[24,32,512]{2,1,0:T(8,128)(2,1)S(1)} %shard_map.77), channel_id=1, source_target_pairs={{0,1},{1,0},{2,3},{3,2},{4,5},{5,4},{6,7},{7,6},{8,9},{9,8},{10,11... | collective-permute-start | bytes 2359304 | tf_op jit(solution)/shard_map/ppermute | solution.py:284
  58.0 12.6 %collective-permute-start.21 = (bf16[8,32,512]{2,1,0:T(8,128)(2,1)S(1)}, bf16[8,32,512]{2,1,0:T(8,128)(2,1)S(1)}, u32[]{:S(2)}, u32[]{:S(2)}) collective-permute-start(bf16[8,32,512]{2,1,0:T(8,128)(2,1)S(1)} %get-tuple-element.142), channel_id=1, source_target_pairs={{0,4},{4,0},{8,12},{12,8},{1,5},{5,1},{9,13},{13,9},{2,6},{6,2},{1... | collective-permute-start | bytes 786440 | tf_op jit(solution)/shard_map/ppermute | solution.py:235
  60.6 19.0 %collective-permute-start.19 = (bf16[8,32,512]{2,1,0:T(8,128)(2,1)S(1)}, bf16[8,32,512]{2,1,0:T(8,128)(2,1)S(1)}, u32[]{:S(2)}, u32[]{:S(2)}) collective-permute-start(bf16[8,32,512]{2,1,0:T(8,128)(2,1)S(1)} %get-tuple-element.139), channel_id=1, source_target_pairs={{0,8},{4,12},{8,0},{12,4},{1,9},{5,13},{9,1},{13,5},{2,10},{6,14},... | collective-permute-start | bytes 786440 | tf_op jit(solution)/shard_map/ppermute | solution.py:235
  61.5 23.2 %collective-permute-start.20 = (bf16[8,32,512]{2,1,0:T(8,128)(2,1)S(1)}, bf16[8,32,512]{2,1,0:T(8,128)(2,1)S(1)}, u32[]{:S(2)}, u32[]{:S(2)}) collective-permute-start(bf16[8,32,512]{2,1,0:T(8,128)(2,1)S(1)} %get-tuple-element.140), channel_id=1, source_target_pairs={{0,12},{4,8},{8,4},{12,0},{1,13},{5,9},{9,5},{13,1},{2,14},{6,10},... | collective-permute-start | bytes 786440 | tf_op jit(solution)/shard_map/ppermute | solution.py:235
  (2 other events, 9.8 us)

commit v21 on v19

--- a/solution.py
+++ b/solution.py
@@ -121,11 +121,11 @@
 
 
 def by_rows(count, ell, first=0):
-    return pl.BlockSpec((count, ROWS, ell), lambda g: (0, g + first // ROWS, 0))
+    return pl.BlockSpec((count, ROWS, ell), lambda g, *_: (0, g + first // ROWS, 0))
 
 
 def fixed(shape):
-    return pl.BlockSpec(shape, lambda g: (0,) * len(shape))
+    return pl.BlockSpec(shape, lambda g, *_: (0,) * len(shape))
 
 
 def sky_specs(skies, first):
@@ -145,37 +145,43 @@
     )(modes, *skies)
 
 
-def restore_kernel(up_ref, ratio_ref, kept_ref, came_ref, *outs, spots):
+def restore_kernel(where, up_ref, ratio_ref, kept_ref, came_ref, *outs, spots, shifted):
     n_modes, _, ell = came_ref.shape
     freqs = up_ref.shape[0] // ROWS // PARTS
     total = kept_ref[...] + came_ref[...].astype(jnp.float32)
     weighted = (total * ratio_ref[...]).astype(jnp.bfloat16).reshape(n_modes * ROWS, ell)
-    for (j, low, high), out in zip(spots, outs):
-        modes = up_ref[(j * freqs + low) * ROWS:(j * freqs + high) * ROWS, :]
+    size = freqs * ROWS
+    for j, out in zip(spots, outs):
+        piece = where[2 * PARTS + 2 + j] if shifted else j
+        modes = up_ref[pl.ds(pl.multiple_of(piece * size, size), size), :]
         value = jnp.dot(modes, weighted, preferred_element_type=jnp.float32)
         out[...] = value.astype(jnp.bfloat16).reshape(out.shape)
 
 
-def restore(kept, came, ratios, up, spots):
+def restore(where, kept, came, ratios, up, spots, shifted):
     n_modes, rows, ell = came.shape
-    return pl.pallas_call(
-        functools.partial(restore_kernel, spots=spots),
-        grid=(rows // ROWS,),
-        in_specs=[fixed(up.shape), fixed(ratios.shape)] + [by_rows(n_modes, ell)] * 2,
-        out_specs=[by_rows(high - low, ell) for _, low, high in spots],
-        out_shape=[jax.ShapeDtypeStruct((high - low, rows, ell), jnp.bfloat16) for _, low, high in spots],
+    freqs = up.shape[0] // ROWS // PARTS
+    return pl.pallas_call(
+        functools.partial(restore_kernel, spots=spots, shifted=shifted),
+        grid_spec=pltpu.PrefetchScalarGridSpec(
+            num_scalar_prefetch=1,
+            grid=(rows // ROWS,),
+            in_specs=[fixed(up.shape), fixed(ratios.shape)] + [by_rows(n_modes, ell)] * 2,
+            out_specs=[by_rows(freqs, ell)] * len(spots),
+        ),
+        out_shape=[jax.ShapeDtypeStruct((freqs, rows, ell), jnp.bfloat16)] * len(spots),
         compiler_params=pltpu.CompilerParams(vmem_limit_bytes=VMEM_LIMIT),
         cost_estimate=pl.CostEstimate(flops=1024, bytes_accessed=1024, transcendentals=0),
-    )(up, ratios, kept, came)
-
-
-def place_kernel(where, *refs, spots, first):
+    )(where, up, ratios, kept, came)
+
+
+def place_kernel(where, *refs, spots, first, shifted):
     count = len(spots)
     pieces, out, sems = refs[:count], refs[-2], refs[-1]
     rows = pieces[0].shape[1]
     copies = [
-        pltpu.make_async_copy(pieces[n], out.at[low:high, where[PARTS + 2 + j], first:first + rows, :], sems.at[n])
-        for n, (j, low, high) in enumerate(spots)
+        pltpu.make_async_copy(pieces[n], out.at[:, where[j if shifted else PARTS + 2 + j], first:first + rows, :], sems.at[n])
+        for n, j in enumerate(spots)
     ]
     for copy in copies:
         copy.start()
@@ -183,12 +189,12 @@
         copy.wait()
 
 
-def place(where, pieces, spots, first, shape, into=None):
+def place(where, pieces, spots, first, shape, shifted, into=None):
     count = len(spots)
     extra = [] if into is None else [into]
     anywhere = pl.BlockSpec(memory_space=pl.ANY)
     return pl.pallas_call(
-        functools.partial(place_kernel, spots=spots, first=first),
+        functools.partial(place_kernel, spots=spots, first=first, shifted=shifted),
         grid_spec=pltpu.PrefetchScalarGridSpec(
             num_scalar_prefetch=1,
             grid=(),
@@ -240,8 +246,9 @@
     def cut(j, first, rows):
         return lax.dynamic_slice(visibility, (0, (z + j) % parts, first, 0), (freqs, 1, rows, base)).reshape(freqs, rows, base)
 
-    index = jnp.arange(2 * parts + 2, dtype=jnp.int32)
+    index = jnp.arange(3 * parts + 2, dtype=jnp.int32)
     where = jnp.where(index < parts, (z - index) % parts, z ^ (index - parts - 2))
+    where = jnp.where(index < 2 * parts + 2, where, z ^ ((z + index - 2 * parts - 2) % parts))
     where = jnp.where(index == parts, (x == p).astype(jnp.int32), where)
     where = jnp.where(index == parts + 1, x * ell_tiles, where).astype(jnp.int32)
     ratio = signal_noise[0] / (1.0 + signal_noise[0])
@@ -269,8 +276,8 @@
     x_1, = anchor([along_x(b[1])], 2_500_000_000)
     b[2] = shift_z(b[2], 2)
     kept = reduce(down, stay_a, (0, 0, 0, 0), n_modes, jnp.float32)
-    spots = [(j, 0, freqs) for j in (1, 2, 3, 0)]
-    outs = restore(kept, lax.ppermute(gone, "pol", other), ratios, up, spots)
+    spots = [1, 2, 3, 0]
+    outs = restore(where, kept, lax.ppermute(gone, "pol", other), ratios, up, spots, False)
     near = project(where, [b[1]], [x_1], held, 1, blocks)
     x_3, b, outs, near = fence((x_3, b, outs, near))
     first = {j: swap_z(outs[j - 1], j) for j in (1, 2, 3)}
@@ -285,12 +292,12 @@
     kept = reduce(down, stays, (ROWS, 0, 0, 0), n_modes, jnp.float32)
     first[3], first[2], first[1], kept = fence((first[3], first[2], first[1], kept))
     first[3], first[2], first[1] = anchor([first[3], first[2], first[1]], 7_500_000_000)
-    outs, first[3], first[2], first[1] = fence((restore(kept, came, ratios, up, spots), first[3], first[2], first[1]))
+    outs, first[3], first[2], first[1] = fence((restore(where, kept, came, ratios, up, spots, True), first[3], first[2], first[1]))
     first[0] = here
-    back = [swap_z(outs[j - 1], j) for j in (1, 2, 3)]
-    result = place(where, [first[j] for j in (1, 2, 3, 0)], spots, 0, shape)
-    result = place(where, [outs[3], back[0]], [spots[3], spots[0]], ROWS, shape, into=result)
-    return place(where, back[1:], spots[1:3], ROWS, shape, into=result)
+    back = [shift_z(outs[j - 1], j) for j in (1, 2, 3)]
+    result = place(where, [first[j] for j in spots], spots, 0, shape, False)
+    result = place(where, [outs[3], back[0]], [0, 1], ROWS, shape, True, into=result)
+    return place(where, back[1:], [2, 3], ROWS, shape, True, into=result)
 
 
 def plain(visibility, beam_transfer, tile_mask, first_block, eigen_modes, signal_noise):

time: 86.3 us -> 86.8 us (level)
  waiting for transfers between devices: 30.4 us -> 28.7 us
  Pallas kernels: 25 us -> 26.1 us
  starting transfers between devices: 27.3 us -> 28.3 us
    ppermute x6 -> x3, waiting for transfers between devices: 22.3 us -> 1.95 us  [swap_z(): return lax.ppermute(value, 'fm', [(i, i ^ j) for i in range(parts)])]
    ppermute x6 -> x9, waiting for transfers between devices: 3.23 us -> 22.4 us  [shift_z(): lax.ppermute(value, 'fm', [(i, (i + j) % parts) for i in range(parts)])]
    ppermute x6 -> x9, starting transfers between devices: 8.2 us -> 13.6 us  [shift_z(): lax.ppermute(value, 'fm', [(i, (i + j) % parts) for i in range(parts)])]
    ppermute x6 -> x3, starting transfers between devices: 9.85 us -> 5.53 us  [swap_z(): return lax.ppermute(value, 'fm', [(i, i ^ j) for i in range(parts)])]
    pallas_call x5, Pallas kernels: 5.82 us -> 6.91 us  [the longest x3 4.06 us: place(): pl.pallas_call(functools.partial(place_kernel, spots=spots, first=first,...]
  transfers between devices with their start and end apart: 22 -> 22, of which waited for: 8 -> 8; matrix products, arithmetic and copies ran while one was open for 2% -> 2% of each run, Pallas kernels for 26% -> 27%
where the time goes in v21:
time: 86.8 us; the launch traced here: 86.5 us
  waiting for transfers between devices  28.7 us (33%)
  starting transfers between devices  28.3 us (33%)
  Pallas kernels  26.1 us (30%)
  local copies, waits for them, and re-layouts  2.39 us (3%)
  between operations  0.93 us (1%)
    ppermute x9, waiting for transfers between devices, shift_z(): lax.ppermute(value, 'fm', [(i, (i + j) % parts) for i in range(parts)])  22.4 us
    ppermute x9, starting transfers between devices, shift_z(): lax.ppermute(value, 'fm', [(i, (i + j) % parts) for i in range(parts)])  13.6 us
    pallas_call x7, Pallas kernels, project(): pl.pallas_call(functools.partial(project_kernel, piece=piece, blocks=bloc...  9.57 us
    ppermute x8, starting transfers between devices, along_x(): return lax.ppermute(value, 'kl', other)  9.13 us
    pallas_call x1, Pallas kernels, hold(): pl.pallas_call(hold_kernel, grid_spec=pltpu.PrefetchScalarGridSpec(num_sc...  7.04 us
    ppermute x3, starting transfers between devices, swap_z(): return lax.ppermute(value, 'fm', [(i, i ^ j) for i in range(parts)])  5.53 us
    ppermute x8, waiting for transfers between devices, along_x(): return lax.ppermute(value, 'kl', other)  4.38 us
    pallas_call x3, Pallas kernels, place(): pl.pallas_call(functools.partial(place_kernel, spots=spots, first=first,...  4.06 us
  transfers between devices with their start and end apart: 22, of which 8 were waited for; matrix products, arithmetic and copies ran while one was open for 2% of the time, Pallas kernels for 27%

profile of v21, /device:TPU:12, one launch (start us, length us, event | category | flops | bytes accessed | tf_op | source)
XLA Modules:
  0.0 86.5 jit_solution(14132862231635274010)
XLA Ops:
  1.1 1.6 %collective-permute-start = (bf16[8,16,512]{2,1,0:T(8,128)(2,1)S(1)}, bf16[8,16,512]{2,1,0:T(8,128)(2,1)S(1)}, u32[]{:S(2)}, u32[]{:S(2)}) collective-permute-start(bf16[8,16,512]{2,1,0:T(8,128)(2,1)S(1)} %get-tuple-element.154), channel_id=1, source_target_pairs={{0,4},{4,8},{8,12},{12,0},{1,5},{5,9},{9,13},{13,1},{2,6},{6,10},{... | collective-permute-start | bytes 393224 | tf_op jit(solution)/shard_map/ppermute | solution.py:238
  3.2 2.6 %collective-permute-start.2 = (bf16[8,16,512]{2,1,0:T(8,128)(2,1)S(1)}, bf16[8,16,512]{2,1,0:T(8,128)(2,1)S(1)}, u32[]{:S(2)}, u32[]{:S(2)}) collective-permute-start(bf16[8,16,512]{2,1,0:T(8,128)(2,1)S(1)} %get-tuple-element.152), channel_id=1, source_target_pairs={{0,8},{4,12},{8,0},{12,4},{1,9},{5,13},{9,1},{13,5},{2,10},{6,14},... | collective-permute-start | bytes 393224 | tf_op jit(solution)/shard_map/ppermute | solution.py:238
  6.8 1.6 %collective-permute-start.3 = (bf16[4,48,512]{2,1,0:T(8,128)(2,1)S(1)}, bf16[4,48,512]{2,1,0:T(8,128)(2,1)S(1)}, u32[]{:S(2)}, u32[]{:S(2)}) collective-permute-start(bf16[4,48,512]{2,1,0:T(8,128)(2,1)S(1)} %get-tuple-element.148.refs_0_), channel_id=1, source_target_pairs={{0,2},{2,0},{1,3},{3,1},{4,6},{6,4},{5,7},{7,5},{8,10},{10,8},{9,1... | collective-permute-start | bytes 589832 | tf_op jit(solution)/shard_map/ppermute | solution.py:244
  9.7 7.0 %shard_map.64 = (bf16[32,512,512]{2,1,0:T(8,128)(2,1)S(1)}, bf16[384,512]{1,0:T(8,128)(2,1)S(1)}, bf16[512,384]{1,0:T(8,128)(2,1)S(1)}) custom-call(s32[14]{0:T(128)S(1)} %compare_select_fusion.7.where, s32[4,4]{1,0:T(4,128)S(1)} %bitcast.27, s32[1]{0:T(128)S(6)} %copy.24.starts, bf16[32,512,512]{2,1,0:T(8,128)(2,1)} %bitcast.28, bf16[32,24]{1,0:T(8,128)(2,1)S(1)} %bitcast.26), custom_call_target="tpu_custom_call" | custom-call | flops 1024 | bytes 1024 | tf_op jit(solution)/shard_map/pallas_call | solution.py:63
  19.0 1.5 %collective-permute-start.6 = (bf16[8,16,512]{2,1,0:T(8,128)(2,1)S(1)}, bf16[8,16,512]{2,1,0:T(8,128)(2,1)S(1)}, u32[]{:S(2)}, u32[]{:S(2)}) collective-permute-start(bf16[8,16,512]{2,1,0:T(8,128)(2,1)S(1)} %collective-permute-done.refs_0_), channel_id=1, source_target_pairs={{0,2},{2,0},{1,3},{3,1},{4,6},{6,4},{5,7},{7,5},{8,10},{10,8},{9,1... | collective-permute-start | bytes 393224 | tf_op jit(solution)/shard_map/ppermute | solution.py:244
  21.0 1.5 %collective-permute-start.8 = (bf16[8,16,512]{2,1,0:T(8,128)(2,1)S(1)}, bf16[8,16,512]{2,1,0:T(8,128)(2,1)S(1)}, u32[]{:S(2)}, u32[]{:S(2)}) collective-permute-start(bf16[8,16,512]{2,1,0:T(8,128)(2,1)S(1)} %collective-permute-done.1.refs_0_), channel_id=1, source_target_pairs={{0,2},{2,0},{1,3},{3,1},{4,6},{6,4},{5,7},{7,5},{8,10},{10,8},{9,1... | collective-permute-start | bytes 393224 | tf_op jit(solution)/shard_map/ppermute | solution.py:244
  22.5 1.4 %shard_map.65 = (bf16[8,48,512]{2,1,0:T(8,128)(2,1)S(1)}, bf16[8,48,512]{2,1,0:T(8,128)(2,1)S(1)}) custom-call(s32[14]{0:T(128)S(1)} %compare_select_fusion.7.where, bf16[4,48,512]{2,1,0:T(8,128)(2,1)S(1)} %get-tuple-element.148.refs_0_, bf16[4,48,512]{2,1,0:T(8,128)(2,1)S(1)} %get-tuple-element.147.refs_1_, ...), custom_call_target="tpu_custom_call" | custom-call | flops 400000000 | bytes 1024 | tf_op jit(solution)/shard_map/pallas_call | solution.py:102
  27.9 1.6 %collective-permute-start.13 = (bf16[8,32,512]{2,1,0:T(8,128)(2,1)S(1)}, bf16[8,32,512]{2,1,0:T(8,128)(2,1)S(1)}, u32[]{:S(2)}, u32[]{:S(2)}) collective-permute-start(bf16[8,32,512]{2,1,0:T(8,128)(2,1)S(1)} %collective-permute-done.10.refs_0_), channel_id=1, source_target_pairs={{0,2},{2,0},{1,3},{3,1},{4,6},{6,4},{5,7},{7,5},{8,10},{10,8},{9,1... | collective-permute-start | bytes 786440 | tf_op jit(solution)/shard_map/ppermute | solution.py:244
  31.2 1.4 %collective-permute-start.9 = (bf16[8,32,512]{2,1,0:T(8,128)(2,1)S(1)}, bf16[8,32,512]{2,1,0:T(8,128)(2,1)S(1)}, u32[]{:S(2)}, u32[]{:S(2)}) collective-permute-start(bf16[8,32,512]{2,1,0:T(8,128)(2,1)S(1)} %collective-permute-done.5.refs_0_), channel_id=1, source_target_pairs={{0,2},{2,0},{1,3},{3,1},{4,6},{6,4},{5,7},{7,5},{8,10},{10,8},{9,1... | collective-permute-start | bytes 786440 | tf_op jit(solution)/shard_map/ppermute | solution.py:244
  32.7 1.5 %collective-permute-start.11 = (bf16[8,32,512]{2,1,0:T(8,128)(2,1)S(1)}, bf16[8,32,512]{2,1,0:T(8,128)(2,1)S(1)}, u32[]{:S(2)}, u32[]{:S(2)}) collective-permute-start(bf16[8,32,512]{2,1,0:T(8,128)(2,1)S(1)} %get-tuple-element.98), channel_id=1, source_target_pairs={{0,8},{4,12},{8,0},{12,4},{1,9},{5,13},{9,1},{13,5},{2,10},{6,14},... | collective-permute-start | bytes 786440 | tf_op jit(solution)/shard_map/ppermute | solution.py:238
  34.2 3.0 %collective-permute-done.13.refs_0_ = bf16[8,32,512]{2,1,0:T(8,128)(2,1)S(1)} collective-permute-done((bf16[8,32,512]{2,1,0:T(8,128)(2,1)S(1)}, bf16[8,32,512]{2,1,0:T(8,128)(2,1)S(1)}, u32[]{:S(2)}, u32[]{:S(2)}) %collective-permute-start.13) | collective-permute-done | bytes 262176 | tf_op jit(solution)/shard_map/ppermute | solution.py:244
  37.5 1.4 %shard_map.73 = (bf16[8,32,512]{2,1,0:T(8,128)(2,1)S(1)}, bf16[8,32,512]{2,1,0:T(8,128)(2,1)S(1)}) custom-call(s32[14]{0:T(128)S(1)} %compare_select_fusion.7.where, bf16[8,32,512]{2,1,0:T(8,128)(2,1)S(1)} %collective-permute-done.10.refs_0_, bf16[8,32,512]{2,1,0:T(8,128)(2,1)S(1)} %shard_map.72.refs_1_, ...), custom_call_target="tpu_custom_call" | custom-call | flops 1024 | bytes 1024 | tf_op jit(solution)/shard_map/pallas_call | solution.py:102
  40.1 3.1 %collective-permute-done.11.refs_0_ = bf16[8,32,512]{2,1,0:T(8,128)(2,1)S(1)} collective-permute-done((bf16[8,32,512]{2,1,0:T(8,128)(2,1)S(1)}, bf16[8,32,512]{2,1,0:T(8,128)(2,1)S(1)}, u32[]{:S(2)}, u32[]{:S(2)}) %collective-permute-start.11) | collective-permute-done | bytes 262176 | tf_op jit(solution)/shard_map/ppermute | solution.py:238
  45.0 4.3 %collective-permute-start.15 = (bf16[8,16,512]{2,1,0:T(8,128)(2,1)S(1)}, bf16[8,16,512]{2,1,0:T(8,128)(2,1)S(1)}, u32[]{:S(2)}, u32[]{:S(2)}) collective-permute-start(bf16[8,16,512]{2,1,0:T(8,128)(2,1)S(1)} %get-tuple-element.111), channel_id=1, source_target_pairs={{0,8},{4,12},{8,0},{12,4},{1,9},{5,13},{9,1},{13,5},{2,10},{6,14},... | collective-permute-start | bytes 393224 | tf_op jit(solution)/shard_map/ppermute | solution.py:241
  49.3 1.4 %shard_map.75 = (bf16[8,32,512]{2,1,0:T(8,128)(2,1)S(1)}, bf16[8,32,512]{2,1,0:T(8,128)(2,1)S(1)}) custom-call(s32[14]{0:T(128)S(1)} %compare_select_fusion.7.where, bf16[8,32,512]{2,1,0:T(8,128)(2,1)S(1)} %collective-permute-done.5.refs_0_, bf16[8,32,512]{2,1,0:T(8,128)(2,1)S(1)} %collective-permute-done.9.refs_1_, ...), custom_call_target="tpu_custom_call" | custom-call | flops 1024 | bytes 1024 | tf_op jit(solution)/shard_map/pallas_call | solution.py:102
  50.7 1.4 %shard_map.74 = (bf16[8,32,512]{2,1,0:T(8,128)(2,1)S(1)}, bf16[8,32,512]{2,1,0:T(8,128)(2,1)S(1)}) custom-call(s32[14]{0:T(128)S(1)} %compare_select_fusion.7.where, bf16[8,32,512]{2,1,0:T(8,128)(2,1)S(1)} %collective-permute-done.11.refs_0_, bf16[8,32,512]{2,1,0:T(8,128)(2,1)S(1)} %collective-permute-done.17.refs_1_, ...), custom_call_target="tpu_custom_call" | custom-call | flops 1024 | bytes 1024 | tf_op jit(solution)/shard_map/pallas_call | solution.py:102
  54.0 1.9 %collective-permute-done.15.refs_1_ = bf16[8,16,512]{2,1,0:T(8,128)(2,1)S(1)} collective-permute-done((bf16[8,16,512]{2,1,0:T(8,128)(2,1)S(1)}, bf16[8,16,512]{2,1,0:T(8,128)(2,1)S(1)}, u32[]{:S(2)}, u32[]{:S(2)}) %collective-permute-start.15) | collective-permute-done | bytes 131104 | tf_op jit(solution)/shard_map/ppermute | solution.py:241
  56.0 1.8 %shard_map.78 = (bf16[8,32,512]{2,1,0:T(8,128)(2,1)S(1)}, bf16[8,32,512]{2,1,0:T(8,128)(2,1)S(1)}, bf16[8,32,512]{2,1,0:T(8,128)(2,1)S(1)}, bf16[8,32,512]{2,1,0:T(8,128)(2,1)S(1)}) custom-call(s32[14]{0:T(128)S(1)} %compare_select_fusion.7.where, bf16[512,384]{1,0:T(8,128)(2,1)S(1)} %get-tuple-element.78.up_ref, ...), custom_call_target="tpu_custom_call" | custom-call | flops 1024 | bytes 1024 | tf_op jit(solution)/shard_map/pallas_call | solution.py:164
  57.8 1.8 %collective-permute-start.21 = (bf16[8,32,512]{2,1,0:T(8,128)(2,1)S(1)}, bf16[8,32,512]{2,1,0:T(8,128)(2,1)S(1)}, u32[]{:S(2)}, u32[]{:S(2)}) collective-permute-start(bf16[8,32,512]{2,1,0:T(8,128)(2,1)S(1)} %get-tuple-element.142), channel_id=1, source_target_pairs={{0,4},{4,8},{8,12},{12,0},{1,5},{5,9},{9,13},{13,1},{2,6},{6,10},{... | collective-permute-start | bytes 786440 | tf_op jit(solution)/shard_map/ppermute | solution.py:238
  59.6 3.2 %collective-permute-start.19 = (bf16[8,32,512]{2,1,0:T(8,128)(2,1)S(1)}, bf16[8,32,512]{2,1,0:T(8,128)(2,1)S(1)}, u32[]{:S(2)}, u32[]{:S(2)}) collective-permute-start(bf16[8,32,512]{2,1,0:T(8,128)(2,1)S(1)} %get-tuple-element.139), channel_id=1, source_target_pairs={{0,8},{4,12},{8,0},{12,4},{1,9},{5,13},{9,1},{13,5},{2,10},{6,14},... | collective-permute-start | bytes 786440 | tf_op jit(solution)/shard_map/ppermute | solution.py:238
  63.2 1.4 %shard_map.80.refs_2_ = bf16[8,4,48,512]{3,2,1,0:T(8,128)(2,1)} custom-call(s32[14]{0:T(128)S(1)} %compare_select_fusion.7.where, bf16[8,16,512]{2,1,0:T(8,128)(2,1)S(1)} %get-tuple-element.143.refs_0_, bf16[8,16,512]{2,1,0:T(8,128)(2,1)S(1)} %get-tuple-element.144.refs_1_, bf16[8,16,512]{2,1,0:T(8,128)(2,1)S(1)} %get-tuple-element.145.refs_2_, ...), custom_call_target="tpu_custom_call" | custom-call | flops 1024 | bytes 1024 | tf_op jit(solution)/shard_map/pallas_call | solution.py:196
  64.5 3.1 %collective-permute-done.21.refs_1_ = bf16[8,32,512]{2,1,0:T(8,128)(2,1)S(1)} collective-permute-done((bf16[8,32,512]{2,1,0:T(8,128)(2,1)S(1)}, bf16[8,32,512]{2,1,0:T(8,128)(2,1)S(1)}, u32[]{:S(2)}, u32[]{:S(2)}) %collective-permute-start.21) | collective-permute-done | bytes 262176 | tf_op jit(solution)/shard_map/ppermute | solution.py:238
  69.0 12.2 %collective-permute-done.19.refs_0_ = bf16[8,32,512]{2,1,0:T(8,128)(2,1)S(1)} collective-permute-done((bf16[8,32,512]{2,1,0:T(8,128)(2,1)S(1)}, bf16[8,32,512]{2,1,0:T(8,128)(2,1)S(1)}, u32[]{:S(2)}, u32[]{:S(2)}) %collective-permute-start.19) | collective-permute-done | bytes 262176 | tf_op jit(solution)/shard_map/ppermute | solution.py:238
  81.2 4.0 %collective-permute-done.20.refs_1_ = bf16[8,32,512]{2,1,0:T(8,128)(2,1)S(1)} collective-permute-done((bf16[8,32,512]{2,1,0:T(8,128)(2,1)S(1)}, bf16[8,32,512]{2,1,0:T(8,128)(2,1)S(1)}, u32[]{:S(2)}, u32[]{:S(2)}) %collective-permute-start.20) | collective-permute-done | bytes 262176 | tf_op jit(solution)/shard_map/ppermute | solution.py:238
  (54 shorter events, 20.1 us)
Async XLA Ops:
  0.0 9.6 %copy-start.2 = (bf16[1,32,24]{1,2,0:T(8,128)(2,1)S(1)}, bf16[1,32,24]{1,2,0:T(8,128)(2,1)}, u32[]{:S(2)}) copy-start(bf16[1,32,24]{1,2,0:T(8,128)(2,1)} %param.10) | copy-start | bytes 4612
  0.0 9.7 %copy-start = (s32[1,4,4]{2,1,0:T(4,128)S(1)}, s32[1,4,4]{2,1,0:T(4,128)}, u32[]{:S(2)}) copy-start(s32[1,4,4]{2,1,0:T(4,128)} %param.8) | copy-start | bytes 196
  1.1 15.7 %collective-permute-start = (bf16[8,16,512]{2,1,0:T(8,128)(2,1)S(1)}, bf16[8,16,512]{2,1,0:T(8,128)(2,1)S(1)}, u32[]{:S(2)}, u32[]{:S(2)}) collective-permute-start(bf16[8,16,512]{2,1,0:T(8,128)(2,1)S(1)} %get-tuple-element.154), channel_id=1, source_target_pairs={{0,4},{4,8},{8,12},{12,0},{1,5},{5,9},{9,13},{13,1},{2,6},{6,10},{... | collective-permute-start | bytes 393224 | tf_op jit(solution)/shard_map/ppermute | solution.py:238
  2.7 14.1 %collective-permute-start.1 = (bf16[8,16,512]{2,1,0:T(8,128)(2,1)S(1)}, bf16[8,16,512]{2,1,0:T(8,128)(2,1)S(1)}, u32[]{:S(2)}, u32[]{:S(2)}) collective-permute-start(bf16[8,16,512]{2,1,0:T(8,128)(2,1)S(1)} %get-tuple-element.153), channel_id=1, source_target_pairs={{0,12},{4,0},{8,4},{12,8},{1,13},{5,1},{9,5},{13,9},{2,14},{6,2},{... | collective-permute-start | bytes 393224 | tf_op jit(solution)/shard_map/ppermute | solution.py:238
  3.2 13.7 %collective-permute-start.2 = (bf16[8,16,512]{2,1,0:T(8,128)(2,1)S(1)}, bf16[8,16,512]{2,1,0:T(8,128)(2,1)S(1)}, u32[]{:S(2)}, u32[]{:S(2)}) collective-permute-start(bf16[8,16,512]{2,1,0:T(8,128)(2,1)S(1)} %get-tuple-element.152), channel_id=1, source_target_pairs={{0,8},{4,12},{8,0},{12,4},{1,9},{5,13},{9,1},{13,5},{2,10},{6,14},... | collective-permute-start | bytes 393224 | tf_op jit(solution)/shard_map/ppermute | solution.py:238
  6.8 10.0 %collective-permute-start.3 = (bf16[4,48,512]{2,1,0:T(8,128)(2,1)S(1)}, bf16[4,48,512]{2,1,0:T(8,128)(2,1)S(1)}, u32[]{:S(2)}, u32[]{:S(2)}) collective-permute-start(bf16[4,48,512]{2,1,0:T(8,128)(2,1)S(1)} %get-tuple-element.148.refs_0_), channel_id=1, source_target_pairs={{0,2},{2,0},{1,3},{3,1},{4,6},{6,4},{5,7},{7,5},{8,10},{10,8},{9,1... | collective-permute-start | bytes 589832 | tf_op jit(solution)/shard_map/ppermute | solution.py:244
  8.4 8.5 %collective-permute-start.4 = (bf16[4,48,512]{2,1,0:T(8,128)(2,1)S(1)}, bf16[4,48,512]{2,1,0:T(8,128)(2,1)S(1)}, u32[]{:S(2)}, u32[]{:S(2)}) collective-permute-start(bf16[4,48,512]{2,1,0:T(8,128)(2,1)S(1)} %get-tuple-element.147.refs_1_), channel_id=1, source_target_pairs={{0,2},{2,0},{1,3},{3,1},{4,6},{6,4},{5,7},{7,5},{8,10},{10,8},{9,1... | collective-permute-start | bytes 589832 | tf_op jit(solution)/shard_map/ppermute | solution.py:244
  16.9 11.0 %collective-permute-start.10 = (bf16[8,32,512]{2,1,0:T(8,128)(2,1)S(1)}, bf16[8,32,512]{2,1,0:T(8,128)(2,1)S(1)}, u32[]{:S(2)}, u32[]{:S(2)}) collective-permute-start(bf16[8,32,512]{2,1,0:T(8,128)(2,1)S(1)} %get-tuple-element.97), channel_id=1, source_target_pairs={{0,4},{4,8},{8,12},{12,0},{1,5},{5,9},{9,13},{13,1},{2,6},{6,10},{... | collective-permute-start | bytes 786440 | tf_op jit(solution)/shard_map/ppermute | solution.py:238
  18.1 13.1 %collective-permute-start.5 = (bf16[8,32,512]{2,1,0:T(8,128)(2,1)S(1)}, bf16[8,32,512]{2,1,0:T(8,128)(2,1)S(1)}, u32[]{:S(2)}, u32[]{:S(2)}) collective-permute-start(bf16[8,32,512]{2,1,0:T(8,128)(2,1)S(1)} %get-tuple-element.79), channel_id=1, source_target_pairs={{0,12},{4,0},{8,4},{12,8},{1,13},{5,1},{9,5},{13,9},{2,14},{6,2},{... | collective-permute-start | bytes 786440 | tf_op jit(solution)/shard_map/ppermute | solution.py:238
  19.0 6.2 %collective-permute-start.6 = (bf16[8,16,512]{2,1,0:T(8,128)(2,1)S(1)}, bf16[8,16,512]{2,1,0:T(8,128)(2,1)S(1)}, u32[]{:S(2)}, u32[]{:S(2)}) collective-permute-start(bf16[8,16,512]{2,1,0:T(8,128)(2,1)S(1)} %collective-permute-done.refs_0_), channel_id=1, source_target_pairs={{0,2},{2,0},{1,3},{3,1},{4,6},{6,4},{5,7},{7,5},{8,10},{10,8},{9,1... | collective-permute-start | bytes 393224 | tf_op jit(solution)/shard_map/ppermute | solution.py:244
  20.5 6.1 %collective-permute-start.7 = (bf16[8,16,512]{2,1,0:T(8,128)(2,1)S(1)}, bf16[8,16,512]{2,1,0:T(8,128)(2,1)S(1)}, u32[]{:S(2)}, u32[]{:S(2)}) collective-permute-start(bf16[8,16,512]{2,1,0:T(8,128)(2,1)S(1)} %collective-permute-done.2.refs_0_), channel_id=1, source_target_pairs={{0,2},{2,0},{1,3},{3,1},{4,6},{6,4},{5,7},{7,5},{8,10},{10,8},{9,1... | collective-permute-start | bytes 393224 | tf_op jit(solution)/shard_map/ppermute | solution.py:244
  21.0 8.5 %collective-permute-start.8 = (bf16[8,16,512]{2,1,0:T(8,128)(2,1)S(1)}, bf16[8,16,512]{2,1,0:T(8,128)(2,1)S(1)}, u32[]{:S(2)}, u32[]{:S(2)}) collective-permute-start(bf16[8,16,512]{2,1,0:T(8,128)(2,1)S(1)} %collective-permute-done.1.refs_0_), channel_id=1, source_target_pairs={{0,2},{2,0},{1,3},{3,1},{4,6},{6,4},{5,7},{7,5},{8,10},{10,8},{9,1... | collective-permute-start | bytes 393224 | tf_op jit(solution)/shard_map/ppermute | solution.py:244
  27.9 9.2 %collective-permute-start.13 = (bf16[8,32,512]{2,1,0:T(8,128)(2,1)S(1)}, bf16[8,32,512]{2,1,0:T(8,128)(2,1)S(1)}, u32[]{:S(2)}, u32[]{:S(2)}) collective-permute-start(bf16[8,32,512]{2,1,0:T(8,128)(2,1)S(1)} %collective-permute-done.10.refs_0_), channel_id=1, source_target_pairs={{0,2},{2,0},{1,3},{3,1},{4,6},{6,4},{5,7},{7,5},{8,10},{10,8},{9,1... | collective-permute-start | bytes 786440 | tf_op jit(solution)/shard_map/ppermute | solution.py:244
  31.2 8.8 %collective-permute-start.9 = (bf16[8,32,512]{2,1,0:T(8,128)(2,1)S(1)}, bf16[8,32,512]{2,1,0:T(8,128)(2,1)S(1)}, u32[]{:S(2)}, u32[]{:S(2)}) collective-permute-start(bf16[8,32,512]{2,1,0:T(8,128)(2,1)S(1)} %collective-permute-done.5.refs_0_), channel_id=1, source_target_pairs={{0,2},{2,0},{1,3},{3,1},{4,6},{6,4},{5,7},{7,5},{8,10},{10,8},{9,1... | collective-permute-start | bytes 786440 | tf_op jit(solution)/shard_map/ppermute | solution.py:244
  32.7 10.5 %collective-permute-start.11 = (bf16[8,32,512]{2,1,0:T(8,128)(2,1)S(1)}, bf16[8,32,512]{2,1,0:T(8,128)(2,1)S(1)}, u32[]{:S(2)}, u32[]{:S(2)}) collective-permute-start(bf16[8,32,512]{2,1,0:T(8,128)(2,1)S(1)} %get-tuple-element.98), channel_id=1, source_target_pairs={{0,8},{4,12},{8,0},{12,4},{1,9},{5,13},{9,1},{13,5},{2,10},{6,14},... | collective-permute-start | bytes 786440 | tf_op jit(solution)/shard_map/ppermute | solution.py:238
  34.1 4.8 %collective-permute-start.12 = (bf16[24,16,512]{2,1,0:T(8,128)(2,1)S(1)}, bf16[24,16,512]{2,1,0:T(8,128)(2,1)S(1)}, u32[]{:S(2)}, u32[]{:S(2)}) collective-permute-start(bf16[24,16,512]{2,1,0:T(8,128)(2,1)S(1)} %shard_map.69), channel_id=1, source_target_pairs={{0,1},{1,0},{2,3},{3,2},{4,5},{5,4},{6,7},{7,6},{8,9},{9,8},{10,11... | collective-permute-start | bytes 1179656 | tf_op jit(solution)/shard_map/ppermute | solution.py:280
  43.2 7.5 %collective-permute-start.17 = (bf16[8,32,512]{2,1,0:T(8,128)(2,1)S(1)}, bf16[8,32,512]{2,1,0:T(8,128)(2,1)S(1)}, u32[]{:S(2)}, u32[]{:S(2)}) collective-permute-start(bf16[8,32,512]{2,1,0:T(8,128)(2,1)S(1)} %collective-permute-done.11.refs_0_), channel_id=1, source_target_pairs={{0,2},{2,0},{1,3},{3,1},{4,6},{6,4},{5,7},{7,5},{8,10},{10,8},{9,1... | collective-permute-start | bytes 786440 | tf_op jit(solution)/shard_map/ppermute | solution.py:244
  43.7 10.3 %collective-permute-start.14 = (bf16[8,16,512]{2,1,0:T(8,128)(2,1)S(1)}, bf16[8,16,512]{2,1,0:T(8,128)(2,1)S(1)}, u32[]{:S(2)}, u32[]{:S(2)}) collective-permute-start(bf16[8,16,512]{2,1,0:T(8,128)(2,1)S(1)} %get-tuple-element.110), channel_id=1, source_target_pairs={{0,12},{4,8},{8,4},{12,0},{1,13},{5,9},{9,5},{13,1},{2,14},{6,10},... | collective-permute-start | bytes 393224 | tf_op jit(solution)/shard_map/ppermute | solution.py:241
  45.0 10.9 %collective-permute-start.15 = (bf16[8,16,512]{2,1,0:T(8,128)(2,1)S(1)}, bf16[8,16,512]{2,1,0:T(8,128)(2,1)S(1)}, u32[]{:S(2)}, u32[]{:S(2)}) collective-permute-start(bf16[8,16,512]{2,1,0:T(8,128)(2,1)S(1)} %get-tuple-element.111), channel_id=1, source_target_pairs={{0,8},{4,12},{8,0},{12,4},{1,9},{5,13},{9,1},{13,5},{2,10},{6,14},... | collective-permute-start | bytes 393224 | tf_op jit(solution)/shard_map/ppermute | solution.py:241
  49.3 6.7 %collective-permute-start.16 = (bf16[8,16,512]{2,1,0:T(8,128)(2,1)S(1)}, bf16[8,16,512]{2,1,0:T(8,128)(2,1)S(1)}, u32[]{:S(2)}, u32[]{:S(2)}) collective-permute-start(bf16[8,16,512]{2,1,0:T(8,128)(2,1)S(1)} %get-tuple-element.112), channel_id=1, source_target_pairs={{0,4},{4,0},{8,12},{12,8},{1,5},{5,1},{9,13},{13,9},{2,6},{6,2},{1... | collective-permute-start | bytes 393224 | tf_op jit(solution)/shard_map/ppermute | solution.py:241
  53.0 3.0 %collective-permute-start.18 = (bf16[24,32,512]{2,1,0:T(8,128)(2,1)S(1)}, bf16[24,32,512]{2,1,0:T(8,128)(2,1)S(1)}, u32[]{:S(2)}, u32[]{:S(2)}) collective-permute-start(bf16[24,32,512]{2,1,0:T(8,128)(2,1)S(1)} %shard_map.76), channel_id=1, source_target_pairs={{0,1},{1,0},{2,3},{3,2},{4,5},{5,4},{6,7},{7,6},{8,9},{9,8},{10,11... | collective-permute-start | bytes 2359304 | tf_op jit(solution)/shard_map/ppermute | solution.py:291
  57.8 9.8 %collective-permute-start.21 = (bf16[8,32,512]{2,1,0:T(8,128)(2,1)S(1)}, bf16[8,32,512]{2,1,0:T(8,128)(2,1)S(1)}, u32[]{:S(2)}, u32[]{:S(2)}) collective-permute-start(bf16[8,32,512]{2,1,0:T(8,128)(2,1)S(1)} %get-tuple-element.142), channel_id=1, source_target_pairs={{0,4},{4,8},{8,12},{12,0},{1,5},{5,9},{9,13},{13,1},{2,6},{6,10},{... | collective-permute-start | bytes 786440 | tf_op jit(solution)/shard_map/ppermute | solution.py:238
  59.6 21.6 %collective-permute-start.19 = (bf16[8,32,512]{2,1,0:T(8,128)(2,1)S(1)}, bf16[8,32,512]{2,1,0:T(8,128)(2,1)S(1)}, u32[]{:S(2)}, u32[]{:S(2)}) collective-permute-start(bf16[8,32,512]{2,1,0:T(8,128)(2,1)S(1)} %get-tuple-element.139), channel_id=1, source_target_pairs={{0,8},{4,12},{8,0},{12,4},{1,9},{5,13},{9,1},{13,5},{2,10},{6,14},... | collective-permute-start | bytes 786440 | tf_op jit(solution)/shard_map/ppermute | solution.py:238
  62.9 22.3 %collective-permute-start.20 = (bf16[8,32,512]{2,1,0:T(8,128)(2,1)S(1)}, bf16[8,32,512]{2,1,0:T(8,128)(2,1)S(1)}, u32[]{:S(2)}, u32[]{:S(2)}) collective-permute-start(bf16[8,32,512]{2,1,0:T(8,128)(2,1)S(1)} %get-tuple-element.140), channel_id=1, source_target_pairs={{0,12},{4,0},{8,4},{12,8},{1,13},{5,1},{9,5},{13,9},{2,14},{6,2},{... | collective-permute-start | bytes 786440 | tf_op jit(solution)/shard_map/ppermute | solution.py:238
  (2 other events, 10.4 us)

commit v22 on v19

--- a/solution.py
+++ b/solution.py
@@ -287,10 +287,10 @@
     first[3], first[2], first[1] = anchor([first[3], first[2], first[1]], 7_500_000_000)
     outs, first[3], first[2], first[1] = fence((restore(kept, came, ratios, up, spots), first[3], first[2], first[1]))
     first[0] = here
-    back = [swap_z(outs[j - 1], j) for j in (1, 2, 3)]
+    back = [swap_z(outs[j - 1], j) for j in (2, 3, 1)]
     result = place(where, [first[j] for j in (1, 2, 3, 0)], spots, 0, shape)
-    result = place(where, [outs[3], back[0]], [spots[3], spots[0]], ROWS, shape, into=result)
-    return place(where, back[1:], spots[1:3], ROWS, shape, into=result)
+    result = place(where, [outs[3]], [spots[3]], ROWS, shape, into=result)
+    return place(where, back, [spots[1], spots[2], spots[0]], ROWS, shape, into=result)
 
 
 def plain(visibility, beam_transfer, tile_mask, first_block, eigen_modes, signal_noise):

time: 86.3 us -> 85.3 us (0.988)
  waiting for transfers between devices: 30.4 us -> 28.4 us
    ppermute x6, waiting for transfers between devices: 22.3 us -> 20.4 us  [swap_z(): return lax.ppermute(value, 'fm', [(i, i ^ j) for i in range(parts)])]
  transfers between devices with their start and end apart: 22 -> 22, of which waited for: 8 -> 7; matrix products, arithmetic and copies ran while one was open for 2% -> 2% of each run, Pallas kernels for 26% -> 26%
where the time goes in v22:
time: 85.3 us; the launch traced here: 84.7 us
  waiting for transfers between devices  28.4 us (33%)
  starting transfers between devices  27.9 us (33%)
  Pallas kernels  25.1 us (29%)
  local copies, waits for them, and re-layouts  2.39 us (3%)
  between operations  0.92 us (1%)
    ppermute x6, waiting for transfers between devices, swap_z(): return lax.ppermute(value, 'fm', [(i, i ^ j) for i in range(parts)])  20.4 us
    ppermute x6, starting transfers between devices, swap_z(): return lax.ppermute(value, 'fm', [(i, i ^ j) for i in range(parts)])  10.5 us
    pallas_call x7, Pallas kernels, project(): pl.pallas_call(functools.partial(project_kernel, piece=piece, blocks=bloc...  9.57 us
    ppermute x8, starting transfers between devices, along_x(): return lax.ppermute(value, 'kl', other)  9.13 us
    ppermute x6, starting transfers between devices, shift_z(): lax.ppermute(value, 'fm', [(i, (i + j) % parts) for i in range(parts)])  8.2 us
    pallas_call x1, Pallas kernels, hold(): pl.pallas_call(hold_kernel, grid_spec=pltpu.PrefetchScalarGridSpec(num_sc...  7.04 us
    ppermute x8, waiting for transfers between devices, along_x(): return lax.ppermute(value, 'kl', other)  4.81 us
    pallas_call x3, Pallas kernels, place(): pl.pallas_call(functools.partial(place_kernel, spots=spots, first=first),...  4.06 us
  transfers between devices with their start and end apart: 22, of which 7 were waited for; matrix products, arithmetic and copies ran while one was open for 2% of the time, Pallas kernels for 26%

profile of v22, /device:TPU:12, one launch (start us, length us, event | category | flops | bytes accessed | tf_op | source)
XLA Modules:
  0.0 84.7 jit_solution(2218243800048134701)
XLA Ops:
  1.1 1.6 %collective-permute-start = (bf16[8,16,512]{2,1,0:T(8,128)(2,1)S(1)}, bf16[8,16,512]{2,1,0:T(8,128)(2,1)S(1)}, u32[]{:S(2)}, u32[]{:S(2)}) collective-permute-start(bf16[8,16,512]{2,1,0:T(8,128)(2,1)S(1)} %get-tuple-element.154), channel_id=1, source_target_pairs={{0,4},{4,8},{8,12},{12,0},{1,5},{5,9},{9,13},{13,1},{2,6},{6,10},{... | collective-permute-start | bytes 393224 | tf_op jit(solution)/shard_map/ppermute | solution.py:232
  3.2 2.6 %collective-permute-start.2 = (bf16[8,16,512]{2,1,0:T(8,128)(2,1)S(1)}, bf16[8,16,512]{2,1,0:T(8,128)(2,1)S(1)}, u32[]{:S(2)}, u32[]{:S(2)}) collective-permute-start(bf16[8,16,512]{2,1,0:T(8,128)(2,1)S(1)} %get-tuple-element.152), channel_id=1, source_target_pairs={{0,8},{4,12},{8,0},{12,4},{1,9},{5,13},{9,1},{13,5},{2,10},{6,14},... | collective-permute-start | bytes 393224 | tf_op jit(solution)/shard_map/ppermute | solution.py:232
  6.8 1.6 %collective-permute-start.3 = (bf16[4,48,512]{2,1,0:T(8,128)(2,1)S(1)}, bf16[4,48,512]{2,1,0:T(8,128)(2,1)S(1)}, u32[]{:S(2)}, u32[]{:S(2)}) collective-permute-start(bf16[4,48,512]{2,1,0:T(8,128)(2,1)S(1)} %get-tuple-element.148.refs_0_), channel_id=1, source_target_pairs={{0,2},{2,0},{1,3},{3,1},{4,6},{6,4},{5,7},{7,5},{8,10},{10,8},{9,1... | collective-permute-start | bytes 589832 | tf_op jit(solution)/shard_map/ppermute | solution.py:238
  9.7 7.0 %shard_map.64 = (bf16[32,512,512]{2,1,0:T(8,128)(2,1)S(1)}, bf16[384,512]{1,0:T(8,128)(2,1)S(1)}, bf16[512,384]{1,0:T(8,128)(2,1)S(1)}) custom-call(s32[10]{0:T(128)S(1)} %compare_select_fusion.4.where, s32[4,4]{1,0:T(4,128)S(1)} %bitcast.27, s32[1]{0:T(128)S(6)} %copy.24.starts, bf16[32,512,512]{2,1,0:T(8,128)(2,1)} %bitcast.28, bf16[32,24]{1,0:T(8,128)(2,1)S(1)} %bitcast.26), custom_call_target="tpu_custom_call" | custom-call | flops 1024 | bytes 1024 | tf_op jit(solution)/shard_map/pallas_call | solution.py:63
  19.0 1.5 %collective-permute-start.6 = (bf16[8,16,512]{2,1,0:T(8,128)(2,1)S(1)}, bf16[8,16,512]{2,1,0:T(8,128)(2,1)S(1)}, u32[]{:S(2)}, u32[]{:S(2)}) collective-permute-start(bf16[8,16,512]{2,1,0:T(8,128)(2,1)S(1)} %collective-permute-done.refs_0_), channel_id=1, source_target_pairs={{0,2},{2,0},{1,3},{3,1},{4,6},{6,4},{5,7},{7,5},{8,10},{10,8},{9,1... | collective-permute-start | bytes 393224 | tf_op jit(solution)/shard_map/ppermute | solution.py:238
  21.0 1.5 %collective-permute-start.8 = (bf16[8,16,512]{2,1,0:T(8,128)(2,1)S(1)}, bf16[8,16,512]{2,1,0:T(8,128)(2,1)S(1)}, u32[]{:S(2)}, u32[]{:S(2)}) collective-permute-start(bf16[8,16,512]{2,1,0:T(8,128)(2,1)S(1)} %collective-permute-done.1.refs_0_), channel_id=1, source_target_pairs={{0,2},{2,0},{1,3},{3,1},{4,6},{6,4},{5,7},{7,5},{8,10},{10,8},{9,1... | collective-permute-start | bytes 393224 | tf_op jit(solution)/shard_map/ppermute | solution.py:238
  22.5 1.4 %shard_map.65 = (bf16[8,48,512]{2,1,0:T(8,128)(2,1)S(1)}, bf16[8,48,512]{2,1,0:T(8,128)(2,1)S(1)}) custom-call(s32[10]{0:T(128)S(1)} %compare_select_fusion.4.where, bf16[4,48,512]{2,1,0:T(8,128)(2,1)S(1)} %get-tuple-element.148.refs_0_, bf16[4,48,512]{2,1,0:T(8,128)(2,1)S(1)} %get-tuple-element.147.refs_1_, ...), custom_call_target="tpu_custom_call" | custom-call | flops 400000000 | bytes 1024 | tf_op jit(solution)/shard_map/pallas_call | solution.py:102
  25.1 1.4 %shard_map.66 = (bf16[8,16,512]{2,1,0:T(8,128)(2,1)S(1)}, bf16[8,16,512]{2,1,0:T(8,128)(2,1)S(1)}) custom-call(s32[10]{0:T(128)S(1)} %compare_select_fusion.4.where, bf16[8,16,512]{2,1,0:T(8,128)(2,1)S(1)} %collective-permute-done.refs_0_, bf16[8,16,512]{2,1,0:T(8,128)(2,1)S(1)} %collective-permute-done.6.refs_1_, ...), custom_call_target="tpu_custom_call" | custom-call | flops 400000000 | bytes 1024 | tf_op jit(solution)/shard_map/pallas_call | solution.py:102
  26.5 1.4 %shard_map.67 = (bf16[8,16,512]{2,1,0:T(8,128)(2,1)S(1)}, bf16[8,16,512]{2,1,0:T(8,128)(2,1)S(1)}) custom-call(s32[10]{0:T(128)S(1)} %compare_select_fusion.4.where, bf16[8,16,512]{2,1,0:T(8,128)(2,1)S(1)} %collective-permute-done.2.refs_0_, bf16[8,16,512]{2,1,0:T(8,128)(2,1)S(1)} %collective-permute-done.7.refs_1_, ...), custom_call_target="tpu_custom_call" | custom-call | flops 400000000 | bytes 1024 | tf_op jit(solution)/shard_map/pallas_call | solution.py:102
  27.9 1.6 %collective-permute-start.13 = (bf16[8,32,512]{2,1,0:T(8,128)(2,1)S(1)}, bf16[8,32,512]{2,1,0:T(8,128)(2,1)S(1)}, u32[]{:S(2)}, u32[]{:S(2)}) collective-permute-start(bf16[8,32,512]{2,1,0:T(8,128)(2,1)S(1)} %collective-permute-done.10.refs_0_), channel_id=1, source_target_pairs={{0,2},{2,0},{1,3},{3,1},{4,6},{6,4},{5,7},{7,5},{8,10},{10,8},{9,1... | collective-permute-start | bytes 786440 | tf_op jit(solution)/shard_map/ppermute | solution.py:238
  31.2 1.4 %collective-permute-start.9 = (bf16[8,32,512]{2,1,0:T(8,128)(2,1)S(1)}, bf16[8,32,512]{2,1,0:T(8,128)(2,1)S(1)}, u32[]{:S(2)}, u32[]{:S(2)}) collective-permute-start(bf16[8,32,512]{2,1,0:T(8,128)(2,1)S(1)} %collective-permute-done.5.refs_0_), channel_id=1, source_target_pairs={{0,2},{2,0},{1,3},{3,1},{4,6},{6,4},{5,7},{7,5},{8,10},{10,8},{9,1... | collective-permute-start | bytes 786440 | tf_op jit(solution)/shard_map/ppermute | solution.py:238
  32.7 1.5 %collective-permute-start.11 = (bf16[8,32,512]{2,1,0:T(8,128)(2,1)S(1)}, bf16[8,32,512]{2,1,0:T(8,128)(2,1)S(1)}, u32[]{:S(2)}, u32[]{:S(2)}) collective-permute-start(bf16[8,32,512]{2,1,0:T(8,128)(2,1)S(1)} %get-tuple-element.98), channel_id=1, source_target_pairs={{0,8},{4,12},{8,0},{12,4},{1,9},{5,13},{9,1},{13,5},{2,10},{6,14},... | collective-permute-start | bytes 786440 | tf_op jit(solution)/shard_map/ppermute | solution.py:232
  34.2 3.0 %collective-permute-done.13.refs_0_ = bf16[8,32,512]{2,1,0:T(8,128)(2,1)S(1)} collective-permute-done((bf16[8,32,512]{2,1,0:T(8,128)(2,1)S(1)}, bf16[8,32,512]{2,1,0:T(8,128)(2,1)S(1)}, u32[]{:S(2)}, u32[]{:S(2)}) %collective-permute-start.13) | collective-permute-done | bytes 262176 | tf_op jit(solution)/shard_map/ppermute | solution.py:238
  37.5 1.4 %shard_map.73 = (bf16[8,32,512]{2,1,0:T(8,128)(2,1)S(1)}, bf16[8,32,512]{2,1,0:T(8,128)(2,1)S(1)}) custom-call(s32[10]{0:T(128)S(1)} %compare_select_fusion.4.where, bf16[8,32,512]{2,1,0:T(8,128)(2,1)S(1)} %collective-permute-done.10.refs_0_, bf16[8,32,512]{2,1,0:T(8,128)(2,1)S(1)} %shard_map.72.refs_1_, ...), custom_call_target="tpu_custom_call" | custom-call | flops 1024 | bytes 1024 | tf_op jit(solution)/shard_map/pallas_call | solution.py:102
  40.0 3.2 %collective-permute-done.11.refs_0_ = bf16[8,32,512]{2,1,0:T(8,128)(2,1)S(1)} collective-permute-done((bf16[8,32,512]{2,1,0:T(8,128)(2,1)S(1)}, bf16[8,32,512]{2,1,0:T(8,128)(2,1)S(1)}, u32[]{:S(2)}, u32[]{:S(2)}) %collective-permute-start.11) | collective-permute-done | bytes 262176 | tf_op jit(solution)/shard_map/ppermute | solution.py:232
  45.0 4.3 %collective-permute-start.15 = (bf16[8,16,512]{2,1,0:T(8,128)(2,1)S(1)}, bf16[8,16,512]{2,1,0:T(8,128)(2,1)S(1)}, u32[]{:S(2)}, u32[]{:S(2)}) collective-permute-start(bf16[8,16,512]{2,1,0:T(8,128)(2,1)S(1)} %get-tuple-element.111), channel_id=1, source_target_pairs={{0,8},{4,12},{8,0},{12,4},{1,9},{5,13},{9,1},{13,5},{2,10},{6,14},... | collective-permute-start | bytes 393224 | tf_op jit(solution)/shard_map/ppermute | solution.py:235
  49.3 1.4 %shard_map.75 = (bf16[8,32,512]{2,1,0:T(8,128)(2,1)S(1)}, bf16[8,32,512]{2,1,0:T(8,128)(2,1)S(1)}) custom-call(s32[10]{0:T(128)S(1)} %compare_select_fusion.4.where, bf16[8,32,512]{2,1,0:T(8,128)(2,1)S(1)} %collective-permute-done.5.refs_0_, bf16[8,32,512]{2,1,0:T(8,128)(2,1)S(1)} %collective-permute-done.9.refs_1_, ...), custom_call_target="tpu_custom_call" | custom-call | flops 1024 | bytes 1024 | tf_op jit(solution)/shard_map/pallas_call | solution.py:102
  50.7 1.4 %shard_map.74 = (bf16[8,32,512]{2,1,0:T(8,128)(2,1)S(1)}, bf16[8,32,512]{2,1,0:T(8,128)(2,1)S(1)}) custom-call(s32[10]{0:T(128)S(1)} %compare_select_fusion.4.where, bf16[8,32,512]{2,1,0:T(8,128)(2,1)S(1)} %collective-permute-done.11.refs_0_, bf16[8,32,512]{2,1,0:T(8,128)(2,1)S(1)} %collective-permute-done.17.refs_1_, ...), custom_call_target="tpu_custom_call" | custom-call | flops 1024 | bytes 1024 | tf_op jit(solution)/shard_map/pallas_call | solution.py:102
  54.0 1.9 %collective-permute-done.15.refs_1_ = bf16[8,16,512]{2,1,0:T(8,128)(2,1)S(1)} collective-permute-done((bf16[8,16,512]{2,1,0:T(8,128)(2,1)S(1)}, bf16[8,16,512]{2,1,0:T(8,128)(2,1)S(1)}, u32[]{:S(2)}, u32[]{:S(2)}) %collective-permute-start.15) | collective-permute-done | bytes 131104 | tf_op jit(solution)/shard_map/ppermute | solution.py:235
  57.2 3.4 %collective-permute-start.19 = (bf16[8,32,512]{2,1,0:T(8,128)(2,1)S(1)}, bf16[8,32,512]{2,1,0:T(8,128)(2,1)S(1)}, u32[]{:S(2)}, u32[]{:S(2)}) collective-permute-start(bf16[8,32,512]{2,1,0:T(8,128)(2,1)S(1)} %get-tuple-element.139), channel_id=1, source_target_pairs={{0,8},{4,12},{8,0},{12,4},{1,9},{5,13},{9,1},{13,5},{2,10},{6,14},... | collective-permute-start | bytes 786440 | tf_op jit(solution)/shard_map/ppermute | solution.py:235
  62.2 1.4 %shard_map.80.refs_1_ = bf16[8,4,48,512]{3,2,1,0:T(8,128)(2,1)} custom-call(s32[10]{0:T(128)S(1)} %compare_select_fusion.4.where, bf16[8,16,512]{2,1,0:T(8,128)(2,1)S(1)} %get-tuple-element.143.refs_0_, bf16[8,16,512]{2,1,0:T(8,128)(2,1)S(1)} %get-tuple-element.144.refs_1_, bf16[8,16,512]{2,1,0:T(8,128)(2,1)S(1)} %get-tuple-element.145.refs_2_, ...), custom_call_target="tpu_custom_call" | custom-call | flops 1024 | bytes 1024 | tf_op jit(solution)/shard_map/pallas_call | solution.py:190
  64.8 12.0 %collective-permute-done.19.refs_0_ = bf16[8,32,512]{2,1,0:T(8,128)(2,1)S(1)} collective-permute-done((bf16[8,32,512]{2,1,0:T(8,128)(2,1)S(1)}, bf16[8,32,512]{2,1,0:T(8,128)(2,1)S(1)}, u32[]{:S(2)}, u32[]{:S(2)}) %collective-permute-start.19) | collective-permute-done | bytes 262176 | tf_op jit(solution)/shard_map/ppermute | solution.py:235
  76.9 6.4 %collective-permute-done.20.refs_1_ = bf16[8,32,512]{2,1,0:T(8,128)(2,1)S(1)} collective-permute-done((bf16[8,32,512]{2,1,0:T(8,128)(2,1)S(1)}, bf16[8,32,512]{2,1,0:T(8,128)(2,1)S(1)}, u32[]{:S(2)}, u32[]{:S(2)}) %collective-permute-start.20) | collective-permute-done | bytes 262176 | tf_op jit(solution)/shard_map/ppermute | solution.py:235
  83.3 1.4 %shard_map.82 = bf16[8,4,48,512]{3,2,1,0:T(8,128)(2,1)} custom-call(s32[10]{0:T(128)S(1)} %compare_select_fusion.4.where, bf16[8,32,512]{2,1,0:T(8,128)(2,1)S(1)} %collective-permute-done.19.refs_0_, bf16[8,32,512]{2,1,0:T(8,128)(2,1)S(1)} %collective-permute-done.20.refs_1_, ...), custom_call_target="tpu_custom_call", output_to_operand_aliasing={{}: (4, {})} | custom-call | flops 1024 | bytes 1024 | tf_op jit(solution)/shard_map/pallas_call | solution.py:190
  (54 shorter events, 18.3 us)
Async XLA Ops:
  0.0 9.6 %copy-start.2 = (bf16[1,32,24]{1,2,0:T(8,128)(2,1)S(1)}, bf16[1,32,24]{1,2,0:T(8,128)(2,1)}, u32[]{:S(2)}) copy-start(bf16[1,32,24]{1,2,0:T(8,128)(2,1)} %param.10) | copy-start | bytes 4612
  0.0 9.7 %copy-start = (s32[1,4,4]{2,1,0:T(4,128)S(1)}, s32[1,4,4]{2,1,0:T(4,128)}, u32[]{:S(2)}) copy-start(s32[1,4,4]{2,1,0:T(4,128)} %param.8) | copy-start | bytes 196
  1.1 15.7 %collective-permute-start = (bf16[8,16,512]{2,1,0:T(8,128)(2,1)S(1)}, bf16[8,16,512]{2,1,0:T(8,128)(2,1)S(1)}, u32[]{:S(2)}, u32[]{:S(2)}) collective-permute-start(bf16[8,16,512]{2,1,0:T(8,128)(2,1)S(1)} %get-tuple-element.154), channel_id=1, source_target_pairs={{0,4},{4,8},{8,12},{12,0},{1,5},{5,9},{9,13},{13,1},{2,6},{6,10},{... | collective-permute-start | bytes 393224 | tf_op jit(solution)/shard_map/ppermute | solution.py:232
  2.7 14.1 %collective-permute-start.1 = (bf16[8,16,512]{2,1,0:T(8,128)(2,1)S(1)}, bf16[8,16,512]{2,1,0:T(8,128)(2,1)S(1)}, u32[]{:S(2)}, u32[]{:S(2)}) collective-permute-start(bf16[8,16,512]{2,1,0:T(8,128)(2,1)S(1)} %get-tuple-element.153), channel_id=1, source_target_pairs={{0,12},{4,0},{8,4},{12,8},{1,13},{5,1},{9,5},{13,9},{2,14},{6,2},{... | collective-permute-start | bytes 393224 | tf_op jit(solution)/shard_map/ppermute | solution.py:232
  3.2 13.7 %collective-permute-start.2 = (bf16[8,16,512]{2,1,0:T(8,128)(2,1)S(1)}, bf16[8,16,512]{2,1,0:T(8,128)(2,1)S(1)}, u32[]{:S(2)}, u32[]{:S(2)}) collective-permute-start(bf16[8,16,512]{2,1,0:T(8,128)(2,1)S(1)} %get-tuple-element.152), channel_id=1, source_target_pairs={{0,8},{4,12},{8,0},{12,4},{1,9},{5,13},{9,1},{13,5},{2,10},{6,14},... | collective-permute-start | bytes 393224 | tf_op jit(solution)/shard_map/ppermute | solution.py:232
  6.8 10.0 %collective-permute-start.3 = (bf16[4,48,512]{2,1,0:T(8,128)(2,1)S(1)}, bf16[4,48,512]{2,1,0:T(8,128)(2,1)S(1)}, u32[]{:S(2)}, u32[]{:S(2)}) collective-permute-start(bf16[4,48,512]{2,1,0:T(8,128)(2,1)S(1)} %get-tuple-element.148.refs_0_), channel_id=1, source_target_pairs={{0,2},{2,0},{1,3},{3,1},{4,6},{6,4},{5,7},{7,5},{8,10},{10,8},{9,1... | collective-permute-start | bytes 589832 | tf_op jit(solution)/shard_map/ppermute | solution.py:238
  8.4 8.5 %collective-permute-start.4 = (bf16[4,48,512]{2,1,0:T(8,128)(2,1)S(1)}, bf16[4,48,512]{2,1,0:T(8,128)(2,1)S(1)}, u32[]{:S(2)}, u32[]{:S(2)}) collective-permute-start(bf16[4,48,512]{2,1,0:T(8,128)(2,1)S(1)} %get-tuple-element.147.refs_1_), channel_id=1, source_target_pairs={{0,2},{2,0},{1,3},{3,1},{4,6},{6,4},{5,7},{7,5},{8,10},{10,8},{9,1... | collective-permute-start | bytes 589832 | tf_op jit(solution)/shard_map/ppermute | solution.py:238
  16.9 11.0 %collective-permute-start.10 = (bf16[8,32,512]{2,1,0:T(8,128)(2,1)S(1)}, bf16[8,32,512]{2,1,0:T(8,128)(2,1)S(1)}, u32[]{:S(2)}, u32[]{:S(2)}) collective-permute-start(bf16[8,32,512]{2,1,0:T(8,128)(2,1)S(1)} %get-tuple-element.97), channel_id=1, source_target_pairs={{0,4},{4,8},{8,12},{12,0},{1,5},{5,9},{9,13},{13,1},{2,6},{6,10},{... | collective-permute-start | bytes 786440 | tf_op jit(solution)/shard_map/ppermute | solution.py:232
  18.1 13.1 %collective-permute-start.5 = (bf16[8,32,512]{2,1,0:T(8,128)(2,1)S(1)}, bf16[8,32,512]{2,1,0:T(8,128)(2,1)S(1)}, u32[]{:S(2)}, u32[]{:S(2)}) collective-permute-start(bf16[8,32,512]{2,1,0:T(8,128)(2,1)S(1)} %get-tuple-element.79), channel_id=1, source_target_pairs={{0,12},{4,0},{8,4},{12,8},{1,13},{5,1},{9,5},{13,9},{2,14},{6,2},{... | collective-permute-start | bytes 786440 | tf_op jit(solution)/shard_map/ppermute | solution.py:232
  19.0 6.2 %collective-permute-start.6 = (bf16[8,16,512]{2,1,0:T(8,128)(2,1)S(1)}, bf16[8,16,512]{2,1,0:T(8,128)(2,1)S(1)}, u32[]{:S(2)}, u32[]{:S(2)}) collective-permute-start(bf16[8,16,512]{2,1,0:T(8,128)(2,1)S(1)} %collective-permute-done.refs_0_), channel_id=1, source_target_pairs={{0,2},{2,0},{1,3},{3,1},{4,6},{6,4},{5,7},{7,5},{8,10},{10,8},{9,1... | collective-permute-start | bytes 393224 | tf_op jit(solution)/shard_map/ppermute | solution.py:238
  20.5 6.1 %collective-permute-start.7 = (bf16[8,16,512]{2,1,0:T(8,128)(2,1)S(1)}, bf16[8,16,512]{2,1,0:T(8,128)(2,1)S(1)}, u32[]{:S(2)}, u32[]{:S(2)}) collective-permute-start(bf16[8,16,512]{2,1,0:T(8,128)(2,1)S(1)} %collective-permute-done.2.refs_0_), channel_id=1, source_target_pairs={{0,2},{2,0},{1,3},{3,1},{4,6},{6,4},{5,7},{7,5},{8,10},{10,8},{9,1... | collective-permute-start | bytes 393224 | tf_op jit(solution)/shard_map/ppermute | solution.py:238
  21.0 8.5 %collective-permute-start.8 = (bf16[8,16,512]{2,1,0:T(8,128)(2,1)S(1)}, bf16[8,16,512]{2,1,0:T(8,128)(2,1)S(1)}, u32[]{:S(2)}, u32[]{:S(2)}) collective-permute-start(bf16[8,16,512]{2,1,0:T(8,128)(2,1)S(1)} %collective-permute-done.1.refs_0_), channel_id=1, source_target_pairs={{0,2},{2,0},{1,3},{3,1},{4,6},{6,4},{5,7},{7,5},{8,10},{10,8},{9,1... | collective-permute-start | bytes 393224 | tf_op jit(solution)/shard_map/ppermute | solution.py:238
  27.9 9.2 %collective-permute-start.13 = (bf16[8,32,512]{2,1,0:T(8,128)(2,1)S(1)}, bf16[8,32,512]{2,1,0:T(8,128)(2,1)S(1)}, u32[]{:S(2)}, u32[]{:S(2)}) collective-permute-start(bf16[8,32,512]{2,1,0:T(8,128)(2,1)S(1)} %collective-permute-done.10.refs_0_), channel_id=1, source_target_pairs={{0,2},{2,0},{1,3},{3,1},{4,6},{6,4},{5,7},{7,5},{8,10},{10,8},{9,1... | collective-permute-start | bytes 786440 | tf_op jit(solution)/shard_map/ppermute | solution.py:238
  31.2 8.7 %collective-permute-start.9 = (bf16[8,32,512]{2,1,0:T(8,128)(2,1)S(1)}, bf16[8,32,512]{2,1,0:T(8,128)(2,1)S(1)}, u32[]{:S(2)}, u32[]{:S(2)}) collective-permute-start(bf16[8,32,512]{2,1,0:T(8,128)(2,1)S(1)} %collective-permute-done.5.refs_0_), channel_id=1, source_target_pairs={{0,2},{2,0},{1,3},{3,1},{4,6},{6,4},{5,7},{7,5},{8,10},{10,8},{9,1... | collective-permute-start | bytes 786440 | tf_op jit(solution)/shard_map/ppermute | solution.py:238
  32.7 10.5 %collective-permute-start.11 = (bf16[8,32,512]{2,1,0:T(8,128)(2,1)S(1)}, bf16[8,32,512]{2,1,0:T(8,128)(2,1)S(1)}, u32[]{:S(2)}, u32[]{:S(2)}) collective-permute-start(bf16[8,32,512]{2,1,0:T(8,128)(2,1)S(1)} %get-tuple-element.98), channel_id=1, source_target_pairs={{0,8},{4,12},{8,0},{12,4},{1,9},{5,13},{9,1},{13,5},{2,10},{6,14},... | collective-permute-start | bytes 786440 | tf_op jit(solution)/shard_map/ppermute | solution.py:232
  34.1 4.8 %collective-permute-start.12 = (bf16[24,16,512]{2,1,0:T(8,128)(2,1)S(1)}, bf16[24,16,512]{2,1,0:T(8,128)(2,1)S(1)}, u32[]{:S(2)}, u32[]{:S(2)}) collective-permute-start(bf16[24,16,512]{2,1,0:T(8,128)(2,1)S(1)} %shard_map.69), channel_id=1, source_target_pairs={{0,1},{1,0},{2,3},{3,2},{4,5},{5,4},{6,7},{7,6},{8,9},{9,8},{10,11... | collective-permute-start | bytes 1179656 | tf_op jit(solution)/shard_map/ppermute | solution.py:273
  43.2 7.5 %collective-permute-start.17 = (bf16[8,32,512]{2,1,0:T(8,128)(2,1)S(1)}, bf16[8,32,512]{2,1,0:T(8,128)(2,1)S(1)}, u32[]{:S(2)}, u32[]{:S(2)}) collective-permute-start(bf16[8,32,512]{2,1,0:T(8,128)(2,1)S(1)} %collective-permute-done.11.refs_0_), channel_id=1, source_target_pairs={{0,2},{2,0},{1,3},{3,1},{4,6},{6,4},{5,7},{7,5},{8,10},{10,8},{9,1... | collective-permute-start | bytes 786440 | tf_op jit(solution)/shard_map/ppermute | solution.py:238
  43.7 10.3 %collective-permute-start.14 = (bf16[8,16,512]{2,1,0:T(8,128)(2,1)S(1)}, bf16[8,16,512]{2,1,0:T(8,128)(2,1)S(1)}, u32[]{:S(2)}, u32[]{:S(2)}) collective-permute-start(bf16[8,16,512]{2,1,0:T(8,128)(2,1)S(1)} %get-tuple-element.110), channel_id=1, source_target_pairs={{0,12},{4,8},{8,4},{12,0},{1,13},{5,9},{9,5},{13,1},{2,14},{6,10},... | collective-permute-start | bytes 393224 | tf_op jit(solution)/shard_map/ppermute | solution.py:235
  45.0 10.9 %collective-permute-start.15 = (bf16[8,16,512]{2,1,0:T(8,128)(2,1)S(1)}, bf16[8,16,512]{2,1,0:T(8,128)(2,1)S(1)}, u32[]{:S(2)}, u32[]{:S(2)}) collective-permute-start(bf16[8,16,512]{2,1,0:T(8,128)(2,1)S(1)} %get-tuple-element.111), channel_id=1, source_target_pairs={{0,8},{4,12},{8,0},{12,4},{1,9},{5,13},{9,1},{13,5},{2,10},{6,14},... | collective-permute-start | bytes 393224 | tf_op jit(solution)/shard_map/ppermute | solution.py:235
  49.3 6.7 %collective-permute-start.16 = (bf16[8,16,512]{2,1,0:T(8,128)(2,1)S(1)}, bf16[8,16,512]{2,1,0:T(8,128)(2,1)S(1)}, u32[]{:S(2)}, u32[]{:S(2)}) collective-permute-start(bf16[8,16,512]{2,1,0:T(8,128)(2,1)S(1)} %get-tuple-element.112), channel_id=1, source_target_pairs={{0,4},{4,0},{8,12},{12,8},{1,5},{5,1},{9,13},{13,9},{2,6},{6,2},{1... | collective-permute-start | bytes 393224 | tf_op jit(solution)/shard_map/ppermute | solution.py:235
  53.0 3.0 %collective-permute-start.18 = (bf16[24,32,512]{2,1,0:T(8,128)(2,1)S(1)}, bf16[24,32,512]{2,1,0:T(8,128)(2,1)S(1)}, u32[]{:S(2)}, u32[]{:S(2)}) collective-permute-start(bf16[24,32,512]{2,1,0:T(8,128)(2,1)S(1)} %shard_map.76), channel_id=1, source_target_pairs={{0,1},{1,0},{2,3},{3,2},{4,5},{5,4},{6,7},{7,6},{8,9},{9,8},{10,11... | collective-permute-start | bytes 2359304 | tf_op jit(solution)/shard_map/ppermute | solution.py:284
  57.2 19.6 %collective-permute-start.19 = (bf16[8,32,512]{2,1,0:T(8,128)(2,1)S(1)}, bf16[8,32,512]{2,1,0:T(8,128)(2,1)S(1)}, u32[]{:S(2)}, u32[]{:S(2)}) collective-permute-start(bf16[8,32,512]{2,1,0:T(8,128)(2,1)S(1)} %get-tuple-element.139), channel_id=1, source_target_pairs={{0,8},{4,12},{8,0},{12,4},{1,9},{5,13},{9,1},{13,5},{2,10},{6,14},... | collective-permute-start | bytes 786440 | tf_op jit(solution)/shard_map/ppermute | solution.py:235
  60.7 22.6 %collective-permute-start.20 = (bf16[8,32,512]{2,1,0:T(8,128)(2,1)S(1)}, bf16[8,32,512]{2,1,0:T(8,128)(2,1)S(1)}, u32[]{:S(2)}, u32[]{:S(2)}) collective-permute-start(bf16[8,32,512]{2,1,0:T(8,128)(2,1)S(1)} %get-tuple-element.140), channel_id=1, source_target_pairs={{0,12},{4,8},{8,4},{12,0},{1,13},{5,9},{9,5},{13,1},{2,14},{6,10},... | collective-permute-start | bytes 786440 | tf_op jit(solution)/shard_map/ppermute | solution.py:235
  61.4 21.8 %collective-permute-start.21 = (bf16[8,32,512]{2,1,0:T(8,128)(2,1)S(1)}, bf16[8,32,512]{2,1,0:T(8,128)(2,1)S(1)}, u32[]{:S(2)}, u32[]{:S(2)}) collective-permute-start(bf16[8,32,512]{2,1,0:T(8,128)(2,1)S(1)} %get-tuple-element.141), channel_id=1, source_target_pairs={{0,4},{4,0},{8,12},{12,8},{1,5},{5,1},{9,13},{13,9},{2,6},{6,2},{1... | collective-permute-start | bytes 786440 | tf_op jit(solution)/shard_map/ppermute | solution.py:235
  (2 other events, 10.4 us)

commit v23 on v22

--- a/solution.py
+++ b/solution.py
@@ -253,12 +253,12 @@
     most, half = rows_all - ROWS, freqs // 2
     blocks = [[(0, f)] for f in range(freqs)]
     halves = [[(f // half, f % half)] for f in range(freqs)]
-    a = {j: shift_z(cut(j, 0, ROWS), j) for j in (1, 3, 2)}
+    a = {j: shift_z(cut(j, 0, ROWS), j) for j in (2, 1, 3)}
     mine = [cut(0, 0, rows_all)[n:n + half] for n in (0, half)]
     others = [along_x(part) for part in mine]
     b = {j: cut(j, ROWS, most) for j in (1, 2, 3)}
     held, down, up = hold(where, tile_mask[0], first_block, beam, eigen_modes[0])
-    (a[1], a[3], a[2]), b, others, down, up = fence(((a[1], a[3], a[2]), b, others, down, up))
+    (a[2], a[1], a[3]), b, others, down, up = fence(((a[2], a[1], a[3]), b, others, down, up))
     b[1], b[3] = shift_z(b[1], 1), shift_z(b[3], 3)
     own = project(where, mine, others, held, 0, halves, 400_000_000)
     skies = [own] + [project(where, [a[j]], [along_x(a[j])], held, j, blocks, 400_000_000) for j in (1, 2, 3)]

time: 85.3 us -> 85.1 us (level)
  starting transfers between devices: 27.9 us -> 29.5 us
  waiting for transfers between devices: 28.4 us -> 26.8 us
    ppermute x6, starting transfers between devices: 8.2 us -> 9.34 us  [shift_z(): lax.ppermute(value, 'fm', [(i, (i + j) % parts) for i in range(parts)])]
where the time goes in v23:
time: 85.1 us; the launch traced here: 84.7 us
  starting transfers between devices  29.5 us (35%)
  waiting for transfers between devices  26.8 us (31%)
  Pallas kernels  25.1 us (29%)
  local copies, waits for them, and re-layouts  2.39 us (3%)
  between operations  0.92 us (1%)
    ppermute x6, waiting for transfers between devices, swap_z(): return lax.ppermute(value, 'fm', [(i, i ^ j) for i in range(parts)])  20.2 us
    ppermute x6, starting transfers between devices, swap_z(): return lax.ppermute(value, 'fm', [(i, i ^ j) for i in range(parts)])  11 us
    pallas_call x7, Pallas kernels, project(): pl.pallas_call(functools.partial(project_kernel, piece=piece, blocks=bloc...  9.57 us
    ppermute x6, starting transfers between devices, shift_z(): lax.ppermute(value, 'fm', [(i, (i + j) % parts) for i in range(parts)])  9.34 us
    ppermute x8, starting transfers between devices, along_x(): return lax.ppermute(value, 'kl', other)  9.13 us
    pallas_call x1, Pallas kernels, hold(): pl.pallas_call(hold_kernel, grid_spec=pltpu.PrefetchScalarGridSpec(num_sc...  7.04 us
    ppermute x8, waiting for transfers between devices, along_x(): return lax.ppermute(value, 'kl', other)  4.17 us
    pallas_call x3, Pallas kernels, place(): pl.pallas_call(functools.partial(place_kernel, spots=spots, first=first),...  4.06 us
  transfers between devices with their start and end apart: 22, of which 7 were waited for; matrix products, arithmetic and copies ran while one was open for 2% of the time, Pallas kernels for 26%

profile of v23, /device:TPU:12, one launch (start us, length us, event | category | flops | bytes accessed | tf_op | source)
XLA Modules:
  0.0 84.7 jit_solution(11515046984891731043)
XLA Ops:
  1.1 2.7 %collective-permute-start = (bf16[8,16,512]{2,1,0:T(8,128)(2,1)S(1)}, bf16[8,16,512]{2,1,0:T(8,128)(2,1)S(1)}, u32[]{:S(2)}, u32[]{:S(2)}) collective-permute-start(bf16[8,16,512]{2,1,0:T(8,128)(2,1)S(1)} %get-tuple-element.154), channel_id=1, source_target_pairs={{0,8},{4,12},{8,0},{12,4},{1,9},{5,13},{9,1},{13,5},{2,10},{6,14},... | collective-permute-start | bytes 393224 | tf_op jit(solution)/shard_map/ppermute | solution.py:232
  3.8 2.0 %collective-permute-start.2 = (bf16[8,16,512]{2,1,0:T(8,128)(2,1)S(1)}, bf16[8,16,512]{2,1,0:T(8,128)(2,1)S(1)}, u32[]{:S(2)}, u32[]{:S(2)}) collective-permute-start(bf16[8,16,512]{2,1,0:T(8,128)(2,1)S(1)} %get-tuple-element.152), channel_id=1, source_target_pairs={{0,12},{4,0},{8,4},{12,8},{1,13},{5,1},{9,5},{13,9},{2,14},{6,2},{... | collective-permute-start | bytes 393224 | tf_op jit(solution)/shard_map/ppermute | solution.py:232
  6.8 1.6 %collective-permute-start.3 = (bf16[4,48,512]{2,1,0:T(8,128)(2,1)S(1)}, bf16[4,48,512]{2,1,0:T(8,128)(2,1)S(1)}, u32[]{:S(2)}, u32[]{:S(2)}) collective-permute-start(bf16[4,48,512]{2,1,0:T(8,128)(2,1)S(1)} %get-tuple-element.148.refs_0_), channel_id=1, source_target_pairs={{0,2},{2,0},{1,3},{3,1},{4,6},{6,4},{5,7},{7,5},{8,10},{10,8},{9,1... | collective-permute-start | bytes 589832 | tf_op jit(solution)/shard_map/ppermute | solution.py:238
  9.7 7.0 %shard_map.64 = (bf16[32,512,512]{2,1,0:T(8,128)(2,1)S(1)}, bf16[384,512]{1,0:T(8,128)(2,1)S(1)}, bf16[512,384]{1,0:T(8,128)(2,1)S(1)}) custom-call(s32[10]{0:T(128)S(1)} %compare_select_fusion.4.where, s32[4,4]{1,0:T(4,128)S(1)} %bitcast.27, s32[1]{0:T(128)S(6)} %copy.24.starts, bf16[32,512,512]{2,1,0:T(8,128)(2,1)} %bitcast.28, bf16[32,24]{1,0:T(8,128)(2,1)S(1)} %bitcast.26), custom_call_target="tpu_custom_call" | custom-call | flops 1024 | bytes 1024 | tf_op jit(solution)/shard_map/pallas_call | solution.py:63
  17.4 1.9 %collective-permute-start.5 = (bf16[8,32,512]{2,1,0:T(8,128)(2,1)S(1)}, bf16[8,32,512]{2,1,0:T(8,128)(2,1)S(1)}, u32[]{:S(2)}, u32[]{:S(2)}) collective-permute-start(bf16[8,32,512]{2,1,0:T(8,128)(2,1)S(1)} %get-tuple-element.79), channel_id=1, source_target_pairs={{0,12},{4,0},{8,4},{12,8},{1,13},{5,1},{9,5},{13,9},{2,14},{6,2},{... | collective-permute-start | bytes 786440 | tf_op jit(solution)/shard_map/ppermute | solution.py:232
  19.3 1.5 %collective-permute-start.6 = (bf16[8,16,512]{2,1,0:T(8,128)(2,1)S(1)}, bf16[8,16,512]{2,1,0:T(8,128)(2,1)S(1)}, u32[]{:S(2)}, u32[]{:S(2)}) collective-permute-start(bf16[8,16,512]{2,1,0:T(8,128)(2,1)S(1)} %collective-permute-done.1.refs_0_), channel_id=1, source_target_pairs={{0,2},{2,0},{1,3},{3,1},{4,6},{6,4},{5,7},{7,5},{8,10},{10,8},{9,1... | collective-permute-start | bytes 393224 | tf_op jit(solution)/shard_map/ppermute | solution.py:238
  21.3 1.5 %collective-permute-start.8 = (bf16[8,16,512]{2,1,0:T(8,128)(2,1)S(1)}, bf16[8,16,512]{2,1,0:T(8,128)(2,1)S(1)}, u32[]{:S(2)}, u32[]{:S(2)}) collective-permute-start(bf16[8,16,512]{2,1,0:T(8,128)(2,1)S(1)} %collective-permute-done.2.refs_0_), channel_id=1, source_target_pairs={{0,2},{2,0},{1,3},{3,1},{4,6},{6,4},{5,7},{7,5},{8,10},{10,8},{9,1... | collective-permute-start | bytes 393224 | tf_op jit(solution)/shard_map/ppermute | solution.py:238
  24.1 1.5 %collective-permute-done.6.refs_1_ = bf16[8,16,512]{2,1,0:T(8,128)(2,1)S(1)} collective-permute-done((bf16[8,16,512]{2,1,0:T(8,128)(2,1)S(1)}, bf16[8,16,512]{2,1,0:T(8,128)(2,1)S(1)}, u32[]{:S(2)}, u32[]{:S(2)}) %collective-permute-start.6) | collective-permute-done | bytes 131104 | tf_op jit(solution)/shard_map/ppermute | solution.py:238
  28.4 1.6 %collective-permute-start.13 = (bf16[8,32,512]{2,1,0:T(8,128)(2,1)S(1)}, bf16[8,32,512]{2,1,0:T(8,128)(2,1)S(1)}, u32[]{:S(2)}, u32[]{:S(2)}) collective-permute-start(bf16[8,32,512]{2,1,0:T(8,128)(2,1)S(1)} %collective-permute-done.10.refs_0_), channel_id=1, source_target_pairs={{0,2},{2,0},{1,3},{3,1},{4,6},{6,4},{5,7},{7,5},{8,10},{10,8},{9,1... | collective-permute-start | bytes 786440 | tf_op jit(solution)/shard_map/ppermute | solution.py:238
  31.7 1.4 %collective-permute-start.9 = (bf16[8,32,512]{2,1,0:T(8,128)(2,1)S(1)}, bf16[8,32,512]{2,1,0:T(8,128)(2,1)S(1)}, u32[]{:S(2)}, u32[]{:S(2)}) collective-permute-start(bf16[8,32,512]{2,1,0:T(8,128)(2,1)S(1)} %collective-permute-done.5.refs_0_), channel_id=1, source_target_pairs={{0,2},{2,0},{1,3},{3,1},{4,6},{6,4},{5,7},{7,5},{8,10},{10,8},{9,1... | collective-permute-start | bytes 786440 | tf_op jit(solution)/shard_map/ppermute | solution.py:238
  33.2 2.3 %collective-permute-start.11 = (bf16[8,32,512]{2,1,0:T(8,128)(2,1)S(1)}, bf16[8,32,512]{2,1,0:T(8,128)(2,1)S(1)}, u32[]{:S(2)}, u32[]{:S(2)}) collective-permute-start(bf16[8,32,512]{2,1,0:T(8,128)(2,1)S(1)} %get-tuple-element.98), channel_id=1, source_target_pairs={{0,8},{4,12},{8,0},{12,4},{1,9},{5,13},{9,1},{13,5},{2,10},{6,14},... | collective-permute-start | bytes 786440 | tf_op jit(solution)/shard_map/ppermute | solution.py:232
  35.5 1.6 %collective-permute-done.13.refs_0_ = bf16[8,32,512]{2,1,0:T(8,128)(2,1)S(1)} collective-permute-done((bf16[8,32,512]{2,1,0:T(8,128)(2,1)S(1)}, bf16[8,32,512]{2,1,0:T(8,128)(2,1)S(1)}, u32[]{:S(2)}, u32[]{:S(2)}) %collective-permute-start.13) | collective-permute-done | bytes 262176 | tf_op jit(solution)/shard_map/ppermute | solution.py:238
  37.5 1.4 %shard_map.73 = (bf16[8,32,512]{2,1,0:T(8,128)(2,1)S(1)}, bf16[8,32,512]{2,1,0:T(8,128)(2,1)S(1)}) custom-call(s32[10]{0:T(128)S(1)} %compare_select_fusion.4.where, bf16[8,32,512]{2,1,0:T(8,128)(2,1)S(1)} %collective-permute-done.10.refs_0_, bf16[8,32,512]{2,1,0:T(8,128)(2,1)S(1)} %shard_map.72.refs_1_, ...), custom_call_target="tpu_custom_call" | custom-call | flops 1024 | bytes 1024 | tf_op jit(solution)/shard_map/pallas_call | solution.py:102
  40.5 2.4 %collective-permute-done.11.refs_0_ = bf16[8,32,512]{2,1,0:T(8,128)(2,1)S(1)} collective-permute-done((bf16[8,32,512]{2,1,0:T(8,128)(2,1)S(1)}, bf16[8,32,512]{2,1,0:T(8,128)(2,1)S(1)}, u32[]{:S(2)}, u32[]{:S(2)}) %collective-permute-start.11) | collective-permute-done | bytes 262176 | tf_op jit(solution)/shard_map/ppermute | solution.py:232
  43.4 2.0 %collective-permute-start.14 = (bf16[8,16,512]{2,1,0:T(8,128)(2,1)S(1)}, bf16[8,16,512]{2,1,0:T(8,128)(2,1)S(1)}, u32[]{:S(2)}, u32[]{:S(2)}) collective-permute-start(bf16[8,16,512]{2,1,0:T(8,128)(2,1)S(1)} %get-tuple-element.110), channel_id=1, source_target_pairs={{0,12},{4,8},{8,4},{12,0},{1,13},{5,9},{9,5},{13,1},{2,14},{6,10},... | collective-permute-start | bytes 393224 | tf_op jit(solution)/shard_map/ppermute | solution.py:235
  45.5 4.3 %collective-permute-start.15 = (bf16[8,16,512]{2,1,0:T(8,128)(2,1)S(1)}, bf16[8,16,512]{2,1,0:T(8,128)(2,1)S(1)}, u32[]{:S(2)}, u32[]{:S(2)}) collective-permute-start(bf16[8,16,512]{2,1,0:T(8,128)(2,1)S(1)} %get-tuple-element.111), channel_id=1, source_target_pairs={{0,8},{4,12},{8,0},{12,4},{1,9},{5,13},{9,1},{13,5},{2,10},{6,14},... | collective-permute-start | bytes 393224 | tf_op jit(solution)/shard_map/ppermute | solution.py:235
  49.7 1.4 %shard_map.75 = (bf16[8,32,512]{2,1,0:T(8,128)(2,1)S(1)}, bf16[8,32,512]{2,1,0:T(8,128)(2,1)S(1)}) custom-call(s32[10]{0:T(128)S(1)} %compare_select_fusion.4.where, bf16[8,32,512]{2,1,0:T(8,128)(2,1)S(1)} %collective-permute-done.5.refs_0_, bf16[8,32,512]{2,1,0:T(8,128)(2,1)S(1)} %collective-permute-done.9.refs_1_, ...), custom_call_target="tpu_custom_call" | custom-call | flops 1024 | bytes 1024 | tf_op jit(solution)/shard_map/pallas_call | solution.py:102
  51.1 1.4 %shard_map.74 = (bf16[8,32,512]{2,1,0:T(8,128)(2,1)S(1)}, bf16[8,32,512]{2,1,0:T(8,128)(2,1)S(1)}) custom-call(s32[10]{0:T(128)S(1)} %compare_select_fusion.4.where, bf16[8,32,512]{2,1,0:T(8,128)(2,1)S(1)} %collective-permute-done.11.refs_0_, bf16[8,32,512]{2,1,0:T(8,128)(2,1)S(1)} %collective-permute-done.17.refs_1_, ...), custom_call_target="tpu_custom_call" | custom-call | flops 1024 | bytes 1024 | tf_op jit(solution)/shard_map/pallas_call | solution.py:102
  54.5 1.8 %collective-permute-done.15.refs_1_ = bf16[8,16,512]{2,1,0:T(8,128)(2,1)S(1)} collective-permute-done((bf16[8,16,512]{2,1,0:T(8,128)(2,1)S(1)}, bf16[8,16,512]{2,1,0:T(8,128)(2,1)S(1)}, u32[]{:S(2)}, u32[]{:S(2)}) %collective-permute-start.15) | collective-permute-done | bytes 131104 | tf_op jit(solution)/shard_map/ppermute | solution.py:235
  57.6 3.1 %collective-permute-start.19 = (bf16[8,32,512]{2,1,0:T(8,128)(2,1)S(1)}, bf16[8,32,512]{2,1,0:T(8,128)(2,1)S(1)}, u32[]{:S(2)}, u32[]{:S(2)}) collective-permute-start(bf16[8,32,512]{2,1,0:T(8,128)(2,1)S(1)} %get-tuple-element.139), channel_id=1, source_target_pairs={{0,8},{4,12},{8,0},{12,4},{1,9},{5,13},{9,1},{13,5},{2,10},{6,14},... | collective-permute-start | bytes 786440 | tf_op jit(solution)/shard_map/ppermute | solution.py:235
  62.3 1.4 %shard_map.80.refs_1_ = bf16[8,4,48,512]{3,2,1,0:T(8,128)(2,1)} custom-call(s32[10]{0:T(128)S(1)} %compare_select_fusion.4.where, bf16[8,16,512]{2,1,0:T(8,128)(2,1)S(1)} %get-tuple-element.143.refs_0_, bf16[8,16,512]{2,1,0:T(8,128)(2,1)S(1)} %get-tuple-element.144.refs_1_, bf16[8,16,512]{2,1,0:T(8,128)(2,1)S(1)} %get-tuple-element.145.refs_2_, ...), custom_call_target="tpu_custom_call" | custom-call | flops 1024 | bytes 1024 | tf_op jit(solution)/shard_map/pallas_call | solution.py:190
  64.9 12.1 %collective-permute-done.19.refs_0_ = bf16[8,32,512]{2,1,0:T(8,128)(2,1)S(1)} collective-permute-done((bf16[8,32,512]{2,1,0:T(8,128)(2,1)S(1)}, bf16[8,32,512]{2,1,0:T(8,128)(2,1)S(1)}, u32[]{:S(2)}, u32[]{:S(2)}) %collective-permute-start.19) | collective-permute-done | bytes 262176 | tf_op jit(solution)/shard_map/ppermute | solution.py:235
  77.0 6.3 %collective-permute-done.20.refs_1_ = bf16[8,32,512]{2,1,0:T(8,128)(2,1)S(1)} collective-permute-done((bf16[8,32,512]{2,1,0:T(8,128)(2,1)S(1)}, bf16[8,32,512]{2,1,0:T(8,128)(2,1)S(1)}, u32[]{:S(2)}, u32[]{:S(2)}) %collective-permute-start.20) | collective-permute-done | bytes 262176 | tf_op jit(solution)/shard_map/ppermute | solution.py:235
  83.3 1.4 %shard_map.82 = bf16[8,4,48,512]{3,2,1,0:T(8,128)(2,1)} custom-call(s32[10]{0:T(128)S(1)} %compare_select_fusion.4.where, bf16[8,32,512]{2,1,0:T(8,128)(2,1)S(1)} %collective-permute-done.19.refs_0_, bf16[8,32,512]{2,1,0:T(8,128)(2,1)S(1)} %collective-permute-done.20.refs_1_, ...), custom_call_target="tpu_custom_call", output_to_operand_aliasing={{}: (4, {})} | custom-call | flops 1024 | bytes 1024 | tf_op jit(solution)/shard_map/pallas_call | solution.py:190
  (54 shorter events, 18.2 us)
Async XLA Ops:
  0.0 9.6 %copy-start.2 = (bf16[1,32,24]{1,2,0:T(8,128)(2,1)S(1)}, bf16[1,32,24]{1,2,0:T(8,128)(2,1)}, u32[]{:S(2)}) copy-start(bf16[1,32,24]{1,2,0:T(8,128)(2,1)} %param.10) | copy-start | bytes 4612
  0.0 9.7 %copy-start = (s32[1,4,4]{2,1,0:T(4,128)S(1)}, s32[1,4,4]{2,1,0:T(4,128)}, u32[]{:S(2)}) copy-start(s32[1,4,4]{2,1,0:T(4,128)} %param.8) | copy-start | bytes 196
  1.1 15.8 %collective-permute-start = (bf16[8,16,512]{2,1,0:T(8,128)(2,1)S(1)}, bf16[8,16,512]{2,1,0:T(8,128)(2,1)S(1)}, u32[]{:S(2)}, u32[]{:S(2)}) collective-permute-start(bf16[8,16,512]{2,1,0:T(8,128)(2,1)S(1)} %get-tuple-element.154), channel_id=1, source_target_pairs={{0,8},{4,12},{8,0},{12,4},{1,9},{5,13},{9,1},{13,5},{2,10},{6,14},... | collective-permute-start | bytes 393224 | tf_op jit(solution)/shard_map/ppermute | solution.py:232
  3.7 13.1 %collective-permute-start.1 = (bf16[8,16,512]{2,1,0:T(8,128)(2,1)S(1)}, bf16[8,16,512]{2,1,0:T(8,128)(2,1)S(1)}, u32[]{:S(2)}, u32[]{:S(2)}) collective-permute-start(bf16[8,16,512]{2,1,0:T(8,128)(2,1)S(1)} %get-tuple-element.153), channel_id=1, source_target_pairs={{0,4},{4,8},{8,12},{12,0},{1,5},{5,9},{9,13},{13,1},{2,6},{6,10},{... | collective-permute-start | bytes 393224 | tf_op jit(solution)/shard_map/ppermute | solution.py:232
  3.8 13.1 %collective-permute-start.2 = (bf16[8,16,512]{2,1,0:T(8,128)(2,1)S(1)}, bf16[8,16,512]{2,1,0:T(8,128)(2,1)S(1)}, u32[]{:S(2)}, u32[]{:S(2)}) collective-permute-start(bf16[8,16,512]{2,1,0:T(8,128)(2,1)S(1)} %get-tuple-element.152), channel_id=1, source_target_pairs={{0,12},{4,0},{8,4},{12,8},{1,13},{5,1},{9,5},{13,9},{2,14},{6,2},{... | collective-permute-start | bytes 393224 | tf_op jit(solution)/shard_map/ppermute | solution.py:232
  6.8 10.0 %collective-permute-start.3 = (bf16[4,48,512]{2,1,0:T(8,128)(2,1)S(1)}, bf16[4,48,512]{2,1,0:T(8,128)(2,1)S(1)}, u32[]{:S(2)}, u32[]{:S(2)}) collective-permute-start(bf16[4,48,512]{2,1,0:T(8,128)(2,1)S(1)} %get-tuple-element.148.refs_0_), channel_id=1, source_target_pairs={{0,2},{2,0},{1,3},{3,1},{4,6},{6,4},{5,7},{7,5},{8,10},{10,8},{9,1... | collective-permute-start | bytes 589832 | tf_op jit(solution)/shard_map/ppermute | solution.py:238
  8.4 8.5 %collective-permute-start.4 = (bf16[4,48,512]{2,1,0:T(8,128)(2,1)S(1)}, bf16[4,48,512]{2,1,0:T(8,128)(2,1)S(1)}, u32[]{:S(2)}, u32[]{:S(2)}) collective-permute-start(bf16[4,48,512]{2,1,0:T(8,128)(2,1)S(1)} %get-tuple-element.147.refs_1_), channel_id=1, source_target_pairs={{0,2},{2,0},{1,3},{3,1},{4,6},{6,4},{5,7},{7,5},{8,10},{10,8},{9,1... | collective-permute-start | bytes 589832 | tf_op jit(solution)/shard_map/ppermute | solution.py:238
  16.9 11.5 %collective-permute-start.10 = (bf16[8,32,512]{2,1,0:T(8,128)(2,1)S(1)}, bf16[8,32,512]{2,1,0:T(8,128)(2,1)S(1)}, u32[]{:S(2)}, u32[]{:S(2)}) collective-permute-start(bf16[8,32,512]{2,1,0:T(8,128)(2,1)S(1)} %get-tuple-element.97), channel_id=1, source_target_pairs={{0,4},{4,8},{8,12},{12,0},{1,5},{5,9},{9,13},{13,1},{2,6},{6,10},{... | collective-permute-start | bytes 786440 | tf_op jit(solution)/shard_map/ppermute | solution.py:232
  17.4 14.4 %collective-permute-start.5 = (bf16[8,32,512]{2,1,0:T(8,128)(2,1)S(1)}, bf16[8,32,512]{2,1,0:T(8,128)(2,1)S(1)}, u32[]{:S(2)}, u32[]{:S(2)}) collective-permute-start(bf16[8,32,512]{2,1,0:T(8,128)(2,1)S(1)} %get-tuple-element.79), channel_id=1, source_target_pairs={{0,12},{4,0},{8,4},{12,8},{1,13},{5,1},{9,5},{13,9},{2,14},{6,2},{... | collective-permute-start | bytes 786440 | tf_op jit(solution)/shard_map/ppermute | solution.py:232
  19.3 6.4 %collective-permute-start.6 = (bf16[8,16,512]{2,1,0:T(8,128)(2,1)S(1)}, bf16[8,16,512]{2,1,0:T(8,128)(2,1)S(1)}, u32[]{:S(2)}, u32[]{:S(2)}) collective-permute-start(bf16[8,16,512]{2,1,0:T(8,128)(2,1)S(1)} %collective-permute-done.1.refs_0_), channel_id=1, source_target_pairs={{0,2},{2,0},{1,3},{3,1},{4,6},{6,4},{5,7},{7,5},{8,10},{10,8},{9,1... | collective-permute-start | bytes 393224 | tf_op jit(solution)/shard_map/ppermute | solution.py:238
  20.8 6.3 %collective-permute-start.7 = (bf16[8,16,512]{2,1,0:T(8,128)(2,1)S(1)}, bf16[8,16,512]{2,1,0:T(8,128)(2,1)S(1)}, u32[]{:S(2)}, u32[]{:S(2)}) collective-permute-start(bf16[8,16,512]{2,1,0:T(8,128)(2,1)S(1)} %collective-permute-done.refs_0_), channel_id=1, source_target_pairs={{0,2},{2,0},{1,3},{3,1},{4,6},{6,4},{5,7},{7,5},{8,10},{10,8},{9,1... | collective-permute-start | bytes 393224 | tf_op jit(solution)/shard_map/ppermute | solution.py:238
  21.3 8.7 %collective-permute-start.8 = (bf16[8,16,512]{2,1,0:T(8,128)(2,1)S(1)}, bf16[8,16,512]{2,1,0:T(8,128)(2,1)S(1)}, u32[]{:S(2)}, u32[]{:S(2)}) collective-permute-start(bf16[8,16,512]{2,1,0:T(8,128)(2,1)S(1)} %collective-permute-done.2.refs_0_), channel_id=1, source_target_pairs={{0,2},{2,0},{1,3},{3,1},{4,6},{6,4},{5,7},{7,5},{8,10},{10,8},{9,1... | collective-permute-start | bytes 393224 | tf_op jit(solution)/shard_map/ppermute | solution.py:238
  28.4 8.7 %collective-permute-start.13 = (bf16[8,32,512]{2,1,0:T(8,128)(2,1)S(1)}, bf16[8,32,512]{2,1,0:T(8,128)(2,1)S(1)}, u32[]{:S(2)}, u32[]{:S(2)}) collective-permute-start(bf16[8,32,512]{2,1,0:T(8,128)(2,1)S(1)} %collective-permute-done.10.refs_0_), channel_id=1, source_target_pairs={{0,2},{2,0},{1,3},{3,1},{4,6},{6,4},{5,7},{7,5},{8,10},{10,8},{9,1... | collective-permute-start | bytes 786440 | tf_op jit(solution)/shard_map/ppermute | solution.py:238
  31.7 8.7 %collective-permute-start.9 = (bf16[8,32,512]{2,1,0:T(8,128)(2,1)S(1)}, bf16[8,32,512]{2,1,0:T(8,128)(2,1)S(1)}, u32[]{:S(2)}, u32[]{:S(2)}) collective-permute-start(bf16[8,32,512]{2,1,0:T(8,128)(2,1)S(1)} %collective-permute-done.5.refs_0_), channel_id=1, source_target_pairs={{0,2},{2,0},{1,3},{3,1},{4,6},{6,4},{5,7},{7,5},{8,10},{10,8},{9,1... | collective-permute-start | bytes 786440 | tf_op jit(solution)/shard_map/ppermute | solution.py:238
  33.2 9.7 %collective-permute-start.11 = (bf16[8,32,512]{2,1,0:T(8,128)(2,1)S(1)}, bf16[8,32,512]{2,1,0:T(8,128)(2,1)S(1)}, u32[]{:S(2)}, u32[]{:S(2)}) collective-permute-start(bf16[8,32,512]{2,1,0:T(8,128)(2,1)S(1)} %get-tuple-element.98), channel_id=1, source_target_pairs={{0,8},{4,12},{8,0},{12,4},{1,9},{5,13},{9,1},{13,5},{2,10},{6,14},... | collective-permute-start | bytes 786440 | tf_op jit(solution)/shard_map/ppermute | solution.py:232
  35.5 3.4 %collective-permute-start.12 = (bf16[24,16,512]{2,1,0:T(8,128)(2,1)S(1)}, bf16[24,16,512]{2,1,0:T(8,128)(2,1)S(1)}, u32[]{:S(2)}, u32[]{:S(2)}) collective-permute-start(bf16[24,16,512]{2,1,0:T(8,128)(2,1)S(1)} %shard_map.69), channel_id=1, source_target_pairs={{0,1},{1,0},{2,3},{3,2},{4,5},{5,4},{6,7},{7,6},{8,9},{9,8},{10,11... | collective-permute-start | bytes 1179656 | tf_op jit(solution)/shard_map/ppermute | solution.py:273
  42.9 8.2 %collective-permute-start.17 = (bf16[8,32,512]{2,1,0:T(8,128)(2,1)S(1)}, bf16[8,32,512]{2,1,0:T(8,128)(2,1)S(1)}, u32[]{:S(2)}, u32[]{:S(2)}) collective-permute-start(bf16[8,32,512]{2,1,0:T(8,128)(2,1)S(1)} %collective-permute-done.11.refs_0_), channel_id=1, source_target_pairs={{0,2},{2,0},{1,3},{3,1},{4,6},{6,4},{5,7},{7,5},{8,10},{10,8},{9,1... | collective-permute-start | bytes 786440 | tf_op jit(solution)/shard_map/ppermute | solution.py:238
  43.4 11.1 %collective-permute-start.14 = (bf16[8,16,512]{2,1,0:T(8,128)(2,1)S(1)}, bf16[8,16,512]{2,1,0:T(8,128)(2,1)S(1)}, u32[]{:S(2)}, u32[]{:S(2)}) collective-permute-start(bf16[8,16,512]{2,1,0:T(8,128)(2,1)S(1)} %get-tuple-element.110), channel_id=1, source_target_pairs={{0,12},{4,8},{8,4},{12,0},{1,13},{5,9},{9,5},{13,1},{2,14},{6,10},... | collective-permute-start | bytes 393224 | tf_op jit(solution)/shard_map/ppermute | solution.py:235
  45.5 10.9 %collective-permute-start.15 = (bf16[8,16,512]{2,1,0:T(8,128)(2,1)S(1)}, bf16[8,16,512]{2,1,0:T(8,128)(2,1)S(1)}, u32[]{:S(2)}, u32[]{:S(2)}) collective-permute-start(bf16[8,16,512]{2,1,0:T(8,128)(2,1)S(1)} %get-tuple-element.111), channel_id=1, source_target_pairs={{0,8},{4,12},{8,0},{12,4},{1,9},{5,13},{9,1},{13,5},{2,10},{6,14},... | collective-permute-start | bytes 393224 | tf_op jit(solution)/shard_map/ppermute | solution.py:235
  49.7 6.6 %collective-permute-start.16 = (bf16[8,16,512]{2,1,0:T(8,128)(2,1)S(1)}, bf16[8,16,512]{2,1,0:T(8,128)(2,1)S(1)}, u32[]{:S(2)}, u32[]{:S(2)}) collective-permute-start(bf16[8,16,512]{2,1,0:T(8,128)(2,1)S(1)} %get-tuple-element.112), channel_id=1, source_target_pairs={{0,4},{4,0},{8,12},{12,8},{1,5},{5,1},{9,13},{13,9},{2,6},{6,2},{1... | collective-permute-start | bytes 393224 | tf_op jit(solution)/shard_map/ppermute | solution.py:235
  53.4 2.9 %collective-permute-start.18 = (bf16[24,32,512]{2,1,0:T(8,128)(2,1)S(1)}, bf16[24,32,512]{2,1,0:T(8,128)(2,1)S(1)}, u32[]{:S(2)}, u32[]{:S(2)}) collective-permute-start(bf16[24,32,512]{2,1,0:T(8,128)(2,1)S(1)} %shard_map.76), channel_id=1, source_target_pairs={{0,1},{1,0},{2,3},{3,2},{4,5},{5,4},{6,7},{7,6},{8,9},{9,8},{10,11... | collective-permute-start | bytes 2359304 | tf_op jit(solution)/shard_map/ppermute | solution.py:284
  57.6 19.4 %collective-permute-start.19 = (bf16[8,32,512]{2,1,0:T(8,128)(2,1)S(1)}, bf16[8,32,512]{2,1,0:T(8,128)(2,1)S(1)}, u32[]{:S(2)}, u32[]{:S(2)}) collective-permute-start(bf16[8,32,512]{2,1,0:T(8,128)(2,1)S(1)} %get-tuple-element.139), channel_id=1, source_target_pairs={{0,8},{4,12},{8,0},{12,4},{1,9},{5,13},{9,1},{13,5},{2,10},{6,14},... | collective-permute-start | bytes 786440 | tf_op jit(solution)/shard_map/ppermute | solution.py:235
  60.7 22.5 %collective-permute-start.20 = (bf16[8,32,512]{2,1,0:T(8,128)(2,1)S(1)}, bf16[8,32,512]{2,1,0:T(8,128)(2,1)S(1)}, u32[]{:S(2)}, u32[]{:S(2)}) collective-permute-start(bf16[8,32,512]{2,1,0:T(8,128)(2,1)S(1)} %get-tuple-element.140), channel_id=1, source_target_pairs={{0,12},{4,8},{8,4},{12,0},{1,13},{5,9},{9,5},{13,1},{2,14},{6,10},... | collective-permute-start | bytes 786440 | tf_op jit(solution)/shard_map/ppermute | solution.py:235
  61.4 21.8 %collective-permute-start.21 = (bf16[8,32,512]{2,1,0:T(8,128)(2,1)S(1)}, bf16[8,32,512]{2,1,0:T(8,128)(2,1)S(1)}, u32[]{:S(2)}, u32[]{:S(2)}) collective-permute-start(bf16[8,32,512]{2,1,0:T(8,128)(2,1)S(1)} %get-tuple-element.141), channel_id=1, source_target_pairs={{0,4},{4,0},{8,12},{12,8},{1,5},{5,1},{9,13},{13,9},{2,6},{6,2},{1... | collective-permute-start | bytes 786440 | tf_op jit(solution)/shard_map/ppermute | solution.py:235
  (2 other events, 11.2 us)

commit v24 on v23

--- a/solution.py
+++ b/solution.py
@@ -285,11 +285,13 @@
     kept = reduce(down, stays, (ROWS, 0, 0, 0), n_modes, jnp.float32)
     first[3], first[2], first[1], kept = fence((first[3], first[2], first[1], kept))
     first[3], first[2], first[1] = anchor([first[3], first[2], first[1]], 7_500_000_000)
-    outs, first[3], first[2], first[1] = fence((restore(kept, came, ratios, up, spots), first[3], first[2], first[1]))
+    out_2, = restore(kept, came, ratios, up, [spots[1]])
+    out_2, first[3], first[2], first[1] = fence((out_2, first[3], first[2], first[1]))
     first[0] = here
-    back = [swap_z(outs[j - 1], j) for j in (2, 3, 1)]
+    out_3, out_1, out_0 = restore(kept, came, ratios, up, [spots[2], spots[0], spots[3]])
+    back = [swap_z(out, j) for out, j in ((out_2, 2), (out_3, 3), (out_1, 1))]
     result = place(where, [first[j] for j in (1, 2, 3, 0)], spots, 0, shape)
-    result = place(where, [outs[3]], [spots[3]], ROWS, shape, into=result)
+    result = place(where, [out_0], [spots[3]], ROWS, shape, into=result)
     return place(where, back, [spots[1], spots[2], spots[0]], ROWS, shape, into=result)
 
 

time: 85.1 us -> 84.6 us (level)
  waiting for transfers between devices: 26.8 us -> 25.7 us
    ppermute x6, waiting for transfers between devices: 20.2 us -> 19.1 us  [swap_z(): return lax.ppermute(value, 'fm', [(i, i ^ j) for i in range(parts)])]
    pallas_call x2 -> x3, Pallas kernels: 1.78 us -> 2.37 us  [restore(): pl.pallas_call(functools.partial(restore_kernel, spots=spots), grid=(rows...]
  transfers between devices with their start and end apart: 22 -> 22, of which waited for: 7 -> 7; matrix products, arithmetic and copies ran while one was open for 2% -> 2% of each run, Pallas kernels for 26% -> 28%
where the time goes in v24:
time: 84.6 us; the launch traced here: 84.2 us
  starting transfers between devices  29.5 us (35%)
  Pallas kernels  25.7 us (30%)
  waiting for transfers between devices  25.7 us (30%)
  local copies, waits for them, and re-layouts  2.39 us (3%)
  between operations  0.93 us (1%)
    ppermute x6, waiting for transfers between devices, swap_z(): return lax.ppermute(value, 'fm', [(i, i ^ j) for i in range(parts)])  19.1 us
    ppermute x6, starting transfers between devices, swap_z(): return lax.ppermute(value, 'fm', [(i, i ^ j) for i in range(parts)])  11 us
    pallas_call x7, Pallas kernels, project(): pl.pallas_call(functools.partial(project_kernel, piece=piece, blocks=bloc...  9.57 us
    ppermute x6, starting transfers between devices, shift_z(): lax.ppermute(value, 'fm', [(i, (i + j) % parts) for i in range(parts)])  9.33 us
    ppermute x8, starting transfers between devices, along_x(): return lax.ppermute(value, 'kl', other)  9.13 us
    pallas_call x1, Pallas kernels, hold(): pl.pallas_call(hold_kernel, grid_spec=pltpu.PrefetchScalarGridSpec(num_sc...  7.04 us
    ppermute x8, waiting for transfers between devices, along_x(): return lax.ppermute(value, 'kl', other)  4.17 us
    pallas_call x3, Pallas kernels, place(): pl.pallas_call(functools.partial(place_kernel, spots=spots, first=first),...  4.06 us
  transfers between devices with their start and end apart: 22, of which 7 were waited for; matrix products, arithmetic and copies ran while one was open for 2% of the time, Pallas kernels for 28%

profile of v24, /device:TPU:12, one launch (start us, length us, event | category | flops | bytes accessed | tf_op | source)
XLA Modules:
  0.0 84.2 jit_solution(5054909323757396268)
XLA Ops:
  1.1 2.7 %collective-permute-start = (bf16[8,16,512]{2,1,0:T(8,128)(2,1)S(1)}, bf16[8,16,512]{2,1,0:T(8,128)(2,1)S(1)}, u32[]{:S(2)}, u32[]{:S(2)}) collective-permute-start(bf16[8,16,512]{2,1,0:T(8,128)(2,1)S(1)} %get-tuple-element.146), channel_id=1, source_target_pairs={{0,8},{4,12},{8,0},{12,4},{1,9},{5,13},{9,1},{13,5},{2,10},{6,14},... | collective-permute-start | bytes 393224 | tf_op jit(solution)/shard_map/ppermute | solution.py:232
  3.8 2.0 %collective-permute-start.2 = (bf16[8,16,512]{2,1,0:T(8,128)(2,1)S(1)}, bf16[8,16,512]{2,1,0:T(8,128)(2,1)S(1)}, u32[]{:S(2)}, u32[]{:S(2)}) collective-permute-start(bf16[8,16,512]{2,1,0:T(8,128)(2,1)S(1)} %get-tuple-element.144), channel_id=1, source_target_pairs={{0,12},{4,0},{8,4},{12,8},{1,13},{5,1},{9,5},{13,9},{2,14},{6,2},{... | collective-permute-start | bytes 393224 | tf_op jit(solution)/shard_map/ppermute | solution.py:232
  6.8 1.6 %collective-permute-start.3 = (bf16[4,48,512]{2,1,0:T(8,128)(2,1)S(1)}, bf16[4,48,512]{2,1,0:T(8,128)(2,1)S(1)}, u32[]{:S(2)}, u32[]{:S(2)}) collective-permute-start(bf16[4,48,512]{2,1,0:T(8,128)(2,1)S(1)} %get-tuple-element.140.refs_0_), channel_id=1, source_target_pairs={{0,2},{2,0},{1,3},{3,1},{4,6},{6,4},{5,7},{7,5},{8,10},{10,8},{9,1... | collective-permute-start | bytes 589832 | tf_op jit(solution)/shard_map/ppermute | solution.py:238
  9.7 7.0 %shard_map.64 = (bf16[32,512,512]{2,1,0:T(8,128)(2,1)S(1)}, bf16[384,512]{1,0:T(8,128)(2,1)S(1)}, bf16[512,384]{1,0:T(8,128)(2,1)S(1)}) custom-call(s32[10]{0:T(128)S(1)} %compare_select_fusion.4.where, s32[4,4]{1,0:T(4,128)S(1)} %bitcast.27, s32[1]{0:T(128)S(6)} %copy.24.starts, bf16[32,512,512]{2,1,0:T(8,128)(2,1)} %bitcast.28, bf16[32,24]{1,0:T(8,128)(2,1)S(1)} %bitcast.26), custom_call_target="tpu_custom_call" | custom-call | flops 1024 | bytes 1024 | tf_op jit(solution)/shard_map/pallas_call | solution.py:63
  17.4 1.9 %collective-permute-start.5 = (bf16[8,32,512]{2,1,0:T(8,128)(2,1)S(1)}, bf16[8,32,512]{2,1,0:T(8,128)(2,1)S(1)}, u32[]{:S(2)}, u32[]{:S(2)}) collective-permute-start(bf16[8,32,512]{2,1,0:T(8,128)(2,1)S(1)} %get-tuple-element.75), channel_id=1, source_target_pairs={{0,12},{4,0},{8,4},{12,8},{1,13},{5,1},{9,5},{13,9},{2,14},{6,2},{... | collective-permute-start | bytes 786440 | tf_op jit(solution)/shard_map/ppermute | solution.py:232
  19.3 1.5 %collective-permute-start.6 = (bf16[8,16,512]{2,1,0:T(8,128)(2,1)S(1)}, bf16[8,16,512]{2,1,0:T(8,128)(2,1)S(1)}, u32[]{:S(2)}, u32[]{:S(2)}) collective-permute-start(bf16[8,16,512]{2,1,0:T(8,128)(2,1)S(1)} %collective-permute-done.1.refs_0_), channel_id=1, source_target_pairs={{0,2},{2,0},{1,3},{3,1},{4,6},{6,4},{5,7},{7,5},{8,10},{10,8},{9,1... | collective-permute-start | bytes 393224 | tf_op jit(solution)/shard_map/ppermute | solution.py:238
  21.3 1.5 %collective-permute-start.8 = (bf16[8,16,512]{2,1,0:T(8,128)(2,1)S(1)}, bf16[8,16,512]{2,1,0:T(8,128)(2,1)S(1)}, u32[]{:S(2)}, u32[]{:S(2)}) collective-permute-start(bf16[8,16,512]{2,1,0:T(8,128)(2,1)S(1)} %collective-permute-done.2.refs_0_), channel_id=1, source_target_pairs={{0,2},{2,0},{1,3},{3,1},{4,6},{6,4},{5,7},{7,5},{8,10},{10,8},{9,1... | collective-permute-start | bytes 393224 | tf_op jit(solution)/shard_map/ppermute | solution.py:238
  24.1 1.5 %collective-permute-done.6.refs_1_ = bf16[8,16,512]{2,1,0:T(8,128)(2,1)S(1)} collective-permute-done((bf16[8,16,512]{2,1,0:T(8,128)(2,1)S(1)}, bf16[8,16,512]{2,1,0:T(8,128)(2,1)S(1)}, u32[]{:S(2)}, u32[]{:S(2)}) %collective-permute-start.6) | collective-permute-done | bytes 131104 | tf_op jit(solution)/shard_map/ppermute | solution.py:238
  28.4 1.6 %collective-permute-start.13 = (bf16[8,32,512]{2,1,0:T(8,128)(2,1)S(1)}, bf16[8,32,512]{2,1,0:T(8,128)(2,1)S(1)}, u32[]{:S(2)}, u32[]{:S(2)}) collective-permute-start(bf16[8,32,512]{2,1,0:T(8,128)(2,1)S(1)} %collective-permute-done.10.refs_0_), channel_id=1, source_target_pairs={{0,2},{2,0},{1,3},{3,1},{4,6},{6,4},{5,7},{7,5},{8,10},{10,8},{9,1... | collective-permute-start | bytes 786440 | tf_op jit(solution)/shard_map/ppermute | solution.py:238
  30.0 1.4 %shard_map.68 = (bf16[8,16,512]{2,1,0:T(8,128)(2,1)S(1)}, bf16[8,16,512]{2,1,0:T(8,128)(2,1)S(1)}) custom-call(s32[10]{0:T(128)S(1)} %compare_select_fusion.4.where, bf16[8,16,512]{2,1,0:T(8,128)(2,1)S(1)} %collective-permute-done.2.refs_0_, bf16[8,16,512]{2,1,0:T(8,128)(2,1)S(1)} %collective-permute-done.8.refs_1_, ...), custom_call_target="tpu_custom_call" | custom-call | flops 400000000 | bytes 1024 | tf_op jit(solution)/shard_map/pallas_call | solution.py:102
  31.7 1.4 %collective-permute-start.9 = (bf16[8,32,512]{2,1,0:T(8,128)(2,1)S(1)}, bf16[8,32,512]{2,1,0:T(8,128)(2,1)S(1)}, u32[]{:S(2)}, u32[]{:S(2)}) collective-permute-start(bf16[8,32,512]{2,1,0:T(8,128)(2,1)S(1)} %collective-permute-done.5.refs_0_), channel_id=1, source_target_pairs={{0,2},{2,0},{1,3},{3,1},{4,6},{6,4},{5,7},{7,5},{8,10},{10,8},{9,1... | collective-permute-start | bytes 786440 | tf_op jit(solution)/shard_map/ppermute | solution.py:238
  33.2 2.3 %collective-permute-start.11 = (bf16[8,32,512]{2,1,0:T(8,128)(2,1)S(1)}, bf16[8,32,512]{2,1,0:T(8,128)(2,1)S(1)}, u32[]{:S(2)}, u32[]{:S(2)}) collective-permute-start(bf16[8,32,512]{2,1,0:T(8,128)(2,1)S(1)} %get-tuple-element.94), channel_id=1, source_target_pairs={{0,8},{4,12},{8,0},{12,4},{1,9},{5,13},{9,1},{13,5},{2,10},{6,14},... | collective-permute-start | bytes 786440 | tf_op jit(solution)/shard_map/ppermute | solution.py:232
  35.5 1.6 %collective-permute-done.13.refs_0_ = bf16[8,32,512]{2,1,0:T(8,128)(2,1)S(1)} collective-permute-done((bf16[8,32,512]{2,1,0:T(8,128)(2,1)S(1)}, bf16[8,32,512]{2,1,0:T(8,128)(2,1)S(1)}, u32[]{:S(2)}, u32[]{:S(2)}) %collective-permute-start.13) | collective-permute-done | bytes 262176 | tf_op jit(solution)/shard_map/ppermute | solution.py:238
  37.5 1.4 %shard_map.73 = (bf16[8,32,512]{2,1,0:T(8,128)(2,1)S(1)}, bf16[8,32,512]{2,1,0:T(8,128)(2,1)S(1)}) custom-call(s32[10]{0:T(128)S(1)} %compare_select_fusion.4.where, bf16[8,32,512]{2,1,0:T(8,128)(2,1)S(1)} %collective-permute-done.10.refs_0_, bf16[8,32,512]{2,1,0:T(8,128)(2,1)S(1)} %shard_map.72.refs_1_, ...), custom_call_target="tpu_custom_call" | custom-call | flops 1024 | bytes 1024 | tf_op jit(solution)/shard_map/pallas_call | solution.py:102
  40.5 2.4 %collective-permute-done.11.refs_0_ = bf16[8,32,512]{2,1,0:T(8,128)(2,1)S(1)} collective-permute-done((bf16[8,32,512]{2,1,0:T(8,128)(2,1)S(1)}, bf16[8,32,512]{2,1,0:T(8,128)(2,1)S(1)}, u32[]{:S(2)}, u32[]{:S(2)}) %collective-permute-start.11) | collective-permute-done | bytes 262176 | tf_op jit(solution)/shard_map/ppermute | solution.py:232
  43.4 2.0 %collective-permute-start.14 = (bf16[8,16,512]{2,1,0:T(8,128)(2,1)S(1)}, bf16[8,16,512]{2,1,0:T(8,128)(2,1)S(1)}, u32[]{:S(2)}, u32[]{:S(2)}) collective-permute-start(bf16[8,16,512]{2,1,0:T(8,128)(2,1)S(1)} %get-tuple-element.106), channel_id=1, source_target_pairs={{0,12},{4,8},{8,4},{12,0},{1,13},{5,9},{9,5},{13,1},{2,14},{6,10},... | collective-permute-start | bytes 393224 | tf_op jit(solution)/shard_map/ppermute | solution.py:235
  45.4 4.3 %collective-permute-start.15 = (bf16[8,16,512]{2,1,0:T(8,128)(2,1)S(1)}, bf16[8,16,512]{2,1,0:T(8,128)(2,1)S(1)}, u32[]{:S(2)}, u32[]{:S(2)}) collective-permute-start(bf16[8,16,512]{2,1,0:T(8,128)(2,1)S(1)} %get-tuple-element.107), channel_id=1, source_target_pairs={{0,8},{4,12},{8,0},{12,4},{1,9},{5,13},{9,1},{13,5},{2,10},{6,14},... | collective-permute-start | bytes 393224 | tf_op jit(solution)/shard_map/ppermute | solution.py:235
  49.7 1.4 %shard_map.75 = (bf16[8,32,512]{2,1,0:T(8,128)(2,1)S(1)}, bf16[8,32,512]{2,1,0:T(8,128)(2,1)S(1)}) custom-call(s32[10]{0:T(128)S(1)} %compare_select_fusion.4.where, bf16[8,32,512]{2,1,0:T(8,128)(2,1)S(1)} %collective-permute-done.5.refs_0_, bf16[8,32,512]{2,1,0:T(8,128)(2,1)S(1)} %collective-permute-done.9.refs_1_, ...), custom_call_target="tpu_custom_call" | custom-call | flops 1024 | bytes 1024 | tf_op jit(solution)/shard_map/pallas_call | solution.py:102
  51.1 1.4 %shard_map.74 = (bf16[8,32,512]{2,1,0:T(8,128)(2,1)S(1)}, bf16[8,32,512]{2,1,0:T(8,128)(2,1)S(1)}) custom-call(s32[10]{0:T(128)S(1)} %compare_select_fusion.4.where, bf16[8,32,512]{2,1,0:T(8,128)(2,1)S(1)} %collective-permute-done.11.refs_0_, bf16[8,32,512]{2,1,0:T(8,128)(2,1)S(1)} %collective-permute-done.17.refs_1_, ...), custom_call_target="tpu_custom_call" | custom-call | flops 1024 | bytes 1024 | tf_op jit(solution)/shard_map/pallas_call | solution.py:102
  54.5 1.8 %collective-permute-done.15.refs_1_ = bf16[8,16,512]{2,1,0:T(8,128)(2,1)S(1)} collective-permute-done((bf16[8,16,512]{2,1,0:T(8,128)(2,1)S(1)}, bf16[8,16,512]{2,1,0:T(8,128)(2,1)S(1)}, u32[]{:S(2)}, u32[]{:S(2)}) %collective-permute-start.15) | collective-permute-done | bytes 131104 | tf_op jit(solution)/shard_map/ppermute | solution.py:235
  57.1 3.1 %collective-permute-start.19 = (bf16[8,32,512]{2,1,0:T(8,128)(2,1)S(1)}, bf16[8,32,512]{2,1,0:T(8,128)(2,1)S(1)}, u32[]{:S(2)}, u32[]{:S(2)}) collective-permute-start(bf16[8,32,512]{2,1,0:T(8,128)(2,1)S(1)} %shard_map.78), channel_id=1, source_target_pairs={{0,8},{4,12},{8,0},{12,4},{1,9},{5,13},{9,1},{13,5},{2,10},{6,14},... | collective-permute-start | bytes 786440 | tf_op jit(solution)/shard_map/ppermute | solution.py:235
  65.5 11.0 %collective-permute-done.19.refs_0_ = bf16[8,32,512]{2,1,0:T(8,128)(2,1)S(1)} collective-permute-done((bf16[8,32,512]{2,1,0:T(8,128)(2,1)S(1)}, bf16[8,32,512]{2,1,0:T(8,128)(2,1)S(1)}, u32[]{:S(2)}, u32[]{:S(2)}) %collective-permute-start.19) | collective-permute-done | bytes 262176 | tf_op jit(solution)/shard_map/ppermute | solution.py:235
  76.5 6.3 %collective-permute-done.20.refs_1_ = bf16[8,32,512]{2,1,0:T(8,128)(2,1)S(1)} collective-permute-done((bf16[8,32,512]{2,1,0:T(8,128)(2,1)S(1)}, bf16[8,32,512]{2,1,0:T(8,128)(2,1)S(1)}, u32[]{:S(2)}, u32[]{:S(2)}) %collective-permute-start.20) | collective-permute-done | bytes 262176 | tf_op jit(solution)/shard_map/ppermute | solution.py:235
  82.8 1.4 %shard_map.83 = bf16[8,4,48,512]{3,2,1,0:T(8,128)(2,1)} custom-call(s32[10]{0:T(128)S(1)} %compare_select_fusion.4.where, bf16[8,32,512]{2,1,0:T(8,128)(2,1)S(1)} %collective-permute-done.19.refs_0_, bf16[8,32,512]{2,1,0:T(8,128)(2,1)S(1)} %collective-permute-done.20.refs_1_, ...), custom_call_target="tpu_custom_call", output_to_operand_aliasing={{}: (4, {})} | custom-call | flops 1024 | bytes 1024 | tf_op jit(solution)/shard_map/pallas_call | solution.py:190
  (55 shorter events, 18.9 us)
Async XLA Ops:
  0.0 9.6 %copy-start.2 = (bf16[1,32,24]{1,2,0:T(8,128)(2,1)S(1)}, bf16[1,32,24]{1,2,0:T(8,128)(2,1)}, u32[]{:S(2)}) copy-start(bf16[1,32,24]{1,2,0:T(8,128)(2,1)} %param.10) | copy-start | bytes 4612
  0.0 9.7 %copy-start = (s32[1,4,4]{2,1,0:T(4,128)S(1)}, s32[1,4,4]{2,1,0:T(4,128)}, u32[]{:S(2)}) copy-start(s32[1,4,4]{2,1,0:T(4,128)} %param.8) | copy-start | bytes 196
  1.1 15.8 %collective-permute-start = (bf16[8,16,512]{2,1,0:T(8,128)(2,1)S(1)}, bf16[8,16,512]{2,1,0:T(8,128)(2,1)S(1)}, u32[]{:S(2)}, u32[]{:S(2)}) collective-permute-start(bf16[8,16,512]{2,1,0:T(8,128)(2,1)S(1)} %get-tuple-element.146), channel_id=1, source_target_pairs={{0,8},{4,12},{8,0},{12,4},{1,9},{5,13},{9,1},{13,5},{2,10},{6,14},... | collective-permute-start | bytes 393224 | tf_op jit(solution)/shard_map/ppermute | solution.py:232
  3.7 13.1 %collective-permute-start.1 = (bf16[8,16,512]{2,1,0:T(8,128)(2,1)S(1)}, bf16[8,16,512]{2,1,0:T(8,128)(2,1)S(1)}, u32[]{:S(2)}, u32[]{:S(2)}) collective-permute-start(bf16[8,16,512]{2,1,0:T(8,128)(2,1)S(1)} %get-tuple-element.145), channel_id=1, source_target_pairs={{0,4},{4,8},{8,12},{12,0},{1,5},{5,9},{9,13},{13,1},{2,6},{6,10},{... | collective-permute-start | bytes 393224 | tf_op jit(solution)/shard_map/ppermute | solution.py:232
  3.8 13.1 %collective-permute-start.2 = (bf16[8,16,512]{2,1,0:T(8,128)(2,1)S(1)}, bf16[8,16,512]{2,1,0:T(8,128)(2,1)S(1)}, u32[]{:S(2)}, u32[]{:S(2)}) collective-permute-start(bf16[8,16,512]{2,1,0:T(8,128)(2,1)S(1)} %get-tuple-element.144), channel_id=1, source_target_pairs={{0,12},{4,0},{8,4},{12,8},{1,13},{5,1},{9,5},{13,9},{2,14},{6,2},{... | collective-permute-start | bytes 393224 | tf_op jit(solution)/shard_map/ppermute | solution.py:232
  6.8 10.0 %collective-permute-start.3 = (bf16[4,48,512]{2,1,0:T(8,128)(2,1)S(1)}, bf16[4,48,512]{2,1,0:T(8,128)(2,1)S(1)}, u32[]{:S(2)}, u32[]{:S(2)}) collective-permute-start(bf16[4,48,512]{2,1,0:T(8,128)(2,1)S(1)} %get-tuple-element.140.refs_0_), channel_id=1, source_target_pairs={{0,2},{2,0},{1,3},{3,1},{4,6},{6,4},{5,7},{7,5},{8,10},{10,8},{9,1... | collective-permute-start | bytes 589832 | tf_op jit(solution)/shard_map/ppermute | solution.py:238
  8.4 8.5 %collective-permute-start.4 = (bf16[4,48,512]{2,1,0:T(8,128)(2,1)S(1)}, bf16[4,48,512]{2,1,0:T(8,128)(2,1)S(1)}, u32[]{:S(2)}, u32[]{:S(2)}) collective-permute-start(bf16[4,48,512]{2,1,0:T(8,128)(2,1)S(1)} %get-tuple-element.139.refs_1_), channel_id=1, source_target_pairs={{0,2},{2,0},{1,3},{3,1},{4,6},{6,4},{5,7},{7,5},{8,10},{10,8},{9,1... | collective-permute-start | bytes 589832 | tf_op jit(solution)/shard_map/ppermute | solution.py:238
  16.9 11.5 %collective-permute-start.10 = (bf16[8,32,512]{2,1,0:T(8,128)(2,1)S(1)}, bf16[8,32,512]{2,1,0:T(8,128)(2,1)S(1)}, u32[]{:S(2)}, u32[]{:S(2)}) collective-permute-start(bf16[8,32,512]{2,1,0:T(8,128)(2,1)S(1)} %get-tuple-element.93), channel_id=1, source_target_pairs={{0,4},{4,8},{8,12},{12,0},{1,5},{5,9},{9,13},{13,1},{2,6},{6,10},{... | collective-permute-start | bytes 786440 | tf_op jit(solution)/shard_map/ppermute | solution.py:232
  17.4 14.4 %collective-permute-start.5 = (bf16[8,32,512]{2,1,0:T(8,128)(2,1)S(1)}, bf16[8,32,512]{2,1,0:T(8,128)(2,1)S(1)}, u32[]{:S(2)}, u32[]{:S(2)}) collective-permute-start(bf16[8,32,512]{2,1,0:T(8,128)(2,1)S(1)} %get-tuple-element.75), channel_id=1, source_target_pairs={{0,12},{4,0},{8,4},{12,8},{1,13},{5,1},{9,5},{13,9},{2,14},{6,2},{... | collective-permute-start | bytes 786440 | tf_op jit(solution)/shard_map/ppermute | solution.py:232
  19.3 6.4 %collective-permute-start.6 = (bf16[8,16,512]{2,1,0:T(8,128)(2,1)S(1)}, bf16[8,16,512]{2,1,0:T(8,128)(2,1)S(1)}, u32[]{:S(2)}, u32[]{:S(2)}) collective-permute-start(bf16[8,16,512]{2,1,0:T(8,128)(2,1)S(1)} %collective-permute-done.1.refs_0_), channel_id=1, source_target_pairs={{0,2},{2,0},{1,3},{3,1},{4,6},{6,4},{5,7},{7,5},{8,10},{10,8},{9,1... | collective-permute-start | bytes 393224 | tf_op jit(solution)/shard_map/ppermute | solution.py:238
  20.8 6.3 %collective-permute-start.7 = (bf16[8,16,512]{2,1,0:T(8,128)(2,1)S(1)}, bf16[8,16,512]{2,1,0:T(8,128)(2,1)S(1)}, u32[]{:S(2)}, u32[]{:S(2)}) collective-permute-start(bf16[8,16,512]{2,1,0:T(8,128)(2,1)S(1)} %collective-permute-done.refs_0_), channel_id=1, source_target_pairs={{0,2},{2,0},{1,3},{3,1},{4,6},{6,4},{5,7},{7,5},{8,10},{10,8},{9,1... | collective-permute-start | bytes 393224 | tf_op jit(solution)/shard_map/ppermute | solution.py:238
  21.3 8.7 %collective-permute-start.8 = (bf16[8,16,512]{2,1,0:T(8,128)(2,1)S(1)}, bf16[8,16,512]{2,1,0:T(8,128)(2,1)S(1)}, u32[]{:S(2)}, u32[]{:S(2)}) collective-permute-start(bf16[8,16,512]{2,1,0:T(8,128)(2,1)S(1)} %collective-permute-done.2.refs_0_), channel_id=1, source_target_pairs={{0,2},{2,0},{1,3},{3,1},{4,6},{6,4},{5,7},{7,5},{8,10},{10,8},{9,1... | collective-permute-start | bytes 393224 | tf_op jit(solution)/shard_map/ppermute | solution.py:238
  28.4 8.7 %collective-permute-start.13 = (bf16[8,32,512]{2,1,0:T(8,128)(2,1)S(1)}, bf16[8,32,512]{2,1,0:T(8,128)(2,1)S(1)}, u32[]{:S(2)}, u32[]{:S(2)}) collective-permute-start(bf16[8,32,512]{2,1,0:T(8,128)(2,1)S(1)} %collective-permute-done.10.refs_0_), channel_id=1, source_target_pairs={{0,2},{2,0},{1,3},{3,1},{4,6},{6,4},{5,7},{7,5},{8,10},{10,8},{9,1... | collective-permute-start | bytes 786440 | tf_op jit(solution)/shard_map/ppermute | solution.py:238
  31.7 8.7 %collective-permute-start.9 = (bf16[8,32,512]{2,1,0:T(8,128)(2,1)S(1)}, bf16[8,32,512]{2,1,0:T(8,128)(2,1)S(1)}, u32[]{:S(2)}, u32[]{:S(2)}) collective-permute-start(bf16[8,32,512]{2,1,0:T(8,128)(2,1)S(1)} %collective-permute-done.5.refs_0_), channel_id=1, source_target_pairs={{0,2},{2,0},{1,3},{3,1},{4,6},{6,4},{5,7},{7,5},{8,10},{10,8},{9,1... | collective-permute-start | bytes 786440 | tf_op jit(solution)/shard_map/ppermute | solution.py:238
  33.2 9.7 %collective-permute-start.11 = (bf16[8,32,512]{2,1,0:T(8,128)(2,1)S(1)}, bf16[8,32,512]{2,1,0:T(8,128)(2,1)S(1)}, u32[]{:S(2)}, u32[]{:S(2)}) collective-permute-start(bf16[8,32,512]{2,1,0:T(8,128)(2,1)S(1)} %get-tuple-element.94), channel_id=1, source_target_pairs={{0,8},{4,12},{8,0},{12,4},{1,9},{5,13},{9,1},{13,5},{2,10},{6,14},... | collective-permute-start | bytes 786440 | tf_op jit(solution)/shard_map/ppermute | solution.py:232
  35.5 3.4 %collective-permute-start.12 = (bf16[24,16,512]{2,1,0:T(8,128)(2,1)S(1)}, bf16[24,16,512]{2,1,0:T(8,128)(2,1)S(1)}, u32[]{:S(2)}, u32[]{:S(2)}) collective-permute-start(bf16[24,16,512]{2,1,0:T(8,128)(2,1)S(1)} %shard_map.69), channel_id=1, source_target_pairs={{0,1},{1,0},{2,3},{3,2},{4,5},{5,4},{6,7},{7,6},{8,9},{9,8},{10,11... | collective-permute-start | bytes 1179656 | tf_op jit(solution)/shard_map/ppermute | solution.py:273
  42.9 8.2 %collective-permute-start.17 = (bf16[8,32,512]{2,1,0:T(8,128)(2,1)S(1)}, bf16[8,32,512]{2,1,0:T(8,128)(2,1)S(1)}, u32[]{:S(2)}, u32[]{:S(2)}) collective-permute-start(bf16[8,32,512]{2,1,0:T(8,128)(2,1)S(1)} %collective-permute-done.11.refs_0_), channel_id=1, source_target_pairs={{0,2},{2,0},{1,3},{3,1},{4,6},{6,4},{5,7},{7,5},{8,10},{10,8},{9,1... | collective-permute-start | bytes 786440 | tf_op jit(solution)/shard_map/ppermute | solution.py:238
  43.4 11.1 %collective-permute-start.14 = (bf16[8,16,512]{2,1,0:T(8,128)(2,1)S(1)}, bf16[8,16,512]{2,1,0:T(8,128)(2,1)S(1)}, u32[]{:S(2)}, u32[]{:S(2)}) collective-permute-start(bf16[8,16,512]{2,1,0:T(8,128)(2,1)S(1)} %get-tuple-element.106), channel_id=1, source_target_pairs={{0,12},{4,8},{8,4},{12,0},{1,13},{5,9},{9,5},{13,1},{2,14},{6,10},... | collective-permute-start | bytes 393224 | tf_op jit(solution)/shard_map/ppermute | solution.py:235
  45.4 10.9 %collective-permute-start.15 = (bf16[8,16,512]{2,1,0:T(8,128)(2,1)S(1)}, bf16[8,16,512]{2,1,0:T(8,128)(2,1)S(1)}, u32[]{:S(2)}, u32[]{:S(2)}) collective-permute-start(bf16[8,16,512]{2,1,0:T(8,128)(2,1)S(1)} %get-tuple-element.107), channel_id=1, source_target_pairs={{0,8},{4,12},{8,0},{12,4},{1,9},{5,13},{9,1},{13,5},{2,10},{6,14},... | collective-permute-start | bytes 393224 | tf_op jit(solution)/shard_map/ppermute | solution.py:235
  49.7 6.6 %collective-permute-start.16 = (bf16[8,16,512]{2,1,0:T(8,128)(2,1)S(1)}, bf16[8,16,512]{2,1,0:T(8,128)(2,1)S(1)}, u32[]{:S(2)}, u32[]{:S(2)}) collective-permute-start(bf16[8,16,512]{2,1,0:T(8,128)(2,1)S(1)} %get-tuple-element.108), channel_id=1, source_target_pairs={{0,4},{4,0},{8,12},{12,8},{1,5},{5,1},{9,13},{13,9},{2,6},{6,2},{1... | collective-permute-start | bytes 393224 | tf_op jit(solution)/shard_map/ppermute | solution.py:235
  53.4 2.9 %collective-permute-start.18 = (bf16[24,32,512]{2,1,0:T(8,128)(2,1)S(1)}, bf16[24,32,512]{2,1,0:T(8,128)(2,1)S(1)}, u32[]{:S(2)}, u32[]{:S(2)}) collective-permute-start(bf16[24,32,512]{2,1,0:T(8,128)(2,1)S(1)} %shard_map.76), channel_id=1, source_target_pairs={{0,1},{1,0},{2,3},{3,2},{4,5},{5,4},{6,7},{7,6},{8,9},{9,8},{10,11... | collective-permute-start | bytes 2359304 | tf_op jit(solution)/shard_map/ppermute | solution.py:284
  57.1 19.4 %collective-permute-start.19 = (bf16[8,32,512]{2,1,0:T(8,128)(2,1)S(1)}, bf16[8,32,512]{2,1,0:T(8,128)(2,1)S(1)}, u32[]{:S(2)}, u32[]{:S(2)}) collective-permute-start(bf16[8,32,512]{2,1,0:T(8,128)(2,1)S(1)} %shard_map.78), channel_id=1, source_target_pairs={{0,8},{4,12},{8,0},{12,4},{1,9},{5,13},{9,1},{13,5},{2,10},{6,14},... | collective-permute-start | bytes 786440 | tf_op jit(solution)/shard_map/ppermute | solution.py:235
  61.3 21.5 %collective-permute-start.20 = (bf16[8,32,512]{2,1,0:T(8,128)(2,1)S(1)}, bf16[8,32,512]{2,1,0:T(8,128)(2,1)S(1)}, u32[]{:S(2)}, u32[]{:S(2)}) collective-permute-start(bf16[8,32,512]{2,1,0:T(8,128)(2,1)S(1)} %get-tuple-element.132), channel_id=1, source_target_pairs={{0,12},{4,8},{8,4},{12,0},{1,13},{5,9},{9,5},{13,1},{2,14},{6,10},... | collective-permute-start | bytes 786440 | tf_op jit(solution)/shard_map/ppermute | solution.py:235
  62.1 20.7 %collective-permute-start.21 = (bf16[8,32,512]{2,1,0:T(8,128)(2,1)S(1)}, bf16[8,32,512]{2,1,0:T(8,128)(2,1)S(1)}, u32[]{:S(2)}, u32[]{:S(2)}) collective-permute-start(bf16[8,32,512]{2,1,0:T(8,128)(2,1)S(1)} %get-tuple-element.133), channel_id=1, source_target_pairs={{0,4},{4,0},{8,12},{12,8},{1,5},{5,1},{9,13},{13,9},{2,6},{6,2},{1... | collective-permute-start | bytes 786440 | tf_op jit(solution)/shard_map/ppermute | solution.py:235
  (2 other events, 11.2 us)

commit v25 on v24

--- a/solution.py
+++ b/solution.py
@@ -283,10 +283,10 @@
     here, stays, gone = fence((first[0], stays, gone))
     came = lax.ppermute(gone, "pol", other)
     kept = reduce(down, stays, (ROWS, 0, 0, 0), n_modes, jnp.float32)
-    first[3], first[2], first[1], kept = fence((first[3], first[2], first[1], kept))
-    first[3], first[2], first[1] = anchor([first[3], first[2], first[1]], 7_500_000_000)
+    first[2], first[3], first[1], kept = fence((first[2], first[3], first[1], kept))
+    first[2], first[3], first[1] = anchor([first[2], first[3], first[1]], 7_500_000_000)
     out_2, = restore(kept, came, ratios, up, [spots[1]])
-    out_2, first[3], first[2], first[1] = fence((out_2, first[3], first[2], first[1]))
+    out_2, first[2], first[3], first[1] = fence((out_2, first[2], first[3], first[1]))
     first[0] = here
     out_3, out_1, out_0 = restore(kept, came, ratios, up, [spots[2], spots[0], spots[3]])
     back = [swap_z(out, j) for out, j in ((out_2, 2), (out_3, 3), (out_1, 1))]

time: 84.6 us -> 85.8 us (1.014)
  waiting for transfers between devices: 25.7 us -> 28.2 us
  starting transfers between devices: 29.5 us -> 28.4 us
    ppermute x6, waiting for transfers between devices: 19.1 us -> 21.5 us  [swap_z(): return lax.ppermute(value, 'fm', [(i, i ^ j) for i in range(parts)])]
    ppermute x6, starting transfers between devices: 11 us -> 9.9 us  [swap_z(): return lax.ppermute(value, 'fm', [(i, i ^ j) for i in range(parts)])]
  transfers between devices with their start and end apart: 22 -> 22, of which waited for: 7 -> 8; matrix products, arithmetic and copies ran while one was open for 2% -> 2% of each run, Pallas kernels for 28% -> 27%
where the time goes in v25:
time: 85.8 us; the launch traced here: 85.6 us
  starting transfers between devices  28.4 us (33%)
  waiting for transfers between devices  28.2 us (33%)
  Pallas kernels  25.7 us (30%)
  local copies, waits for them, and re-layouts  2.39 us (3%)
  between operations  0.93 us (1%)
    ppermute x6, waiting for transfers between devices, swap_z(): return lax.ppermute(value, 'fm', [(i, i ^ j) for i in range(parts)])  21.5 us
    ppermute x6, starting transfers between devices, swap_z(): return lax.ppermute(value, 'fm', [(i, i ^ j) for i in range(parts)])  9.9 us
    pallas_call x7, Pallas kernels, project(): pl.pallas_call(functools.partial(project_kernel, piece=piece, blocks=bloc...  9.57 us
    ppermute x6, starting transfers between devices, shift_z(): lax.ppermute(value, 'fm', [(i, (i + j) % parts) for i in range(parts)])  9.33 us
    ppermute x8, starting transfers between devices, along_x(): return lax.ppermute(value, 'kl', other)  9.13 us
    pallas_call x1, Pallas kernels, hold(): pl.pallas_call(hold_kernel, grid_spec=pltpu.PrefetchScalarGridSpec(num_sc...  7.04 us
    ppermute x8, waiting for transfers between devices, along_x(): return lax.ppermute(value, 'kl', other)  4.17 us
    pallas_call x3, Pallas kernels, place(): pl.pallas_call(functools.partial(place_kernel, spots=spots, first=first),...  4.06 us
  transfers between devices with their start and end apart: 22, of which 8 were waited for; matrix products, arithmetic and copies ran while one was open for 2% of the time, Pallas kernels for 27%

profile of v25, /device:TPU:12, one launch (start us, length us, event | category | flops | bytes accessed | tf_op | source)
XLA Modules:
  0.0 85.6 jit_solution(13761557680758523249)
XLA Ops:
  1.1 2.7 %collective-permute-start = (bf16[8,16,512]{2,1,0:T(8,128)(2,1)S(1)}, bf16[8,16,512]{2,1,0:T(8,128)(2,1)S(1)}, u32[]{:S(2)}, u32[]{:S(2)}) collective-permute-start(bf16[8,16,512]{2,1,0:T(8,128)(2,1)S(1)} %get-tuple-element.146), channel_id=1, source_target_pairs={{0,8},{4,12},{8,0},{12,4},{1,9},{5,13},{9,1},{13,5},{2,10},{6,14},... | collective-permute-start | bytes 393224 | tf_op jit(solution)/shard_map/ppermute | solution.py:232
  3.8 2.0 %collective-permute-start.2 = (bf16[8,16,512]{2,1,0:T(8,128)(2,1)S(1)}, bf16[8,16,512]{2,1,0:T(8,128)(2,1)S(1)}, u32[]{:S(2)}, u32[]{:S(2)}) collective-permute-start(bf16[8,16,512]{2,1,0:T(8,128)(2,1)S(1)} %get-tuple-element.144), channel_id=1, source_target_pairs={{0,12},{4,0},{8,4},{12,8},{1,13},{5,1},{9,5},{13,9},{2,14},{6,2},{... | collective-permute-start | bytes 393224 | tf_op jit(solution)/shard_map/ppermute | solution.py:232
  6.8 1.6 %collective-permute-start.3 = (bf16[4,48,512]{2,1,0:T(8,128)(2,1)S(1)}, bf16[4,48,512]{2,1,0:T(8,128)(2,1)S(1)}, u32[]{:S(2)}, u32[]{:S(2)}) collective-permute-start(bf16[4,48,512]{2,1,0:T(8,128)(2,1)S(1)} %get-tuple-element.140.refs_0_), channel_id=1, source_target_pairs={{0,2},{2,0},{1,3},{3,1},{4,6},{6,4},{5,7},{7,5},{8,10},{10,8},{9,1... | collective-permute-start | bytes 589832 | tf_op jit(solution)/shard_map/ppermute | solution.py:238
  9.7 7.0 %shard_map.64 = (bf16[32,512,512]{2,1,0:T(8,128)(2,1)S(1)}, bf16[384,512]{1,0:T(8,128)(2,1)S(1)}, bf16[512,384]{1,0:T(8,128)(2,1)S(1)}) custom-call(s32[10]{0:T(128)S(1)} %compare_select_fusion.4.where, s32[4,4]{1,0:T(4,128)S(1)} %bitcast.27, s32[1]{0:T(128)S(6)} %copy.24.starts, bf16[32,512,512]{2,1,0:T(8,128)(2,1)} %bitcast.28, bf16[32,24]{1,0:T(8,128)(2,1)S(1)} %bitcast.26), custom_call_target="tpu_custom_call" | custom-call | flops 1024 | bytes 1024 | tf_op jit(solution)/shard_map/pallas_call | solution.py:63
  17.4 1.9 %collective-permute-start.5 = (bf16[8,32,512]{2,1,0:T(8,128)(2,1)S(1)}, bf16[8,32,512]{2,1,0:T(8,128)(2,1)S(1)}, u32[]{:S(2)}, u32[]{:S(2)}) collective-permute-start(bf16[8,32,512]{2,1,0:T(8,128)(2,1)S(1)} %get-tuple-element.75), channel_id=1, source_target_pairs={{0,12},{4,0},{8,4},{12,8},{1,13},{5,1},{9,5},{13,9},{2,14},{6,2},{... | collective-permute-start | bytes 786440 | tf_op jit(solution)/shard_map/ppermute | solution.py:232
  19.3 1.5 %collective-permute-start.6 = (bf16[8,16,512]{2,1,0:T(8,128)(2,1)S(1)}, bf16[8,16,512]{2,1,0:T(8,128)(2,1)S(1)}, u32[]{:S(2)}, u32[]{:S(2)}) collective-permute-start(bf16[8,16,512]{2,1,0:T(8,128)(2,1)S(1)} %collective-permute-done.1.refs_0_), channel_id=1, source_target_pairs={{0,2},{2,0},{1,3},{3,1},{4,6},{6,4},{5,7},{7,5},{8,10},{10,8},{9,1... | collective-permute-start | bytes 393224 | tf_op jit(solution)/shard_map/ppermute | solution.py:238
  21.3 1.5 %collective-permute-start.8 = (bf16[8,16,512]{2,1,0:T(8,128)(2,1)S(1)}, bf16[8,16,512]{2,1,0:T(8,128)(2,1)S(1)}, u32[]{:S(2)}, u32[]{:S(2)}) collective-permute-start(bf16[8,16,512]{2,1,0:T(8,128)(2,1)S(1)} %collective-permute-done.2.refs_0_), channel_id=1, source_target_pairs={{0,2},{2,0},{1,3},{3,1},{4,6},{6,4},{5,7},{7,5},{8,10},{10,8},{9,1... | collective-permute-start | bytes 393224 | tf_op jit(solution)/shard_map/ppermute | solution.py:238
  24.1 1.5 %collective-permute-done.6.refs_1_ = bf16[8,16,512]{2,1,0:T(8,128)(2,1)S(1)} collective-permute-done((bf16[8,16,512]{2,1,0:T(8,128)(2,1)S(1)}, bf16[8,16,512]{2,1,0:T(8,128)(2,1)S(1)}, u32[]{:S(2)}, u32[]{:S(2)}) %collective-permute-start.6) | collective-permute-done | bytes 131104 | tf_op jit(solution)/shard_map/ppermute | solution.py:238
  28.4 1.6 %collective-permute-start.13 = (bf16[8,32,512]{2,1,0:T(8,128)(2,1)S(1)}, bf16[8,32,512]{2,1,0:T(8,128)(2,1)S(1)}, u32[]{:S(2)}, u32[]{:S(2)}) collective-permute-start(bf16[8,32,512]{2,1,0:T(8,128)(2,1)S(1)} %collective-permute-done.10.refs_0_), channel_id=1, source_target_pairs={{0,2},{2,0},{1,3},{3,1},{4,6},{6,4},{5,7},{7,5},{8,10},{10,8},{9,1... | collective-permute-start | bytes 786440 | tf_op jit(solution)/shard_map/ppermute | solution.py:238
  31.7 1.4 %collective-permute-start.9 = (bf16[8,32,512]{2,1,0:T(8,128)(2,1)S(1)}, bf16[8,32,512]{2,1,0:T(8,128)(2,1)S(1)}, u32[]{:S(2)}, u32[]{:S(2)}) collective-permute-start(bf16[8,32,512]{2,1,0:T(8,128)(2,1)S(1)} %collective-permute-done.5.refs_0_), channel_id=1, source_target_pairs={{0,2},{2,0},{1,3},{3,1},{4,6},{6,4},{5,7},{7,5},{8,10},{10,8},{9,1... | collective-permute-start | bytes 786440 | tf_op jit(solution)/shard_map/ppermute | solution.py:238
  33.2 2.3 %collective-permute-start.11 = (bf16[8,32,512]{2,1,0:T(8,128)(2,1)S(1)}, bf16[8,32,512]{2,1,0:T(8,128)(2,1)S(1)}, u32[]{:S(2)}, u32[]{:S(2)}) collective-permute-start(bf16[8,32,512]{2,1,0:T(8,128)(2,1)S(1)} %get-tuple-element.94), channel_id=1, source_target_pairs={{0,8},{4,12},{8,0},{12,4},{1,9},{5,13},{9,1},{13,5},{2,10},{6,14},... | collective-permute-start | bytes 786440 | tf_op jit(solution)/shard_map/ppermute | solution.py:232
  35.5 1.6 %collective-permute-done.13.refs_0_ = bf16[8,32,512]{2,1,0:T(8,128)(2,1)S(1)} collective-permute-done((bf16[8,32,512]{2,1,0:T(8,128)(2,1)S(1)}, bf16[8,32,512]{2,1,0:T(8,128)(2,1)S(1)}, u32[]{:S(2)}, u32[]{:S(2)}) %collective-permute-start.13) | collective-permute-done | bytes 262176 | tf_op jit(solution)/shard_map/ppermute | solution.py:238
  37.5 1.4 %shard_map.73 = (bf16[8,32,512]{2,1,0:T(8,128)(2,1)S(1)}, bf16[8,32,512]{2,1,0:T(8,128)(2,1)S(1)}) custom-call(s32[10]{0:T(128)S(1)} %compare_select_fusion.4.where, bf16[8,32,512]{2,1,0:T(8,128)(2,1)S(1)} %collective-permute-done.10.refs_0_, bf16[8,32,512]{2,1,0:T(8,128)(2,1)S(1)} %shard_map.72.refs_1_, ...), custom_call_target="tpu_custom_call" | custom-call | flops 1024 | bytes 1024 | tf_op jit(solution)/shard_map/pallas_call | solution.py:102
  40.5 2.4 %collective-permute-done.11.refs_0_ = bf16[8,32,512]{2,1,0:T(8,128)(2,1)S(1)} collective-permute-done((bf16[8,32,512]{2,1,0:T(8,128)(2,1)S(1)}, bf16[8,32,512]{2,1,0:T(8,128)(2,1)S(1)}, u32[]{:S(2)}, u32[]{:S(2)}) %collective-permute-start.11) | collective-permute-done | bytes 262176 | tf_op jit(solution)/shard_map/ppermute | solution.py:232
  43.4 3.4 %collective-permute-start.14 = (bf16[8,16,512]{2,1,0:T(8,128)(2,1)S(1)}, bf16[8,16,512]{2,1,0:T(8,128)(2,1)S(1)}, u32[]{:S(2)}, u32[]{:S(2)}) collective-permute-start(bf16[8,16,512]{2,1,0:T(8,128)(2,1)S(1)} %get-tuple-element.106), channel_id=1, source_target_pairs={{0,8},{4,12},{8,0},{12,4},{1,9},{5,13},{9,1},{13,5},{2,10},{6,14},... | collective-permute-start | bytes 393224 | tf_op jit(solution)/shard_map/ppermute | solution.py:235
  46.8 2.0 %collective-permute-start.15 = (bf16[8,16,512]{2,1,0:T(8,128)(2,1)S(1)}, bf16[8,16,512]{2,1,0:T(8,128)(2,1)S(1)}, u32[]{:S(2)}, u32[]{:S(2)}) collective-permute-start(bf16[8,16,512]{2,1,0:T(8,128)(2,1)S(1)} %get-tuple-element.107), channel_id=1, source_target_pairs={{0,12},{4,8},{8,4},{12,0},{1,13},{5,9},{9,5},{13,1},{2,14},{6,10},... | collective-permute-start | bytes 393224 | tf_op jit(solution)/shard_map/ppermute | solution.py:235
  48.8 1.4 %shard_map.75 = (bf16[8,32,512]{2,1,0:T(8,128)(2,1)S(1)}, bf16[8,32,512]{2,1,0:T(8,128)(2,1)S(1)}) custom-call(s32[10]{0:T(128)S(1)} %compare_select_fusion.4.where, bf16[8,32,512]{2,1,0:T(8,128)(2,1)S(1)} %collective-permute-done.5.refs_0_, bf16[8,32,512]{2,1,0:T(8,128)(2,1)S(1)} %collective-permute-done.9.refs_1_, ...), custom_call_target="tpu_custom_call" | custom-call | flops 1024 | bytes 1024 | tf_op jit(solution)/shard_map/pallas_call | solution.py:102
  50.2 1.4 %shard_map.74 = (bf16[8,32,512]{2,1,0:T(8,128)(2,1)S(1)}, bf16[8,32,512]{2,1,0:T(8,128)(2,1)S(1)}) custom-call(s32[10]{0:T(128)S(1)} %compare_select_fusion.4.where, bf16[8,32,512]{2,1,0:T(8,128)(2,1)S(1)} %collective-permute-done.11.refs_0_, bf16[8,32,512]{2,1,0:T(8,128)(2,1)S(1)} %collective-permute-done.17.refs_1_, ...), custom_call_target="tpu_custom_call" | custom-call | flops 1024 | bytes 1024 | tf_op jit(solution)/shard_map/pallas_call | solution.py:102
  54.6 3.6 %collective-permute-done.15.refs_1_ = bf16[8,16,512]{2,1,0:T(8,128)(2,1)S(1)} collective-permute-done((bf16[8,16,512]{2,1,0:T(8,128)(2,1)S(1)}, bf16[8,16,512]{2,1,0:T(8,128)(2,1)S(1)}, u32[]{:S(2)}, u32[]{:S(2)}) %collective-permute-start.15) | collective-permute-done | bytes 131104 | tf_op jit(solution)/shard_map/ppermute | solution.py:235
  60.2 1.9 %collective-permute-start.20 = (bf16[8,32,512]{2,1,0:T(8,128)(2,1)S(1)}, bf16[8,32,512]{2,1,0:T(8,128)(2,1)S(1)}, u32[]{:S(2)}, u32[]{:S(2)}) collective-permute-start(bf16[8,32,512]{2,1,0:T(8,128)(2,1)S(1)} %get-tuple-element.132), channel_id=1, source_target_pairs={{0,12},{4,8},{8,4},{12,0},{1,13},{5,9},{9,5},{13,1},{2,14},{6,10},... | collective-permute-start | bytes 786440 | tf_op jit(solution)/shard_map/ppermute | solution.py:235
  62.1 2.5 %collective-permute-start.21 = (bf16[8,32,512]{2,1,0:T(8,128)(2,1)S(1)}, bf16[8,32,512]{2,1,0:T(8,128)(2,1)S(1)}, u32[]{:S(2)}, u32[]{:S(2)}) collective-permute-start(bf16[8,32,512]{2,1,0:T(8,128)(2,1)S(1)} %get-tuple-element.133), channel_id=1, source_target_pairs={{0,4},{4,0},{8,12},{12,8},{1,5},{5,1},{9,13},{13,9},{2,6},{6,2},{1... | collective-permute-start | bytes 786440 | tf_op jit(solution)/shard_map/ppermute | solution.py:235
  67.2 9.4 %collective-permute-done.19.refs_0_ = bf16[8,32,512]{2,1,0:T(8,128)(2,1)S(1)} collective-permute-done((bf16[8,32,512]{2,1,0:T(8,128)(2,1)S(1)}, bf16[8,32,512]{2,1,0:T(8,128)(2,1)S(1)}, u32[]{:S(2)}, u32[]{:S(2)}) %collective-permute-start.19) | collective-permute-done | bytes 262176 | tf_op jit(solution)/shard_map/ppermute | solution.py:235
  76.6 7.6 %collective-permute-done.20.refs_1_ = bf16[8,32,512]{2,1,0:T(8,128)(2,1)S(1)} collective-permute-done((bf16[8,32,512]{2,1,0:T(8,128)(2,1)S(1)}, bf16[8,32,512]{2,1,0:T(8,128)(2,1)S(1)}, u32[]{:S(2)}, u32[]{:S(2)}) %collective-permute-start.20) | collective-permute-done | bytes 262176 | tf_op jit(solution)/shard_map/ppermute | solution.py:235
  84.2 1.4 %shard_map.83 = bf16[8,4,48,512]{3,2,1,0:T(8,128)(2,1)} custom-call(s32[10]{0:T(128)S(1)} %compare_select_fusion.4.where, bf16[8,32,512]{2,1,0:T(8,128)(2,1)S(1)} %collective-permute-done.19.refs_0_, bf16[8,32,512]{2,1,0:T(8,128)(2,1)S(1)} %collective-permute-done.20.refs_1_, ...), custom_call_target="tpu_custom_call", output_to_operand_aliasing={{}: (4, {})} | custom-call | flops 1024 | bytes 1024 | tf_op jit(solution)/shard_map/pallas_call | solution.py:190
  (55 shorter events, 19.8 us)
Async XLA Ops:
  0.0 9.6 %copy-start.2 = (bf16[1,32,24]{1,2,0:T(8,128)(2,1)S(1)}, bf16[1,32,24]{1,2,0:T(8,128)(2,1)}, u32[]{:S(2)}) copy-start(bf16[1,32,24]{1,2,0:T(8,128)(2,1)} %param.10) | copy-start | bytes 4612
  0.0 9.7 %copy-start = (s32[1,4,4]{2,1,0:T(4,128)S(1)}, s32[1,4,4]{2,1,0:T(4,128)}, u32[]{:S(2)}) copy-start(s32[1,4,4]{2,1,0:T(4,128)} %param.8) | copy-start | bytes 196
  1.1 15.8 %collective-permute-start = (bf16[8,16,512]{2,1,0:T(8,128)(2,1)S(1)}, bf16[8,16,512]{2,1,0:T(8,128)(2,1)S(1)}, u32[]{:S(2)}, u32[]{:S(2)}) collective-permute-start(bf16[8,16,512]{2,1,0:T(8,128)(2,1)S(1)} %get-tuple-element.146), channel_id=1, source_target_pairs={{0,8},{4,12},{8,0},{12,4},{1,9},{5,13},{9,1},{13,5},{2,10},{6,14},... | collective-permute-start | bytes 393224 | tf_op jit(solution)/shard_map/ppermute | solution.py:232
  3.7 13.1 %collective-permute-start.1 = (bf16[8,16,512]{2,1,0:T(8,128)(2,1)S(1)}, bf16[8,16,512]{2,1,0:T(8,128)(2,1)S(1)}, u32[]{:S(2)}, u32[]{:S(2)}) collective-permute-start(bf16[8,16,512]{2,1,0:T(8,128)(2,1)S(1)} %get-tuple-element.145), channel_id=1, source_target_pairs={{0,4},{4,8},{8,12},{12,0},{1,5},{5,9},{9,13},{13,1},{2,6},{6,10},{... | collective-permute-start | bytes 393224 | tf_op jit(solution)/shard_map/ppermute | solution.py:232
  3.8 13.1 %collective-permute-start.2 = (bf16[8,16,512]{2,1,0:T(8,128)(2,1)S(1)}, bf16[8,16,512]{2,1,0:T(8,128)(2,1)S(1)}, u32[]{:S(2)}, u32[]{:S(2)}) collective-permute-start(bf16[8,16,512]{2,1,0:T(8,128)(2,1)S(1)} %get-tuple-element.144), channel_id=1, source_target_pairs={{0,12},{4,0},{8,4},{12,8},{1,13},{5,1},{9,5},{13,9},{2,14},{6,2},{... | collective-permute-start | bytes 393224 | tf_op jit(solution)/shard_map/ppermute | solution.py:232
  6.8 10.0 %collective-permute-start.3 = (bf16[4,48,512]{2,1,0:T(8,128)(2,1)S(1)}, bf16[4,48,512]{2,1,0:T(8,128)(2,1)S(1)}, u32[]{:S(2)}, u32[]{:S(2)}) collective-permute-start(bf16[4,48,512]{2,1,0:T(8,128)(2,1)S(1)} %get-tuple-element.140.refs_0_), channel_id=1, source_target_pairs={{0,2},{2,0},{1,3},{3,1},{4,6},{6,4},{5,7},{7,5},{8,10},{10,8},{9,1... | collective-permute-start | bytes 589832 | tf_op jit(solution)/shard_map/ppermute | solution.py:238
  8.4 8.5 %collective-permute-start.4 = (bf16[4,48,512]{2,1,0:T(8,128)(2,1)S(1)}, bf16[4,48,512]{2,1,0:T(8,128)(2,1)S(1)}, u32[]{:S(2)}, u32[]{:S(2)}) collective-permute-start(bf16[4,48,512]{2,1,0:T(8,128)(2,1)S(1)} %get-tuple-element.139.refs_1_), channel_id=1, source_target_pairs={{0,2},{2,0},{1,3},{3,1},{4,6},{6,4},{5,7},{7,5},{8,10},{10,8},{9,1... | collective-permute-start | bytes 589832 | tf_op jit(solution)/shard_map/ppermute | solution.py:238
  16.9 11.5 %collective-permute-start.10 = (bf16[8,32,512]{2,1,0:T(8,128)(2,1)S(1)}, bf16[8,32,512]{2,1,0:T(8,128)(2,1)S(1)}, u32[]{:S(2)}, u32[]{:S(2)}) collective-permute-start(bf16[8,32,512]{2,1,0:T(8,128)(2,1)S(1)} %get-tuple-element.93), channel_id=1, source_target_pairs={{0,4},{4,8},{8,12},{12,0},{1,5},{5,9},{9,13},{13,1},{2,6},{6,10},{... | collective-permute-start | bytes 786440 | tf_op jit(solution)/shard_map/ppermute | solution.py:232
  17.4 14.4 %collective-permute-start.5 = (bf16[8,32,512]{2,1,0:T(8,128)(2,1)S(1)}, bf16[8,32,512]{2,1,0:T(8,128)(2,1)S(1)}, u32[]{:S(2)}, u32[]{:S(2)}) collective-permute-start(bf16[8,32,512]{2,1,0:T(8,128)(2,1)S(1)} %get-tuple-element.75), channel_id=1, source_target_pairs={{0,12},{4,0},{8,4},{12,8},{1,13},{5,1},{9,5},{13,9},{2,14},{6,2},{... | collective-permute-start | bytes 786440 | tf_op jit(solution)/shard_map/ppermute | solution.py:232
  19.3 6.4 %collective-permute-start.6 = (bf16[8,16,512]{2,1,0:T(8,128)(2,1)S(1)}, bf16[8,16,512]{2,1,0:T(8,128)(2,1)S(1)}, u32[]{:S(2)}, u32[]{:S(2)}) collective-permute-start(bf16[8,16,512]{2,1,0:T(8,128)(2,1)S(1)} %collective-permute-done.1.refs_0_), channel_id=1, source_target_pairs={{0,2},{2,0},{1,3},{3,1},{4,6},{6,4},{5,7},{7,5},{8,10},{10,8},{9,1... | collective-permute-start | bytes 393224 | tf_op jit(solution)/shard_map/ppermute | solution.py:238
  20.8 6.3 %collective-permute-start.7 = (bf16[8,16,512]{2,1,0:T(8,128)(2,1)S(1)}, bf16[8,16,512]{2,1,0:T(8,128)(2,1)S(1)}, u32[]{:S(2)}, u32[]{:S(2)}) collective-permute-start(bf16[8,16,512]{2,1,0:T(8,128)(2,1)S(1)} %collective-permute-done.refs_0_), channel_id=1, source_target_pairs={{0,2},{2,0},{1,3},{3,1},{4,6},{6,4},{5,7},{7,5},{8,10},{10,8},{9,1... | collective-permute-start | bytes 393224 | tf_op jit(solution)/shard_map/ppermute | solution.py:238
  21.3 8.7 %collective-permute-start.8 = (bf16[8,16,512]{2,1,0:T(8,128)(2,1)S(1)}, bf16[8,16,512]{2,1,0:T(8,128)(2,1)S(1)}, u32[]{:S(2)}, u32[]{:S(2)}) collective-permute-start(bf16[8,16,512]{2,1,0:T(8,128)(2,1)S(1)} %collective-permute-done.2.refs_0_), channel_id=1, source_target_pairs={{0,2},{2,0},{1,3},{3,1},{4,6},{6,4},{5,7},{7,5},{8,10},{10,8},{9,1... | collective-permute-start | bytes 393224 | tf_op jit(solution)/shard_map/ppermute | solution.py:238
  28.4 8.7 %collective-permute-start.13 = (bf16[8,32,512]{2,1,0:T(8,128)(2,1)S(1)}, bf16[8,32,512]{2,1,0:T(8,128)(2,1)S(1)}, u32[]{:S(2)}, u32[]{:S(2)}) collective-permute-start(bf16[8,32,512]{2,1,0:T(8,128)(2,1)S(1)} %collective-permute-done.10.refs_0_), channel_id=1, source_target_pairs={{0,2},{2,0},{1,3},{3,1},{4,6},{6,4},{5,7},{7,5},{8,10},{10,8},{9,1... | collective-permute-start | bytes 786440 | tf_op jit(solution)/shard_map/ppermute | solution.py:238
  31.7 8.7 %collective-permute-start.9 = (bf16[8,32,512]{2,1,0:T(8,128)(2,1)S(1)}, bf16[8,32,512]{2,1,0:T(8,128)(2,1)S(1)}, u32[]{:S(2)}, u32[]{:S(2)}) collective-permute-start(bf16[8,32,512]{2,1,0:T(8,128)(2,1)S(1)} %collective-permute-done.5.refs_0_), channel_id=1, source_target_pairs={{0,2},{2,0},{1,3},{3,1},{4,6},{6,4},{5,7},{7,5},{8,10},{10,8},{9,1... | collective-permute-start | bytes 786440 | tf_op jit(solution)/shard_map/ppermute | solution.py:238
  33.2 9.7 %collective-permute-start.11 = (bf16[8,32,512]{2,1,0:T(8,128)(2,1)S(1)}, bf16[8,32,512]{2,1,0:T(8,128)(2,1)S(1)}, u32[]{:S(2)}, u32[]{:S(2)}) collective-permute-start(bf16[8,32,512]{2,1,0:T(8,128)(2,1)S(1)} %get-tuple-element.94), channel_id=1, source_target_pairs={{0,8},{4,12},{8,0},{12,4},{1,9},{5,13},{9,1},{13,5},{2,10},{6,14},... | collective-permute-start | bytes 786440 | tf_op jit(solution)/shard_map/ppermute | solution.py:232
  35.5 3.4 %collective-permute-start.12 = (bf16[24,16,512]{2,1,0:T(8,128)(2,1)S(1)}, bf16[24,16,512]{2,1,0:T(8,128)(2,1)S(1)}, u32[]{:S(2)}, u32[]{:S(2)}) collective-permute-start(bf16[24,16,512]{2,1,0:T(8,128)(2,1)S(1)} %shard_map.69), channel_id=1, source_target_pairs={{0,1},{1,0},{2,3},{3,2},{4,5},{5,4},{6,7},{7,6},{8,9},{9,8},{10,11... | collective-permute-start | bytes 1179656 | tf_op jit(solution)/shard_map/ppermute | solution.py:273
  42.9 7.3 %collective-permute-start.17 = (bf16[8,32,512]{2,1,0:T(8,128)(2,1)S(1)}, bf16[8,32,512]{2,1,0:T(8,128)(2,1)S(1)}, u32[]{:S(2)}, u32[]{:S(2)}) collective-permute-start(bf16[8,32,512]{2,1,0:T(8,128)(2,1)S(1)} %collective-permute-done.11.refs_0_), channel_id=1, source_target_pairs={{0,2},{2,0},{1,3},{3,1},{4,6},{6,4},{5,7},{7,5},{8,10},{10,8},{9,1... | collective-permute-start | bytes 786440 | tf_op jit(solution)/shard_map/ppermute | solution.py:238
  43.4 11.2 %collective-permute-start.14 = (bf16[8,16,512]{2,1,0:T(8,128)(2,1)S(1)}, bf16[8,16,512]{2,1,0:T(8,128)(2,1)S(1)}, u32[]{:S(2)}, u32[]{:S(2)}) collective-permute-start(bf16[8,16,512]{2,1,0:T(8,128)(2,1)S(1)} %get-tuple-element.106), channel_id=1, source_target_pairs={{0,8},{4,12},{8,0},{12,4},{1,9},{5,13},{9,1},{13,5},{2,10},{6,14},... | collective-permute-start | bytes 393224 | tf_op jit(solution)/shard_map/ppermute | solution.py:235
  46.8 11.4 %collective-permute-start.15 = (bf16[8,16,512]{2,1,0:T(8,128)(2,1)S(1)}, bf16[8,16,512]{2,1,0:T(8,128)(2,1)S(1)}, u32[]{:S(2)}, u32[]{:S(2)}) collective-permute-start(bf16[8,16,512]{2,1,0:T(8,128)(2,1)S(1)} %get-tuple-element.107), channel_id=1, source_target_pairs={{0,12},{4,8},{8,4},{12,0},{1,13},{5,9},{9,5},{13,1},{2,14},{6,10},... | collective-permute-start | bytes 393224 | tf_op jit(solution)/shard_map/ppermute | solution.py:235
  48.8 9.3 %collective-permute-start.16 = (bf16[8,16,512]{2,1,0:T(8,128)(2,1)S(1)}, bf16[8,16,512]{2,1,0:T(8,128)(2,1)S(1)}, u32[]{:S(2)}, u32[]{:S(2)}) collective-permute-start(bf16[8,16,512]{2,1,0:T(8,128)(2,1)S(1)} %get-tuple-element.108), channel_id=1, source_target_pairs={{0,4},{4,0},{8,12},{12,8},{1,5},{5,1},{9,13},{13,9},{2,6},{6,2},{1... | collective-permute-start | bytes 393224 | tf_op jit(solution)/shard_map/ppermute | solution.py:235
  52.5 5.6 %collective-permute-start.18 = (bf16[24,32,512]{2,1,0:T(8,128)(2,1)S(1)}, bf16[24,32,512]{2,1,0:T(8,128)(2,1)S(1)}, u32[]{:S(2)}, u32[]{:S(2)}) collective-permute-start(bf16[24,32,512]{2,1,0:T(8,128)(2,1)S(1)} %shard_map.76), channel_id=1, source_target_pairs={{0,1},{1,0},{2,3},{3,2},{4,5},{5,4},{6,7},{7,6},{8,9},{9,8},{10,11... | collective-permute-start | bytes 2359304 | tf_op jit(solution)/shard_map/ppermute | solution.py:284
  59.0 17.6 %collective-permute-start.19 = (bf16[8,32,512]{2,1,0:T(8,128)(2,1)S(1)}, bf16[8,32,512]{2,1,0:T(8,128)(2,1)S(1)}, u32[]{:S(2)}, u32[]{:S(2)}) collective-permute-start(bf16[8,32,512]{2,1,0:T(8,128)(2,1)S(1)} %shard_map.78), channel_id=1, source_target_pairs={{0,8},{4,12},{8,0},{12,4},{1,9},{5,13},{9,1},{13,5},{2,10},{6,14},... | collective-permute-start | bytes 786440 | tf_op jit(solution)/shard_map/ppermute | solution.py:235
  60.2 24.0 %collective-permute-start.20 = (bf16[8,32,512]{2,1,0:T(8,128)(2,1)S(1)}, bf16[8,32,512]{2,1,0:T(8,128)(2,1)S(1)}, u32[]{:S(2)}, u32[]{:S(2)}) collective-permute-start(bf16[8,32,512]{2,1,0:T(8,128)(2,1)S(1)} %get-tuple-element.132), channel_id=1, source_target_pairs={{0,12},{4,8},{8,4},{12,0},{1,13},{5,9},{9,5},{13,1},{2,14},{6,10},... | collective-permute-start | bytes 786440 | tf_op jit(solution)/shard_map/ppermute | solution.py:235
  62.1 22.1 %collective-permute-start.21 = (bf16[8,32,512]{2,1,0:T(8,128)(2,1)S(1)}, bf16[8,32,512]{2,1,0:T(8,128)(2,1)S(1)}, u32[]{:S(2)}, u32[]{:S(2)}) collective-permute-start(bf16[8,32,512]{2,1,0:T(8,128)(2,1)S(1)} %get-tuple-element.133), channel_id=1, source_target_pairs={{0,4},{4,0},{8,12},{12,8},{1,5},{5,1},{9,13},{13,9},{2,6},{6,2},{1... | collective-permute-start | bytes 786440 | tf_op jit(solution)/shard_map/ppermute | solution.py:235
  (2 other events, 11.2 us)

commit v26 on v24

--- a/solution.py
+++ b/solution.py
@@ -174,8 +174,11 @@
     pieces, out, sems = refs[:count], refs[-2], refs[-1]
     rows = pieces[0].shape[1]
     copies = [
-        pltpu.make_async_copy(pieces[n], out.at[low:high, where[PARTS + 2 + j], first:first + rows, :], sems.at[n])
+        pltpu.make_async_copy(
+            pieces[n].at[f], out.at[low + f, where[PARTS + 2 + j], first:first + rows, :], sems.at[n, f]
+        )
         for n, (j, low, high) in enumerate(spots)
+        for f in range(high - low)
     ]
     for copy in copies:
         copy.start()
@@ -194,7 +197,7 @@
             grid=(),
             in_specs=[pl.BlockSpec(memory_space=pltpu.VMEM)] * count + [anywhere] * len(extra),
             out_specs=anywhere,
-            scratch_shapes=[pltpu.SemaphoreType.DMA((count,))],
+            scratch_shapes=[pltpu.SemaphoreType.DMA((count, shape[0]))],
         ),
         out_shape=jax.ShapeDtypeStruct(shape, jnp.bfloat16),
         input_output_aliases={count + 1: 0} if extra else {},

time: 84.6 us -> 84.8 us (level)
  no operation moved by 1% of the time
where the time goes in v26:
time: 84.8 us; the launch traced here: 84.4 us
  starting transfers between devices  29.5 us (35%)
  Pallas kernels  26.1 us (31%)
  waiting for transfers between devices  25.4 us (30%)
  local copies, waits for them, and re-layouts  2.39 us (3%)
  between operations  0.93 us (1%)
    ppermute x6, waiting for transfers between devices, swap_z(): return lax.ppermute(value, 'fm', [(i, i ^ j) for i in range(parts)])  18.8 us
    ppermute x6, starting transfers between devices, swap_z(): return lax.ppermute(value, 'fm', [(i, i ^ j) for i in range(parts)])  11 us
    pallas_call x7, Pallas kernels, project(): pl.pallas_call(functools.partial(project_kernel, piece=piece, blocks=bloc...  9.57 us
    ppermute x6, starting transfers between devices, shift_z(): lax.ppermute(value, 'fm', [(i, (i + j) % parts) for i in range(parts)])  9.33 us
    ppermute x8, starting transfers between devices, along_x(): return lax.ppermute(value, 'kl', other)  9.13 us
    pallas_call x1, Pallas kernels, hold(): pl.pallas_call(hold_kernel, grid_spec=pltpu.PrefetchScalarGridSpec(num_sc...  7.04 us
    pallas_call x3, Pallas kernels, place(): pl.pallas_call(functools.partial(place_kernel, spots=spots, first=first),...  4.52 us
    ppermute x8, waiting for transfers between devices, along_x(): return lax.ppermute(value, 'kl', other)  4.17 us
  transfers between devices with their start and end apart: 22, of which 7 were waited for; matrix products, arithmetic and copies ran while one was open for 2% of the time, Pallas kernels for 28%

profile of v26, /device:TPU:12, one launch (start us, length us, event | category | flops | bytes accessed | tf_op | source)
XLA Modules:
  0.0 84.4 jit_solution(12031798662990073521)
XLA Ops:
  1.1 2.7 %collective-permute-start = (bf16[8,16,512]{2,1,0:T(8,128)(2,1)S(1)}, bf16[8,16,512]{2,1,0:T(8,128)(2,1)S(1)}, u32[]{:S(2)}, u32[]{:S(2)}) collective-permute-start(bf16[8,16,512]{2,1,0:T(8,128)(2,1)S(1)} %get-tuple-element.146), channel_id=1, source_target_pairs={{0,8},{4,12},{8,0},{12,4},{1,9},{5,13},{9,1},{13,5},{2,10},{6,14},... | collective-permute-start | bytes 393224 | tf_op jit(solution)/shard_map/ppermute | solution.py:235
  3.8 2.0 %collective-permute-start.2 = (bf16[8,16,512]{2,1,0:T(8,128)(2,1)S(1)}, bf16[8,16,512]{2,1,0:T(8,128)(2,1)S(1)}, u32[]{:S(2)}, u32[]{:S(2)}) collective-permute-start(bf16[8,16,512]{2,1,0:T(8,128)(2,1)S(1)} %get-tuple-element.144), channel_id=1, source_target_pairs={{0,12},{4,0},{8,4},{12,8},{1,13},{5,1},{9,5},{13,9},{2,14},{6,2},{... | collective-permute-start | bytes 393224 | tf_op jit(solution)/shard_map/ppermute | solution.py:235
  6.8 1.6 %collective-permute-start.3 = (bf16[4,48,512]{2,1,0:T(8,128)(2,1)S(1)}, bf16[4,48,512]{2,1,0:T(8,128)(2,1)S(1)}, u32[]{:S(2)}, u32[]{:S(2)}) collective-permute-start(bf16[4,48,512]{2,1,0:T(8,128)(2,1)S(1)} %get-tuple-element.140.refs_0_), channel_id=1, source_target_pairs={{0,2},{2,0},{1,3},{3,1},{4,6},{6,4},{5,7},{7,5},{8,10},{10,8},{9,1... | collective-permute-start | bytes 589832 | tf_op jit(solution)/shard_map/ppermute | solution.py:241
  9.7 7.0 %shard_map.64 = (bf16[32,512,512]{2,1,0:T(8,128)(2,1)S(1)}, bf16[384,512]{1,0:T(8,128)(2,1)S(1)}, bf16[512,384]{1,0:T(8,128)(2,1)S(1)}) custom-call(s32[10]{0:T(128)S(1)} %compare_select_fusion.4.where, s32[4,4]{1,0:T(4,128)S(1)} %bitcast.27, s32[1]{0:T(128)S(6)} %copy.24.starts, bf16[32,512,512]{2,1,0:T(8,128)(2,1)} %bitcast.28, bf16[32,24]{1,0:T(8,128)(2,1)S(1)} %bitcast.26), custom_call_target="tpu_custom_call" | custom-call | flops 1024 | bytes 1024 | tf_op jit(solution)/shard_map/pallas_call | solution.py:63
  17.4 1.9 %collective-permute-start.5 = (bf16[8,32,512]{2,1,0:T(8,128)(2,1)S(1)}, bf16[8,32,512]{2,1,0:T(8,128)(2,1)S(1)}, u32[]{:S(2)}, u32[]{:S(2)}) collective-permute-start(bf16[8,32,512]{2,1,0:T(8,128)(2,1)S(1)} %get-tuple-element.75), channel_id=1, source_target_pairs={{0,12},{4,0},{8,4},{12,8},{1,13},{5,1},{9,5},{13,9},{2,14},{6,2},{... | collective-permute-start | bytes 786440 | tf_op jit(solution)/shard_map/ppermute | solution.py:235
  19.3 1.5 %collective-permute-start.6 = (bf16[8,16,512]{2,1,0:T(8,128)(2,1)S(1)}, bf16[8,16,512]{2,1,0:T(8,128)(2,1)S(1)}, u32[]{:S(2)}, u32[]{:S(2)}) collective-permute-start(bf16[8,16,512]{2,1,0:T(8,128)(2,1)S(1)} %collective-permute-done.1.refs_0_), channel_id=1, source_target_pairs={{0,2},{2,0},{1,3},{3,1},{4,6},{6,4},{5,7},{7,5},{8,10},{10,8},{9,1... | collective-permute-start | bytes 393224 | tf_op jit(solution)/shard_map/ppermute | solution.py:241
  21.3 1.5 %collective-permute-start.8 = (bf16[8,16,512]{2,1,0:T(8,128)(2,1)S(1)}, bf16[8,16,512]{2,1,0:T(8,128)(2,1)S(1)}, u32[]{:S(2)}, u32[]{:S(2)}) collective-permute-start(bf16[8,16,512]{2,1,0:T(8,128)(2,1)S(1)} %collective-permute-done.2.refs_0_), channel_id=1, source_target_pairs={{0,2},{2,0},{1,3},{3,1},{4,6},{6,4},{5,7},{7,5},{8,10},{10,8},{9,1... | collective-permute-start | bytes 393224 | tf_op jit(solution)/shard_map/ppermute | solution.py:241
  24.1 1.5 %collective-permute-done.6.refs_1_ = bf16[8,16,512]{2,1,0:T(8,128)(2,1)S(1)} collective-permute-done((bf16[8,16,512]{2,1,0:T(8,128)(2,1)S(1)}, bf16[8,16,512]{2,1,0:T(8,128)(2,1)S(1)}, u32[]{:S(2)}, u32[]{:S(2)}) %collective-permute-start.6) | collective-permute-done | bytes 131104 | tf_op jit(solution)/shard_map/ppermute | solution.py:241
  28.4 1.6 %collective-permute-start.13 = (bf16[8,32,512]{2,1,0:T(8,128)(2,1)S(1)}, bf16[8,32,512]{2,1,0:T(8,128)(2,1)S(1)}, u32[]{:S(2)}, u32[]{:S(2)}) collective-permute-start(bf16[8,32,512]{2,1,0:T(8,128)(2,1)S(1)} %collective-permute-done.10.refs_0_), channel_id=1, source_target_pairs={{0,2},{2,0},{1,3},{3,1},{4,6},{6,4},{5,7},{7,5},{8,10},{10,8},{9,1... | collective-permute-start | bytes 786440 | tf_op jit(solution)/shard_map/ppermute | solution.py:241
  31.7 1.4 %collective-permute-start.9 = (bf16[8,32,512]{2,1,0:T(8,128)(2,1)S(1)}, bf16[8,32,512]{2,1,0:T(8,128)(2,1)S(1)}, u32[]{:S(2)}, u32[]{:S(2)}) collective-permute-start(bf16[8,32,512]{2,1,0:T(8,128)(2,1)S(1)} %collective-permute-done.5.refs_0_), channel_id=1, source_target_pairs={{0,2},{2,0},{1,3},{3,1},{4,6},{6,4},{5,7},{7,5},{8,10},{10,8},{9,1... | collective-permute-start | bytes 786440 | tf_op jit(solution)/shard_map/ppermute | solution.py:241
  33.2 2.3 %collective-permute-start.11 = (bf16[8,32,512]{2,1,0:T(8,128)(2,1)S(1)}, bf16[8,32,512]{2,1,0:T(8,128)(2,1)S(1)}, u32[]{:S(2)}, u32[]{:S(2)}) collective-permute-start(bf16[8,32,512]{2,1,0:T(8,128)(2,1)S(1)} %get-tuple-element.94), channel_id=1, source_target_pairs={{0,8},{4,12},{8,0},{12,4},{1,9},{5,13},{9,1},{13,5},{2,10},{6,14},... | collective-permute-start | bytes 786440 | tf_op jit(solution)/shard_map/ppermute | solution.py:235
  35.5 1.6 %collective-permute-done.13.refs_0_ = bf16[8,32,512]{2,1,0:T(8,128)(2,1)S(1)} collective-permute-done((bf16[8,32,512]{2,1,0:T(8,128)(2,1)S(1)}, bf16[8,32,512]{2,1,0:T(8,128)(2,1)S(1)}, u32[]{:S(2)}, u32[]{:S(2)}) %collective-permute-start.13) | collective-permute-done | bytes 262176 | tf_op jit(solution)/shard_map/ppermute | solution.py:241
  37.5 1.4 %shard_map.73 = (bf16[8,32,512]{2,1,0:T(8,128)(2,1)S(1)}, bf16[8,32,512]{2,1,0:T(8,128)(2,1)S(1)}) custom-call(s32[10]{0:T(128)S(1)} %compare_select_fusion.4.where, bf16[8,32,512]{2,1,0:T(8,128)(2,1)S(1)} %collective-permute-done.10.refs_0_, bf16[8,32,512]{2,1,0:T(8,128)(2,1)S(1)} %shard_map.72.refs_1_, ...), custom_call_target="tpu_custom_call" | custom-call | flops 1024 | bytes 1024 | tf_op jit(solution)/shard_map/pallas_call | solution.py:102
  40.5 2.4 %collective-permute-done.11.refs_0_ = bf16[8,32,512]{2,1,0:T(8,128)(2,1)S(1)} collective-permute-done((bf16[8,32,512]{2,1,0:T(8,128)(2,1)S(1)}, bf16[8,32,512]{2,1,0:T(8,128)(2,1)S(1)}, u32[]{:S(2)}, u32[]{:S(2)}) %collective-permute-start.11) | collective-permute-done | bytes 262176 | tf_op jit(solution)/shard_map/ppermute | solution.py:235
  43.4 2.0 %collective-permute-start.14 = (bf16[8,16,512]{2,1,0:T(8,128)(2,1)S(1)}, bf16[8,16,512]{2,1,0:T(8,128)(2,1)S(1)}, u32[]{:S(2)}, u32[]{:S(2)}) collective-permute-start(bf16[8,16,512]{2,1,0:T(8,128)(2,1)S(1)} %get-tuple-element.106), channel_id=1, source_target_pairs={{0,12},{4,8},{8,4},{12,0},{1,13},{5,9},{9,5},{13,1},{2,14},{6,10},... | collective-permute-start | bytes 393224 | tf_op jit(solution)/shard_map/ppermute | solution.py:238
  45.4 4.3 %collective-permute-start.15 = (bf16[8,16,512]{2,1,0:T(8,128)(2,1)S(1)}, bf16[8,16,512]{2,1,0:T(8,128)(2,1)S(1)}, u32[]{:S(2)}, u32[]{:S(2)}) collective-permute-start(bf16[8,16,512]{2,1,0:T(8,128)(2,1)S(1)} %get-tuple-element.107), channel_id=1, source_target_pairs={{0,8},{4,12},{8,0},{12,4},{1,9},{5,13},{9,1},{13,5},{2,10},{6,14},... | collective-permute-start | bytes 393224 | tf_op jit(solution)/shard_map/ppermute | solution.py:238
  49.7 1.4 %shard_map.75 = (bf16[8,32,512]{2,1,0:T(8,128)(2,1)S(1)}, bf16[8,32,512]{2,1,0:T(8,128)(2,1)S(1)}) custom-call(s32[10]{0:T(128)S(1)} %compare_select_fusion.4.where, bf16[8,32,512]{2,1,0:T(8,128)(2,1)S(1)} %collective-permute-done.5.refs_0_, bf16[8,32,512]{2,1,0:T(8,128)(2,1)S(1)} %collective-permute-done.9.refs_1_, ...), custom_call_target="tpu_custom_call" | custom-call | flops 1024 | bytes 1024 | tf_op jit(solution)/shard_map/pallas_call | solution.py:102
  51.1 1.4 %shard_map.74 = (bf16[8,32,512]{2,1,0:T(8,128)(2,1)S(1)}, bf16[8,32,512]{2,1,0:T(8,128)(2,1)S(1)}) custom-call(s32[10]{0:T(128)S(1)} %compare_select_fusion.4.where, bf16[8,32,512]{2,1,0:T(8,128)(2,1)S(1)} %collective-permute-done.11.refs_0_, bf16[8,32,512]{2,1,0:T(8,128)(2,1)S(1)} %collective-permute-done.17.refs_1_, ...), custom_call_target="tpu_custom_call" | custom-call | flops 1024 | bytes 1024 | tf_op jit(solution)/shard_map/pallas_call | solution.py:102
  54.5 1.8 %collective-permute-done.15.refs_1_ = bf16[8,16,512]{2,1,0:T(8,128)(2,1)S(1)} collective-permute-done((bf16[8,16,512]{2,1,0:T(8,128)(2,1)S(1)}, bf16[8,16,512]{2,1,0:T(8,128)(2,1)S(1)}, u32[]{:S(2)}, u32[]{:S(2)}) %collective-permute-start.15) | collective-permute-done | bytes 131104 | tf_op jit(solution)/shard_map/ppermute | solution.py:238
  57.1 3.1 %collective-permute-start.19 = (bf16[8,32,512]{2,1,0:T(8,128)(2,1)S(1)}, bf16[8,32,512]{2,1,0:T(8,128)(2,1)S(1)}, u32[]{:S(2)}, u32[]{:S(2)}) collective-permute-start(bf16[8,32,512]{2,1,0:T(8,128)(2,1)S(1)} %shard_map.78), channel_id=1, source_target_pairs={{0,8},{4,12},{8,0},{12,4},{1,9},{5,13},{9,1},{13,5},{2,10},{6,14},... | collective-permute-start | bytes 786440 | tf_op jit(solution)/shard_map/ppermute | solution.py:238
  62.9 1.6 %shard_map.81.refs_1_ = bf16[8,4,48,512]{3,2,1,0:T(8,128)(2,1)} custom-call(s32[10]{0:T(128)S(1)} %compare_select_fusion.4.where, bf16[8,16,512]{2,1,0:T(8,128)(2,1)S(1)} %get-tuple-element.135.refs_0_, bf16[8,16,512]{2,1,0:T(8,128)(2,1)S(1)} %get-tuple-element.136.refs_1_, bf16[8,16,512]{2,1,0:T(8,128)(2,1)S(1)} %get-tuple-element.137.refs_2_, ...), custom_call_target="tpu_custom_call" | custom-call | flops 1024 | bytes 1024 | tf_op jit(solution)/shard_map/pallas_call | solution.py:193
  65.8 10.7 %collective-permute-done.19.refs_0_ = bf16[8,32,512]{2,1,0:T(8,128)(2,1)S(1)} collective-permute-done((bf16[8,32,512]{2,1,0:T(8,128)(2,1)S(1)}, bf16[8,32,512]{2,1,0:T(8,128)(2,1)S(1)}, u32[]{:S(2)}, u32[]{:S(2)}) %collective-permute-start.19) | collective-permute-done | bytes 262176 | tf_op jit(solution)/shard_map/ppermute | solution.py:238
  76.5 6.3 %collective-permute-done.20.refs_1_ = bf16[8,32,512]{2,1,0:T(8,128)(2,1)S(1)} collective-permute-done((bf16[8,32,512]{2,1,0:T(8,128)(2,1)S(1)}, bf16[8,32,512]{2,1,0:T(8,128)(2,1)S(1)}, u32[]{:S(2)}, u32[]{:S(2)}) %collective-permute-start.20) | collective-permute-done | bytes 262176 | tf_op jit(solution)/shard_map/ppermute | solution.py:238
  82.8 1.6 %shard_map.83 = bf16[8,4,48,512]{3,2,1,0:T(8,128)(2,1)} custom-call(s32[10]{0:T(128)S(1)} %compare_select_fusion.4.where, bf16[8,32,512]{2,1,0:T(8,128)(2,1)S(1)} %collective-permute-done.19.refs_0_, bf16[8,32,512]{2,1,0:T(8,128)(2,1)S(1)} %collective-permute-done.20.refs_1_, ...), custom_call_target="tpu_custom_call", output_to_operand_aliasing={{}: (4, {})} | custom-call | flops 1024 | bytes 1024 | tf_op jit(solution)/shard_map/pallas_call | solution.py:193
  (55 shorter events, 18.9 us)
Async XLA Ops:
  0.0 9.6 %copy-start.2 = (bf16[1,32,24]{1,2,0:T(8,128)(2,1)S(1)}, bf16[1,32,24]{1,2,0:T(8,128)(2,1)}, u32[]{:S(2)}) copy-start(bf16[1,32,24]{1,2,0:T(8,128)(2,1)} %param.10) | copy-start | bytes 4612
  0.0 9.7 %copy-start = (s32[1,4,4]{2,1,0:T(4,128)S(1)}, s32[1,4,4]{2,1,0:T(4,128)}, u32[]{:S(2)}) copy-start(s32[1,4,4]{2,1,0:T(4,128)} %param.8) | copy-start | bytes 196
  1.1 15.8 %collective-permute-start = (bf16[8,16,512]{2,1,0:T(8,128)(2,1)S(1)}, bf16[8,16,512]{2,1,0:T(8,128)(2,1)S(1)}, u32[]{:S(2)}, u32[]{:S(2)}) collective-permute-start(bf16[8,16,512]{2,1,0:T(8,128)(2,1)S(1)} %get-tuple-element.146), channel_id=1, source_target_pairs={{0,8},{4,12},{8,0},{12,4},{1,9},{5,13},{9,1},{13,5},{2,10},{6,14},... | collective-permute-start | bytes 393224 | tf_op jit(solution)/shard_map/ppermute | solution.py:235
  3.7 13.1 %collective-permute-start.1 = (bf16[8,16,512]{2,1,0:T(8,128)(2,1)S(1)}, bf16[8,16,512]{2,1,0:T(8,128)(2,1)S(1)}, u32[]{:S(2)}, u32[]{:S(2)}) collective-permute-start(bf16[8,16,512]{2,1,0:T(8,128)(2,1)S(1)} %get-tuple-element.145), channel_id=1, source_target_pairs={{0,4},{4,8},{8,12},{12,0},{1,5},{5,9},{9,13},{13,1},{2,6},{6,10},{... | collective-permute-start | bytes 393224 | tf_op jit(solution)/shard_map/ppermute | solution.py:235
  3.8 13.1 %collective-permute-start.2 = (bf16[8,16,512]{2,1,0:T(8,128)(2,1)S(1)}, bf16[8,16,512]{2,1,0:T(8,128)(2,1)S(1)}, u32[]{:S(2)}, u32[]{:S(2)}) collective-permute-start(bf16[8,16,512]{2,1,0:T(8,128)(2,1)S(1)} %get-tuple-element.144), channel_id=1, source_target_pairs={{0,12},{4,0},{8,4},{12,8},{1,13},{5,1},{9,5},{13,9},{2,14},{6,2},{... | collective-permute-start | bytes 393224 | tf_op jit(solution)/shard_map/ppermute | solution.py:235
  6.8 10.0 %collective-permute-start.3 = (bf16[4,48,512]{2,1,0:T(8,128)(2,1)S(1)}, bf16[4,48,512]{2,1,0:T(8,128)(2,1)S(1)}, u32[]{:S(2)}, u32[]{:S(2)}) collective-permute-start(bf16[4,48,512]{2,1,0:T(8,128)(2,1)S(1)} %get-tuple-element.140.refs_0_), channel_id=1, source_target_pairs={{0,2},{2,0},{1,3},{3,1},{4,6},{6,4},{5,7},{7,5},{8,10},{10,8},{9,1... | collective-permute-start | bytes 589832 | tf_op jit(solution)/shard_map/ppermute | solution.py:241
  8.4 8.5 %collective-permute-start.4 = (bf16[4,48,512]{2,1,0:T(8,128)(2,1)S(1)}, bf16[4,48,512]{2,1,0:T(8,128)(2,1)S(1)}, u32[]{:S(2)}, u32[]{:S(2)}) collective-permute-start(bf16[4,48,512]{2,1,0:T(8,128)(2,1)S(1)} %get-tuple-element.139.refs_1_), channel_id=1, source_target_pairs={{0,2},{2,0},{1,3},{3,1},{4,6},{6,4},{5,7},{7,5},{8,10},{10,8},{9,1... | collective-permute-start | bytes 589832 | tf_op jit(solution)/shard_map/ppermute | solution.py:241
  16.9 11.5 %collective-permute-start.10 = (bf16[8,32,512]{2,1,0:T(8,128)(2,1)S(1)}, bf16[8,32,512]{2,1,0:T(8,128)(2,1)S(1)}, u32[]{:S(2)}, u32[]{:S(2)}) collective-permute-start(bf16[8,32,512]{2,1,0:T(8,128)(2,1)S(1)} %get-tuple-element.93), channel_id=1, source_target_pairs={{0,4},{4,8},{8,12},{12,0},{1,5},{5,9},{9,13},{13,1},{2,6},{6,10},{... | collective-permute-start | bytes 786440 | tf_op jit(solution)/shard_map/ppermute | solution.py:235
  17.4 14.4 %collective-permute-start.5 = (bf16[8,32,512]{2,1,0:T(8,128)(2,1)S(1)}, bf16[8,32,512]{2,1,0:T(8,128)(2,1)S(1)}, u32[]{:S(2)}, u32[]{:S(2)}) collective-permute-start(bf16[8,32,512]{2,1,0:T(8,128)(2,1)S(1)} %get-tuple-element.75), channel_id=1, source_target_pairs={{0,12},{4,0},{8,4},{12,8},{1,13},{5,1},{9,5},{13,9},{2,14},{6,2},{... | collective-permute-start | bytes 786440 | tf_op jit(solution)/shard_map/ppermute | solution.py:235
  19.3 6.4 %collective-permute-start.6 = (bf16[8,16,512]{2,1,0:T(8,128)(2,1)S(1)}, bf16[8,16,512]{2,1,0:T(8,128)(2,1)S(1)}, u32[]{:S(2)}, u32[]{:S(2)}) collective-permute-start(bf16[8,16,512]{2,1,0:T(8,128)(2,1)S(1)} %collective-permute-done.1.refs_0_), channel_id=1, source_target_pairs={{0,2},{2,0},{1,3},{3,1},{4,6},{6,4},{5,7},{7,5},{8,10},{10,8},{9,1... | collective-permute-start | bytes 393224 | tf_op jit(solution)/shard_map/ppermute | solution.py:241
  20.8 6.3 %collective-permute-start.7 = (bf16[8,16,512]{2,1,0:T(8,128)(2,1)S(1)}, bf16[8,16,512]{2,1,0:T(8,128)(2,1)S(1)}, u32[]{:S(2)}, u32[]{:S(2)}) collective-permute-start(bf16[8,16,512]{2,1,0:T(8,128)(2,1)S(1)} %collective-permute-done.refs_0_), channel_id=1, source_target_pairs={{0,2},{2,0},{1,3},{3,1},{4,6},{6,4},{5,7},{7,5},{8,10},{10,8},{9,1... | collective-permute-start | bytes 393224 | tf_op jit(solution)/shard_map/ppermute | solution.py:241
  21.3 8.7 %collective-permute-start.8 = (bf16[8,16,512]{2,1,0:T(8,128)(2,1)S(1)}, bf16[8,16,512]{2,1,0:T(8,128)(2,1)S(1)}, u32[]{:S(2)}, u32[]{:S(2)}) collective-permute-start(bf16[8,16,512]{2,1,0:T(8,128)(2,1)S(1)} %collective-permute-done.2.refs_0_), channel_id=1, source_target_pairs={{0,2},{2,0},{1,3},{3,1},{4,6},{6,4},{5,7},{7,5},{8,10},{10,8},{9,1... | collective-permute-start | bytes 393224 | tf_op jit(solution)/shard_map/ppermute | solution.py:241
  28.4 8.7 %collective-permute-start.13 = (bf16[8,32,512]{2,1,0:T(8,128)(2,1)S(1)}, bf16[8,32,512]{2,1,0:T(8,128)(2,1)S(1)}, u32[]{:S(2)}, u32[]{:S(2)}) collective-permute-start(bf16[8,32,512]{2,1,0:T(8,128)(2,1)S(1)} %collective-permute-done.10.refs_0_), channel_id=1, source_target_pairs={{0,2},{2,0},{1,3},{3,1},{4,6},{6,4},{5,7},{7,5},{8,10},{10,8},{9,1... | collective-permute-start | bytes 786440 | tf_op jit(solution)/shard_map/ppermute | solution.py:241
  31.7 8.7 %collective-permute-start.9 = (bf16[8,32,512]{2,1,0:T(8,128)(2,1)S(1)}, bf16[8,32,512]{2,1,0:T(8,128)(2,1)S(1)}, u32[]{:S(2)}, u32[]{:S(2)}) collective-permute-start(bf16[8,32,512]{2,1,0:T(8,128)(2,1)S(1)} %collective-permute-done.5.refs_0_), channel_id=1, source_target_pairs={{0,2},{2,0},{1,3},{3,1},{4,6},{6,4},{5,7},{7,5},{8,10},{10,8},{9,1... | collective-permute-start | bytes 786440 | tf_op jit(solution)/shard_map/ppermute | solution.py:241
  33.2 9.7 %collective-permute-start.11 = (bf16[8,32,512]{2,1,0:T(8,128)(2,1)S(1)}, bf16[8,32,512]{2,1,0:T(8,128)(2,1)S(1)}, u32[]{:S(2)}, u32[]{:S(2)}) collective-permute-start(bf16[8,32,512]{2,1,0:T(8,128)(2,1)S(1)} %get-tuple-element.94), channel_id=1, source_target_pairs={{0,8},{4,12},{8,0},{12,4},{1,9},{5,13},{9,1},{13,5},{2,10},{6,14},... | collective-permute-start | bytes 786440 | tf_op jit(solution)/shard_map/ppermute | solution.py:235
  35.5 3.4 %collective-permute-start.12 = (bf16[24,16,512]{2,1,0:T(8,128)(2,1)S(1)}, bf16[24,16,512]{2,1,0:T(8,128)(2,1)S(1)}, u32[]{:S(2)}, u32[]{:S(2)}) collective-permute-start(bf16[24,16,512]{2,1,0:T(8,128)(2,1)S(1)} %shard_map.69), channel_id=1, source_target_pairs={{0,1},{1,0},{2,3},{3,2},{4,5},{5,4},{6,7},{7,6},{8,9},{9,8},{10,11... | collective-permute-start | bytes 1179656 | tf_op jit(solution)/shard_map/ppermute | solution.py:276
  42.9 8.2 %collective-permute-start.17 = (bf16[8,32,512]{2,1,0:T(8,128)(2,1)S(1)}, bf16[8,32,512]{2,1,0:T(8,128)(2,1)S(1)}, u32[]{:S(2)}, u32[]{:S(2)}) collective-permute-start(bf16[8,32,512]{2,1,0:T(8,128)(2,1)S(1)} %collective-permute-done.11.refs_0_), channel_id=1, source_target_pairs={{0,2},{2,0},{1,3},{3,1},{4,6},{6,4},{5,7},{7,5},{8,10},{10,8},{9,1... | collective-permute-start | bytes 786440 | tf_op jit(solution)/shard_map/ppermute | solution.py:241
  43.4 11.1 %collective-permute-start.14 = (bf16[8,16,512]{2,1,0:T(8,128)(2,1)S(1)}, bf16[8,16,512]{2,1,0:T(8,128)(2,1)S(1)}, u32[]{:S(2)}, u32[]{:S(2)}) collective-permute-start(bf16[8,16,512]{2,1,0:T(8,128)(2,1)S(1)} %get-tuple-element.106), channel_id=1, source_target_pairs={{0,12},{4,8},{8,4},{12,0},{1,13},{5,9},{9,5},{13,1},{2,14},{6,10},... | collective-permute-start | bytes 393224 | tf_op jit(solution)/shard_map/ppermute | solution.py:238
  45.4 10.9 %collective-permute-start.15 = (bf16[8,16,512]{2,1,0:T(8,128)(2,1)S(1)}, bf16[8,16,512]{2,1,0:T(8,128)(2,1)S(1)}, u32[]{:S(2)}, u32[]{:S(2)}) collective-permute-start(bf16[8,16,512]{2,1,0:T(8,128)(2,1)S(1)} %get-tuple-element.107), channel_id=1, source_target_pairs={{0,8},{4,12},{8,0},{12,4},{1,9},{5,13},{9,1},{13,5},{2,10},{6,14},... | collective-permute-start | bytes 393224 | tf_op jit(solution)/shard_map/ppermute | solution.py:238
  49.7 6.6 %collective-permute-start.16 = (bf16[8,16,512]{2,1,0:T(8,128)(2,1)S(1)}, bf16[8,16,512]{2,1,0:T(8,128)(2,1)S(1)}, u32[]{:S(2)}, u32[]{:S(2)}) collective-permute-start(bf16[8,16,512]{2,1,0:T(8,128)(2,1)S(1)} %get-tuple-element.108), channel_id=1, source_target_pairs={{0,4},{4,0},{8,12},{12,8},{1,5},{5,1},{9,13},{13,9},{2,6},{6,2},{1... | collective-permute-start | bytes 393224 | tf_op jit(solution)/shard_map/ppermute | solution.py:238
  53.4 2.9 %collective-permute-start.18 = (bf16[24,32,512]{2,1,0:T(8,128)(2,1)S(1)}, bf16[24,32,512]{2,1,0:T(8,128)(2,1)S(1)}, u32[]{:S(2)}, u32[]{:S(2)}) collective-permute-start(bf16[24,32,512]{2,1,0:T(8,128)(2,1)S(1)} %shard_map.76), channel_id=1, source_target_pairs={{0,1},{1,0},{2,3},{3,2},{4,5},{5,4},{6,7},{7,6},{8,9},{9,8},{10,11... | collective-permute-start | bytes 2359304 | tf_op jit(solution)/shard_map/ppermute | solution.py:287
  57.1 19.4 %collective-permute-start.19 = (bf16[8,32,512]{2,1,0:T(8,128)(2,1)S(1)}, bf16[8,32,512]{2,1,0:T(8,128)(2,1)S(1)}, u32[]{:S(2)}, u32[]{:S(2)}) collective-permute-start(bf16[8,32,512]{2,1,0:T(8,128)(2,1)S(1)} %shard_map.78), channel_id=1, source_target_pairs={{0,8},{4,12},{8,0},{12,4},{1,9},{5,13},{9,1},{13,5},{2,10},{6,14},... | collective-permute-start | bytes 786440 | tf_op jit(solution)/shard_map/ppermute | solution.py:238
  61.3 21.5 %collective-permute-start.20 = (bf16[8,32,512]{2,1,0:T(8,128)(2,1)S(1)}, bf16[8,32,512]{2,1,0:T(8,128)(2,1)S(1)}, u32[]{:S(2)}, u32[]{:S(2)}) collective-permute-start(bf16[8,32,512]{2,1,0:T(8,128)(2,1)S(1)} %get-tuple-element.132), channel_id=1, source_target_pairs={{0,12},{4,8},{8,4},{12,0},{1,13},{5,9},{9,5},{13,1},{2,14},{6,10},... | collective-permute-start | bytes 786440 | tf_op jit(solution)/shard_map/ppermute | solution.py:238
  62.1 20.7 %collective-permute-start.21 = (bf16[8,32,512]{2,1,0:T(8,128)(2,1)S(1)}, bf16[8,32,512]{2,1,0:T(8,128)(2,1)S(1)}, u32[]{:S(2)}, u32[]{:S(2)}) collective-permute-start(bf16[8,32,512]{2,1,0:T(8,128)(2,1)S(1)} %get-tuple-element.133), channel_id=1, source_target_pairs={{0,4},{4,0},{8,12},{12,8},{1,5},{5,1},{9,13},{13,9},{2,6},{6,2},{1... | collective-permute-start | bytes 786440 | tf_op jit(solution)/shard_map/ppermute | solution.py:238
  (2 other events, 11.2 us)

commit v27 on v24

--- a/solution.py
+++ b/solution.py
@@ -272,11 +272,11 @@
     spots = [(j, 0, freqs) for j in (1, 2, 3, 0)]
     outs = restore(kept, lax.ppermute(gone, "pol", other), ratios, up, spots)
     near = project(where, [b[1]], [x_1], held, 1, blocks)
-    x_3, b, outs, near = fence((x_3, b, outs, near))
+    last = project(where, [b[3]], [x_3], held, 3, blocks)
+    last, b, outs, near = fence((last, b, outs, near))
     first = {j: swap_z(outs[j - 1], j) for j in (1, 2, 3)}
     first[0] = outs[3]
     x_2 = along_x(b[2])
-    last = project(where, [b[3]], [x_3], held, 3, blocks)
     skies = [own, near, project(where, [b[2]], [x_2], held, 2, blocks), last]
     gone = reduce(down, [leave for _, leave in skies], (ROWS, 0, 0, 0), n_modes)
     stays = [stay for stay, _ in skies]

time: 84.6 us -> 84.2 us (level)
    ppermute x6, waiting for transfers between devices: 2.44 us -> 0.02 us  [shift_z(): lax.ppermute(value, 'fm', [(i, (i + j) % parts) for i in range(parts)])]
    ppermute x8, waiting for transfers between devices: 4.17 us -> 6.18 us  [along_x(): return lax.ppermute(value, 'kl', other)]
    ppermute x6, starting transfers between devices: 11 us -> 9.57 us  [swap_z(): return lax.ppermute(value, 'fm', [(i, i ^ j) for i in range(parts)])]
    ppermute x8, starting transfers between devices: 9.13 us -> 10.2 us  [along_x(): return lax.ppermute(value, 'kl', other)]
  transfers between devices with their start and end apart: 22 -> 22, of which waited for: 7 -> 6; matrix products, arithmetic and copies ran while one was open for 2% -> 2% of each run, Pallas kernels for 28% -> 28%
where the time goes in v27:
time: 84.2 us; the launch traced here: 83.9 us
  starting transfers between devices  29.1 us (35%)
  Pallas kernels  25.7 us (31%)
  waiting for transfers between devices  25.7 us (31%)
  local copies, waits for them, and re-layouts  2.39 us (3%)
  between operations  0.93 us (1%)
    ppermute x6, waiting for transfers between devices, swap_z(): return lax.ppermute(value, 'fm', [(i, i ^ j) for i in range(parts)])  19.5 us
    ppermute x8, starting transfers between devices, along_x(): return lax.ppermute(value, 'kl', other)  10.2 us
    pallas_call x7, Pallas kernels, project(): pl.pallas_call(functools.partial(project_kernel, piece=piece, blocks=bloc...  9.58 us
    ppermute x6, starting transfers between devices, swap_z(): return lax.ppermute(value, 'fm', [(i, i ^ j) for i in range(parts)])  9.57 us
    ppermute x6, starting transfers between devices, shift_z(): lax.ppermute(value, 'fm', [(i, (i + j) % parts) for i in range(parts)])  9.33 us
    pallas_call x1, Pallas kernels, hold(): pl.pallas_call(hold_kernel, grid_spec=pltpu.PrefetchScalarGridSpec(num_sc...  7.04 us
    ppermute x8, waiting for transfers between devices, along_x(): return lax.ppermute(value, 'kl', other)  6.18 us
    pallas_call x3, Pallas kernels, place(): pl.pallas_call(functools.partial(place_kernel, spots=spots, first=first),...  4.06 us
  transfers between devices with their start and end apart: 22, of which 6 were waited for; matrix products, arithmetic and copies ran while one was open for 2% of the time, Pallas kernels for 28%

profile of v27, /device:TPU:12, one launch (start us, length us, event | category | flops | bytes accessed | tf_op | source)
XLA Modules:
  0.0 83.9 jit_solution(10505888249581650324)
XLA Ops:
  1.1 2.7 %collective-permute-start = (bf16[8,16,512]{2,1,0:T(8,128)(2,1)S(1)}, bf16[8,16,512]{2,1,0:T(8,128)(2,1)S(1)}, u32[]{:S(2)}, u32[]{:S(2)}) collective-permute-start(bf16[8,16,512]{2,1,0:T(8,128)(2,1)S(1)} %get-tuple-element.146), channel_id=1, source_target_pairs={{0,8},{4,12},{8,0},{12,4},{1,9},{5,13},{9,1},{13,5},{2,10},{6,14},... | collective-permute-start | bytes 393224 | tf_op jit(solution)/shard_map/ppermute | solution.py:232
  3.8 2.0 %collective-permute-start.2 = (bf16[8,16,512]{2,1,0:T(8,128)(2,1)S(1)}, bf16[8,16,512]{2,1,0:T(8,128)(2,1)S(1)}, u32[]{:S(2)}, u32[]{:S(2)}) collective-permute-start(bf16[8,16,512]{2,1,0:T(8,128)(2,1)S(1)} %get-tuple-element.144), channel_id=1, source_target_pairs={{0,12},{4,0},{8,4},{12,8},{1,13},{5,1},{9,5},{13,9},{2,14},{6,2},{... | collective-permute-start | bytes 393224 | tf_op jit(solution)/shard_map/ppermute | solution.py:232
  6.8 1.6 %collective-permute-start.3 = (bf16[4,48,512]{2,1,0:T(8,128)(2,1)S(1)}, bf16[4,48,512]{2,1,0:T(8,128)(2,1)S(1)}, u32[]{:S(2)}, u32[]{:S(2)}) collective-permute-start(bf16[4,48,512]{2,1,0:T(8,128)(2,1)S(1)} %get-tuple-element.140.refs_0_), channel_id=1, source_target_pairs={{0,2},{2,0},{1,3},{3,1},{4,6},{6,4},{5,7},{7,5},{8,10},{10,8},{9,1... | collective-permute-start | bytes 589832 | tf_op jit(solution)/shard_map/ppermute | solution.py:238
  9.7 7.0 %shard_map.64 = (bf16[32,512,512]{2,1,0:T(8,128)(2,1)S(1)}, bf16[384,512]{1,0:T(8,128)(2,1)S(1)}, bf16[512,384]{1,0:T(8,128)(2,1)S(1)}) custom-call(s32[10]{0:T(128)S(1)} %compare_select_fusion.4.where, s32[4,4]{1,0:T(4,128)S(1)} %bitcast.27, s32[1]{0:T(128)S(6)} %copy.24.starts, bf16[32,512,512]{2,1,0:T(8,128)(2,1)} %bitcast.28, bf16[32,24]{1,0:T(8,128)(2,1)S(1)} %bitcast.26), custom_call_target="tpu_custom_call" | custom-call | flops 1024 | bytes 1024 | tf_op jit(solution)/shard_map/pallas_call | solution.py:63
  17.4 1.9 %collective-permute-start.5 = (bf16[8,32,512]{2,1,0:T(8,128)(2,1)S(1)}, bf16[8,32,512]{2,1,0:T(8,128)(2,1)S(1)}, u32[]{:S(2)}, u32[]{:S(2)}) collective-permute-start(bf16[8,32,512]{2,1,0:T(8,128)(2,1)S(1)} %get-tuple-element.75), channel_id=1, source_target_pairs={{0,12},{4,0},{8,4},{12,8},{1,13},{5,1},{9,5},{13,9},{2,14},{6,2},{... | collective-permute-start | bytes 786440 | tf_op jit(solution)/shard_map/ppermute | solution.py:232
  19.3 1.5 %collective-permute-start.6 = (bf16[8,16,512]{2,1,0:T(8,128)(2,1)S(1)}, bf16[8,16,512]{2,1,0:T(8,128)(2,1)S(1)}, u32[]{:S(2)}, u32[]{:S(2)}) collective-permute-start(bf16[8,16,512]{2,1,0:T(8,128)(2,1)S(1)} %collective-permute-done.1.refs_0_), channel_id=1, source_target_pairs={{0,2},{2,0},{1,3},{3,1},{4,6},{6,4},{5,7},{7,5},{8,10},{10,8},{9,1... | collective-permute-start | bytes 393224 | tf_op jit(solution)/shard_map/ppermute | solution.py:238
  21.3 1.5 %collective-permute-start.8 = (bf16[8,16,512]{2,1,0:T(8,128)(2,1)S(1)}, bf16[8,16,512]{2,1,0:T(8,128)(2,1)S(1)}, u32[]{:S(2)}, u32[]{:S(2)}) collective-permute-start(bf16[8,16,512]{2,1,0:T(8,128)(2,1)S(1)} %collective-permute-done.2.refs_0_), channel_id=1, source_target_pairs={{0,2},{2,0},{1,3},{3,1},{4,6},{6,4},{5,7},{7,5},{8,10},{10,8},{9,1... | collective-permute-start | bytes 393224 | tf_op jit(solution)/shard_map/ppermute | solution.py:238
  24.1 1.5 %collective-permute-done.6.refs_1_ = bf16[8,16,512]{2,1,0:T(8,128)(2,1)S(1)} collective-permute-done((bf16[8,16,512]{2,1,0:T(8,128)(2,1)S(1)}, bf16[8,16,512]{2,1,0:T(8,128)(2,1)S(1)}, u32[]{:S(2)}, u32[]{:S(2)}) %collective-permute-start.6) | collective-permute-done | bytes 131104 | tf_op jit(solution)/shard_map/ppermute | solution.py:238
  28.4 1.6 %collective-permute-start.13 = (bf16[8,32,512]{2,1,0:T(8,128)(2,1)S(1)}, bf16[8,32,512]{2,1,0:T(8,128)(2,1)S(1)}, u32[]{:S(2)}, u32[]{:S(2)}) collective-permute-start(bf16[8,32,512]{2,1,0:T(8,128)(2,1)S(1)} %collective-permute-done.10.refs_0_), channel_id=1, source_target_pairs={{0,2},{2,0},{1,3},{3,1},{4,6},{6,4},{5,7},{7,5},{8,10},{10,8},{9,1... | collective-permute-start | bytes 786440 | tf_op jit(solution)/shard_map/ppermute | solution.py:238
  31.7 1.4 %collective-permute-start.9 = (bf16[8,32,512]{2,1,0:T(8,128)(2,1)S(1)}, bf16[8,32,512]{2,1,0:T(8,128)(2,1)S(1)}, u32[]{:S(2)}, u32[]{:S(2)}) collective-permute-start(bf16[8,32,512]{2,1,0:T(8,128)(2,1)S(1)} %collective-permute-done.5.refs_0_), channel_id=1, source_target_pairs={{0,2},{2,0},{1,3},{3,1},{4,6},{6,4},{5,7},{7,5},{8,10},{10,8},{9,1... | collective-permute-start | bytes 786440 | tf_op jit(solution)/shard_map/ppermute | solution.py:238
  33.2 2.3 %collective-permute-start.11 = (bf16[8,32,512]{2,1,0:T(8,128)(2,1)S(1)}, bf16[8,32,512]{2,1,0:T(8,128)(2,1)S(1)}, u32[]{:S(2)}, u32[]{:S(2)}) collective-permute-start(bf16[8,32,512]{2,1,0:T(8,128)(2,1)S(1)} %get-tuple-element.96), channel_id=1, source_target_pairs={{0,8},{4,12},{8,0},{12,4},{1,9},{5,13},{9,1},{13,5},{2,10},{6,14},... | collective-permute-start | bytes 786440 | tf_op jit(solution)/shard_map/ppermute | solution.py:232
  37.1 3.4 %collective-permute-done.9.refs_1_ = bf16[8,32,512]{2,1,0:T(8,128)(2,1)S(1)} collective-permute-done((bf16[8,32,512]{2,1,0:T(8,128)(2,1)S(1)}, bf16[8,32,512]{2,1,0:T(8,128)(2,1)S(1)}, u32[]{:S(2)}, u32[]{:S(2)}) %collective-permute-start.9) | collective-permute-done | bytes 262176 | tf_op jit(solution)/shard_map/ppermute | solution.py:238
  40.5 1.4 %shard_map.70 = (bf16[8,32,512]{2,1,0:T(8,128)(2,1)S(1)}, bf16[8,32,512]{2,1,0:T(8,128)(2,1)S(1)}) custom-call(s32[10]{0:T(128)S(1)} %compare_select_fusion.4.where, bf16[8,32,512]{2,1,0:T(8,128)(2,1)S(1)} %collective-permute-done.5.refs_0_, bf16[8,32,512]{2,1,0:T(8,128)(2,1)S(1)} %collective-permute-done.9.refs_1_, ...), custom_call_target="tpu_custom_call" | custom-call | flops 1024 | bytes 1024 | tf_op jit(solution)/shard_map/pallas_call | solution.py:102
  41.9 1.4 %shard_map.74 = (bf16[8,32,512]{2,1,0:T(8,128)(2,1)S(1)}, bf16[8,32,512]{2,1,0:T(8,128)(2,1)S(1)}) custom-call(s32[10]{0:T(128)S(1)} %compare_select_fusion.4.where, bf16[8,32,512]{2,1,0:T(8,128)(2,1)S(1)} %collective-permute-done.10.refs_0_, bf16[8,32,512]{2,1,0:T(8,128)(2,1)S(1)} %shard_map.73.refs_1_, ...), custom_call_target="tpu_custom_call" | custom-call | flops 1024 | bytes 1024 | tf_op jit(solution)/shard_map/pallas_call | solution.py:102
  43.9 1.6 %collective-permute-start.17 = (bf16[8,32,512]{2,1,0:T(8,128)(2,1)S(1)}, bf16[8,32,512]{2,1,0:T(8,128)(2,1)S(1)}, u32[]{:S(2)}, u32[]{:S(2)}) collective-permute-start(bf16[8,32,512]{2,1,0:T(8,128)(2,1)S(1)} %collective-permute-done.11.refs_0_), channel_id=1, source_target_pairs={{0,2},{2,0},{1,3},{3,1},{4,6},{6,4},{5,7},{7,5},{8,10},{10,8},{9,1... | collective-permute-start | bytes 786440 | tf_op jit(solution)/shard_map/ppermute | solution.py:238
  46.2 4.3 %collective-permute-start.15 = (bf16[8,16,512]{2,1,0:T(8,128)(2,1)S(1)}, bf16[8,16,512]{2,1,0:T(8,128)(2,1)S(1)}, u32[]{:S(2)}, u32[]{:S(2)}) collective-permute-start(bf16[8,16,512]{2,1,0:T(8,128)(2,1)S(1)} %get-tuple-element.109), channel_id=1, source_target_pairs={{0,8},{4,12},{8,0},{12,4},{1,9},{5,13},{9,1},{13,5},{2,10},{6,14},... | collective-permute-start | bytes 393224 | tf_op jit(solution)/shard_map/ppermute | solution.py:235
  50.5 1.4 %shard_map.75 = (bf16[8,32,512]{2,1,0:T(8,128)(2,1)S(1)}, bf16[8,32,512]{2,1,0:T(8,128)(2,1)S(1)}) custom-call(s32[10]{0:T(128)S(1)} %compare_select_fusion.4.where, bf16[8,32,512]{2,1,0:T(8,128)(2,1)S(1)} %collective-permute-done.11.refs_0_, bf16[8,32,512]{2,1,0:T(8,128)(2,1)S(1)} %collective-permute-done.17.refs_1_, ...), custom_call_target="tpu_custom_call" | custom-call | flops 1024 | bytes 1024 | tf_op jit(solution)/shard_map/pallas_call | solution.py:102
  53.8 2.9 %collective-permute-done.14.refs_0_ = bf16[8,16,512]{2,1,0:T(8,128)(2,1)S(1)} collective-permute-done((bf16[8,16,512]{2,1,0:T(8,128)(2,1)S(1)}, bf16[8,16,512]{2,1,0:T(8,128)(2,1)S(1)}, u32[]{:S(2)}, u32[]{:S(2)}) %collective-permute-start.14) | collective-permute-done | bytes 131104 | tf_op jit(solution)/shard_map/ppermute | solution.py:235
  57.6 2.6 %collective-permute-start.19 = (bf16[8,32,512]{2,1,0:T(8,128)(2,1)S(1)}, bf16[8,32,512]{2,1,0:T(8,128)(2,1)S(1)}, u32[]{:S(2)}, u32[]{:S(2)}) collective-permute-start(bf16[8,32,512]{2,1,0:T(8,128)(2,1)S(1)} %shard_map.78), channel_id=1, source_target_pairs={{0,8},{4,12},{8,0},{12,4},{1,9},{5,13},{9,1},{13,5},{2,10},{6,14},... | collective-permute-start | bytes 786440 | tf_op jit(solution)/shard_map/ppermute | solution.py:235
  61.3 1.8 %collective-permute-start.20 = (bf16[8,32,512]{2,1,0:T(8,128)(2,1)S(1)}, bf16[8,32,512]{2,1,0:T(8,128)(2,1)S(1)}, u32[]{:S(2)}, u32[]{:S(2)}) collective-permute-start(bf16[8,32,512]{2,1,0:T(8,128)(2,1)S(1)} %get-tuple-element.132), channel_id=1, source_target_pairs={{0,12},{4,8},{8,4},{12,0},{1,13},{5,9},{9,5},{13,1},{2,14},{6,10},... | collective-permute-start | bytes 786440 | tf_op jit(solution)/shard_map/ppermute | solution.py:235
  63.2 1.4 %shard_map.81.refs_1_ = bf16[8,4,48,512]{3,2,1,0:T(8,128)(2,1)} custom-call(s32[10]{0:T(128)S(1)} %compare_select_fusion.4.where, bf16[8,16,512]{2,1,0:T(8,128)(2,1)S(1)} %get-tuple-element.135.refs_0_, bf16[8,16,512]{2,1,0:T(8,128)(2,1)S(1)} %get-tuple-element.136.refs_1_, bf16[8,16,512]{2,1,0:T(8,128)(2,1)S(1)} %get-tuple-element.137.refs_2_, ...), custom_call_target="tpu_custom_call" | custom-call | flops 1024 | bytes 1024 | tf_op jit(solution)/shard_map/pallas_call | solution.py:190
  65.8 10.7 %collective-permute-done.19.refs_0_ = bf16[8,32,512]{2,1,0:T(8,128)(2,1)S(1)} collective-permute-done((bf16[8,32,512]{2,1,0:T(8,128)(2,1)S(1)}, bf16[8,32,512]{2,1,0:T(8,128)(2,1)S(1)}, u32[]{:S(2)}, u32[]{:S(2)}) %collective-permute-start.19) | collective-permute-done | bytes 262176 | tf_op jit(solution)/shard_map/ppermute | solution.py:235
  76.5 5.9 %collective-permute-done.20.refs_1_ = bf16[8,32,512]{2,1,0:T(8,128)(2,1)S(1)} collective-permute-done((bf16[8,32,512]{2,1,0:T(8,128)(2,1)S(1)}, bf16[8,32,512]{2,1,0:T(8,128)(2,1)S(1)}, u32[]{:S(2)}, u32[]{:S(2)}) %collective-permute-start.20) | collective-permute-done | bytes 262176 | tf_op jit(solution)/shard_map/ppermute | solution.py:235
  82.4 1.4 %shard_map.83 = bf16[8,4,48,512]{3,2,1,0:T(8,128)(2,1)} custom-call(s32[10]{0:T(128)S(1)} %compare_select_fusion.4.where, bf16[8,32,512]{2,1,0:T(8,128)(2,1)S(1)} %collective-permute-done.19.refs_0_, bf16[8,32,512]{2,1,0:T(8,128)(2,1)S(1)} %collective-permute-done.20.refs_1_, ...), custom_call_target="tpu_custom_call", output_to_operand_aliasing={{}: (4, {})} | custom-call | flops 1024 | bytes 1024 | tf_op jit(solution)/shard_map/pallas_call | solution.py:190
  (55 shorter events, 17.9 us)
Async XLA Ops:
  0.0 9.6 %copy-start.2 = (bf16[1,32,24]{1,2,0:T(8,128)(2,1)S(1)}, bf16[1,32,24]{1,2,0:T(8,128)(2,1)}, u32[]{:S(2)}) copy-start(bf16[1,32,24]{1,2,0:T(8,128)(2,1)} %param.10) | copy-start | bytes 4612
  0.0 9.7 %copy-start = (s32[1,4,4]{2,1,0:T(4,128)S(1)}, s32[1,4,4]{2,1,0:T(4,128)}, u32[]{:S(2)}) copy-start(s32[1,4,4]{2,1,0:T(4,128)} %param.8) | copy-start | bytes 196
  1.1 15.7 %collective-permute-start = (bf16[8,16,512]{2,1,0:T(8,128)(2,1)S(1)}, bf16[8,16,512]{2,1,0:T(8,128)(2,1)S(1)}, u32[]{:S(2)}, u32[]{:S(2)}) collective-permute-start(bf16[8,16,512]{2,1,0:T(8,128)(2,1)S(1)} %get-tuple-element.146), channel_id=1, source_target_pairs={{0,8},{4,12},{8,0},{12,4},{1,9},{5,13},{9,1},{13,5},{2,10},{6,14},... | collective-permute-start | bytes 393224 | tf_op jit(solution)/shard_map/ppermute | solution.py:232
  3.7 13.1 %collective-permute-start.1 = (bf16[8,16,512]{2,1,0:T(8,128)(2,1)S(1)}, bf16[8,16,512]{2,1,0:T(8,128)(2,1)S(1)}, u32[]{:S(2)}, u32[]{:S(2)}) collective-permute-start(bf16[8,16,512]{2,1,0:T(8,128)(2,1)S(1)} %get-tuple-element.145), channel_id=1, source_target_pairs={{0,4},{4,8},{8,12},{12,0},{1,5},{5,9},{9,13},{13,1},{2,6},{6,10},{... | collective-permute-start | bytes 393224 | tf_op jit(solution)/shard_map/ppermute | solution.py:232
  3.8 13.1 %collective-permute-start.2 = (bf16[8,16,512]{2,1,0:T(8,128)(2,1)S(1)}, bf16[8,16,512]{2,1,0:T(8,128)(2,1)S(1)}, u32[]{:S(2)}, u32[]{:S(2)}) collective-permute-start(bf16[8,16,512]{2,1,0:T(8,128)(2,1)S(1)} %get-tuple-element.144), channel_id=1, source_target_pairs={{0,12},{4,0},{8,4},{12,8},{1,13},{5,1},{9,5},{13,9},{2,14},{6,2},{... | collective-permute-start | bytes 393224 | tf_op jit(solution)/shard_map/ppermute | solution.py:232
  6.8 10.0 %collective-permute-start.3 = (bf16[4,48,512]{2,1,0:T(8,128)(2,1)S(1)}, bf16[4,48,512]{2,1,0:T(8,128)(2,1)S(1)}, u32[]{:S(2)}, u32[]{:S(2)}) collective-permute-start(bf16[4,48,512]{2,1,0:T(8,128)(2,1)S(1)} %get-tuple-element.140.refs_0_), channel_id=1, source_target_pairs={{0,2},{2,0},{1,3},{3,1},{4,6},{6,4},{5,7},{7,5},{8,10},{10,8},{9,1... | collective-permute-start | bytes 589832 | tf_op jit(solution)/shard_map/ppermute | solution.py:238
  8.4 8.5 %collective-permute-start.4 = (bf16[4,48,512]{2,1,0:T(8,128)(2,1)S(1)}, bf16[4,48,512]{2,1,0:T(8,128)(2,1)S(1)}, u32[]{:S(2)}, u32[]{:S(2)}) collective-permute-start(bf16[4,48,512]{2,1,0:T(8,128)(2,1)S(1)} %get-tuple-element.139.refs_1_), channel_id=1, source_target_pairs={{0,2},{2,0},{1,3},{3,1},{4,6},{6,4},{5,7},{7,5},{8,10},{10,8},{9,1... | collective-permute-start | bytes 589832 | tf_op jit(solution)/shard_map/ppermute | solution.py:238
  16.9 11.5 %collective-permute-start.10 = (bf16[8,32,512]{2,1,0:T(8,128)(2,1)S(1)}, bf16[8,32,512]{2,1,0:T(8,128)(2,1)S(1)}, u32[]{:S(2)}, u32[]{:S(2)}) collective-permute-start(bf16[8,32,512]{2,1,0:T(8,128)(2,1)S(1)} %get-tuple-element.95), channel_id=1, source_target_pairs={{0,4},{4,8},{8,12},{12,0},{1,5},{5,9},{9,13},{13,1},{2,6},{6,10},{... | collective-permute-start | bytes 786440 | tf_op jit(solution)/shard_map/ppermute | solution.py:232
  17.4 14.4 %collective-permute-start.5 = (bf16[8,32,512]{2,1,0:T(8,128)(2,1)S(1)}, bf16[8,32,512]{2,1,0:T(8,128)(2,1)S(1)}, u32[]{:S(2)}, u32[]{:S(2)}) collective-permute-start(bf16[8,32,512]{2,1,0:T(8,128)(2,1)S(1)} %get-tuple-element.75), channel_id=1, source_target_pairs={{0,12},{4,0},{8,4},{12,8},{1,13},{5,1},{9,5},{13,9},{2,14},{6,2},{... | collective-permute-start | bytes 786440 | tf_op jit(solution)/shard_map/ppermute | solution.py:232
  19.3 6.4 %collective-permute-start.6 = (bf16[8,16,512]{2,1,0:T(8,128)(2,1)S(1)}, bf16[8,16,512]{2,1,0:T(8,128)(2,1)S(1)}, u32[]{:S(2)}, u32[]{:S(2)}) collective-permute-start(bf16[8,16,512]{2,1,0:T(8,128)(2,1)S(1)} %collective-permute-done.1.refs_0_), channel_id=1, source_target_pairs={{0,2},{2,0},{1,3},{3,1},{4,6},{6,4},{5,7},{7,5},{8,10},{10,8},{9,1... | collective-permute-start | bytes 393224 | tf_op jit(solution)/shard_map/ppermute | solution.py:238
  20.8 6.3 %collective-permute-start.7 = (bf16[8,16,512]{2,1,0:T(8,128)(2,1)S(1)}, bf16[8,16,512]{2,1,0:T(8,128)(2,1)S(1)}, u32[]{:S(2)}, u32[]{:S(2)}) collective-permute-start(bf16[8,16,512]{2,1,0:T(8,128)(2,1)S(1)} %collective-permute-done.refs_0_), channel_id=1, source_target_pairs={{0,2},{2,0},{1,3},{3,1},{4,6},{6,4},{5,7},{7,5},{8,10},{10,8},{9,1... | collective-permute-start | bytes 393224 | tf_op jit(solution)/shard_map/ppermute | solution.py:238
  21.3 8.7 %collective-permute-start.8 = (bf16[8,16,512]{2,1,0:T(8,128)(2,1)S(1)}, bf16[8,16,512]{2,1,0:T(8,128)(2,1)S(1)}, u32[]{:S(2)}, u32[]{:S(2)}) collective-permute-start(bf16[8,16,512]{2,1,0:T(8,128)(2,1)S(1)} %collective-permute-done.2.refs_0_), channel_id=1, source_target_pairs={{0,2},{2,0},{1,3},{3,1},{4,6},{6,4},{5,7},{7,5},{8,10},{10,8},{9,1... | collective-permute-start | bytes 393224 | tf_op jit(solution)/shard_map/ppermute | solution.py:238
  28.4 8.7 %collective-permute-start.13 = (bf16[8,32,512]{2,1,0:T(8,128)(2,1)S(1)}, bf16[8,32,512]{2,1,0:T(8,128)(2,1)S(1)}, u32[]{:S(2)}, u32[]{:S(2)}) collective-permute-start(bf16[8,32,512]{2,1,0:T(8,128)(2,1)S(1)} %collective-permute-done.10.refs_0_), channel_id=1, source_target_pairs={{0,2},{2,0},{1,3},{3,1},{4,6},{6,4},{5,7},{7,5},{8,10},{10,8},{9,1... | collective-permute-start | bytes 786440 | tf_op jit(solution)/shard_map/ppermute | solution.py:238
  31.7 8.7 %collective-permute-start.9 = (bf16[8,32,512]{2,1,0:T(8,128)(2,1)S(1)}, bf16[8,32,512]{2,1,0:T(8,128)(2,1)S(1)}, u32[]{:S(2)}, u32[]{:S(2)}) collective-permute-start(bf16[8,32,512]{2,1,0:T(8,128)(2,1)S(1)} %collective-permute-done.5.refs_0_), channel_id=1, source_target_pairs={{0,2},{2,0},{1,3},{3,1},{4,6},{6,4},{5,7},{7,5},{8,10},{10,8},{9,1... | collective-permute-start | bytes 786440 | tf_op jit(solution)/shard_map/ppermute | solution.py:238
  33.2 10.7 %collective-permute-start.11 = (bf16[8,32,512]{2,1,0:T(8,128)(2,1)S(1)}, bf16[8,32,512]{2,1,0:T(8,128)(2,1)S(1)}, u32[]{:S(2)}, u32[]{:S(2)}) collective-permute-start(bf16[8,32,512]{2,1,0:T(8,128)(2,1)S(1)} %get-tuple-element.96), channel_id=1, source_target_pairs={{0,8},{4,12},{8,0},{12,4},{1,9},{5,13},{9,1},{13,5},{2,10},{6,14},... | collective-permute-start | bytes 786440 | tf_op jit(solution)/shard_map/ppermute | solution.py:232
  35.5 7.8 %collective-permute-start.12 = (bf16[24,16,512]{2,1,0:T(8,128)(2,1)S(1)}, bf16[24,16,512]{2,1,0:T(8,128)(2,1)S(1)}, u32[]{:S(2)}, u32[]{:S(2)}) collective-permute-start(bf16[24,16,512]{2,1,0:T(8,128)(2,1)S(1)} %shard_map.69), channel_id=1, source_target_pairs={{0,1},{1,0},{2,3},{3,2},{4,5},{5,4},{6,7},{7,6},{8,9},{9,8},{10,11... | collective-permute-start | bytes 1179656 | tf_op jit(solution)/shard_map/ppermute | solution.py:273
  43.9 6.6 %collective-permute-start.17 = (bf16[8,32,512]{2,1,0:T(8,128)(2,1)S(1)}, bf16[8,32,512]{2,1,0:T(8,128)(2,1)S(1)}, u32[]{:S(2)}, u32[]{:S(2)}) collective-permute-start(bf16[8,32,512]{2,1,0:T(8,128)(2,1)S(1)} %collective-permute-done.11.refs_0_), channel_id=1, source_target_pairs={{0,2},{2,0},{1,3},{3,1},{4,6},{6,4},{5,7},{7,5},{8,10},{10,8},{9,1... | collective-permute-start | bytes 786440 | tf_op jit(solution)/shard_map/ppermute | solution.py:238
  45.4 11.4 %collective-permute-start.14 = (bf16[8,16,512]{2,1,0:T(8,128)(2,1)S(1)}, bf16[8,16,512]{2,1,0:T(8,128)(2,1)S(1)}, u32[]{:S(2)}, u32[]{:S(2)}) collective-permute-start(bf16[8,16,512]{2,1,0:T(8,128)(2,1)S(1)} %get-tuple-element.108), channel_id=1, source_target_pairs={{0,12},{4,8},{8,4},{12,0},{1,13},{5,9},{9,5},{13,1},{2,14},{6,10},... | collective-permute-start | bytes 393224 | tf_op jit(solution)/shard_map/ppermute | solution.py:235
  46.2 10.6 %collective-permute-start.15 = (bf16[8,16,512]{2,1,0:T(8,128)(2,1)S(1)}, bf16[8,16,512]{2,1,0:T(8,128)(2,1)S(1)}, u32[]{:S(2)}, u32[]{:S(2)}) collective-permute-start(bf16[8,16,512]{2,1,0:T(8,128)(2,1)S(1)} %get-tuple-element.109), channel_id=1, source_target_pairs={{0,8},{4,12},{8,0},{12,4},{1,9},{5,13},{9,1},{13,5},{2,10},{6,14},... | collective-permute-start | bytes 393224 | tf_op jit(solution)/shard_map/ppermute | solution.py:235
  50.5 6.3 %collective-permute-start.16 = (bf16[8,16,512]{2,1,0:T(8,128)(2,1)S(1)}, bf16[8,16,512]{2,1,0:T(8,128)(2,1)S(1)}, u32[]{:S(2)}, u32[]{:S(2)}) collective-permute-start(bf16[8,16,512]{2,1,0:T(8,128)(2,1)S(1)} %get-tuple-element.110), channel_id=1, source_target_pairs={{0,4},{4,0},{8,12},{12,8},{1,5},{5,1},{9,13},{13,9},{2,6},{6,2},{1... | collective-permute-start | bytes 393224 | tf_op jit(solution)/shard_map/ppermute | solution.py:235
  52.8 4.0 %collective-permute-start.18 = (bf16[24,32,512]{2,1,0:T(8,128)(2,1)S(1)}, bf16[24,32,512]{2,1,0:T(8,128)(2,1)S(1)}, u32[]{:S(2)}, u32[]{:S(2)}) collective-permute-start(bf16[24,32,512]{2,1,0:T(8,128)(2,1)S(1)} %shard_map.76), channel_id=1, source_target_pairs={{0,1},{1,0},{2,3},{3,2},{4,5},{5,4},{6,7},{7,6},{8,9},{9,8},{10,11... | collective-permute-start | bytes 2359304 | tf_op jit(solution)/shard_map/ppermute | solution.py:284
  57.6 18.9 %collective-permute-start.19 = (bf16[8,32,512]{2,1,0:T(8,128)(2,1)S(1)}, bf16[8,32,512]{2,1,0:T(8,128)(2,1)S(1)}, u32[]{:S(2)}, u32[]{:S(2)}) collective-permute-start(bf16[8,32,512]{2,1,0:T(8,128)(2,1)S(1)} %shard_map.78), channel_id=1, source_target_pairs={{0,8},{4,12},{8,0},{12,4},{1,9},{5,13},{9,1},{13,5},{2,10},{6,14},... | collective-permute-start | bytes 786440 | tf_op jit(solution)/shard_map/ppermute | solution.py:235
  61.3 21.1 %collective-permute-start.20 = (bf16[8,32,512]{2,1,0:T(8,128)(2,1)S(1)}, bf16[8,32,512]{2,1,0:T(8,128)(2,1)S(1)}, u32[]{:S(2)}, u32[]{:S(2)}) collective-permute-start(bf16[8,32,512]{2,1,0:T(8,128)(2,1)S(1)} %get-tuple-element.132), channel_id=1, source_target_pairs={{0,12},{4,8},{8,4},{12,0},{1,13},{5,9},{9,5},{13,1},{2,14},{6,10},... | collective-permute-start | bytes 786440 | tf_op jit(solution)/shard_map/ppermute | solution.py:235
  63.1 19.3 %collective-permute-start.21 = (bf16[8,32,512]{2,1,0:T(8,128)(2,1)S(1)}, bf16[8,32,512]{2,1,0:T(8,128)(2,1)S(1)}, u32[]{:S(2)}, u32[]{:S(2)}) collective-permute-start(bf16[8,32,512]{2,1,0:T(8,128)(2,1)S(1)} %get-tuple-element.133), channel_id=1, source_target_pairs={{0,4},{4,0},{8,12},{12,8},{1,5},{5,1},{9,13},{13,9},{2,6},{6,2},{1... | collective-permute-start | bytes 786440 | tf_op jit(solution)/shard_map/ppermute | solution.py:235
  (2 other events, 11.2 us)

commit v28 on v27

--- a/solution.py
+++ b/solution.py
@@ -267,7 +267,7 @@
     b[3], b[2], stay_a, gone = fence((b[3], b[2], stay_a, gone))
     x_3 = along_x(b[3])
     x_1, = anchor([along_x(b[1])], 2_500_000_000)
-    b[2] = shift_z(b[2], 2)
+    b[2], = anchor([shift_z(b[2], 2)], 2_000_000_000)
     kept = reduce(down, stay_a, (0, 0, 0, 0), n_modes, jnp.float32)
     spots = [(j, 0, freqs) for j in (1, 2, 3, 0)]
     outs = restore(kept, lax.ppermute(gone, "pol", other), ratios, up, spots)

time: 84.2 us -> 84.9 us (level)
  transfers between devices with their start and end apart: 22 -> 22, of which waited for: 6 -> 6; matrix products, arithmetic and copies ran while one was open for 2% -> 1% of each run, Pallas kernels for 28% -> 27%
where the time goes in v28:
time: 84.9 us; the launch traced here: 84.5 us
  starting transfers between devices  29.1 us (34%)
  waiting for transfers between devices  26.4 us (31%)
  Pallas kernels  25.7 us (30%)
  local copies, waits for them, and re-layouts  2.39 us (3%)
  between operations  0.94 us (1%)
    ppermute x6, waiting for transfers between devices, swap_z(): return lax.ppermute(value, 'fm', [(i, i ^ j) for i in range(parts)])  20.2 us
    ppermute x8, starting transfers between devices, along_x(): return lax.ppermute(value, 'kl', other)  10.2 us
    pallas_call x7, Pallas kernels, project(): pl.pallas_call(functools.partial(project_kernel, piece=piece, blocks=bloc...  9.58 us
    ppermute x6, starting transfers between devices, swap_z(): return lax.ppermute(value, 'fm', [(i, i ^ j) for i in range(parts)])  9.57 us
    ppermute x6, starting transfers between devices, shift_z(): lax.ppermute(value, 'fm', [(i, (i + j) % parts) for i in range(parts)])  9.33 us
    pallas_call x1, Pallas kernels, hold(): pl.pallas_call(hold_kernel, grid_spec=pltpu.PrefetchScalarGridSpec(num_sc...  7.04 us
    ppermute x8, waiting for transfers between devices, along_x(): return lax.ppermute(value, 'kl', other)  6.18 us
    pallas_call x3, Pallas kernels, place(): pl.pallas_call(functools.partial(place_kernel, spots=spots, first=first),...  4.06 us
  transfers between devices with their start and end apart: 22, of which 6 were waited for; matrix products, arithmetic and copies ran while one was open for 1% of the time, Pallas kernels for 27%

profile of v28, /device:TPU:12, one launch (start us, length us, event | category | flops | bytes accessed | tf_op | source)
XLA Modules:
  0.0 84.5 jit_solution(1228327009842530157)
XLA Ops:
  1.1 2.7 %collective-permute-start = (bf16[8,16,512]{2,1,0:T(8,128)(2,1)S(1)}, bf16[8,16,512]{2,1,0:T(8,128)(2,1)S(1)}, u32[]{:S(2)}, u32[]{:S(2)}) collective-permute-start(bf16[8,16,512]{2,1,0:T(8,128)(2,1)S(1)} %get-tuple-element.146), channel_id=1, source_target_pairs={{0,8},{4,12},{8,0},{12,4},{1,9},{5,13},{9,1},{13,5},{2,10},{6,14},... | collective-permute-start | bytes 393224 | tf_op jit(solution)/shard_map/ppermute | solution.py:232
  3.8 2.0 %collective-permute-start.2 = (bf16[8,16,512]{2,1,0:T(8,128)(2,1)S(1)}, bf16[8,16,512]{2,1,0:T(8,128)(2,1)S(1)}, u32[]{:S(2)}, u32[]{:S(2)}) collective-permute-start(bf16[8,16,512]{2,1,0:T(8,128)(2,1)S(1)} %get-tuple-element.144), channel_id=1, source_target_pairs={{0,12},{4,0},{8,4},{12,8},{1,13},{5,1},{9,5},{13,9},{2,14},{6,2},{... | collective-permute-start | bytes 393224 | tf_op jit(solution)/shard_map/ppermute | solution.py:232
  6.8 1.6 %collective-permute-start.3 = (bf16[4,48,512]{2,1,0:T(8,128)(2,1)S(1)}, bf16[4,48,512]{2,1,0:T(8,128)(2,1)S(1)}, u32[]{:S(2)}, u32[]{:S(2)}) collective-permute-start(bf16[4,48,512]{2,1,0:T(8,128)(2,1)S(1)} %get-tuple-element.140.refs_0_), channel_id=1, source_target_pairs={{0,2},{2,0},{1,3},{3,1},{4,6},{6,4},{5,7},{7,5},{8,10},{10,8},{9,1... | collective-permute-start | bytes 589832 | tf_op jit(solution)/shard_map/ppermute | solution.py:238
  9.7 7.0 %shard_map.64 = (bf16[32,512,512]{2,1,0:T(8,128)(2,1)S(1)}, bf16[384,512]{1,0:T(8,128)(2,1)S(1)}, bf16[512,384]{1,0:T(8,128)(2,1)S(1)}) custom-call(s32[10]{0:T(128)S(1)} %compare_select_fusion.4.where, s32[4,4]{1,0:T(4,128)S(1)} %bitcast.27, s32[1]{0:T(128)S(6)} %copy.26.starts, bf16[32,512,512]{2,1,0:T(8,128)(2,1)} %bitcast.28, bf16[32,24]{1,0:T(8,128)(2,1)S(1)} %bitcast.26), custom_call_target="tpu_custom_call" | custom-call | flops 1024 | bytes 1024 | tf_op jit(solution)/shard_map/pallas_call | solution.py:63
  17.4 1.9 %collective-permute-start.5 = (bf16[8,32,512]{2,1,0:T(8,128)(2,1)S(1)}, bf16[8,32,512]{2,1,0:T(8,128)(2,1)S(1)}, u32[]{:S(2)}, u32[]{:S(2)}) collective-permute-start(bf16[8,32,512]{2,1,0:T(8,128)(2,1)S(1)} %get-tuple-element.75), channel_id=1, source_target_pairs={{0,12},{4,0},{8,4},{12,8},{1,13},{5,1},{9,5},{13,9},{2,14},{6,2},{... | collective-permute-start | bytes 786440 | tf_op jit(solution)/shard_map/ppermute | solution.py:232
  19.3 1.5 %collective-permute-start.6 = (bf16[8,16,512]{2,1,0:T(8,128)(2,1)S(1)}, bf16[8,16,512]{2,1,0:T(8,128)(2,1)S(1)}, u32[]{:S(2)}, u32[]{:S(2)}) collective-permute-start(bf16[8,16,512]{2,1,0:T(8,128)(2,1)S(1)} %collective-permute-done.1.refs_0_), channel_id=1, source_target_pairs={{0,2},{2,0},{1,3},{3,1},{4,6},{6,4},{5,7},{7,5},{8,10},{10,8},{9,1... | collective-permute-start | bytes 393224 | tf_op jit(solution)/shard_map/ppermute | solution.py:238
  21.3 1.5 %collective-permute-start.8 = (bf16[8,16,512]{2,1,0:T(8,128)(2,1)S(1)}, bf16[8,16,512]{2,1,0:T(8,128)(2,1)S(1)}, u32[]{:S(2)}, u32[]{:S(2)}) collective-permute-start(bf16[8,16,512]{2,1,0:T(8,128)(2,1)S(1)} %collective-permute-done.2.refs_0_), channel_id=1, source_target_pairs={{0,2},{2,0},{1,3},{3,1},{4,6},{6,4},{5,7},{7,5},{8,10},{10,8},{9,1... | collective-permute-start | bytes 393224 | tf_op jit(solution)/shard_map/ppermute | solution.py:238
  24.1 1.5 %collective-permute-done.6.refs_1_ = bf16[8,16,512]{2,1,0:T(8,128)(2,1)S(1)} collective-permute-done((bf16[8,16,512]{2,1,0:T(8,128)(2,1)S(1)}, bf16[8,16,512]{2,1,0:T(8,128)(2,1)S(1)}, u32[]{:S(2)}, u32[]{:S(2)}) %collective-permute-start.6) | collective-permute-done | bytes 131104 | tf_op jit(solution)/shard_map/ppermute | solution.py:238
  28.4 1.6 %collective-permute-start.13 = (bf16[8,32,512]{2,1,0:T(8,128)(2,1)S(1)}, bf16[8,32,512]{2,1,0:T(8,128)(2,1)S(1)}, u32[]{:S(2)}, u32[]{:S(2)}) collective-permute-start(bf16[8,32,512]{2,1,0:T(8,128)(2,1)S(1)} %collective-permute-done.10.refs_0_), channel_id=1, source_target_pairs={{0,2},{2,0},{1,3},{3,1},{4,6},{6,4},{5,7},{7,5},{8,10},{10,8},{9,1... | collective-permute-start | bytes 786440 | tf_op jit(solution)/shard_map/ppermute | solution.py:238
  30.0 1.4 %shard_map.68 = (bf16[8,16,512]{2,1,0:T(8,128)(2,1)S(1)}, bf16[8,16,512]{2,1,0:T(8,128)(2,1)S(1)}) custom-call(s32[10]{0:T(128)S(1)} %compare_select_fusion.4.where, bf16[8,16,512]{2,1,0:T(8,128)(2,1)S(1)} %collective-permute-done.2.refs_0_, bf16[8,16,512]{2,1,0:T(8,128)(2,1)S(1)} %collective-permute-done.8.refs_1_, ...), custom_call_target="tpu_custom_call" | custom-call | flops 400000000 | bytes 1024 | tf_op jit(solution)/shard_map/pallas_call | solution.py:102
  31.7 1.4 %collective-permute-start.9 = (bf16[8,32,512]{2,1,0:T(8,128)(2,1)S(1)}, bf16[8,32,512]{2,1,0:T(8,128)(2,1)S(1)}, u32[]{:S(2)}, u32[]{:S(2)}) collective-permute-start(bf16[8,32,512]{2,1,0:T(8,128)(2,1)S(1)} %collective-permute-done.5.refs_0_), channel_id=1, source_target_pairs={{0,2},{2,0},{1,3},{3,1},{4,6},{6,4},{5,7},{7,5},{8,10},{10,8},{9,1... | collective-permute-start | bytes 786440 | tf_op jit(solution)/shard_map/ppermute | solution.py:238
  33.2 2.3 %collective-permute-start.11 = (bf16[8,32,512]{2,1,0:T(8,128)(2,1)S(1)}, bf16[8,32,512]{2,1,0:T(8,128)(2,1)S(1)}, u32[]{:S(2)}, u32[]{:S(2)}) collective-permute-start(bf16[8,32,512]{2,1,0:T(8,128)(2,1)S(1)} %get-tuple-element.96), channel_id=1, source_target_pairs={{0,8},{4,12},{8,0},{12,4},{1,9},{5,13},{9,1},{13,5},{2,10},{6,14},... | collective-permute-start | bytes 786440 | tf_op jit(solution)/shard_map/ppermute | solution.py:232
  37.1 3.4 %collective-permute-done.9.refs_1_ = bf16[8,32,512]{2,1,0:T(8,128)(2,1)S(1)} collective-permute-done((bf16[8,32,512]{2,1,0:T(8,128)(2,1)S(1)}, bf16[8,32,512]{2,1,0:T(8,128)(2,1)S(1)}, u32[]{:S(2)}, u32[]{:S(2)}) %collective-permute-start.9) | collective-permute-done | bytes 262176 | tf_op jit(solution)/shard_map/ppermute | solution.py:238
  40.5 1.4 %shard_map.70 = (bf16[8,32,512]{2,1,0:T(8,128)(2,1)S(1)}, bf16[8,32,512]{2,1,0:T(8,128)(2,1)S(1)}) custom-call(s32[10]{0:T(128)S(1)} %compare_select_fusion.4.where, bf16[8,32,512]{2,1,0:T(8,128)(2,1)S(1)} %collective-permute-done.5.refs_0_, bf16[8,32,512]{2,1,0:T(8,128)(2,1)S(1)} %collective-permute-done.9.refs_1_, ...), custom_call_target="tpu_custom_call" | custom-call | flops 1024 | bytes 1024 | tf_op jit(solution)/shard_map/pallas_call | solution.py:102
  41.8 1.4 %shard_map.75 = (bf16[8,32,512]{2,1,0:T(8,128)(2,1)S(1)}, bf16[8,32,512]{2,1,0:T(8,128)(2,1)S(1)}) custom-call(s32[10]{0:T(128)S(1)} %compare_select_fusion.4.where, bf16[8,32,512]{2,1,0:T(8,128)(2,1)S(1)} %collective-permute-done.10.refs_0_, bf16[8,32,512]{2,1,0:T(8,128)(2,1)S(1)} %shard_map.74.refs_1_, ...), custom_call_target="tpu_custom_call" | custom-call | flops 1024 | bytes 1024 | tf_op jit(solution)/shard_map/pallas_call | solution.py:102
  43.9 1.6 %collective-permute-start.17 = (bf16[8,32,512]{2,1,0:T(8,128)(2,1)S(1)}, bf16[8,32,512]{2,1,0:T(8,128)(2,1)S(1)}, u32[]{:S(2)}, u32[]{:S(2)}) collective-permute-start(bf16[8,32,512]{2,1,0:T(8,128)(2,1)S(1)} %shard_map.71.refs_0_), channel_id=1, source_target_pairs={{0,2},{2,0},{1,3},{3,1},{4,6},{6,4},{5,7},{7,5},{8,10},{10,8},{9,1... | collective-permute-start | bytes 786440 | tf_op jit(solution)/shard_map/ppermute | solution.py:238
  46.2 4.3 %collective-permute-start.15 = (bf16[8,16,512]{2,1,0:T(8,128)(2,1)S(1)}, bf16[8,16,512]{2,1,0:T(8,128)(2,1)S(1)}, u32[]{:S(2)}, u32[]{:S(2)}) collective-permute-start(bf16[8,16,512]{2,1,0:T(8,128)(2,1)S(1)} %get-tuple-element.109), channel_id=1, source_target_pairs={{0,8},{4,12},{8,0},{12,4},{1,9},{5,13},{9,1},{13,5},{2,10},{6,14},... | collective-permute-start | bytes 393224 | tf_op jit(solution)/shard_map/ppermute | solution.py:235
  50.5 1.4 %shard_map.76 = (bf16[8,32,512]{2,1,0:T(8,128)(2,1)S(1)}, bf16[8,32,512]{2,1,0:T(8,128)(2,1)S(1)}) custom-call(s32[10]{0:T(128)S(1)} %compare_select_fusion.4.where, bf16[8,32,512]{2,1,0:T(8,128)(2,1)S(1)} %shard_map.71.refs_0_, bf16[8,32,512]{2,1,0:T(8,128)(2,1)S(1)} %collective-permute-done.17.refs_1_, ...), custom_call_target="tpu_custom_call" | custom-call | flops 1024 | bytes 1024 | tf_op jit(solution)/shard_map/pallas_call | solution.py:102
  53.9 3.5 %collective-permute-done.14.refs_0_ = bf16[8,16,512]{2,1,0:T(8,128)(2,1)S(1)} collective-permute-done((bf16[8,16,512]{2,1,0:T(8,128)(2,1)S(1)}, bf16[8,16,512]{2,1,0:T(8,128)(2,1)S(1)}, u32[]{:S(2)}, u32[]{:S(2)}) %collective-permute-start.14) | collective-permute-done | bytes 131104 | tf_op jit(solution)/shard_map/ppermute | solution.py:235
  58.2 2.7 %collective-permute-start.19 = (bf16[8,32,512]{2,1,0:T(8,128)(2,1)S(1)}, bf16[8,32,512]{2,1,0:T(8,128)(2,1)S(1)}, u32[]{:S(2)}, u32[]{:S(2)}) collective-permute-start(bf16[8,32,512]{2,1,0:T(8,128)(2,1)S(1)} %shard_map.79), channel_id=1, source_target_pairs={{0,8},{4,12},{8,0},{12,4},{1,9},{5,13},{9,1},{13,5},{2,10},{6,14},... | collective-permute-start | bytes 786440 | tf_op jit(solution)/shard_map/ppermute | solution.py:235
  62.0 1.8 %collective-permute-start.20 = (bf16[8,32,512]{2,1,0:T(8,128)(2,1)S(1)}, bf16[8,32,512]{2,1,0:T(8,128)(2,1)S(1)}, u32[]{:S(2)}, u32[]{:S(2)}) collective-permute-start(bf16[8,32,512]{2,1,0:T(8,128)(2,1)S(1)} %get-tuple-element.132), channel_id=1, source_target_pairs={{0,12},{4,8},{8,4},{12,0},{1,13},{5,9},{9,5},{13,1},{2,14},{6,10},... | collective-permute-start | bytes 786440 | tf_op jit(solution)/shard_map/ppermute | solution.py:235
  66.4 10.8 %collective-permute-done.19.refs_0_ = bf16[8,32,512]{2,1,0:T(8,128)(2,1)S(1)} collective-permute-done((bf16[8,32,512]{2,1,0:T(8,128)(2,1)S(1)}, bf16[8,32,512]{2,1,0:T(8,128)(2,1)S(1)}, u32[]{:S(2)}, u32[]{:S(2)}) %collective-permute-start.19) | collective-permute-done | bytes 262176 | tf_op jit(solution)/shard_map/ppermute | solution.py:235
  77.2 5.9 %collective-permute-done.20.refs_1_ = bf16[8,32,512]{2,1,0:T(8,128)(2,1)S(1)} collective-permute-done((bf16[8,32,512]{2,1,0:T(8,128)(2,1)S(1)}, bf16[8,32,512]{2,1,0:T(8,128)(2,1)S(1)}, u32[]{:S(2)}, u32[]{:S(2)}) %collective-permute-start.20) | collective-permute-done | bytes 262176 | tf_op jit(solution)/shard_map/ppermute | solution.py:235
  83.1 1.4 %shard_map.84 = bf16[8,4,48,512]{3,2,1,0:T(8,128)(2,1)} custom-call(s32[10]{0:T(128)S(1)} %compare_select_fusion.4.where, bf16[8,32,512]{2,1,0:T(8,128)(2,1)S(1)} %collective-permute-done.19.refs_0_, bf16[8,32,512]{2,1,0:T(8,128)(2,1)S(1)} %collective-permute-done.20.refs_1_, ...), custom_call_target="tpu_custom_call", output_to_operand_aliasing={{}: (4, {})} | custom-call | flops 1024 | bytes 1024 | tf_op jit(solution)/shard_map/pallas_call | solution.py:190
  (56 shorter events, 17.9 us)
Async XLA Ops:
  0.0 9.6 %copy-start.2 = (bf16[1,32,24]{1,2,0:T(8,128)(2,1)S(1)}, bf16[1,32,24]{1,2,0:T(8,128)(2,1)}, u32[]{:S(2)}) copy-start(bf16[1,32,24]{1,2,0:T(8,128)(2,1)} %param.10) | copy-start | bytes 4612
  0.0 9.7 %copy-start = (s32[1,4,4]{2,1,0:T(4,128)S(1)}, s32[1,4,4]{2,1,0:T(4,128)}, u32[]{:S(2)}) copy-start(s32[1,4,4]{2,1,0:T(4,128)} %param.8) | copy-start | bytes 196
  1.1 15.8 %collective-permute-start = (bf16[8,16,512]{2,1,0:T(8,128)(2,1)S(1)}, bf16[8,16,512]{2,1,0:T(8,128)(2,1)S(1)}, u32[]{:S(2)}, u32[]{:S(2)}) collective-permute-start(bf16[8,16,512]{2,1,0:T(8,128)(2,1)S(1)} %get-tuple-element.146), channel_id=1, source_target_pairs={{0,8},{4,12},{8,0},{12,4},{1,9},{5,13},{9,1},{13,5},{2,10},{6,14},... | collective-permute-start | bytes 393224 | tf_op jit(solution)/shard_map/ppermute | solution.py:232
  3.7 13.1 %collective-permute-start.1 = (bf16[8,16,512]{2,1,0:T(8,128)(2,1)S(1)}, bf16[8,16,512]{2,1,0:T(8,128)(2,1)S(1)}, u32[]{:S(2)}, u32[]{:S(2)}) collective-permute-start(bf16[8,16,512]{2,1,0:T(8,128)(2,1)S(1)} %get-tuple-element.145), channel_id=1, source_target_pairs={{0,4},{4,8},{8,12},{12,0},{1,5},{5,9},{9,13},{13,1},{2,6},{6,10},{... | collective-permute-start | bytes 393224 | tf_op jit(solution)/shard_map/ppermute | solution.py:232
  3.8 13.1 %collective-permute-start.2 = (bf16[8,16,512]{2,1,0:T(8,128)(2,1)S(1)}, bf16[8,16,512]{2,1,0:T(8,128)(2,1)S(1)}, u32[]{:S(2)}, u32[]{:S(2)}) collective-permute-start(bf16[8,16,512]{2,1,0:T(8,128)(2,1)S(1)} %get-tuple-element.144), channel_id=1, source_target_pairs={{0,12},{4,0},{8,4},{12,8},{1,13},{5,1},{9,5},{13,9},{2,14},{6,2},{... | collective-permute-start | bytes 393224 | tf_op jit(solution)/shard_map/ppermute | solution.py:232
  6.8 10.0 %collective-permute-start.3 = (bf16[4,48,512]{2,1,0:T(8,128)(2,1)S(1)}, bf16[4,48,512]{2,1,0:T(8,128)(2,1)S(1)}, u32[]{:S(2)}, u32[]{:S(2)}) collective-permute-start(bf16[4,48,512]{2,1,0:T(8,128)(2,1)S(1)} %get-tuple-element.140.refs_0_), channel_id=1, source_target_pairs={{0,2},{2,0},{1,3},{3,1},{4,6},{6,4},{5,7},{7,5},{8,10},{10,8},{9,1... | collective-permute-start | bytes 589832 | tf_op jit(solution)/shard_map/ppermute | solution.py:238
  8.4 8.5 %collective-permute-start.4 = (bf16[4,48,512]{2,1,0:T(8,128)(2,1)S(1)}, bf16[4,48,512]{2,1,0:T(8,128)(2,1)S(1)}, u32[]{:S(2)}, u32[]{:S(2)}) collective-permute-start(bf16[4,48,512]{2,1,0:T(8,128)(2,1)S(1)} %get-tuple-element.139.refs_1_), channel_id=1, source_target_pairs={{0,2},{2,0},{1,3},{3,1},{4,6},{6,4},{5,7},{7,5},{8,10},{10,8},{9,1... | collective-permute-start | bytes 589832 | tf_op jit(solution)/shard_map/ppermute | solution.py:238
  16.9 11.5 %collective-permute-start.10 = (bf16[8,32,512]{2,1,0:T(8,128)(2,1)S(1)}, bf16[8,32,512]{2,1,0:T(8,128)(2,1)S(1)}, u32[]{:S(2)}, u32[]{:S(2)}) collective-permute-start(bf16[8,32,512]{2,1,0:T(8,128)(2,1)S(1)} %get-tuple-element.95), channel_id=1, source_target_pairs={{0,4},{4,8},{8,12},{12,0},{1,5},{5,9},{9,13},{13,1},{2,6},{6,10},{... | collective-permute-start | bytes 786440 | tf_op jit(solution)/shard_map/ppermute | solution.py:232
  17.4 14.4 %collective-permute-start.5 = (bf16[8,32,512]{2,1,0:T(8,128)(2,1)S(1)}, bf16[8,32,512]{2,1,0:T(8,128)(2,1)S(1)}, u32[]{:S(2)}, u32[]{:S(2)}) collective-permute-start(bf16[8,32,512]{2,1,0:T(8,128)(2,1)S(1)} %get-tuple-element.75), channel_id=1, source_target_pairs={{0,12},{4,0},{8,4},{12,8},{1,13},{5,1},{9,5},{13,9},{2,14},{6,2},{... | collective-permute-start | bytes 786440 | tf_op jit(solution)/shard_map/ppermute | solution.py:232
  19.3 6.4 %collective-permute-start.6 = (bf16[8,16,512]{2,1,0:T(8,128)(2,1)S(1)}, bf16[8,16,512]{2,1,0:T(8,128)(2,1)S(1)}, u32[]{:S(2)}, u32[]{:S(2)}) collective-permute-start(bf16[8,16,512]{2,1,0:T(8,128)(2,1)S(1)} %collective-permute-done.1.refs_0_), channel_id=1, source_target_pairs={{0,2},{2,0},{1,3},{3,1},{4,6},{6,4},{5,7},{7,5},{8,10},{10,8},{9,1... | collective-permute-start | bytes 393224 | tf_op jit(solution)/shard_map/ppermute | solution.py:238
  20.8 6.3 %collective-permute-start.7 = (bf16[8,16,512]{2,1,0:T(8,128)(2,1)S(1)}, bf16[8,16,512]{2,1,0:T(8,128)(2,1)S(1)}, u32[]{:S(2)}, u32[]{:S(2)}) collective-permute-start(bf16[8,16,512]{2,1,0:T(8,128)(2,1)S(1)} %collective-permute-done.refs_0_), channel_id=1, source_target_pairs={{0,2},{2,0},{1,3},{3,1},{4,6},{6,4},{5,7},{7,5},{8,10},{10,8},{9,1... | collective-permute-start | bytes 393224 | tf_op jit(solution)/shard_map/ppermute | solution.py:238
  21.3 8.7 %collective-permute-start.8 = (bf16[8,16,512]{2,1,0:T(8,128)(2,1)S(1)}, bf16[8,16,512]{2,1,0:T(8,128)(2,1)S(1)}, u32[]{:S(2)}, u32[]{:S(2)}) collective-permute-start(bf16[8,16,512]{2,1,0:T(8,128)(2,1)S(1)} %collective-permute-done.2.refs_0_), channel_id=1, source_target_pairs={{0,2},{2,0},{1,3},{3,1},{4,6},{6,4},{5,7},{7,5},{8,10},{10,8},{9,1... | collective-permute-start | bytes 393224 | tf_op jit(solution)/shard_map/ppermute | solution.py:238
  28.4 8.7 %collective-permute-start.13 = (bf16[8,32,512]{2,1,0:T(8,128)(2,1)S(1)}, bf16[8,32,512]{2,1,0:T(8,128)(2,1)S(1)}, u32[]{:S(2)}, u32[]{:S(2)}) collective-permute-start(bf16[8,32,512]{2,1,0:T(8,128)(2,1)S(1)} %collective-permute-done.10.refs_0_), channel_id=1, source_target_pairs={{0,2},{2,0},{1,3},{3,1},{4,6},{6,4},{5,7},{7,5},{8,10},{10,8},{9,1... | collective-permute-start | bytes 786440 | tf_op jit(solution)/shard_map/ppermute | solution.py:238
  31.7 8.7 %collective-permute-start.9 = (bf16[8,32,512]{2,1,0:T(8,128)(2,1)S(1)}, bf16[8,32,512]{2,1,0:T(8,128)(2,1)S(1)}, u32[]{:S(2)}, u32[]{:S(2)}) collective-permute-start(bf16[8,32,512]{2,1,0:T(8,128)(2,1)S(1)} %collective-permute-done.5.refs_0_), channel_id=1, source_target_pairs={{0,2},{2,0},{1,3},{3,1},{4,6},{6,4},{5,7},{7,5},{8,10},{10,8},{9,1... | collective-permute-start | bytes 786440 | tf_op jit(solution)/shard_map/ppermute | solution.py:238
  33.2 10.1 %collective-permute-start.11 = (bf16[8,32,512]{2,1,0:T(8,128)(2,1)S(1)}, bf16[8,32,512]{2,1,0:T(8,128)(2,1)S(1)}, u32[]{:S(2)}, u32[]{:S(2)}) collective-permute-start(bf16[8,32,512]{2,1,0:T(8,128)(2,1)S(1)} %get-tuple-element.96), channel_id=1, source_target_pairs={{0,8},{4,12},{8,0},{12,4},{1,9},{5,13},{9,1},{13,5},{2,10},{6,14},... | collective-permute-start | bytes 786440 | tf_op jit(solution)/shard_map/ppermute | solution.py:232
  35.5 7.8 %collective-permute-start.12 = (bf16[24,16,512]{2,1,0:T(8,128)(2,1)S(1)}, bf16[24,16,512]{2,1,0:T(8,128)(2,1)S(1)}, u32[]{:S(2)}, u32[]{:S(2)}) collective-permute-start(bf16[24,16,512]{2,1,0:T(8,128)(2,1)S(1)} %shard_map.69), channel_id=1, source_target_pairs={{0,1},{1,0},{2,3},{3,2},{4,5},{5,4},{6,7},{7,6},{8,9},{9,8},{10,11... | collective-permute-start | bytes 1179656 | tf_op jit(solution)/shard_map/ppermute | solution.py:273
  43.9 6.6 %collective-permute-start.17 = (bf16[8,32,512]{2,1,0:T(8,128)(2,1)S(1)}, bf16[8,32,512]{2,1,0:T(8,128)(2,1)S(1)}, u32[]{:S(2)}, u32[]{:S(2)}) collective-permute-start(bf16[8,32,512]{2,1,0:T(8,128)(2,1)S(1)} %shard_map.71.refs_0_), channel_id=1, source_target_pairs={{0,2},{2,0},{1,3},{3,1},{4,6},{6,4},{5,7},{7,5},{8,10},{10,8},{9,1... | collective-permute-start | bytes 786440 | tf_op jit(solution)/shard_map/ppermute | solution.py:238
  45.4 11.9 %collective-permute-start.14 = (bf16[8,16,512]{2,1,0:T(8,128)(2,1)S(1)}, bf16[8,16,512]{2,1,0:T(8,128)(2,1)S(1)}, u32[]{:S(2)}, u32[]{:S(2)}) collective-permute-start(bf16[8,16,512]{2,1,0:T(8,128)(2,1)S(1)} %get-tuple-element.108), channel_id=1, source_target_pairs={{0,12},{4,8},{8,4},{12,0},{1,13},{5,9},{9,5},{13,1},{2,14},{6,10},... | collective-permute-start | bytes 393224 | tf_op jit(solution)/shard_map/ppermute | solution.py:235
  46.2 11.2 %collective-permute-start.15 = (bf16[8,16,512]{2,1,0:T(8,128)(2,1)S(1)}, bf16[8,16,512]{2,1,0:T(8,128)(2,1)S(1)}, u32[]{:S(2)}, u32[]{:S(2)}) collective-permute-start(bf16[8,16,512]{2,1,0:T(8,128)(2,1)S(1)} %get-tuple-element.109), channel_id=1, source_target_pairs={{0,8},{4,12},{8,0},{12,4},{1,9},{5,13},{9,1},{13,5},{2,10},{6,14},... | collective-permute-start | bytes 393224 | tf_op jit(solution)/shard_map/ppermute | solution.py:235
  50.5 6.9 %collective-permute-start.16 = (bf16[8,16,512]{2,1,0:T(8,128)(2,1)S(1)}, bf16[8,16,512]{2,1,0:T(8,128)(2,1)S(1)}, u32[]{:S(2)}, u32[]{:S(2)}) collective-permute-start(bf16[8,16,512]{2,1,0:T(8,128)(2,1)S(1)} %get-tuple-element.110), channel_id=1, source_target_pairs={{0,4},{4,0},{8,12},{12,8},{1,5},{5,1},{9,13},{13,9},{2,6},{6,2},{1... | collective-permute-start | bytes 393224 | tf_op jit(solution)/shard_map/ppermute | solution.py:235
  52.8 4.6 %collective-permute-start.18 = (bf16[24,32,512]{2,1,0:T(8,128)(2,1)S(1)}, bf16[24,32,512]{2,1,0:T(8,128)(2,1)S(1)}, u32[]{:S(2)}, u32[]{:S(2)}) collective-permute-start(bf16[24,32,512]{2,1,0:T(8,128)(2,1)S(1)} %shard_map.77), channel_id=1, source_target_pairs={{0,1},{1,0},{2,3},{3,2},{4,5},{5,4},{6,7},{7,6},{8,9},{9,8},{10,11... | collective-permute-start | bytes 2359304 | tf_op jit(solution)/shard_map/ppermute | solution.py:284
  58.2 19.0 %collective-permute-start.19 = (bf16[8,32,512]{2,1,0:T(8,128)(2,1)S(1)}, bf16[8,32,512]{2,1,0:T(8,128)(2,1)S(1)}, u32[]{:S(2)}, u32[]{:S(2)}) collective-permute-start(bf16[8,32,512]{2,1,0:T(8,128)(2,1)S(1)} %shard_map.79), channel_id=1, source_target_pairs={{0,8},{4,12},{8,0},{12,4},{1,9},{5,13},{9,1},{13,5},{2,10},{6,14},... | collective-permute-start | bytes 786440 | tf_op jit(solution)/shard_map/ppermute | solution.py:235
  62.0 21.1 %collective-permute-start.20 = (bf16[8,32,512]{2,1,0:T(8,128)(2,1)S(1)}, bf16[8,32,512]{2,1,0:T(8,128)(2,1)S(1)}, u32[]{:S(2)}, u32[]{:S(2)}) collective-permute-start(bf16[8,32,512]{2,1,0:T(8,128)(2,1)S(1)} %get-tuple-element.132), channel_id=1, source_target_pairs={{0,12},{4,8},{8,4},{12,0},{1,13},{5,9},{9,5},{13,1},{2,14},{6,10},... | collective-permute-start | bytes 786440 | tf_op jit(solution)/shard_map/ppermute | solution.py:235
  63.8 19.3 %collective-permute-start.21 = (bf16[8,32,512]{2,1,0:T(8,128)(2,1)S(1)}, bf16[8,32,512]{2,1,0:T(8,128)(2,1)S(1)}, u32[]{:S(2)}, u32[]{:S(2)}) collective-permute-start(bf16[8,32,512]{2,1,0:T(8,128)(2,1)S(1)} %get-tuple-element.133), channel_id=1, source_target_pairs={{0,4},{4,0},{8,12},{12,8},{1,5},{5,1},{9,13},{13,9},{2,6},{6,2},{1... | collective-permute-start | bytes 786440 | tf_op jit(solution)/shard_map/ppermute | solution.py:235
  (2 other events, 11.2 us)
